TPU v7x, 32 devices: a whole 2x2x4 slice. The times are simulated.
32 devices in a mesh: ctx: 4 (over y, x), tp: 2 (over core), fsdp: 4 (over z).
Axes of the slice: x: 2, y: 2, z: 4, core: 2. Of those that a mesh axis runs over, the one named last changes fastest.
Arguments:
- block_input: bfloat16 [8, 2048, 2048], P('fsdp', 'ctx'), may hold values from -6 to 6
- doc_start: int32 [8, 2048], P('fsdp', 'ctx'), may hold values from 0 to 2047, as said below
- gain_mix: float32 [2048], replicated, may hold values from 0.5 to 1.5
- query_weight: float32 [2048, 2048], P(('ctx', 'fsdp'), 'tp'), may hold values from -0.125 to 0.125
- key_weight: float32 [2048, 2048], P(('ctx', 'fsdp'), 'tp'), may hold values from -0.125 to 0.125
- value_weight: float32 [2048, 2048], P(('ctx', 'fsdp'), 'tp'), may hold values from -0.125 to 0.125
- beta_weight: float32 [2048, 16], P(('ctx', 'fsdp'), 'tp'), may hold values from -0.125 to 0.125
- beta_bias: float32 [16], P('tp'), may hold values from -5 to 0
- conv_weight: float32 [3, 4, 2048], P(None, None, 'tp'), may hold values from -3 to 3
- gain_o: float32 [128], replicated, may hold values from 0.5 to 1.5
- out_weight: float32 [2048, 2048], P('tp', ('ctx', 'fsdp')), may hold values from -0.25 to 0.25
- gain_ffn: float32 [2048], replicated, may hold values from 0.5 to 1.5
- gate_weight: float32 [2048, 5632], P(('ctx', 'fsdp'), 'tp'), may hold values from -0.125 to 0.125
- up_weight: float32 [2048, 5632], P(('ctx', 'fsdp'), 'tp'), may hold values from -0.125 to 0.125
- down_weight: float32 [5632, 2048], P('tp', ('ctx', 'fsdp')), may hold values from -0.15625 to 0.15625
- out_grad: bfloat16 [8, 2048, 2048], P('fsdp', 'ctx'), may hold values from -6 to 6
Outputs:
- block_output: bfloat16 [8, 2048, 2048], P('fsdp', 'ctx')
- input_grad: bfloat16 [8, 2048, 2048], P('fsdp', 'ctx')
- gain_mix_grad: float32 [2048], replicated
- query_weight_grad: float32 [2048, 2048], P(('ctx', 'fsdp'), 'tp')
- key_weight_grad: float32 [2048, 2048], P(('ctx', 'fsdp'), 'tp')
- value_weight_grad: float32 [2048, 2048], P(('ctx', 'fsdp'), 'tp')
- beta_weight_grad: float32 [2048, 16], P(('ctx', 'fsdp'), 'tp')
- beta_bias_grad: float32 [16], P('tp')
- conv_weight_grad: float32 [3, 4, 2048], P(None, None, 'tp')
- gain_o_grad: float32 [128], replicated
- out_weight_grad: float32 [2048, 2048], P('tp', ('ctx', 'fsdp'))
- gain_ffn_grad: float32 [2048], replicated
- gate_weight_grad: float32 [2048, 5632], P(('ctx', 'fsdp'), 'tp')
- up_weight_grad: float32 [2048, 5632], P(('ctx', 'fsdp'), 'tp')
- down_weight_grad: float32 [5632, 2048], P('tp', ('ctx', 'fsdp'))
Inputs may be any that keep to these rules, and one draw needn't show every extreme that they name: doc_start[s, t] is the position in sequence s of the first token of the document that holds token t; documents are contiguous runs and doc_start[s, 0] = 0.
All inputs are finite; a program needn't handle non-finite values.
Results may differ from a plain program's by a relative error of at most 0.024.
Values may be sent and summed in bfloat16 or wider, within the bound.
No kernel may reach another device: no remote copies, remote signals or barrier semaphores. Data moves between devices by JAX's collectives and lax.ppermute only.
A program may use at most 512 MiB of HBM per device.

v0:
```python
import jax
import jax.numpy as jnp
from jax import lax
from jax.sharding import PartitionSpec as P

GROUP = 64


EPSILON = 1e-06
HEAD_FLOOR = 0.01
HIGHEST = lax.Precision.HIGHEST


def from_behind(block, axis, distance):
    devices = range(lax.axis_size(axis))
    route = [(i - distance, i) for i in devices if i - distance in devices]
    return lax.ppermute(block, axis, route)


def invert_unit_lower(strict):
    size = strict.shape[-1]
    identity = jnp.eye(size, dtype=jnp.float32)
    power = -strict
    result = identity + power
    for repeat in range(size.bit_length() - 2):
        power = jnp.matmul(power, power, precision=HIGHEST)
        result = jnp.matmul(result, identity + power, precision=HIGHEST)
    return result


def block_step(state_mat, inputs):
    queries, key_vecs, values, strengths, starts, first_pos = inputs
    size = key_vecs.shape[-2]
    order = jnp.arange(size)
    carried = (starts < first_pos).astype(jnp.float32)
    same_doc = starts[..., :, None] == starts[..., None, :]
    below = order[:, None] > order[None, :]
    upto = order[:, None] >= order[None, :]
    key_gram = jnp.einsum("...td,...sd->...ts", key_vecs, key_vecs, precision=HIGHEST)
    strict = jnp.where(same_doc & below, strengths[..., :, None] * key_gram, 0.0)
    from_state = jnp.einsum("...td,...de->...te", key_vecs, state_mat, precision=HIGHEST)
    targets = strengths[..., None] * (values - carried[..., None] * from_state)
    updates = jnp.matmul(invert_unit_lower(strict), targets, precision=HIGHEST)
    scores = jnp.where(
        same_doc & upto, jnp.einsum("...td,...sd->...ts", queries, key_vecs, precision=HIGHEST), 0.0
    )
    outputs = carried[..., None] * jnp.einsum(
        "...td,...de->...te", queries, state_mat, precision=HIGHEST
    )
    outputs = outputs + jnp.einsum("...ts,...se->...te", scores, updates, precision=HIGHEST)
    last_doc = (starts == starts[..., -1:]).astype(jnp.float32)
    new_state = carried[..., -1:, None] * state_mat + jnp.einsum(
        "...sd,...se->...de", key_vecs * last_doc[..., None], updates, precision=HIGHEST
    )
    return (new_state, outputs)


def delta_local(queries, key_vecs, values, strengths, doc_start, first_pos):
    seq_count, heads_here, length, head_dim = queries.shape
    blocks = length // GROUP
    values_ext = jnp.concatenate([values, jnp.zeros_like(queries)], axis=-1)
    start_state = jnp.concatenate(
        [
            jnp.zeros((seq_count, heads_here, head_dim, values.shape[-1]), jnp.float32),
            jnp.broadcast_to(
                jnp.eye(head_dim, dtype=jnp.float32), (seq_count, heads_here, head_dim, head_dim)
            ),
        ],
        axis=-1,
    )

    def by_block(array):
        return array.reshape(seq_count, heads_here, blocks, GROUP, -1).transpose(2, 0, 1, 3, 4)

    block_strengths = strengths.reshape(seq_count, heads_here, blocks, GROUP).transpose(2, 0, 1, 3)
    block_starts = doc_start.reshape(seq_count, 1, blocks, GROUP).transpose(2, 0, 1, 3)
    firsts = first_pos + jnp.arange(blocks, dtype=jnp.int32) * GROUP
    final, outputs = lax.scan(
        block_step,
        start_state,
        (
            by_block(queries),
            by_block(key_vecs),
            by_block(values_ext),
            block_strengths,
            block_starts,
            firsts,
        ),
    )
    return (outputs.transpose(1, 2, 0, 3, 4).reshape(seq_count, heads_here, length, -1), final)


def unit_norm(values):
    return values * lax.rsqrt(jnp.sum(values * values, axis=-1, keepdims=True) + EPSILON)


def mixer_inputs(extended, conv_weight, doc_start, positions, heads_here):
    taps = conv_weight.shape[1]
    length = extended.shape[2] - taps + 1
    total = jnp.zeros(
        (extended.shape[0], extended.shape[1], length, extended.shape[3]), jnp.float32
    )
    for tap_index in range(taps):
        shift_back = taps - 1 - tap_index
        valid = ((positions - shift_back)[None, :] >= doc_start).astype(jnp.float32)
        total = (
            total
            + conv_weight[:, tap_index][:, None, None, :]
            * extended[:, :, tap_index : tap_index + length, :]
            * valid[None, :, :, None]
        )
    activated = jax.nn.silu(total)
    split_heads = activated.reshape(3, extended.shape[1], length, heads_here, -1).transpose(
        0, 1, 3, 2, 4
    )
    return (unit_norm(split_heads[0]), unit_norm(split_heads[1]), split_heads[2])


def rms_scale(values, floor_value):
    return lax.rsqrt(jnp.mean(values * values, axis=-1, keepdims=True) + floor_value)


def norm_backward(grad_normed, inputs, scale, gain):
    normed = inputs * scale
    weighted = grad_normed * gain
    return (
        scale * (weighted - normed * jnp.mean(weighted * normed, axis=-1, keepdims=True)),
        normed,
    )


def times_transposed(left, right):
    return lax.dot_general(
        left, right, (((1,), (1,)), ((), ())), preferred_element_type=jnp.float32
    )


def outer_rows(left, right):
    return lax.dot_general(
        left, right, (((0,), (0,)), ((), ())), preferred_element_type=jnp.float32
    )


def heads_combine(partial_value):
    return lax.psum(partial_value.astype(jnp.bfloat16), "tp").astype(jnp.float32)


def rows_own(held):
    count = held.shape[0] // lax.axis_size("tp")
    return lax.dynamic_slice_in_dim(held, lax.axis_index("tp") * count, count, 0)


def local(
    block_input,
    doc_start,
    gain_mix,
    query_weight,
    key_weight,
    value_weight,
    beta_weight,
    beta_bias,
    conv_weight,
    gain_o,
    out_weight,
    gain_ffn,
    gate_weight,
    up_weight,
    down_weight,
    out_grad,
):
    seq_count, local_len, width = block_input.shape
    row_count = seq_count * local_len
    heads_here = beta_weight.shape[1]
    query_full, key_full, value_full, beta_full, out_full, gate_full, up_full, down_full = (
        lax.all_gather(query_weight.astype(jnp.bfloat16), ("ctx", "fsdp"), axis=0, tiled=True),
        lax.all_gather(key_weight.astype(jnp.bfloat16), ("ctx", "fsdp"), axis=0, tiled=True),
        lax.all_gather(value_weight.astype(jnp.bfloat16), ("ctx", "fsdp"), axis=0, tiled=True),
        lax.all_gather(beta_weight.astype(jnp.bfloat16), ("ctx", "fsdp"), axis=0, tiled=True),
        lax.all_gather(out_weight.astype(jnp.bfloat16), ("ctx", "fsdp"), axis=1, tiled=True),
        lax.all_gather(gate_weight.astype(jnp.bfloat16), ("ctx", "fsdp"), axis=0, tiled=True),
        lax.all_gather(up_weight.astype(jnp.bfloat16), ("ctx", "fsdp"), axis=0, tiled=True),
        lax.all_gather(down_weight.astype(jnp.bfloat16), ("ctx", "fsdp"), axis=1, tiled=True),
    )
    inputs = block_input.astype(jnp.float32).reshape(row_count, width)
    scale_mix = rms_scale(inputs, EPSILON)
    normed_mix = (inputs * scale_mix * gain_mix).astype(jnp.bfloat16)
    query_pre = jnp.dot(normed_mix, query_full, preferred_element_type=jnp.float32)
    key_pre = jnp.dot(normed_mix, key_full, preferred_element_type=jnp.float32)
    value_pre = jnp.dot(normed_mix, value_full, preferred_element_type=jnp.float32)
    strength_rows = jax.nn.sigmoid(
        jnp.dot(normed_mix, beta_full, preferred_element_type=jnp.float32) + beta_bias
    )
    stacked = jnp.stack([query_pre, key_pre, value_pre]).reshape(3, seq_count, local_len, -1)
    margin = conv_weight.shape[1] - 1
    before = from_behind(stacked[:, :, local_len - margin :, :], "ctx", 1)
    extended = jnp.concatenate([before, stacked], axis=2)
    first_pos = lax.axis_index("ctx") * local_len
    positions = first_pos + jnp.arange(local_len, dtype=jnp.int32)

    def make_inputs(ext_arr, conv_arr):
        return mixer_inputs(ext_arr, conv_arr, doc_start, positions, heads_here)

    def run_local(query_in, key_in, value_in, strength_in):
        return delta_local(query_in, key_in, value_in, strength_in, doc_start, first_pos)

    queries, key_vecs, values = make_inputs(extended, conv_weight)
    strengths = strength_rows.reshape(seq_count, local_len, heads_here).transpose(0, 2, 1)
    outputs_ext, final = run_local(queries, key_vecs, values, strengths)
    head_dim = values.shape[-1]
    own_out = outputs_ext[..., :head_dim]
    carried_q = outputs_ext[..., head_dim:]
    end_local = final[..., :head_dim]
    transfer = final[..., head_dim:]
    flipped = jnp.swapaxes(transfer, -1, -2)
    state_in = jnp.zeros_like(end_local)
    state_out = end_local
    for repeat in range(lax.axis_size("ctx") - 1):
        state_in = from_behind(state_out.astype(jnp.bfloat16), "ctx", 1).astype(state_out.dtype)
        state_out = jnp.matmul(transfer, state_in, precision=HIGHEST) + end_local
    mixed = own_out + jnp.einsum("shtk,shkv->shtv", carried_q, state_in, precision=HIGHEST)
    scale_head = rms_scale(mixed, HEAD_FLOOR)
    unit_head = mixed * scale_head
    mixed_rows = (
        (unit_head * gain_o).transpose(0, 2, 1, 3).reshape(row_count, -1).astype(jnp.bfloat16)
    )
    branch_part = jnp.dot(mixed_rows, out_full, preferred_element_type=jnp.float32)
    residual = inputs + heads_combine(branch_part)
    scale_ffn = rms_scale(residual, EPSILON)
    normed_ffn = (residual * scale_ffn * gain_ffn).astype(jnp.bfloat16)
    gate = jnp.dot(normed_ffn, gate_full, preferred_element_type=jnp.float32)
    up_val = jnp.dot(normed_ffn, up_full, preferred_element_type=jnp.float32)
    sigmoid_gate = jax.nn.sigmoid(gate)
    activated = gate * sigmoid_gate
    hidden = (activated * up_val).astype(jnp.bfloat16)
    ffn_part = jnp.dot(hidden, down_full, preferred_element_type=jnp.float32)
    output_held = (residual + heads_combine(ffn_part)).astype(jnp.bfloat16)
    block_output = output_held.reshape(seq_count, local_len, width)
    grad_rows = out_grad.reshape(row_count, width)
    grad_hidden = times_transposed(grad_rows, down_full)
    down_grad = outer_rows(hidden, grad_rows)
    grad_gate = (grad_hidden * up_val * sigmoid_gate * (1.0 + gate * (1.0 - sigmoid_gate))).astype(
        jnp.bfloat16
    )
    grad_up = (grad_hidden * activated).astype(jnp.bfloat16)
    gate_grad = outer_rows(normed_ffn, grad_gate)
    up_grad = outer_rows(normed_ffn, grad_up)
    grad_normed = times_transposed(grad_gate, gate_full) + times_transposed(grad_up, up_full)
    grad_normed_held = heads_combine(grad_normed)
    back_ffn, unit_ffn = norm_backward(grad_normed_held, residual, scale_ffn, gain_ffn)
    grad_residual = grad_rows.astype(jnp.float32) + back_ffn
    gain_ffn_part = jnp.sum(rows_own(grad_normed_held * unit_ffn), axis=0)
    grad_branch = grad_residual.astype(jnp.bfloat16)
    out_weight_part = outer_rows(mixed_rows, grad_branch)
    grad_head_normed = (
        times_transposed(grad_branch, out_full)
        .reshape(seq_count, local_len, heads_here, -1)
        .transpose(0, 2, 1, 3)
    )
    gain_o_part = jnp.sum(grad_head_normed * unit_head, axis=(0, 1, 2))
    grad_mixed, unused_unit = norm_backward(grad_head_normed, mixed, scale_head, gain_o)
    across = jnp.einsum("shtk,shtv->shkv", carried_q, grad_mixed, precision=HIGHEST)
    grad_carried = jnp.einsum("shtv,shkv->shtk", grad_mixed, state_in, precision=HIGHEST)
    grad_end = jnp.zeros_like(across)
    grad_now = across
    for repeat in range(lax.axis_size("ctx") - 1):
        grad_end = from_behind(grad_now.astype(jnp.bfloat16), "ctx", -1).astype(grad_now.dtype)
        grad_now = across + jnp.matmul(flipped, grad_end, precision=HIGHEST)
    grad_transfer = jnp.einsum("shkv,shjv->shkj", grad_end, state_in, precision=HIGHEST)
    local_out, local_pullback = jax.vjp(run_local, queries, key_vecs, values, strengths)
    grad_query, grad_key, grad_value, grad_strength = local_pullback(
        (
            jnp.concatenate([grad_mixed, grad_carried], axis=-1),
            jnp.concatenate([grad_end, grad_transfer], axis=-1),
        )
    )
    conv_out, conv_pullback = jax.vjp(make_inputs, extended, conv_weight)
    grad_ext, conv_part = conv_pullback((grad_query, grad_key, grad_value))
    from_next = from_behind(grad_ext[:, :, :margin, :], "ctx", -1)
    grad_stacked = grad_ext[:, :, margin:, :].at[:, :, local_len - margin :, :].add(from_next)
    grad_pre = grad_stacked.reshape(3, row_count, -1).astype(jnp.bfloat16)
    grad_logits = (
        grad_strength.transpose(0, 2, 1).reshape(row_count, heads_here)
        * strength_rows
        * (1.0 - strength_rows)
    )
    bias_part = jnp.sum(grad_logits, axis=0)
    grad_logit_low = grad_logits.astype(jnp.bfloat16)
    grad_normed_mix = (
        times_transposed(grad_pre[0], query_full)
        + times_transposed(grad_pre[1], key_full)
        + times_transposed(grad_pre[2], value_full)
        + times_transposed(grad_logit_low, beta_full)
    )
    query_part = outer_rows(normed_mix, grad_pre[0])
    key_part = outer_rows(normed_mix, grad_pre[1])
    value_part = outer_rows(normed_mix, grad_pre[2])
    beta_part = outer_rows(normed_mix, grad_logit_low)
    grad_mix_held = heads_combine(grad_normed_mix)
    back_mix, unit_mix = norm_backward(grad_mix_held, inputs, scale_mix, gain_mix)
    input_held = (grad_residual + back_mix).astype(jnp.bfloat16)
    input_grad = input_held.reshape(seq_count, local_len, width)
    gain_mix_part = jnp.sum(rows_own(grad_mix_held * unit_mix), axis=0)
    query_grad, key_grad, value_grad, beta_grad, out_grad_w, gate_grad_s, up_grad_s, down_grad_s = (
        lax.psum_scatter(
            query_part.astype(jnp.bfloat16), ("ctx", "fsdp"), scatter_dimension=0, tiled=True
        ).astype(jnp.float32),
        lax.psum_scatter(
            key_part.astype(jnp.bfloat16), ("ctx", "fsdp"), scatter_dimension=0, tiled=True
        ).astype(jnp.float32),
        lax.psum_scatter(
            value_part.astype(jnp.bfloat16), ("ctx", "fsdp"), scatter_dimension=0, tiled=True
        ).astype(jnp.float32),
        lax.psum_scatter(
            beta_part.astype(jnp.bfloat16), ("ctx", "fsdp"), scatter_dimension=0, tiled=True
        ).astype(jnp.float32),
        lax.psum_scatter(
            out_weight_part.astype(jnp.bfloat16), ("ctx", "fsdp"), scatter_dimension=1, tiled=True
        ).astype(jnp.float32),
        lax.psum_scatter(
            gate_grad.astype(jnp.bfloat16), ("ctx", "fsdp"), scatter_dimension=0, tiled=True
        ).astype(jnp.float32),
        lax.psum_scatter(
            up_grad.astype(jnp.bfloat16), ("ctx", "fsdp"), scatter_dimension=0, tiled=True
        ).astype(jnp.float32),
        lax.psum_scatter(
            down_grad.astype(jnp.bfloat16), ("ctx", "fsdp"), scatter_dimension=1, tiled=True
        ).astype(jnp.float32),
    )
    gain_mix_grad, gain_ffn_grad, gain_o_grad = lax.psum(
        (gain_mix_part, gain_ffn_part, gain_o_part), ("ctx", "tp", "fsdp")
    )
    conv_grad, bias_grad = lax.psum((conv_part, bias_part), ("ctx", "fsdp"))
    return (
        block_output,
        input_grad,
        gain_mix_grad,
        query_grad,
        key_grad,
        value_grad,
        beta_grad,
        bias_grad,
        conv_grad,
        gain_o_grad,
        out_grad_w,
        gain_ffn_grad,
        gate_grad_s,
        up_grad_s,
        down_grad_s,
    )


def solution(mesh):
    placed = (
        P("fsdp", "ctx", None),
        P("fsdp", "ctx"),
        P(),
        P(("ctx", "fsdp"), "tp"),
        P(("ctx", "fsdp"), "tp"),
        P(("ctx", "fsdp"), "tp"),
        P(("ctx", "fsdp"), "tp"),
        P("tp"),
        P(None, None, "tp"),
        P(),
        P("tp", ("ctx", "fsdp")),
        P(),
        P(("ctx", "fsdp"), "tp"),
        P(("ctx", "fsdp"), "tp"),
        P("tp", ("ctx", "fsdp")),
        P("fsdp", "ctx", None),
    )
    return jax.shard_map(
        local,
        mesh=mesh,
        in_specs=placed,
        out_specs=(
            P("fsdp", "ctx", None),
            P("fsdp", "ctx", None),
            P(),
            P(("ctx", "fsdp"), "tp"),
            P(("ctx", "fsdp"), "tp"),
            P(("ctx", "fsdp"), "tp"),
            P(("ctx", "fsdp"), "tp"),
            P("tp"),
            P(None, None, "tp"),
            P(),
            P("tp", ("ctx", "fsdp")),
            P(),
            P(("ctx", "fsdp"), "tp"),
            P(("ctx", "fsdp"), "tp"),
            P("tp", ("ctx", "fsdp")),
        ),
        check_vma=False,
    )
```

profile of v0, /device:TPU:0, one launch (start us, length us, event | category | flops | bytes accessed | tf_op | source)
XLA Modules:
  0.0 3578.8 jit_solution(17060101244281482657)
XLA Ops:
  17.9 43.0 %all_gather.27 = bf16[2048,8]{0,1:T(8,128)(2,1)S(1)} all-gather(bf16[128,8]{0,1:T(8,128)(2,1)S(1)} %convert_element_type.327), channel_id=1, replica_groups=mesh['ctx'=4,'tp'=2,'fsdp'=4] {'ctx','fsdp'}, dimensions={0}, use_global_device_ids=true | all-gather | bytes 34816 | tf_op jit(solution)/shard_map/all_gather | solution.py:178
  75.0 15.2 all-gather.12.cloned.1.call-done
  90.2 10.0 fusion.292
  100.2 67.8 %all-gather.10.cloned.1.call-done = bf16[2048,1024]{1,0:T(8,128)(2,1)} async-done(((bf16[128,1024]{1,0:T(8,128)(2,1)}), bf16[2048,1024]{1,0:T(8,128)(2,1)}) %all-gather.10.cloned.1.call-update) | async-done | bytes 4194320 | tf_op jit(solution)/shard_map/all_gather | solution.py:176
  168.0 9.9 fusion.289
  177.9 67.8 %all-gather.8.cloned.1.call-done = bf16[2048,1024]{1,0:T(8,128)(2,1)} async-done(((bf16[128,1024]{1,0:T(8,128)(2,1)}), bf16[2048,1024]{1,0:T(8,128)(2,1)}) %all-gather.8.cloned.1.call-update) | async-done | bytes 4194320 | tf_op jit(solution)/shard_map/all_gather | solution.py:175
  245.7 10.6 fusion.286
  256.3 10.3 pad_maximum_fusion
  278.4 15.9 multiply_bitcast_fusion
  294.4 10.9 copy.264
  305.3 5.7 fusion.272
  311.0 9.9 fusion.327
  341.9 202.8 %while.111 = (s32[]{:T(128)}, f32[2,8,128,256]{3,2,1,0:T(8,128)S(1)}, f32[8,2,8,64,256]{4,3,2,1,0:T(8,128)}, s32[8,2,1,64]{3,1,2,0:T(2,128)S(1)}, s32[8]{0:T(128...) while((s32[]{:T(128)}, ...), condition=%wide.region_4.5_spmd, body=%wide.region_3.4_spmd.sunk | while | flops 2318443008 | bytes 28745544 | solution.py:78
  549.3 8.6 collective-permute-done.1
  563.1 7.6 collective-permute-done.2
  571.4 5.3 collective-permute-start.3
  591.8 9.0 convolution_convert_fusion.8
  605.7 31.3 all-reduce.20.cloned.1.call-done
  642.9 6.1 multiply_convert_fusion.3
  649.1 134.8 %all-gather.18.cloned.1.call-done = bf16[2048,2816]{1,0:T(8,128)(2,1)} async-done(((bf16[128,2816]{1,0:T(8,128)(2,1)}), bf16[2048,2816]{1,0:T(8,128)(2,1)}) %all-gather.18.cloned.1.call-update) | async-done | bytes 11534352 | tf_op jit(solution)/shard_map/all_gather | solution.py:181
  783.9 18.7 fusion.338
  802.6 125.3 %all-gather.16.cloned.1.call-done = bf16[2048,2816]{1,0:T(8,128)(2,1)} async-done(((bf16[128,2816]{1,0:T(8,128)(2,1)}), bf16[2048,2816]{1,0:T(8,128)(2,1)}) %all-gather.16.cloned.1.call-update) | async-done | bytes 11534352 | tf_op jit(solution)/shard_map/all_gather | solution.py:180
  927.9 18.8 fusion.337
  946.7 165.6 %all-gather.20.cloned.1.call-done = bf16[2816,2048]{1,0:T(8,128)(2,1)} async-done(((bf16[2816,128]{1,0:T(8,128)(2,1)}), bf16[2816,2048]{1,0:T(8,128)(2,1)}) %all-gather.20.cloned.1.call-update) | async-done | bytes 11534352 | tf_op jit(solution)/shard_map/all_gather | solution.py:182
  1112.3 26.2 multiply_convert_fusion
  1138.5 19.1 fusion.339
  1157.6 17.7 add_convert_fusion.2
  1175.6 26.5 all-reduce.22.cloned.1.call-done
  1202.1 5.9 multiply_reduce_fusion.5
  1209.1 5.3 multiply_add_fusion.3
  1214.4 8.0 convolution_bitcast_fusion
  1230.7 7.8 fusion.330
  1252.8 338.5 %while.113 = (s32[]{:T(128)}, f32[2,8,128,256]{3,2,1,0:T(8,128)S(1)}, f32[8,2,8,64,64]{4,3,2,1,0:T(8,128)}, f32[8,2,8,64,1]{3,2,1,4,0:T(8,128)S(1)}, pred[8,2,8,...) while((s32[]{:T(128)}, ...), condition=%wide.region_13.14_spmd.clone.clone, body=%wide.region_12.13_spmd.clone.clone.sunk | while | flops 1715053696 | bytes 44245604 | solution.py:78
  1595.0 18.1 convolution_convert_fusion.3
  1622.3 9.1 collective-permute-done.6
  1641.7 671.8 %while.112 = (s32[]{:T(128)}, f32[2,8,128,256]{3,2,1,0:T(8,128)S(1)}, f32[8,2,8,64,128]{4,3,0,2,1:T(8,128)}, f32[8,2,8,64,128]{4,3,0,2,1:T(8,128)}, f32[8,2,8,64...) while((s32[]{:T(128)}, ...), condition=%wide.region_17.18_spmd, body=%wide.region_14.17_spmd.sunk | while | flops 4637129728 | bytes 90265576 | solution.py:78
  1705.4 5.2 fusion.734
  2036.9 5.2 fusion.734
  2318.3 9.6 convolution_convert_fusion.4
  2327.9 6.4 copy.185
  2340.6 6.2 fusion.270
  2347.0 12.4 add_add_fusion.2
  2359.5 29.2 multiply_reduce_fusion.2
  2388.7 18.1 multiply_multiply_fusion.3
  2409.7 17.1 pad_add_fusion
  2426.8 7.4 slice.165
  2450.3 6.9 fusion.343
  2457.2 7.2 add_convert_fusion.1
  2464.6 9.5 convolution_convert_fusion.7
  2474.2 9.5 convolution_convert_fusion.6
  2483.8 8.4 convolution_convert_fusion.5
  2492.4 17.9 convolution_convert_fusion
  2510.3 16.1 copy.187
  2526.5 19.2 convolution_convert_fusion.1
  2546.1 18.2 convolution_convert_fusion.2
  2570.6 86.7 %all-reduce.14 = (f32[8]{0:T(128)}, f32[3,4,1024]{2,0,1:T(4,128)S(1)}) all-reduce(f32[8]{0:T(128)S(1)} %copy-done.84, f32[3,4,1024]{2,0,1:T(4,128)S(1)} %pad_add_fusion.2), channel_id=1, replica_groups=mesh['ctx'=4,'tp'=2,'fsdp'=4] {'ctx','fsdp'}, use_global_device_ids=true, to_apply=%region_29.30 | all-reduce | flops 12296 | bytes 98368 | tf_op jit(solution)/shard_map/psum | solution.py:332
  2661.4 6.5 convert_element_type.359
  2669.7 64.3 %reduce-scatter.17.cloned.1.call-done = bf16[128,1024]{1,0:T(8,128)(2,1)} async-done(((bf16[2048,1024]{1,0:T(8,128)(2,1)}), bf16[128,1024]{1,0:T(8,128)(2,1)}) %reduce-scatter.17.cloned.1.call-update) | async-done | bytes 262160 | tf_op jit(solution)/shard_map/reduce_scatter | solution.py:307
  2735.8 95.0 %reduce-scatter.19.cloned.1.call-done = bf16[128,1024]{1,0:T(8,128)(2,1)} async-done(((bf16[2048,1024]{1,0:T(8,128)(2,1)}), bf16[128,1024]{1,0:T(8,128)(2,1)}) %reduce-scatter.19.cloned.1.call-update) | async-done | bytes 262160 | tf_op jit(solution)/shard_map/reduce_scatter | solution.py:310
  2836.6 42.5 %all-reduce.13 = (f32[2048]{0:T(1024)}, f32[128]{0:T(128)}, f32[2048]{0:T(1024)}) all-reduce(f32[2048]{0:T(1024)S(1)} %fusion.268, f32[128]{0:T(128)S(1)} %copy-done.85, f32[2048]{0:T(1024)S(1)} %fusion.267), channel_id=1, replica_groups=mesh['ctx'=4,'tp'=2,'fsdp'=4] {'ctx','tp','fsdp'}, use_global_device_ids=true, to_apply=%region_23.24 | all-reduce | flops 4224 | bytes 33792 | tf_op jit(solution)/shard_map/psum | solution.py:329
  2885.1 11.5 add_convert_fusion
  2896.6 181.3 %reduce-scatter.29.cloned.1.call-done = bf16[128,2816]{1,0:T(8,128)(2,1)} async-done(((bf16[2048,2816]{1,0:T(8,128)(2,1)}), bf16[128,2816]{1,0:T(8,128)(2,1)}) %reduce-scatter.29.cloned.1.call-update) | async-done | bytes 720912
  3080.6 243.1 %reduce-scatter.23.cloned.1.call-done = bf16[128,2816]{1,0:T(8,128)(2,1)} async-done(((bf16[2048,2816]{1,0:T(8,128)(2,1)}), bf16[128,2816]{1,0:T(8,128)(2,1)}) %reduce-scatter.23.cloned.1.call-update) | async-done | bytes 720912 | tf_op jit(solution)/shard_map/reduce_scatter | solution.py:322
  3326.0 243.5 %reduce-scatter.21.cloned.1.call-done = bf16[128,2816]{1,0:T(8,128)(2,1)} async-done(((bf16[2048,2816]{1,0:T(8,128)(2,1)}), bf16[128,2816]{1,0:T(8,128)(2,1)}) %reduce-scatter.21.cloned.1.call-update) | async-done | bytes 720912 | tf_op jit(solution)/shard_map/reduce_scatter | solution.py:319
  (1167 shorter events, 1381.0 us)
Async XLA Ops:
  7.2 10.7 copy-start.79
  7.2 53.8 %copy-start.78 = (f32[3,4,1024]{2,1,0:T(4,128)S(1)}, f32[3,4,1024]{2,1,0:T(4,128)}, u32[]{:S(2)}) copy-start(f32[3,4,1024]{2,1,0:T(4,128)} %param.32) | copy-start | bytes 147460
  7.2 83.0 %all-gather.12.cloned.1.call-start = ((), (), s32[]{:S(2)}) async-start(), calls=%async_computation.10 | async-start | bytes 4456448 | tf_op jit(solution)/shard_map/all_gather | solution.py:177
  9.1 158.9 %all-gather.10.cloned.1.call-start = ((), (), s32[]{:S(2)}) async-start(), calls=%async_computation.9 | async-start | bytes 4456448 | tf_op jit(solution)/shard_map/all_gather | solution.py:176
  10.9 234.8 %all-gather.8.cloned.1.call-start = ((), (), s32[]{:S(2)}) async-start(), calls=%async_computation.8 | async-start | bytes 4456448 | tf_op jit(solution)/shard_map/all_gather | solution.py:175
  12.8 579.0 %all-gather.14.cloned.1.call-start = ((), (), s32[]{:S(2)}) async-start(), calls=%async_computation.11 | async-start | bytes 4456448 | tf_op jit(solution)/shard_map/all_gather | solution.py:179
  14.6 622.4 %all-reduce.20.cloned.1.call-start = ((), (), s32[]{:S(2)}) async-start(), calls=%async_computation.12 | async-start | bytes 8388608 | tf_op jit(solution)/shard_map/psum | solution.py:145
  17.9 49.3 %copy-start.64 = (f32[1,4,2,128]{3,1,2,0:T(4,128)}, f32[1,4,2,128]{3,1,2,0:T(4,128)S(1)}, u32[]{:S(2)}) copy-start(f32[1,4,2,128]{3,1,2,0:T(4,128)S(1)} %copy.242) | copy-start | bytes 12292
  61.0 10.6 copy-start.50
  74.8 25.5 copy-start.40
  74.9 203.5 %copy-start.52 = (f32[3,1024]{1,0:T(4,128)}, f32[3,1024]{1,0:T(4,128)S(1)}, u32[]{:S(2)}) copy-start(f32[3,1024]{1,0:T(4,128)S(1)} %get-tuple-element.2198) | copy-start | bytes 36868
  74.9 203.5 %copy-start.54 = (f32[3,1024]{1,0:T(4,128)}, f32[3,1024]{1,0:T(4,128)S(1)}, u32[]{:S(2)}) copy-start(f32[3,1024]{1,0:T(4,128)S(1)} %get-tuple-element.2199) | copy-start | bytes 36868
  74.9 203.5 %copy-start.56 = (f32[3,1024]{1,0:T(4,128)}, f32[3,1024]{1,0:T(4,128)S(1)}, u32[]{:S(2)}) copy-start(f32[3,1024]{1,0:T(4,128)S(1)} %get-tuple-element.2196) | copy-start | bytes 36868
  74.9 203.5 %copy-start.58 = (f32[3,1024]{1,0:T(4,128)}, f32[3,1024]{1,0:T(4,128)S(1)}, u32[]{:S(2)}) copy-start(f32[3,1024]{1,0:T(4,128)S(1)} %get-tuple-element.2197) | copy-start | bytes 36868
  75.0 203.4 %copy-start.70 = (f32[2,512]{1,0:T(2,128)}, f32[2,512]{1,0:T(2,128)S(1)}, u32[]{:S(2)}) copy-start(f32[2,512]{1,0:T(2,128)S(1)} %get-tuple-element.2184) | copy-start | bytes 12292
  75.0 203.4 %copy-start.72 = (f32[2,512]{1,0:T(2,128)}, f32[2,512]{1,0:T(2,128)S(1)}, u32[]{:S(2)}) copy-start(f32[2,512]{1,0:T(2,128)S(1)} %get-tuple-element.2185) | copy-start | bytes 12292
  75.0 203.4 %copy-start.74 = (f32[2,512]{1,0:T(2,128)}, f32[2,512]{1,0:T(2,128)S(1)}, u32[]{:S(2)}) copy-start(f32[2,512]{1,0:T(2,128)S(1)} %get-tuple-element.2186) | copy-start | bytes 12292
  75.0 203.4 %copy-start.76 = (f32[2,512]{1,0:T(2,128)}, f32[2,512]{1,0:T(2,128)S(1)}, u32[]{:S(2)}) copy-start(f32[2,512]{1,0:T(2,128)S(1)} %get-tuple-element.2187) | copy-start | bytes 12292
  245.7 10.6 copy-start.14
  267.6 5.6 collective-permute-start
  278.3 16.0 copy-start.5
  311.0 9.9 copy-start.48
  544.7 36.0 %copy-start.2 = (f32[2,8,128,256]{3,2,1,0:T(8,128)}, f32[2,8,128,256]{3,2,1,0:T(8,128)S(1)}, u32[]{:S(2)}) copy-start(f32[2,8,128,256]{3,2,1,0:T(8,128)S(1)} %get-tuple-element.1472) | copy-start | bytes 6291460
  544.7 36.0 %copy-start.37 = (f32[8,2,8,64]{3,2,1,0:T(8,128)}, f32[8,2,8,64]{3,2,1,0:T(8,128)S(1)}, u32[]{:S(2)}) copy-start(f32[8,2,8,64]{3,2,1,0:T(8,128)S(1)} %get-tuple-element.3156) | copy-start | bytes 98308
  544.7 36.0 %copy-start.60 = (s32[8,2,1,64]{3,1,2,0:T(2,128)}, s32[8,2,1,64]{3,1,2,0:T(2,128)S(1)}, u32[]{:S(2)}) copy-start(s32[8,2,1,64]{3,1,2,0:T(2,128)S(1)} %get-tuple-element.3169) | copy-start | bytes 12292
  544.7 36.0 %copy-start.89 = (s32[8]{0:T(128)}, s32[8]{0:T(128)S(1)}, u32[]{:S(2)}) copy-start(s32[8]{0:T(128)S(1)} %get-tuple-element.3182) | copy-start | bytes 100
  544.8 13.1 collective-permute-start.1
  558.6 12.1 collective-permute-start.2
  571.4 12.0 collective-permute-start.3
  600.8 183.1 %all-gather.18.cloned.1.call-start = ((), (), s32[]{:S(2)}) async-start(), calls=%async_computation.14 | async-start | bytes 12255232 | tf_op jit(solution)/shard_map/all_gather | solution.py:181
  603.1 324.8 %all-gather.16.cloned.1.call-start = ((), (), s32[]{:S(2)}) async-start(), calls=%async_computation.13 | async-start | bytes 12255232 | tf_op jit(solution)/shard_map/all_gather | solution.py:180
  604.1 508.2 %all-gather.20.cloned.1.call-start = ((), (), s32[]{:S(2)}) async-start(), calls=%async_computation.15 | async-start | bytes 12255232 | tf_op jit(solution)/shard_map/all_gather | solution.py:182
  605.7 36.4 %copy-start.63 = (f32[2048]{0:T(1024)S(1)}, f32[2048]{0:T(1024)}, u32[]{:S(2)}) copy-start(f32[2048]{0:T(1024)} %param.35) | copy-start | bytes 24580
  605.7 596.4 %all-reduce.22.cloned.1.call-start = ((), (), s32[]{:S(2)}) async-start(), calls=%async_computation.16 | async-start | bytes 8388608 | tf_op jit(solution)/shard_map/psum | solution.py:145
  1138.5 19.1 copy-start.91
  1175.3 1482.7 %reduce-scatter.25.cloned.1.call-start = ((), (), s32[]{:S(2)}) async-start(), calls=%async_computation.22 | async-start | bytes 557056
  1238.5 352.8 %collective-permute-start.4 = (bf16[2,8,128,128]{3,2,1,0:T(8,128)(2,1)}, bf16[2,8,128,128]{3,2,1,0:T(8,128)(2,1)}, u32[]{:S(2)}, u32[]{:S(2)}) collective-permute-start(bf16[2,8,128,128]{3,2,1,0:T(8,128)(2,1)} %get-tuple-element.2190), channel_id=1, source_target_pairs={{8,0},{16,8},{24,16},{9,1},{17,9},{25,17},{10,2},{18,10},{26,18},{... | collective-permute-start | bytes 1572872 | tf_op jit(solution)/shard_map/ppermute | solution.py:17
  1593.7 19.5 collective-permute-start.5
  1595.0 18.2 copy-start.3
  1595.0 20.5 copy-start.13
  1595.0 20.5 copy-start.28
  1614.1 17.3 collective-permute-start.6
  1641.7 672.0 %copy-start.41 = (f32[1024,8]{0,1:T(8,128)S(1)}, f32[1024,8]{0,1:T(8,128)}, u32[]{:S(2)}) copy-start(f32[1024,8]{0,1:T(8,128)} %copy-done.40) | copy-start | bytes 98308
  2318.2 341.2 %reduce-scatter.27.cloned.1.call-start = ((), (), s32[]{:S(2)}) async-start(), calls=%async_computation.23 | async-start | bytes 4456448
  2334.3 327.1 %all-reduce.24.cloned.1.call-start = ((), (), s32[]{:S(2)}) async-start(), calls=%async_computation.25 | async-start | bytes 16777216 | tf_op jit(solution)/shard_map/psum | solution.py:145
  2347.0 12.5 copy-start.15
  2347.0 12.5 copy-start.16
  2347.0 12.5 copy-start.71
  2347.0 12.5 copy-start.73
  2347.0 12.5 copy-start.75
  2347.0 12.5 copy-start.77
  2359.5 29.2 copy-start.53
  2359.5 29.2 copy-start.55
  2359.5 29.2 copy-start.57
  2359.5 29.2 copy-start.59
  2408.0 26.3 collective-permute-start.7
  2464.4 203.5 %reduce-scatter.15.cloned.1.call-start = ((), (), s32[]{:S(2)}) async-start(), calls=%async_computation.17 | async-start | bytes 4456448 | tf_op jit(solution)/shard_map/reduce_scatter | solution.py:304
  2474.2 259.8 %reduce-scatter.17.cloned.1.call-start = ((), (), s32[]{:S(2)}) async-start(), calls=%async_computation.18 | async-start | bytes 4456448 | tf_op jit(solution)/shard_map/reduce_scatter | solution.py:307
  2483.7 347.1 %reduce-scatter.19.cloned.1.call-start = ((), (), s32[]{:S(2)}) async-start(), calls=%async_computation.19 | async-start | bytes 4456448 | tf_op jit(solution)/shard_map/reduce_scatter | solution.py:310
  2492.2 585.8 %reduce-scatter.29.cloned.1.call-start = ((), (), s32[]{:S(2)}) async-start(), calls=%async_computation.24 | async-start | bytes 12255232
  2526.5 797.2 %reduce-scatter.23.cloned.1.call-start = ((), (), s32[]{:S(2)}) async-start(), calls=%async_computation.21 | async-start | bytes 12255232 | tf_op jit(solution)/shard_map/reduce_scatter | solution.py:322
  2545.7 1023.8 %reduce-scatter.21.cloned.1.call-start = ((), (), s32[]{:S(2)}) async-start(), calls=%async_computation.20 | async-start | bytes 12255232 | tf_op jit(solution)/shard_map/reduce_scatter | solution.py:319
  2832.6 46.5 %copy-start.62 = (f32[2048]{0:T(1024)S(1)}, f32[2048]{0:T(1024)}, u32[]{:S(2)}) copy-start(f32[2048]{0:T(1024)} %param.26) | copy-start | bytes 24580
  2832.6 46.5 %copy-start.65 = (f32[1,4,2,128]{3,1,2,0:T(4,128)S(1)}, f32[1,4,2,128]{3,1,2,0:T(4,128)}, u32[]{:S(2)}) copy-start(f32[1,4,2,128]{3,1,2,0:T(4,128)} %copy-done.64) | copy-start | bytes 12292
  (63 other events, 325.3 us)
Sparse Core Ops, SparseCore 0:
  11.4 78.8 all-gather.11
  93.6 74.3 all-gather.9
  171.3 74.3 all-gather.7
  248.9 88.8 all-gather.13
  600.9 36.0 all-reduce.19
  640.5 143.3 all-gather.17
  787.5 140.3 all-gather.15
  931.5 180.7 all-gather.19
  1175.4 26.6 all-reduce.21
  2318.3 78.6 reduce-scatter.24
  2399.4 92.7 reduce-scatter.26
  2495.4 37.1 all-reduce.23
  2535.0 101.6 reduce-scatter.14
  2638.9 95.0 reduce-scatter.16
  2736.3 94.5 reduce-scatter.18
  2833.1 244.7 reduce-scatter.28
  3080.2 243.4 reduce-scatter.22
  3326.0 243.4 reduce-scatter.20
where the time goes:
time: 3600 us; the launch traced here: 3580 us
  waiting for transfers between devices  1490 us (41%)
  matrix products  1370 us (38%)
  other arithmetic  300 us (8%)
  local copies, waits for them, and re-layouts  175 us (5%)
  blocking collectives  172 us (5%)
    dot_general x160, matrix products, invert_unit_lower(): power = jnp.matmul(power, power, precision=HIGHEST)  263 us
    dot_general x160, matrix products, invert_unit_lower(): result = jnp.matmul(result, identity + power, precision=HIGHEST)  253 us
    reduce_scatter x1, waiting for transfers between devices, local(): lax.psum_scatter(gate_grad.astype(jnp.bfloat16), ('ctx', 'fsdp'), scatter...  243 us
    reduce_scatter x1, waiting for transfers between devices, local(): lax.psum_scatter(up_grad.astype(jnp.bfloat16), ('ctx', 'fsdp'), scatter_d...  243 us
    unnamed x21, waiting for transfers between devices  182 us
    all_gather x1, waiting for transfers between devices, local(): lax.all_gather(down_weight.astype(jnp.bfloat16), ('ctx', 'fsdp'), axis=1,...  166 us
    all_gather x1, waiting for transfers between devices, local(): lax.all_gather(up_weight.astype(jnp.bfloat16), ('ctx', 'fsdp'), axis=0, t...  135 us
    all_gather x1, waiting for transfers between devices, local(): lax.all_gather(gate_weight.astype(jnp.bfloat16), ('ctx', 'fsdp'), axis=0,...  125 us
  transfers between devices with their start and end apart: 26, of which 18 were waited for; matrix products, arithmetic and copies ran while one was open for 29% of the time, Pallas kernels for 0%

commit v1 on v0

v1 whole, which is shorter than its diff:
```python
import functools
import jax
import jax.numpy as jnp
from jax import lax
from jax.experimental import pallas as pl
from jax.experimental.pallas import tpu as pltpu
from jax.sharding import PartitionSpec as P

LANES = 128
CHUNK = 128
HALO = 8
EPSILON = 1e-06
HEAD_FLOOR = 0.01
VMEM_BYTES = 60 * 1024 * 1024


def low(value):
    return value.astype(jnp.bfloat16)


def mul_nn(left, right):
    return lax.dot_general(low(left), low(right), (((1,), (0,)), ((), ())), preferred_element_type=jnp.float32)


def mul_nt(left, right):
    return lax.dot_general(low(left), low(right), (((1,), (1,)), ((), ())), preferred_element_type=jnp.float32)


def mul_tn(left, right):
    return lax.dot_general(low(left), low(right), (((0,), (0,)), ((), ())), preferred_element_type=jnp.float32)


def iota(shape, axis):
    return lax.broadcasted_iota(jnp.int32, shape, axis)


def chunk_masks(col, row, first):
    size = col.shape[0]
    same = col == row
    order, other = iota((size, size), 0), iota((size, size), 1)
    upto = same & (order >= other)
    below = same & (order > other)
    carried = (col < first).astype(jnp.float32)
    last = (col == row[:, size - 1 :]).astype(jnp.float32)
    keep = (row[:, size - 1 :] < first).astype(jnp.float32)
    return upto, below, carried, last, keep


def invert_units(systems):
    size = systems[0].shape[0]
    order, other = iota((size, size), 0), iota((size, size), 1)
    identity = (order == other).astype(jnp.float32)
    span = 1
    found = None
    while span < size:
        pair = (order // (2 * span) == other // (2 * span)) & (order // span != other // span)
        parts = [jnp.where(pair, system, 0.0) for system in systems]
        if found is None:
            found = [identity - part for part in parts]
        else:
            right = [mul_nn(part, value) for part, value in zip(parts, found)]
            found = [value - mul_nn(value, part) for value, part in zip(found, right)]
        span *= 2
    return found


def conv_rows(ext, conv, col, offset, size, lane, taps):
    total = None
    moved = []
    position = iota((size, 1), 0) + offset
    for tap in range(taps):
        back = taps - 1 - tap
        values = ext[pl.ds(HALO + offset - back, size), lane : lane + LANES]
        values = jnp.where(position - back >= col, values, 0.0)
        moved.append(values)
        term = conv[tap : tap + 1, lane : lane + LANES] * values
        total = term if total is None else total + term
    return total, moved


def unit(values):
    return values * lax.rsqrt(jnp.sum(values * values, axis=-1, keepdims=True) + EPSILON)


def head_column(values, head):
    return jnp.sum(jnp.where(iota(values.shape, 1) == head, values, 0.0), axis=-1, keepdims=True)


def forward_kernel(taps, heads, pre, beta, bias, halo, conv, col_ref, row_ref, own, carry, final, inv, upd, states, ext):
    length = pre.shape[0]
    ext[:HALO] = halo[0]
    ext[HALO:] = pre[...]
    head = pl.program_id(1) * heads
    jobs = [(i, j) for j in range(length // CHUNK) for i in range(heads)]
    data = {}
    for j in range(length // CHUNK):
        rows = pl.ds(j * CHUNK, CHUNK)
        col, row = col_ref[0, rows], row_ref[0, :, rows]
        masks = chunk_masks(col, row, j * CHUNK)
        strengths = jax.nn.sigmoid(beta[rows] + bias[...])
        for i in range(heads):
            acts = []
            for kind in range(3):
                total, _ = conv_rows(ext, conv, col, j * CHUNK, CHUNK, (3 * i + kind) * LANES, taps)
                acts.append(total * jax.nn.sigmoid(total))
            query, key, value = unit(acts[0]), unit(acts[1]), acts[2]
            strength = head_column(strengths, head + i)
            grams = mul_nt(jnp.concatenate([low(key), low(query)], axis=0), key)
            system = jnp.where(masks[1], strength * grams[:CHUNK], 0.0)
            scores = low(jnp.where(masks[0], grams[CHUNK:], 0.0))
            data[i, j] = (low(query), low(key), value, strength, scores, masks, system)
    inverses = dict(zip(jobs, invert_units([data[job][6] for job in jobs])))
    for i in range(heads):
        state = jnp.concatenate(
            [
                jnp.zeros((LANES, LANES), jnp.float32),
                (iota((LANES, LANES), 0) == iota((LANES, LANES), 1)).astype(jnp.float32),
            ],
            axis=1,
        )
        final[0, i] = state
    for j in range(length // CHUNK):
        rows = pl.ds(j * CHUNK, CHUNK)
        for i in range(heads):
            query, key, value, strength, scores, masks, _ = data[i, j]
            _, _, carried, last, keep = masks
            inverse = low(inverses[i, j])
            state = final[0, i]
            state_low = low(state)
            read = mul_nn(jnp.concatenate([key, query], axis=0), state_low)
            wide = jnp.concatenate([value, jnp.zeros_like(value)], axis=1)
            targets = strength * (wide - carried * read[:CHUNK])
            update = low(mul_nn(inverse, targets))
            result = carried * read[CHUNK:] + mul_nn(scores, update)
            final[0, i] = keep * state + mul_tn(key * low(last), update)
            lanes = slice(i * LANES, (i + 1) * LANES)
            own[rows, lanes] = result[:, :LANES]
            carry[rows, lanes] = low(result[:, LANES:])
            inv[0, i, j] = inverse
            upd[0, i, j] = update
            states[0, i, j] = state_low


def mixer_forward(pre, bias, halo, conv, col, row, taps, heads_here, group):
    seqs, length = col.shape[0], col.shape[1]
    steps = heads_here // group
    chunks = length // CHUNK
    wide = 3 * LANES * group
    rows = seqs * length

    def tile(*tail, kind):
        return jax.ShapeDtypeStruct((seqs, heads_here) + tail, kind)

    def spec(*tail):
        return pl.BlockSpec((1, group) + tail, lambda s, h: (s, h) + (0,) * len(tail))

    flat = pl.BlockSpec((length, LANES * group), lambda s, h: (s, h))
    last = 3 * heads_here
    return pl.pallas_call(
        functools.partial(forward_kernel, taps, group),
        grid=(seqs, steps),
        in_specs=[
            pl.BlockSpec((length, wide), lambda s, h: (s, h)),
            pl.BlockSpec((length, LANES), lambda s, h: (s, last)),
            pl.BlockSpec((1, LANES), lambda s, h: (0, 0)),
            pl.BlockSpec((1, HALO, wide), lambda s, h: (s, 0, h)),
            pl.BlockSpec((conv.shape[0], wide), lambda s, h: (0, h)),
            pl.BlockSpec((1, length, 1), lambda s, h: (s, 0, 0)),
            pl.BlockSpec((1, 1, length), lambda s, h: (s, 0, 0)),
        ],
        out_specs=[
            flat,
            flat,
            spec(LANES, 2 * LANES),
            spec(chunks, CHUNK, CHUNK),
            spec(chunks, CHUNK, 2 * LANES),
            spec(chunks, LANES, 2 * LANES),
        ],
        out_shape=[
            jax.ShapeDtypeStruct((rows, heads_here * LANES), jnp.float32),
            jax.ShapeDtypeStruct((rows, heads_here * LANES), jnp.bfloat16),
            tile(LANES, 2 * LANES, kind=jnp.float32),
            tile(chunks, CHUNK, CHUNK, kind=jnp.bfloat16),
            tile(chunks, CHUNK, 2 * LANES, kind=jnp.bfloat16),
            tile(chunks, LANES, 2 * LANES, kind=jnp.bfloat16),
        ],
        scratch_shapes=[pltpu.VMEM((length + HALO, wide), jnp.float32)],
        compiler_params=pltpu.CompilerParams(vmem_limit_bytes=VMEM_BYTES),
        cost_estimate=pl.CostEstimate(
            flops=60 * rows * heads_here * CHUNK * LANES, bytes_accessed=40 * rows * heads_here * LANES, transcendentals=0
        ),
    )(pre, pre, bias, halo, conv, col, row)


def backward_kernel(
    taps, heads, pre, beta, bias, halo, conv, col_ref, row_ref, grad_ref, inv, upd, states, start, end,
    grad_pre, tail, before, conv_grad, bias_grad, ext, grad_ext, logits,
):
    length = pre.shape[0]
    step = pl.program_id(1)
    head = step * heads
    ext[:HALO] = halo[0]
    ext[HALO:] = pre[...]
    grad_ext[...] = jnp.zeros_like(grad_ext)

    @pl.when(step == 0)
    def _():
        logits[...] = jnp.zeros_like(logits)

    grad_states = [end[0, i] for i in range(heads)]
    entry = [low(start[0, i]) for i in range(heads)]
    tap_sums = {}
    for j in reversed(range(length // CHUNK)):
        offset = j * CHUNK
        rows = pl.ds(offset, CHUNK)
        col, row = col_ref[0, rows], row_ref[0, :, rows]
        upto, below, carried, last, keep = chunk_masks(col, row, offset)
        strengths = jax.nn.sigmoid(beta[rows] + bias[...])
        grad_logit = jnp.zeros((CHUNK, LANES), jnp.float32)
        for i in range(heads):
            raw, taps_in = [], []
            for kind in range(3):
                total, moved = conv_rows(ext, conv, col, offset, CHUNK, (3 * i + kind) * LANES, taps)
                raw.append(total)
                taps_in.append(moved)
            gates = [jax.nn.sigmoid(total) for total in raw]
            acts = [total * gate for total, gate in zip(raw, gates)]
            scales = [lax.rsqrt(jnp.sum(act * act, axis=-1, keepdims=True) + EPSILON) for act in acts[:2]]
            query, key, value = acts[0] * scales[0], acts[1] * scales[1], acts[2]
            strength = head_column(strengths, head + i)
            lanes = slice(i * LANES, (i + 1) * LANES)
            query_low, key_low = low(query), low(key)
            grams = mul_nt(jnp.concatenate([key_low, query_low], axis=0), key_low)
            gram = jnp.where(below, grams[:CHUNK], 0.0)
            scores = jnp.where(upto, grams[CHUNK:], 0.0)
            inverse = inv[0, i, j]
            update = upd[0, i, j]
            update = low(update[:, :LANES].astype(jnp.float32) + mul_nn(update[:, LANES:], entry[i]))
            state = states[0, i, j]
            state = low(state[:, :LANES].astype(jnp.float32) + mul_nn(state[:, LANES:], entry[i]))
            grad_out = grad_ref[rows, lanes]
            grad_state = grad_states[i]
            grad_state_low = low(grad_state)
            key_last = key_low * low(last)
            grad_update = mul_tn(scores, grad_out) + mul_nn(key_last, grad_state_low)
            grad_target = mul_tn(inverse, grad_update)
            weighted = strength * grad_target
            passed = carried * weighted
            out_carried = carried * grad_out.astype(jnp.float32)
            query_carried = query_low * low(carried)
            grad_states[i] = (
                keep * grad_state + mul_tn(query_carried, grad_out) - mul_tn(key_low, passed)
            )
            grad_scores = jnp.where(upto, mul_nt(grad_out, update), 0.0)
            grad_system = jnp.where(below, mul_nt(grad_target, update), 0.0)
            remainder = value - carried * mul_nn(key_low, state)
            grad_strength = jnp.sum(grad_target * remainder - grad_system * gram, axis=-1, keepdims=True)
            scaled = strength * grad_system
            from_state = mul_nt(jnp.concatenate([low(out_carried), low(passed)], axis=0), state)
            from_keys = mul_nn(jnp.concatenate([low(grad_scores), low(scaled + scaled.T)], axis=0), key_low)
            grad_query = from_state[:CHUNK] + from_keys[:CHUNK]
            grad_key = (
                mul_tn(grad_scores, query_low)
                + last * mul_nt(update, grad_state_low)
                - from_state[CHUNK:]
                - from_keys[CHUNK:]
            )
            grad_logit = grad_logit + jnp.where(
                iota((CHUNK, LANES), 1) == head + i, grad_strength * strength * (1.0 - strength), 0.0
            )
            grads = [
                scales[0] * (grad_query - query * jnp.sum(grad_query * query, axis=-1, keepdims=True)),
                scales[1] * (grad_key - key * jnp.sum(grad_key * key, axis=-1, keepdims=True)),
                weighted,
            ]
            position = iota((CHUNK, 1), 0) + offset
            for kind in range(3):
                gate, total = gates[kind], raw[kind]
                grad_conv = grads[kind] * gate * (1.0 + total * (1.0 - gate))
                lane = (3 * i + kind) * LANES
                for tap in range(taps):
                    back = taps - 1 - tap
                    part = jnp.sum(grad_conv * taps_in[kind][tap], axis=0, keepdims=True)
                    spot = (i, kind, tap)
                    tap_sums[spot] = part if spot not in tap_sums else tap_sums[spot] + part
                    back_part = jnp.where(
                        position - back >= col, grad_conv * conv[tap : tap + 1, lane : lane + LANES], 0.0
                    )
                    where = pl.ds(HALO + offset - back, CHUNK)
                    grad_ext[where, lane : lane + LANES] += back_part
        logits[rows] += grad_logit
    wide = 3 * LANES * heads
    place = pl.multiple_of(step * wide, LANES)
    grad_pre[:, pl.ds(place, wide)] = low(grad_ext[HALO:])
    before[0] = grad_ext[:HALO]
    tail[0] = grad_ext[length:]
    for i in range(heads):
        for kind in range(3):
            lane = (3 * i + kind) * LANES
            for tap in range(taps):
                conv_grad[0, tap : tap + 1, lane : lane + LANES] = tap_sums[i, kind, tap]

    @pl.when(step == pl.num_programs(1) - 1)
    def _():
        total = logits[...]
        grad_pre[:, grad_pre.shape[1] - LANES :] = low(total)
        bias_grad[0] = jnp.sum(total, axis=0, keepdims=True)


def mixer_backward(pre, bias, halo, conv, col, row, grad_mixed, inv, upd, states, start, end, taps, heads_here, group):
    seqs, length = col.shape[0], col.shape[1]
    steps = heads_here // group
    chunks = length // CHUNK
    wide = 3 * LANES * group
    rows = seqs * length
    total = pre.shape[1]

    def spec(*tail):
        return pl.BlockSpec((1, group) + tail, lambda s, h: (s, h) + (0,) * len(tail))

    last = 3 * heads_here
    part = pl.BlockSpec((1, HALO, wide), lambda s, h: (s, 0, h))
    edge = jax.ShapeDtypeStruct((seqs, HALO, 3 * LANES * heads_here), jnp.float32)
    return pl.pallas_call(
        functools.partial(backward_kernel, taps, group),
        grid=(seqs, steps),
        in_specs=[
            pl.BlockSpec((length, wide), lambda s, h: (s, h)),
            pl.BlockSpec((length, LANES), lambda s, h: (s, last)),
            pl.BlockSpec((1, LANES), lambda s, h: (0, 0)),
            part,
            pl.BlockSpec((conv.shape[0], wide), lambda s, h: (0, h)),
            pl.BlockSpec((1, length, 1), lambda s, h: (s, 0, 0)),
            pl.BlockSpec((1, 1, length), lambda s, h: (s, 0, 0)),
            pl.BlockSpec((length, LANES * group), lambda s, h: (s, h)),
            spec(chunks, CHUNK, CHUNK),
            spec(chunks, CHUNK, 2 * LANES),
            spec(chunks, LANES, 2 * LANES),
            spec(LANES, LANES),
            spec(LANES, LANES),
        ],
        out_specs=[
            pl.BlockSpec((length, total), lambda s, h: (s, 0)),
            part,
            part,
            part,
            pl.BlockSpec((1, 1, LANES), lambda s, h: (s, 0, 0)),
        ],
        out_shape=[
            jax.ShapeDtypeStruct((rows, total), jnp.bfloat16),
            edge,
            edge,
            edge,
            jax.ShapeDtypeStruct((seqs, 1, LANES), jnp.float32),
        ],
        scratch_shapes=[
            pltpu.VMEM((length + HALO, wide), jnp.float32),
            pltpu.VMEM((length + HALO, wide), jnp.float32),
            pltpu.VMEM((length, LANES), jnp.float32),
        ],
        compiler_params=pltpu.CompilerParams(vmem_limit_bytes=VMEM_BYTES),
        cost_estimate=pl.CostEstimate(
            flops=60 * rows * heads_here * CHUNK * LANES, bytes_accessed=40 * rows * heads_here * LANES, transcendentals=0
        ),
    )(pre, pre, bias, halo, conv, col, row, grad_mixed, inv, upd, states, start, end)


def mixed_rows_of(own, carry, start):
    return own + mul_nn(carry, start)


def output_kernel(heads, own, carry, start, gain, out):
    for i in range(heads):
        lanes = slice(i * LANES, (i + 1) * LANES)
        mixed = mixed_rows_of(own[:, lanes], carry[:, lanes], start[0, i])
        scale = lax.rsqrt(jnp.mean(mixed * mixed, axis=-1, keepdims=True) + HEAD_FLOOR)
        out[:, lanes] = low(mixed * scale * gain[...])


def output_backward_kernel(heads, own, carry, start, gain, grad, out, across, gain_grad):
    total = jnp.zeros((1, LANES), jnp.float32)
    for i in range(heads):
        lanes = slice(i * LANES, (i + 1) * LANES)
        carried = carry[:, lanes]
        mixed = mixed_rows_of(own[:, lanes], carried, start[0, i])
        scale = lax.rsqrt(jnp.mean(mixed * mixed, axis=-1, keepdims=True) + HEAD_FLOOR)
        normed = mixed * scale
        upper = grad[:, lanes].astype(jnp.float32)
        total = total + jnp.sum(upper * normed, axis=0, keepdims=True)
        weighted = upper * gain[...]
        back = scale * (weighted - normed * jnp.mean(weighted * normed, axis=-1, keepdims=True))
        out[:, lanes] = low(back)
        across[0, i] = mul_tn(carried, back)
    gain_grad[0, 0] = total


def mixer_output(own, carry, start, gain, group):
    seqs, heads_here = start.shape[:2]
    rows = own.shape[0]
    length = rows // seqs
    flat = pl.BlockSpec((length, LANES * group), lambda s, h: (s, h))
    square = pl.BlockSpec((1, group, LANES, LANES), lambda s, h: (s, h, 0, 0))
    return pl.pallas_call(
        functools.partial(output_kernel, group),
        grid=(seqs, heads_here // group),
        in_specs=[flat, flat, square, pl.BlockSpec((1, LANES), lambda s, h: (0, 0))],
        out_specs=flat,
        out_shape=jax.ShapeDtypeStruct(own.shape, jnp.bfloat16),
        compiler_params=pltpu.CompilerParams(vmem_limit_bytes=VMEM_BYTES),
        cost_estimate=pl.CostEstimate(
            flops=2 * own.size * LANES, bytes_accessed=8 * own.size, transcendentals=0
        ),
    )(own, carry, start, gain)


def mixer_output_backward(own, carry, start, gain, grad, group):
    seqs, heads_here = start.shape[:2]
    rows = own.shape[0]
    length = rows // seqs
    steps = heads_here // group
    flat = pl.BlockSpec((length, LANES * group), lambda s, h: (s, h))
    square = pl.BlockSpec((1, group, LANES, LANES), lambda s, h: (s, h, 0, 0))
    return pl.pallas_call(
        functools.partial(output_backward_kernel, group),
        grid=(seqs, steps),
        in_specs=[flat, flat, square, pl.BlockSpec((1, LANES), lambda s, h: (0, 0)), flat],
        out_specs=[flat, square, pl.BlockSpec((1, 1, 1, LANES), lambda s, h: (s, h, 0, 0))],
        out_shape=[
            jax.ShapeDtypeStruct(own.shape, jnp.bfloat16),
            jax.ShapeDtypeStruct(start.shape, jnp.float32),
            jax.ShapeDtypeStruct((seqs, steps, 1, LANES), jnp.float32),
        ],
        compiler_params=pltpu.CompilerParams(vmem_limit_bytes=VMEM_BYTES),
        cost_estimate=pl.CostEstimate(
            flops=4 * own.size * LANES, bytes_accessed=12 * own.size, transcendentals=0
        ),
    )(own, carry, start, gain, grad)


def flip(value, axis, bit):
    devices = range(lax.axis_size(axis))
    return lax.ppermute(value, axis, [(i, i ^ bit) for i in devices])


def shift(value, axis, distance):
    count = lax.axis_size(axis)
    return lax.ppermute(value, axis, [(i, (i + distance) % count) for i in range(count)])


def put(buffer, piece, index):
    start = (index,) + (0,) * piece.ndim
    return lax.dynamic_update_slice(buffer, piece[None], start)


def after(value, *earlier):
    return lax.optimization_barrier((value,) + earlier)[0]


def gather_line(shard):
    count, place = lax.axis_size("fsdp"), lax.axis_index("fsdp")
    buffer = put(jnp.zeros((count,) + shard.shape, shard.dtype), shard, place)
    for distance in range(1, count):
        buffer = put(buffer, shift(shard, "fsdp", distance), (place - distance) % count)
    return buffer.reshape(count * shard.shape[0], shard.shape[1])


def gather_square(piece):
    place = lax.axis_index("ctx")
    half = piece.shape[0] // 2
    beside = flip(piece, "ctx", 1)
    across = flip(piece, "ctx", 2)
    upper = flip(beside[:half], "ctx", 2)
    lower = flip(across[half:], "ctx", 1)
    buffer = put(jnp.zeros((4,) + piece.shape, piece.dtype), piece, place)
    buffer = put(buffer, beside, place ^ 1)
    buffer = put(buffer, across, place ^ 2)
    buffer = put(buffer, jnp.concatenate([upper, lower], axis=0), place ^ 3)
    return buffer.reshape(4 * piece.shape[0], piece.shape[1])


def gather_groups(shards):
    if lax.axis_size("ctx") != 4:
        return [lax.all_gather(shard, ("ctx", "fsdp"), axis=0, tiled=True) for shard in shards]
    full = []
    line = None
    for shard in shards:
        line = gather_line(shard if line is None else after(shard, line))
        full.append(gather_square(line if not full else after(line, full[-1])))
    return full


def relative_columns(rows):
    width = rows.shape[1] // 4
    part = width // lax.axis_size("fsdp")
    place, line = lax.axis_index("ctx"), lax.axis_index("fsdp")
    blocks = []
    for bit in range(4):
        block = lax.dynamic_slice_in_dim(rows, (place ^ bit) * width, width, 1)
        twice = jnp.concatenate([block, block], axis=1)
        blocks.append(lax.dynamic_slice_in_dim(twice, line * part, width, 1))
    return blocks


def outer_scatter(rows, grads, blocks=None):
    if lax.axis_size("ctx") != 4:
        return lax.psum_scatter(
            outer_rows(rows, grads).astype(jnp.bfloat16), ("ctx", "fsdp"), scatter_dimension=0, tiled=True
        ).astype(jnp.float32)
    if blocks is None:
        blocks = relative_columns(rows)
    half = blocks[0].shape[1] // 2
    low = jnp.bfloat16

    def halves(bit):
        block = blocks[bit]
        return outer_rows(block[:, :half], grads), outer_rows(block[:, half:], grads)

    diag_up, diag_down = halves(3)
    from_across = flip(diag_up.astype(low), "ctx", 2)
    from_beside = flip(diag_down.astype(low), "ctx", 1)
    beside_up, beside_down = halves(1)
    across_up, across_down = halves(2)
    beside_down = flip(beside_down.astype(low), "ctx", 1)
    across_up = flip(across_up.astype(low), "ctx", 2)
    beside_up = flip((beside_up + from_across).astype(low), "ctx", 1)
    across_down = flip((across_down + from_beside).astype(low), "ctx", 2)
    own_up, own_down = halves(0)
    own_up = own_up + beside_up + across_up
    own_down = own_down + beside_down + across_down
    count = lax.axis_size("fsdp")
    part = 2 * half // count
    own = jnp.concatenate([own_up, own_down], axis=0)
    total = own[:part]
    for distance in range(1, count):
        piece = own[distance * part : (distance + 1) * part].astype(low)
        total = total + shift(piece, "fsdp", distance)
    return total


def butterfly(value, axes):
    for axis in axes:
        count, bit = lax.axis_size(axis), 1
        while bit < count:
            value = value + flip(value, axis, bit)
            bit *= 2
    return value


def from_behind(block, axis, distance):
    devices = range(lax.axis_size(axis))
    route = [(i - distance, i) for i in devices if i - distance in devices]
    return lax.ppermute(block, axis, route)


def rms_scale(values, floor_value):
    return lax.rsqrt(jnp.mean(values * values, axis=-1, keepdims=True) + floor_value)


def norm_backward(grad_normed, inputs, scale, gain):
    normed = inputs * scale
    weighted = grad_normed * gain
    return (
        scale * (weighted - normed * jnp.mean(weighted * normed, axis=-1, keepdims=True)),
        normed,
    )


def times(left, right):
    return jnp.dot(left, right, preferred_element_type=jnp.float32)


def times_transposed(left, right):
    return lax.dot_general(
        left, right, (((1,), (1,)), ((), ())), preferred_element_type=jnp.float32
    )


def outer_rows(left, right):
    return lax.dot_general(
        left, right, (((0,), (0,)), ((), ())), preferred_element_type=jnp.float32
    )


def heads_combine(partial_value):
    part = low(partial_value)
    if lax.axis_size("tp") != 2:
        return lax.psum(part, "tp").astype(jnp.float32)
    return part.astype(jnp.float32) + flip(part, "tp", 1).astype(jnp.float32)


def rows_own(held):
    count = held.shape[0] // lax.axis_size("tp")
    return lax.dynamic_slice_in_dim(held, lax.axis_index("tp") * count, count, 0)


def by_head(parts):
    lead = parts[0].shape[:-1]
    split = [part.reshape(lead + (-1, LANES)) for part in parts]
    return jnp.stack(split, axis=-2).reshape(lead + (-1,))


def by_kind(joined):
    lead = joined.shape[:-1]
    split = joined.reshape(lead + (-1, 3, LANES))
    return [split[..., kind, :].reshape(lead + (-1,)) for kind in range(3)]


def local(
    block_input,
    doc_start,
    gain_mix,
    query_weight,
    key_weight,
    value_weight,
    beta_weight,
    beta_bias,
    conv_weight,
    gain_o,
    out_weight,
    gain_ffn,
    gate_weight,
    up_weight,
    down_weight,
    out_grad,
):
    seq_count, local_len, width = block_input.shape
    row_count = seq_count * local_len
    heads_here = beta_weight.shape[1]
    taps = conv_weight.shape[1]
    group = 2 if heads_here % 2 == 0 else 1
    hidden_cols = gate_weight.shape[1]
    head_cols = 3 * heads_here * LANES
    spare = LANES - heads_here
    mix_full, out_full, ffn_full, down_full = gather_groups(
        [
            jnp.concatenate(
                [
                    by_head([low(query_weight), low(key_weight), low(value_weight)]),
                    jnp.pad(low(beta_weight), ((0, 0), (0, spare))),
                ],
                axis=1,
            ),
            low(out_weight).T,
            jnp.concatenate([low(gate_weight), low(up_weight)], axis=1),
            low(down_weight).T,
        ]
    )
    first_pos = lax.axis_index("ctx") * local_len
    starts = doc_start - first_pos
    col, row = starts[:, :, None], starts[:, None, :]
    conv = by_head([conv_weight[0], conv_weight[1], conv_weight[2]])
    bias = jnp.pad(beta_bias, (0, spare))[None]
    gain_head = gain_o[None]

    inputs = block_input.astype(jnp.float32).reshape(row_count, width)
    scale_mix = rms_scale(inputs, EPSILON)
    normed_mix = low(inputs * scale_mix * gain_mix)
    pre = times(normed_mix, mix_full)
    ends = pre.reshape(seq_count, local_len, -1)[:, local_len - HALO :, :head_cols]
    halo = from_behind(ends, "ctx", 1)
    own, carry, final, inverses, updates, states = mixer_forward(
        pre, bias, halo, conv, col, row, taps, heads_here, group
    )
    transfer = low(final[..., LANES:])
    entered = jnp.zeros_like(final[..., :LANES])
    leaving = final[..., :LANES]
    for repeat in range(lax.axis_size("ctx") - 1):
        entered = from_behind(low(leaving), "ctx", 1)
        leaving = final[..., :LANES] + jnp.einsum(
            "shij,shjk->shik", transfer, entered, preferred_element_type=jnp.float32
        )
    entered = entered.astype(jnp.float32)
    mixed_rows = mixer_output(own, carry, entered, gain_head, group)
    residual = inputs + heads_combine(times_transposed(mixed_rows, out_full))
    scale_ffn = rms_scale(residual, EPSILON)
    normed_ffn = low(residual * scale_ffn * gain_ffn)

    both = times(normed_ffn, ffn_full)
    gate, up_val = both[:, :hidden_cols], both[:, hidden_cols:]
    sigmoid_gate = jax.nn.sigmoid(gate)
    activated = gate * sigmoid_gate
    hidden = low(activated * up_val)
    grad_rows = out_grad.reshape(row_count, width)
    grad_hidden = times(grad_rows, down_full)
    grad_gate = low(grad_hidden * up_val * sigmoid_gate * (1.0 + gate * (1.0 - sigmoid_gate)))
    grad_up = low(grad_hidden * activated)
    grad_both = jnp.concatenate([grad_gate, grad_up], axis=1)
    grad_normed = heads_combine(times_transposed(grad_both, ffn_full))
    output_held = low(residual + heads_combine(times_transposed(hidden, down_full)))
    down_grad = outer_scatter(grad_rows, hidden).T
    both_grad = outer_scatter(normed_ffn, grad_both)
    gate_grad, up_grad = both_grad[:, :hidden_cols], both_grad[:, hidden_cols:]

    back_ffn, unit_ffn = norm_backward(grad_normed, residual, scale_ffn, gain_ffn)
    grad_residual = grad_rows.astype(jnp.float32) + back_ffn
    gain_ffn_part = jnp.sum(rows_own(grad_normed * unit_ffn), axis=0)
    grad_branch = low(grad_residual)
    out_grad_w = outer_scatter(grad_branch, mixed_rows).T
    grad_heads = times(grad_branch, out_full)
    grad_mixed, across, gain_o_part = mixer_output_backward(
        own, carry, entered, gain_head, grad_heads, group
    )
    grad_end = jnp.zeros_like(across)
    grad_now = across
    for repeat in range(lax.axis_size("ctx") - 1):
        grad_end = from_behind(low(grad_now), "ctx", -1)
        grad_now = across + jnp.einsum(
            "shji,shjk->shik", transfer, grad_end, preferred_element_type=jnp.float32
        )
    grad_end = grad_end.astype(jnp.float32)
    grad_mix, tail, before, conv_part, bias_part = mixer_backward(
        pre, bias, halo, conv, col, row, grad_mixed, inverses, updates, states, entered, grad_end,
        taps, heads_here, group,
    )
    tail = low(tail + from_behind(before, "ctx", -1))
    grad_mix = lax.dynamic_update_slice(
        grad_mix.reshape(seq_count, local_len, -1), tail, (0, local_len - HALO, 0)
    ).reshape(row_count, -1)
    mix_back = heads_combine(times_transposed(grad_mix, mix_full))
    mix_grad = outer_scatter(normed_mix, grad_mix)
    query_grad, key_grad, value_grad = by_kind(mix_grad[:, :head_cols])
    beta_grad = mix_grad[:, head_cols : head_cols + heads_here]
    back_mix, unit_mix = norm_backward(mix_back, inputs, scale_mix, gain_mix)
    input_held = low(grad_residual + back_mix)
    gain_mix_part = jnp.sum(rows_own(mix_back * unit_mix), axis=0)

    small = butterfly(
        jnp.concatenate([gain_mix_part, gain_ffn_part, jnp.sum(gain_o_part, axis=(0, 1, 2))]),
        ("tp", "ctx", "fsdp"),
    )
    gain_mix_grad, gain_ffn_grad, gain_o_grad = jnp.split(small, [width, 2 * width])
    conv_grad = butterfly(jnp.sum(conv_part, axis=0)[:taps], ("ctx", "fsdp"))
    conv_grad = jnp.stack(by_kind(conv_grad))
    bias_grad = butterfly(jnp.sum(bias_part, axis=(0, 1))[:heads_here], ("ctx", "fsdp"))
    return (
        output_held.reshape(seq_count, local_len, width),
        input_held.reshape(seq_count, local_len, width),
        gain_mix_grad,
        query_grad,
        key_grad,
        value_grad,
        beta_grad,
        bias_grad,
        conv_grad,
        gain_o_grad,
        out_grad_w,
        gain_ffn_grad,
        gate_grad,
        up_grad,
        down_grad,
    )


def solution(mesh):
    placed = (
        P("fsdp", "ctx", None),
        P("fsdp", "ctx"),
        P(),
        P(("ctx", "fsdp"), "tp"),
        P(("ctx", "fsdp"), "tp"),
        P(("ctx", "fsdp"), "tp"),
        P(("ctx", "fsdp"), "tp"),
        P("tp"),
        P(None, None, "tp"),
        P(),
        P("tp", ("ctx", "fsdp")),
        P(),
        P(("ctx", "fsdp"), "tp"),
        P(("ctx", "fsdp"), "tp"),
        P("tp", ("ctx", "fsdp")),
        P("fsdp", "ctx", None),
    )
    return jax.shard_map(
        local,
        mesh=mesh,
        in_specs=placed,
        out_specs=(
            P("fsdp", "ctx", None),
            P("fsdp", "ctx", None),
            P(),
            P(("ctx", "fsdp"), "tp"),
            P(("ctx", "fsdp"), "tp"),
            P(("ctx", "fsdp"), "tp"),
            P(("ctx", "fsdp"), "tp"),
            P("tp"),
            P(None, None, "tp"),
            P(),
            P("tp", ("ctx", "fsdp")),
            P(),
            P(("ctx", "fsdp"), "tp"),
            P(("ctx", "fsdp"), "tp"),
            P("tp", ("ctx", "fsdp")),
        ),
        check_vma=False,
    )
```

time: 3600 us -> 1610 us (0.45)
  matrix products: 1370 us -> 288 us
  waiting for transfers between devices: 1490 us -> 689 us
  starting transfers between devices: 24.8 us -> 205 us
  other arithmetic: 300 us -> 124 us
  blocking collectives: 172 us -> 0 us
  Pallas kernels: 0 us -> 135 us
    dot_general x544 -> x8, matrix products: 1180 us -> 87.3 us  [the longest x4 85 us: times(): return jnp.dot(left, right, preferred_element_type=jnp.float32)]
    ppermute x0 -> x81, waiting for transfers between devices: none -> 648 us  [the longest x57 593 us: flip(): return lax.ppermute(value, axis, [(i, i ^ bit) for i in devices])]
    reduce_scatter x5 -> x0, waiting for transfers between devices: 646 us -> none  [the longest x1 243 us: local(): lax.psum_scatter(gate_grad.astype(jnp.bfloat16), ('ctx', 'fsdp'), scatter...]
    all_gather x7 -> x0, waiting for transfers between devices: 577 us -> none  [the longest x1 166 us: local(): lax.all_gather(down_weight.astype(jnp.bfloat16), ('ctx', 'fsdp'), axis=1,...]
    ppermute x0 -> x81, starting transfers between devices: none -> 182 us  [the longest x24 111 us: shift(): lax.ppermute(value, axis, [(i, (i + distance) % count) for i in range(cou...]
    unnamed x21 -> x0, waiting for transfers between devices: 182 us -> none
    pallas_call x0 -> x4, Pallas kernels: none -> 135 us  [the longest x1 64.7 us: mixer_backward(): pl.pallas_call(functools.partial(backward_kernel, taps, group), grid=(seq...]
    psum x2 -> x0, blocking collectives: 129 us -> none  [the longest x1 86.7 us: local(): conv_grad, bias_grad = lax.psum((conv_part, bias_part), ('ctx', 'fsdp'))]
  transfers between devices with their start and end apart: 26 -> 89, of which waited for: 18 -> 38; matrix products, arithmetic and copies ran while one was open for 29% -> 27% of each run, Pallas kernels for 0% -> 8%
where the time goes in v1:
time: 1610 us; the launch traced here: 1590 us
  waiting for transfers between devices  689 us (43%)
  matrix products  288 us (18%)
  starting transfers between devices  205 us (13%)
  local copies, waits for them, and re-layouts  148 us (9%)
  Pallas kernels  135 us (8%)
  other arithmetic  124 us (8%)
    ppermute x57, waiting for transfers between devices, flip(): return lax.ppermute(value, axis, [(i, i ^ bit) for i in devices])  593 us
    dot_general x32, matrix products, outer_rows(): lax.dot_general(left, right, (((0,), (0,)), ((), ())), preferred_element_...  124 us
    ppermute x24, starting transfers between devices, shift(): lax.ppermute(value, axis, [(i, (i + distance) % count) for i in range(cou...  111 us
    dot_general x4, matrix products, times(): return jnp.dot(left, right, preferred_element_type=jnp.float32)  85 us
    dot_general x4, matrix products, times_transposed(): lax.dot_general(left, right, (((1,), (1,)), ((), ())), preferred_element_...  77.1 us
    ppermute x57, starting transfers between devices, flip(): return lax.ppermute(value, axis, [(i, i ^ bit) for i in devices])  70.2 us
    pallas_call x1, Pallas kernels, mixer_backward(): pl.pallas_call(functools.partial(backward_kernel, taps, group), grid=(seq...  64.7 us
    dynamic_update_slice x28, local copies, waits for them, and re-layouts, put(): return lax.dynamic_update_slice(buffer, piece[None], start)  57.3 us
  transfers between devices with their start and end apart: 89, of which 38 were waited for; matrix products, arithmetic and copies ran while one was open for 27% of the time, Pallas kernels for 8%

profile of v1, /device:TPU:0, one launch (start us, length us, event | category | flops | bytes accessed | tf_op | source)
XLA Modules:
  0.0 1591.4 jit_solution(9668053356948708755)
XLA Ops:
  27.5 5.2 fusion.7
  45.9 19.3 %collective-permute-done.1 = bf16[128,3200]{0,1:T(8,128)(2,1)} collective-permute-done((bf16[128,3200]{0,1:T(8,128)(2,1)}, bf16[128,3200]{0,1:T(8,128)(2,1)}, u32[]{:S(2)}, u32[]{:S(2)}) %collective-permute-start.1) | collective-permute-done | bytes 819232 | tf_op jit(solution)/shard_map/ppermute | solution.py:447
  82.2 16.2 %collective-permute-start.11 = (bf16[128,1024]{1,0:T(8,128)(2,1)}, bf16[128,1024]{1,0:T(8,128)(2,1)S(1)}, u32[]{:S(2)}, u32[]{:S(2)}) collective-permute-start(bf16[128,1024]{1,0:T(8,128)(2,1)} %bitcast.163), channel_id=1, source_target_pairs={{0,1},{1,2},{2,3},{3,0},{4,5},{5,6},{6,7},{7,4},{8,9},{9,10},{10,1... | collective-permute-start | bytes 786440 | tf_op jit(solution)/shard_map/ppermute | solution.py:447
  101.8 5.6 broadcast_in_dim.137
  117.7 37.0 %collective-permute-start.19 = (bf16[128,5632]{1,0:T(8,128)(2,1)S(1)}, bf16[128,5632]{1,0:T(8,128)(2,1)}, u32[]{:S(2)}, u32[]{:S(2)}) collective-permute-start(bf16[128,5632]{1,0:T(8,128)(2,1)S(1)} %pad_maximum_fusion.1), channel_id=1, source_target_pairs={{0,1},{1,2},{2,3},{3,0},{4,5},{5,6},{6,7},{7,4},{8,9},{9,10},{10,1... | collective-permute-start | bytes 4325384 | tf_op jit(solution)/shard_map/ppermute | solution.py:447
  171.8 29.8 %collective-permute-done.5 = bf16[256,3200]{1,0:T(8,128)(2,1)S(1)} collective-permute-done((bf16[256,3200]{1,0:T(8,128)(2,1)S(1)}, bf16[256,3200]{1,0:T(8,128)(2,1)S(1)}, u32[]{:S(2)}, u32[]{:S(2)}) %collective-permute-start.5) | collective-permute-done | bytes 1638432 | tf_op jit(solution)/shard_map/ppermute | solution.py:442
  204.0 17.7 %fusion.119.pre.beta = f32[1024,3200]{1,0:T(8,128)S(1)} fusion(bf16[1024,2048]{1,0:T(8,128)(2,1)} %bitcast.254, bf16[2048,3200]{1,0:T(8,128)(2,1)S(1)} %bitcast.239), kind=kOutput, calls=%fused_computation.287 | convolution fusion | flops 13421772800 | bytes 30408704 | tf_op jit(solution)/shard_map/dot_general | solution.py:569
  232.6 52.4 %shard_map.271 = (f32[1024,1024]{1,0:T(8,128)}, bf16[1024,1024]{1,0:T(8,128)(2,1)}, f32[2,8,128,256]{3,2,1,0:T(8,128)}, bf16[2,8,4,128,128]{4,3,2,1,0:T(8,128)(2...) custom-call(f32[1024,3200]{1,0:T(8,128)} %copy-done.3, f32[1024,3200]{1,0:T(8,128)} %copy-done.3, ...), custom_call_target="tpu_custom_call" | custom-call | flops 8053063680 | bytes 41943040 | tf_op jit(solution)/shard_map/pallas_call | solution.py:159
  297.2 6.4 collective-permute-done.8
  303.9 5.3 collective-permute-start.9
  318.6 11.3 collective-permute-done.14
  330.7 6.6 collective-permute-done.9
  337.6 5.4 collective-permute-start.10
  345.1 6.0 collective-permute-done.16
  358.0 7.9 shard_map.272
  365.9 7.4 convolution_convert_fusion.15
  383.5 8.0 broadcast_in_dim.160
  391.4 5.7 bitcast_dynamic-update-slice_fusion.2
  399.2 5.8 multiply_convert_fusion.2
  412.5 91.2 %collective-permute-done.22 = bf16[512,5632]{1,0:T(8,128)(2,1)S(1)} collective-permute-done((bf16[512,5632]{1,0:T(8,128)(2,1)}, bf16[512,5632]{1,0:T(8,128)(2,1)S(1)}, u32[]{:S(2)}, u32[]{:S(2)}) %collective-permute-start.22) | collective-permute-done | bytes 5767200 | tf_op jit(solution)/shard_map/ppermute | solution.py:442
  512.8 5.5 bitcast_dynamic-update-slice_fusion
  518.3 51.2 %collective-permute-done.24 = bf16[256,5632]{1,0:T(8,128)(2,1)S(1)} collective-permute-done((bf16[256,5632]{1,0:T(8,128)(2,1)S(1)}, bf16[256,5632]{1,0:T(8,128)(2,1)S(1)}, u32[]{:S(2)}, u32[]{:S(2)}) %collective-permute-start.24) | collective-permute-done | bytes 2883616 | tf_op jit(solution)/shard_map/ppermute | solution.py:442
  577.4 34.4 %fusion.120 = f32[1024,5632]{1,0:T(8,128)} fusion(bf16[1024,2048]{1,0:T(8,128)(2,1)} %copy-done.8, bf16[2048,5632]{1,0:T(8,128)(2,1)} %bitcast.235), kind=kOutput, calls=%fused_computation.288 | convolution fusion | flops 23622320128 | bytes 50331648 | tf_op jit(solution)/shard_map/dot_general | solution.py:569
  618.6 19.8 %collective-permute-done.29 = bf16[512,2816]{1,0:T(8,128)(2,1)} collective-permute-done((bf16[512,2816]{1,0:T(8,128)(2,1)S(1)}, bf16[512,2816]{1,0:T(8,128)(2,1)}, u32[]{:S(2)}, u32[]{:S(2)}) %collective-permute-start.29) | collective-permute-done | bytes 2883616 | tf_op jit(solution)/shard_map/ppermute | solution.py:442
  650.1 20.4 %collective-permute-done.31 = bf16[256,2816]{1,0:T(8,128)(2,1)S(1)} collective-permute-done((bf16[256,2816]{1,0:T(8,128)(2,1)S(1)}, bf16[256,2816]{1,0:T(8,128)(2,1)S(1)}, u32[]{:S(2)}, u32[]{:S(2)}) %collective-permute-start.31) | collective-permute-done | bytes 1441824 | tf_op jit(solution)/shard_map/ppermute | solution.py:442
  674.3 24.8 %fusion.2 = (bf16[1024,2816]{1,0:T(8,128)(2,1)}, bf16[1024,2816]{1,0:T(8,128)(2,1)}, bf16[1024,2816]{1,0:T(8,128)(2,1)S(1)}) fusion(f32[1024,5632]{1,0:T(8,128)} %fusion.120, bf16[1024,2048]{1,0:T(8,128)(2,1)} %bitcast.234, bf16[2048,2816]{1,0:T(8,128)(2,1)} %bitcast.241), kind=kOutput, calls=%fused_computation.5 | convolution fusion | flops 11854413824 | bytes 56098816 | tf_op jit(solution)/shard_map/dot_general | solution.py:569
  710.5 7.3 convolution_convert_fusion
  717.9 7.1 convolution_convert_fusion.3
  725.0 31.6 %convolution_convert_fusion.13 = bf16[1024,2048]{1,0:T(8,128)(2,1)} fusion(bf16[2048,5632]{1,0:T(8,128)(2,1)} %bitcast.236, bf16[1024,2816]{1,0:T(8,128)(2,1)} %get-tuple-element.106, bf16[1024,2816]{1,0:T(8,128)(2,1)} %get-tuple-element.105), kind=kOutput, calls=%fused_computation.63 | convolution fusion | flops 23647485952 | bytes 38797312 | tf_op jit(solution)/shard_map/dot_general | solution.py:573
  756.5 18.4 %convolution_convert_fusion.14 = bf16[1024,2048]{1,0:T(8,128)(2,1)} fusion(bf16[1024,2816]{1,0:T(8,128)(2,1)} %copy-done, bf16[2048,2816]{1,0:T(8,128)(2,1)} %bitcast.242), kind=kOutput, calls=%fused_computation.64 | convolution fusion | flops 11813257216 | bytes 21495808 | tf_op jit(solution)/shard_map/dot_general | solution.py:573
  777.4 9.2 convolution_convert_fusion.1
  786.7 10.1 fusion.75
  805.3 9.1 convolution_convert_fusion.2
  823.6 47.8 %collective-permute-done.76 = bf16[256,5632]{1,0:T(8,128)(2,1)} collective-permute-done((bf16[256,5632]{1,0:T(8,128)(2,1)}, bf16[256,5632]{1,0:T(8,128)(2,1)}, u32[]{:S(2)}, u32[]{:S(2)}) %collective-permute-start.76) | collective-permute-done | bytes 2883616 | tf_op jit(solution)/shard_map/ppermute | solution.py:442
  872.8 10.0 add_convert_fusion.3
  882.9 19.5 %collective-permute-done.84 = bf16[256,2816]{1,0:T(8,128)(2,1)} collective-permute-done((bf16[256,2816]{1,0:T(8,128)(2,1)S(1)}, bf16[256,2816]{1,0:T(8,128)(2,1)}, u32[]{:S(2)}, u32[]{:S(2)}) %collective-permute-start.84) | collective-permute-done | bytes 1441824 | tf_op jit(solution)/shard_map/ppermute | solution.py:442
  905.4 84.6 %collective-permute-done.81 = bf16[256,2816]{1,0:T(8,128)(2,1)S(1)} collective-permute-done((bf16[256,2816]{1,0:T(8,128)(2,1)S(1)}, bf16[256,2816]{1,0:T(8,128)(2,1)S(1)}, u32[]{:S(2)}, u32[]{:S(2)}) %collective-permute-start.81) | collective-permute-done | bytes 1441824 | tf_op jit(solution)/shard_map/ppermute | solution.py:442
  994.0 9.9 add_convert_fusion.4
  1008.6 10.4 collective-permute-done.83
  1020.8 7.7 multiply_reduce_fusion.1
  1028.6 7.8 fusion.110
  1041.7 8.2 fusion.121.grad
  1054.8 10.2 shard_map.273
  1073.3 10.7 collective-permute-done.35
  1088.2 10.0 collective-permute-done.62
  1101.4 10.2 collective-permute-start.63
  1115.7 13.0 collective-permute-start.69
  1134.5 10.4 collective-permute-start.65
  1146.0 64.7 %shard_map.274 = (bf16[1024,3200]{1,0:T(8,128)(2,1)}, f32[2,8,3072]{2,1,0:T(8,128)}, f32[2,8,3072]{2,1,0:T(8,128)}, f32[2,8,3072]{2,1,0:T(8,128)}, f32[2,1,128]{2,1,0:T(1,128)}) custom-call(f32[1024,3200]{1,0:T(8,128)} %copy-done.3, f32[1024,3200]{1,0:T(8,128)} %copy-done.3, f32[1,128]{1,0:T(1,128)} %pad_bitcast_fusion.bias, f32[2,8,3072]{2,1,0:T(8,128)} %copy-done.38, ...), custom_call_target="tpu_custom_call" | custom-call | flops 8053063680 | bytes 41943040 | tf_op jit(solution)/shard_map/pallas_call | solution.py:324
  1215.7 13.9 collective-permute-done.38
  1234.1 19.8 %convolution_convert_fusion.12 = bf16[1024,2048]{1,0:T(8,128)(2,1)} fusion(bf16[1024,3200]{1,0:T(8,128)(2,1)} %bitcast.219, bf16[2048,3200]{1,0:T(8,128)(2,1)} %bitcast.240), kind=kOutput, calls=%fused_computation.62 | convolution fusion | flops 13423869952 | bytes 23855104 | tf_op jit(solution)/shard_map/dot_general | solution.py:573
  1253.9 22.1 %collective-permute-done.77 = bf16[256,5632]{1,0:T(8,128)(2,1)} collective-permute-done((bf16[256,5632]{1,0:T(8,128)(2,1)}, bf16[256,5632]{1,0:T(8,128)(2,1)}, u32[]{:S(2)}, u32[]{:S(2)}) %collective-permute-start.77) | collective-permute-done | bytes 2883616 | tf_op jit(solution)/shard_map/ppermute | solution.py:442
  1279.7 16.2 %collective-permute-done.58 = f32[4,3072]{1,0:T(4,128)S(1)} collective-permute-done((f32[4,3072]{1,0:T(4,128)S(1)}, f32[4,3072]{1,0:T(4,128)S(1)}, u32[]{:S(2)}, u32[]{:S(2)}) %collective-permute-start.58) | collective-permute-done | bytes 49184 | tf_op jit(solution)/shard_map/ppermute | solution.py:442
  1303.2 9.5 convert_add_fusion.2
  1318.2 12.8 collective-permute-done.60
  1342.7 23.0 %collective-permute-done.57 = f32[8]{0:T(128)S(1)} collective-permute-done((f32[8]{0:T(128)S(1)}, f32[8]{0:T(128)S(1)}, u32[]{:S(2)}, u32[]{:S(2)}) %collective-permute-start.57) | collective-permute-done | bytes 64 | tf_op jit(solution)/shard_map/ppermute | solution.py:442
  1369.2 8.4 convert_add_fusion
  1379.2 26.5 %convert_add_fusion.1 = (f32[1024,2048]{1,0:T(8,128)}, bf16[1024,2048]{1,0:T(8,128)(2,1)}, bf16[1024,2048]{1,0:T(8,128)(2,1)}, f32[1024,2048]{1,0:T(8,128)}, bf16[1024,2048]{1,0:T(8,128)(2,1)}) fusion(bf16[1024,2048]{1,0:T(8,128)(2,1)} %collective-permute-done.34, bf16[1024,2048]{1,0:T(8,128)(2,1)} %convolution_convert_fusion.13, ...), kind=kLoop, calls=%fused_computation.23 | loop fusion | flops 65011712 | bytes 79724544 | tf_op jit(solution)/shard_map/add | solution.py:588
  1425.3 26.9 %collective-permute-done.50 = bf16[256,3200]{1,0:T(8,128)(2,1)} collective-permute-done((bf16[256,3200]{1,0:T(8,128)(2,1)}, bf16[256,3200]{1,0:T(8,128)(2,1)}, u32[]{:S(2)}, u32[]{:S(2)}) %collective-permute-start.50) | collective-permute-done | bytes 1638432 | tf_op jit(solution)/shard_map/ppermute | solution.py:442
  1462.0 23.8 %collective-permute-done.41 = f32[4224]{0:T(1024)S(1)} collective-permute-done((f32[4224]{0:T(1024)S(1)}, f32[4224]{0:T(1024)S(1)}, u32[]{:S(2)}, u32[]{:S(2)}) %collective-permute-start.41) | collective-permute-done | bytes 16928 | tf_op jit(solution)/shard_map/ppermute | solution.py:442
  1488.6 34.6 %collective-permute-done.42 = f32[4224]{0:T(1024)S(1)} collective-permute-done((f32[4224]{0:T(1024)S(1)}, f32[4224]{0:T(1024)S(1)}, u32[]{:S(2)}, u32[]{:S(2)}) %collective-permute-start.42) | collective-permute-done | bytes 16928 | tf_op jit(solution)/shard_map/ppermute | solution.py:442
  1539.4 17.6 %collective-permute-done.47 = bf16[256,3200]{1,0:T(8,128)(2,1)S(1)} collective-permute-done((bf16[256,3200]{1,0:T(8,128)(2,1)S(1)}, bf16[256,3200]{1,0:T(8,128)(2,1)S(1)}, u32[]{:S(2)}, u32[]{:S(2)}) %collective-permute-start.47) | collective-permute-done | bytes 1638432 | tf_op jit(solution)/shard_map/ppermute | solution.py:442
  1557.0 5.6 collective-permute-done.46
  1569.8 16.5 %collective-permute-done.52 = bf16[128,3200]{1,0:T(8,128)(2,1)S(1)} collective-permute-done((bf16[128,3200]{1,0:T(8,128)(2,1)S(1)}, bf16[128,3200]{1,0:T(8,128)(2,1)S(1)}, u32[]{:S(2)}, u32[]{:S(2)}) %collective-permute-start.52) | collective-permute-done | bytes 819232 | tf_op jit(solution)/shard_map/ppermute | solution.py:447
  (466 shorter events, 378.0 us)
Async XLA Ops:
  6.4 37.9 %collective-permute-start = (bf16[128,3200]{0,1:T(8,128)(2,1)}, bf16[128,3200]{0,1:T(8,128)(2,1)}, u32[]{:S(2)}, u32[]{:S(2)}) collective-permute-start(bf16[128,3200]{0,1:T(8,128)(2,1)} %get-tuple-element.144), channel_id=1, source_target_pairs={{0,1},{1,2},{2,3},{3,0},{4,5},{5,6},{6,7},{7,4},{8,9},{9,10},{10,1... | collective-permute-start | bytes 2457608 | tf_op jit(solution)/shard_map/ppermute | solution.py:447
  9.4 55.8 %collective-permute-start.1 = (bf16[128,3200]{0,1:T(8,128)(2,1)}, bf16[128,3200]{0,1:T(8,128)(2,1)}, u32[]{:S(2)}, u32[]{:S(2)}) collective-permute-start(bf16[128,3200]{0,1:T(8,128)(2,1)} %get-tuple-element.144), channel_id=1, source_target_pairs={{0,2},{1,3},{2,0},{3,1},{4,6},{5,7},{6,4},{7,5},{8,10},{9,11},{10,... | collective-permute-start | bytes 2457608 | tf_op jit(solution)/shard_map/ppermute | solution.py:447
  12.0 55.4 %collective-permute-start.2 = (bf16[128,3200]{0,1:T(8,128)(2,1)}, bf16[128,3200]{0,1:T(8,128)(2,1)}, u32[]{:S(2)}, u32[]{:S(2)}) collective-permute-start(bf16[128,3200]{0,1:T(8,128)(2,1)} %get-tuple-element.144), channel_id=1, source_target_pairs={{0,3},{1,0},{2,1},{3,2},{4,7},{5,4},{6,5},{7,6},{8,11},{9,8},{10,9... | collective-permute-start | bytes 2457608 | tf_op jit(solution)/shard_map/ppermute | solution.py:447
  74.7 87.3 %collective-permute-start.3 = (bf16[512,3200]{1,0:T(8,128)(2,1)}, bf16[512,3200]{1,0:T(8,128)(2,1)}, u32[]{:S(2)}, u32[]{:S(2)}) collective-permute-start(bf16[512,3200]{1,0:T(8,128)(2,1)} %bitcast.11), channel_id=1, source_target_pairs={{0,8},{8,0},{16,24},{24,16},{1,9},{9,1},{17,25},{25,17},{2,10},{10... | collective-permute-start | bytes 9830408 | tf_op jit(solution)/shard_map/ppermute | solution.py:442
  76.2 88.7 %collective-permute-start.4 = (bf16[512,3200]{1,0:T(8,128)(2,1)}, bf16[512,3200]{1,0:T(8,128)(2,1)}, u32[]{:S(2)}, u32[]{:S(2)}) collective-permute-start(bf16[512,3200]{1,0:T(8,128)(2,1)} %bitcast.11), channel_id=1, source_target_pairs={{0,16},{8,24},{16,0},{24,8},{1,17},{9,25},{17,1},{25,9},{2,18},{10... | collective-permute-start | bytes 9830408 | tf_op jit(solution)/shard_map/ppermute | solution.py:442
  82.2 30.2 %collective-permute-start.11 = (bf16[128,1024]{1,0:T(8,128)(2,1)}, bf16[128,1024]{1,0:T(8,128)(2,1)S(1)}, u32[]{:S(2)}, u32[]{:S(2)}) collective-permute-start(bf16[128,1024]{1,0:T(8,128)(2,1)} %bitcast.163), channel_id=1, source_target_pairs={{0,1},{1,2},{2,3},{3,0},{4,5},{5,6},{6,7},{7,4},{8,9},{9,10},{10,1... | collective-permute-start | bytes 786440 | tf_op jit(solution)/shard_map/ppermute | solution.py:447
  117.7 111.6 %collective-permute-start.19 = (bf16[128,5632]{1,0:T(8,128)(2,1)S(1)}, bf16[128,5632]{1,0:T(8,128)(2,1)}, u32[]{:S(2)}, u32[]{:S(2)}) collective-permute-start(bf16[128,5632]{1,0:T(8,128)(2,1)S(1)} %pad_maximum_fusion.1), channel_id=1, source_target_pairs={{0,1},{1,2},{2,3},{3,0},{4,5},{5,6},{6,7},{7,4},{8,9},{9,10},{10,1... | collective-permute-start | bytes 4325384 | tf_op jit(solution)/shard_map/ppermute | solution.py:447
  154.7 136.5 %collective-permute-start.20 = (bf16[128,5632]{1,0:T(8,128)(2,1)S(1)}, bf16[128,5632]{1,0:T(8,128)(2,1)}, u32[]{:S(2)}, u32[]{:S(2)}) collective-permute-start(bf16[128,5632]{1,0:T(8,128)(2,1)S(1)} %pad_maximum_fusion.1), channel_id=1, source_target_pairs={{0,2},{1,3},{2,0},{3,1},{4,6},{5,7},{6,4},{7,5},{8,10},{9,11},{10,... | collective-permute-start | bytes 4325384 | tf_op jit(solution)/shard_map/ppermute | solution.py:447
  154.7 154.5 %collective-permute-start.21 = (bf16[128,5632]{1,0:T(8,128)(2,1)S(1)}, bf16[128,5632]{1,0:T(8,128)(2,1)}, u32[]{:S(2)}, u32[]{:S(2)}) collective-permute-start(bf16[128,5632]{1,0:T(8,128)(2,1)S(1)} %pad_maximum_fusion.1), channel_id=1, source_target_pairs={{0,3},{1,0},{2,1},{3,2},{4,7},{5,4},{6,5},{7,6},{8,11},{9,8},{10,9... | collective-permute-start | bytes 4325384 | tf_op jit(solution)/shard_map/ppermute | solution.py:447
  164.3 37.3 %collective-permute-start.5 = (bf16[256,3200]{1,0:T(8,128)(2,1)S(1)}, bf16[256,3200]{1,0:T(8,128)(2,1)S(1)}, u32[]{:S(2)}, u32[]{:S(2)}) collective-permute-start(bf16[256,3200]{1,0:T(8,128)(2,1)S(1)} %slice.319), channel_id=1, source_target_pairs={{0,16},{8,24},{16,0},{24,8},{1,17},{9,25},{17,1},{25,9},{2,18},{10... | collective-permute-start | bytes 4915208 | tf_op jit(solution)/shard_map/ppermute | solution.py:442
  166.4 37.1 %collective-permute-start.6 = (bf16[256,3200]{1,0:T(8,128)(2,1)S(1)}, bf16[256,3200]{1,0:T(8,128)(2,1)S(1)}, u32[]{:S(2)}, u32[]{:S(2)}) collective-permute-start(bf16[256,3200]{1,0:T(8,128)(2,1)S(1)} %slice.320), channel_id=1, source_target_pairs={{0,8},{8,0},{16,24},{24,16},{1,9},{9,1},{17,25},{25,17},{2,10},{10... | collective-permute-start | bytes 4915208 | tf_op jit(solution)/shard_map/ppermute | solution.py:442
  293.9 36.0 %collective-permute-start.14 = (bf16[512,1024]{1,0:T(8,128)(2,1)S(1)}, bf16[512,1024]{1,0:T(8,128)(2,1)S(1)}, u32[]{:S(2)}, u32[]{:S(2)}) collective-permute-start(bf16[512,1024]{1,0:T(8,128)(2,1)S(1)} %bitcast.251), channel_id=1, source_target_pairs={{0,8},{8,0},{16,24},{24,16},{1,9},{9,1},{17,25},{25,17},{2,10},{10... | collective-permute-start | bytes 3145736 | tf_op jit(solution)/shard_map/ppermute | solution.py:442
  297.2 32.8 %collective-permute-start.15 = (bf16[512,1024]{1,0:T(8,128)(2,1)S(1)}, bf16[512,1024]{1,0:T(8,128)(2,1)S(1)}, u32[]{:S(2)}, u32[]{:S(2)}) collective-permute-start(bf16[512,1024]{1,0:T(8,128)(2,1)S(1)} %bitcast.252), channel_id=1, source_target_pairs={{0,16},{8,24},{16,0},{24,8},{1,17},{9,25},{17,1},{25,9},{2,18},{10... | collective-permute-start | bytes 3145736 | tf_op jit(solution)/shard_map/ppermute | solution.py:442
  303.9 33.4 %collective-permute-start.9 = (bf16[2,8,128,128]{3,2,1,0:T(8,128)(2,1)S(1)}, bf16[2,8,128,128]{3,2,1,0:T(8,128)(2,1)S(1)}, u32[]{:S(2)}, u32[]{:S(2)}) collective-permute-start(bf16[2,8,128,128]{3,2,1,0:T(8,128)(2,1)S(1)} %fusion.31), channel_id=1, source_target_pairs={{0,8},{8,16},{16,24},{1,9},{9,17},{17,25},{2,10},{10,18},{18,26},{... | collective-permute-start | bytes 1572872 | tf_op jit(solution)/shard_map/ppermute | solution.py:552
  311.8 63.4 %collective-permute-start.26 = (bf16[128,2816]{1,0:T(8,128)(2,1)}, bf16[128,2816]{1,0:T(8,128)(2,1)}, u32[]{:S(2)}, u32[]{:S(2)}) collective-permute-start(bf16[128,2816]{1,0:T(8,128)(2,1)} %bitcast.162), channel_id=1, source_target_pairs={{0,1},{1,2},{2,3},{3,0},{4,5},{5,6},{6,7},{7,4},{8,9},{9,10},{10,1... | collective-permute-start | bytes 2162696 | tf_op jit(solution)/shard_map/ppermute | solution.py:447
  313.0 68.1 %collective-permute-start.27 = (bf16[128,2816]{1,0:T(8,128)(2,1)}, bf16[128,2816]{1,0:T(8,128)(2,1)}, u32[]{:S(2)}, u32[]{:S(2)}) collective-permute-start(bf16[128,2816]{1,0:T(8,128)(2,1)} %bitcast.162), channel_id=1, source_target_pairs={{0,2},{1,3},{2,0},{3,1},{4,6},{5,7},{6,4},{7,5},{8,10},{9,11},{10,... | collective-permute-start | bytes 2162696 | tf_op jit(solution)/shard_map/ppermute | solution.py:447
  351.1 31.2 %collective-permute-start.28 = (bf16[128,2816]{1,0:T(8,128)(2,1)}, bf16[128,2816]{1,0:T(8,128)(2,1)}, u32[]{:S(2)}, u32[]{:S(2)}) collective-permute-start(bf16[128,2816]{1,0:T(8,128)(2,1)} %bitcast.162), channel_id=1, source_target_pairs={{0,3},{1,0},{2,1},{3,2},{4,7},{5,4},{6,5},{7,6},{8,11},{9,8},{10,9... | collective-permute-start | bytes 2162696 | tf_op jit(solution)/shard_map/ppermute | solution.py:447
  376.4 127.3 %collective-permute-start.22 = (bf16[512,5632]{1,0:T(8,128)(2,1)}, bf16[512,5632]{1,0:T(8,128)(2,1)S(1)}, u32[]{:S(2)}, u32[]{:S(2)}) collective-permute-start(bf16[512,5632]{1,0:T(8,128)(2,1)} %bitcast.38), channel_id=1, source_target_pairs={{0,8},{8,0},{16,24},{24,16},{1,9},{9,1},{17,25},{25,17},{2,10},{10... | collective-permute-start | bytes 17301512 | tf_op jit(solution)/shard_map/ppermute | solution.py:442
  379.1 128.5 %collective-permute-start.23 = (bf16[512,5632]{1,0:T(8,128)(2,1)}, bf16[512,5632]{1,0:T(8,128)(2,1)}, u32[]{:S(2)}, u32[]{:S(2)}) collective-permute-start(bf16[512,5632]{1,0:T(8,128)(2,1)} %bitcast.38), channel_id=1, source_target_pairs={{0,16},{8,24},{16,0},{24,8},{1,17},{9,25},{17,1},{25,9},{2,18},{10... | collective-permute-start | bytes 17301512 | tf_op jit(solution)/shard_map/ppermute | solution.py:442
  503.9 65.6 %collective-permute-start.24 = (bf16[256,5632]{1,0:T(8,128)(2,1)S(1)}, bf16[256,5632]{1,0:T(8,128)(2,1)S(1)}, u32[]{:S(2)}, u32[]{:S(2)}) collective-permute-start(bf16[256,5632]{1,0:T(8,128)(2,1)S(1)} %slice.325), channel_id=1, source_target_pairs={{0,16},{8,24},{16,0},{24,8},{1,17},{9,25},{17,1},{25,9},{2,18},{10... | collective-permute-start | bytes 8650760 | tf_op jit(solution)/shard_map/ppermute | solution.py:442
  509.6 63.4 %collective-permute-start.25 = (bf16[256,5632]{1,0:T(8,128)(2,1)S(1)}, bf16[256,5632]{1,0:T(8,128)(2,1)S(1)}, u32[]{:S(2)}, u32[]{:S(2)}) collective-permute-start(bf16[256,5632]{1,0:T(8,128)(2,1)S(1)} %slice.326), channel_id=1, source_target_pairs={{0,8},{8,0},{16,24},{24,16},{1,9},{9,1},{17,25},{25,17},{2,10},{10... | collective-permute-start | bytes 8650760 | tf_op jit(solution)/shard_map/ppermute | solution.py:442
  575.9 62.5 %collective-permute-start.29 = (bf16[512,2816]{1,0:T(8,128)(2,1)S(1)}, bf16[512,2816]{1,0:T(8,128)(2,1)}, u32[]{:S(2)}, u32[]{:S(2)}) collective-permute-start(bf16[512,2816]{1,0:T(8,128)(2,1)S(1)} %bitcast.243), channel_id=1, source_target_pairs={{0,8},{8,0},{16,24},{24,16},{1,9},{9,1},{17,25},{25,17},{2,10},{10... | collective-permute-start | bytes 8650760 | tf_op jit(solution)/shard_map/ppermute | solution.py:442
  576.5 64.0 %collective-permute-start.30 = (bf16[512,2816]{1,0:T(8,128)(2,1)S(1)}, bf16[512,2816]{1,0:T(8,128)(2,1)}, u32[]{:S(2)}, u32[]{:S(2)}) collective-permute-start(bf16[512,2816]{1,0:T(8,128)(2,1)S(1)} %bitcast.244), channel_id=1, source_target_pairs={{0,16},{8,24},{16,0},{24,8},{1,17},{9,25},{17,1},{25,9},{2,18},{10... | collective-permute-start | bytes 8650760 | tf_op jit(solution)/shard_map/ppermute | solution.py:442
  639.9 30.6 %collective-permute-start.31 = (bf16[256,2816]{1,0:T(8,128)(2,1)S(1)}, bf16[256,2816]{1,0:T(8,128)(2,1)S(1)}, u32[]{:S(2)}, u32[]{:S(2)}) collective-permute-start(bf16[256,2816]{1,0:T(8,128)(2,1)S(1)} %slice.329), channel_id=1, source_target_pairs={{0,16},{8,24},{16,0},{24,8},{1,17},{9,25},{17,1},{25,9},{2,18},{10... | collective-permute-start | bytes 4325384 | tf_op jit(solution)/shard_map/ppermute | solution.py:442
  641.9 30.6 %collective-permute-start.32 = (bf16[256,2816]{1,0:T(8,128)(2,1)S(1)}, bf16[256,2816]{1,0:T(8,128)(2,1)S(1)}, u32[]{:S(2)}, u32[]{:S(2)}) collective-permute-start(bf16[256,2816]{1,0:T(8,128)(2,1)S(1)} %slice.330), channel_id=1, source_target_pairs={{0,8},{8,0},{16,24},{24,16},{1,9},{9,1},{17,25},{25,17},{2,10},{10... | collective-permute-start | bytes 4325384 | tf_op jit(solution)/shard_map/ppermute | solution.py:442
  774.9 39.5 %collective-permute-start.85 = (bf16[256,2816]{1,0:T(8,128)(2,1)S(1)}, bf16[256,2816]{1,0:T(8,128)(2,1)S(1)}, u32[]{:S(2)}, u32[]{:S(2)}) collective-permute-start(bf16[256,2816]{1,0:T(8,128)(2,1)S(1)} %copy-done.26), channel_id=1, source_target_pairs={{0,8},{8,0},{16,24},{24,16},{1,9},{9,1},{17,25},{25,17},{2,10},{10... | collective-permute-start | bytes 4325384 | tf_op jit(solution)/shard_map/ppermute | solution.py:442
  775.7 44.7 %collective-permute-start.80 = (bf16[256,2816]{1,0:T(8,128)(2,1)S(1)}, bf16[256,2816]{1,0:T(8,128)(2,1)S(1)}, u32[]{:S(2)}, u32[]{:S(2)}) collective-permute-start(bf16[256,2816]{1,0:T(8,128)(2,1)S(1)} %convolution_convert_fusion.11), channel_id=1, source_target_pairs={{0,16},{8,24},{16,0},{24,8},{1,17},{9,25},{17,1},{25,9},{2,18},{10... | collective-permute-start | bytes 4325384 | tf_op jit(solution)/shard_map/ppermute | solution.py:442
  796.8 74.7 %collective-permute-start.76 = (bf16[256,5632]{1,0:T(8,128)(2,1)}, bf16[256,5632]{1,0:T(8,128)(2,1)}, u32[]{:S(2)}, u32[]{:S(2)}) collective-permute-start(bf16[256,5632]{1,0:T(8,128)(2,1)} %convolution_convert_fusion), channel_id=1, source_target_pairs={{0,8},{8,0},{16,24},{24,16},{1,9},{9,1},{17,25},{25,17},{2,10},{10... | collective-permute-start | bytes 8650760 | tf_op jit(solution)/shard_map/ppermute | solution.py:442
  802.1 100.2 %collective-permute-start.84 = (bf16[256,2816]{1,0:T(8,128)(2,1)S(1)}, bf16[256,2816]{1,0:T(8,128)(2,1)}, u32[]{:S(2)}, u32[]{:S(2)}) collective-permute-start(bf16[256,2816]{1,0:T(8,128)(2,1)S(1)} %convolution_convert_fusion.9), channel_id=1, source_target_pairs={{0,8},{8,0},{16,24},{24,16},{1,9},{9,1},{17,25},{25,17},{2,10},{10... | collective-permute-start | bytes 4325384 | tf_op jit(solution)/shard_map/ppermute | solution.py:442
  804.9 100.0 %collective-permute-start.82 = (bf16[256,2816]{1,0:T(8,128)(2,1)S(1)}, bf16[256,2816]{1,0:T(8,128)(2,1)}, u32[]{:S(2)}, u32[]{:S(2)}) collective-permute-start(bf16[256,2816]{1,0:T(8,128)(2,1)S(1)} %convolution_convert_fusion.10), channel_id=1, source_target_pairs={{0,16},{8,24},{16,0},{24,8},{1,17},{9,25},{17,1},{25,9},{2,18},{10... | collective-permute-start | bytes 4325384 | tf_op jit(solution)/shard_map/ppermute | solution.py:442
  815.5 438.4 %collective-permute-start.75 = (bf16[256,5632]{1,0:T(8,128)(2,1)}, bf16[256,5632]{1,0:T(8,128)(2,1)}, u32[]{:S(2)}, u32[]{:S(2)}) collective-permute-start(bf16[256,5632]{1,0:T(8,128)(2,1)} %convolution_convert_fusion.1), channel_id=1, source_target_pairs={{0,8},{8,0},{16,24},{24,16},{1,9},{9,1},{17,25},{25,17},{2,10},{10... | collective-permute-start | bytes 8650760 | tf_op jit(solution)/shard_map/ppermute | solution.py:442
  820.4 81.9 %collective-permute-start.86 = (bf16[256,2816]{1,0:T(8,128)(2,1)S(1)}, bf16[256,2816]{1,0:T(8,128)(2,1)S(1)}, u32[]{:S(2)}, u32[]{:S(2)}) collective-permute-start(bf16[256,2816]{1,0:T(8,128)(2,1)S(1)} %add_convert_fusion.6), channel_id=1, source_target_pairs={{0,16},{8,24},{16,0},{24,8},{1,17},{9,25},{17,1},{25,9},{2,18},{10... | collective-permute-start | bytes 4325384 | tf_op jit(solution)/shard_map/ppermute | solution.py:442
  871.4 122.4 %collective-permute-start.71 = (bf16[256,5632]{1,0:T(8,128)(2,1)}, bf16[256,5632]{1,0:T(8,128)(2,1)}, u32[]{:S(2)}, u32[]{:S(2)}) collective-permute-start(bf16[256,5632]{1,0:T(8,128)(2,1)} %convolution_convert_fusion.3), channel_id=1, source_target_pairs={{0,16},{8,24},{16,0},{24,8},{1,17},{9,25},{17,1},{25,9},{2,18},{10... | collective-permute-start | bytes 8650760 | tf_op jit(solution)/shard_map/ppermute | solution.py:442
  902.3 118.5 %collective-permute-start.34 = (bf16[1024,2048]{1,0:T(8,128)(2,1)}, bf16[1024,2048]{1,0:T(8,128)(2,1)}, u32[]{:S(2)}, u32[]{:S(2)}) collective-permute-start(bf16[1024,2048]{1,0:T(8,128)(2,1)} %convolution_convert_fusion.13), channel_id=1, source_target_pairs={{0,4},{4,0},{1,5},{5,1},{2,6},{6,2},{3,7},{7,3},{8,12},{12,8},{9,1... | collective-permute-start | bytes 12582920 | tf_op jit(solution)/shard_map/ppermute | solution.py:442
  902.3 87.7 %collective-permute-start.81 = (bf16[256,2816]{1,0:T(8,128)(2,1)S(1)}, bf16[256,2816]{1,0:T(8,128)(2,1)S(1)}, u32[]{:S(2)}, u32[]{:S(2)}) collective-permute-start(bf16[256,2816]{1,0:T(8,128)(2,1)S(1)} %add_convert_fusion.7), channel_id=1, source_target_pairs={{0,8},{8,0},{16,24},{24,16},{1,9},{9,1},{17,25},{25,17},{2,10},{10... | collective-permute-start | bytes 4325384 | tf_op jit(solution)/shard_map/ppermute | solution.py:442
  905.0 98.9 %collective-permute-start.87 = (bf16[128,2816]{1,0:T(8,128)(2,1)S(1)}, bf16[128,2816]{1,0:T(8,128)(2,1)S(1)}, u32[]{:S(2)}, u32[]{:S(2)}) collective-permute-start(bf16[128,2816]{1,0:T(8,128)(2,1)S(1)} %get-tuple-element.142), channel_id=1, source_target_pairs={{0,2},{1,3},{2,0},{3,1},{4,6},{5,7},{6,4},{7,5},{8,10},{9,11},{10,... | collective-permute-start | bytes 2162696 | tf_op jit(solution)/shard_map/ppermute | solution.py:447
  1003.9 296.9 %collective-permute-start.73 = (bf16[256,5632]{1,0:T(8,128)(2,1)}, bf16[256,5632]{1,0:T(8,128)(2,1)}, u32[]{:S(2)}, u32[]{:S(2)}) collective-permute-start(bf16[256,5632]{1,0:T(8,128)(2,1)} %convolution_convert_fusion.2), channel_id=1, source_target_pairs={{0,16},{8,24},{16,0},{24,8},{1,17},{9,25},{17,1},{25,9},{2,18},{10... | collective-permute-start | bytes 8650760 | tf_op jit(solution)/shard_map/ppermute | solution.py:442
  1052.8 48.6 %collective-permute-start.66 = (bf16[256,1024]{1,0:T(8,128)(2,1)}, bf16[256,1024]{1,0:T(8,128)(2,1)}, u32[]{:S(2)}, u32[]{:S(2)}) collective-permute-start(bf16[256,1024]{1,0:T(8,128)(2,1)} %convolution_convert_fusion.17), channel_id=1, source_target_pairs={{0,8},{8,0},{16,24},{24,16},{1,9},{9,1},{17,25},{25,17},{2,10},{10... | collective-permute-start | bytes 1572872 | tf_op jit(solution)/shard_map/ppermute | solution.py:442
  1053.2 33.0 %collective-permute-start.67 = (bf16[256,1024]{1,0:T(8,128)(2,1)}, bf16[256,1024]{1,0:T(8,128)(2,1)S(1)}, u32[]{:S(2)}, u32[]{:S(2)}) collective-permute-start(bf16[256,1024]{1,0:T(8,128)(2,1)} %convolution_convert_fusion.16), channel_id=1, source_target_pairs={{0,8},{8,0},{16,24},{24,16},{1,9},{9,1},{17,25},{25,17},{2,10},{10... | collective-permute-start | bytes 1572872 | tf_op jit(solution)/shard_map/ppermute | solution.py:442
  1101.4 27.3 %collective-permute-start.63 = (bf16[256,1024]{1,0:T(8,128)(2,1)S(1)}, bf16[256,1024]{1,0:T(8,128)(2,1)S(1)}, u32[]{:S(2)}, u32[]{:S(2)}) collective-permute-start(bf16[256,1024]{1,0:T(8,128)(2,1)S(1)} %fusion.29), channel_id=1, source_target_pairs={{0,8},{8,0},{16,24},{24,16},{1,9},{9,1},{17,25},{25,17},{2,10},{10... | collective-permute-start | bytes 1572872 | tf_op jit(solution)/shard_map/ppermute | solution.py:442
  1115.7 94.9 %collective-permute-start.69 = (bf16[128,1024]{1,0:T(8,128)(2,1)}, bf16[128,1024]{1,0:T(8,128)(2,1)S(1)}, u32[]{:S(2)}, u32[]{:S(2)}) collective-permute-start(bf16[128,1024]{1,0:T(8,128)(2,1)} %get-tuple-element.146), channel_id=1, source_target_pairs={{0,2},{1,3},{2,0},{3,1},{4,6},{5,7},{6,4},{7,5},{8,10},{9,11},{10,... | collective-permute-start | bytes 786440 | tf_op jit(solution)/shard_map/ppermute | solution.py:447
  1128.7 82.0 %collective-permute-start.70 = (bf16[128,1024]{1,0:T(8,128)(2,1)}, bf16[128,1024]{1,0:T(8,128)(2,1)S(1)}, u32[]{:S(2)}, u32[]{:S(2)}) collective-permute-start(bf16[128,1024]{1,0:T(8,128)(2,1)} %get-tuple-element.147), channel_id=1, source_target_pairs={{0,3},{1,0},{2,1},{3,2},{4,7},{5,4},{6,5},{7,6},{8,11},{9,8},{10,9... | collective-permute-start | bytes 786440 | tf_op jit(solution)/shard_map/ppermute | solution.py:447
  1134.5 77.4 %collective-permute-start.65 = (bf16[128,1024]{1,0:T(8,128)(2,1)S(1)}, bf16[128,1024]{1,0:T(8,128)(2,1)S(1)}, u32[]{:S(2)}, u32[]{:S(2)}) collective-permute-start(bf16[128,1024]{1,0:T(8,128)(2,1)S(1)} %slice.517), channel_id=1, source_target_pairs={{0,1},{1,2},{2,3},{3,0},{4,5},{5,6},{6,7},{7,4},{8,9},{9,10},{10,1... | collective-permute-start | bytes 786440 | tf_op jit(solution)/shard_map/ppermute | solution.py:447
  1210.7 166.9 %collective-permute-start.33 = (bf16[1024,2048]{1,0:T(8,128)(2,1)}, bf16[1024,2048]{1,0:T(8,128)(2,1)}, u32[]{:S(2)}, u32[]{:S(2)}) collective-permute-start(bf16[1024,2048]{1,0:T(8,128)(2,1)} %convolution_convert_fusion.14), channel_id=1, source_target_pairs={{0,4},{4,0},{1,5},{5,1},{2,6},{6,2},{3,7},{7,3},{8,12},{12,8},{9,1... | collective-permute-start | bytes 12582920 | tf_op jit(solution)/shard_map/ppermute | solution.py:442
  1210.8 65.2 %collective-permute-start.77 = (bf16[256,5632]{1,0:T(8,128)(2,1)}, bf16[256,5632]{1,0:T(8,128)(2,1)}, u32[]{:S(2)}, u32[]{:S(2)}) collective-permute-start(bf16[256,5632]{1,0:T(8,128)(2,1)} %add_convert_fusion.3), channel_id=1, source_target_pairs={{0,16},{8,24},{16,0},{24,8},{1,17},{9,25},{17,1},{25,9},{2,18},{10... | collective-permute-start | bytes 8650760 | tf_op jit(solution)/shard_map/ppermute | solution.py:442
  1229.6 73.6 %collective-permute-start.72 = (bf16[256,5632]{1,0:T(8,128)(2,1)}, bf16[256,5632]{1,0:T(8,128)(2,1)}, u32[]{:S(2)}, u32[]{:S(2)}) collective-permute-start(bf16[256,5632]{1,0:T(8,128)(2,1)} %add_convert_fusion.4), channel_id=1, source_target_pairs={{0,8},{8,0},{16,24},{24,16},{1,9},{9,1},{17,25},{25,17},{2,10},{10... | collective-permute-start | bytes 8650760 | tf_op jit(solution)/shard_map/ppermute | solution.py:442
  1253.9 42.0 %collective-permute-start.58 = (f32[4,3072]{1,0:T(4,128)S(1)}, f32[4,3072]{1,0:T(4,128)S(1)}, u32[]{:S(2)}, u32[]{:S(2)}) collective-permute-start(f32[4,3072]{1,0:T(4,128)S(1)} %slice.348), channel_id=1, source_target_pairs={{0,8},{8,0},{16,24},{24,16},{1,9},{9,1},{17,25},{25,17},{2,10},{10... | collective-permute-start | bytes 147464 | tf_op jit(solution)/shard_map/ppermute | solution.py:442
  1276.0 93.1 %collective-permute-start.39 = (bf16[1024,2048]{1,0:T(8,128)(2,1)}, bf16[1024,2048]{1,0:T(8,128)(2,1)}, u32[]{:S(2)}, u32[]{:S(2)}) collective-permute-start(bf16[1024,2048]{1,0:T(8,128)(2,1)} %convolution_convert_fusion.12), channel_id=1, source_target_pairs={{0,4},{4,0},{1,5},{5,1},{2,6},{6,2},{3,7},{7,3},{8,12},{12,8},{9,1... | collective-permute-start | bytes 12582920 | tf_op jit(solution)/shard_map/ppermute | solution.py:442
  1300.1 156.1 %collective-permute-start.78 = (bf16[128,5632]{1,0:T(8,128)(2,1)}, bf16[128,5632]{1,0:T(8,128)(2,1)}, u32[]{:S(2)}, u32[]{:S(2)}) collective-permute-start(bf16[128,5632]{1,0:T(8,128)(2,1)} %get-tuple-element.133), channel_id=1, source_target_pairs={{0,2},{1,3},{2,0},{3,1},{4,6},{5,7},{6,4},{7,5},{8,10},{9,11},{10,... | collective-permute-start | bytes 4325384 | tf_op jit(solution)/shard_map/ppermute | solution.py:447
  1300.8 30.2 %collective-permute-start.60 = (f32[4,3072]{1,0:T(4,128)S(1)}, f32[4,3072]{1,0:T(4,128)S(1)}, u32[]{:S(2)}, u32[]{:S(2)}) collective-permute-start(f32[4,3072]{1,0:T(4,128)S(1)} %add.383), channel_id=1, source_target_pairs={{0,1},{1,0},{2,3},{3,2},{4,5},{5,4},{6,7},{7,6},{8,9},{9,8},{10,11... | collective-permute-start | bytes 147464 | tf_op jit(solution)/shard_map/ppermute | solution.py:442
  1331.0 36.8 %collective-permute-start.61 = (f32[4,3072]{1,0:T(4,128)S(1)}, f32[4,3072]{1,0:T(4,128)S(1)}, u32[]{:S(2)}, u32[]{:S(2)}) collective-permute-start(f32[4,3072]{1,0:T(4,128)S(1)} %add.384), channel_id=1, source_target_pairs={{0,2},{1,3},{2,0},{3,1},{4,6},{5,7},{6,4},{7,5},{8,10},{9,11},{10,... | collective-permute-start | bytes 147464 | tf_op jit(solution)/shard_map/ppermute | solution.py:442
  1365.7 92.0 %collective-permute-start.79 = (bf16[128,5632]{1,0:T(8,128)(2,1)}, bf16[128,5632]{1,0:T(8,128)(2,1)}, u32[]{:S(2)}, u32[]{:S(2)}) collective-permute-start(bf16[128,5632]{1,0:T(8,128)(2,1)} %get-tuple-element.134), channel_id=1, source_target_pairs={{0,3},{1,0},{2,1},{3,2},{4,7},{5,4},{6,5},{7,6},{8,11},{9,8},{10,9... | collective-permute-start | bytes 4325384 | tf_op jit(solution)/shard_map/ppermute | solution.py:447
  1367.8 91.4 %collective-permute-start.74 = (bf16[128,5632]{1,0:T(8,128)(2,1)}, bf16[128,5632]{1,0:T(8,128)(2,1)}, u32[]{:S(2)}, u32[]{:S(2)}) collective-permute-start(bf16[128,5632]{1,0:T(8,128)(2,1)} %slice.512), channel_id=1, source_target_pairs={{0,1},{1,2},{2,3},{3,0},{4,5},{5,6},{6,7},{7,4},{8,9},{9,10},{10,1... | collective-permute-start | bytes 4325384 | tf_op jit(solution)/shard_map/ppermute | solution.py:447
  1413.1 39.1 %collective-permute-start.50 = (bf16[256,3200]{1,0:T(8,128)(2,1)}, bf16[256,3200]{1,0:T(8,128)(2,1)}, u32[]{:S(2)}, u32[]{:S(2)}) collective-permute-start(bf16[256,3200]{1,0:T(8,128)(2,1)} %convolution_convert_fusion.4), channel_id=1, source_target_pairs={{0,8},{8,0},{16,24},{24,16},{1,9},{9,1},{17,25},{25,17},{2,10},{10... | collective-permute-start | bytes 4915208 | tf_op jit(solution)/shard_map/ppermute | solution.py:442
  1423.8 108.7 %collective-permute-start.49 = (bf16[256,3200]{1,0:T(8,128)(2,1)S(1)}, bf16[256,3200]{1,0:T(8,128)(2,1)S(1)}, u32[]{:S(2)}, u32[]{:S(2)}) collective-permute-start(bf16[256,3200]{1,0:T(8,128)(2,1)S(1)} %convolution_convert_fusion.5), channel_id=1, source_target_pairs={{0,8},{8,0},{16,24},{24,16},{1,9},{9,1},{17,25},{25,17},{2,10},{10... | collective-permute-start | bytes 4915208 | tf_op jit(solution)/shard_map/ppermute | solution.py:442
  1452.2 76.8 %collective-permute-start.45 = (bf16[256,3200]{1,0:T(8,128)(2,1)S(1)}, bf16[256,3200]{1,0:T(8,128)(2,1)S(1)}, u32[]{:S(2)}, u32[]{:S(2)}) collective-permute-start(bf16[256,3200]{1,0:T(8,128)(2,1)S(1)} %convolution_convert_fusion.7), channel_id=1, source_target_pairs={{0,16},{8,24},{16,0},{24,8},{1,17},{9,25},{17,1},{25,9},{2,18},{10... | collective-permute-start | bytes 4915208 | tf_op jit(solution)/shard_map/ppermute | solution.py:442
  1456.2 29.6 %collective-permute-start.41 = (f32[4224]{0:T(1024)S(1)}, f32[4224]{0:T(1024)S(1)}, u32[]{:S(2)}, u32[]{:S(2)}) collective-permute-start(f32[4224]{0:T(1024)S(1)} %fusion.108), channel_id=1, source_target_pairs={{0,8},{8,0},{16,24},{24,16},{1,9},{9,1},{17,25},{25,17},{2,10},{10... | collective-permute-start | bytes 50696 | tf_op jit(solution)/shard_map/ppermute | solution.py:442
  1457.7 74.8 %collective-permute-start.51 = (bf16[256,3200]{1,0:T(8,128)(2,1)S(1)}, bf16[256,3200]{1,0:T(8,128)(2,1)S(1)}, u32[]{:S(2)}, u32[]{:S(2)}) collective-permute-start(bf16[256,3200]{1,0:T(8,128)(2,1)S(1)} %fusion.13), channel_id=1, source_target_pairs={{0,16},{8,24},{16,0},{24,8},{1,17},{9,25},{17,1},{25,9},{2,18},{10... | collective-permute-start | bytes 4915208 | tf_op jit(solution)/shard_map/ppermute | solution.py:442
  1485.8 37.4 %collective-permute-start.42 = (f32[4224]{0:T(1024)S(1)}, f32[4224]{0:T(1024)S(1)}, u32[]{:S(2)}, u32[]{:S(2)}) collective-permute-start(f32[4224]{0:T(1024)S(1)} %add.360), channel_id=1, source_target_pairs={{0,16},{8,24},{16,0},{24,8},{1,17},{9,25},{17,1},{25,9},{2,18},{10... | collective-permute-start | bytes 50696 | tf_op jit(solution)/shard_map/ppermute | solution.py:442
  1523.6 33.4 %collective-permute-start.47 = (bf16[256,3200]{1,0:T(8,128)(2,1)S(1)}, bf16[256,3200]{1,0:T(8,128)(2,1)S(1)}, u32[]{:S(2)}, u32[]{:S(2)}) collective-permute-start(bf16[256,3200]{1,0:T(8,128)(2,1)S(1)} %convolution_convert_fusion.6), channel_id=1, source_target_pairs={{0,16},{8,24},{16,0},{24,8},{1,17},{9,25},{17,1},{25,9},{2,18},{10... | collective-permute-start | bytes 4915208 | tf_op jit(solution)/shard_map/ppermute | solution.py:442
  1527.0 41.7 %collective-permute-start.44 = (f32[4224]{0:T(1024)S(1)}, f32[4224]{0:T(1024)S(1)}, u32[]{:S(2)}, u32[]{:S(2)}) collective-permute-start(f32[4224]{0:T(1024)S(1)} %add.362), channel_id=1, source_target_pairs={{0,2},{1,3},{2,0},{3,1},{4,6},{5,7},{6,4},{7,5},{8,10},{9,11},{10,... | collective-permute-start | bytes 50696 | tf_op jit(solution)/shard_map/ppermute | solution.py:442
  1531.0 31.6 %collective-permute-start.46 = (bf16[256,3200]{1,0:T(8,128)(2,1)S(1)}, bf16[256,3200]{1,0:T(8,128)(2,1)S(1)}, u32[]{:S(2)}, u32[]{:S(2)}) collective-permute-start(bf16[256,3200]{1,0:T(8,128)(2,1)S(1)} %fusion.11), channel_id=1, source_target_pairs={{0,8},{8,0},{16,24},{24,16},{1,9},{9,1},{17,25},{25,17},{2,10},{10... | collective-permute-start | bytes 4915208 | tf_op jit(solution)/shard_map/ppermute | solution.py:442
  1534.9 51.4 %collective-permute-start.52 = (bf16[128,3200]{1,0:T(8,128)(2,1)S(1)}, bf16[128,3200]{1,0:T(8,128)(2,1)S(1)}, u32[]{:S(2)}, u32[]{:S(2)}) collective-permute-start(bf16[128,3200]{1,0:T(8,128)(2,1)S(1)} %get-tuple-element.137), channel_id=1, source_target_pairs={{0,2},{1,3},{2,0},{3,1},{4,6},{5,7},{6,4},{7,5},{8,10},{9,11},{10,... | collective-permute-start | bytes 2457608 | tf_op jit(solution)/shard_map/ppermute | solution.py:447
  1536.0 50.3 %collective-permute-start.53 = (bf16[128,3200]{1,0:T(8,128)(2,1)S(1)}, bf16[128,3200]{1,0:T(8,128)(2,1)S(1)}, u32[]{:S(2)}, u32[]{:S(2)}) collective-permute-start(bf16[128,3200]{1,0:T(8,128)(2,1)S(1)} %get-tuple-element.138), channel_id=1, source_target_pairs={{0,3},{1,0},{2,1},{3,2},{4,7},{5,4},{6,5},{7,6},{8,11},{9,8},{10,9... | collective-permute-start | bytes 2457608 | tf_op jit(solution)/shard_map/ppermute | solution.py:447
  (89 other events, 1671.6 us)

commit v2 on v1

--- a/solution.py
+++ b/solution.py
@@ -86,11 +86,11 @@
     return jnp.sum(jnp.where(iota(values.shape, 1) == head, values, 0.0), axis=-1, keepdims=True)
 
 
-def forward_kernel(taps, heads, pre, beta, bias, halo, conv, col_ref, row_ref, own, carry, final, inv, upd, states, ext):
+def forward_kernel(taps, heads, first, pre, beta, bias, halo, conv, col_ref, row_ref, own, carry, final, inv, upd, states, ext):
     length = pre.shape[0]
     ext[:HALO] = halo[0]
     ext[HALO:] = pre[...]
-    head = pl.program_id(1) * heads
+    head = first + pl.program_id(1) * heads
     jobs = [(i, j) for j in range(length // CHUNK) for i in range(heads)]
     data = {}
     for j in range(length // CHUNK):
@@ -141,7 +141,7 @@
             states[0, i, j] = state_low
 
 
-def mixer_forward(pre, bias, halo, conv, col, row, taps, heads_here, group):
+def mixer_forward(pre, logit, bias, halo, conv, col, row, taps, first, heads_here, group):
     seqs, length = col.shape[0], col.shape[1]
     steps = heads_here // group
     chunks = length // CHUNK
@@ -155,9 +155,9 @@
         return pl.BlockSpec((1, group) + tail, lambda s, h: (s, h) + (0,) * len(tail))
 
     flat = pl.BlockSpec((length, LANES * group), lambda s, h: (s, h))
-    last = 3 * heads_here
+    last = logit.shape[1] // LANES - 1
     return pl.pallas_call(
-        functools.partial(forward_kernel, taps, group),
+        functools.partial(forward_kernel, taps, group, first),
         grid=(seqs, steps),
         in_specs=[
             pl.BlockSpec((length, wide), lambda s, h: (s, h)),
@@ -189,16 +189,16 @@
         cost_estimate=pl.CostEstimate(
             flops=60 * rows * heads_here * CHUNK * LANES, bytes_accessed=40 * rows * heads_here * LANES, transcendentals=0
         ),
-    )(pre, pre, bias, halo, conv, col, row)
+    )(pre, logit, bias, halo, conv, col, row)
 
 
 def backward_kernel(
-    taps, heads, pre, beta, bias, halo, conv, col_ref, row_ref, grad_ref, inv, upd, states, start, end,
-    grad_pre, tail, before, conv_grad, bias_grad, ext, grad_ext, logits,
+    taps, heads, first, pre, beta, bias, halo, conv, col_ref, row_ref, grad_ref, inv, upd, states, start, end,
+    grad_pre, tail, before, conv_grad, logits, ext, grad_ext,
 ):
     length = pre.shape[0]
     step = pl.program_id(1)
-    head = step * heads
+    head = first + step * heads
     ext[:HALO] = halo[0]
     ext[HALO:] = pre[...]
     grad_ext[...] = jnp.zeros_like(grad_ext)
@@ -289,9 +289,7 @@
                     where = pl.ds(HALO + offset - back, CHUNK)
                     grad_ext[where, lane : lane + LANES] += back_part
         logits[rows] += grad_logit
-    wide = 3 * LANES * heads
-    place = pl.multiple_of(step * wide, LANES)
-    grad_pre[:, pl.ds(place, wide)] = low(grad_ext[HALO:])
+    grad_pre[...] = low(grad_ext[HALO:])
     before[0] = grad_ext[:HALO]
     tail[0] = grad_ext[length:]
     for i in range(heads):
@@ -300,29 +298,24 @@
             for tap in range(taps):
                 conv_grad[0, tap : tap + 1, lane : lane + LANES] = tap_sums[i, kind, tap]
 
-    @pl.when(step == pl.num_programs(1) - 1)
-    def _():
-        total = logits[...]
-        grad_pre[:, grad_pre.shape[1] - LANES :] = low(total)
-        bias_grad[0] = jnp.sum(total, axis=0, keepdims=True)
-
-
-def mixer_backward(pre, bias, halo, conv, col, row, grad_mixed, inv, upd, states, start, end, taps, heads_here, group):
+
+def mixer_backward(
+    pre, logit, bias, halo, conv, col, row, grad_mixed, inv, upd, states, start, end, taps, first, heads_here, group
+):
     seqs, length = col.shape[0], col.shape[1]
     steps = heads_here // group
     chunks = length // CHUNK
     wide = 3 * LANES * group
     rows = seqs * length
-    total = pre.shape[1]
 
     def spec(*tail):
         return pl.BlockSpec((1, group) + tail, lambda s, h: (s, h) + (0,) * len(tail))
 
-    last = 3 * heads_here
+    last = logit.shape[1] // LANES - 1
     part = pl.BlockSpec((1, HALO, wide), lambda s, h: (s, 0, h))
     edge = jax.ShapeDtypeStruct((seqs, HALO, 3 * LANES * heads_here), jnp.float32)
     return pl.pallas_call(
-        functools.partial(backward_kernel, taps, group),
+        functools.partial(backward_kernel, taps, group, first),
         grid=(seqs, steps),
         in_specs=[
             pl.BlockSpec((length, wide), lambda s, h: (s, h)),
@@ -340,29 +333,28 @@
             spec(LANES, LANES),
         ],
         out_specs=[
-            pl.BlockSpec((length, total), lambda s, h: (s, 0)),
+            pl.BlockSpec((length, wide), lambda s, h: (s, h)),
             part,
             part,
             part,
-            pl.BlockSpec((1, 1, LANES), lambda s, h: (s, 0, 0)),
+            pl.BlockSpec((length, LANES), lambda s, h: (s, 0)),
         ],
         out_shape=[
-            jax.ShapeDtypeStruct((rows, total), jnp.bfloat16),
+            jax.ShapeDtypeStruct((rows, 3 * LANES * heads_here), jnp.bfloat16),
             edge,
             edge,
             edge,
-            jax.ShapeDtypeStruct((seqs, 1, LANES), jnp.float32),
+            jax.ShapeDtypeStruct((rows, LANES), jnp.float32),
         ],
         scratch_shapes=[
             pltpu.VMEM((length + HALO, wide), jnp.float32),
             pltpu.VMEM((length + HALO, wide), jnp.float32),
-            pltpu.VMEM((length, LANES), jnp.float32),
         ],
         compiler_params=pltpu.CompilerParams(vmem_limit_bytes=VMEM_BYTES),
         cost_estimate=pl.CostEstimate(
             flops=60 * rows * heads_here * CHUNK * LANES, bytes_accessed=40 * rows * heads_here * LANES, transcendentals=0
         ),
-    )(pre, pre, bias, halo, conv, col, row, grad_mixed, inv, upd, states, start, end)
+    )(pre, logit, bias, halo, conv, col, row, grad_mixed, inv, upd, states, start, end)
 
 
 def mixed_rows_of(own, carry, start):
@@ -413,17 +405,19 @@
     )(own, carry, start, gain)
 
 
-def mixer_output_backward(own, carry, start, gain, grad, group):
+def mixer_output_backward(own, carry, start, gain, grad, first, group):
     seqs, heads_here = start.shape[:2]
     rows = own.shape[0]
     length = rows // seqs
     steps = heads_here // group
     flat = pl.BlockSpec((length, LANES * group), lambda s, h: (s, h))
+    base = first // group
+    shifted = pl.BlockSpec((length, LANES * group), lambda s, h: (s, base + h))
     square = pl.BlockSpec((1, group, LANES, LANES), lambda s, h: (s, h, 0, 0))
     return pl.pallas_call(
         functools.partial(output_backward_kernel, group),
         grid=(seqs, steps),
-        in_specs=[flat, flat, square, pl.BlockSpec((1, LANES), lambda s, h: (0, 0)), flat],
+        in_specs=[flat, flat, square, pl.BlockSpec((1, LANES), lambda s, h: (0, 0)), shifted],
         out_specs=[flat, square, pl.BlockSpec((1, 1, 1, LANES), lambda s, h: (s, h, 0, 0))],
         out_shape=[
             jax.ShapeDtypeStruct(own.shape, jnp.bfloat16),
@@ -437,6 +431,46 @@
     )(own, carry, start, gain, grad)
 
 
+def ffn_kernel(rows, grads, gate_w, up_w, down_w, hidden, grad_gate, grad_up, grad_rows, result):
+    gate = mul_nt(rows[...], gate_w[...])
+    up = mul_nt(rows[...], up_w[...])
+    grad_hidden = mul_nt(grads[...], down_w[...])
+    sigmoid = jax.nn.sigmoid(gate)
+    active = gate * sigmoid
+    kept = low(active * up)
+    back_gate = low(grad_hidden * up * sigmoid * (1.0 + gate * (1.0 - sigmoid)))
+    back_up = low(grad_hidden * active)
+    hidden[...] = kept
+    grad_gate[...] = back_gate
+    grad_up[...] = back_up
+    grad_rows[...] = low(mul_nn(back_gate, gate_w[...]) + mul_nn(back_up, up_w[...]))
+    result[...] = low(mul_nn(kept, down_w[...]))
+
+
+def ffn_both(rows, grads, weights):
+    count, width = rows.shape
+    units = weights.shape[0] // 3
+    tile = min(256, count)
+    wide = pl.BlockSpec((tile, width), lambda i: (i, 0))
+    narrow = pl.BlockSpec((tile, units), lambda i: (i, 0))
+
+    def third(index):
+        return pl.BlockSpec((units, width), lambda i: (index, 0))
+
+    return pl.pallas_call(
+        ffn_kernel,
+        grid=(count // tile,),
+        in_specs=[wide, wide, third(0), third(1), third(2)],
+        out_specs=[narrow, narrow, narrow, wide, wide],
+        out_shape=[jax.ShapeDtypeStruct((count, units), jnp.bfloat16)] * 3
+        + [jax.ShapeDtypeStruct((count, width), jnp.bfloat16)] * 2,
+        compiler_params=pltpu.CompilerParams(vmem_limit_bytes=VMEM_BYTES),
+        cost_estimate=pl.CostEstimate(
+            flops=12 * count * width * units, bytes_accessed=8 * count * width + 6 * units * width, transcendentals=0
+        ),
+    )(rows, grads, weights, weights, weights)
+
+
 def flip(value, axis, bit):
     devices = range(lax.axis_size(axis))
     return lax.ppermute(value, axis, [(i, i ^ bit) for i in devices])
@@ -447,94 +481,144 @@
     return lax.ppermute(value, axis, [(i, (i + distance) % count) for i in range(count)])
 
 
-def put(buffer, piece, index):
-    start = (index,) + (0,) * piece.ndim
-    return lax.dynamic_update_slice(buffer, piece[None], start)
-
-
-def after(value, *earlier):
+def from_behind(block, axis, distance):
+    devices = range(lax.axis_size(axis))
+    route = [(i - distance, i) for i in devices if i - distance in devices]
+    return lax.ppermute(block, axis, route)
+
+
+def tie(value, *earlier):
     return lax.optimization_barrier((value,) + earlier)[0]
 
 
+def put(buffer, piece, *start):
+    return lax.dynamic_update_slice(buffer, piece, start)
+
+
+def wide(value):
+    return value.astype(jnp.float32)
+
+
+def features(rows):
+    count, width = rows.shape
+    squares, lines = lax.axis_size("ctx"), lax.axis_size("fsdp")
+    part = width // (squares * lines)
+    order = rows.reshape(count, squares, lines, part).transpose(0, 2, 1, 3).reshape(count, width)
+    twice = jnp.concatenate([order, order], axis=1)
+    return lax.dynamic_slice_in_dim(twice, lax.axis_index("fsdp") * squares * part, width, 1)
+
+
+def features_back(rows):
+    count, width = rows.shape
+    squares, lines = lax.axis_size("ctx"), lax.axis_size("fsdp")
+    part = width // (squares * lines)
+    twice = jnp.concatenate([rows, rows], axis=1)
+    turn = (lines - lax.axis_index("fsdp")) % lines
+    order = lax.dynamic_slice_in_dim(twice, turn * squares * part, width, 1)
+    return order.reshape(count, lines, squares, part).transpose(0, 2, 1, 3).reshape(count, width)
+
+
 def gather_line(shard):
-    count, place = lax.axis_size("fsdp"), lax.axis_index("fsdp")
-    buffer = put(jnp.zeros((count,) + shard.shape, shard.dtype), shard, place)
-    for distance in range(1, count):
-        buffer = put(buffer, shift(shard, "fsdp", distance), (place - distance) % count)
-    return buffer.reshape(count * shard.shape[0], shard.shape[1])
-
-
-def gather_square(piece):
+    count = lax.axis_size("fsdp")
+    return jnp.stack([shard] + [shift(shard, "fsdp", count - r) for r in range(1, count)])
+
+
+class Square:
+    def __init__(self, own):
+        self.own = own
+        self.half = own.shape[0] // 2
+        self.beside = flip(own, "ctx", 1)
+        self.across = flip(own, "ctx", 2)
+
+    def forward(self, *earlier):
+        upper = self.beside[: self.half]
+        lower = self.across[self.half :]
+        if earlier:
+            upper, lower = lax.optimization_barrier((upper, lower) + earlier)[:2]
+        self.upper = flip(upper, "ctx", 2)
+        self.lower = flip(lower, "ctx", 1)
+        return self
+
+    def done(self):
+        return (self.upper, self.lower)
+
+    def weights(self):
+        lines, rows, columns = self.own.shape
+        place = lax.axis_index("ctx")
+        buffer = jnp.zeros((lines, 4, rows, columns), self.own.dtype)
+        buffer = put(buffer, self.own[:, None], 0, place, 0, 0)
+        buffer = put(buffer, self.beside[:, None], 0, place ^ 1, 0, 0)
+        buffer = put(buffer, self.across[:, None], 0, place ^ 2, 0, 0)
+        buffer = put(buffer, self.upper[:, None], 0, place ^ 3, 0, 0)
+        buffer = put(buffer, self.lower[:, None], self.half, place ^ 3, 0, 0)
+        return buffer.reshape(4 * lines * rows, columns)
+
+    def rows(self):
+        parts = [self.own, self.beside, self.across, self.upper, self.lower]
+        if lax.axis_size("tp") == 2:
+            return jnp.concatenate(parts + [flip(part, "tp", 1) for part in parts], axis=0)
+        return lax.all_gather(jnp.concatenate(parts, axis=0), "tp", axis=0, tiled=True)
+
+
+def square_sum(blocks):
+    from_across = flip(low(blocks(3, 0)), "ctx", 2)
+    from_beside = flip(low(blocks(3, 1)), "ctx", 1)
+    beside_down = flip(low(blocks(1, 1)), "ctx", 1)
+    across_up = flip(low(blocks(2, 0)), "ctx", 2)
+    beside_up = flip(low(blocks(1, 0) + wide(from_across)), "ctx", 1)
+    across_down = flip(low(blocks(2, 1) + wide(from_beside)), "ctx", 2)
+    upper = blocks(0, 0) + wide(beside_up) + wide(across_up)
+    lower = blocks(0, 1) + wide(beside_down) + wide(across_down)
+    return jnp.concatenate([upper, lower], axis=0)
+
+
+def collect_rows(partial):
+    count = lax.axis_size("tp")
+    size = partial.shape[0] // count
+    if count == 2:
+        total = wide(partial[:size]) + wide(flip(partial[size:], "tp", 1))
+    else:
+        total = wide(lax.psum_scatter(partial, "tp", scatter_dimension=0, tiled=True))
+    half = size // 8
+    return square_sum(lambda bit, low_half: total[(2 * bit + low_half) * half :][:half])
+
+
+def neighbour_columns(rows):
+    lines = lax.axis_size("fsdp")
+    count, width = rows.shape
+    split = rows.reshape(count, lines, 4, width // (4 * lines))
     place = lax.axis_index("ctx")
-    half = piece.shape[0] // 2
-    beside = flip(piece, "ctx", 1)
-    across = flip(piece, "ctx", 2)
-    upper = flip(beside[:half], "ctx", 2)
-    lower = flip(across[half:], "ctx", 1)
-    buffer = put(jnp.zeros((4,) + piece.shape, piece.dtype), piece, place)
-    buffer = put(buffer, beside, place ^ 1)
-    buffer = put(buffer, across, place ^ 2)
-    buffer = put(buffer, jnp.concatenate([upper, lower], axis=0), place ^ 3)
-    return buffer.reshape(4 * piece.shape[0], piece.shape[1])
-
-
-def gather_groups(shards):
-    if lax.axis_size("ctx") != 4:
-        return [lax.all_gather(shard, ("ctx", "fsdp"), axis=0, tiled=True) for shard in shards]
-    full = []
-    line = None
-    for shard in shards:
-        line = gather_line(shard if line is None else after(shard, line))
-        full.append(gather_square(line if not full else after(line, full[-1])))
-    return full
-
-
-def relative_columns(rows):
-    width = rows.shape[1] // 4
-    part = width // lax.axis_size("fsdp")
-    place, line = lax.axis_index("ctx"), lax.axis_index("fsdp")
-    blocks = []
+    return [
+        lax.dynamic_index_in_dim(split, place ^ bit, 2, keepdims=False).reshape(count, width // 4)
+        for bit in range(4)
+    ]
+
+
+def line_sum(own):
+    total = own[0]
+    for distance in range(1, own.shape[0]):
+        total = total + wide(shift(low(own[distance]), "fsdp", distance))
+    return total
+
+
+def outer_scatter(columns, grads):
+    half = columns[0].shape[1] // 2
+
+    def block(bit, low_half):
+        return outer_rows(columns[bit][:, low_half * half : (low_half + 1) * half], grads)
+
+    own = square_sum(block)
+    lines = lax.axis_size("fsdp")
+    return line_sum(own.reshape(lines, own.shape[0] // lines, own.shape[1]))
+
+
+def swap_square(pieces):
+    place = lax.axis_index("ctx")
+    arrived = jnp.zeros(pieces.shape, jnp.bfloat16)
     for bit in range(4):
-        block = lax.dynamic_slice_in_dim(rows, (place ^ bit) * width, width, 1)
-        twice = jnp.concatenate([block, block], axis=1)
-        blocks.append(lax.dynamic_slice_in_dim(twice, line * part, width, 1))
-    return blocks
-
-
-def outer_scatter(rows, grads, blocks=None):
-    if lax.axis_size("ctx") != 4:
-        return lax.psum_scatter(
-            outer_rows(rows, grads).astype(jnp.bfloat16), ("ctx", "fsdp"), scatter_dimension=0, tiled=True
-        ).astype(jnp.float32)
-    if blocks is None:
-        blocks = relative_columns(rows)
-    half = blocks[0].shape[1] // 2
-    low = jnp.bfloat16
-
-    def halves(bit):
-        block = blocks[bit]
-        return outer_rows(block[:, :half], grads), outer_rows(block[:, half:], grads)
-
-    diag_up, diag_down = halves(3)
-    from_across = flip(diag_up.astype(low), "ctx", 2)
-    from_beside = flip(diag_down.astype(low), "ctx", 1)
-    beside_up, beside_down = halves(1)
-    across_up, across_down = halves(2)
-    beside_down = flip(beside_down.astype(low), "ctx", 1)
-    across_up = flip(across_up.astype(low), "ctx", 2)
-    beside_up = flip((beside_up + from_across).astype(low), "ctx", 1)
-    across_down = flip((across_down + from_beside).astype(low), "ctx", 2)
-    own_up, own_down = halves(0)
-    own_up = own_up + beside_up + across_up
-    own_down = own_down + beside_down + across_down
-    count = lax.axis_size("fsdp")
-    part = 2 * half // count
-    own = jnp.concatenate([own_up, own_down], axis=0)
-    total = own[:part]
-    for distance in range(1, count):
-        piece = own[distance * part : (distance + 1) * part].astype(low)
-        total = total + shift(piece, "fsdp", distance)
-    return total
+        piece = low(lax.dynamic_index_in_dim(pieces, place ^ bit, 0))
+        arrived = put(arrived, flip(piece, "ctx", bit) if bit else piece, place ^ bit, 0, 0)
+    return arrived
 
 
 def butterfly(value, axes):
@@ -546,12 +630,6 @@
     return value
 
 
-def from_behind(block, axis, distance):
-    devices = range(lax.axis_size(axis))
-    route = [(i - distance, i) for i in devices if i - distance in devices]
-    return lax.ppermute(block, axis, route)
-
-
 def rms_scale(values, floor_value):
     return lax.rsqrt(jnp.mean(values * values, axis=-1, keepdims=True) + floor_value)
 
@@ -581,16 +659,26 @@
     )
 
 
-def heads_combine(partial_value):
-    part = low(partial_value)
+def rows_mine(rows):
+    count = rows.shape[1] // lax.axis_size("tp")
+    return lax.dynamic_slice_in_dim(rows, lax.axis_index("tp") * count, count, 1)
+
+
+def rows_scatter(partial):
     if lax.axis_size("tp") != 2:
-        return lax.psum(part, "tp").astype(jnp.float32)
-    return part.astype(jnp.float32) + flip(part, "tp", 1).astype(jnp.float32)
-
-
-def rows_own(held):
-    count = held.shape[0] // lax.axis_size("tp")
-    return lax.dynamic_slice_in_dim(held, lax.axis_index("tp") * count, count, 0)
+        return wide(lax.psum_scatter(partial, "tp", scatter_dimension=1, tiled=True))
+    count = partial.shape[1] // 2
+    other = lax.dynamic_slice_in_dim(partial, (1 - lax.axis_index("tp")) * count, count, 1)
+    return wide(rows_mine(partial)) + wide(flip(other, "tp", 1))
+
+
+def rows_full(mine):
+    if lax.axis_size("tp") != 2:
+        return lax.all_gather(mine, "tp", axis=1, tiled=True)
+    other = flip(mine, "tp", 1)
+    pair = jnp.concatenate([mine, other, mine], axis=1)
+    count = mine.shape[1]
+    return lax.dynamic_slice_in_dim(pair, lax.axis_index("tp") * count, 2 * count, 1)
 
 
 def by_head(parts):
@@ -603,6 +691,16 @@
     lead = joined.shape[:-1]
     split = joined.reshape(lead + (-1, 3, LANES))
     return [split[..., kind, :].reshape(lead + (-1,)) for kind in range(3)]
+
+
+def pass_states(own, transfer, forward):
+    rule = "shij,shjk->shik" if forward == 1 else "shji,shjk->shik"
+    leaving = own
+    entered = low(jnp.zeros_like(own))
+    for repeat in range(lax.axis_size("ctx") - 1):
+        entered = from_behind(low(leaving), "ctx", forward)
+        leaving = own + jnp.einsum(rule, transfer, entered, preferred_element_type=jnp.float32)
+    return wide(entered)
 
 
 def local(
@@ -627,114 +725,169 @@
     row_count = seq_count * local_len
     heads_here = beta_weight.shape[1]
     taps = conv_weight.shape[1]
-    group = 2 if heads_here % 2 == 0 else 1
-    hidden_cols = gate_weight.shape[1]
-    head_cols = 3 * heads_here * LANES
+    parts = 2 if heads_here % 2 == 0 else 1
+    part_heads = heads_here // parts
+    group = 2 if part_heads % 2 == 0 else 1
+    part_cols = 3 * part_heads * LANES
     spare = LANES - heads_here
-    mix_full, out_full, ffn_full, down_full = gather_groups(
-        [
-            jnp.concatenate(
-                [
-                    by_head([low(query_weight), low(key_weight), low(value_weight)]),
-                    jnp.pad(low(beta_weight), ((0, 0), (0, spare))),
-                ],
-                axis=1,
-            ),
-            low(out_weight).T,
-            jnp.concatenate([low(gate_weight), low(up_weight)], axis=1),
-            low(down_weight).T,
-        ]
-    )
+    units_here = gate_weight.shape[1]
+    shard_rows = gate_weight.shape[0]
+    seqs = range(seq_count)
+
+    joined = by_head([low(query_weight), low(key_weight), low(value_weight)])
+    shards = [joined[:, p * part_cols : (p + 1) * part_cols] for p in range(parts)]
+    shards[0] = jnp.concatenate([shards[0], jnp.pad(low(beta_weight), ((0, 0), (0, spare)))], axis=1)
+    shards.append(low(out_weight).T)
+    lines = []
+    for shard in shards:
+        lines.append(gather_line(tie(shard, lines[-1]) if lines else shard))
+    units = units_here // 4
+    pieces = jnp.stack([low(gate_weight).T, low(up_weight).T, low(down_weight)])
+    pieces = pieces.reshape(3, 4, units, shard_rows).transpose(1, 0, 2, 3)
+    ffn_line = swap_square(pieces.reshape(4, 3 * units, shard_rows))
+    ffn_line = ffn_line.transpose(1, 0, 2).reshape(3 * units, 4 * shard_rows)
+    ffn_parts = gather_line(tie(ffn_line, lines[-1]))
+
     first_pos = lax.axis_index("ctx") * local_len
     starts = doc_start - first_pos
     col, row = starts[:, :, None], starts[:, None, :]
     conv = by_head([conv_weight[0], conv_weight[1], conv_weight[2]])
     bias = jnp.pad(beta_bias, (0, spare))[None]
     gain_head = gain_o[None]
-
-    inputs = block_input.astype(jnp.float32).reshape(row_count, width)
-    scale_mix = rms_scale(inputs, EPSILON)
-    normed_mix = low(inputs * scale_mix * gain_mix)
-    pre = times(normed_mix, mix_full)
-    ends = pre.reshape(seq_count, local_len, -1)[:, local_len - HALO :, :head_cols]
-    halo = from_behind(ends, "ctx", 1)
-    own, carry, final, inverses, updates, states = mixer_forward(
-        pre, bias, halo, conv, col, row, taps, heads_here, group
-    )
-    transfer = low(final[..., LANES:])
-    entered = jnp.zeros_like(final[..., :LANES])
-    leaving = final[..., :LANES]
-    for repeat in range(lax.axis_size("ctx") - 1):
-        entered = from_behind(low(leaving), "ctx", 1)
-        leaving = final[..., :LANES] + jnp.einsum(
-            "shij,shjk->shik", transfer, entered, preferred_element_type=jnp.float32
+    gain_mix, gain_ffn = features(gain_mix[None]), features(gain_ffn[None])
+
+    tokens = features(block_input.reshape(row_count, width))
+    inputs = wide(tokens)
+    normed_mix = low(inputs * rms_scale(inputs, EPSILON) * gain_mix)
+    inputs_mine = wide(rows_mine(tokens.reshape(seq_count, local_len, width)))
+    grads_mine = rows_mine(features(out_grad.reshape(row_count, width)).reshape(seq_count, local_len, width))
+
+    square = Square(lines[0]).forward()
+    mix_full, kept, pre = [], [], []
+    for p in range(parts):
+        mix_full.append(square.weights())
+        square = Square(tie(lines[p + 1], *square.done()))
+        if p == parts - 1:
+            grad_squares = [Square(tie(grads_mine[0], mix_full[-1]))]
+        pre.append(times(normed_mix, mix_full[p]))
+        ends = pre[p].reshape(seq_count, local_len, -1)[:, local_len - HALO :, :part_cols]
+        halo = from_behind(ends, "ctx", 1)
+        convs = conv[:, p * part_cols : (p + 1) * part_cols]
+        kept.append(
+            [halo, convs]
+            + list(
+                mixer_forward(
+                    pre[p], pre[0], bias, halo, convs, col, row, taps, p * part_heads, part_heads, group
+                )
+            )
         )
-    entered = entered.astype(jnp.float32)
-    mixed_rows = mixer_output(own, carry, entered, gain_head, group)
-    residual = inputs + heads_combine(times_transposed(mixed_rows, out_full))
-    scale_ffn = rms_scale(residual, EPSILON)
-    normed_ffn = low(residual * scale_ffn * gain_ffn)
-
-    both = times(normed_ffn, ffn_full)
-    gate, up_val = both[:, :hidden_cols], both[:, hidden_cols:]
-    sigmoid_gate = jax.nn.sigmoid(gate)
-    activated = gate * sigmoid_gate
-    hidden = low(activated * up_val)
-    grad_rows = out_grad.reshape(row_count, width)
-    grad_hidden = times(grad_rows, down_full)
-    grad_gate = low(grad_hidden * up_val * sigmoid_gate * (1.0 + gate * (1.0 - sigmoid_gate)))
-    grad_up = low(grad_hidden * activated)
-    grad_both = jnp.concatenate([grad_gate, grad_up], axis=1)
-    grad_normed = heads_combine(times_transposed(grad_both, ffn_full))
-    output_held = low(residual + heads_combine(times_transposed(hidden, down_full)))
-    down_grad = outer_scatter(grad_rows, hidden).T
-    both_grad = outer_scatter(normed_ffn, grad_both)
-    gate_grad, up_grad = both_grad[:, :hidden_cols], both_grad[:, hidden_cols:]
-
-    back_ffn, unit_ffn = norm_backward(grad_normed, residual, scale_ffn, gain_ffn)
-    grad_residual = grad_rows.astype(jnp.float32) + back_ffn
-    gain_ffn_part = jnp.sum(rows_own(grad_normed * unit_ffn), axis=0)
-    grad_branch = low(grad_residual)
-    out_grad_w = outer_scatter(grad_branch, mixed_rows).T
+        square.forward(kept[p][2])
+    grad_squares[0].forward(kept[-1][2])
+    for s in seqs[1:]:
+        grad_squares.append(Square(tie(grads_mine[s], *grad_squares[-1].done())).forward())
+    out_full = square.weights()
+
+    entered, transfers, mixed_rows = [], [], []
+    for _, _, own, carry, final, _, _, _ in kept:
+        transfers.append(low(final[..., LANES:]))
+        entered.append(pass_states(final[..., :LANES], transfers[-1], 1))
+        mixed_rows.append(mixer_output(own, carry, entered[-1], gain_head, group))
+    mixed_rows = jnp.concatenate(mixed_rows, axis=1)
+
+    residual, scale_ffn, normed_ffn, squares = [], [], [], []
+    for s in seqs:
+        branch = times_transposed(mixed_rows[s * local_len : (s + 1) * local_len], out_full)
+        residual.append(inputs_mine[s] + rows_scatter(low(branch)[None])[0])
+        scale_ffn.append(rms_scale(residual[s], EPSILON))
+        squares.append(Square(low(residual[s] * scale_ffn[s] * gain_ffn)).forward())
+    ffn_parts = tie(ffn_parts, squares[0].own)
+    ffn_full = jnp.concatenate([ffn_parts[i] for i in range(ffn_parts.shape[0])], axis=1)
+    ffn_rows, grad_rows, ffn_out = [], [], []
+    for s in seqs:
+        ffn_rows.append(squares[s].rows())
+        grad_rows.append(grad_squares[s].rows())
+        ffn_out.append(ffn_both(ffn_rows[s], grad_rows[s], ffn_full))
+
+    grad_residual, grad_branch, gain_ffn_part = [], [], 0.0
+    for s in seqs:
+        grad_normed = collect_rows(ffn_out[s][3])
+        back_ffn, unit_ffn = norm_backward(grad_normed, residual[s], scale_ffn[s], gain_ffn)
+        grad_residual.append(wide(grads_mine[s]) + back_ffn)
+        gain_ffn_part = gain_ffn_part + jnp.sum(grad_normed * unit_ffn, axis=0)
+        grad_branch.append(rows_full(low(grad_residual[s])[None])[0])
+    grad_branch = jnp.concatenate(grad_branch, axis=0)
+    held = []
+    for s in seqs:
+        total = collect_rows(tie(ffn_out[s][4], grad_branch))
+        held.append(low(residual[s] + total))
+    block_output = features_back(rows_full(jnp.stack(held)).reshape(row_count, width))
+
     grad_heads = times(grad_branch, out_full)
-    grad_mixed, across, gain_o_part = mixer_output_backward(
-        own, carry, entered, gain_head, grad_heads, group
-    )
-    grad_end = jnp.zeros_like(across)
-    grad_now = across
-    for repeat in range(lax.axis_size("ctx") - 1):
-        grad_end = from_behind(low(grad_now), "ctx", -1)
-        grad_now = across + jnp.einsum(
-            "shji,shjk->shik", transfer, grad_end, preferred_element_type=jnp.float32
+    backs, acrosses, gain_o_part = [], [], 0.0
+    for p in range(parts):
+        _, _, own, carry, _, _, _, _ = kept[p]
+        back, across, gain_part = mixer_output_backward(
+            own, carry, entered[p], gain_head, grad_heads, p * part_heads, group
         )
-    grad_end = grad_end.astype(jnp.float32)
-    grad_mix, tail, before, conv_part, bias_part = mixer_backward(
-        pre, bias, halo, conv, col, row, grad_mixed, inverses, updates, states, entered, grad_end,
-        taps, heads_here, group,
-    )
-    tail = low(tail + from_behind(before, "ctx", -1))
-    grad_mix = lax.dynamic_update_slice(
-        grad_mix.reshape(seq_count, local_len, -1), tail, (0, local_len - HALO, 0)
-    ).reshape(row_count, -1)
-    mix_back = heads_combine(times_transposed(grad_mix, mix_full))
-    mix_grad = outer_scatter(normed_mix, grad_mix)
-    query_grad, key_grad, value_grad = by_kind(mix_grad[:, :head_cols])
-    beta_grad = mix_grad[:, head_cols : head_cols + heads_here]
-    back_mix, unit_mix = norm_backward(mix_back, inputs, scale_mix, gain_mix)
-    input_held = low(grad_residual + back_mix)
-    gain_mix_part = jnp.sum(rows_own(mix_back * unit_mix), axis=0)
-
+        backs.append(back)
+        acrosses.append(across)
+        gain_o_part = gain_o_part + jnp.sum(gain_part, axis=(0, 1, 2))
+    grad_end = pass_states(jnp.concatenate(acrosses, axis=1), jnp.concatenate(transfers, axis=1), -1)
+
+    sums = []
+    for kind, sources in ((1, ffn_rows), (2, ffn_rows), (0, grad_rows)):
+        total = 0.0
+        for s in seqs:
+            total = total + outer_rows(ffn_out[s][kind], sources[s])
+        count = lax.axis_size("fsdp")
+        sums.append(line_sum(jnp.stack([total[:, i * 4 * shard_rows : (i + 1) * 4 * shard_rows] for i in range(count)])))
+    sums = jnp.stack(sums).reshape(3 * units, 4, shard_rows).transpose(1, 0, 2)
+    arrived = swap_square(sums).reshape(4, 3, units, shard_rows)
+    gate_grad, up_grad, down_grad = (wide(arrived[:, i].reshape(units_here, shard_rows)) for i in range(3))
+
+    out_grad_w = outer_scatter(neighbour_columns(grad_branch), mixed_rows).T
+
+    columns = neighbour_columns(normed_mix)
+    mix_back, mix_grads, conv_parts = 0.0, [None] * parts, [None] * parts
+    logits = 0.0
+    for p in reversed(range(parts)):
+        halo, convs, own, carry, final, inverses, updates, states = kept[p]
+        heads = slice(p * part_heads, (p + 1) * part_heads)
+        grad_mix, tail, before, conv_parts[p], logit = mixer_backward(
+            pre[p], pre[0], bias, halo, convs, col, row, backs[p], inverses, updates, states,
+            entered[p], grad_end[:, heads], taps, p * part_heads, part_heads, group,
+        )
+        logits = logits + logit
+        tail = low(tail + from_behind(before, "ctx", -1))
+        grad_mix = put(grad_mix.reshape(seq_count, local_len, -1), tail, 0, local_len - HALO, 0)
+        grad_mix = grad_mix.reshape(row_count, -1)
+        if p == 0:
+            grad_mix = jnp.concatenate([grad_mix, low(logits)], axis=1)
+        mix_back = mix_back + times_transposed(grad_mix, mix_full[p])
+        mix_grads[p] = outer_scatter(columns, grad_mix)
+    joined = jnp.concatenate([grad[:, :part_cols] for grad in mix_grads], axis=1)
+    query_grad, key_grad, value_grad = by_kind(joined)
+    beta_grad = mix_grads[0][:, part_cols : part_cols + heads_here]
+
+    mix_back = rows_scatter(low(mix_back).reshape(seq_count, local_len, width))
+    back_mix, unit_mix = norm_backward(mix_back, inputs_mine, rms_scale(inputs_mine, EPSILON), gain_mix)
+    input_held = low(jnp.stack(grad_residual) + back_mix)
+    input_grad = features_back(rows_full(input_held).reshape(row_count, width))
+    gain_mix_part = jnp.sum(mix_back * unit_mix, axis=(0, 1))
+
+    gains = features_back(jnp.stack([gain_mix_part, gain_ffn_part]))
     small = butterfly(
-        jnp.concatenate([gain_mix_part, gain_ffn_part, jnp.sum(gain_o_part, axis=(0, 1, 2))]),
-        ("tp", "ctx", "fsdp"),
+        jnp.concatenate([gains[0], gains[1], gain_o_part]), ("tp", "ctx", "fsdp")
     )
     gain_mix_grad, gain_ffn_grad, gain_o_grad = jnp.split(small, [width, 2 * width])
-    conv_grad = butterfly(jnp.sum(conv_part, axis=0)[:taps], ("ctx", "fsdp"))
-    conv_grad = jnp.stack(by_kind(conv_grad))
-    bias_grad = butterfly(jnp.sum(bias_part, axis=(0, 1))[:heads_here], ("ctx", "fsdp"))
+    conv_cols = jnp.concatenate([jnp.sum(part, axis=0)[:taps] for part in conv_parts], axis=1)
+    sums = jnp.concatenate([conv_cols.reshape(-1), jnp.sum(logits, axis=0)])
+    sums = butterfly(sums, ("ctx", "fsdp"))
+    conv_grad = jnp.stack(by_kind(sums[:-LANES].reshape(taps, -1)))
+    bias_grad = sums[sums.shape[0] - LANES :][:heads_here]
     return (
-        output_held.reshape(seq_count, local_len, width),
-        input_held.reshape(seq_count, local_len, width),
+        block_output.reshape(seq_count, local_len, width),
+        input_grad.reshape(seq_count, local_len, width),
         gain_mix_grad,
         query_grad,
         key_grad,
@@ -745,8 +898,8 @@
         gain_o_grad,
         out_grad_w,
         gain_ffn_grad,
-        gate_grad,
-        up_grad,
+        gate_grad.T,
+        up_grad.T,
         down_grad,
     )
 

time: 1610 us -> 1610 us (level)
  waiting for transfers between devices: 689 us -> 473 us
  local copies, waits for them, and re-layouts: 148 us -> 305 us
  matrix products: 288 us -> 167 us
  Pallas kernels: 135 us -> 241 us
  starting transfers between devices: 205 us -> 253 us
  other arithmetic: 124 us -> 156 us
    ppermute x57 -> x116, waiting for transfers between devices: 593 us -> 295 us  [flip(): return lax.ppermute(value, axis, [(i, i ^ bit) for i in devices])]
    pallas_call x2 -> x6, Pallas kernels: 117 us -> 221 us  [the longest x2 98.9 us: ffn_both(): pl.pallas_call(ffn_kernel, grid=(count // tile,), in_specs=[wide, wide, t...]
    ppermute x24 -> x30, waiting for transfers between devices: 55.1 us -> 130 us  [shift(): lax.ppermute(value, axis, [(i, (i + distance) % count) for i in range(cou...]
    dot_general x4 -> x3, matrix products: 85 us -> 30.9 us  [times(): return jnp.dot(left, right, preferred_element_type=jnp.float32)]
    dot_general x4, matrix products: 77.1 us -> 24.5 us  [times_transposed(): lax.dot_general(left, right, (((1,), (1,)), ((), ())), preferred_element_...]
    another operation x4 -> x12, local copies, waits for them, and re-layouts: 0.04 us -> 50.8 us  [the longest x3 23.3 us: features(): rows.reshape(count, squares, lines, part).transpose(0, 2, 1, 3)]
    unnamed x139 -> x288, local copies, waits for them, and re-layouts: 24.3 us -> 70.9 us
    another operation x3 -> x15, other arithmetic: 6.19 us -> 52.5 us
  transfers between devices with their start and end apart: 89 -> 159, of which waited for: 38 -> 54; matrix products, arithmetic and copies ran while one was open for 27% -> 31% of each run, Pallas kernels for 8% -> 11%
where the time goes in v2:
time: 1610 us; the launch traced here: 1600 us
  waiting for transfers between devices  473 us (29%)
  local copies, waits for them, and re-layouts  305 us (19%)
  starting transfers between devices  253 us (16%)
  Pallas kernels  241 us (15%)
  matrix products  167 us (10%)
  other arithmetic  156 us (10%)
    ppermute x116, waiting for transfers between devices, flip(): return lax.ppermute(value, axis, [(i, i ^ bit) for i in devices])  295 us
    ppermute x30, waiting for transfers between devices, shift(): lax.ppermute(value, axis, [(i, (i + distance) % count) for i in range(cou...  130 us
    ppermute x30, starting transfers between devices, shift(): lax.ppermute(value, axis, [(i, (i + distance) % count) for i in range(cou...  113 us
    dot_general x30, matrix products, outer_rows(): lax.dot_general(left, right, (((0,), (0,)), ((), ())), preferred_element_...  107 us
    ppermute x116, starting transfers between devices, flip(): return lax.ppermute(value, axis, [(i, i ^ bit) for i in devices])  103 us
    pallas_call x2, Pallas kernels, ffn_both(): pl.pallas_call(ffn_kernel, grid=(count // tile,), in_specs=[wide, wide, t...  98.9 us
    unnamed x288, local copies, waits for them, and re-layouts  70.9 us
    pallas_call x2, Pallas kernels, mixer_backward(): pl.pallas_call(functools.partial(backward_kernel, taps, group, first), gr...  66.7 us
  transfers between devices with their start and end apart: 159, of which 54 were waited for; matrix products, arithmetic and copies ran while one was open for 31% of the time, Pallas kernels for 11%

profile of v2, /device:TPU:0, one launch (start us, length us, event | category | flops | bytes accessed | tf_op | source)
XLA Modules:
  0.0 1599.2 jit_solution(14711545624029934100)
XLA Ops:
  23.1 8.2 reshape_reshape.15
  31.4 7.4 copy.99
  51.8 7.7 reshape_reshape.16
  65.9 7.8 reshape.534
  118.3 11.7 collective-permute-done.12
  131.3 11.7 collective-permute-start.24
  190.1 13.4 fusion.171.pre.beta
  218.6 27.5 %shard_map.271 = (f32[1024,512]{1,0:T(8,128)}, bf16[1024,512]{1,0:T(8,128)(2,1)}, f32[2,4,128,256]{3,2,1,0:T(8,128)}, bf16[2,4,4,128,128]{4,3,2,1,0:T(8,128)(2,1...) custom-call(f32[1024,1664]{1,0:T(8,128)} %fusion.171.pre.beta, ...), custom_call_target="tpu_custom_call" | custom-call | flops 4026531840 | bytes 20971520 | tf_op jit(solution)/shard_map/pallas_call | solution.py:159
  278.9 10.4 fusion.172.pre
  300.0 27.5 %shard_map.273 = (f32[1024,512]{1,0:T(8,128)}, bf16[1024,512]{1,0:T(8,128)(2,1)}, f32[2,4,128,256]{3,2,1,0:T(8,128)}, bf16[2,4,4,128,128]{4,3,2,1,0:T(8,128)(2,1...) custom-call(f32[1024,1536]{1,0:T(8,128)} %copy-done.27, f32[1024,1664]{1,0:T(8,128)} %fusion.171.pre.beta, ...), custom_call_target="tpu_custom_call" | custom-call | flops 4026531840 | bytes 20971520 | tf_op jit(solution)/shard_map/pallas_call | solution.py:159
  363.0 29.2 %collective-permute-done.20 = bf16[2,4,128,128]{3,2,1,0:T(8,128)(2,1)S(1)} collective-permute-done((bf16[2,4,128,128]{3,2,1,0:T(8,128)(2,1)S(1)}, bf16[2,4,128,128]{3,2,1,0:T(8,128)(2,1)S(1)}, u32[]{:S(2)}, u32[]{:S(2)}) %collective-permute-start.20) | collective-permute-done | bytes 262176 | tf_op jit(solution)/shard_map/ppermute | solution.py:487
  426.3 12.3 collective-permute-done.41
  457.0 9.8 collective-permute-done.73
  467.9 7.0 collective-permute-done.72
  499.6 17.0 %collective-permute-done.63 = bf16[256,2048]{1,0:T(8,128)(2,1)S(1)} collective-permute-done((bf16[256,2048]{1,0:T(8,128)(2,1)S(1)}, bf16[256,2048]{1,0:T(8,128)(2,1)S(1)}, u32[]{:S(2)}, u32[]{:S(2)}) %collective-permute-start.63) | collective-permute-done | bytes 1048608 | tf_op jit(solution)/shard_map/ppermute | solution.py:476
  519.3 18.9 %collective-permute-done.30 = bf16[256,2048]{1,0:T(8,128)(2,1)S(1)} collective-permute-done((bf16[256,2048]{1,0:T(8,128)(2,1)S(1)}, bf16[256,2048]{1,0:T(8,128)(2,1)S(1)}, u32[]{:S(2)}, u32[]{:S(2)}) %collective-permute-start.30) | collective-permute-done | bytes 1048608 | tf_op jit(solution)/shard_map/ppermute | solution.py:476
  545.2 8.5 collective-permute-done.65
  558.7 8.6 collective-permute-done.32
  577.4 49.3 %shard_map.276 = (bf16[2048,704]{1,0:T(8,128)(2,1)}, bf16[2048,704]{1,0:T(8,128)(2,1)}, bf16[2048,704]{1,0:T(8,128)(2,1)}, bf16[2048,2048]{1,0:T(8,128)(2,1)}, bf16[2048,2048]{1,0:T(8,128)(2,1)}) custom-call(bf16[2048,2048]{1,0:T(8,128)(2,1)} %constant_dynamic-update-slice_fusion.20.rows, bf16[2048,2048]{1,0:T(8,128)(2,1)} %constant_dynamic-update-slice_fusion.30.grads, ...), custom_call_target="tpu_custom_call" | custom-call | flops 35433480192 | bytes 42205184 | tf_op jit(solution)/shard_map/pallas_call | solution.py:460
  626.8 11.3 fusion.175
  639.8 49.6 %shard_map.275 = (bf16[2048,704]{1,0:T(8,128)(2,1)}, bf16[2048,704]{1,0:T(8,128)(2,1)}, bf16[2048,704]{1,0:T(8,128)(2,1)}, bf16[2048,2048]{1,0:T(8,128)(2,1)}, bf16[2048,2048]{1,0:T(8,128)(2,1)}) custom-call(bf16[2048,2048]{1,0:T(8,128)(2,1)} %constant_dynamic-update-slice_fusion.rows, bf16[2048,2048]{1,0:T(8,128)(2,1)} %constant_dynamic-update-slice_fusion.10.grads, ...), custom_call_target="tpu_custom_call" | custom-call | flops 35433480192 | bytes 42205184 | tf_op jit(solution)/shard_map/pallas_call | solution.py:460
  689.4 12.1 fusion.168
  705.6 9.4 fusion.173
  715.0 8.9 fusion.174
  724.0 10.4 fusion.169
  739.5 10.5 fusion.170
  753.6 30.9 %collective-permute-done.154 = bf16[704,512]{1,0:T(8,128)(2,1)S(1)} collective-permute-done((bf16[704,512]{1,0:T(8,128)(2,1)S(1)}, bf16[704,512]{1,0:T(8,128)(2,1)S(1)}, u32[]{:S(2)}, u32[]{:S(2)}) %collective-permute-start.154) | collective-permute-done | bytes 720928 | tf_op jit(solution)/shard_map/ppermute | solution.py:481
  784.5 15.1 collective-permute-start.149
  799.6 38.2 %collective-permute-start.148 = (bf16[704,512]{1,0:T(8,128)(2,1)}, bf16[704,512]{1,0:T(8,128)(2,1)}, u32[]{:S(2)}, u32[]{:S(2)}) collective-permute-start(bf16[704,512]{1,0:T(8,128)(2,1)} %get-tuple-element.255), channel_id=1, source_target_pairs={{0,2},{1,3},{2,0},{3,1},{4,6},{5,7},{6,4},{7,5},{8,10},{9,11},{10,... | collective-permute-start | bytes 2162696 | tf_op jit(solution)/shard_map/ppermute | solution.py:481
  851.4 9.5 collective-permute-done.151
  863.1 27.7 %collective-permute-done.148 = bf16[704,512]{1,0:T(8,128)(2,1)} collective-permute-done((bf16[704,512]{1,0:T(8,128)(2,1)}, bf16[704,512]{1,0:T(8,128)(2,1)}, u32[]{:S(2)}, u32[]{:S(2)}) %collective-permute-start.148) | collective-permute-done | bytes 720928 | tf_op jit(solution)/shard_map/ppermute | solution.py:481
  901.3 11.3 constant_dynamic-slice_fusion.2
  916.9 11.1 collective-permute-done.156
  928.1 9.7 collective-permute-done.158
  950.1 8.9 fusion.138
  965.2 15.8 collective-permute-done.82
  988.6 18.7 %collective-permute-done.56 = bf16[128,2048]{1,0:T(8,128)(2,1)S(1)} collective-permute-done((bf16[128,2048]{1,0:T(8,128)(2,1)S(1)}, bf16[128,2048]{1,0:T(8,128)(2,1)S(1)}, u32[]{:S(2)}, u32[]{:S(2)}) %collective-permute-start.56) | collective-permute-done | bytes 524320 | tf_op jit(solution)/shard_map/ppermute | solution.py:476
  1041.7 7.1 fusion.142.grad
  1096.9 11.4 collective-permute-done.138
  1109.0 11.3 collective-permute-start.139
  1121.1 7.5 collective-permute-done.105
  1130.3 9.6 collective-permute-done.139
  1151.2 33.3 %shard_map.279 = (bf16[1024,1536]{1,0:T(8,128)(2,1)}, f32[2,8,1536]{2,1,0:T(8,128)}, f32[2,8,1536]{2,1,0:T(8,128)}, f32[2,8,1536]{2,1,0:T(8,128)}, f32[1024,128]{1,0:T(8,128)}) custom-call(f32[1024,1536]{1,0:T(8,128)} %copy-done.27, f32[1024,1664]{1,0:T(8,128)} %fusion.171.pre.beta, f32[1,128]{1,0:T(1,128)} %pad_bitcast_fusion.bias, ...), custom_call_target="tpu_custom_call" | custom-call | flops 4026531840 | bytes 20971520 | tf_op jit(solution)/shard_map/pallas_call | solution.py:317
  1185.4 33.3 %shard_map.280 = (bf16[1024,1536]{1,0:T(8,128)(2,1)}, f32[2,8,1536]{2,1,0:T(8,128)}, f32[2,8,1536]{2,1,0:T(8,128)}, f32[2,8,1536]{2,1,0:T(8,128)}, f32[1024,128]{1,0:T(8,128)}) custom-call(f32[1024,1664]{1,0:T(8,128)} %fusion.171.pre.beta, f32[1024,1664]{1,0:T(8,128)} %fusion.171.pre.beta, f32[1,128]{1,0:T(1,128)} %pad_bitcast_fusion.bias, ...), custom_call_target="tpu_custom_call" | custom-call | flops 4026531840 | bytes 20971520 | tf_op jit(solution)/shard_map/pallas_call | solution.py:317
  1252.2 10.1 fusion.143
  1271.1 9.6 add_convert_fusion
  1291.2 15.4 collective-permute-done.130
  1308.8 16.1 %collective-permute-done.121 = bf16[256,1664]{1,0:T(8,128)(2,1)} collective-permute-done((bf16[256,1664]{1,0:T(8,128)(2,1)}, bf16[256,1664]{1,0:T(8,128)(2,1)}, u32[]{:S(2)}, u32[]{:S(2)}) %collective-permute-start.121) | collective-permute-done | bytes 852000 | tf_op jit(solution)/shard_map/ppermute | solution.py:476
  1330.5 8.3 collective-permute-done.126
  1341.1 16.5 %collective-permute-done.131 = bf16[256,1536]{1,0:T(8,128)(2,1)S(1)} collective-permute-done((bf16[256,1536]{1,0:T(8,128)(2,1)S(1)}, bf16[256,1536]{1,0:T(8,128)(2,1)S(1)}, u32[]{:S(2)}, u32[]{:S(2)}) %collective-permute-start.131) | collective-permute-done | bytes 786464 | tf_op jit(solution)/shard_map/ppermute | solution.py:476
  1361.4 13.2 collective-permute-done.117
  1388.1 8.9 fusion.140
  1402.1 8.0 fusion.139
  1415.5 18.9 %collective-permute-done.90 = bf16[128,2048]{1,0:T(8,128)(2,1)S(1)} collective-permute-done((bf16[128,2048]{1,0:T(8,128)(2,1)S(1)}, bf16[128,2048]{1,0:T(8,128)(2,1)S(1)}, u32[]{:S(2)}, u32[]{:S(2)}) %collective-permute-start.90) | collective-permute-done | bytes 524320 | tf_op jit(solution)/shard_map/ppermute | solution.py:476
  1438.8 10.4 collective-permute-done.98
  1453.4 7.1 collective-permute-done.93
  1462.5 7.3 collective-permute-done.91
  1477.2 10.3 collective-permute-start.124
  1489.7 23.2 %collective-permute-done.123 = bf16[128,1664]{1,0:T(8,128)(2,1)S(1)} collective-permute-done((bf16[128,1664]{1,0:T(8,128)(2,1)S(1)}, bf16[128,1664]{1,0:T(8,128)(2,1)S(1)}, u32[]{:S(2)}, u32[]{:S(2)}) %collective-permute-start.123) | collective-permute-done | bytes 426016 | tf_op jit(solution)/shard_map/ppermute | solution.py:481
  1512.9 9.0 collective-permute-done.124
  1561.1 7.9 copy.138
  1569.0 7.8 reshape_reshape.18
  1583.3 7.9 copy.132
  1591.2 7.8 reshape_reshape.17
  (832 shorter events, 655.4 us)
Async XLA Ops:
  6.9 81.9 %collective-permute-start.1 = (bf16[128,1664]{0,1:T(8,128)(2,1)}, bf16[128,1664]{0,1:T(8,128)(2,1)S(1)}, u32[]{:S(2)}, u32[]{:S(2)}) collective-permute-start(bf16[128,1664]{0,1:T(8,128)(2,1)} %get-tuple-element.291), channel_id=1, source_target_pairs={{0,2},{1,3},{2,0},{3,1},{4,6},{5,7},{6,4},{7,5},{8,10},{9,11},{10,... | collective-permute-start | bytes 1277960 | tf_op jit(solution)/shard_map/ppermute | solution.py:481
  11.0 78.4 %collective-permute-start = (bf16[128,1664]{0,1:T(8,128)(2,1)}, bf16[128,1664]{0,1:T(8,128)(2,1)}, u32[]{:S(2)}, u32[]{:S(2)}) collective-permute-start(bf16[128,1664]{0,1:T(8,128)(2,1)} %get-tuple-element.291), channel_id=1, source_target_pairs={{0,3},{1,0},{2,1},{3,2},{4,7},{5,4},{6,5},{7,6},{8,11},{9,8},{10,9... | collective-permute-start | bytes 1277960 | tf_op jit(solution)/shard_map/ppermute | solution.py:481
  12.3 77.0 %collective-permute-start.2 = (bf16[128,1664]{0,1:T(8,128)(2,1)}, bf16[128,1664]{0,1:T(8,128)(2,1)}, u32[]{:S(2)}, u32[]{:S(2)}) collective-permute-start(bf16[128,1664]{0,1:T(8,128)(2,1)} %get-tuple-element.291), channel_id=1, source_target_pairs={{0,1},{1,2},{2,3},{3,0},{4,5},{5,6},{6,7},{7,4},{8,9},{9,10},{10,1... | collective-permute-start | bytes 1277960 | tf_op jit(solution)/shard_map/ppermute | solution.py:481
  19.8 87.1 %collective-permute-start.50 = (bf16[1,2112,128]{2,1,0:T(8,128)(2,1)}, bf16[1,2112,128]{2,1,0:T(8,128)(2,1)}, u32[]{:S(2)}, u32[]{:S(2)}) collective-permute-start(bf16[1,2112,128]{2,1,0:T(8,128)(2,1)} %get-tuple-element.265), channel_id=1, source_target_pairs={{0,24},{8,16},{16,8},{24,0},{1,25},{9,17},{17,9},{25,1},{2,26},{10... | collective-permute-start | bytes 1622024 | tf_op jit(solution)/shard_map/ppermute | solution.py:476
  22.3 87.0 %collective-permute-start.49 = (bf16[1,2112,128]{2,1,0:T(8,128)(2,1)}, bf16[1,2112,128]{2,1,0:T(8,128)(2,1)}, u32[]{:S(2)}, u32[]{:S(2)}) collective-permute-start(bf16[1,2112,128]{2,1,0:T(8,128)(2,1)} %get-tuple-element.266), channel_id=1, source_target_pairs={{0,16},{8,24},{16,0},{24,8},{1,17},{9,25},{17,1},{25,9},{2,18},{10... | collective-permute-start | bytes 1622024 | tf_op jit(solution)/shard_map/ppermute | solution.py:476
  92.0 53.6 %collective-permute-start.4 = (bf16[4,128,1664]{1,2,0:T(8,128)(2,1)}, bf16[4,128,1664]{1,2,0:T(8,128)(2,1)}, u32[]{:S(2)}, u32[]{:S(2)}) collective-permute-start(bf16[4,128,1664]{1,2,0:T(8,128)(2,1)} %get-tuple-element.270), channel_id=1, source_target_pairs={{0,16},{8,24},{16,0},{24,8},{1,17},{9,25},{17,1},{25,9},{2,18},{10... | collective-permute-start | bytes 5111816 | tf_op jit(solution)/shard_map/ppermute | solution.py:476
  93.5 54.7 %collective-permute-start.3 = (bf16[4,128,1664]{1,2,0:T(8,128)(2,1)}, bf16[4,128,1664]{1,2,0:T(8,128)(2,1)}, u32[]{:S(2)}, u32[]{:S(2)}) collective-permute-start(bf16[4,128,1664]{1,2,0:T(8,128)(2,1)} %get-tuple-element.270), channel_id=1, source_target_pairs={{0,8},{8,0},{16,24},{24,16},{1,9},{9,1},{17,25},{25,17},{2,10},{10... | collective-permute-start | bytes 5111816 | tf_op jit(solution)/shard_map/ppermute | solution.py:476
  147.7 34.3 %collective-permute-start.6 = (bf16[2,128,1664]{1,2,0:T(8,128)(2,1)}, bf16[2,128,1664]{1,2,0:T(8,128)(2,1)S(1)}, u32[]{:S(2)}, u32[]{:S(2)}) collective-permute-start(bf16[2,128,1664]{1,2,0:T(8,128)(2,1)} %slice.669), channel_id=1, source_target_pairs={{0,8},{8,0},{16,24},{24,16},{1,9},{9,1},{17,25},{25,17},{2,10},{10... | collective-permute-start | bytes 2555912 | tf_op jit(solution)/shard_map/ppermute | solution.py:476
  161.2 181.9 %collective-permute-start.53 = (bf16[2112,512]{1,0:T(8,128)(2,1)S(1)}, bf16[2112,512]{1,0:T(8,128)(2,1)}, u32[]{:S(2)}, u32[]{:S(2)}) collective-permute-start(bf16[2112,512]{1,0:T(8,128)(2,1)S(1)} %copy_bitcast_fusion), channel_id=1, source_target_pairs={{0,1},{1,2},{2,3},{3,0},{4,5},{5,6},{6,7},{7,4},{8,9},{9,10},{10,1... | collective-permute-start | bytes 6488072 | tf_op jit(solution)/shard_map/ppermute | solution.py:481
  167.0 177.6 %collective-permute-start.52 = (bf16[2112,512]{1,0:T(8,128)(2,1)S(1)}, bf16[2112,512]{1,0:T(8,128)(2,1)}, u32[]{:S(2)}, u32[]{:S(2)}) collective-permute-start(bf16[2112,512]{1,0:T(8,128)(2,1)S(1)} %copy_bitcast_fusion), channel_id=1, source_target_pairs={{0,2},{1,3},{2,0},{3,1},{4,6},{5,7},{6,4},{7,5},{8,10},{9,11},{10,... | collective-permute-start | bytes 6488072 | tf_op jit(solution)/shard_map/ppermute | solution.py:481
  181.9 64.2 %collective-permute-start.15 = (bf16[4,128,1536]{1,2,0:T(8,128)(2,1)}, bf16[4,128,1536]{1,2,0:T(8,128)(2,1)}, u32[]{:S(2)}, u32[]{:S(2)}) collective-permute-start(bf16[4,128,1536]{1,2,0:T(8,128)(2,1)} %pad_maximum_fusion.10), channel_id=1, source_target_pairs={{0,16},{8,24},{16,0},{24,8},{1,17},{9,25},{17,1},{25,9},{2,18},{10... | collective-permute-start | bytes 4718600 | tf_op jit(solution)/shard_map/ppermute | solution.py:476
  182.7 65.4 %collective-permute-start.14 = (bf16[4,128,1536]{1,2,0:T(8,128)(2,1)}, bf16[4,128,1536]{1,2,0:T(8,128)(2,1)}, u32[]{:S(2)}, u32[]{:S(2)}) collective-permute-start(bf16[4,128,1536]{1,2,0:T(8,128)(2,1)} %pad_maximum_fusion.10), channel_id=1, source_target_pairs={{0,8},{8,0},{16,24},{24,16},{1,9},{9,1},{17,25},{25,17},{2,10},{10... | collective-permute-start | bytes 4718600 | tf_op jit(solution)/shard_map/ppermute | solution.py:476
  218.0 128.7 %collective-permute-start.51 = (bf16[2112,512]{1,0:T(8,128)(2,1)S(1)}, bf16[2112,512]{1,0:T(8,128)(2,1)}, u32[]{:S(2)}, u32[]{:S(2)}) collective-permute-start(bf16[2112,512]{1,0:T(8,128)(2,1)S(1)} %copy_bitcast_fusion), channel_id=1, source_target_pairs={{0,3},{1,0},{2,1},{3,2},{4,7},{5,4},{6,5},{7,6},{8,11},{9,8},{10,9... | collective-permute-start | bytes 6488072 | tf_op jit(solution)/shard_map/ppermute | solution.py:481
  296.4 37.5 %collective-permute-start.9 = (bf16[2,4,128,128]{3,2,1,0:T(8,128)(2,1)S(1)}, bf16[2,4,128,128]{3,2,1,0:T(8,128)(2,1)S(1)}, u32[]{:S(2)}, u32[]{:S(2)}) collective-permute-start(bf16[2,4,128,128]{3,2,1,0:T(8,128)(2,1)S(1)} %fusion.50), channel_id=1, source_target_pairs={{0,8},{8,16},{16,24},{1,9},{9,17},{17,25},{2,10},{10,18},{18,26},{... | collective-permute-start | bytes 786440 | tf_op jit(solution)/shard_map/ppermute | solution.py:487
  340.9 66.3 %collective-permute-start.40 = (bf16[256,2048]{1,0:T(8,128)(2,1)}, bf16[256,2048]{1,0:T(8,128)(2,1)}, u32[]{:S(2)}, u32[]{:S(2)}) collective-permute-start(bf16[256,2048]{1,0:T(8,128)(2,1)} %get-tuple-element.83), channel_id=1, source_target_pairs={{0,16},{8,24},{16,0},{24,8},{1,17},{9,25},{17,1},{25,9},{2,18},{10... | collective-permute-start | bytes 3145736 | tf_op jit(solution)/shard_map/ppermute | solution.py:476
  343.1 65.2 %collective-permute-start.39 = (bf16[256,2048]{1,0:T(8,128)(2,1)}, bf16[256,2048]{1,0:T(8,128)(2,1)}, u32[]{:S(2)}, u32[]{:S(2)}) collective-permute-start(bf16[256,2048]{1,0:T(8,128)(2,1)} %get-tuple-element.83), channel_id=1, source_target_pairs={{0,8},{8,0},{16,24},{24,16},{1,9},{9,1},{17,25},{25,17},{2,10},{10... | collective-permute-start | bytes 3145736 | tf_op jit(solution)/shard_map/ppermute | solution.py:476
  344.6 64.8 %collective-permute-start.26 = (bf16[4,128,1024]{2,1,0:T(8,128)(2,1)}, bf16[4,128,1024]{2,1,0:T(8,128)(2,1)}, u32[]{:S(2)}, u32[]{:S(2)}) collective-permute-start(bf16[4,128,1024]{2,1,0:T(8,128)(2,1)} %pad_maximum_fusion.12), channel_id=1, source_target_pairs={{0,16},{8,24},{16,0},{24,8},{1,17},{9,25},{17,1},{25,9},{2,18},{10... | collective-permute-start | bytes 3145736 | tf_op jit(solution)/shard_map/ppermute | solution.py:476
  346.7 63.8 %collective-permute-start.25 = (bf16[4,128,1024]{2,1,0:T(8,128)(2,1)}, bf16[4,128,1024]{2,1,0:T(8,128)(2,1)}, u32[]{:S(2)}, u32[]{:S(2)}) collective-permute-start(bf16[4,128,1024]{2,1,0:T(8,128)(2,1)} %pad_maximum_fusion.12), channel_id=1, source_target_pairs={{0,8},{8,0},{16,24},{24,16},{1,9},{9,1},{17,25},{25,17},{2,10},{10... | collective-permute-start | bytes 3145736 | tf_op jit(solution)/shard_map/ppermute | solution.py:476
  346.8 45.5 %collective-permute-start.20 = (bf16[2,4,128,128]{3,2,1,0:T(8,128)(2,1)S(1)}, bf16[2,4,128,128]{3,2,1,0:T(8,128)(2,1)S(1)}, u32[]{:S(2)}, u32[]{:S(2)}) collective-permute-start(bf16[2,4,128,128]{3,2,1,0:T(8,128)(2,1)S(1)} %fusion.52), channel_id=1, source_target_pairs={{0,8},{8,16},{16,24},{1,9},{9,17},{17,25},{2,10},{10,18},{18,26},{... | collective-permute-start | bytes 786440 | tf_op jit(solution)/shard_map/ppermute | solution.py:487
  401.8 47.0 %collective-permute-start.43 = (bf16[256,2048]{1,0:T(8,128)(2,1)S(1)}, bf16[256,2048]{1,0:T(8,128)(2,1)}, u32[]{:S(2)}, u32[]{:S(2)}) collective-permute-start(bf16[256,2048]{1,0:T(8,128)(2,1)S(1)} %copy-done.36), channel_id=1, source_target_pairs={{0,4},{4,0},{1,5},{5,1},{2,6},{6,2},{3,7},{7,3},{8,12},{12,8},{9,1... | collective-permute-start | bytes 3145736 | tf_op jit(solution)/shard_map/ppermute | solution.py:476
  455.7 38.1 %collective-permute-start.76 = (bf16[256,2048]{1,0:T(8,128)(2,1)S(1)}, bf16[256,2048]{1,0:T(8,128)(2,1)S(1)}, u32[]{:S(2)}, u32[]{:S(2)}) collective-permute-start(bf16[256,2048]{1,0:T(8,128)(2,1)S(1)} %copy-done.35), channel_id=1, source_target_pairs={{0,4},{4,0},{1,5},{5,1},{2,6},{6,2},{3,7},{7,3},{8,12},{12,8},{9,1... | collective-permute-start | bytes 3145736 | tf_op jit(solution)/shard_map/ppermute | solution.py:476
  493.8 44.4 %collective-permute-start.30 = (bf16[256,2048]{1,0:T(8,128)(2,1)S(1)}, bf16[256,2048]{1,0:T(8,128)(2,1)S(1)}, u32[]{:S(2)}, u32[]{:S(2)}) collective-permute-start(bf16[256,2048]{1,0:T(8,128)(2,1)S(1)} %get-tuple-element.304), channel_id=1, source_target_pairs={{0,8},{8,0},{16,24},{24,16},{1,9},{9,1},{17,25},{25,17},{2,10},{10... | collective-permute-start | bytes 3145736 | tf_op jit(solution)/shard_map/ppermute | solution.py:476
  496.1 43.3 %collective-permute-start.31 = (bf16[256,2048]{1,0:T(8,128)(2,1)S(1)}, bf16[256,2048]{1,0:T(8,128)(2,1)S(1)}, u32[]{:S(2)}, u32[]{:S(2)}) collective-permute-start(bf16[256,2048]{1,0:T(8,128)(2,1)S(1)} %get-tuple-element.304), channel_id=1, source_target_pairs={{0,16},{8,24},{16,0},{24,8},{1,17},{9,25},{17,1},{25,9},{2,18},{10... | collective-permute-start | bytes 3145736 | tf_op jit(solution)/shard_map/ppermute | solution.py:476
  498.6 58.5 %collective-permute-start.67 = (bf16[256,2048]{1,0:T(8,128)(2,1)S(1)}, bf16[256,2048]{1,0:T(8,128)(2,1)S(1)}, u32[]{:S(2)}, u32[]{:S(2)}) collective-permute-start(bf16[256,2048]{1,0:T(8,128)(2,1)S(1)} %get-tuple-element.182), channel_id=1, source_target_pairs={{0,4},{4,0},{1,5},{5,1},{2,6},{6,2},{3,7},{7,3},{8,12},{12,8},{9,1... | collective-permute-start | bytes 3145736 | tf_op jit(solution)/shard_map/ppermute | solution.py:476
  516.6 52.9 %collective-permute-start.34 = (bf16[256,2048]{1,0:T(8,128)(2,1)S(1)}, bf16[256,2048]{1,0:T(8,128)(2,1)S(1)}, u32[]{:S(2)}, u32[]{:S(2)}) collective-permute-start(bf16[256,2048]{1,0:T(8,128)(2,1)S(1)} %get-tuple-element.304), channel_id=1, source_target_pairs={{0,4},{4,0},{1,5},{5,1},{2,6},{6,2},{3,7},{7,3},{8,12},{12,8},{9,1... | collective-permute-start | bytes 3145736 | tf_op jit(solution)/shard_map/ppermute | solution.py:476
  572.0 66.9 %collective-permute-start.38 = (bf16[128,2048]{1,0:T(8,128)(2,1)S(1)}, bf16[128,2048]{1,0:T(8,128)(2,1)S(1)}, u32[]{:S(2)}, u32[]{:S(2)}) collective-permute-start(bf16[128,2048]{1,0:T(8,128)(2,1)S(1)} %collective-permute-done.33), channel_id=1, source_target_pairs={{0,4},{4,0},{1,5},{5,1},{2,6},{6,2},{3,7},{7,3},{8,12},{12,8},{9,1... | collective-permute-start | bytes 1572872 | tf_op jit(solution)/shard_map/ppermute | solution.py:476
  573.1 64.9 %collective-permute-start.37 = (bf16[128,2048]{1,0:T(8,128)(2,1)S(1)}, bf16[128,2048]{1,0:T(8,128)(2,1)S(1)}, u32[]{:S(2)}, u32[]{:S(2)}) collective-permute-start(bf16[128,2048]{1,0:T(8,128)(2,1)S(1)} %collective-permute-done.32), channel_id=1, source_target_pairs={{0,4},{4,0},{1,5},{5,1},{2,6},{6,2},{3,7},{7,3},{8,12},{12,8},{9,1... | collective-permute-start | bytes 1572872 | tf_op jit(solution)/shard_map/ppermute | solution.py:476
  701.7 48.3 %collective-permute-start.153 = (bf16[704,512]{1,0:T(8,128)(2,1)S(1)}, bf16[704,512]{1,0:T(8,128)(2,1)S(1)}, u32[]{:S(2)}, u32[]{:S(2)}) collective-permute-start(bf16[704,512]{1,0:T(8,128)(2,1)S(1)} %get-tuple-element.259), channel_id=1, source_target_pairs={{0,1},{1,2},{2,3},{3,0},{4,5},{5,6},{6,7},{7,4},{8,9},{9,10},{10,1... | collective-permute-start | bytes 2162696 | tf_op jit(solution)/shard_map/ppermute | solution.py:481
  702.7 50.9 %collective-permute-start.155 = (bf16[704,512]{1,0:T(8,128)(2,1)S(1)}, bf16[704,512]{1,0:T(8,128)(2,1)S(1)}, u32[]{:S(2)}, u32[]{:S(2)}) collective-permute-start(bf16[704,512]{1,0:T(8,128)(2,1)S(1)} %get-tuple-element.260), channel_id=1, source_target_pairs={{0,3},{1,0},{2,1},{3,2},{4,7},{5,4},{6,5},{7,6},{8,11},{9,8},{10,9... | collective-permute-start | bytes 2162696 | tf_op jit(solution)/shard_map/ppermute | solution.py:481
  705.6 79.0 %collective-permute-start.154 = (bf16[704,512]{1,0:T(8,128)(2,1)S(1)}, bf16[704,512]{1,0:T(8,128)(2,1)S(1)}, u32[]{:S(2)}, u32[]{:S(2)}) collective-permute-start(bf16[704,512]{1,0:T(8,128)(2,1)S(1)} %get-tuple-element.261), channel_id=1, source_target_pairs={{0,2},{1,3},{2,0},{3,1},{4,6},{5,7},{6,4},{7,5},{8,10},{9,11},{10,... | collective-permute-start | bytes 2162696 | tf_op jit(solution)/shard_map/ppermute | solution.py:481
  735.7 64.0 %collective-permute-start.150 = (bf16[704,512]{1,0:T(8,128)(2,1)S(1)}, bf16[704,512]{1,0:T(8,128)(2,1)S(1)}, u32[]{:S(2)}, u32[]{:S(2)}) collective-permute-start(bf16[704,512]{1,0:T(8,128)(2,1)S(1)} %get-tuple-element.256), channel_id=1, source_target_pairs={{0,1},{1,2},{2,3},{3,0},{4,5},{5,6},{6,7},{7,4},{8,9},{9,10},{10,1... | collective-permute-start | bytes 2162696 | tf_op jit(solution)/shard_map/ppermute | solution.py:481
  736.2 115.1 %collective-permute-start.152 = (bf16[704,512]{1,0:T(8,128)(2,1)}, bf16[704,512]{1,0:T(8,128)(2,1)}, u32[]{:S(2)}, u32[]{:S(2)}) collective-permute-start(bf16[704,512]{1,0:T(8,128)(2,1)} %get-tuple-element.257), channel_id=1, source_target_pairs={{0,3},{1,0},{2,1},{3,2},{4,7},{5,4},{6,5},{7,6},{8,11},{9,8},{10,9... | collective-permute-start | bytes 2162696 | tf_op jit(solution)/shard_map/ppermute | solution.py:481
  750.0 110.9 %collective-permute-start.151 = (bf16[704,512]{1,0:T(8,128)(2,1)}, bf16[704,512]{1,0:T(8,128)(2,1)}, u32[]{:S(2)}, u32[]{:S(2)}) collective-permute-start(bf16[704,512]{1,0:T(8,128)(2,1)} %get-tuple-element.258), channel_id=1, source_target_pairs={{0,2},{1,3},{2,0},{3,1},{4,6},{5,7},{6,4},{7,5},{8,10},{9,11},{10,... | collective-permute-start | bytes 2162696 | tf_op jit(solution)/shard_map/ppermute | solution.py:481
  753.6 109.5 %collective-permute-start.147 = (bf16[704,512]{1,0:T(8,128)(2,1)}, bf16[704,512]{1,0:T(8,128)(2,1)}, u32[]{:S(2)}, u32[]{:S(2)}) collective-permute-start(bf16[704,512]{1,0:T(8,128)(2,1)} %get-tuple-element.253), channel_id=1, source_target_pairs={{0,1},{1,2},{2,3},{3,0},{4,5},{5,6},{6,7},{7,4},{8,9},{9,10},{10,1... | collective-permute-start | bytes 2162696 | tf_op jit(solution)/shard_map/ppermute | solution.py:481
  784.5 78.5 %collective-permute-start.149 = (bf16[704,512]{1,0:T(8,128)(2,1)}, bf16[704,512]{1,0:T(8,128)(2,1)}, u32[]{:S(2)}, u32[]{:S(2)}) collective-permute-start(bf16[704,512]{1,0:T(8,128)(2,1)} %get-tuple-element.254), channel_id=1, source_target_pairs={{0,3},{1,0},{2,1},{3,2},{4,7},{5,4},{6,5},{7,6},{8,11},{9,8},{10,9... | collective-permute-start | bytes 2162696 | tf_op jit(solution)/shard_map/ppermute | solution.py:481
  799.6 91.2 %collective-permute-start.148 = (bf16[704,512]{1,0:T(8,128)(2,1)}, bf16[704,512]{1,0:T(8,128)(2,1)}, u32[]{:S(2)}, u32[]{:S(2)}) collective-permute-start(bf16[704,512]{1,0:T(8,128)(2,1)} %get-tuple-element.255), channel_id=1, source_target_pairs={{0,2},{1,3},{2,0},{3,1},{4,6},{5,7},{6,4},{7,5},{8,10},{9,11},{10,... | collective-permute-start | bytes 2162696 | tf_op jit(solution)/shard_map/ppermute | solution.py:481
  851.3 88.0 %collective-permute-start.54 = (bf16[1024,2048]{1,0:T(8,128)(2,1)}, bf16[1024,2048]{1,0:T(8,128)(2,1)}, u32[]{:S(2)}, u32[]{:S(2)}) collective-permute-start(bf16[1024,2048]{1,0:T(8,128)(2,1)} %slice.561), channel_id=1, source_target_pairs={{0,4},{4,0},{1,5},{5,1},{2,6},{6,2},{3,7},{7,3},{8,12},{12,8},{9,1... | collective-permute-start | bytes 12582920 | tf_op jit(solution)/shard_map/ppermute | solution.py:476
  860.9 89.2 %collective-permute-start.81 = (bf16[1024,2048]{1,0:T(8,128)(2,1)}, bf16[1024,2048]{1,0:T(8,128)(2,1)}, u32[]{:S(2)}, u32[]{:S(2)}) collective-permute-start(bf16[1024,2048]{1,0:T(8,128)(2,1)} %slice.578), channel_id=1, source_target_pairs={{0,4},{4,0},{1,5},{5,1},{2,6},{6,2},{3,7},{7,3},{8,12},{12,8},{9,1... | collective-permute-start | bytes 12582920 | tf_op jit(solution)/shard_map/ppermute | solution.py:476
  948.6 37.4 %collective-permute-start.58 = (bf16[128,2048]{1,0:T(8,128)(2,1)}, bf16[128,2048]{1,0:T(8,128)(2,1)S(1)}, u32[]{:S(2)}, u32[]{:S(2)}) collective-permute-start(bf16[128,2048]{1,0:T(8,128)(2,1)} %get-tuple-element.243), channel_id=1, source_target_pairs={{0,8},{8,0},{16,24},{24,16},{1,9},{9,1},{17,25},{25,17},{2,10},{10... | collective-permute-start | bytes 1572872 | tf_op jit(solution)/shard_map/ppermute | solution.py:476
  949.3 38.0 %collective-permute-start.57 = (bf16[128,2048]{1,0:T(8,128)(2,1)S(1)}, bf16[128,2048]{1,0:T(8,128)(2,1)S(1)}, u32[]{:S(2)}, u32[]{:S(2)}) collective-permute-start(bf16[128,2048]{1,0:T(8,128)(2,1)S(1)} %get-tuple-element.244), channel_id=1, source_target_pairs={{0,16},{8,24},{16,0},{24,8},{1,17},{9,25},{17,1},{25,9},{2,18},{10... | collective-permute-start | bytes 1572872 | tf_op jit(solution)/shard_map/ppermute | solution.py:476
  963.0 45.7 %collective-permute-start.85 = (bf16[128,2048]{1,0:T(8,128)(2,1)S(1)}, bf16[128,2048]{1,0:T(8,128)(2,1)S(1)}, u32[]{:S(2)}, u32[]{:S(2)}) collective-permute-start(bf16[128,2048]{1,0:T(8,128)(2,1)S(1)} %get-tuple-element.247), channel_id=1, source_target_pairs={{0,8},{8,0},{16,24},{24,16},{1,9},{9,1},{17,25},{25,17},{2,10},{10... | collective-permute-start | bytes 1572872 | tf_op jit(solution)/shard_map/ppermute | solution.py:476
  1081.8 48.5 %collective-permute-start.140 = (bf16[256,1024]{1,0:T(8,128)(2,1)S(1)}, bf16[256,1024]{1,0:T(8,128)(2,1)S(1)}, u32[]{:S(2)}, u32[]{:S(2)}) collective-permute-start(bf16[256,1024]{1,0:T(8,128)(2,1)S(1)} %convolution_convert_fusion.12), channel_id=1, source_target_pairs={{0,16},{8,24},{16,0},{24,8},{1,17},{9,25},{17,1},{25,9},{2,18},{10... | collective-permute-start | bytes 1572872 | tf_op jit(solution)/shard_map/ppermute | solution.py:476
  1085.3 35.0 %collective-permute-start.143 = (bf16[256,1024]{1,0:T(8,128)(2,1)S(1)}, bf16[256,1024]{1,0:T(8,128)(2,1)S(1)}, u32[]{:S(2)}, u32[]{:S(2)}) collective-permute-start(bf16[256,1024]{1,0:T(8,128)(2,1)S(1)} %copy-done.105), channel_id=1, source_target_pairs={{0,8},{8,0},{16,24},{24,16},{1,9},{9,1},{17,25},{25,17},{2,10},{10... | collective-permute-start | bytes 1572872 | tf_op jit(solution)/shard_map/ppermute | solution.py:476
  1087.2 54.1 %collective-permute-start.142 = (bf16[256,1024]{1,0:T(8,128)(2,1)S(1)}, bf16[256,1024]{1,0:T(8,128)(2,1)S(1)}, u32[]{:S(2)}, u32[]{:S(2)}) collective-permute-start(bf16[256,1024]{1,0:T(8,128)(2,1)S(1)} %convolution_convert_fusion.11), channel_id=1, source_target_pairs={{0,8},{8,0},{16,24},{24,16},{1,9},{9,1},{17,25},{25,17},{2,10},{10... | collective-permute-start | bytes 1572872 | tf_op jit(solution)/shard_map/ppermute | solution.py:476
  1141.4 82.0 %collective-permute-start.141 = (bf16[128,1024]{1,0:T(8,128)(2,1)}, bf16[128,1024]{1,0:T(8,128)(2,1)}, u32[]{:S(2)}, u32[]{:S(2)}) collective-permute-start(bf16[128,1024]{1,0:T(8,128)(2,1)} %slice.984), channel_id=1, source_target_pairs={{0,1},{1,2},{2,3},{3,0},{4,5},{5,6},{6,7},{7,4},{8,9},{9,10},{10,1... | collective-permute-start | bytes 786440 | tf_op jit(solution)/shard_map/ppermute | solution.py:481
  1142.9 80.4 %collective-permute-start.145 = (bf16[128,1024]{1,0:T(8,128)(2,1)}, bf16[128,1024]{1,0:T(8,128)(2,1)S(1)}, u32[]{:S(2)}, u32[]{:S(2)}) collective-permute-start(bf16[128,1024]{1,0:T(8,128)(2,1)} %get-tuple-element.286), channel_id=1, source_target_pairs={{0,2},{1,3},{2,0},{3,1},{4,6},{5,7},{6,4},{7,5},{8,10},{9,11},{10,... | collective-permute-start | bytes 786440 | tf_op jit(solution)/shard_map/ppermute | solution.py:481
  1144.8 78.6 %collective-permute-start.146 = (bf16[128,1024]{1,0:T(8,128)(2,1)}, bf16[128,1024]{1,0:T(8,128)(2,1)}, u32[]{:S(2)}, u32[]{:S(2)}) collective-permute-start(bf16[128,1024]{1,0:T(8,128)(2,1)} %get-tuple-element.287), channel_id=1, source_target_pairs={{0,3},{1,0},{2,1},{3,2},{4,7},{5,4},{6,5},{7,6},{8,11},{9,8},{10,9... | collective-permute-start | bytes 786440 | tf_op jit(solution)/shard_map/ppermute | solution.py:481
  1228.7 42.3 %collective-permute-start.135 = (f32[12416]{0:T(1024)S(1)}, f32[12416]{0:T(1024)S(1)}, u32[]{:S(2)}, u32[]{:S(2)}) collective-permute-start(f32[12416]{0:T(1024)S(1)} %fusion.135), channel_id=1, source_target_pairs={{0,16},{8,24},{16,0},{24,8},{1,17},{9,25},{17,1},{25,9},{2,18},{10... | collective-permute-start | bytes 149000 | tf_op jit(solution)/shard_map/ppermute | solution.py:476
  1267.0 63.5 %collective-permute-start.127 = (bf16[256,1536]{1,0:T(8,128)(2,1)}, bf16[256,1536]{1,0:T(8,128)(2,1)}, u32[]{:S(2)}, u32[]{:S(2)}) collective-permute-start(bf16[256,1536]{1,0:T(8,128)(2,1)} %convolution_convert_fusion.4), channel_id=1, source_target_pairs={{0,16},{8,24},{16,0},{24,8},{1,17},{9,25},{17,1},{25,9},{2,18},{10... | collective-permute-start | bytes 2359304 | tf_op jit(solution)/shard_map/ppermute | solution.py:476
  1269.0 72.0 %collective-permute-start.129 = (bf16[256,1536]{1,0:T(8,128)(2,1)}, bf16[256,1536]{1,0:T(8,128)(2,1)}, u32[]{:S(2)}, u32[]{:S(2)}) collective-permute-start(bf16[256,1536]{1,0:T(8,128)(2,1)} %convolution_convert_fusion.3), channel_id=1, source_target_pairs={{0,8},{8,0},{16,24},{24,16},{1,9},{9,1},{17,25},{25,17},{2,10},{10... | collective-permute-start | bytes 2359304 | tf_op jit(solution)/shard_map/ppermute | solution.py:476
  1269.0 37.6 %collective-permute-start.130 = (bf16[256,1536]{1,0:T(8,128)(2,1)}, bf16[256,1536]{1,0:T(8,128)(2,1)}, u32[]{:S(2)}, u32[]{:S(2)}) collective-permute-start(bf16[256,1536]{1,0:T(8,128)(2,1)} %convolution_convert_fusion.2), channel_id=1, source_target_pairs={{0,8},{8,0},{16,24},{24,16},{1,9},{9,1},{17,25},{25,17},{2,10},{10... | collective-permute-start | bytes 2359304 | tf_op jit(solution)/shard_map/ppermute | solution.py:476
  1285.9 39.0 %collective-permute-start.121 = (bf16[256,1664]{1,0:T(8,128)(2,1)}, bf16[256,1664]{1,0:T(8,128)(2,1)}, u32[]{:S(2)}, u32[]{:S(2)}) collective-permute-start(bf16[256,1664]{1,0:T(8,128)(2,1)} %convolution_convert_fusion.6), channel_id=1, source_target_pairs={{0,8},{8,0},{16,24},{24,16},{1,9},{9,1},{17,25},{25,17},{2,10},{10... | collective-permute-start | bytes 2555912 | tf_op jit(solution)/shard_map/ppermute | solution.py:476
  1287.8 39.5 %collective-permute-start.116 = (bf16[256,1664]{1,0:T(8,128)(2,1)}, bf16[256,1664]{1,0:T(8,128)(2,1)S(1)}, u32[]{:S(2)}, u32[]{:S(2)}) collective-permute-start(bf16[256,1664]{1,0:T(8,128)(2,1)} %convolution_convert_fusion.9), channel_id=1, source_target_pairs={{0,16},{8,24},{16,0},{24,8},{1,17},{9,25},{17,1},{25,9},{2,18},{10... | collective-permute-start | bytes 2555912 | tf_op jit(solution)/shard_map/ppermute | solution.py:476
  1324.9 35.4 %collective-permute-start.118 = (bf16[256,1664]{1,0:T(8,128)(2,1)S(1)}, bf16[256,1664]{1,0:T(8,128)(2,1)S(1)}, u32[]{:S(2)}, u32[]{:S(2)}) collective-permute-start(bf16[256,1664]{1,0:T(8,128)(2,1)S(1)} %copy-done.104), channel_id=1, source_target_pairs={{0,16},{8,24},{16,0},{24,8},{1,17},{9,25},{17,1},{25,9},{2,18},{10... | collective-permute-start | bytes 2555912 | tf_op jit(solution)/shard_map/ppermute | solution.py:476
  1330.4 57.7 %collective-permute-start.96 = (bf16[1024,2048]{1,0:T(8,128)(2,1)}, bf16[1024,2048]{1,0:T(8,128)(2,1)}, u32[]{:S(2)}, u32[]{:S(2)}) collective-permute-start(bf16[1024,2048]{1,0:T(8,128)(2,1)} %slice.598), channel_id=1, source_target_pairs={{0,4},{4,0},{1,5},{5,1},{2,6},{6,2},{3,7},{7,3},{8,12},{12,8},{9,1... | collective-permute-start | bytes 12582920 | tf_op jit(solution)/shard_map/ppermute | solution.py:476
  1338.9 36.1 %collective-permute-start.120 = (bf16[256,1664]{1,0:T(8,128)(2,1)S(1)}, bf16[256,1664]{1,0:T(8,128)(2,1)S(1)}, u32[]{:S(2)}, u32[]{:S(2)}) collective-permute-start(bf16[256,1664]{1,0:T(8,128)(2,1)S(1)} %copy-done.103), channel_id=1, source_target_pairs={{0,8},{8,0},{16,24},{24,16},{1,9},{9,1},{17,25},{25,17},{2,10},{10... | collective-permute-start | bytes 2555912 | tf_op jit(solution)/shard_map/ppermute | solution.py:476
  1341.1 36.2 %collective-permute-start.109 = (bf16[2,256,2048]{2,1,0:T(8,128)(2,1)S(1)}, bf16[2,256,2048]{2,1,0:T(8,128)(2,1)S(1)}, u32[]{:S(2)}, u32[]{:S(2)}) collective-permute-start(bf16[2,256,2048]{2,1,0:T(8,128)(2,1)S(1)} %copy-done.51), channel_id=1, source_target_pairs={{0,4},{4,0},{1,5},{5,1},{2,6},{6,2},{3,7},{7,3},{8,12},{12,8},{9,1... | collective-permute-start | bytes 6291464 | tf_op jit(solution)/shard_map/ppermute | solution.py:476
  1375.0 99.1 %collective-permute-start.128 = (bf16[128,1536]{1,0:T(8,128)(2,1)S(1)}, bf16[128,1536]{1,0:T(8,128)(2,1)}, u32[]{:S(2)}, u32[]{:S(2)}) collective-permute-start(bf16[128,1536]{1,0:T(8,128)(2,1)S(1)} %slice.983), channel_id=1, source_target_pairs={{0,1},{1,2},{2,3},{3,0},{4,5},{5,6},{6,7},{7,4},{8,9},{9,10},{10,1... | collective-permute-start | bytes 1179656 | tf_op jit(solution)/shard_map/ppermute | solution.py:481
  1398.9 37.5 %collective-permute-start.100 = (bf16[128,2048]{1,0:T(8,128)(2,1)}, bf16[128,2048]{1,0:T(8,128)(2,1)S(1)}, u32[]{:S(2)}, u32[]{:S(2)}) collective-permute-start(bf16[128,2048]{1,0:T(8,128)(2,1)} %get-tuple-element.235), channel_id=1, source_target_pairs={{0,8},{8,0},{16,24},{24,16},{1,9},{9,1},{17,25},{25,17},{2,10},{10... | collective-permute-start | bytes 1572872 | tf_op jit(solution)/shard_map/ppermute | solution.py:476
  1400.4 36.7 %collective-permute-start.99 = (bf16[128,2048]{1,0:T(8,128)(2,1)S(1)}, bf16[128,2048]{1,0:T(8,128)(2,1)S(1)}, u32[]{:S(2)}, u32[]{:S(2)}) collective-permute-start(bf16[128,2048]{1,0:T(8,128)(2,1)S(1)} %get-tuple-element.236), channel_id=1, source_target_pairs={{0,16},{8,24},{16,0},{24,8},{1,17},{9,25},{17,1},{25,9},{2,18},{10... | collective-permute-start | bytes 1572872 | tf_op jit(solution)/shard_map/ppermute | solution.py:476
  1469.9 66.9 %collective-permute-start.110 = (bf16[2,256,2048]{2,1,0:T(8,128)(2,1)}, bf16[2,256,2048]{2,1,0:T(8,128)(2,1)}, u32[]{:S(2)}, u32[]{:S(2)}) collective-permute-start(bf16[2,256,2048]{2,1,0:T(8,128)(2,1)} %fusion.13), channel_id=1, source_target_pairs={{0,4},{4,0},{1,5},{5,1},{2,6},{6,2},{3,7},{7,3},{8,12},{12,8},{9,1... | collective-permute-start | bytes 6291464 | tf_op jit(solution)/shard_map/ppermute | solution.py:476
  1477.1 35.9 %collective-permute-start.123 = (bf16[128,1664]{1,0:T(8,128)(2,1)S(1)}, bf16[128,1664]{1,0:T(8,128)(2,1)S(1)}, u32[]{:S(2)}, u32[]{:S(2)}) collective-permute-start(bf16[128,1664]{1,0:T(8,128)(2,1)S(1)} %copy-done.77), channel_id=1, source_target_pairs={{0,2},{1,3},{2,0},{3,1},{4,6},{5,7},{6,4},{7,5},{8,10},{9,11},{10,... | collective-permute-start | bytes 1277960 | tf_op jit(solution)/shard_map/ppermute | solution.py:481
  1477.2 44.7 %collective-permute-start.124 = (bf16[128,1664]{1,0:T(8,128)(2,1)S(1)}, bf16[128,1664]{1,0:T(8,128)(2,1)S(1)}, u32[]{:S(2)}, u32[]{:S(2)}) collective-permute-start(bf16[128,1664]{1,0:T(8,128)(2,1)S(1)} %copy-done.76), channel_id=1, source_target_pairs={{0,3},{1,0},{2,1},{3,2},{4,7},{5,4},{6,5},{7,6},{8,11},{9,8},{10,9... | collective-permute-start | bytes 1277960 | tf_op jit(solution)/shard_map/ppermute | solution.py:481
  1487.5 55.2 %collective-permute-start.103 = (bf16[2,256,2048]{2,1,0:T(8,128)(2,1)}, bf16[2,256,2048]{2,1,0:T(8,128)(2,1)}, u32[]{:S(2)}, u32[]{:S(2)}) collective-permute-start(bf16[2,256,2048]{2,1,0:T(8,128)(2,1)} %pad_maximum_fusion.8), channel_id=1, source_target_pairs={{0,4},{4,0},{1,5},{5,1},{2,6},{6,2},{3,7},{7,3},{8,12},{12,8},{9,1... | collective-permute-start | bytes 6291464 | tf_op jit(solution)/shard_map/ppermute | solution.py:476
  (215 other events, 3647.7 us)

commit v3 on v2

--- a/solution.py
+++ b/solution.py
@@ -1,4 +1,5 @@
 import functools
+import math
 import jax
 import jax.numpy as jnp
 from jax import lax
@@ -471,6 +472,79 @@
     )(rows, grads, weights, weights, weights)
 
 
+def place_kernel(count, targets, *refs):
+    pieces, out, done = refs[:count], refs[count], refs[count + 1]
+    copies = []
+    for i, piece in enumerate(pieces):
+        target = out.at[pl.ds(targets[i], piece.shape[0])]
+        copies.append(pltpu.make_async_copy(piece, target, done.at[i]))
+    for copy in copies:
+        copy.start()
+    for copy in copies:
+        copy.wait()
+
+
+def place_blocks(pieces, targets, blocks):
+    count = len(pieces)
+    shape = (blocks,) + pieces[0].shape[1:]
+    anywhere = pl.BlockSpec(memory_space=pl.ANY)
+    return pl.pallas_call(
+        functools.partial(place_kernel, count),
+        grid_spec=pltpu.PrefetchScalarGridSpec(
+            num_scalar_prefetch=1,
+            grid=(1,),
+            in_specs=[anywhere] * count,
+            out_specs=anywhere,
+            scratch_shapes=[pltpu.SemaphoreType.DMA((count,))],
+        ),
+        out_shape=jax.ShapeDtypeStruct(shape, pieces[0].dtype),
+        cost_estimate=pl.CostEstimate(flops=0, bytes_accessed=4 * math.prod(shape), transcendentals=0),
+    )(jnp.stack(targets).astype(jnp.int32), *pieces)
+
+
+def join_kernel(line, source, *refs):
+    refs[-1][...] = source[...]
+
+
+def columns_join(full, piece, line, lines, squares):
+    rows, columns = piece.shape
+    part = columns // squares
+    known = [] if full is None else [full]
+    return pl.pallas_call(
+        join_kernel,
+        grid_spec=pltpu.PrefetchScalarGridSpec(
+            num_scalar_prefetch=1,
+            grid=(squares,),
+            in_specs=[pl.BlockSpec((rows, part), lambda j, line: (0, j))]
+            + [pl.BlockSpec(memory_space=pl.ANY) for _ in known],
+            out_specs=pl.BlockSpec((rows, part), lambda j, line: (0, j * lines + line[0])),
+        ),
+        out_shape=jax.ShapeDtypeStruct((rows, lines * columns), piece.dtype),
+        input_output_aliases={2: 0} if known else {},
+        compiler_params=pltpu.CompilerParams(vmem_limit_bytes=VMEM_BYTES),
+        cost_estimate=pl.CostEstimate(flops=0, bytes_accessed=4 * piece.size, transcendentals=0),
+    )(jnp.reshape(line, (1,)).astype(jnp.int32), piece, *known)
+
+
+def columns_split_kernel(first, second, third, out):
+    for i, ref in enumerate((first, second, third)):
+        out[0, i] = low(ref[...])
+
+
+def columns_split(arrays, lines, squares):
+    rows, columns = arrays[0].shape
+    part = columns // (lines * squares)
+    return pl.pallas_call(
+        columns_split_kernel,
+        grid=(lines, squares),
+        in_specs=[pl.BlockSpec((rows, part), lambda i, j: (0, j * lines + i))] * 3,
+        out_specs=pl.BlockSpec((1, 3, rows, part), lambda i, j: (i, 0, 0, j)),
+        out_shape=jax.ShapeDtypeStruct((lines, 3, rows, squares * part), jnp.bfloat16),
+        compiler_params=pltpu.CompilerParams(vmem_limit_bytes=VMEM_BYTES),
+        cost_estimate=pl.CostEstimate(flops=0, bytes_accessed=18 * arrays[0].size, transcendentals=0),
+    )(*arrays)
+
+
 def flip(value, axis, bit):
     devices = range(lax.axis_size(axis))
     return lax.ppermute(value, axis, [(i, i ^ bit) for i in devices])
@@ -499,28 +573,10 @@
     return value.astype(jnp.float32)
 
 
-def features(rows):
-    count, width = rows.shape
-    squares, lines = lax.axis_size("ctx"), lax.axis_size("fsdp")
-    part = width // (squares * lines)
-    order = rows.reshape(count, squares, lines, part).transpose(0, 2, 1, 3).reshape(count, width)
-    twice = jnp.concatenate([order, order], axis=1)
-    return lax.dynamic_slice_in_dim(twice, lax.axis_index("fsdp") * squares * part, width, 1)
-
-
-def features_back(rows):
-    count, width = rows.shape
-    squares, lines = lax.axis_size("ctx"), lax.axis_size("fsdp")
-    part = width // (squares * lines)
-    twice = jnp.concatenate([rows, rows], axis=1)
-    turn = (lines - lax.axis_index("fsdp")) % lines
-    order = lax.dynamic_slice_in_dim(twice, turn * squares * part, width, 1)
-    return order.reshape(count, lines, squares, part).transpose(0, 2, 1, 3).reshape(count, width)
-
-
 def gather_line(shard):
-    count = lax.axis_size("fsdp")
-    return jnp.stack([shard] + [shift(shard, "fsdp", count - r) for r in range(1, count)])
+    count, place = lax.axis_size("fsdp"), lax.axis_index("fsdp")
+    pieces = [shard[None]] + [shift(shard, "fsdp", d)[None] for d in range(1, count)]
+    return place_blocks(pieces, [(place - d) % count for d in range(count)], count)
 
 
 class Square:
@@ -545,80 +601,69 @@
     def weights(self):
         lines, rows, columns = self.own.shape
         place = lax.axis_index("ctx")
-        buffer = jnp.zeros((lines, 4, rows, columns), self.own.dtype)
-        buffer = put(buffer, self.own[:, None], 0, place, 0, 0)
-        buffer = put(buffer, self.beside[:, None], 0, place ^ 1, 0, 0)
-        buffer = put(buffer, self.across[:, None], 0, place ^ 2, 0, 0)
-        buffer = put(buffer, self.upper[:, None], 0, place ^ 3, 0, 0)
-        buffer = put(buffer, self.lower[:, None], self.half, place ^ 3, 0, 0)
-        return buffer.reshape(4 * lines * rows, columns)
-
-    def rows(self):
-        parts = [self.own, self.beside, self.across, self.upper, self.lower]
-        if lax.axis_size("tp") == 2:
-            return jnp.concatenate(parts + [flip(part, "tp", 1) for part in parts], axis=0)
-        return lax.all_gather(jnp.concatenate(parts, axis=0), "tp", axis=0, tiled=True)
-
-
-def square_sum(blocks):
-    from_across = flip(low(blocks(3, 0)), "ctx", 2)
-    from_beside = flip(low(blocks(3, 1)), "ctx", 1)
-    beside_down = flip(low(blocks(1, 1)), "ctx", 1)
-    across_up = flip(low(blocks(2, 0)), "ctx", 2)
-    beside_up = flip(low(blocks(1, 0) + wide(from_across)), "ctx", 1)
-    across_down = flip(low(blocks(2, 1) + wide(from_beside)), "ctx", 2)
-    upper = blocks(0, 0) + wide(beside_up) + wide(across_up)
-    lower = blocks(0, 1) + wide(beside_down) + wide(across_down)
-    return jnp.concatenate([upper, lower], axis=0)
-
-
-def collect_rows(partial):
-    count = lax.axis_size("tp")
-    size = partial.shape[0] // count
-    if count == 2:
-        total = wide(partial[:size]) + wide(flip(partial[size:], "tp", 1))
-    else:
-        total = wide(lax.psum_scatter(partial, "tp", scatter_dimension=0, tiled=True))
-    half = size // 8
-    return square_sum(lambda bit, low_half: total[(2 * bit + low_half) * half :][:half])
+        starts = [(place ^ bit) * lines for bit in range(4)]
+        full = place_blocks(
+            [self.own, self.beside, self.across, self.upper, self.lower],
+            starts + [starts[3] + self.half],
+            4 * lines,
+        )
+        return full.reshape(4 * lines * rows, columns)
+
+    def far(self):
+        return jnp.concatenate([self.upper, self.lower], axis=0)
+
+
+def all_cores(rows):
+    if lax.axis_size("tp") != 2:
+        return lax.all_gather(rows, "tp", axis=0, tiled=True)
+    return jnp.concatenate([rows, flip(rows, "tp", 1)], axis=0)
+
+
+def core_sum(partial):
+    if lax.axis_size("tp") != 2:
+        return wide(lax.psum_scatter(partial, "tp", scatter_dimension=0, tiled=True))
+    half = partial.shape[0] // 2
+    return wide(partial[:half]) + wide(flip(partial[half:], "tp", 1))
 
 
 def neighbour_columns(rows):
-    lines = lax.axis_size("fsdp")
-    count, width = rows.shape
-    split = rows.reshape(count, lines, 4, width // (4 * lines))
+    width = rows.shape[1] // 4
     place = lax.axis_index("ctx")
-    return [
-        lax.dynamic_index_in_dim(split, place ^ bit, 2, keepdims=False).reshape(count, width // 4)
-        for bit in range(4)
-    ]
+    return [lax.dynamic_slice_in_dim(rows, (place ^ bit) * width, width, 1) for bit in range(4)]
 
 
 def line_sum(own):
-    total = own[0]
-    for distance in range(1, own.shape[0]):
-        total = total + wide(shift(low(own[distance]), "fsdp", distance))
+    count, place = own.shape[0], lax.axis_index("fsdp")
+    total = lax.dynamic_index_in_dim(own, place, 0, keepdims=False)
+    for distance in range(1, count):
+        piece = lax.dynamic_index_in_dim(own, (place + distance) % count, 0, keepdims=False)
+        total = total + wide(shift(low(piece), "fsdp", distance))
     return total
 
 
-def outer_scatter(columns, grads):
-    half = columns[0].shape[1] // 2
-
-    def block(bit, low_half):
-        return outer_rows(columns[bit][:, low_half * half : (low_half + 1) * half], grads)
-
-    own = square_sum(block)
-    lines = lax.axis_size("fsdp")
-    return line_sum(own.reshape(lines, own.shape[0] // lines, own.shape[1]))
-
-
-def swap_square(pieces):
-    place = lax.axis_index("ctx")
-    arrived = jnp.zeros(pieces.shape, jnp.bfloat16)
-    for bit in range(4):
-        piece = low(lax.dynamic_index_in_dim(pieces, place ^ bit, 0))
-        arrived = put(arrived, flip(piece, "ctx", bit) if bit else piece, place ^ bit, 0, 0)
-    return arrived
+class Scatter:
+    def __init__(self, columns, grads):
+        self.columns, self.grads = columns, grads
+        self.half = columns[0].shape[1] // 2
+        self.sent = [low(self.block(*which)) for which in ((3, 0), (3, 1), (1, 1), (2, 0))]
+        self.first = tuple(flip(part, "ctx", bit) for part, bit in zip(self.sent, (2, 1, 1, 2)))
+
+    def block(self, bit, lower):
+        return outer_rows(self.columns[bit][:, lower * self.half : (lower + 1) * self.half], self.grads)
+
+    def finish(self, *earlier):
+        first = self.first
+        if earlier:
+            first = lax.optimization_barrier(first + earlier)[:4]
+        from_across, from_beside, beside_lower, across_upper = first
+        beside_upper = flip(low(self.block(1, 0) + wide(from_across)), "ctx", 1)
+        across_lower = flip(low(self.block(2, 1) + wide(from_beside)), "ctx", 2)
+        self.last = (beside_upper, across_lower)
+        upper = self.block(0, 0) + wide(beside_upper) + wide(across_upper)
+        lower = self.block(0, 1) + wide(beside_lower) + wide(across_lower)
+        own = jnp.concatenate([upper, lower], axis=0)
+        lines = lax.axis_size("fsdp")
+        return line_sum(own.reshape(lines, own.shape[0] // lines, own.shape[1]))
 
 
 def butterfly(value, axes):
@@ -732,7 +777,6 @@
     spare = LANES - heads_here
     units_here = gate_weight.shape[1]
     shard_rows = gate_weight.shape[0]
-    seqs = range(seq_count)
 
     joined = by_head([low(query_weight), low(key_weight), low(value_weight)])
     shards = [joined[:, p * part_cols : (p + 1) * part_cols] for p in range(parts)]
@@ -744,9 +788,12 @@
     units = units_here // 4
     pieces = jnp.stack([low(gate_weight).T, low(up_weight).T, low(down_weight)])
     pieces = pieces.reshape(3, 4, units, shard_rows).transpose(1, 0, 2, 3)
-    ffn_line = swap_square(pieces.reshape(4, 3 * units, shard_rows))
+    ffn_line = lax.all_to_all(pieces.reshape(4, 3 * units, shard_rows), "ctx", 0, 0)
     ffn_line = ffn_line.transpose(1, 0, 2).reshape(3 * units, 4 * shard_rows)
-    ffn_parts = gather_line(tie(ffn_line, lines[-1]))
+    line_count, line_place = lax.axis_size("fsdp"), lax.axis_index("fsdp")
+    ffn_full = columns_join(None, ffn_line, line_place, line_count, 4)
+    ends_apart = sorted({1 % line_count, line_count - 1} - {0})
+    ffn_near = {d: shift(tie(ffn_line, lines[parts - 1]), "fsdp", d) for d in ends_apart}
 
     first_pos = lax.axis_index("ctx") * local_len
     starts = doc_start - first_pos
@@ -754,74 +801,95 @@
     conv = by_head([conv_weight[0], conv_weight[1], conv_weight[2]])
     bias = jnp.pad(beta_bias, (0, spare))[None]
     gain_head = gain_o[None]
-    gain_mix, gain_ffn = features(gain_mix[None]), features(gain_ffn[None])
-
-    tokens = features(block_input.reshape(row_count, width))
+    tokens = block_input.reshape(row_count, width)
     inputs = wide(tokens)
     normed_mix = low(inputs * rms_scale(inputs, EPSILON) * gain_mix)
-    inputs_mine = wide(rows_mine(tokens.reshape(seq_count, local_len, width)))
-    grads_mine = rows_mine(features(out_grad.reshape(row_count, width)).reshape(seq_count, local_len, width))
-
-    square = Square(lines[0]).forward()
+    inputs_mine = wide(rows_mine(block_input).reshape(-1, width))
+    grads_mine = rows_mine(out_grad).reshape(-1, width)
+
+    square = Square(tie(lines[0], ffn_line)).forward()
     mix_full, kept, pre = [], [], []
     for p in range(parts):
         mix_full.append(square.weights())
         square = Square(tie(lines[p + 1], *square.done()))
-        if p == parts - 1:
-            grad_squares = [Square(tie(grads_mine[0], mix_full[-1]))]
-        pre.append(times(normed_mix, mix_full[p]))
+        if p == 0:
+            pre.append(times(normed_mix, mix_full[p]))
+        else:
+            pre.append(times(tie(normed_mix, lines[-1]), mix_full[p]))
         ends = pre[p].reshape(seq_count, local_len, -1)[:, local_len - HALO :, :part_cols]
         halo = from_behind(ends, "ctx", 1)
         convs = conv[:, p * part_cols : (p + 1) * part_cols]
+        held = pre[p]
+        if p > 0:
+            held = tie(held, grad_square.beside, grad_square.across)
         kept.append(
             [halo, convs]
             + list(
                 mixer_forward(
-                    pre[p], pre[0], bias, halo, convs, col, row, taps, p * part_heads, part_heads, group
+                    held, pre[0], bias, halo, convs, col, row, taps, p * part_heads, part_heads, group
                 )
             )
         )
         square.forward(kept[p][2])
-    grad_squares[0].forward(kept[-1][2])
-    for s in seqs[1:]:
-        grad_squares.append(Square(tie(grads_mine[s], *grad_squares[-1].done())).forward())
+        if p == 0:
+            ffn_near = dict(zip(ends_apart, lax.optimization_barrier(tuple(ffn_near.values()))))
+            for d in ends_apart:
+                ffn_full = columns_join(ffn_full, ffn_near[d], (line_place - d) % line_count, line_count, 4)
+            cut = 3 * units // 2
+            ffn_far = {
+                d: shift(tie(ffn_line[:cut], *ffn_near.values()), "fsdp", d) for d in range(2, line_count - 1)
+            }
+            square.upper = tie(square.upper, *ffn_near.values())
+            grad_square = Square(tie(grads_mine, kept[p][2]))
+        if p == parts - 1:
+            grad_square.forward()
     out_full = square.weights()
 
     entered, transfers, mixed_rows = [], [], []
     for _, _, own, carry, final, _, _, _ in kept:
         transfers.append(low(final[..., LANES:]))
-        entered.append(pass_states(final[..., :LANES], transfers[-1], 1))
+        first = final[..., :LANES]
+        if len(entered) == parts - 1:
+            first = tie(first, *grad_square.done(), *ffn_far.values())
+            ffn_far = {
+                d: [piece, shift(tie(ffn_line[cut:], piece), "fsdp", d)] for d, piece in ffn_far.items()
+            }
+        entered.append(pass_states(first, transfers[-1], 1))
+        if len(entered) == parts:
+            carry = tie(carry, *(piece[1] for piece in ffn_far.values()))
         mixed_rows.append(mixer_output(own, carry, entered[-1], gain_head, group))
     mixed_rows = jnp.concatenate(mixed_rows, axis=1)
 
-    residual, scale_ffn, normed_ffn, squares = [], [], [], []
-    for s in seqs:
-        branch = times_transposed(mixed_rows[s * local_len : (s + 1) * local_len], out_full)
-        residual.append(inputs_mine[s] + rows_scatter(low(branch)[None])[0])
-        scale_ffn.append(rms_scale(residual[s], EPSILON))
-        squares.append(Square(low(residual[s] * scale_ffn[s] * gain_ffn)).forward())
-    ffn_parts = tie(ffn_parts, squares[0].own)
-    ffn_full = jnp.concatenate([ffn_parts[i] for i in range(ffn_parts.shape[0])], axis=1)
-    ffn_rows, grad_rows, ffn_out = [], [], []
-    for s in seqs:
-        ffn_rows.append(squares[s].rows())
-        grad_rows.append(grad_squares[s].rows())
-        ffn_out.append(ffn_both(ffn_rows[s], grad_rows[s], ffn_full))
-
-    grad_residual, grad_branch, gain_ffn_part = [], [], 0.0
-    for s in seqs:
-        grad_normed = collect_rows(ffn_out[s][3])
-        back_ffn, unit_ffn = norm_backward(grad_normed, residual[s], scale_ffn[s], gain_ffn)
-        grad_residual.append(wide(grads_mine[s]) + back_ffn)
-        gain_ffn_part = gain_ffn_part + jnp.sum(grad_normed * unit_ffn, axis=0)
-        grad_branch.append(rows_full(low(grad_residual[s])[None])[0])
-    grad_branch = jnp.concatenate(grad_branch, axis=0)
-    held = []
-    for s in seqs:
-        total = collect_rows(tie(ffn_out[s][4], grad_branch))
-        held.append(low(residual[s] + total))
-    block_output = features_back(rows_full(jnp.stack(held)).reshape(row_count, width))
-
+    branch = low(times_transposed(mixed_rows, out_full)).reshape(seq_count, local_len, width)
+    residual = inputs_mine + rows_scatter(branch).reshape(-1, width)
+    scale_ffn = rms_scale(residual, EPSILON)
+    square = Square(low(residual * scale_ffn * gain_ffn))
+    for d, pieces in ffn_far.items():
+        piece = jnp.concatenate(pieces, axis=0)
+        ffn_full = columns_join(ffn_full, piece, (line_place - d) % line_count, line_count, 4)
+
+    ffn_rows = [all_cores(square.own)]
+    grad_rows = [all_cores(part) for part in (grad_square.own, grad_square.beside, grad_square.across, grad_square.far())]
+    ffn_out = [ffn_both(ffn_rows[0], grad_rows[0], ffn_full)]
+    square.forward(ffn_out[0][0])
+    ffn_rows.append(all_cores(tie(square.beside, ffn_out[0][0])))
+    ffn_out.append(ffn_both(ffn_rows[1], grad_rows[1], ffn_full))
+    ffn_rows.append(all_cores(tie(square.across, ffn_out[0][0], *square.done())))
+    ffn_out.append(ffn_both(tie(ffn_rows[2], ffn_out[1][0]), grad_rows[2], ffn_full))
+    beside_sums, across_sums = low(core_sum(ffn_out[1][3])), low(core_sum(ffn_out[2][3]))
+    ffn_rows.append(tie(all_cores(square.far()), beside_sums, across_sums))
+    ffn_out.append(ffn_both(ffn_rows[3], grad_rows[3], ffn_full))
+    near_sums = (flip(beside_sums, "ctx", 1), flip(across_sums, "ctx", 2))
+    far_sums = core_sum(tie(ffn_out[3][3], *near_sums))
+    ffn_rows[0] = tie(ffn_rows[0], ffn_out[2][3])
+    for i in (1, 2, 3):
+        ffn_rows[i], grad_rows[i] = tie(ffn_rows[i], far_sums), tie(grad_rows[i], far_sums)
+    far_sums = flip(low(far_sums), "ctx", 3)
+    grad_normed = core_sum(ffn_out[0][3]) + wide(near_sums[0]) + wide(near_sums[1]) + wide(far_sums)
+    back_ffn, unit_ffn = norm_backward(grad_normed, residual, scale_ffn, gain_ffn)
+    grad_residual = wide(grads_mine) + back_ffn
+    gain_ffn_part = jnp.sum(grad_normed * unit_ffn, axis=0)
+    grad_branch = rows_full(low(grad_residual).reshape(seq_count, -1, width)).reshape(row_count, width)
     grad_heads = times(grad_branch, out_full)
     backs, acrosses, gain_o_part = [], [], 0.0
     for p in range(parts):
@@ -833,61 +901,90 @@
         acrosses.append(across)
         gain_o_part = gain_o_part + jnp.sum(gain_part, axis=(0, 1, 2))
     grad_end = pass_states(jnp.concatenate(acrosses, axis=1), jnp.concatenate(transfers, axis=1), -1)
+    result_near = [
+        flip(tie(low(core_sum(tie(ffn_out[bit][4], grad_branch))), grad_end), "ctx", bit) for bit in (1, 2)
+    ]
+    result_far = core_sum(tie(ffn_out[3][4], grad_branch))
+    result_own = core_sum(tie(ffn_out[0][4], grad_branch))
 
     sums = []
     for kind, sources in ((1, ffn_rows), (2, ffn_rows), (0, grad_rows)):
         total = 0.0
-        for s in seqs:
-            total = total + outer_rows(ffn_out[s][kind], sources[s])
-        count = lax.axis_size("fsdp")
-        sums.append(line_sum(jnp.stack([total[:, i * 4 * shard_rows : (i + 1) * 4 * shard_rows] for i in range(count)])))
-    sums = jnp.stack(sums).reshape(3 * units, 4, shard_rows).transpose(1, 0, 2)
-    arrived = swap_square(sums).reshape(4, 3, units, shard_rows)
-    gate_grad, up_grad, down_grad = (wide(arrived[:, i].reshape(units_here, shard_rows)) for i in range(3))
-
-    out_grad_w = outer_scatter(neighbour_columns(grad_branch), mixed_rows).T
+        for out, source in zip(ffn_out, sources):
+            total = total + outer_rows(out[kind], source)
+        sums.append(total)
+    sums = columns_split(sums, line_count, 4).reshape(line_count, 3 * units, 4 * shard_rows)
+
+    def line_piece(distance):
+        return lax.dynamic_index_in_dim(sums, (line_place + distance) % line_count, 0, keepdims=False)
+
+    total = wide(line_piece(0))
+    cut = 3 * units // 2
+    line_sends = [(d, 0, 3 * units) for d in ends_apart]
+    line_sends += [(d, at, at + cut) for d in range(2, line_count - 1) for at in (0, cut)]
+    line_got = []
+    for d, low_row, high_row in line_sends:
+        piece = line_piece(d)[low_row:high_row]
+        if line_got:
+            piece = tie(piece, grad_end, line_got[-1])
+        line_got.append(shift(piece, "fsdp", d))
+
+    out_grad_w = low(outer_rows(grad_branch, mixed_rows))
+    out_grad_w = wide(lax.psum_scatter(out_grad_w, ("ctx", "fsdp"), scatter_dimension=0, tiled=True)).T
 
     columns = neighbour_columns(normed_mix)
     mix_back, mix_grads, conv_parts = 0.0, [None] * parts, [None] * parts
     logits = 0.0
+    scatter = None
     for p in reversed(range(parts)):
         halo, convs, own, carry, final, inverses, updates, states = kept[p]
         heads = slice(p * part_heads, (p + 1) * part_heads)
+        back = tie(backs[p], *line_got[:1]) if scatter is None else tie(backs[p], *scatter.sent)
         grad_mix, tail, before, conv_parts[p], logit = mixer_backward(
-            pre[p], pre[0], bias, halo, convs, col, row, backs[p], inverses, updates, states,
+            pre[p], pre[0], bias, halo, convs, col, row, back, inverses, updates, states,
             entered[p], grad_end[:, heads], taps, p * part_heads, part_heads, group,
         )
         logits = logits + logit
         tail = low(tail + from_behind(before, "ctx", -1))
         grad_mix = put(grad_mix.reshape(seq_count, local_len, -1), tail, 0, local_len - HALO, 0)
         grad_mix = grad_mix.reshape(row_count, -1)
+        if scatter is not None:
+            mix_grads[p + 1] = scatter.finish(grad_mix)
+        else:
+            grad_mix = tie(grad_mix, *result_near, *line_got[1:2])
         if p == 0:
-            grad_mix = jnp.concatenate([grad_mix, low(logits)], axis=1)
+            grad_mix = tie(jnp.concatenate([grad_mix, low(logits)], axis=1), *line_got[2:3])
         mix_back = mix_back + times_transposed(grad_mix, mix_full[p])
-        mix_grads[p] = outer_scatter(columns, grad_mix)
+        scatter = Scatter(columns, grad_mix)
+    mix_grads[0] = scatter.finish()
+    for (_, low_row, high_row), part in zip(line_sends, line_got):
+        total = total + jnp.pad(wide(part), ((low_row, total.shape[0] - high_row), (0, 0)))
+    sums = tie(low(total), grad_mix).reshape(3 * units, 4, shard_rows).transpose(1, 0, 2)
+    arrived = lax.all_to_all(sums, "ctx", 0, 0).reshape(4, 3, units, shard_rows)
+    gate_grad, up_grad, down_grad = (wide(arrived[:, i].reshape(units_here, shard_rows)) for i in range(3))
+    result = result_own + wide(result_near[0]) + wide(result_near[1])
+    result = result + wide(flip(low(tie(result_far, *scatter.last)), "ctx", 3))
+    block_output = rows_full(low(residual + result).reshape(seq_count, -1, width))
     joined = jnp.concatenate([grad[:, :part_cols] for grad in mix_grads], axis=1)
     query_grad, key_grad, value_grad = by_kind(joined)
     beta_grad = mix_grads[0][:, part_cols : part_cols + heads_here]
 
-    mix_back = rows_scatter(low(mix_back).reshape(seq_count, local_len, width))
+    mix_back = rows_scatter(low(mix_back).reshape(seq_count, local_len, width)).reshape(-1, width)
     back_mix, unit_mix = norm_backward(mix_back, inputs_mine, rms_scale(inputs_mine, EPSILON), gain_mix)
-    input_held = low(jnp.stack(grad_residual) + back_mix)
-    input_grad = features_back(rows_full(input_held).reshape(row_count, width))
-    gain_mix_part = jnp.sum(mix_back * unit_mix, axis=(0, 1))
-
-    gains = features_back(jnp.stack([gain_mix_part, gain_ffn_part]))
-    small = butterfly(
-        jnp.concatenate([gains[0], gains[1], gain_o_part]), ("tp", "ctx", "fsdp")
-    )
-    gain_mix_grad, gain_ffn_grad, gain_o_grad = jnp.split(small, [width, 2 * width])
+    input_grad = rows_full(low(grad_residual + back_mix).reshape(seq_count, -1, width))
+    gain_mix_part = jnp.sum(mix_back * unit_mix, axis=0)
+
     conv_cols = jnp.concatenate([jnp.sum(part, axis=0)[:taps] for part in conv_parts], axis=1)
-    sums = jnp.concatenate([conv_cols.reshape(-1), jnp.sum(logits, axis=0)])
+    gains = butterfly(jnp.concatenate([gain_mix_part, gain_ffn_part, gain_o_part]), ("tp",))
+    sums = jnp.concatenate([gains, conv_cols.reshape(-1), jnp.sum(logits, axis=0)])
     sums = butterfly(sums, ("ctx", "fsdp"))
-    conv_grad = jnp.stack(by_kind(sums[:-LANES].reshape(taps, -1)))
-    bias_grad = sums[sums.shape[0] - LANES :][:heads_here]
+    ends = [width, 2 * width, 2 * width + LANES, sums.shape[0] - LANES]
+    gain_mix_grad, gain_ffn_grad, gain_o_grad, conv_grad, bias_grad = jnp.split(sums, ends)
+    conv_grad = jnp.stack(by_kind(conv_grad.reshape(taps, -1)))
+    bias_grad = bias_grad[:heads_here]
     return (
-        block_output.reshape(seq_count, local_len, width),
-        input_grad.reshape(seq_count, local_len, width),
+        block_output,
+        input_grad,
         gain_mix_grad,
         query_grad,
         key_grad,

time: 1610 us -> 1930 us (1.20)
  Pallas kernels: 241 us -> 949 us
  local copies, waits for them, and re-layouts: 305 us -> 150 us
  starting transfers between devices: 253 us -> 132 us
  waiting for transfers between devices: 473 us -> 362 us
  other arithmetic: 156 us -> 128 us
    pallas_call x0 -> x11, Pallas kernels: none -> 697 us  [the longest x6 666 us: place_blocks(): pl.pallas_call(functools.partial(place_kernel, count), grid_spec=pltpu.Pr...]
    ppermute x116 -> x64, waiting for transfers between devices: 295 us -> 155 us  [flip(): return lax.ppermute(value, axis, [(i, i ^ bit) for i in devices])]
    ppermute x30 -> x23, starting transfers between devices: 113 us -> 35 us  [shift(): lax.ppermute(value, axis, [(i, (i + distance) % count) for i in range(cou...]
    ppermute x116 -> x64, starting transfers between devices: 103 us -> 50.6 us  [flip(): return lax.ppermute(value, axis, [(i, i ^ bit) for i in devices])]
    another operation x15 -> x2, other arithmetic: 52.5 us -> 1.27 us  [the longest x1 0.64 us: place_blocks(): jnp.stack(targets).astype(jnp.int32)]
    another operation x11 -> x8, local copies, waits for them, and re-layouts: 50.8 us -> 4.72 us  [the longest x3 4.07 us: by_kind(): return [split[..., kind, :].reshape(lead + (-1,)) for kind in range(3)]]
    ppermute x30 -> x23, waiting for transfers between devices: 130 us -> 166 us  [shift(): lax.ppermute(value, axis, [(i, (i + distance) % count) for i in range(cou...]
    convert_element_type x18, other arithmetic: 24.6 us -> 50.5 us  [low(): return value.astype(jnp.bfloat16)]
  transfers between devices with their start and end apart: 159 -> 103, of which waited for: 54 -> 33; matrix products, arithmetic and copies ran while one was open for 31% -> 21% of each run, Pallas kernels for 11% -> 49%
where the time goes in v3:
time: 1930 us; the launch traced here: 1920 us
  Pallas kernels  949 us (49%)
  waiting for transfers between devices  362 us (19%)
  matrix products  178 us (9%)
  local copies, waits for them, and re-layouts  150 us (8%)
  starting transfers between devices  132 us (7%)
  other arithmetic  128 us (7%)
    pallas_call x6, Pallas kernels, place_blocks(): pl.pallas_call(functools.partial(place_kernel, count), grid_spec=pltpu.Pr...  666 us
    ppermute x23, waiting for transfers between devices, shift(): lax.ppermute(value, axis, [(i, (i + distance) % count) for i in range(cou...  166 us
    ppermute x64, waiting for transfers between devices, flip(): return lax.ppermute(value, axis, [(i, i ^ bit) for i in devices])  155 us
    dot_general x29, matrix products, outer_rows(): lax.dot_general(left, right, (((0,), (0,)), ((), ())), preferred_element_...  121 us
    pallas_call x4, Pallas kernels, ffn_both(): pl.pallas_call(ffn_kernel, grid=(count // tile,), in_specs=[wide, wide, t...  110 us
    pallas_call x2, Pallas kernels, mixer_backward(): pl.pallas_call(functools.partial(backward_kernel, taps, group, first), gr...  66.8 us
    pallas_call x2, Pallas kernels, mixer_forward(): pl.pallas_call(functools.partial(forward_kernel, taps, group, first), gri...  55 us
    ppermute x64, starting transfers between devices, flip(): return lax.ppermute(value, axis, [(i, i ^ bit) for i in devices])  50.6 us
  transfers between devices with their start and end apart: 103, of which 33 were waited for; matrix products, arithmetic and copies ran while one was open for 21% of the time, Pallas kernels for 49%

profile of v3, /device:TPU:0, one launch (start us, length us, event | category | flops | bytes accessed | tf_op | source)
XLA Modules:
  0.0 1915.6 jit_solution(4388188481314246294)
XLA Ops:
  12.6 5.2 all-to-all-start
  27.8 24.9 %collective-permute-done.1 = bf16[128,1664]{1,0:T(8,128)(2,1)} collective-permute-done((bf16[128,1664]{1,0:T(8,128)(2,1)S(1)}, bf16[128,1664]{1,0:T(8,128)(2,1)}, u32[]{:S(2)}, u32[]{:S(2)}) %collective-permute-start.1) | collective-permute-done | bytes 426016 | tf_op jit(solution)/shard_map/ppermute | solution.py:555
  53.1 53.4 %shard_map.271.refs_0_ = bf16[4,128,1664]{2,1,0:T(8,128)(2,1)} custom-call(s32[4]{0:T(128)} %pad_add_fusion.targets, bf16[1,128,1664]{2,1,0:T(8,128)(2,1)} %get-tuple-element.335.refs_0_, bf16[1,128,1664]{2,1,0:T(8,128)(2,1)} %bitcast.16.refs_1_, bf16[1,128,1664]{2,1,0:T(8,128)(2,1)} %bitcast.17.refs_2_, bf16[1,128,1664]{2,1,0:T(8,128)(2,1)} %bitcast.18.refs_3_), custom_call_target="tpu_custom_call" | custom-call | bytes 3407872 | tf_op jit(solution)/shard_map/pallas_call | solution.py:491
  120.1 24.9 %collective-permute-done.4.refs_2_ = bf16[4,128,1664]{2,1,0:T(8,128)(2,1)} collective-permute-done((bf16[4,128,1664]{2,1,0:T(8,128)(2,1)}, bf16[4,128,1664]{2,1,0:T(8,128)(2,1)}, u32[]{:S(2)}, u32[]{:S(2)}) %collective-permute-start.4) | collective-permute-done | bytes 1703968 | tf_op jit(solution)/shard_map/ppermute | solution.py:550
  159.0 9.7 collective-permute-start.12
  174.7 27.2 %collective-permute-done.12 = bf16[128,1536]{1,0:T(8,128)(2,1)S(1)} collective-permute-done((bf16[128,1536]{1,0:T(8,128)(2,1)S(1)}, bf16[128,1536]{1,0:T(8,128)(2,1)S(1)}, u32[]{:S(2)}, u32[]{:S(2)}) %collective-permute-start.12) | collective-permute-done | bytes 393248 | tf_op jit(solution)/shard_map/ppermute | solution.py:555
  203.3 49.4 %shard_map.275.refs_0_ = bf16[4,128,1536]{2,1,0:T(8,128)(2,1)} custom-call(s32[4]{0:T(128)} %pad_add_fusion.targets, bf16[1,128,1536]{2,1,0:T(8,128)(2,1)} %bitcast.334, bf16[1,128,1536]{2,1,0:T(8,128)(2,1)} %bitcast.351, bf16[1,128,1536]{2,1,0:T(8,128)(2,1)} %bitcast.350, bf16[1,128,1536]{2,1,0:T(8,128)(2,1)} %bitcast.349), custom_call_target="tpu_custom_call" | custom-call | bytes 3145728 | tf_op jit(solution)/shard_map/pallas_call | solution.py:491
  254.8 208.3 %shard_map.272 = bf16[16,128,1664]{2,1,0:T(8,128)(2,1)} custom-call(s32[5]{0:T(128)} %stack.81.targets, bf16[4,128,1664]{2,1,0:T(8,128)(2,1)} %shard_map.271.refs_0_, bf16[4,128,1664]{2,1,0:T(8,128)(2,1)} %collective-permute-done.3.refs_1_, bf16[4,128,1664]{2,1,0:T(8,128)(2,1)} %collective-permute-done.4.refs_2_, ...), custom_call_target="tpu_custom_call" | custom-call | bytes 13631488 | tf_op jit(solution)/shard_map/pallas_call | solution.py:491
  463.1 11.5 fusion.97.pre.beta
  484.6 27.5 %shard_map.273 = (f32[1024,512]{1,0:T(8,128)}, bf16[1024,512]{1,0:T(8,128)(2,1)}, f32[2,4,128,256]{3,2,1,0:T(8,128)}, bf16[2,4,4,128,128]{4,3,2,1,0:T(8,128)(2,1...) custom-call(f32[1024,1664]{1,0:T(8,128)} %copy-done.5, f32[1024,1664]{1,0:T(8,128)} %copy-done.5, ...), custom_call_target="tpu_custom_call" | custom-call | flops 4026531840 | bytes 20971520 | tf_op jit(solution)/shard_map/pallas_call | solution.py:160
  512.1 27.0 %collective-permute-done.15 = bf16[128,1024]{1,0:T(8,128)(2,1)S(1)} collective-permute-done((bf16[128,1024]{1,0:T(8,128)(2,1)S(1)}, bf16[128,1024]{1,0:T(8,128)(2,1)S(1)}, u32[]{:S(2)}, u32[]{:S(2)}) %collective-permute-start.15) | collective-permute-done | bytes 262176 | tf_op jit(solution)/shard_map/ppermute | solution.py:555
  551.8 5.2 fusion.1
  557.0 33.6 %shard_map.276.refs_0_ = bf16[4,128,1024]{2,1,0:T(8,128)(2,1)} custom-call(s32[4]{0:T(128)} %pad_add_fusion.targets, bf16[1,128,1024]{2,1,0:T(8,128)(2,1)} %bitcast.338, bf16[1,128,1024]{2,1,0:T(8,128)(2,1)} %bitcast.354, bf16[1,128,1024]{2,1,0:T(8,128)(2,1)} %bitcast.353, bf16[1,128,1024]{2,1,0:T(8,128)(2,1)} %bitcast.352), custom_call_target="tpu_custom_call" | custom-call | bytes 2097152 | tf_op jit(solution)/shard_map/pallas_call | solution.py:491
  606.1 192.4 %shard_map.277 = bf16[16,128,1536]{2,1,0:T(8,128)(2,1)} custom-call(s32[5]{0:T(128)} %stack.81.targets, bf16[4,128,1536]{2,1,0:T(8,128)(2,1)} %shard_map.275.refs_0_, bf16[4,128,1536]{2,1,0:T(8,128)(2,1)} %collective-permute-done.17.refs_1_, bf16[4,128,1536]{2,1,0:T(8,128)(2,1)} %collective-permute-done.18.refs_2_, ...), custom_call_target="tpu_custom_call" | custom-call | bytes 12582912 | tf_op jit(solution)/shard_map/pallas_call | solution.py:491
  798.5 10.1 fusion.98.pre
  816.6 27.5 %shard_map.278 = (f32[1024,512]{1,0:T(8,128)}, bf16[1024,512]{1,0:T(8,128)(2,1)}, f32[2,4,128,256]{3,2,1,0:T(8,128)}, bf16[2,4,4,128,128]{4,3,2,1,0:T(8,128)(2,1...) custom-call(f32[1024,1536]{1,0:T(8,128)} %copy-done.22, f32[1024,1664]{1,0:T(8,128)} %copy-done.5, ...), custom_call_target="tpu_custom_call" | custom-call | flops 4026531840 | bytes 20971520 | tf_op jit(solution)/shard_map/pallas_call | solution.py:160
  882.8 6.4 collective-permute-done.27
  889.2 128.9 %shard_map.280 = bf16[16,128,1024]{2,1,0:T(8,128)(2,1)} custom-call(s32[5]{0:T(128)} %stack.81.targets, bf16[4,128,1024]{2,1,0:T(8,128)(2,1)} %shard_map.276.refs_0_, bf16[4,128,1024]{2,1,0:T(8,128)(2,1)} %collective-permute-done.33.refs_1_, bf16[4,128,1024]{2,1,0:T(8,128)(2,1)} %collective-permute-done.34.refs_2_, ...), custom_call_target="tpu_custom_call" | custom-call | bytes 8388608 | tf_op jit(solution)/shard_map/pallas_call | solution.py:491
  1024.4 7.4 convolution_convert_fusion.1
  1032.5 5.9 collective-permute-done.37
  1074.8 27.5 %shard_map.285 = (bf16[1024,704]{1,0:T(8,128)(2,1)}, bf16[1024,704]{1,0:T(8,128)(2,1)}, bf16[1024,704]{1,0:T(8,128)(2,1)}, bf16[1024,2048]{1,0:T(8,128)(2,1)}, bf16[1024,2048]{1,0:T(8,128)(2,1)}) custom-call(bf16[1024,2048]{1,0:T(8,128)(2,1)} %pad_maximum_fusion.rows, bf16[1024,2048]{1,0:T(8,128)(2,1)} %constant_dynamic-update-slice_fusion.grads, ...), custom_call_target="tpu_custom_call" | custom-call | flops 17716740096 | bytes 25427968 | tf_op jit(solution)/shard_map/pallas_call | solution.py:461
  1102.3 11.1 collective-permute-done.41
  1131.0 11.3 collective-permute-done.47
  1146.2 27.3 %shard_map.286 = (bf16[1024,704]{1,0:T(8,128)(2,1)}, bf16[1024,704]{1,0:T(8,128)(2,1)}, bf16[1024,704]{1,0:T(8,128)(2,1)}, bf16[1024,2048]{1,0:T(8,128)(2,1)}, bf16[1024,2048]{1,0:T(8,128)(2,1)}) custom-call(bf16[1024,2048]{1,0:T(8,128)(2,1)} %constant_dynamic-update-slice_fusion.2.rows, bf16[1024,2048]{1,0:T(8,128)(2,1)} %copy-done.51, ...), custom_call_target="tpu_custom_call" | custom-call | flops 17716740096 | bytes 25427968 | tf_op jit(solution)/shard_map/pallas_call | solution.py:461
  1180.5 27.6 %shard_map.287 = (bf16[1024,704]{1,0:T(8,128)(2,1)}, bf16[1024,704]{1,0:T(8,128)(2,1)}, bf16[1024,704]{1,0:T(8,128)(2,1)}, bf16[1024,2048]{1,0:T(8,128)(2,1)}, bf16[1024,2048]{1,0:T(8,128)(2,1)}) custom-call(bf16[1024,2048]{1,0:T(8,128)(2,1)} %constant_dynamic-update-slice_fusion.6.rows, bf16[1024,2048]{1,0:T(8,128)(2,1)} %copy-done.14, ...), custom_call_target="tpu_custom_call" | custom-call | flops 17716740096 | bytes 25427968 | tf_op jit(solution)/shard_map/pallas_call | solution.py:461
  1238.0 27.8 %shard_map.288 = (bf16[1024,704]{1,0:T(8,128)(2,1)}, bf16[1024,704]{1,0:T(8,128)(2,1)}, bf16[1024,704]{1,0:T(8,128)(2,1)}, bf16[1024,2048]{1,0:T(8,128)(2,1)}, bf16[1024,2048]{1,0:T(8,128)(2,1)}) custom-call(bf16[1024,2048]{1,0:T(8,128)(2,1)} %pad_maximum_fusion.1.rows, bf16[1024,2048]{1,0:T(8,128)(2,1)} %copy-done.63, ...), custom_call_target="tpu_custom_call" | custom-call | flops 17716740096 | bytes 25427968 | tf_op jit(solution)/shard_map/pallas_call | solution.py:461
  1265.8 6.4 collective-permute-done.45
  1281.8 5.3 fusion.103
  1297.4 8.0 fusion.104
  1305.3 8.2 fusion.101
  1313.6 5.1 fusion.105
  1318.7 13.6 add_add_fusion.1.second
  1332.3 6.5 fusion.102
  1338.9 11.7 add_add_fusion.2.first
  1350.6 6.2 multiply_reduce_fusion.1
  1359.4 5.1 fusion.108
  1364.6 5.3 add_add_fusion.third
  1369.9 14.8 shard_map.291
  1389.3 6.0 fusion.11
  1397.3 6.0 fusion.99.grad
  1403.3 5.7 shard_map.290
  1409.0 5.8 shard_map.289
  1422.1 10.2 collective-permute-done.60
  1435.4 13.0 collective-permute-done.61
  1454.8 9.3 collective-permute-done.62
  1477.9 33.2 %shard_map.292 = (bf16[1024,1536]{1,0:T(8,128)(2,1)}, f32[2,8,1536]{2,1,0:T(8,128)}, f32[2,8,1536]{2,1,0:T(8,128)}, f32[2,8,1536]{2,1,0:T(8,128)}, f32[1024,128]{1,0:T(8,128)}) custom-call(f32[1024,1536]{1,0:T(8,128)} %copy-done.22, f32[1024,1664]{1,0:T(8,128)} %copy-done.5, f32[1,128]{1,0:T(1,128)} %pad_bitcast_fusion.bias, f32[2,8,1536]{2,1,0:T(8,128)} %copy-done.71, ...), custom_call_target="tpu_custom_call" | custom-call | flops 4026531840 | bytes 20971520 | tf_op jit(solution)/shard_map/pallas_call | solution.py:318
  1512.7 8.5 convolution_convert_fusion
  1524.7 5.7 convert_add_fusion.3
  1542.8 33.5 %shard_map.293 = (bf16[1024,1536]{1,0:T(8,128)(2,1)}, f32[2,8,1536]{2,1,0:T(8,128)}, f32[2,8,1536]{2,1,0:T(8,128)}, f32[2,8,1536]{2,1,0:T(8,128)}, f32[1024,128]{1,0:T(8,128)}) custom-call(f32[1024,1664]{1,0:T(8,128)} %copy-done.5, f32[1024,1664]{1,0:T(8,128)} %copy-done.5, f32[1,128]{1,0:T(1,128)} %pad_bitcast_fusion.bias, f32[2,8,1536]{2,1,0:T(8,128)} %copy-done.70, ...), custom_call_target="tpu_custom_call" | custom-call | flops 4026531840 | bytes 20971520 | tf_op jit(solution)/shard_map/pallas_call | solution.py:318
  1580.0 6.3 collective-permute-done.70
  1590.2 35.5 %collective-permute-done.71 = bf16[1056,512]{1,0:T(8,128)(2,1)} collective-permute-done((bf16[1056,512]{1,0:T(8,128)(2,1)}, bf16[1056,512]{1,0:T(8,128)(2,1)}, u32[]{:S(2)}, u32[]{:S(2)}) %collective-permute-start.71) | collective-permute-done | bytes 1081376 | tf_op jit(solution)/shard_map/ppermute | solution.py:555
  1629.9 10.2 fusion.109
  1640.0 9.2 add_convert_fusion
  1663.8 15.9 collective-permute-done.72
  1684.3 13.9 collective-permute-done.94
  1722.9 6.0 fusion.5
  1741.7 8.5 collective-permute-done.97
  1756.3 29.2 %collective-permute-done.86 = bf16[256,1664]{1,0:T(8,128)(2,1)S(1)} collective-permute-done((bf16[256,1664]{1,0:T(8,128)(2,1)}, bf16[256,1664]{1,0:T(8,128)(2,1)S(1)}, u32[]{:S(2)}, u32[]{:S(2)}) %collective-permute-start.86) | collective-permute-done | bytes 852000 | tf_op jit(solution)/shard_map/ppermute | solution.py:550
  1791.2 5.2 fusion.19
  1813.4 26.4 %collective-permute-done.88 = bf16[128,1664]{0,1:T(8,128)(2,1)S(1)} collective-permute-done((bf16[128,1664]{0,1:T(8,128)(2,1)S(1)}, bf16[128,1664]{0,1:T(8,128)(2,1)S(1)}, u32[]{:S(2)}, u32[]{:S(2)}) %collective-permute-start.88) | collective-permute-done | bytes 426016 | tf_op jit(solution)/shard_map/ppermute | solution.py:555
  1840.0 17.3 collective-permute-done.82
  1873.7 11.4 fusion.15
  1894.5 6.7 fusion.9
  1901.2 7.1 fusion.7
  (588 shorter events, 438.3 us)
Async XLA Ops:
  12.6 93.9 %all-to-all-start = ((bf16[4,2112,128]{2,1,0:T(8,128)(2,1)}), bf16[4,2112,128]{2,1,0:T(8,128)(2,1)S(1)}, u32[]{:S(2)}, u32[]{:S(2)}) async-start(bf16[4,2112,128]{2,1,0:T(8,128)(2,1)} %bitcast.299), calls=%async_computation | async-start | bytes 4325376 | tf_op jit(solution)/shard_map/all_to_all | solution.py:791
  17.8 1874.7 %reduce-scatter.2.cloned.1.call-start = ((), (), s32[]{:S(2)}) async-start(), calls=%async_computation.3 | async-start | bytes 4456448 | tf_op jit(solution)/shard_map/reduce_scatter | solution.py:933
  108.3 36.8 %collective-permute-start.4 = (bf16[4,128,1664]{2,1,0:T(8,128)(2,1)}, bf16[4,128,1664]{2,1,0:T(8,128)(2,1)}, u32[]{:S(2)}, u32[]{:S(2)}) collective-permute-start(bf16[4,128,1664]{2,1,0:T(8,128)(2,1)} %shard_map.271.refs_0_), channel_id=1, source_target_pairs={{0,16},{8,24},{16,0},{24,8},{1,17},{9,25},{17,1},{25,9},{2,18},{10... | collective-permute-start | bytes 5111816 | tf_op jit(solution)/shard_map/ppermute | solution.py:550
  109.9 38.9 %collective-permute-start.3 = (bf16[4,128,1664]{2,1,0:T(8,128)(2,1)}, bf16[4,128,1664]{2,1,0:T(8,128)(2,1)}, u32[]{:S(2)}, u32[]{:S(2)}) collective-permute-start(bf16[4,128,1664]{2,1,0:T(8,128)(2,1)} %shard_map.271.refs_0_), channel_id=1, source_target_pairs={{0,8},{8,0},{16,24},{24,16},{1,9},{9,1},{17,25},{25,17},{2,10},{10... | collective-permute-start | bytes 5111816 | tf_op jit(solution)/shard_map/ppermute | solution.py:550
  147.2 106.7 %collective-permute-start.6 = (bf16[2,128,1664]{2,1,0:T(8,128)(2,1)}, bf16[2,128,1664]{2,1,0:T(8,128)(2,1)}, u32[]{:S(2)}, u32[]{:S(2)}) collective-permute-start(bf16[2,128,1664]{2,1,0:T(8,128)(2,1)} %slice.297), channel_id=1, source_target_pairs={{0,8},{8,0},{16,24},{24,16},{1,9},{9,1},{17,25},{25,17},{2,10},{10... | collective-permute-start | bytes 2555912 | tf_op jit(solution)/shard_map/ppermute | solution.py:550
  150.9 102.9 %collective-permute-start.5 = (bf16[2,128,1664]{2,1,0:T(8,128)(2,1)}, bf16[2,128,1664]{2,1,0:T(8,128)(2,1)}, u32[]{:S(2)}, u32[]{:S(2)}) collective-permute-start(bf16[2,128,1664]{2,1,0:T(8,128)(2,1)} %slice.296), channel_id=1, source_target_pairs={{0,16},{8,24},{16,0},{24,8},{1,17},{9,25},{17,1},{25,9},{2,18},{10... | collective-permute-start | bytes 2555912 | tf_op jit(solution)/shard_map/ppermute | solution.py:550
  159.0 42.8 %collective-permute-start.12 = (bf16[128,1536]{1,0:T(8,128)(2,1)S(1)}, bf16[128,1536]{1,0:T(8,128)(2,1)S(1)}, u32[]{:S(2)}, u32[]{:S(2)}) collective-permute-start(bf16[128,1536]{1,0:T(8,128)(2,1)S(1)} %copy.218), channel_id=1, source_target_pairs={{0,2},{1,3},{2,0},{3,1},{4,6},{5,7},{6,4},{7,5},{8,10},{9,11},{10,... | collective-permute-start | bytes 1179656 | tf_op jit(solution)/shard_map/ppermute | solution.py:555
  168.7 33.1 %collective-permute-start.11 = (bf16[128,1536]{1,0:T(8,128)(2,1)S(1)}, bf16[128,1536]{1,0:T(8,128)(2,1)S(1)}, u32[]{:S(2)}, u32[]{:S(2)}) collective-permute-start(bf16[128,1536]{1,0:T(8,128)(2,1)S(1)} %copy.218), channel_id=1, source_target_pairs={{0,1},{1,2},{2,3},{3,0},{4,5},{5,6},{6,7},{7,4},{8,9},{9,10},{10,1... | collective-permute-start | bytes 1179656 | tf_op jit(solution)/shard_map/ppermute | solution.py:555
  252.8 228.7 %collective-permute-start.16 = (bf16[128,1024]{1,0:T(8,128)(2,1)S(1)}, bf16[128,1024]{1,0:T(8,128)(2,1)S(1)}, u32[]{:S(2)}, u32[]{:S(2)}) collective-permute-start(bf16[128,1024]{1,0:T(8,128)(2,1)S(1)} %bitcast.335), channel_id=1, source_target_pairs={{0,3},{1,0},{2,1},{3,2},{4,7},{5,4},{6,5},{7,6},{8,11},{9,8},{10,9... | collective-permute-start | bytes 786440 | tf_op jit(solution)/shard_map/ppermute | solution.py:555
  252.9 298.4 %collective-permute-start.21 = (bf16[2112,512]{1,0:T(8,128)(2,1)}, bf16[2112,512]{1,0:T(8,128)(2,1)}, u32[]{:S(2)}, u32[]{:S(2)}) collective-permute-start(bf16[2112,512]{1,0:T(8,128)(2,1)} %copy_bitcast_fusion.source), channel_id=1, source_target_pairs={{0,3},{1,0},{2,1},{3,2},{4,7},{5,4},{6,5},{7,6},{8,11},{9,8},{10,9... | collective-permute-start | bytes 6488072 | tf_op jit(solution)/shard_map/ppermute | solution.py:555
  253.9 286.7 %collective-permute-start.18 = (bf16[4,128,1536]{2,1,0:T(8,128)(2,1)}, bf16[4,128,1536]{2,1,0:T(8,128)(2,1)}, u32[]{:S(2)}, u32[]{:S(2)}) collective-permute-start(bf16[4,128,1536]{2,1,0:T(8,128)(2,1)} %shard_map.275.refs_0_), channel_id=1, source_target_pairs={{0,16},{8,24},{16,0},{24,8},{1,17},{9,25},{17,1},{25,9},{2,18},{10... | collective-permute-start | bytes 4718600 | tf_op jit(solution)/shard_map/ppermute | solution.py:550
  254.4 286.3 %collective-permute-start.17 = (bf16[4,128,1536]{2,1,0:T(8,128)(2,1)}, bf16[4,128,1536]{2,1,0:T(8,128)(2,1)}, u32[]{:S(2)}, u32[]{:S(2)}) collective-permute-start(bf16[4,128,1536]{2,1,0:T(8,128)(2,1)} %shard_map.275.refs_0_), channel_id=1, source_target_pairs={{0,8},{8,0},{16,24},{24,16},{1,9},{9,1},{17,25},{25,17},{2,10},{10... | collective-permute-start | bytes 4718600 | tf_op jit(solution)/shard_map/ppermute | solution.py:550
  481.5 57.6 %collective-permute-start.15 = (bf16[128,1024]{1,0:T(8,128)(2,1)S(1)}, bf16[128,1024]{1,0:T(8,128)(2,1)S(1)}, u32[]{:S(2)}, u32[]{:S(2)}) collective-permute-start(bf16[128,1024]{1,0:T(8,128)(2,1)S(1)} %bitcast.336), channel_id=1, source_target_pairs={{0,2},{1,3},{2,0},{3,1},{4,6},{5,7},{6,4},{7,5},{8,10},{9,11},{10,... | collective-permute-start | bytes 786440 | tf_op jit(solution)/shard_map/ppermute | solution.py:555
  484.0 109.5 %collective-permute-start.20 = (bf16[2112,512]{1,0:T(8,128)(2,1)}, bf16[2112,512]{1,0:T(8,128)(2,1)}, u32[]{:S(2)}, u32[]{:S(2)}) collective-permute-start(bf16[2112,512]{1,0:T(8,128)(2,1)} %copy_bitcast_fusion.source), channel_id=1, source_target_pairs={{0,1},{1,2},{2,3},{3,0},{4,5},{5,6},{6,7},{7,4},{8,9},{9,10},{10,1... | collective-permute-start | bytes 6488072 | tf_op jit(solution)/shard_map/ppermute | solution.py:555
  539.1 54.3 %collective-permute-start.24 = (bf16[512,2048]{1,0:T(8,128)(2,1)S(1)}, bf16[512,2048]{1,0:T(8,128)(2,1)}, u32[]{:S(2)}, u32[]{:S(2)}) collective-permute-start(bf16[512,2048]{1,0:T(8,128)(2,1)S(1)} %bitcast.281), channel_id=1, source_target_pairs={{0,16},{8,24},{16,0},{24,8},{1,17},{9,25},{17,1},{25,9},{2,18},{10... | collective-permute-start | bytes 6291464 | tf_op jit(solution)/shard_map/ppermute | solution.py:550
  540.6 56.6 %collective-permute-start.23 = (bf16[512,2048]{1,0:T(8,128)(2,1)S(1)}, bf16[512,2048]{1,0:T(8,128)(2,1)}, u32[]{:S(2)}, u32[]{:S(2)}) collective-permute-start(bf16[512,2048]{1,0:T(8,128)(2,1)S(1)} %bitcast.282), channel_id=1, source_target_pairs={{0,8},{8,0},{16,24},{24,16},{1,9},{9,1},{17,25},{25,17},{2,10},{10... | collective-permute-start | bytes 6291464 | tf_op jit(solution)/shard_map/ppermute | solution.py:550
  549.5 55.1 %collective-permute-start.19 = (bf16[2,128,1536]{2,1,0:T(8,128)(2,1)}, bf16[2,128,1536]{2,1,0:T(8,128)(2,1)}, u32[]{:S(2)}, u32[]{:S(2)}) collective-permute-start(bf16[2,128,1536]{2,1,0:T(8,128)(2,1)} %slice.302), channel_id=1, source_target_pairs={{0,16},{8,24},{16,0},{24,8},{1,17},{9,25},{17,1},{25,9},{2,18},{10... | collective-permute-start | bytes 2359304 | tf_op jit(solution)/shard_map/ppermute | solution.py:550
  551.2 54.9 %collective-permute-start.22 = (bf16[2,128,1536]{2,1,0:T(8,128)(2,1)}, bf16[2,128,1536]{2,1,0:T(8,128)(2,1)}, u32[]{:S(2)}, u32[]{:S(2)}) collective-permute-start(bf16[2,128,1536]{2,1,0:T(8,128)(2,1)} %slice.303), channel_id=1, source_target_pairs={{0,8},{8,0},{16,24},{24,16},{1,9},{9,1},{17,25},{25,17},{2,10},{10... | collective-permute-start | bytes 2359304 | tf_op jit(solution)/shard_map/ppermute | solution.py:550
  593.5 221.5 %collective-permute-start.26 = (bf16[1056,512]{1,0:T(8,128)(2,1)}, bf16[1056,512]{1,0:T(8,128)(2,1)}, u32[]{:S(2)}, u32[]{:S(2)}) collective-permute-start(bf16[1056,512]{1,0:T(8,128)(2,1)} %bitcast.274), channel_id=1, source_target_pairs={{0,2},{1,3},{2,0},{3,1},{4,6},{5,7},{6,4},{7,5},{8,10},{9,11},{10,... | collective-permute-start | bytes 3244040 | tf_op jit(solution)/shard_map/ppermute | solution.py:555
  595.8 249.6 %collective-permute-start.29 = (bf16[256,2048]{1,0:T(8,128)(2,1)}, bf16[256,2048]{1,0:T(8,128)(2,1)}, u32[]{:S(2)}, u32[]{:S(2)}) collective-permute-start(bf16[256,2048]{1,0:T(8,128)(2,1)} %slice.309), channel_id=1, source_target_pairs={{0,8},{8,0},{16,24},{24,16},{1,9},{9,1},{17,25},{25,17},{2,10},{10... | collective-permute-start | bytes 3145736 | tf_op jit(solution)/shard_map/ppermute | solution.py:550
  599.6 245.8 %collective-permute-start.28 = (bf16[256,2048]{1,0:T(8,128)(2,1)}, bf16[256,2048]{1,0:T(8,128)(2,1)}, u32[]{:S(2)}, u32[]{:S(2)}) collective-permute-start(bf16[256,2048]{1,0:T(8,128)(2,1)} %slice.308), channel_id=1, source_target_pairs={{0,16},{8,24},{16,0},{24,8},{1,17},{9,25},{17,1},{25,9},{2,18},{10... | collective-permute-start | bytes 3145736 | tf_op jit(solution)/shard_map/ppermute | solution.py:550
  811.5 38.3 %collective-permute-start.8 = (bf16[2,4,128,128]{3,2,1,0:T(8,128)(2,1)S(1)}, bf16[2,4,128,128]{3,2,1,0:T(8,128)(2,1)S(1)}, u32[]{:S(2)}, u32[]{:S(2)}) collective-permute-start(bf16[2,4,128,128]{3,2,1,0:T(8,128)(2,1)S(1)} %get-tuple-element.328), channel_id=1, source_target_pairs={{0,8},{8,16},{16,24},{1,9},{9,17},{17,25},{2,10},{10,18},{18,26},{... | collective-permute-start | bytes 786440 | tf_op jit(solution)/shard_map/ppermute | solution.py:561
  814.9 51.3 %collective-permute-start.34 = (bf16[4,128,1024]{2,1,0:T(8,128)(2,1)}, bf16[4,128,1024]{2,1,0:T(8,128)(2,1)}, u32[]{:S(2)}, u32[]{:S(2)}) collective-permute-start(bf16[4,128,1024]{2,1,0:T(8,128)(2,1)} %shard_map.276.refs_0_), channel_id=1, source_target_pairs={{0,16},{8,24},{16,0},{24,8},{1,17},{9,25},{17,1},{25,9},{2,18},{10... | collective-permute-start | bytes 3145736 | tf_op jit(solution)/shard_map/ppermute | solution.py:550
  815.8 52.4 %collective-permute-start.33 = (bf16[4,128,1024]{2,1,0:T(8,128)(2,1)}, bf16[4,128,1024]{2,1,0:T(8,128)(2,1)}, u32[]{:S(2)}, u32[]{:S(2)}) collective-permute-start(bf16[4,128,1024]{2,1,0:T(8,128)(2,1)} %shard_map.276.refs_0_), channel_id=1, source_target_pairs={{0,8},{8,0},{16,24},{24,16},{1,9},{9,1},{17,25},{25,17},{2,10},{10... | collective-permute-start | bytes 3145736 | tf_op jit(solution)/shard_map/ppermute | solution.py:550
  849.8 39.4 %collective-permute-start.27 = (bf16[1056,512]{1,0:T(8,128)(2,1)}, bf16[1056,512]{1,0:T(8,128)(2,1)S(1)}, u32[]{:S(2)}, u32[]{:S(2)}) collective-permute-start(bf16[1056,512]{1,0:T(8,128)(2,1)} %bitcast.275), channel_id=1, source_target_pairs={{0,2},{1,3},{2,0},{3,1},{4,6},{5,7},{6,4},{7,5},{8,10},{9,11},{10,... | collective-permute-start | bytes 3244040 | tf_op jit(solution)/shard_map/ppermute | solution.py:555
  872.3 145.7 %collective-permute-start.32 = (bf16[2,4,128,128]{3,2,1,0:T(8,128)(2,1)}, bf16[2,4,128,128]{3,2,1,0:T(8,128)(2,1)}, u32[]{:S(2)}, u32[]{:S(2)}) collective-permute-start(bf16[2,4,128,128]{3,2,1,0:T(8,128)(2,1)} %fusion.37), channel_id=1, source_target_pairs={{0,8},{8,16},{16,24},{1,9},{9,17},{17,25},{2,10},{10,18},{18,26},{... | collective-permute-start | bytes 786440 | tf_op jit(solution)/shard_map/ppermute | solution.py:561
  1032.0 34.9 %collective-permute-start.39 = (bf16[512,2048]{1,0:T(8,128)(2,1)S(1)}, bf16[512,2048]{1,0:T(8,128)(2,1)}, u32[]{:S(2)}, u32[]{:S(2)}) collective-permute-start(bf16[512,2048]{1,0:T(8,128)(2,1)S(1)} %bitcast.283), channel_id=1, source_target_pairs={{0,4},{4,0},{1,5},{5,1},{2,6},{6,2},{3,7},{7,3},{8,12},{12,8},{9,1... | collective-permute-start | bytes 6291464 | tf_op jit(solution)/shard_map/ppermute | solution.py:550
  1064.2 58.8 %collective-permute-start.50 = (bf16[512,2048]{1,0:T(8,128)(2,1)}, bf16[512,2048]{1,0:T(8,128)(2,1)}, u32[]{:S(2)}, u32[]{:S(2)}) collective-permute-start(bf16[512,2048]{1,0:T(8,128)(2,1)} %collective-permute-done.24), channel_id=1, source_target_pairs={{0,4},{4,0},{1,5},{5,1},{2,6},{6,2},{3,7},{7,3},{8,12},{12,8},{9,1... | collective-permute-start | bytes 6291464 | tf_op jit(solution)/shard_map/ppermute | solution.py:550
  1064.6 56.7 %collective-permute-start.43 = (bf16[512,2048]{1,0:T(8,128)(2,1)}, bf16[512,2048]{1,0:T(8,128)(2,1)}, u32[]{:S(2)}, u32[]{:S(2)}) collective-permute-start(bf16[512,2048]{1,0:T(8,128)(2,1)} %collective-permute-done.23), channel_id=1, source_target_pairs={{0,4},{4,0},{1,5},{5,1},{2,6},{6,2},{3,7},{7,3},{8,12},{12,8},{9,1... | collective-permute-start | bytes 6291464 | tf_op jit(solution)/shard_map/ppermute | solution.py:550
  1064.7 48.6 %collective-permute-start.41 = (bf16[512,2048]{1,0:T(8,128)(2,1)}, bf16[512,2048]{1,0:T(8,128)(2,1)}, u32[]{:S(2)}, u32[]{:S(2)}) collective-permute-start(bf16[512,2048]{1,0:T(8,128)(2,1)} %get-tuple-element.302), channel_id=1, source_target_pairs={{0,8},{8,0},{16,24},{24,16},{1,9},{9,1},{17,25},{25,17},{2,10},{10... | collective-permute-start | bytes 6291464 | tf_op jit(solution)/shard_map/ppermute | solution.py:550
  1070.0 47.8 %collective-permute-start.46 = (bf16[512,2048]{1,0:T(8,128)(2,1)}, bf16[512,2048]{1,0:T(8,128)(2,1)S(1)}, u32[]{:S(2)}, u32[]{:S(2)}) collective-permute-start(bf16[512,2048]{1,0:T(8,128)(2,1)} %get-tuple-element.302), channel_id=1, source_target_pairs={{0,16},{8,24},{16,0},{24,8},{1,17},{9,25},{17,1},{25,9},{2,18},{10... | collective-permute-start | bytes 6291464 | tf_op jit(solution)/shard_map/ppermute | solution.py:550
  1143.1 34.1 %collective-permute-start.49 = (bf16[512,2048]{1,0:T(8,128)(2,1)S(1)}, bf16[512,2048]{1,0:T(8,128)(2,1)}, u32[]{:S(2)}, u32[]{:S(2)}) collective-permute-start(bf16[512,2048]{1,0:T(8,128)(2,1)S(1)} %collective-permute-done.46), channel_id=1, source_target_pairs={{0,4},{4,0},{1,5},{5,1},{2,6},{6,2},{3,7},{7,3},{8,12},{12,8},{9,1... | collective-permute-start | bytes 6291464 | tf_op jit(solution)/shard_map/ppermute | solution.py:550
  1176.7 42.5 %collective-permute-start.44 = (bf16[512,2048]{1,0:T(8,128)(2,1)}, bf16[512,2048]{1,0:T(8,128)(2,1)}, u32[]{:S(2)}, u32[]{:S(2)}) collective-permute-start(bf16[512,2048]{1,0:T(8,128)(2,1)} %slice.252), channel_id=1, source_target_pairs={{0,4},{4,0},{1,5},{5,1},{2,6},{6,2},{3,7},{7,3},{8,12},{12,8},{9,1... | collective-permute-start | bytes 6291464 | tf_op jit(solution)/shard_map/ppermute | solution.py:550
  1223.9 48.3 %collective-permute-start.45 = (bf16[512,2048]{1,0:T(8,128)(2,1)}, bf16[512,2048]{1,0:T(8,128)(2,1)}, u32[]{:S(2)}, u32[]{:S(2)}) collective-permute-start(bf16[512,2048]{1,0:T(8,128)(2,1)} %add_convert_fusion.5), channel_id=1, source_target_pairs={{0,8},{8,0},{16,24},{24,16},{1,9},{9,1},{17,25},{25,17},{2,10},{10... | collective-permute-start | bytes 6291464 | tf_op jit(solution)/shard_map/ppermute | solution.py:550
  1228.8 47.9 %collective-permute-start.52 = (bf16[512,2048]{1,0:T(8,128)(2,1)}, bf16[512,2048]{1,0:T(8,128)(2,1)}, u32[]{:S(2)}, u32[]{:S(2)}) collective-permute-start(bf16[512,2048]{1,0:T(8,128)(2,1)} %add_convert_fusion.4), channel_id=1, source_target_pairs={{0,16},{8,24},{16,0},{24,8},{1,17},{9,25},{17,1},{25,9},{2,18},{10... | collective-permute-start | bytes 6291464 | tf_op jit(solution)/shard_map/ppermute | solution.py:550
  1234.5 116.1 %collective-permute-start.40 = (bf16[512,2048]{1,0:T(8,128)(2,1)}, bf16[512,2048]{1,0:T(8,128)(2,1)}, u32[]{:S(2)}, u32[]{:S(2)}) collective-permute-start(bf16[512,2048]{1,0:T(8,128)(2,1)} %slice.250), channel_id=1, source_target_pairs={{0,4},{4,0},{1,5},{5,1},{2,6},{6,2},{3,7},{7,3},{8,12},{12,8},{9,1... | collective-permute-start | bytes 6291464 | tf_op jit(solution)/shard_map/ppermute | solution.py:550
  1295.9 54.7 %collective-permute-start.56 = (bf16[512,2048]{1,0:T(8,128)(2,1)}, bf16[512,2048]{1,0:T(8,128)(2,1)S(1)}, u32[]{:S(2)}, u32[]{:S(2)}) collective-permute-start(bf16[512,2048]{1,0:T(8,128)(2,1)} %fusion.86), channel_id=1, source_target_pairs={{0,24},{8,16},{16,8},{24,0},{1,25},{9,17},{17,9},{25,1},{2,26},{10... | collective-permute-start | bytes 6291464 | tf_op jit(solution)/shard_map/ppermute | solution.py:550
  1389.3 65.5 %collective-permute-start.67 = (bf16[2112,512]{1,0:T(8,128)(2,1)}, bf16[2112,512]{1,0:T(8,128)(2,1)}, u32[]{:S(2)}, u32[]{:S(2)}) collective-permute-start(bf16[2112,512]{1,0:T(8,128)(2,1)} %get-tuple-element.307), channel_id=1, source_target_pairs={{0,1},{1,2},{2,3},{3,0},{4,5},{5,6},{6,7},{7,4},{8,9},{9,10},{10,1... | collective-permute-start | bytes 6488072 | tf_op jit(solution)/shard_map/ppermute | solution.py:555
  1420.8 46.9 %collective-permute-start.64 = (bf16[512,2048]{1,0:T(8,128)(2,1)}, bf16[512,2048]{1,0:T(8,128)(2,1)}, u32[]{:S(2)}, u32[]{:S(2)}) collective-permute-start(bf16[512,2048]{1,0:T(8,128)(2,1)} %slice.264), channel_id=1, source_target_pairs={{0,4},{4,0},{1,5},{5,1},{2,6},{6,2},{3,7},{7,3},{8,12},{12,8},{9,1... | collective-permute-start | bytes 6291464 | tf_op jit(solution)/shard_map/ppermute | solution.py:550
  1435.4 36.7 %collective-permute-start.59 = (bf16[512,2048]{1,0:T(8,128)(2,1)}, bf16[512,2048]{1,0:T(8,128)(2,1)}, u32[]{:S(2)}, u32[]{:S(2)}) collective-permute-start(bf16[512,2048]{1,0:T(8,128)(2,1)} %slice.262), channel_id=1, source_target_pairs={{0,4},{4,0},{1,5},{5,1},{2,6},{6,2},{3,7},{7,3},{8,12},{12,8},{9,1... | collective-permute-start | bytes 6291464 | tf_op jit(solution)/shard_map/ppermute | solution.py:550
  1454.8 69.9 %collective-permute-start.66 = (bf16[512,2048]{1,0:T(8,128)(2,1)}, bf16[512,2048]{1,0:T(8,128)(2,1)}, u32[]{:S(2)}, u32[]{:S(2)}) collective-permute-start(bf16[512,2048]{1,0:T(8,128)(2,1)} %slice.266), channel_id=1, source_target_pairs={{0,4},{4,0},{1,5},{5,1},{2,6},{6,2},{3,7},{7,3},{8,12},{12,8},{9,1... | collective-permute-start | bytes 6291464 | tf_op jit(solution)/shard_map/ppermute | solution.py:550
  1464.1 66.2 %collective-permute-start.69 = (bf16[2112,512]{1,0:T(8,128)(2,1)}, bf16[2112,512]{1,0:T(8,128)(2,1)}, u32[]{:S(2)}, u32[]{:S(2)}) collective-permute-start(bf16[2112,512]{1,0:T(8,128)(2,1)} %get-tuple-element.193), channel_id=1, source_target_pairs={{0,3},{1,0},{2,1},{3,2},{4,7},{5,4},{6,5},{7,6},{8,11},{9,8},{10,9... | collective-permute-start | bytes 6488072 | tf_op jit(solution)/shard_map/ppermute | solution.py:555
  1471.4 58.9 %collective-permute-start.65 = (bf16[512,2048]{1,0:T(8,128)(2,1)}, bf16[512,2048]{1,0:T(8,128)(2,1)}, u32[]{:S(2)}, u32[]{:S(2)}) collective-permute-start(bf16[512,2048]{1,0:T(8,128)(2,1)} %add_convert_fusion.2), channel_id=1, source_target_pairs={{0,16},{8,24},{16,0},{24,8},{1,17},{9,25},{17,1},{25,9},{2,18},{10... | collective-permute-start | bytes 6291464 | tf_op jit(solution)/shard_map/ppermute | solution.py:550
  1476.0 54.4 %collective-permute-start.63 = (bf16[512,2048]{1,0:T(8,128)(2,1)}, bf16[512,2048]{1,0:T(8,128)(2,1)}, u32[]{:S(2)}, u32[]{:S(2)}) collective-permute-start(bf16[512,2048]{1,0:T(8,128)(2,1)} %add_convert_fusion.3), channel_id=1, source_target_pairs={{0,8},{8,0},{16,24},{24,16},{1,9},{9,1},{17,25},{25,17},{2,10},{10... | collective-permute-start | bytes 6291464 | tf_op jit(solution)/shard_map/ppermute | solution.py:550
  1530.3 95.3 %collective-permute-start.71 = (bf16[1056,512]{1,0:T(8,128)(2,1)}, bf16[1056,512]{1,0:T(8,128)(2,1)}, u32[]{:S(2)}, u32[]{:S(2)}) collective-permute-start(bf16[1056,512]{1,0:T(8,128)(2,1)} %get-tuple-element.204), channel_id=1, source_target_pairs={{0,2},{1,3},{2,0},{3,1},{4,6},{5,7},{6,4},{7,5},{8,10},{9,11},{10,... | collective-permute-start | bytes 3244040 | tf_op jit(solution)/shard_map/ppermute | solution.py:555
  1538.1 114.6 %collective-permute-start.90 = (bf16[256,1536]{1,0:T(8,128)(2,1)}, bf16[256,1536]{1,0:T(8,128)(2,1)}, u32[]{:S(2)}, u32[]{:S(2)}) collective-permute-start(bf16[256,1536]{1,0:T(8,128)(2,1)} %convolution_convert_fusion.5), channel_id=1, source_target_pairs={{0,16},{8,24},{16,0},{24,8},{1,17},{9,25},{17,1},{25,9},{2,18},{10... | collective-permute-start | bytes 2359304 | tf_op jit(solution)/shard_map/ppermute | solution.py:550
  1540.7 114.9 %collective-permute-start.91 = (bf16[256,1536]{1,0:T(8,128)(2,1)}, bf16[256,1536]{1,0:T(8,128)(2,1)}, u32[]{:S(2)}, u32[]{:S(2)}) collective-permute-start(bf16[256,1536]{1,0:T(8,128)(2,1)} %convolution_convert_fusion.4), channel_id=1, source_target_pairs={{0,8},{8,0},{16,24},{24,16},{1,9},{9,1},{17,25},{25,17},{2,10},{10... | collective-permute-start | bytes 2359304 | tf_op jit(solution)/shard_map/ppermute | solution.py:550
  1542.8 114.8 %collective-permute-start.92 = (bf16[256,1536]{1,0:T(8,128)(2,1)}, bf16[256,1536]{1,0:T(8,128)(2,1)}, u32[]{:S(2)}, u32[]{:S(2)}) collective-permute-start(bf16[256,1536]{1,0:T(8,128)(2,1)} %convolution_convert_fusion.3), channel_id=1, source_target_pairs={{0,8},{8,0},{16,24},{24,16},{1,9},{9,1},{17,25},{25,17},{2,10},{10... | collective-permute-start | bytes 2359304 | tf_op jit(solution)/shard_map/ppermute | solution.py:550
  1586.3 71.3 %collective-permute-start.93 = (bf16[256,1536]{1,0:T(8,128)(2,1)}, bf16[256,1536]{1,0:T(8,128)(2,1)}, u32[]{:S(2)}, u32[]{:S(2)}) collective-permute-start(bf16[256,1536]{1,0:T(8,128)(2,1)} %convolution_convert_fusion.2), channel_id=1, source_target_pairs={{0,16},{8,24},{16,0},{24,8},{1,17},{9,25},{17,1},{25,9},{2,18},{10... | collective-permute-start | bytes 2359304 | tf_op jit(solution)/shard_map/ppermute | solution.py:550
  1640.0 80.8 %collective-permute-start.99 = (bf16[1056,512]{1,0:T(8,128)(2,1)}, bf16[1056,512]{1,0:T(8,128)(2,1)}, u32[]{:S(2)}, u32[]{:S(2)}) collective-permute-start(bf16[1056,512]{1,0:T(8,128)(2,1)} %get-tuple-element.215), channel_id=1, source_target_pairs={{0,2},{1,3},{2,0},{3,1},{4,6},{5,7},{6,4},{7,5},{8,10},{9,11},{10,... | collective-permute-start | bytes 3244040 | tf_op jit(solution)/shard_map/ppermute | solution.py:555
  1655.6 53.4 %collective-permute-start.74 = (bf16[256,1664]{1,0:T(8,128)(2,1)}, bf16[256,1664]{1,0:T(8,128)(2,1)}, u32[]{:S(2)}, u32[]{:S(2)}) collective-permute-start(bf16[256,1664]{1,0:T(8,128)(2,1)} %convolution_convert_fusion.8), channel_id=1, source_target_pairs={{0,8},{8,0},{16,24},{24,16},{1,9},{9,1},{17,25},{25,17},{2,10},{10... | collective-permute-start | bytes 2555912 | tf_op jit(solution)/shard_map/ppermute | solution.py:550
  1659.7 38.5 %collective-permute-start.94 = (bf16[256,1536]{1,0:T(8,128)(2,1)S(1)}, bf16[256,1536]{1,0:T(8,128)(2,1)S(1)}, u32[]{:S(2)}, u32[]{:S(2)}) collective-permute-start(bf16[256,1536]{1,0:T(8,128)(2,1)S(1)} %fusion.28), channel_id=1, source_target_pairs={{0,8},{8,0},{16,24},{24,16},{1,9},{9,1},{17,25},{25,17},{2,10},{10... | collective-permute-start | bytes 2359304 | tf_op jit(solution)/shard_map/ppermute | solution.py:550
  1662.0 38.4 %collective-permute-start.95 = (bf16[256,1536]{1,0:T(8,128)(2,1)S(1)}, bf16[256,1536]{1,0:T(8,128)(2,1)S(1)}, u32[]{:S(2)}, u32[]{:S(2)}) collective-permute-start(bf16[256,1536]{1,0:T(8,128)(2,1)S(1)} %fusion.29), channel_id=1, source_target_pairs={{0,16},{8,24},{16,0},{24,8},{1,17},{9,25},{17,1},{25,9},{2,18},{10... | collective-permute-start | bytes 2359304 | tf_op jit(solution)/shard_map/ppermute | solution.py:550
  1679.7 73.9 %collective-permute-start.85 = (bf16[256,1664]{1,0:T(8,128)(2,1)}, bf16[256,1664]{1,0:T(8,128)(2,1)}, u32[]{:S(2)}, u32[]{:S(2)}) collective-permute-start(bf16[256,1664]{1,0:T(8,128)(2,1)} %convolution_convert_fusion.7), channel_id=1, source_target_pairs={{0,16},{8,24},{16,0},{24,8},{1,17},{9,25},{17,1},{25,9},{2,18},{10... | collective-permute-start | bytes 2555912 | tf_op jit(solution)/shard_map/ppermute | solution.py:550
  1698.2 89.9 %collective-permute-start.78 = (bf16[2,256,2048]{2,1,0:T(8,128)(2,1)}, bf16[2,256,2048]{2,1,0:T(8,128)(2,1)}, u32[]{:S(2)}, u32[]{:S(2)}) collective-permute-start(bf16[2,256,2048]{2,1,0:T(8,128)(2,1)} %constant_dynamic-slice_fusion.8), channel_id=1, source_target_pairs={{0,4},{4,0},{1,5},{5,1},{2,6},{6,2},{3,7},{7,3},{8,12},{12,8},{9,1... | collective-permute-start | bytes 6291464 | tf_op jit(solution)/shard_map/ppermute | solution.py:550
  1700.4 53.2 %collective-permute-start.73 = (bf16[256,1664]{1,0:T(8,128)(2,1)}, bf16[256,1664]{1,0:T(8,128)(2,1)}, u32[]{:S(2)}, u32[]{:S(2)}) collective-permute-start(bf16[256,1664]{1,0:T(8,128)(2,1)} %fusion.30), channel_id=1, source_target_pairs={{0,8},{8,0},{16,24},{24,16},{1,9},{9,1},{17,25},{25,17},{2,10},{10... | collective-permute-start | bytes 2555912 | tf_op jit(solution)/shard_map/ppermute | solution.py:550
  1737.2 133.6 %all-to-all-start.1 = ((bf16[4,2112,128]{2,1,0:T(8,128)(2,1)}), bf16[4,2112,128]{2,1,0:T(8,128)(2,1)}, u32[]{:S(2)}, u32[]{:S(2)}) async-start(bf16[4,2112,128]{2,1,0:T(8,128)(2,1)} %copy.208), calls=%async_computation.2 | async-start | bytes 4325376 | tf_op jit(solution)/shard_map/all_to_all | solution.py:963
  1750.1 35.4 %collective-permute-start.86 = (bf16[256,1664]{1,0:T(8,128)(2,1)}, bf16[256,1664]{1,0:T(8,128)(2,1)S(1)}, u32[]{:S(2)}, u32[]{:S(2)}) collective-permute-start(bf16[256,1664]{1,0:T(8,128)(2,1)} %convolution_convert_fusion.6), channel_id=1, source_target_pairs={{0,8},{8,0},{16,24},{24,16},{1,9},{9,1},{17,25},{25,17},{2,10},{10... | collective-permute-start | bytes 2555912 | tf_op jit(solution)/shard_map/ppermute | solution.py:550
  1750.7 34.9 %collective-permute-start.75 = (bf16[256,1664]{1,0:T(8,128)(2,1)}, bf16[256,1664]{1,0:T(8,128)(2,1)S(1)}, u32[]{:S(2)}, u32[]{:S(2)}) collective-permute-start(bf16[256,1664]{1,0:T(8,128)(2,1)} %fusion.31), channel_id=1, source_target_pairs={{0,16},{8,24},{16,0},{24,8},{1,17},{9,25},{17,1},{25,9},{2,18},{10... | collective-permute-start | bytes 2555912 | tf_op jit(solution)/shard_map/ppermute | solution.py:550
  1753.6 120.1 %collective-permute-start.58 = (bf16[512,2048]{1,0:T(8,128)(2,1)}, bf16[512,2048]{1,0:T(8,128)(2,1)}, u32[]{:S(2)}, u32[]{:S(2)}) collective-permute-start(bf16[512,2048]{1,0:T(8,128)(2,1)} %slice.260), channel_id=1, source_target_pairs={{0,4},{4,0},{1,5},{5,1},{2,6},{6,2},{3,7},{7,3},{8,12},{12,8},{9,1... | collective-permute-start | bytes 6291464 | tf_op jit(solution)/shard_map/ppermute | solution.py:550
  1801.4 38.4 %collective-permute-start.88 = (bf16[128,1664]{0,1:T(8,128)(2,1)S(1)}, bf16[128,1664]{0,1:T(8,128)(2,1)S(1)}, u32[]{:S(2)}, u32[]{:S(2)}) collective-permute-start(bf16[128,1664]{0,1:T(8,128)(2,1)S(1)} %bitcast.345), channel_id=1, source_target_pairs={{0,2},{1,3},{2,0},{3,1},{4,6},{5,7},{6,4},{7,5},{8,10},{9,11},{10,... | collective-permute-start | bytes 1277960 | tf_op jit(solution)/shard_map/ppermute | solution.py:555
  1802.0 37.8 %collective-permute-start.87 = (bf16[128,1664]{0,1:T(8,128)(2,1)}, bf16[128,1664]{0,1:T(8,128)(2,1)S(1)}, u32[]{:S(2)}, u32[]{:S(2)}) collective-permute-start(bf16[128,1664]{0,1:T(8,128)(2,1)} %bitcast.344), channel_id=1, source_target_pairs={{0,1},{1,2},{2,3},{3,0},{4,5},{5,6},{6,7},{7,4},{8,9},{9,10},{10,1... | collective-permute-start | bytes 1277960 | tf_op jit(solution)/shard_map/ppermute | solution.py:555
  1808.3 65.4 %collective-permute-start.76 = (bf16[512,2048]{1,0:T(8,128)(2,1)}, bf16[512,2048]{1,0:T(8,128)(2,1)}, u32[]{:S(2)}, u32[]{:S(2)}) collective-permute-start(bf16[512,2048]{1,0:T(8,128)(2,1)} %convert_add_fusion.3), channel_id=1, source_target_pairs={{0,24},{8,16},{16,8},{24,0},{1,25},{9,17},{17,9},{25,1},{2,26},{10... | collective-permute-start | bytes 6291464 | tf_op jit(solution)/shard_map/ppermute | solution.py:550
  1811.9 45.3 %collective-permute-start.82 = (f32[16640]{0:T(1024)S(1)}, f32[16640]{0:T(1024)S(1)}, u32[]{:S(2)}, u32[]{:S(2)}) collective-permute-start(f32[16640]{0:T(1024)S(1)} %fusion.170), channel_id=1, source_target_pairs={{0,16},{8,24},{16,0},{24,8},{1,17},{9,25},{17,1},{25,9},{2,18},{10... | collective-permute-start | bytes 199688 | tf_op jit(solution)/shard_map/ppermute | solution.py:550
  (139 other events, 3231.8 us)
Sparse Core Ops, SparseCore 0:
  1524.7 167.2 reduce-scatter.1

commit v4 on v3

--- a/solution.py
+++ b/solution.py
@@ -432,74 +432,172 @@
     )(own, carry, start, gain, grad)
 
 
-def ffn_kernel(rows, grads, gate_w, up_w, down_w, hidden, grad_gate, grad_up, grad_rows, result):
-    gate = mul_nt(rows[...], gate_w[...])
-    up = mul_nt(rows[...], up_w[...])
-    grad_hidden = mul_nt(grads[...], down_w[...])
+def ffn_kernel(mine, other, mine_grads, other_grads, gate_w, up_w, down_w, *outs):
+    rows = jnp.concatenate([mine[...], other[...]], axis=0)
+    grads = jnp.concatenate([mine_grads[...], other_grads[...]], axis=0)
+    half = mine.shape[0]
+    gate = mul_nt(rows, gate_w[...])
+    up = mul_nt(rows, up_w[...])
+    grad_hidden = mul_nt(grads, down_w[...])
     sigmoid = jax.nn.sigmoid(gate)
     active = gate * sigmoid
     kept = low(active * up)
     back_gate = low(grad_hidden * up * sigmoid * (1.0 + gate * (1.0 - sigmoid)))
     back_up = low(grad_hidden * active)
-    hidden[...] = kept
-    grad_gate[...] = back_gate
-    grad_up[...] = back_up
-    grad_rows[...] = low(mul_nn(back_gate, gate_w[...]) + mul_nn(back_up, up_w[...]))
-    result[...] = low(mul_nn(kept, down_w[...]))
+    grad_rows = low(mul_nn(back_gate, gate_w[...]) + mul_nn(back_up, up_w[...]))
+    result = low(mul_nn(kept, down_w[...]))
+    for side in range(2):
+        here = slice(side * half, (side + 1) * half)
+        acts, grad_out, result_out = outs[3 * side : 3 * side + 3]
+        for kind, value in enumerate((back_gate, back_up, kept)):
+            acts[kind] = value[here]
+        grad_out[...] = grad_rows[here]
+        result_out[...] = result[here]
 
 
 def ffn_both(rows, grads, weights):
-    count, width = rows.shape
+    count, width = rows[0].shape
     units = weights.shape[0] // 3
     tile = min(256, count)
-    wide = pl.BlockSpec((tile, width), lambda i: (i, 0))
-    narrow = pl.BlockSpec((tile, units), lambda i: (i, 0))
+    wide_rows = pl.BlockSpec((tile, width), lambda i: (i, 0))
+    narrow = pl.BlockSpec((3, tile, units), lambda i: (0, i, 0))
 
     def third(index):
         return pl.BlockSpec((units, width), lambda i: (index, 0))
 
-    return pl.pallas_call(
+    flat = jax.ShapeDtypeStruct((count, width), jnp.bfloat16)
+    outs = pl.pallas_call(
         ffn_kernel,
         grid=(count // tile,),
-        in_specs=[wide, wide, third(0), third(1), third(2)],
-        out_specs=[narrow, narrow, narrow, wide, wide],
-        out_shape=[jax.ShapeDtypeStruct((count, units), jnp.bfloat16)] * 3
-        + [jax.ShapeDtypeStruct((count, width), jnp.bfloat16)] * 2,
+        in_specs=[wide_rows] * 4 + [third(0), third(1), third(2)],
+        out_specs=[narrow, wide_rows, wide_rows] * 2,
+        out_shape=[jax.ShapeDtypeStruct((3, count, units), jnp.bfloat16), flat, flat] * 2,
         compiler_params=pltpu.CompilerParams(vmem_limit_bytes=VMEM_BYTES),
         cost_estimate=pl.CostEstimate(
-            flops=12 * count * width * units, bytes_accessed=8 * count * width + 6 * units * width, transcendentals=0
+            flops=24 * count * width * units, bytes_accessed=16 * count * width + 6 * units * width, transcendentals=0
         ),
-    )(rows, grads, weights, weights, weights)
-
-
-def place_kernel(count, targets, *refs):
-    pieces, out, done = refs[:count], refs[count], refs[count + 1]
-    copies = []
-    for i, piece in enumerate(pieces):
-        target = out.at[pl.ds(targets[i], piece.shape[0])]
-        copies.append(pltpu.make_async_copy(piece, target, done.at[i]))
-    for copy in copies:
-        copy.start()
-    for copy in copies:
-        copy.wait()
-
-
-def place_blocks(pieces, targets, blocks):
-    count = len(pieces)
-    shape = (blocks,) + pieces[0].shape[1:]
-    anywhere = pl.BlockSpec(memory_space=pl.ANY)
+    )(*rows, *grads, weights, weights, weights)
+    return outs[:3], outs[3:]
+
+
+def ffn_weights_kernel(count, lines, *refs):
+    acts, rows, grads = refs[:count], refs[count : 2 * count], refs[2 * count : 3 * count]
+    out, total = refs[-2:]
+    part = out.shape[-1]
+
+    def add(sources):
+        for i in range(count):
+            value = mul_tn(acts[i][0], sources[i][...])
+            if i == 0:
+                total[...] = value
+            else:
+                total[...] += value
+
+    @pl.when(pl.program_id(0) < 2)
+    def _():
+        add(rows)
+
+    @pl.when(pl.program_id(0) == 2)
+    def _():
+        add(grads)
+
+    for line in range(lines):
+        out[line, 0] = low(total[:, line * part : (line + 1) * part])
+
+
+def ffn_weights(acts, rows, grads, lines, squares):
+    count, width = len(acts), rows[0].shape[1]
+    size, units = acts[0].shape[1:]
+    block = width // squares
+    part = block // lines
+    act_spec = pl.BlockSpec((1, size, units), lambda k, c: (k, 0, 0))
+    row_spec = pl.BlockSpec((size, block), lambda k, c: (0, jnp.where(k < 2, c, squares - 1)))
+    grad_spec = pl.BlockSpec((size, block), lambda k, c: (0, jnp.where(k < 2, 0, c)))
     return pl.pallas_call(
-        functools.partial(place_kernel, count),
+        functools.partial(ffn_weights_kernel, count, lines),
+        grid=(3, squares),
+        in_specs=[act_spec] * count + [row_spec] * count + [grad_spec] * count,
+        out_specs=pl.BlockSpec((lines, 1, units, part), lambda k, c: (0, k, 0, c)),
+        out_shape=jax.ShapeDtypeStruct((lines, 3, units, squares * part), jnp.bfloat16),
+        scratch_shapes=[pltpu.VMEM((units, block), jnp.float32)],
+        compiler_params=pltpu.CompilerParams(vmem_limit_bytes=VMEM_BYTES),
+        cost_estimate=pl.CostEstimate(
+            flops=6 * count * size * width * units, bytes_accessed=8 * count * size * width, transcendentals=0
+        ),
+    )(*acts, *rows, *grads)
+
+
+def block_columns(place, bit, size):
+    return pl.multiple_of((place[0] ^ bit) * size, size)
+
+
+def gathered_kernel(place, rows, *refs):
+    out = refs[-1]
+    own, beside, across, upper, lower = refs[:-1]
+    size, half = own.shape[0], upper.shape[0]
+    total = None
+    for bit, skip, ref in ((0, 0, own), (1, 0, beside), (2, 0, across), (3, 0, upper), (3, half, lower)):
+        start = pl.multiple_of(block_columns(place, bit, size) + skip, half)
+        value = mul_nn(rows[:, pl.ds(start, ref.shape[0])], ref[...])
+        total = value if total is None else total + value
+    out[...] = total
+
+
+def gathered_times(rows, place, pieces):
+    count, width = rows.shape
+    columns = pieces[0].shape[1]
+    tile = min(256, count)
+    whole = [pl.BlockSpec(piece.shape, lambda i, place: (0, 0)) for piece in pieces]
+    return pl.pallas_call(
+        gathered_kernel,
         grid_spec=pltpu.PrefetchScalarGridSpec(
             num_scalar_prefetch=1,
-            grid=(1,),
-            in_specs=[anywhere] * count,
-            out_specs=anywhere,
-            scratch_shapes=[pltpu.SemaphoreType.DMA((count,))],
+            grid=(count // tile,),
+            in_specs=[pl.BlockSpec((tile, width), lambda i, place: (i, 0))] + whole,
+            out_specs=pl.BlockSpec((tile, columns), lambda i, place: (i, 0)),
         ),
-        out_shape=jax.ShapeDtypeStruct(shape, pieces[0].dtype),
-        cost_estimate=pl.CostEstimate(flops=0, bytes_accessed=4 * math.prod(shape), transcendentals=0),
-    )(jnp.stack(targets).astype(jnp.int32), *pieces)
+        out_shape=jax.ShapeDtypeStruct((count, columns), jnp.float32),
+        compiler_params=pltpu.CompilerParams(vmem_limit_bytes=VMEM_BYTES),
+        cost_estimate=pl.CostEstimate(
+            flops=2 * count * width * columns, bytes_accessed=2 * (count + columns) * width, transcendentals=0
+        ),
+    )(jnp.reshape(place, (1,)).astype(jnp.int32), rows, *pieces)
+
+
+def gathered_transposed_kernel(count, place, *refs):
+    factors, pieces, out = refs[:count], refs[count:-1], refs[-1]
+    size, half = pieces[0].shape[0], pieces[3].shape[0]
+    for i, (bit, skip) in enumerate(((0, 0), (1, 0), (2, 0), (3, 0), (3, half))):
+        start = pl.multiple_of(block_columns(place, bit, size) + skip, half)
+        total = None
+        for p in range(count):
+            value = mul_nt(factors[p][...], pieces[5 * p + i][...])
+            total = value if total is None else total + value
+        out[:, pl.ds(start, pieces[i].shape[0])] = low(total)
+
+
+def gathered_times_transposed(factors, place, pieces):
+    count, rows = len(factors), factors[0].shape[0]
+    width = 4 * pieces[0][0].shape[0]
+    tile = min(256, rows)
+    flat = [piece for some in pieces for piece in some]
+    whole = [pl.BlockSpec(piece.shape, lambda i, place: (0, 0)) for piece in flat]
+    wides = [pl.BlockSpec((tile, factor.shape[1]), lambda i, place: (i, 0)) for factor in factors]
+    columns = sum(factor.shape[1] for factor in factors)
+    return pl.pallas_call(
+        functools.partial(gathered_transposed_kernel, count),
+        grid_spec=pltpu.PrefetchScalarGridSpec(
+            num_scalar_prefetch=1,
+            grid=(rows // tile,),
+            in_specs=wides + whole,
+            out_specs=pl.BlockSpec((tile, width), lambda i, place: (i, 0)),
+        ),
+        out_shape=jax.ShapeDtypeStruct((rows, width), jnp.bfloat16),
+        compiler_params=pltpu.CompilerParams(vmem_limit_bytes=VMEM_BYTES),
+        cost_estimate=pl.CostEstimate(
+            flops=2 * rows * width * columns, bytes_accessed=2 * (rows + columns) * width, transcendentals=0
+        ),
+    )(jnp.reshape(place, (1,)).astype(jnp.int32), *factors, *flat)
 
 
 def join_kernel(line, source, *refs):
@@ -526,25 +624,6 @@
     )(jnp.reshape(line, (1,)).astype(jnp.int32), piece, *known)
 
 
-def columns_split_kernel(first, second, third, out):
-    for i, ref in enumerate((first, second, third)):
-        out[0, i] = low(ref[...])
-
-
-def columns_split(arrays, lines, squares):
-    rows, columns = arrays[0].shape
-    part = columns // (lines * squares)
-    return pl.pallas_call(
-        columns_split_kernel,
-        grid=(lines, squares),
-        in_specs=[pl.BlockSpec((rows, part), lambda i, j: (0, j * lines + i))] * 3,
-        out_specs=pl.BlockSpec((1, 3, rows, part), lambda i, j: (i, 0, 0, j)),
-        out_shape=jax.ShapeDtypeStruct((lines, 3, rows, squares * part), jnp.bfloat16),
-        compiler_params=pltpu.CompilerParams(vmem_limit_bytes=VMEM_BYTES),
-        cost_estimate=pl.CostEstimate(flops=0, bytes_accessed=18 * arrays[0].size, transcendentals=0),
-    )(*arrays)
-
-
 def flip(value, axis, bit):
     devices = range(lax.axis_size(axis))
     return lax.ppermute(value, axis, [(i, i ^ bit) for i in devices])
@@ -575,8 +654,9 @@
 
 def gather_line(shard):
     count, place = lax.axis_size("fsdp"), lax.axis_index("fsdp")
-    pieces = [shard[None]] + [shift(shard, "fsdp", d)[None] for d in range(1, count)]
-    return place_blocks(pieces, [(place - d) % count for d in range(count)], count)
+    pieces = [shard] + [shift(shard, "fsdp", d) for d in range(1, count)]
+    order = [(place - i) % count for i in range(count)]
+    return jnp.concatenate([lax.select_n(which, *pieces) for which in order], axis=0)
 
 
 class Square:
@@ -598,32 +678,26 @@
     def done(self):
         return (self.upper, self.lower)
 
-    def weights(self):
-        lines, rows, columns = self.own.shape
-        place = lax.axis_index("ctx")
-        starts = [(place ^ bit) * lines for bit in range(4)]
-        full = place_blocks(
-            [self.own, self.beside, self.across, self.upper, self.lower],
-            starts + [starts[3] + self.half],
-            4 * lines,
-        )
-        return full.reshape(4 * lines * rows, columns)
+    def pieces(self):
+        return [self.own, self.beside, self.across, self.upper, self.lower]
 
     def far(self):
         return jnp.concatenate([self.upper, self.lower], axis=0)
 
 
-def all_cores(rows):
-    if lax.axis_size("tp") != 2:
-        return lax.all_gather(rows, "tp", axis=0, tiled=True)
-    return jnp.concatenate([rows, flip(rows, "tp", 1)], axis=0)
-
-
-def core_sum(partial):
-    if lax.axis_size("tp") != 2:
-        return wide(lax.psum_scatter(partial, "tp", scatter_dimension=0, tiled=True))
-    half = partial.shape[0] // 2
-    return wide(partial[:half]) + wide(flip(partial[half:], "tp", 1))
+def both_sides(rows):
+    if lax.axis_size("tp") == 2:
+        return rows, flip(rows, "tp", 1)
+    every = lax.all_gather(rows, "tp", axis=0, tiled=True)
+    half = every.shape[0] // 2
+    return every[:half], every[half:]
+
+
+def core_sum(mine, other):
+    if lax.axis_size("tp") == 2:
+        return wide(mine) + wide(flip(other, "tp", 1))
+    both = jnp.concatenate([mine, other], axis=0)
+    return wide(lax.psum_scatter(both, "tp", scatter_dimension=0, tiled=True))
 
 
 def neighbour_columns(rows):
@@ -721,9 +795,8 @@
     if lax.axis_size("tp") != 2:
         return lax.all_gather(mine, "tp", axis=1, tiled=True)
     other = flip(mine, "tp", 1)
-    pair = jnp.concatenate([mine, other, mine], axis=1)
-    count = mine.shape[1]
-    return lax.dynamic_slice_in_dim(pair, lax.axis_index("tp") * count, 2 * count, 1)
+    lower = lax.axis_index("tp") == 0
+    return jnp.concatenate([jnp.where(lower, mine, other), jnp.where(lower, other, mine)], axis=1)
 
 
 def by_head(parts):
@@ -795,7 +868,8 @@
     ends_apart = sorted({1 % line_count, line_count - 1} - {0})
     ffn_near = {d: shift(tie(ffn_line, lines[parts - 1]), "fsdp", d) for d in ends_apart}
 
-    first_pos = lax.axis_index("ctx") * local_len
+    ctx_place = lax.axis_index("ctx")
+    first_pos = ctx_place * local_len
     starts = doc_start - first_pos
     col, row = starts[:, :, None], starts[:, None, :]
     conv = by_head([conv_weight[0], conv_weight[1], conv_weight[2]])
@@ -810,18 +884,18 @@
     square = Square(tie(lines[0], ffn_line)).forward()
     mix_full, kept, pre = [], [], []
     for p in range(parts):
-        mix_full.append(square.weights())
+        mix_full.append(square.pieces())
         square = Square(tie(lines[p + 1], *square.done()))
         if p == 0:
-            pre.append(times(normed_mix, mix_full[p]))
+            pre.append(gathered_times(normed_mix, ctx_place, mix_full[p]))
         else:
-            pre.append(times(tie(normed_mix, lines[-1]), mix_full[p]))
+            pre.append(gathered_times(tie(normed_mix, lines[-1]), ctx_place, mix_full[p]))
         ends = pre[p].reshape(seq_count, local_len, -1)[:, local_len - HALO :, :part_cols]
         halo = from_behind(ends, "ctx", 1)
         convs = conv[:, p * part_cols : (p + 1) * part_cols]
         held = pre[p]
         if p > 0:
-            held = tie(held, grad_square.beside, grad_square.across)
+            held, ffn_full = lax.optimization_barrier((held, ffn_full, grad_square.beside, grad_square.across))[:2]
         kept.append(
             [halo, convs]
             + list(
@@ -843,7 +917,7 @@
             grad_square = Square(tie(grads_mine, kept[p][2]))
         if p == parts - 1:
             grad_square.forward()
-    out_full = square.weights()
+    out_full = square.pieces()
 
     entered, transfers, mixed_rows = [], [], []
     for _, _, own, carry, final, _, _, _ in kept:
@@ -860,7 +934,7 @@
         mixed_rows.append(mixer_output(own, carry, entered[-1], gain_head, group))
     mixed_rows = jnp.concatenate(mixed_rows, axis=1)
 
-    branch = low(times_transposed(mixed_rows, out_full)).reshape(seq_count, local_len, width)
+    branch = gathered_times_transposed([mixed_rows], ctx_place, [out_full]).reshape(seq_count, local_len, width)
     residual = inputs_mine + rows_scatter(branch).reshape(-1, width)
     scale_ffn = rms_scale(residual, EPSILON)
     square = Square(low(residual * scale_ffn * gain_ffn))
@@ -868,29 +942,43 @@
         piece = jnp.concatenate(pieces, axis=0)
         ffn_full = columns_join(ffn_full, piece, (line_place - d) % line_count, line_count, 4)
 
-    ffn_rows = [all_cores(square.own)]
-    grad_rows = [all_cores(part) for part in (grad_square.own, grad_square.beside, grad_square.across, grad_square.far())]
+    ffn_rows = [both_sides(square.own)]
+    grad_rows = [
+        both_sides(part) for part in (grad_square.own, grad_square.beside, grad_square.across, grad_square.far())
+    ]
     ffn_out = [ffn_both(ffn_rows[0], grad_rows[0], ffn_full)]
-    square.forward(ffn_out[0][0])
-    ffn_rows.append(all_cores(tie(square.beside, ffn_out[0][0])))
+    square.forward(ffn_out[0][0][0])
+    ffn_rows.append(both_sides(tie(square.beside, ffn_out[0][0][0])))
     ffn_out.append(ffn_both(ffn_rows[1], grad_rows[1], ffn_full))
-    ffn_rows.append(all_cores(tie(square.across, ffn_out[0][0], *square.done())))
-    ffn_out.append(ffn_both(tie(ffn_rows[2], ffn_out[1][0]), grad_rows[2], ffn_full))
-    beside_sums, across_sums = low(core_sum(ffn_out[1][3])), low(core_sum(ffn_out[2][3]))
-    ffn_rows.append(tie(all_cores(square.far()), beside_sums, across_sums))
-    ffn_out.append(ffn_both(ffn_rows[3], grad_rows[3], ffn_full))
+    ffn_rows.append(both_sides(tie(square.across, ffn_out[0][0][0], *square.done())))
+    mine, other = ffn_rows[2]
+    ffn_out.append(ffn_both((tie(mine, ffn_out[1][0][0]), other), grad_rows[2], ffn_full))
+    beside_sums, across_sums = (low(core_sum(*(side[1] for side in ffn_out[bit]))) for bit in (1, 2))
+    ffn_rows.append(both_sides(square.far()))
+    mine, other = ffn_rows[3]
+    ffn_out.append(ffn_both((tie(mine, beside_sums, across_sums), other), grad_rows[3], ffn_full))
     near_sums = (flip(beside_sums, "ctx", 1), flip(across_sums, "ctx", 2))
-    far_sums = core_sum(tie(ffn_out[3][3], *near_sums))
-    ffn_rows[0] = tie(ffn_rows[0], ffn_out[2][3])
-    for i in (1, 2, 3):
-        ffn_rows[i], grad_rows[i] = tie(ffn_rows[i], far_sums), tie(grad_rows[i], far_sums)
-    far_sums = flip(low(far_sums), "ctx", 3)
-    grad_normed = core_sum(ffn_out[0][3]) + wide(near_sums[0]) + wide(near_sums[1]) + wide(far_sums)
+    mine, other = (side[1] for side in ffn_out[3])
+    far_sums = low(core_sum(mine, tie(other, *near_sums)))
+    acts = [side[0] for outs in ffn_out for side in outs]
+    acts[0] = tie(acts[0], far_sums)
+    far_sums = flip(far_sums, "ctx", 3)
+    sums = ffn_weights(
+        acts,
+        [side for sides in ffn_rows for side in sides],
+        [side for sides in grad_rows for side in sides],
+        line_count,
+        4,
+    ).reshape(line_count, 3 * units, 4 * shard_rows)
+
+    far_sums, sums = lax.optimization_barrier((far_sums, sums))
+    grad_normed = core_sum(*(side[1] for side in ffn_out[0]))
+    grad_normed = grad_normed + wide(near_sums[0]) + wide(near_sums[1]) + wide(far_sums)
     back_ffn, unit_ffn = norm_backward(grad_normed, residual, scale_ffn, gain_ffn)
     grad_residual = wide(grads_mine) + back_ffn
     gain_ffn_part = jnp.sum(grad_normed * unit_ffn, axis=0)
     grad_branch = rows_full(low(grad_residual).reshape(seq_count, -1, width)).reshape(row_count, width)
-    grad_heads = times(grad_branch, out_full)
+    grad_heads = gathered_times(grad_branch, ctx_place, out_full)
     backs, acrosses, gain_o_part = [], [], 0.0
     for p in range(parts):
         _, _, own, carry, _, _, _, _ = kept[p]
@@ -901,19 +989,12 @@
         acrosses.append(across)
         gain_o_part = gain_o_part + jnp.sum(gain_part, axis=(0, 1, 2))
     grad_end = pass_states(jnp.concatenate(acrosses, axis=1), jnp.concatenate(transfers, axis=1), -1)
-    result_near = [
-        flip(tie(low(core_sum(tie(ffn_out[bit][4], grad_branch))), grad_end), "ctx", bit) for bit in (1, 2)
-    ]
-    result_far = core_sum(tie(ffn_out[3][4], grad_branch))
-    result_own = core_sum(tie(ffn_out[0][4], grad_branch))
-
-    sums = []
-    for kind, sources in ((1, ffn_rows), (2, ffn_rows), (0, grad_rows)):
-        total = 0.0
-        for out, source in zip(ffn_out, sources):
-            total = total + outer_rows(out[kind], source)
-        sums.append(total)
-    sums = columns_split(sums, line_count, 4).reshape(line_count, 3 * units, 4 * shard_rows)
+    results = []
+    for outs in ffn_out:
+        mine, other = (side[2] for side in outs)
+        results.append(core_sum(mine, tie(other, grad_branch)))
+    result_near = [flip(tie(low(results[bit]), grad_end), "ctx", bit) for bit in (1, 2)]
+    result_own, result_far = results[0], results[3]
 
     def line_piece(distance):
         return lax.dynamic_index_in_dim(sums, (line_place + distance) % line_count, 0, keepdims=False)
@@ -933,7 +1014,7 @@
     out_grad_w = wide(lax.psum_scatter(out_grad_w, ("ctx", "fsdp"), scatter_dimension=0, tiled=True)).T
 
     columns = neighbour_columns(normed_mix)
-    mix_back, mix_grads, conv_parts = 0.0, [None] * parts, [None] * parts
+    grad_mixes, mix_grads, conv_parts = [None] * parts, [None] * parts, [None] * parts
     logits = 0.0
     scatter = None
     for p in reversed(range(parts)):
@@ -954,7 +1035,7 @@
             grad_mix = tie(grad_mix, *result_near, *line_got[1:2])
         if p == 0:
             grad_mix = tie(jnp.concatenate([grad_mix, low(logits)], axis=1), *line_got[2:3])
-        mix_back = mix_back + times_transposed(grad_mix, mix_full[p])
+        grad_mixes[p] = grad_mix
         scatter = Scatter(columns, grad_mix)
     mix_grads[0] = scatter.finish()
     for (_, low_row, high_row), part in zip(line_sends, line_got):
@@ -969,7 +1050,8 @@
     query_grad, key_grad, value_grad = by_kind(joined)
     beta_grad = mix_grads[0][:, part_cols : part_cols + heads_here]
 
-    mix_back = rows_scatter(low(mix_back).reshape(seq_count, local_len, width)).reshape(-1, width)
+    mix_back = gathered_times_transposed(grad_mixes, ctx_place, mix_full)
+    mix_back = rows_scatter(mix_back.reshape(seq_count, local_len, width)).reshape(-1, width)
     back_mix, unit_mix = norm_backward(mix_back, inputs_mine, rms_scale(inputs_mine, EPSILON), gain_mix)
     input_grad = rows_full(low(grad_residual + back_mix).reshape(seq_count, -1, width))
     gain_mix_part = jnp.sum(mix_back * unit_mix, axis=0)

time: 1930 us -> 1240 us (0.64)
  Pallas kernels: 949 us -> 389 us
  matrix products: 178 us -> 48.1 us
  local copies, waits for them, and re-layouts: 150 us -> 102 us
  starting transfers between devices: 132 us -> 163 us
  waiting for transfers between devices: 362 us -> 392 us
    pallas_call x11 -> x10, Pallas kernels: 791 us -> 231 us  [the longest x4 119 us: ffn_both(): pl.pallas_call(ffn_kernel, grid=(count // tile,), in_specs=[wide_rows] *...]
    dot_general x29 -> x17, matrix products: 121 us -> 45.8 us  [outer_rows(): lax.dot_general(left, right, (((0,), (0,)), ((), ())), preferred_element_...]
    dot_general x6 -> x0, matrix products: 54.3 us -> none  [the longest x3 27.6 us: times(): return jnp.dot(left, right, preferred_element_type=jnp.float32)]
    ppermute x23, starting transfers between devices: 35 us -> 64.2 us  [shift(): lax.ppermute(value, axis, [(i, (i + distance) % count) for i in range(cou...]
    ppermute x64, waiting for transfers between devices: 155 us -> 183 us  [flip(): return lax.ppermute(value, axis, [(i, i ^ bit) for i in devices])]
    ppermute x23, waiting for transfers between devices: 166 us -> 140 us  [shift(): lax.ppermute(value, axis, [(i, (i + distance) % count) for i in range(cou...]
    ppermute x13, waiting for transfers between devices: 41 us -> 67.4 us  [from_behind(): return lax.ppermute(block, axis, route)]
    unnamed x227 -> x134, local copies, waits for them, and re-layouts: 48.5 us -> 28.6 us
  transfers between devices with their start and end apart: 103 -> 103, of which waited for: 33 -> 39; matrix products, arithmetic and copies ran while one was open for 21% -> 19% of each run, Pallas kernels for 49% -> 31%
where the time goes in v4:
time: 1240 us; the launch traced here: 1230 us
  waiting for transfers between devices  392 us (32%)
  Pallas kernels  389 us (31%)
  starting transfers between devices  163 us (13%)
  other arithmetic  117 us (9%)
  local copies, waits for them, and re-layouts  102 us (8%)
  matrix products  48.1 us (4%)
  between operations  15.7 us (1%)
    ppermute x64, waiting for transfers between devices, flip(): return lax.ppermute(value, axis, [(i, i ^ bit) for i in devices])  183 us
    ppermute x23, waiting for transfers between devices, shift(): lax.ppermute(value, axis, [(i, (i + distance) % count) for i in range(cou...  140 us
    pallas_call x4, Pallas kernels, ffn_both(): pl.pallas_call(ffn_kernel, grid=(count // tile,), in_specs=[wide_rows] *...  119 us
    ppermute x13, waiting for transfers between devices, from_behind(): return lax.ppermute(block, axis, route)  67.4 us
    pallas_call x2, Pallas kernels, mixer_backward(): pl.pallas_call(functools.partial(backward_kernel, taps, group, first), gr...  66.6 us
    ppermute x23, starting transfers between devices, shift(): lax.ppermute(value, axis, [(i, (i + distance) % count) for i in range(cou...  64.2 us
    ppermute x64, starting transfers between devices, flip(): return lax.ppermute(value, axis, [(i, i ^ bit) for i in devices])  57.5 us
    pallas_call x2, Pallas kernels, mixer_forward(): pl.pallas_call(functools.partial(forward_kernel, taps, group, first), gri...  55 us
  transfers between devices with their start and end apart: 103, of which 39 were waited for; matrix products, arithmetic and copies ran while one was open for 19% of the time, Pallas kernels for 31%

profile of v4, /device:TPU:0, one launch (start us, length us, event | category | flops | bytes accessed | tf_op | source)
XLA Modules:
  0.0 1226.9 jit_solution(15058303717717924804)
XLA Ops:
  32.0 6.7 collective-permute-done.1
  38.7 8.7 collective-permute-done
  57.5 5.2 fusion.1.rows
  65.8 6.2 collective-permute-start.12
  77.3 16.4 %collective-permute-done.4.refs_2_.refs_4_ = bf16[512,1664]{1,0:T(8,128)(2,1)} collective-permute-done((bf16[512,1664]{1,0:T(8,128)(2,1)}, bf16[512,1664]{1,0:T(8,128)(2,1)}, u32[]{:S(2)}, u32[]{:S(2)}) %collective-permute-start.4) | collective-permute-done | bytes 1703968 | tf_op jit(solution)/shard_map/ppermute | solution.py:629
  101.8 4.4 collective-permute-done.12
  108.7 6.3 collective-permute-done.6.refs_4_.refs_6_
  121.4 6.6 collective-permute-start.20
  128.6 12.8 %shard_map.271.pre.beta = f32[1024,1664]{1,0:T(8,128)} custom-call(s32[1]{0:T(128)} %bitcast.1.place, bf16[1024,2048]{1,0:T(8,128)(2,1)} %fusion.1.rows, bf16[512,1664]{1,0:T(8,128)(2,1)} %pad_maximum_fusion.8.refs_0_.refs_2_, bf16[512,1664]{1,0:T(8,128)(2,1)} %collective-permute-done.3.refs_1_.refs_3_, ...), custom_call_target="tpu_custom_call" | custom-call | flops 6979321856 | bytes 11010048 | tf_op jit(solution)/shard_map/pallas_call | solution.py:551
  146.3 15.8 %collective-permute-done.7.halo = f32[2,8,1536]{2,1,0:T(8,128)S(1)} collective-permute-done((f32[2,8,1536]{2,1,0:T(8,128)S(1)}, f32[2,8,1536]{2,1,0:T(8,128)S(1)}, u32[]{:S(2)}, u32[]{:S(2)}) %collective-permute-start.7) | collective-permute-done | bytes 98336 | tf_op jit(solution)/shard_map/ppermute | solution.py:640
  162.1 4.9 collective-permute-start.16
  167.0 27.5 %shard_map.272 = (f32[1024,512]{1,0:T(8,128)}, bf16[1024,512]{1,0:T(8,128)(2,1)}, f32[2,4,128,256]{3,2,1,0:T(8,128)}, bf16[2,4,4,128,128]{4,3,2,1,0:T(8,128)(2,1...) custom-call(f32[1024,1664]{1,0:T(8,128)} %shard_map.271.pre.beta, ...), custom_call_target="tpu_custom_call" | custom-call | flops 4026531840 | bytes 20971520 | tf_op jit(solution)/shard_map/pallas_call | solution.py:160
  194.5 28.7 %collective-permute-done.16 = bf16[128,1024]{1,0:T(8,128)(2,1)S(1)} collective-permute-done((bf16[128,1024]{1,0:T(8,128)(2,1)S(1)}, bf16[128,1024]{1,0:T(8,128)(2,1)S(1)}, u32[]{:S(2)}, u32[]{:S(2)}) %collective-permute-start.16) | collective-permute-done | bytes 262176 | tf_op jit(solution)/shard_map/ppermute | solution.py:634
  224.3 7.7 collective-permute-start.15
  239.3 4.7 collective-permute-start.19
  247.2 9.8 collective-permute-done.14
  257.0 7.2 collective-permute-start.26
  289.5 11.5 shard_map.274.pre
  314.5 27.5 %shard_map.278 = (f32[1024,512]{1,0:T(8,128)}, bf16[1024,512]{1,0:T(8,128)(2,1)}, f32[2,4,128,256]{3,2,1,0:T(8,128)}, bf16[2,4,4,128,128]{4,3,2,1,0:T(8,128)(2,1...) custom-call(f32[1024,1536]{1,0:T(8,128)} %shard_map.274.pre, ...), custom_call_target="tpu_custom_call" | custom-call | flops 4026531840 | bytes 20971520 | tf_op jit(solution)/shard_map/pallas_call | solution.py:160
  347.0 7.6 collective-permute-start.27
  354.8 4.8 collective-permute-start.9
  366.6 4.4 collective-permute-start.10
  379.9 4.5 shard_map.273
  384.4 5.4 collective-permute-done.27
  390.6 4.5 shard_map.279
  398.1 8.8 shard_map.280
  409.4 5.8 collective-permute-done.37
  431.3 29.5 %shard_map.282 = (bf16[3,512,704]{2,1,0:T(8,128)(2,1)}, bf16[512,2048]{1,0:T(8,128)(2,1)}, bf16[512,2048]{1,0:T(8,128)(2,1)}, bf16[3,512,704]{2,1,0:T(8,128)(2,1...) custom-call(bf16[512,2048]{1,0:T(8,128)(2,1)} %get-tuple-element.304.mine.refs_8_, ...), custom_call_target="tpu_custom_call" | custom-call | flops 17716740096 | bytes 25427968 | tf_op jit(solution)/shard_map/pallas_call | solution.py:469
  460.8 10.3 collective-permute-done.41.mine.refs_10_
  472.4 7.2 collective-permute-done.46.mine.refs_12_
  482.6 23.1 %collective-permute-done.47 = bf16[256,2048]{1,0:T(8,128)(2,1)S(1)} collective-permute-done((bf16[256,2048]{1,0:T(8,128)(2,1)S(1)}, bf16[256,2048]{1,0:T(8,128)(2,1)S(1)}, u32[]{:S(2)}, u32[]{:S(2)}) %collective-permute-start.47) | collective-permute-done | bytes 1048608 | tf_op jit(solution)/shard_map/ppermute | solution.py:629
  507.3 29.7 %shard_map.283 = (bf16[3,512,704]{2,1,0:T(8,128)(2,1)}, bf16[512,2048]{1,0:T(8,128)(2,1)}, bf16[512,2048]{1,0:T(8,128)(2,1)}, bf16[3,512,704]{2,1,0:T(8,128)(2,1...) custom-call(bf16[512,2048]{1,0:T(8,128)(2,1)} %collective-permute-done.41.mine.refs_10_, ...), custom_call_target="tpu_custom_call" | custom-call | flops 17716740096 | bytes 25427968 | tf_op jit(solution)/shard_map/pallas_call | solution.py:469
  537.5 29.8 %shard_map.284 = (bf16[3,512,704]{2,1,0:T(8,128)(2,1)}, bf16[512,2048]{1,0:T(8,128)(2,1)}, bf16[512,2048]{1,0:T(8,128)(2,1)}, bf16[3,512,704]{2,1,0:T(8,128)(2,1...) custom-call(bf16[512,2048]{1,0:T(8,128)(2,1)} %collective-permute-done.46.mine.refs_12_, ...), custom_call_target="tpu_custom_call" | custom-call | flops 17716740096 | bytes 25427968 | tf_op jit(solution)/shard_map/pallas_call | solution.py:469
  580.4 29.5 %shard_map.285 = (bf16[3,512,704]{2,1,0:T(8,128)(2,1)}, bf16[512,2048]{1,0:T(8,128)(2,1)}, bf16[512,2048]{1,0:T(8,128)(2,1)}, bf16[3,512,704]{2,1,0:T(8,128)(2,1...) custom-call(bf16[512,2048]{1,0:T(8,128)(2,1)} %copy-done.37, ...), custom_call_target="tpu_custom_call" | custom-call | flops 17716740096 | bytes 25427968 | tf_op jit(solution)/shard_map/pallas_call | solution.py:469
  609.9 12.8 %collective-permute-done.45 = bf16[512,2048]{1,0:T(8,128)(2,1)S(1)} collective-permute-done((bf16[512,2048]{1,0:T(8,128)(2,1)}, bf16[512,2048]{1,0:T(8,128)(2,1)S(1)}, u32[]{:S(2)}, u32[]{:S(2)}) %collective-permute-start.45) | collective-permute-done | bytes 2097184 | tf_op jit(solution)/shard_map/ppermute | solution.py:629
  626.3 6.8 collective-permute-done.55
  638.7 48.4 %shard_map.286 = bf16[4,3,704,512]{3,2,1,0:T(8,128)(2,1)} custom-call(bf16[3,512,704]{2,1,0:T(8,128)(2,1)} %get-tuple-element.163.refs_0_, bf16[3,512,704]{2,1,0:T(8,128)(2,1)} %get-tuple-element.164.refs_1_, bf16[3,512,704]{2,1,0:T(8,128)(2,1)} %get-tuple-element.155.refs_2_, bf16[3,512,704]{2,1,0:T(8,128)(2,1)} %get-tuple-element.165.refs_3_, ...), custom_call_target="tpu_custom_call" | custom-call | flops 35433480192 | bytes 67108864 | tf_op jit(solution)/shard_map/pallas_call | solution.py:516
  687.2 6.2 multiply_reduce_fusion.1
  695.5 4.5 dynamic-slice_bitcast_fusion
  704.5 8.9 shard_map.287.grad
  713.4 5.7 shard_map.289
  719.2 5.8 shard_map.288
  729.2 13.3 %collective-permute-done.60 = bf16[2,8,128,128]{3,2,1,0:T(8,128)(2,1)S(1)} collective-permute-done((bf16[2,8,128,128]{3,2,1,0:T(8,128)(2,1)S(1)}, bf16[2,8,128,128]{3,2,1,0:T(8,128)(2,1)S(1)}, u32[]{:S(2)}, u32[]{:S(2)}) %collective-permute-start.60) | collective-permute-done | bytes 524320 | tf_op jit(solution)/shard_map/ppermute | solution.py:640
  744.3 14.4 %collective-permute-done.61 = bf16[2,8,128,128]{3,2,1,0:T(8,128)(2,1)S(1)} collective-permute-done((bf16[2,8,128,128]{3,2,1,0:T(8,128)(2,1)S(1)}, bf16[2,8,128,128]{3,2,1,0:T(8,128)(2,1)S(1)}, u32[]{:S(2)}, u32[]{:S(2)}) %collective-permute-start.61) | collective-permute-done | bytes 524320 | tf_op jit(solution)/shard_map/ppermute | solution.py:640
  763.8 10.9 collective-permute-done.62
  788.6 33.2 %shard_map.290 = (bf16[1024,1536]{1,0:T(8,128)(2,1)}, f32[2,8,1536]{2,1,0:T(8,128)}, f32[2,8,1536]{2,1,0:T(8,128)}, f32[2,8,1536]{2,1,0:T(8,128)}, f32[1024,128]{1,0:T(8,128)}) custom-call(f32[1024,1536]{1,0:T(8,128)} %shard_map.274.pre, f32[1024,1664]{1,0:T(8,128)} %shard_map.271.pre.beta, f32[1,128]{1,0:T(1,128)} %pad_bitcast_fusion.bias, ...), custom_call_target="tpu_custom_call" | custom-call | flops 4026531840 | bytes 20971520 | tf_op jit(solution)/shard_map/pallas_call | solution.py:318
  823.4 8.5 convolution_convert_fusion
  834.8 5.6 convert_add_fusion.3
  853.6 33.4 %shard_map.291 = (bf16[1024,1536]{1,0:T(8,128)(2,1)}, f32[2,8,1536]{2,1,0:T(8,128)}, f32[2,8,1536]{2,1,0:T(8,128)}, f32[2,8,1536]{2,1,0:T(8,128)}, f32[1024,128]{1,0:T(8,128)}) custom-call(f32[1024,1664]{1,0:T(8,128)} %shard_map.271.pre.beta, f32[1024,1664]{1,0:T(8,128)} %shard_map.271.pre.beta, f32[1,128]{1,0:T(1,128)} %pad_bitcast_fusion.bias, ...), custom_call_target="tpu_custom_call" | custom-call | flops 4026531840 | bytes 20971520 | tf_op jit(solution)/shard_map/pallas_call | solution.py:318
  890.4 6.6 collective-permute-done.70
  900.7 36.1 %collective-permute-done.71 = bf16[1056,512]{1,0:T(8,128)(2,1)} collective-permute-done((bf16[1056,512]{1,0:T(8,128)(2,1)}, bf16[1056,512]{1,0:T(8,128)(2,1)}, u32[]{:S(2)}, u32[]{:S(2)}) %collective-permute-start.71) | collective-permute-done | bytes 1081376 | tf_op jit(solution)/shard_map/ppermute | solution.py:634
  943.0 22.0 %shard_map.292 = bf16[1024,2048]{1,0:T(8,128)(2,1)} custom-call(s32[1]{0:T(128)} %bitcast.1.place, bf16[1024,1664]{1,0:T(8,128)(2,1)} %copy-done.5, bf16[1024,1536]{1,0:T(8,128)(2,1)} %bitcast.232, bf16[512,1664]{1,0:T(8,128)(2,1)} %pad_maximum_fusion.8.refs_0_.refs_2_, bf16[512,1664]{1,0:T(8,128)(2,1)} %collective-permute-done.3.refs_1_.refs_3_, ...), custom_call_target="tpu_custom_call" | custom-call | flops 13421772800 | bytes 17301504 | tf_op jit(solution)/shard_map/pallas_call | solution.py:587
  982.3 12.9 %collective-permute-done.72 = bf16[256,1664]{1,0:T(8,128)(2,1)S(1)} collective-permute-done((bf16[256,1664]{1,0:T(8,128)(2,1)S(1)}, bf16[256,1664]{1,0:T(8,128)(2,1)S(1)}, u32[]{:S(2)}, u32[]{:S(2)}) %collective-permute-start.72) | collective-permute-done | bytes 852000 | tf_op jit(solution)/shard_map/ppermute | solution.py:629
  1000.2 15.6 %collective-permute-done.94 = bf16[256,1536]{1,0:T(8,128)(2,1)S(1)} collective-permute-done((bf16[256,1536]{1,0:T(8,128)(2,1)S(1)}, bf16[256,1536]{1,0:T(8,128)(2,1)S(1)}, u32[]{:S(2)}, u32[]{:S(2)}) %collective-permute-start.94) | collective-permute-done | bytes 786464 | tf_op jit(solution)/shard_map/ppermute | solution.py:629
  1040.8 6.2 fusion.5
  1046.9 4.1 copy.207
  1051.1 4.1 copy.208
  1055.2 4.5 all-to-all-start.1
  1059.7 8.2 collective-permute-done.97
  1073.8 29.8 %collective-permute-done.86 = bf16[256,1664]{1,0:T(8,128)(2,1)S(1)} collective-permute-done((bf16[256,1664]{1,0:T(8,128)(2,1)}, bf16[256,1664]{1,0:T(8,128)(2,1)S(1)}, u32[]{:S(2)}, u32[]{:S(2)}) %collective-permute-start.86) | collective-permute-done | bytes 852000 | tf_op jit(solution)/shard_map/ppermute | solution.py:629
  1109.2 5.2 fusion.13
  1131.3 26.3 %collective-permute-done.88 = bf16[128,1664]{0,1:T(8,128)(2,1)S(1)} collective-permute-done((bf16[128,1664]{0,1:T(8,128)(2,1)}, bf16[128,1664]{0,1:T(8,128)(2,1)S(1)}, u32[]{:S(2)}, u32[]{:S(2)}) %collective-permute-start.88) | collective-permute-done | bytes 426016 | tf_op jit(solution)/shard_map/ppermute | solution.py:634
  1157.9 17.2 %collective-permute-done.82 = f32[16640]{0:T(1024)S(1)} collective-permute-done((f32[16640]{0:T(1024)S(1)}, f32[16640]{0:T(1024)S(1)}, u32[]{:S(2)}, u32[]{:S(2)}) %collective-permute-start.82) | collective-permute-done | bytes 66592 | tf_op jit(solution)/shard_map/ppermute | solution.py:629
  1191.0 11.5 fusion.9
  (466 shorter events, 358.9 us)
Async XLA Ops:
  19.1 28.3 %collective-permute-start = (bf16[128,1664]{1,0:T(8,128)(2,1)}, bf16[128,1664]{1,0:T(8,128)(2,1)}, u32[]{:S(2)}, u32[]{:S(2)}) collective-permute-start(bf16[128,1664]{1,0:T(8,128)(2,1)} %fusion.53), channel_id=1, source_target_pairs={{0,1},{1,2},{2,3},{3,0},{4,5},{5,6},{6,7},{7,4},{8,9},{9,10},{10,1... | collective-permute-start | bytes 1277960 | tf_op jit(solution)/shard_map/ppermute | solution.py:634
  25.1 28.6 %all-to-all-start = ((bf16[4,2112,128]{2,1,0:T(8,128)(2,1)}), bf16[4,2112,128]{2,1,0:T(8,128)(2,1)S(1)}, u32[]{:S(2)}, u32[]{:S(2)}) async-start(bf16[4,2112,128]{2,1,0:T(8,128)(2,1)} %bitcast.243), calls=%async_computation | async-start | bytes 4325376 | tf_op jit(solution)/shard_map/all_to_all | solution.py:864
  28.8 1178.9 %reduce-scatter.2.cloned.1.call-start = ((), (), s32[]{:S(2)}) async-start(), calls=%async_computation.3 | async-start | bytes 4456448 | tf_op jit(solution)/shard_map/reduce_scatter | solution.py:1014
  55.2 38.4 %collective-permute-start.4 = (bf16[512,1664]{1,0:T(8,128)(2,1)}, bf16[512,1664]{1,0:T(8,128)(2,1)}, u32[]{:S(2)}, u32[]{:S(2)}) collective-permute-start(bf16[512,1664]{1,0:T(8,128)(2,1)} %pad_maximum_fusion.8.refs_0_.refs_2_), channel_id=1, source_target_pairs={{0,16},{8,24},{16,0},{24,8},{1,17},{9,25},{17,1},{25,9},{2,18},{10... | collective-permute-start | bytes 5111816 | tf_op jit(solution)/shard_map/ppermute | solution.py:629
  56.7 39.4 %collective-permute-start.3 = (bf16[512,1664]{1,0:T(8,128)(2,1)}, bf16[512,1664]{1,0:T(8,128)(2,1)}, u32[]{:S(2)}, u32[]{:S(2)}) collective-permute-start(bf16[512,1664]{1,0:T(8,128)(2,1)} %pad_maximum_fusion.8.refs_0_.refs_2_), channel_id=1, source_target_pairs={{0,8},{8,0},{16,24},{24,16},{1,9},{9,1},{17,25},{25,17},{2,10},{10... | collective-permute-start | bytes 5111816 | tf_op jit(solution)/shard_map/ppermute | solution.py:629
  62.7 39.1 %collective-permute-start.13 = (bf16[128,1536]{1,0:T(8,128)(2,1)S(1)}, bf16[128,1536]{1,0:T(8,128)(2,1)S(1)}, u32[]{:S(2)}, u32[]{:S(2)}) collective-permute-start(bf16[128,1536]{1,0:T(8,128)(2,1)S(1)} %copy.218), channel_id=1, source_target_pairs={{0,3},{1,0},{2,1},{3,2},{4,7},{5,4},{6,5},{7,6},{8,11},{9,8},{10,9... | collective-permute-start | bytes 1179656 | tf_op jit(solution)/shard_map/ppermute | solution.py:634
  65.8 40.4 %collective-permute-start.12 = (bf16[128,1536]{1,0:T(8,128)(2,1)S(1)}, bf16[128,1536]{1,0:T(8,128)(2,1)}, u32[]{:S(2)}, u32[]{:S(2)}) collective-permute-start(bf16[128,1536]{1,0:T(8,128)(2,1)S(1)} %copy.218), channel_id=1, source_target_pairs={{0,2},{1,3},{2,0},{3,1},{4,6},{5,7},{6,4},{7,5},{8,10},{9,11},{10,... | collective-permute-start | bytes 1179656 | tf_op jit(solution)/shard_map/ppermute | solution.py:634
  72.1 34.1 %collective-permute-start.11 = (bf16[128,1536]{1,0:T(8,128)(2,1)S(1)}, bf16[128,1536]{1,0:T(8,128)(2,1)}, u32[]{:S(2)}, u32[]{:S(2)}) collective-permute-start(bf16[128,1536]{1,0:T(8,128)(2,1)S(1)} %copy.218), channel_id=1, source_target_pairs={{0,1},{1,2},{2,3},{3,0},{4,5},{5,6},{6,7},{7,4},{8,9},{9,10},{10,1... | collective-permute-start | bytes 1179656 | tf_op jit(solution)/shard_map/ppermute | solution.py:634
  117.4 106.4 %collective-permute-start.18 = (bf16[512,1536]{1,0:T(8,128)(2,1)}, bf16[512,1536]{1,0:T(8,128)(2,1)}, u32[]{:S(2)}, u32[]{:S(2)}) collective-permute-start(bf16[512,1536]{1,0:T(8,128)(2,1)} %pad_maximum_fusion.9.refs_0_.refs_7_), channel_id=1, source_target_pairs={{0,16},{8,24},{16,0},{24,8},{1,17},{9,25},{17,1},{25,9},{2,18},{10... | collective-permute-start | bytes 4718600 | tf_op jit(solution)/shard_map/ppermute | solution.py:629
  118.3 125.6 %collective-permute-start.21 = (bf16[2112,512]{1,0:T(8,128)(2,1)}, bf16[2112,512]{1,0:T(8,128)(2,1)}, u32[]{:S(2)}, u32[]{:S(2)}) collective-permute-start(bf16[2112,512]{1,0:T(8,128)(2,1)} %copy_bitcast_fusion.source), channel_id=1, source_target_pairs={{0,3},{1,0},{2,1},{3,2},{4,7},{5,4},{6,5},{7,6},{8,11},{9,8},{10,9... | collective-permute-start | bytes 6488072 | tf_op jit(solution)/shard_map/ppermute | solution.py:634
  121.4 124.5 %collective-permute-start.20 = (bf16[2112,512]{1,0:T(8,128)(2,1)}, bf16[2112,512]{1,0:T(8,128)(2,1)}, u32[]{:S(2)}, u32[]{:S(2)}) collective-permute-start(bf16[2112,512]{1,0:T(8,128)(2,1)} %copy_bitcast_fusion.source), channel_id=1, source_target_pairs={{0,1},{1,2},{2,3},{3,0},{4,5},{5,6},{6,7},{7,4},{8,9},{9,10},{10,1... | collective-permute-start | bytes 6488072 | tf_op jit(solution)/shard_map/ppermute | solution.py:634
  128.0 96.2 %collective-permute-start.17 = (bf16[512,1536]{1,0:T(8,128)(2,1)}, bf16[512,1536]{1,0:T(8,128)(2,1)}, u32[]{:S(2)}, u32[]{:S(2)}) collective-permute-start(bf16[512,1536]{1,0:T(8,128)(2,1)} %pad_maximum_fusion.9.refs_0_.refs_7_), channel_id=1, source_target_pairs={{0,8},{8,0},{16,24},{24,16},{1,9},{9,1},{17,25},{25,17},{2,10},{10... | collective-permute-start | bytes 4718600 | tf_op jit(solution)/shard_map/ppermute | solution.py:629
  162.1 61.1 %collective-permute-start.16 = (bf16[128,1024]{1,0:T(8,128)(2,1)S(1)}, bf16[128,1024]{1,0:T(8,128)(2,1)S(1)}, u32[]{:S(2)}, u32[]{:S(2)}) collective-permute-start(bf16[128,1024]{1,0:T(8,128)(2,1)S(1)} %bitcast.265), channel_id=1, source_target_pairs={{0,3},{1,0},{2,1},{3,2},{4,7},{5,4},{6,5},{7,6},{8,11},{9,8},{10,9... | collective-permute-start | bytes 786440 | tf_op jit(solution)/shard_map/ppermute | solution.py:634
  223.2 53.9 %collective-permute-start.24 = (bf16[512,2048]{1,0:T(8,128)(2,1)}, bf16[512,2048]{1,0:T(8,128)(2,1)}, u32[]{:S(2)}, u32[]{:S(2)}) collective-permute-start(bf16[512,2048]{1,0:T(8,128)(2,1)} %bitcast.222), channel_id=1, source_target_pairs={{0,16},{8,24},{16,0},{24,8},{1,17},{9,25},{17,1},{25,9},{2,18},{10... | collective-permute-start | bytes 6291464 | tf_op jit(solution)/shard_map/ppermute | solution.py:629
  223.7 57.8 %collective-permute-start.23 = (bf16[512,2048]{1,0:T(8,128)(2,1)}, bf16[512,2048]{1,0:T(8,128)(2,1)}, u32[]{:S(2)}, u32[]{:S(2)}) collective-permute-start(bf16[512,2048]{1,0:T(8,128)(2,1)} %bitcast.223), channel_id=1, source_target_pairs={{0,8},{8,0},{16,24},{24,16},{1,9},{9,1},{17,25},{25,17},{2,10},{10... | collective-permute-start | bytes 6291464 | tf_op jit(solution)/shard_map/ppermute | solution.py:629
  239.3 48.3 %collective-permute-start.19 = (bf16[256,1536]{1,0:T(8,128)(2,1)}, bf16[256,1536]{1,0:T(8,128)(2,1)}, u32[]{:S(2)}, u32[]{:S(2)}) collective-permute-start(bf16[256,1536]{1,0:T(8,128)(2,1)} %slice.238), channel_id=1, source_target_pairs={{0,16},{8,24},{16,0},{24,8},{1,17},{9,25},{17,1},{25,9},{2,18},{10... | collective-permute-start | bytes 2359304 | tf_op jit(solution)/shard_map/ppermute | solution.py:629
  243.9 45.5 %collective-permute-start.22 = (bf16[256,1536]{1,0:T(8,128)(2,1)}, bf16[256,1536]{1,0:T(8,128)(2,1)}, u32[]{:S(2)}, u32[]{:S(2)}) collective-permute-start(bf16[256,1536]{1,0:T(8,128)(2,1)} %slice.239), channel_id=1, source_target_pairs={{0,8},{8,0},{16,24},{24,16},{1,9},{9,1},{17,25},{25,17},{2,10},{10... | collective-permute-start | bytes 2359304 | tf_op jit(solution)/shard_map/ppermute | solution.py:629
  257.0 51.4 %collective-permute-start.26 = (bf16[1056,512]{1,0:T(8,128)(2,1)}, bf16[1056,512]{1,0:T(8,128)(2,1)}, u32[]{:S(2)}, u32[]{:S(2)}) collective-permute-start(bf16[1056,512]{1,0:T(8,128)(2,1)} %bitcast.217), channel_id=1, source_target_pairs={{0,2},{1,3},{2,0},{3,1},{4,6},{5,7},{6,4},{7,5},{8,10},{9,11},{10,... | collective-permute-start | bytes 3244040 | tf_op jit(solution)/shard_map/ppermute | solution.py:634
  279.5 63.8 %collective-permute-start.29 = (bf16[256,2048]{1,0:T(8,128)(2,1)}, bf16[256,2048]{1,0:T(8,128)(2,1)}, u32[]{:S(2)}, u32[]{:S(2)}) collective-permute-start(bf16[256,2048]{1,0:T(8,128)(2,1)} %slice.245), channel_id=1, source_target_pairs={{0,8},{8,0},{16,24},{24,16},{1,9},{9,1},{17,25},{25,17},{2,10},{10... | collective-permute-start | bytes 3145736 | tf_op jit(solution)/shard_map/ppermute | solution.py:629
  283.8 59.4 %collective-permute-start.28 = (bf16[256,2048]{1,0:T(8,128)(2,1)}, bf16[256,2048]{1,0:T(8,128)(2,1)}, u32[]{:S(2)}, u32[]{:S(2)}) collective-permute-start(bf16[256,2048]{1,0:T(8,128)(2,1)} %slice.244), channel_id=1, source_target_pairs={{0,16},{8,24},{16,0},{24,8},{1,17},{9,25},{17,1},{25,9},{2,18},{10... | collective-permute-start | bytes 3145736 | tf_op jit(solution)/shard_map/ppermute | solution.py:629
  305.1 49.5 %collective-permute-start.8 = (bf16[2,4,128,128]{3,2,1,0:T(8,128)(2,1)}, bf16[2,4,128,128]{3,2,1,0:T(8,128)(2,1)S(1)}, u32[]{:S(2)}, u32[]{:S(2)}) collective-permute-start(bf16[2,4,128,128]{3,2,1,0:T(8,128)(2,1)} %get-tuple-element.343), channel_id=1, source_target_pairs={{0,8},{8,16},{16,24},{1,9},{9,17},{17,25},{2,10},{10,18},{18,26},{... | collective-permute-start | bytes 786440 | tf_op jit(solution)/shard_map/ppermute | solution.py:640
  308.4 62.6 %collective-permute-start.34 = (bf16[512,1024]{1,0:T(8,128)(2,1)}, bf16[512,1024]{1,0:T(8,128)(2,1)}, u32[]{:S(2)}, u32[]{:S(2)}) collective-permute-start(bf16[512,1024]{1,0:T(8,128)(2,1)} %pad_maximum_fusion.11.refs_1_.refs_0_), channel_id=1, source_target_pairs={{0,16},{8,24},{16,0},{24,8},{1,17},{9,25},{17,1},{25,9},{2,18},{10... | collective-permute-start | bytes 3145736 | tf_op jit(solution)/shard_map/ppermute | solution.py:629
  312.0 60.1 %collective-permute-start.33 = (bf16[512,1024]{1,0:T(8,128)(2,1)}, bf16[512,1024]{1,0:T(8,128)(2,1)}, u32[]{:S(2)}, u32[]{:S(2)}) collective-permute-start(bf16[512,1024]{1,0:T(8,128)(2,1)} %pad_maximum_fusion.11.refs_1_.refs_0_), channel_id=1, source_target_pairs={{0,8},{8,0},{16,24},{24,16},{1,9},{9,1},{17,25},{25,17},{2,10},{10... | collective-permute-start | bytes 3145736 | tf_op jit(solution)/shard_map/ppermute | solution.py:629
  347.0 42.8 %collective-permute-start.27 = (bf16[1056,512]{1,0:T(8,128)(2,1)}, bf16[1056,512]{1,0:T(8,128)(2,1)S(1)}, u32[]{:S(2)}, u32[]{:S(2)}) collective-permute-start(bf16[1056,512]{1,0:T(8,128)(2,1)} %bitcast.218), channel_id=1, source_target_pairs={{0,2},{1,3},{2,0},{3,1},{4,6},{5,7},{6,4},{7,5},{8,10},{9,11},{10,... | collective-permute-start | bytes 3244040 | tf_op jit(solution)/shard_map/ppermute | solution.py:634
  422.9 48.2 %collective-permute-start.41 = (bf16[512,2048]{1,0:T(8,128)(2,1)}, bf16[512,2048]{1,0:T(8,128)(2,1)}, u32[]{:S(2)}, u32[]{:S(2)}) collective-permute-start(bf16[512,2048]{1,0:T(8,128)(2,1)} %get-tuple-element.304.mine.refs_8_), channel_id=1, source_target_pairs={{0,8},{8,0},{16,24},{24,16},{1,9},{9,1},{17,25},{25,17},{2,10},{10... | collective-permute-start | bytes 6291464 | tf_op jit(solution)/shard_map/ppermute | solution.py:629
  427.3 78.7 %collective-permute-start.43 = (bf16[512,2048]{1,0:T(8,128)(2,1)}, bf16[512,2048]{1,0:T(8,128)(2,1)}, u32[]{:S(2)}, u32[]{:S(2)}) collective-permute-start(bf16[512,2048]{1,0:T(8,128)(2,1)} %collective-permute-done.23.mine_grads.refs_18_), channel_id=1, source_target_pairs={{0,4},{4,0},{1,5},{5,1},{2,6},{6,2},{3,7},{7,3},{8,12},{12,8},{9,1... | collective-permute-start | bytes 6291464 | tf_op jit(solution)/shard_map/ppermute | solution.py:629
  431.3 48.3 %collective-permute-start.46 = (bf16[512,2048]{1,0:T(8,128)(2,1)}, bf16[512,2048]{1,0:T(8,128)(2,1)}, u32[]{:S(2)}, u32[]{:S(2)}) collective-permute-start(bf16[512,2048]{1,0:T(8,128)(2,1)} %get-tuple-element.304.mine.refs_8_), channel_id=1, source_target_pairs={{0,16},{8,24},{16,0},{24,8},{1,17},{9,25},{17,1},{25,9},{2,18},{10... | collective-permute-start | bytes 6291464 | tf_op jit(solution)/shard_map/ppermute | solution.py:629
  471.1 34.8 %collective-permute-start.42 = (bf16[512,2048]{1,0:T(8,128)(2,1)}, bf16[512,2048]{1,0:T(8,128)(2,1)S(1)}, u32[]{:S(2)}, u32[]{:S(2)}) collective-permute-start(bf16[512,2048]{1,0:T(8,128)(2,1)} %collective-permute-done.41.mine.refs_10_), channel_id=1, source_target_pairs={{0,4},{4,0},{1,5},{5,1},{2,6},{6,2},{3,7},{7,3},{8,12},{12,8},{9,1... | collective-permute-start | bytes 6291464 | tf_op jit(solution)/shard_map/ppermute | solution.py:629
  482.5 55.0 %collective-permute-start.50 = (bf16[512,2048]{1,0:T(8,128)(2,1)}, bf16[512,2048]{1,0:T(8,128)(2,1)}, u32[]{:S(2)}, u32[]{:S(2)}) collective-permute-start(bf16[512,2048]{1,0:T(8,128)(2,1)} %collective-permute-done.24.mine_grads.refs_20_), channel_id=1, source_target_pairs={{0,4},{4,0},{1,5},{5,1},{2,6},{6,2},{3,7},{7,3},{8,12},{12,8},{9,1... | collective-permute-start | bytes 6291464 | tf_op jit(solution)/shard_map/ppermute | solution.py:629
  505.9 31.6 %collective-permute-start.49 = (bf16[512,2048]{1,0:T(8,128)(2,1)}, bf16[512,2048]{1,0:T(8,128)(2,1)}, u32[]{:S(2)}, u32[]{:S(2)}) collective-permute-start(bf16[512,2048]{1,0:T(8,128)(2,1)} %collective-permute-done.46.mine.refs_12_), channel_id=1, source_target_pairs={{0,4},{4,0},{1,5},{5,1},{2,6},{6,2},{3,7},{7,3},{8,12},{12,8},{9,1... | collective-permute-start | bytes 6291464 | tf_op jit(solution)/shard_map/ppermute | solution.py:629
  537.0 35.8 %collective-permute-start.44 = (bf16[512,2048]{1,0:T(8,128)(2,1)}, bf16[512,2048]{1,0:T(8,128)(2,1)S(1)}, u32[]{:S(2)}, u32[]{:S(2)}) collective-permute-start(bf16[512,2048]{1,0:T(8,128)(2,1)} %get-tuple-element.151), channel_id=1, source_target_pairs={{0,4},{4,0},{1,5},{5,1},{2,6},{6,2},{3,7},{7,3},{8,12},{12,8},{9,1... | collective-permute-start | bytes 6291464 | tf_op jit(solution)/shard_map/ppermute | solution.py:629
  574.9 47.8 %collective-permute-start.45 = (bf16[512,2048]{1,0:T(8,128)(2,1)}, bf16[512,2048]{1,0:T(8,128)(2,1)S(1)}, u32[]{:S(2)}, u32[]{:S(2)}) collective-permute-start(bf16[512,2048]{1,0:T(8,128)(2,1)} %add_convert_fusion.5), channel_id=1, source_target_pairs={{0,8},{8,0},{16,24},{24,16},{1,9},{9,1},{17,25},{25,17},{2,10},{10... | collective-permute-start | bytes 6291464 | tf_op jit(solution)/shard_map/ppermute | solution.py:629
  578.2 47.6 %collective-permute-start.52 = (bf16[512,2048]{1,0:T(8,128)(2,1)}, bf16[512,2048]{1,0:T(8,128)(2,1)}, u32[]{:S(2)}, u32[]{:S(2)}) collective-permute-start(bf16[512,2048]{1,0:T(8,128)(2,1)} %add_convert_fusion.4), channel_id=1, source_target_pairs={{0,16},{8,24},{16,0},{24,8},{1,17},{9,25},{17,1},{25,9},{2,18},{10... | collective-permute-start | bytes 6291464 | tf_op jit(solution)/shard_map/ppermute | solution.py:629
  625.8 61.4 %collective-permute-start.40 = (bf16[512,2048]{1,0:T(8,128)(2,1)}, bf16[512,2048]{1,0:T(8,128)(2,1)}, u32[]{:S(2)}, u32[]{:S(2)}) collective-permute-start(bf16[512,2048]{1,0:T(8,128)(2,1)} %get-tuple-element.147), channel_id=1, source_target_pairs={{0,4},{4,0},{1,5},{5,1},{2,6},{6,2},{3,7},{7,3},{8,12},{12,8},{9,1... | collective-permute-start | bytes 6291464 | tf_op jit(solution)/shard_map/ppermute | solution.py:629
  636.8 50.3 %collective-permute-start.56 = (bf16[512,2048]{1,0:T(8,128)(2,1)}, bf16[512,2048]{1,0:T(8,128)(2,1)}, u32[]{:S(2)}, u32[]{:S(2)}) collective-permute-start(bf16[512,2048]{1,0:T(8,128)(2,1)} %add_convert_fusion.3), channel_id=1, source_target_pairs={{0,24},{8,16},{16,8},{24,0},{1,25},{9,17},{17,9},{25,1},{2,26},{10... | collective-permute-start | bytes 6291464 | tf_op jit(solution)/shard_map/ppermute | solution.py:629
  700.0 63.8 %collective-permute-start.67 = (bf16[2112,512]{1,0:T(8,128)(2,1)}, bf16[2112,512]{1,0:T(8,128)(2,1)}, u32[]{:S(2)}, u32[]{:S(2)}) collective-permute-start(bf16[2112,512]{1,0:T(8,128)(2,1)} %get-tuple-element.309), channel_id=1, source_target_pairs={{0,1},{1,2},{2,3},{3,0},{4,5},{5,6},{6,7},{7,4},{8,9},{9,10},{10,1... | collective-permute-start | bytes 6488072 | tf_op jit(solution)/shard_map/ppermute | solution.py:634
  727.6 50.8 %collective-permute-start.59 = (bf16[512,2048]{1,0:T(8,128)(2,1)}, bf16[512,2048]{1,0:T(8,128)(2,1)}, u32[]{:S(2)}, u32[]{:S(2)}) collective-permute-start(bf16[512,2048]{1,0:T(8,128)(2,1)} %get-tuple-element.174), channel_id=1, source_target_pairs={{0,4},{4,0},{1,5},{5,1},{2,6},{6,2},{3,7},{7,3},{8,12},{12,8},{9,1... | collective-permute-start | bytes 6291464 | tf_op jit(solution)/shard_map/ppermute | solution.py:629
  744.2 40.7 %collective-permute-start.64 = (bf16[512,2048]{1,0:T(8,128)(2,1)}, bf16[512,2048]{1,0:T(8,128)(2,1)}, u32[]{:S(2)}, u32[]{:S(2)}) collective-permute-start(bf16[512,2048]{1,0:T(8,128)(2,1)} %get-tuple-element.180), channel_id=1, source_target_pairs={{0,4},{4,0},{1,5},{5,1},{2,6},{6,2},{3,7},{7,3},{8,12},{12,8},{9,1... | collective-permute-start | bytes 6291464 | tf_op jit(solution)/shard_map/ppermute | solution.py:629
  763.8 71.0 %collective-permute-start.66 = (bf16[512,2048]{1,0:T(8,128)(2,1)}, bf16[512,2048]{1,0:T(8,128)(2,1)}, u32[]{:S(2)}, u32[]{:S(2)}) collective-permute-start(bf16[512,2048]{1,0:T(8,128)(2,1)} %get-tuple-element.184), channel_id=1, source_target_pairs={{0,4},{4,0},{1,5},{5,1},{2,6},{6,2},{3,7},{7,3},{8,12},{12,8},{9,1... | collective-permute-start | bytes 6291464 | tf_op jit(solution)/shard_map/ppermute | solution.py:629
  774.7 65.8 %collective-permute-start.69 = (bf16[2112,512]{1,0:T(8,128)(2,1)}, bf16[2112,512]{1,0:T(8,128)(2,1)}, u32[]{:S(2)}, u32[]{:S(2)}) collective-permute-start(bf16[2112,512]{1,0:T(8,128)(2,1)} %get-tuple-element.195), channel_id=1, source_target_pairs={{0,3},{1,0},{2,1},{3,2},{4,7},{5,4},{6,5},{7,6},{8,11},{9,8},{10,9... | collective-permute-start | bytes 6488072 | tf_op jit(solution)/shard_map/ppermute | solution.py:634
  782.2 58.2 %collective-permute-start.63 = (bf16[512,2048]{1,0:T(8,128)(2,1)}, bf16[512,2048]{1,0:T(8,128)(2,1)}, u32[]{:S(2)}, u32[]{:S(2)}) collective-permute-start(bf16[512,2048]{1,0:T(8,128)(2,1)} %add_convert_fusion.2), channel_id=1, source_target_pairs={{0,8},{8,0},{16,24},{24,16},{1,9},{9,1},{17,25},{25,17},{2,10},{10... | collective-permute-start | bytes 6291464 | tf_op jit(solution)/shard_map/ppermute | solution.py:629
  788.6 51.8 %collective-permute-start.65 = (bf16[512,2048]{1,0:T(8,128)(2,1)}, bf16[512,2048]{1,0:T(8,128)(2,1)}, u32[]{:S(2)}, u32[]{:S(2)}) collective-permute-start(bf16[512,2048]{1,0:T(8,128)(2,1)} %add_convert_fusion.1), channel_id=1, source_target_pairs={{0,16},{8,24},{16,0},{24,8},{1,17},{9,25},{17,1},{25,9},{2,18},{10... | collective-permute-start | bytes 6291464 | tf_op jit(solution)/shard_map/ppermute | solution.py:629
  840.4 96.4 %collective-permute-start.71 = (bf16[1056,512]{1,0:T(8,128)(2,1)}, bf16[1056,512]{1,0:T(8,128)(2,1)}, u32[]{:S(2)}, u32[]{:S(2)}) collective-permute-start(bf16[1056,512]{1,0:T(8,128)(2,1)} %get-tuple-element.206), channel_id=1, source_target_pairs={{0,2},{1,3},{2,0},{3,1},{4,6},{5,7},{6,4},{7,5},{8,10},{9,11},{10,... | collective-permute-start | bytes 3244040 | tf_op jit(solution)/shard_map/ppermute | solution.py:634
  848.2 121.3 %collective-permute-start.90 = (bf16[256,1536]{1,0:T(8,128)(2,1)}, bf16[256,1536]{1,0:T(8,128)(2,1)}, u32[]{:S(2)}, u32[]{:S(2)}) collective-permute-start(bf16[256,1536]{1,0:T(8,128)(2,1)} %convolution_convert_fusion.4), channel_id=1, source_target_pairs={{0,16},{8,24},{16,0},{24,8},{1,17},{9,25},{17,1},{25,9},{2,18},{10... | collective-permute-start | bytes 2359304 | tf_op jit(solution)/shard_map/ppermute | solution.py:629
  850.8 121.5 %collective-permute-start.91 = (bf16[256,1536]{1,0:T(8,128)(2,1)}, bf16[256,1536]{1,0:T(8,128)(2,1)}, u32[]{:S(2)}, u32[]{:S(2)}) collective-permute-start(bf16[256,1536]{1,0:T(8,128)(2,1)} %convolution_convert_fusion.3), channel_id=1, source_target_pairs={{0,8},{8,0},{16,24},{24,16},{1,9},{9,1},{17,25},{25,17},{2,10},{10... | collective-permute-start | bytes 2359304 | tf_op jit(solution)/shard_map/ppermute | solution.py:629
  853.5 121.9 %collective-permute-start.92 = (bf16[256,1536]{1,0:T(8,128)(2,1)}, bf16[256,1536]{1,0:T(8,128)(2,1)}, u32[]{:S(2)}, u32[]{:S(2)}) collective-permute-start(bf16[256,1536]{1,0:T(8,128)(2,1)} %convolution_convert_fusion.2), channel_id=1, source_target_pairs={{0,8},{8,0},{16,24},{24,16},{1,9},{9,1},{17,25},{25,17},{2,10},{10... | collective-permute-start | bytes 2359304 | tf_op jit(solution)/shard_map/ppermute | solution.py:629
  897.0 78.4 %collective-permute-start.93 = (bf16[256,1536]{1,0:T(8,128)(2,1)}, bf16[256,1536]{1,0:T(8,128)(2,1)}, u32[]{:S(2)}, u32[]{:S(2)}) collective-permute-start(bf16[256,1536]{1,0:T(8,128)(2,1)} %convolution_convert_fusion.1), channel_id=1, source_target_pairs={{0,16},{8,24},{16,0},{24,8},{1,17},{9,25},{17,1},{25,9},{2,18},{10... | collective-permute-start | bytes 2359304 | tf_op jit(solution)/shard_map/ppermute | solution.py:629
  943.0 95.8 %collective-permute-start.99 = (bf16[1056,512]{1,0:T(8,128)(2,1)}, bf16[1056,512]{1,0:T(8,128)(2,1)}, u32[]{:S(2)}, u32[]{:S(2)}) collective-permute-start(bf16[1056,512]{1,0:T(8,128)(2,1)} %get-tuple-element.217), channel_id=1, source_target_pairs={{0,2},{1,3},{2,0},{3,1},{4,6},{5,7},{6,4},{7,5},{8,10},{9,11},{10,... | collective-permute-start | bytes 3244040 | tf_op jit(solution)/shard_map/ppermute | solution.py:634
  972.3 54.6 %collective-permute-start.74 = (bf16[256,1664]{1,0:T(8,128)(2,1)}, bf16[256,1664]{1,0:T(8,128)(2,1)}, u32[]{:S(2)}, u32[]{:S(2)}) collective-permute-start(bf16[256,1664]{1,0:T(8,128)(2,1)} %convolution_convert_fusion.7), channel_id=1, source_target_pairs={{0,8},{8,0},{16,24},{24,16},{1,9},{9,1},{17,25},{25,17},{2,10},{10... | collective-permute-start | bytes 2555912 | tf_op jit(solution)/shard_map/ppermute | solution.py:629
  977.6 38.2 %collective-permute-start.94 = (bf16[256,1536]{1,0:T(8,128)(2,1)S(1)}, bf16[256,1536]{1,0:T(8,128)(2,1)S(1)}, u32[]{:S(2)}, u32[]{:S(2)}) collective-permute-start(bf16[256,1536]{1,0:T(8,128)(2,1)S(1)} %fusion.22), channel_id=1, source_target_pairs={{0,8},{8,0},{16,24},{24,16},{1,9},{9,1},{17,25},{25,17},{2,10},{10... | collective-permute-start | bytes 2359304 | tf_op jit(solution)/shard_map/ppermute | solution.py:629
  980.0 38.0 %collective-permute-start.95 = (bf16[256,1536]{1,0:T(8,128)(2,1)S(1)}, bf16[256,1536]{1,0:T(8,128)(2,1)S(1)}, u32[]{:S(2)}, u32[]{:S(2)}) collective-permute-start(bf16[256,1536]{1,0:T(8,128)(2,1)S(1)} %fusion.23), channel_id=1, source_target_pairs={{0,16},{8,24},{16,0},{24,8},{1,17},{9,25},{17,1},{25,9},{2,18},{10... | collective-permute-start | bytes 2359304 | tf_op jit(solution)/shard_map/ppermute | solution.py:629
  995.2 75.9 %collective-permute-start.85 = (bf16[256,1664]{1,0:T(8,128)(2,1)}, bf16[256,1664]{1,0:T(8,128)(2,1)}, u32[]{:S(2)}, u32[]{:S(2)}) collective-permute-start(bf16[256,1664]{1,0:T(8,128)(2,1)} %convolution_convert_fusion.6), channel_id=1, source_target_pairs={{0,16},{8,24},{16,0},{24,8},{1,17},{9,25},{17,1},{25,9},{2,18},{10... | collective-permute-start | bytes 2555912 | tf_op jit(solution)/shard_map/ppermute | solution.py:629
  1015.8 90.3 %collective-permute-start.78 = (bf16[2,256,2048]{2,1,0:T(8,128)(2,1)}, bf16[2,256,2048]{2,1,0:T(8,128)(2,1)}, u32[]{:S(2)}, u32[]{:S(2)}) collective-permute-start(bf16[2,256,2048]{2,1,0:T(8,128)(2,1)} %constant_dynamic-slice_fusion.8), channel_id=1, source_target_pairs={{0,4},{4,0},{1,5},{5,1},{2,6},{6,2},{3,7},{7,3},{8,12},{12,8},{9,1... | collective-permute-start | bytes 6291464 | tf_op jit(solution)/shard_map/ppermute | solution.py:629
  1018.0 53.1 %collective-permute-start.73 = (bf16[256,1664]{1,0:T(8,128)(2,1)}, bf16[256,1664]{1,0:T(8,128)(2,1)}, u32[]{:S(2)}, u32[]{:S(2)}) collective-permute-start(bf16[256,1664]{1,0:T(8,128)(2,1)} %fusion.24), channel_id=1, source_target_pairs={{0,8},{8,0},{16,24},{24,16},{1,9},{9,1},{17,25},{25,17},{2,10},{10... | collective-permute-start | bytes 2555912 | tf_op jit(solution)/shard_map/ppermute | solution.py:629
  1038.8 29.0 %collective-permute-start.97 = (bf16[128,1536]{0,1:T(8,128)(2,1)}, bf16[128,1536]{0,1:T(8,128)(2,1)}, u32[]{:S(2)}, u32[]{:S(2)}) collective-permute-start(bf16[128,1536]{0,1:T(8,128)(2,1)} %bitcast.277), channel_id=1, source_target_pairs={{0,2},{1,3},{2,0},{3,1},{4,6},{5,7},{6,4},{7,5},{8,10},{9,11},{10,... | collective-permute-start | bytes 1179656 | tf_op jit(solution)/shard_map/ppermute | solution.py:634
  1038.8 29.3 %collective-permute-start.96 = (bf16[128,1536]{0,1:T(8,128)(2,1)}, bf16[128,1536]{0,1:T(8,128)(2,1)}, u32[]{:S(2)}, u32[]{:S(2)}) collective-permute-start(bf16[128,1536]{0,1:T(8,128)(2,1)} %bitcast.276), channel_id=1, source_target_pairs={{0,1},{1,2},{2,3},{3,0},{4,5},{5,6},{6,7},{7,4},{8,9},{9,10},{10,1... | collective-permute-start | bytes 1179656 | tf_op jit(solution)/shard_map/ppermute | solution.py:634
  1055.2 132.8 %all-to-all-start.1 = ((bf16[4,2112,128]{2,1,0:T(8,128)(2,1)}), bf16[4,2112,128]{2,1,0:T(8,128)(2,1)}, u32[]{:S(2)}, u32[]{:S(2)}) async-start(bf16[4,2112,128]{2,1,0:T(8,128)(2,1)} %copy.208), calls=%async_computation.2 | async-start | bytes 4325376 | tf_op jit(solution)/shard_map/all_to_all | solution.py:1044
  1067.8 35.7 %collective-permute-start.86 = (bf16[256,1664]{1,0:T(8,128)(2,1)}, bf16[256,1664]{1,0:T(8,128)(2,1)S(1)}, u32[]{:S(2)}, u32[]{:S(2)}) collective-permute-start(bf16[256,1664]{1,0:T(8,128)(2,1)} %convolution_convert_fusion.5), channel_id=1, source_target_pairs={{0,8},{8,0},{16,24},{24,16},{1,9},{9,1},{17,25},{25,17},{2,10},{10... | collective-permute-start | bytes 2555912 | tf_op jit(solution)/shard_map/ppermute | solution.py:629
  1068.1 35.4 %collective-permute-start.75 = (bf16[256,1664]{1,0:T(8,128)(2,1)}, bf16[256,1664]{1,0:T(8,128)(2,1)S(1)}, u32[]{:S(2)}, u32[]{:S(2)}) collective-permute-start(bf16[256,1664]{1,0:T(8,128)(2,1)} %fusion.25), channel_id=1, source_target_pairs={{0,16},{8,24},{16,0},{24,8},{1,17},{9,25},{17,1},{25,9},{2,18},{10... | collective-permute-start | bytes 2555912 | tf_op jit(solution)/shard_map/ppermute | solution.py:629
  1071.0 119.7 %collective-permute-start.58 = (bf16[512,2048]{1,0:T(8,128)(2,1)}, bf16[512,2048]{1,0:T(8,128)(2,1)}, u32[]{:S(2)}, u32[]{:S(2)}) collective-permute-start(bf16[512,2048]{1,0:T(8,128)(2,1)} %get-tuple-element.171), channel_id=1, source_target_pairs={{0,4},{4,0},{1,5},{5,1},{2,6},{6,2},{3,7},{7,3},{8,12},{12,8},{9,1... | collective-permute-start | bytes 6291464 | tf_op jit(solution)/shard_map/ppermute | solution.py:629
  1119.3 38.3 %collective-permute-start.88 = (bf16[128,1664]{0,1:T(8,128)(2,1)}, bf16[128,1664]{0,1:T(8,128)(2,1)S(1)}, u32[]{:S(2)}, u32[]{:S(2)}) collective-permute-start(bf16[128,1664]{0,1:T(8,128)(2,1)} %bitcast.275), channel_id=1, source_target_pairs={{0,2},{1,3},{2,0},{3,1},{4,6},{5,7},{6,4},{7,5},{8,10},{9,11},{10,... | collective-permute-start | bytes 1277960 | tf_op jit(solution)/shard_map/ppermute | solution.py:634
  1119.9 37.8 %collective-permute-start.87 = (bf16[128,1664]{0,1:T(8,128)(2,1)S(1)}, bf16[128,1664]{0,1:T(8,128)(2,1)S(1)}, u32[]{:S(2)}, u32[]{:S(2)}) collective-permute-start(bf16[128,1664]{0,1:T(8,128)(2,1)S(1)} %bitcast.274), channel_id=1, source_target_pairs={{0,1},{1,2},{2,3},{3,0},{4,5},{5,6},{6,7},{7,4},{8,9},{9,10},{10,1... | collective-permute-start | bytes 1277960 | tf_op jit(solution)/shard_map/ppermute | solution.py:634
  1126.2 64.5 %collective-permute-start.76 = (bf16[512,2048]{1,0:T(8,128)(2,1)}, bf16[512,2048]{1,0:T(8,128)(2,1)}, u32[]{:S(2)}, u32[]{:S(2)}) collective-permute-start(bf16[512,2048]{1,0:T(8,128)(2,1)} %convert_add_fusion.3), channel_id=1, source_target_pairs={{0,24},{8,16},{16,8},{24,0},{1,25},{9,17},{17,9},{25,1},{2,26},{10... | collective-permute-start | bytes 6291464 | tf_op jit(solution)/shard_map/ppermute | solution.py:629
  1129.8 45.3 %collective-permute-start.82 = (f32[16640]{0:T(1024)S(1)}, f32[16640]{0:T(1024)S(1)}, u32[]{:S(2)}, u32[]{:S(2)}) collective-permute-start(f32[16640]{0:T(1024)S(1)} %fusion.111), channel_id=1, source_target_pairs={{0,16},{8,24},{16,0},{24,8},{1,17},{9,25},{17,1},{25,9},{2,18},{10... | collective-permute-start | bytes 199688 | tf_op jit(solution)/shard_map/ppermute | solution.py:629
  (95 other events, 1273.7 us)
Sparse Core Ops, SparseCore 0:
  832.1 175.2 reduce-scatter.1

commit v5 on v4

--- a/solution.py
+++ b/solution.py
@@ -455,9 +455,9 @@
         result_out[...] = result[here]
 
 
-def ffn_both(rows, grads, weights):
+def ffn_both(rows, grads, gate_up, down):
     count, width = rows[0].shape
-    units = weights.shape[0] // 3
+    units = down.shape[0]
     tile = min(256, count)
     wide_rows = pl.BlockSpec((tile, width), lambda i: (i, 0))
     narrow = pl.BlockSpec((3, tile, units), lambda i: (0, i, 0))
@@ -469,14 +469,14 @@
     outs = pl.pallas_call(
         ffn_kernel,
         grid=(count // tile,),
-        in_specs=[wide_rows] * 4 + [third(0), third(1), third(2)],
+        in_specs=[wide_rows] * 4 + [third(0), third(1), third(0)],
         out_specs=[narrow, wide_rows, wide_rows] * 2,
         out_shape=[jax.ShapeDtypeStruct((3, count, units), jnp.bfloat16), flat, flat] * 2,
         compiler_params=pltpu.CompilerParams(vmem_limit_bytes=VMEM_BYTES),
         cost_estimate=pl.CostEstimate(
             flops=24 * count * width * units, bytes_accessed=16 * count * width + 6 * units * width, transcendentals=0
         ),
-    )(*rows, *grads, weights, weights, weights)
+    )(*rows, *grads, gate_up, gate_up, down)
     return outs[:3], outs[3:]
 
 
@@ -600,28 +600,22 @@
     )(jnp.reshape(place, (1,)).astype(jnp.int32), *factors, *flat)
 
 
-def join_kernel(line, source, *refs):
-    refs[-1][...] = source[...]
-
-
-def columns_join(full, piece, line, lines, squares):
-    rows, columns = piece.shape
+def join_kernel(source, target):
+    target[...] = source[0]
+
+
+def columns_join(parts, squares):
+    lines, rows, columns = parts.shape
     part = columns // squares
-    known = [] if full is None else [full]
     return pl.pallas_call(
         join_kernel,
-        grid_spec=pltpu.PrefetchScalarGridSpec(
-            num_scalar_prefetch=1,
-            grid=(squares,),
-            in_specs=[pl.BlockSpec((rows, part), lambda j, line: (0, j))]
-            + [pl.BlockSpec(memory_space=pl.ANY) for _ in known],
-            out_specs=pl.BlockSpec((rows, part), lambda j, line: (0, j * lines + line[0])),
-        ),
-        out_shape=jax.ShapeDtypeStruct((rows, lines * columns), piece.dtype),
-        input_output_aliases={2: 0} if known else {},
+        grid=(lines, squares),
+        in_specs=[pl.BlockSpec((1, rows, part), lambda i, j: (i, 0, j))],
+        out_specs=pl.BlockSpec((rows, part), lambda i, j: (0, j * lines + i)),
+        out_shape=jax.ShapeDtypeStruct((rows, lines * columns), parts.dtype),
         compiler_params=pltpu.CompilerParams(vmem_limit_bytes=VMEM_BYTES),
-        cost_estimate=pl.CostEstimate(flops=0, bytes_accessed=4 * piece.size, transcendentals=0),
-    )(jnp.reshape(line, (1,)).astype(jnp.int32), piece, *known)
+        cost_estimate=pl.CostEstimate(flops=0, bytes_accessed=4 * parts.size, transcendentals=0),
+    )(parts)
 
 
 def flip(value, axis, bit):
@@ -719,22 +713,32 @@
     def __init__(self, columns, grads):
         self.columns, self.grads = columns, grads
         self.half = columns[0].shape[1] // 2
-        self.sent = [low(self.block(*which)) for which in ((3, 0), (3, 1), (1, 1), (2, 0))]
-        self.first = tuple(flip(part, "ctx", bit) for part, bit in zip(self.sent, (2, 1, 1, 2)))
-
-    def block(self, bit, lower):
-        return outer_rows(self.columns[bit][:, lower * self.half : (lower + 1) * self.half], self.grads)
-
-    def finish(self, *earlier):
+        beside, across = (
+            jnp.concatenate([self.side(3, 1), self.side(1, 1)], axis=1),
+            jnp.concatenate([self.side(3, 0), self.side(2, 0)], axis=1),
+        )
+        self.sent = [low(outer_rows(beside, grads)), low(outer_rows(across, grads))]
+        self.first = (flip(self.sent[0], "ctx", 1), flip(self.sent[1], "ctx", 2))
+
+    def side(self, bit, lower):
+        return self.columns[bit][:, lower * self.half : (lower + 1) * self.half]
+
+    def second(self, *earlier):
         first = self.first
         if earlier:
-            first = lax.optimization_barrier(first + earlier)[:4]
-        from_across, from_beside, beside_lower, across_upper = first
-        beside_upper = flip(low(self.block(1, 0) + wide(from_across)), "ctx", 1)
-        across_lower = flip(low(self.block(2, 1) + wide(from_beside)), "ctx", 2)
+            first = lax.optimization_barrier(first + earlier)[:2]
+        beside, across = (wide(part) for part in first)
+        beside_upper = flip(low(outer_rows(self.side(1, 0), self.grads) + across[: self.half]), "ctx", 1)
+        across_lower = flip(low(outer_rows(self.side(2, 1), self.grads) + beside[: self.half]), "ctx", 2)
         self.last = (beside_upper, across_lower)
-        upper = self.block(0, 0) + wide(beside_upper) + wide(across_upper)
-        lower = self.block(0, 1) + wide(beside_lower) + wide(across_lower)
+        self.kept = (beside, across)
+
+    def finish(self, *earlier):
+        beside_upper, across_lower = lax.optimization_barrier(self.last + earlier)[:2]
+        beside, across = self.kept
+        own = outer_rows(self.columns[0], self.grads)
+        upper = own[: self.half] + wide(beside_upper) + across[self.half :]
+        lower = own[self.half :] + beside[self.half :] + wide(across_lower)
         own = jnp.concatenate([upper, lower], axis=0)
         lines = lax.axis_size("fsdp")
         return line_sum(own.reshape(lines, own.shape[0] // lines, own.shape[1]))
@@ -800,15 +804,22 @@
 
 
 def by_head(parts):
-    lead = parts[0].shape[:-1]
-    split = [part.reshape(lead + (-1, LANES)) for part in parts]
-    return jnp.stack(split, axis=-2).reshape(lead + (-1,))
+    heads = range(parts[0].shape[-1] // LANES)
+    return jnp.concatenate([part[..., h * LANES : (h + 1) * LANES] for h in heads for part in parts], axis=-1)
 
 
 def by_kind(joined):
-    lead = joined.shape[:-1]
-    split = joined.reshape(lead + (-1, 3, LANES))
-    return [split[..., kind, :].reshape(lead + (-1,)) for kind in range(3)]
+    return [
+        jnp.concatenate(
+            [
+                some[..., at : at + LANES]
+                for some in joined
+                for at in range(kind * LANES, some.shape[-1], 3 * LANES)
+            ],
+            axis=-1,
+        )
+        for kind in range(3)
+    ]
 
 
 def pass_states(own, transfer, forward):
@@ -863,10 +874,9 @@
     pieces = pieces.reshape(3, 4, units, shard_rows).transpose(1, 0, 2, 3)
     ffn_line = lax.all_to_all(pieces.reshape(4, 3 * units, shard_rows), "ctx", 0, 0)
     ffn_line = ffn_line.transpose(1, 0, 2).reshape(3 * units, 4 * shard_rows)
-    line_count, line_place = lax.axis_size("fsdp"), lax.axis_index("fsdp")
-    ffn_full = columns_join(None, ffn_line, line_place, line_count, 4)
-    ends_apart = sorted({1 % line_count, line_count - 1} - {0})
-    ffn_near = {d: shift(tie(ffn_line, lines[parts - 1]), "fsdp", d) for d in ends_apart}
+    gate_up_parts = lax.all_gather(ffn_line[: 2 * units], "fsdp", axis=0)
+    down_parts = lax.all_gather(ffn_line[2 * units :], "fsdp", axis=0)
+    line_count = lax.axis_size("fsdp")
 
     ctx_place = lax.axis_index("ctx")
     first_pos = ctx_place * local_len
@@ -886,16 +896,15 @@
     for p in range(parts):
         mix_full.append(square.pieces())
         square = Square(tie(lines[p + 1], *square.done()))
-        if p == 0:
-            pre.append(gathered_times(normed_mix, ctx_place, mix_full[p]))
-        else:
-            pre.append(gathered_times(tie(normed_mix, lines[-1]), ctx_place, mix_full[p]))
-        ends = pre[p].reshape(seq_count, local_len, -1)[:, local_len - HALO :, :part_cols]
-        halo = from_behind(ends, "ctx", 1)
+        rows = tie(normed_mix, lines[-1]) if p == 0 else normed_mix
+        ends = rows.reshape(seq_count, local_len, width)[:, local_len - HALO :].reshape(seq_count * HALO, width)
+        ends = gathered_times(ends, ctx_place, mix_full[p])[:, :part_cols]
+        halo = from_behind(ends.reshape(seq_count, HALO, part_cols), "ctx", 1)
+        pre.append(gathered_times(tie(rows, ends), ctx_place, mix_full[p]))
         convs = conv[:, p * part_cols : (p + 1) * part_cols]
         held = pre[p]
         if p > 0:
-            held, ffn_full = lax.optimization_barrier((held, ffn_full, grad_square.beside, grad_square.across))[:2]
+            held = tie(held, grad_square.beside, grad_square.across)
         kept.append(
             [halo, convs]
             + list(
@@ -906,14 +915,6 @@
         )
         square.forward(kept[p][2])
         if p == 0:
-            ffn_near = dict(zip(ends_apart, lax.optimization_barrier(tuple(ffn_near.values()))))
-            for d in ends_apart:
-                ffn_full = columns_join(ffn_full, ffn_near[d], (line_place - d) % line_count, line_count, 4)
-            cut = 3 * units // 2
-            ffn_far = {
-                d: shift(tie(ffn_line[:cut], *ffn_near.values()), "fsdp", d) for d in range(2, line_count - 1)
-            }
-            square.upper = tie(square.upper, *ffn_near.values())
             grad_square = Square(tie(grads_mine, kept[p][2]))
         if p == parts - 1:
             grad_square.forward()
@@ -924,39 +925,35 @@
         transfers.append(low(final[..., LANES:]))
         first = final[..., :LANES]
         if len(entered) == parts - 1:
-            first = tie(first, *grad_square.done(), *ffn_far.values())
-            ffn_far = {
-                d: [piece, shift(tie(ffn_line[cut:], piece), "fsdp", d)] for d, piece in ffn_far.items()
-            }
+            first, gate_up_parts = lax.optimization_barrier((first, gate_up_parts) + grad_square.done())[:2]
         entered.append(pass_states(first, transfers[-1], 1))
         if len(entered) == parts:
-            carry = tie(carry, *(piece[1] for piece in ffn_far.values()))
+            carry, down_parts = lax.optimization_barrier((carry, down_parts))
         mixed_rows.append(mixer_output(own, carry, entered[-1], gain_head, group))
     mixed_rows = jnp.concatenate(mixed_rows, axis=1)
+    grad_rows = [
+        both_sides(part) for part in (grad_square.own, grad_square.beside, grad_square.across, grad_square.far())
+    ]
+    mixed_rows = tie(mixed_rows, *(other for _, other in grad_rows))
 
     branch = gathered_times_transposed([mixed_rows], ctx_place, [out_full]).reshape(seq_count, local_len, width)
     residual = inputs_mine + rows_scatter(branch).reshape(-1, width)
     scale_ffn = rms_scale(residual, EPSILON)
     square = Square(low(residual * scale_ffn * gain_ffn))
-    for d, pieces in ffn_far.items():
-        piece = jnp.concatenate(pieces, axis=0)
-        ffn_full = columns_join(ffn_full, piece, (line_place - d) % line_count, line_count, 4)
+    ffn_full = (columns_join(gate_up_parts, 4), columns_join(down_parts, 4))
 
     ffn_rows = [both_sides(square.own)]
-    grad_rows = [
-        both_sides(part) for part in (grad_square.own, grad_square.beside, grad_square.across, grad_square.far())
-    ]
-    ffn_out = [ffn_both(ffn_rows[0], grad_rows[0], ffn_full)]
+    ffn_out = [ffn_both(ffn_rows[0], grad_rows[0], *ffn_full)]
     square.forward(ffn_out[0][0][0])
     ffn_rows.append(both_sides(tie(square.beside, ffn_out[0][0][0])))
-    ffn_out.append(ffn_both(ffn_rows[1], grad_rows[1], ffn_full))
-    ffn_rows.append(both_sides(tie(square.across, ffn_out[0][0][0], *square.done())))
+    ffn_out.append(ffn_both(ffn_rows[1], grad_rows[1], *ffn_full))
+    ffn_rows.append(both_sides(tie(square.across, ffn_out[0][0][0])))
     mine, other = ffn_rows[2]
-    ffn_out.append(ffn_both((tie(mine, ffn_out[1][0][0]), other), grad_rows[2], ffn_full))
+    ffn_out.append(ffn_both((tie(mine, ffn_out[1][0][0], *square.done()), other), grad_rows[2], *ffn_full))
     beside_sums, across_sums = (low(core_sum(*(side[1] for side in ffn_out[bit]))) for bit in (1, 2))
     ffn_rows.append(both_sides(square.far()))
     mine, other = ffn_rows[3]
-    ffn_out.append(ffn_both((tie(mine, beside_sums, across_sums), other), grad_rows[3], ffn_full))
+    ffn_out.append(ffn_both((tie(mine, beside_sums, across_sums), other), grad_rows[3], *ffn_full))
     near_sums = (flip(beside_sums, "ctx", 1), flip(across_sums, "ctx", 2))
     mine, other = (side[1] for side in ffn_out[3])
     far_sums = low(core_sum(mine, tie(other, *near_sums)))
@@ -972,6 +969,10 @@
     ).reshape(line_count, 3 * units, 4 * shard_rows)
 
     far_sums, sums = lax.optimization_barrier((far_sums, sums))
+    result_near = []
+    for bit in (1, 2):
+        mine, other = (side[2] for side in ffn_out[bit])
+        result_near.append(flip(low(core_sum(mine, tie(other, far_sums))), "ctx", bit))
     grad_normed = core_sum(*(side[1] for side in ffn_out[0]))
     grad_normed = grad_normed + wide(near_sums[0]) + wide(near_sums[1]) + wide(far_sums)
     back_ffn, unit_ffn = norm_backward(grad_normed, residual, scale_ffn, gain_ffn)
@@ -988,31 +989,17 @@
         backs.append(back)
         acrosses.append(across)
         gain_o_part = gain_o_part + jnp.sum(gain_part, axis=(0, 1, 2))
+    acrosses[0] = tie(acrosses[0], *result_near)
     grad_end = pass_states(jnp.concatenate(acrosses, axis=1), jnp.concatenate(transfers, axis=1), -1)
-    results = []
-    for outs in ffn_out:
-        mine, other = (side[2] for side in outs)
-        results.append(core_sum(mine, tie(other, grad_branch)))
-    result_near = [flip(tie(low(results[bit]), grad_end), "ctx", bit) for bit in (1, 2)]
-    result_own, result_far = results[0], results[3]
-
-    def line_piece(distance):
-        return lax.dynamic_index_in_dim(sums, (line_place + distance) % line_count, 0, keepdims=False)
-
-    total = wide(line_piece(0))
-    cut = 3 * units // 2
-    line_sends = [(d, 0, 3 * units) for d in ends_apart]
-    line_sends += [(d, at, at + cut) for d in range(2, line_count - 1) for at in (0, cut)]
-    line_got = []
-    for d, low_row, high_row in line_sends:
-        piece = line_piece(d)[low_row:high_row]
-        if line_got:
-            piece = tie(piece, grad_end, line_got[-1])
-        line_got.append(shift(piece, "fsdp", d))
+    total = lax.psum_scatter(sums, "fsdp", scatter_dimension=0, tiled=True)
 
     out_grad_w = low(outer_rows(grad_branch, mixed_rows))
-    out_grad_w = wide(lax.psum_scatter(out_grad_w, ("ctx", "fsdp"), scatter_dimension=0, tiled=True)).T
-
+    out_grad_w = lax.psum_scatter(out_grad_w, ("ctx", "fsdp"), scatter_dimension=0, tiled=True)
+
+    mine, other = (side[2] for side in ffn_out[0])
+    result_own = core_sum(mine, tie(other, grad_branch))
+    mine, other = (side[2] for side in ffn_out[3])
+    result_far = flip(tie(low(core_sum(mine, tie(other, grad_branch))), grad_end), "ctx", 3)
     columns = neighbour_columns(normed_mix)
     grad_mixes, mix_grads, conv_parts = [None] * parts, [None] * parts, [None] * parts
     logits = 0.0
@@ -1020,7 +1007,7 @@
     for p in reversed(range(parts)):
         halo, convs, own, carry, final, inverses, updates, states = kept[p]
         heads = slice(p * part_heads, (p + 1) * part_heads)
-        back = tie(backs[p], *line_got[:1]) if scatter is None else tie(backs[p], *scatter.sent)
+        back = backs[p] if scatter is None else tie(backs[p], total, *scatter.sent)
         grad_mix, tail, before, conv_parts[p], logit = mixer_backward(
             pre[p], pre[0], bias, halo, convs, col, row, back, inverses, updates, states,
             entered[p], grad_end[:, heads], taps, p * part_heads, part_heads, group,
@@ -1030,26 +1017,15 @@
         grad_mix = put(grad_mix.reshape(seq_count, local_len, -1), tail, 0, local_len - HALO, 0)
         grad_mix = grad_mix.reshape(row_count, -1)
         if scatter is not None:
-            mix_grads[p + 1] = scatter.finish(grad_mix)
+            scatter.second(grad_mix)
+            mix_grads[p + 1] = scatter.finish()
         else:
-            grad_mix = tie(grad_mix, *result_near, *line_got[1:2])
+            grad_mix = tie(grad_mix, result_far)
         if p == 0:
-            grad_mix = tie(jnp.concatenate([grad_mix, low(logits)], axis=1), *line_got[2:3])
+            grad_mix = jnp.concatenate([grad_mix, low(logits)], axis=1)
         grad_mixes[p] = grad_mix
         scatter = Scatter(columns, grad_mix)
-    mix_grads[0] = scatter.finish()
-    for (_, low_row, high_row), part in zip(line_sends, line_got):
-        total = total + jnp.pad(wide(part), ((low_row, total.shape[0] - high_row), (0, 0)))
-    sums = tie(low(total), grad_mix).reshape(3 * units, 4, shard_rows).transpose(1, 0, 2)
-    arrived = lax.all_to_all(sums, "ctx", 0, 0).reshape(4, 3, units, shard_rows)
-    gate_grad, up_grad, down_grad = (wide(arrived[:, i].reshape(units_here, shard_rows)) for i in range(3))
-    result = result_own + wide(result_near[0]) + wide(result_near[1])
-    result = result + wide(flip(low(tie(result_far, *scatter.last)), "ctx", 3))
-    block_output = rows_full(low(residual + result).reshape(seq_count, -1, width))
-    joined = jnp.concatenate([grad[:, :part_cols] for grad in mix_grads], axis=1)
-    query_grad, key_grad, value_grad = by_kind(joined)
-    beta_grad = mix_grads[0][:, part_cols : part_cols + heads_here]
-
+    grad_mixes[0] = tie(grad_mixes[0], *scatter.sent)
     mix_back = gathered_times_transposed(grad_mixes, ctx_place, mix_full)
     mix_back = rows_scatter(mix_back.reshape(seq_count, local_len, width)).reshape(-1, width)
     back_mix, unit_mix = norm_backward(mix_back, inputs_mine, rms_scale(inputs_mine, EPSILON), gain_mix)
@@ -1059,11 +1035,23 @@
     conv_cols = jnp.concatenate([jnp.sum(part, axis=0)[:taps] for part in conv_parts], axis=1)
     gains = butterfly(jnp.concatenate([gain_mix_part, gain_ffn_part, gain_o_part]), ("tp",))
     sums = jnp.concatenate([gains, conv_cols.reshape(-1), jnp.sum(logits, axis=0)])
+    scatter.second()
     sums = butterfly(sums, ("ctx", "fsdp"))
+    mix_grads[0] = scatter.finish(sums)
     ends = [width, 2 * width, 2 * width + LANES, sums.shape[0] - LANES]
     gain_mix_grad, gain_ffn_grad, gain_o_grad, conv_grad, bias_grad = jnp.split(sums, ends)
-    conv_grad = jnp.stack(by_kind(conv_grad.reshape(taps, -1)))
+    conv_grad = jnp.stack(by_kind([conv_grad.reshape(taps, -1)]))
     bias_grad = bias_grad[:heads_here]
+    out_grad_w = wide(tie(out_grad_w, *scatter.last)).T
+    pieces = tie(total, *scatter.last).reshape(3 * units, 4, shard_rows).transpose(1, 0, 2)
+    arrived = lax.all_to_all(pieces, "ctx", 0, 0).reshape(4, 3, units, shard_rows)
+    gate_grad, up_grad, down_grad = (wide(arrived[:, i].reshape(units_here, shard_rows)) for i in range(3))
+    result = result_own + wide(result_near[0]) + wide(result_near[1])
+    result = result + wide(result_far)
+    block_output = rows_full(low(residual + result).reshape(seq_count, -1, width))
+    query_grad, key_grad, value_grad = by_kind([grad[:, :part_cols] for grad in mix_grads])
+    beta_grad = mix_grads[0][:, part_cols : part_cols + heads_here]
+
     return (
         block_output,
         input_grad,

time: 1240 us -> 1260 us (1.016)
  waiting for transfers between devices: 392 us -> 352 us
  starting transfers between devices: 163 us -> 198 us
  Pallas kernels: 389 us -> 402 us
    ppermute x64 -> x60, waiting for transfers between devices: 183 us -> 126 us  [flip(): return lax.ppermute(value, axis, [(i, i ^ bit) for i in devices])]
    ppermute x23 -> x15, waiting for transfers between devices: 140 us -> 104 us  [shift(): lax.ppermute(value, axis, [(i, (i + distance) % count) for i in range(cou...]
    ppermute x13, waiting for transfers between devices: 67.4 us -> 99.4 us  [from_behind(): return lax.ppermute(block, axis, route)]
    ppermute x23 -> x15, starting transfers between devices: 64.2 us -> 84.5 us  [shift(): lax.ppermute(value, axis, [(i, (i + distance) % count) for i in range(cou...]
    all_to_all x1, waiting for transfers between devices: 2.25 us -> 21.6 us  [local(): lax.all_to_all(pieces.reshape(4, 3 * units, shard_rows), 'ctx', 0, 0)]
    convert_element_type x3 -> x8, other arithmetic: 2.9 us -> 17.9 us  [wide(): return value.astype(jnp.float32)]
    ppermute x64 -> x60, starting transfers between devices: 57.5 us -> 70.3 us  [flip(): return lax.ppermute(value, axis, [(i, i ^ bit) for i in devices])]
    pallas_call x3 -> x5, Pallas kernels: 33.2 us -> 42.3 us  [gathered_times(): pl.pallas_call(gathered_kernel, grid_spec=pltpu.PrefetchScalarGridSpec(nu...]
  transfers between devices with their start and end apart: 103 -> 94, of which waited for: 39 -> 37; matrix products, arithmetic and copies ran while one was open for 19% -> 19% of each run, Pallas kernels for 31% -> 29%
where the time goes in v5:
time: 1260 us; the launch traced here: 1250 us
  Pallas kernels  402 us (32%)
  waiting for transfers between devices  352 us (28%)
  starting transfers between devices  198 us (16%)
  other arithmetic  121 us (10%)
  local copies, waits for them, and re-layouts  105 us (8%)
  matrix products  52.1 us (4%)
  between operations  15.8 us (1%)
    ppermute x60, waiting for transfers between devices, flip(): return lax.ppermute(value, axis, [(i, i ^ bit) for i in devices])  126 us
    pallas_call x4, Pallas kernels, ffn_both(): pl.pallas_call(ffn_kernel, grid=(count // tile,), in_specs=[wide_rows] *...  119 us
    ppermute x15, waiting for transfers between devices, shift(): lax.ppermute(value, axis, [(i, (i + distance) % count) for i in range(cou...  104 us
    ppermute x13, waiting for transfers between devices, from_behind(): return lax.ppermute(block, axis, route)  99.4 us
    ppermute x15, starting transfers between devices, shift(): lax.ppermute(value, axis, [(i, (i + distance) % count) for i in range(cou...  84.5 us
    ppermute x60, starting transfers between devices, flip(): return lax.ppermute(value, axis, [(i, i ^ bit) for i in devices])  70.3 us
    pallas_call x2, Pallas kernels, mixer_backward(): pl.pallas_call(functools.partial(backward_kernel, taps, group, first), gr...  67 us
    pallas_call x2, Pallas kernels, mixer_forward(): pl.pallas_call(functools.partial(forward_kernel, taps, group, first), gri...  55 us
  transfers between devices with their start and end apart: 94, of which 37 were waited for; matrix products, arithmetic and copies ran while one was open for 19% of the time, Pallas kernels for 29%

profile of v5, /device:TPU:0, one launch (start us, length us, event | category | flops | bytes accessed | tf_op | source)
XLA Modules:
  0.0 1245.6 jit_solution(1066438433734915036)
XLA Ops:
  29.7 21.6 %all-to-all-done = bf16[4,2112,128]{2,1,0:T(8,128)(2,1)S(1)} async-done(((bf16[4,2112,128]{2,1,0:T(8,128)(2,1)}), bf16[4,2112,128]{2,1,0:T(8,128)(2,1)S(1)}, u32[]{:S(2)}, u32[]{:S(2)}) %all-to-all-start) | async-done | bytes 2162720 | tf_op jit(solution)/shard_map/all_to_all | solution.py:875
  58.0 5.2 fusion.1.rows
  74.4 18.3 %collective-permute-done.3 = bf16[128,1536]{1,0:T(8,128)(2,1)S(1)} collective-permute-done((bf16[128,1536]{1,0:T(8,128)(2,1)S(1)}, bf16[128,1536]{1,0:T(8,128)(2,1)S(1)}, u32[]{:S(2)}, u32[]{:S(2)}) %collective-permute-start.3) | collective-permute-done | bytes 393248 | tf_op jit(solution)/shard_map/ppermute | solution.py:628
  92.7 27.1 %collective-permute-done.4 = bf16[128,1536]{1,0:T(8,128)(2,1)S(1)} collective-permute-done((bf16[128,1536]{1,0:T(8,128)(2,1)S(1)}, bf16[128,1536]{1,0:T(8,128)(2,1)S(1)}, u32[]{:S(2)}, u32[]{:S(2)}) %collective-permute-start.4) | collective-permute-done | bytes 393248 | tf_op jit(solution)/shard_map/ppermute | solution.py:628
  123.1 26.5 %collective-permute-start.6 = (bf16[128,1024]{1,0:T(8,128)(2,1)S(1)}, bf16[128,1024]{1,0:T(8,128)(2,1)S(1)}, u32[]{:S(2)}, u32[]{:S(2)}) collective-permute-start(bf16[128,1024]{1,0:T(8,128)(2,1)S(1)} %bitcast.202), channel_id=1, source_target_pairs={{0,1},{1,2},{2,3},{3,0},{4,5},{5,6},{6,7},{7,4},{8,9},{9,10},{10,1... | collective-permute-start | bytes 786440 | tf_op jit(solution)/shard_map/ppermute | solution.py:628
  158.1 4.5 collective-permute-done.6
  162.6 16.3 %collective-permute-done.7 = bf16[128,1024]{1,0:T(8,128)(2,1)S(1)} collective-permute-done((bf16[128,1024]{1,0:T(8,128)(2,1)S(1)}, bf16[128,1024]{1,0:T(8,128)(2,1)S(1)}, u32[]{:S(2)}, u32[]{:S(2)}) %collective-permute-start.7) | collective-permute-done | bytes 262176 | tf_op jit(solution)/shard_map/ppermute | solution.py:628
  188.9 4.6 shard_map.271
  197.3 12.9 %shard_map.272.pre.beta = f32[1024,1664]{1,0:T(8,128)} custom-call(s32[1]{0:T(128)} %bitcast.1.place, bf16[1024,2048]{1,0:T(8,128)(2,1)} %fusion.1.rows, bf16[512,1664]{1,0:T(8,128)(2,1)} %pad_maximum_fusion.7.refs_0_.refs_2_, bf16[512,1664]{1,0:T(8,128)(2,1)} %collective-permute-done.9.refs_1_.refs_3_, ...), custom_call_target="tpu_custom_call" | custom-call | flops 6979321856 | bytes 11010048 | tf_op jit(solution)/shard_map/pallas_call | solution.py:551
  210.2 10.7 collective-permute-done.13.halo
  221.5 27.5 %shard_map.273 = (f32[1024,512]{1,0:T(8,128)}, bf16[1024,512]{1,0:T(8,128)(2,1)}, f32[2,4,128,256]{3,2,1,0:T(8,128)}, bf16[2,4,4,128,128]{4,3,2,1,0:T(8,128)(2,1...) custom-call(f32[1024,1664]{1,0:T(8,128)} %shard_map.272.pre.beta, ...), custom_call_target="tpu_custom_call" | custom-call | flops 4026531840 | bytes 20971520 | tf_op jit(solution)/shard_map/pallas_call | solution.py:160
  258.3 6.5 convert_element_type.442
  271.1 32.2 %collective-permute-done.14 = bf16[2,4,128,128]{3,2,1,0:T(8,128)(2,1)} collective-permute-done((bf16[2,4,128,128]{3,2,1,0:T(8,128)(2,1)}, bf16[2,4,128,128]{3,2,1,0:T(8,128)(2,1)}, u32[]{:S(2)}, u32[]{:S(2)}) %collective-permute-start.14) | collective-permute-done | bytes 262176 | tf_op jit(solution)/shard_map/ppermute | solution.py:634
  317.1 5.6 collective-permute-done.15
  333.3 6.7 collective-permute-start.23
  340.0 11.5 shard_map.276.pre
  356.1 27.6 %shard_map.277 = (f32[1024,512]{1,0:T(8,128)}, bf16[1024,512]{1,0:T(8,128)(2,1)}, f32[2,4,128,256]{3,2,1,0:T(8,128)}, bf16[2,4,4,128,128]{4,3,2,1,0:T(8,128)(2,1...) custom-call(f32[1024,1536]{1,0:T(8,128)} %shard_map.276.pre, ...), custom_call_target="tpu_custom_call" | custom-call | flops 4026531840 | bytes 20971520 | tf_op jit(solution)/shard_map/pallas_call | solution.py:160
  394.5 4.6 collective-permute-start.27
  399.2 5.7 collective-permute-done.27
  404.9 5.3 collective-permute-start.34
  410.4 22.5 %collective-permute-done.34.refs_3_.refs_2_ = bf16[512,1024]{1,0:T(8,128)(2,1)S(1)} collective-permute-done((bf16[512,1024]{1,0:T(8,128)(2,1)}, bf16[512,1024]{1,0:T(8,128)(2,1)S(1)}, u32[]{:S(2)}, u32[]{:S(2)}) %collective-permute-start.34) | collective-permute-done | bytes 1048608 | tf_op jit(solution)/shard_map/ppermute | solution.py:623
  438.7 5.6 collective-permute-start.36
  445.2 4.5 shard_map.274
  460.5 8.6 shard_map.279
  482.4 10.1 shard_map.281.down_w
  492.5 10.9 shard_map.280.gate_w.up_w
  507.3 29.7 %shard_map.282 = (bf16[3,512,704]{2,1,0:T(8,128)(2,1)}, bf16[512,2048]{1,0:T(8,128)(2,1)}, bf16[512,2048]{1,0:T(8,128)(2,1)}, bf16[3,512,704]{2,1,0:T(8,128)(2,1...) custom-call(bf16[512,2048]{1,0:T(8,128)(2,1)} %copy-done.40, ...), custom_call_target="tpu_custom_call" | custom-call | flops 17716740096 | bytes 25427968 | tf_op jit(solution)/shard_map/pallas_call | solution.py:469
  537.1 16.2 %collective-permute-done.44.mine.refs_12_ = bf16[512,2048]{1,0:T(8,128)(2,1)} collective-permute-done((bf16[512,2048]{1,0:T(8,128)(2,1)S(1)}, bf16[512,2048]{1,0:T(8,128)(2,1)}, u32[]{:S(2)}, u32[]{:S(2)}) %collective-permute-start.44) | collective-permute-done | bytes 2097184 | tf_op jit(solution)/shard_map/ppermute | solution.py:623
  559.2 29.5 %shard_map.283 = (bf16[3,512,704]{2,1,0:T(8,128)(2,1)}, bf16[512,2048]{1,0:T(8,128)(2,1)}, bf16[512,2048]{1,0:T(8,128)(2,1)}, bf16[3,512,704]{2,1,0:T(8,128)(2,1...) custom-call(bf16[512,2048]{1,0:T(8,128)(2,1)} %collective-permute-done.40.mine.refs_10_, ...), custom_call_target="tpu_custom_call" | custom-call | flops 17716740096 | bytes 25427968 | tf_op jit(solution)/shard_map/pallas_call | solution.py:469
  588.7 29.6 %shard_map.284 = (bf16[3,512,704]{2,1,0:T(8,128)(2,1)}, bf16[512,2048]{1,0:T(8,128)(2,1)}, bf16[512,2048]{1,0:T(8,128)(2,1)}, bf16[3,512,704]{2,1,0:T(8,128)(2,1...) custom-call(bf16[512,2048]{1,0:T(8,128)(2,1)} %collective-permute-done.44.mine.refs_12_, ...), custom_call_target="tpu_custom_call" | custom-call | flops 17716740096 | bytes 25427968 | tf_op jit(solution)/shard_map/pallas_call | solution.py:469
  632.4 29.8 %shard_map.285 = (bf16[3,512,704]{2,1,0:T(8,128)(2,1)}, bf16[512,2048]{1,0:T(8,128)(2,1)}, bf16[512,2048]{1,0:T(8,128)(2,1)}, bf16[3,512,704]{2,1,0:T(8,128)(2,1...) custom-call(bf16[512,2048]{1,0:T(8,128)(2,1)} %copy-done.48, ...), custom_call_target="tpu_custom_call" | custom-call | flops 17716740096 | bytes 25427968 | tf_op jit(solution)/shard_map/pallas_call | solution.py:469
  662.2 10.6 collective-permute-done.49
  672.7 6.1 collective-permute-done.43
  688.2 47.8 %shard_map.286 = bf16[4,3,704,512]{3,2,1,0:T(8,128)(2,1)} custom-call(bf16[3,512,704]{2,1,0:T(8,128)(2,1)} %get-tuple-element.155.refs_0_, bf16[3,512,704]{2,1,0:T(8,128)(2,1)} %get-tuple-element.156.refs_1_, bf16[3,512,704]{2,1,0:T(8,128)(2,1)} %get-tuple-element.145.refs_2_, bf16[3,512,704]{2,1,0:T(8,128)(2,1)} %get-tuple-element.157.refs_3_, ...), custom_call_target="tpu_custom_call" | custom-call | flops 35433480192 | bytes 67108864 | tf_op jit(solution)/shard_map/pallas_call | solution.py:516
  736.0 11.7 copy.176
  749.8 6.6 collective-permute-done.39
  756.4 7.0 multiply_reduce_fusion.1
  778.7 8.9 shard_map.287.grad
  787.7 5.7 shard_map.288
  793.4 5.8 shard_map.289
  799.2 17.6 %collective-permute-done.58 = bf16[512,2048]{1,0:T(8,128)(2,1)} collective-permute-done((bf16[512,2048]{1,0:T(8,128)(2,1)}, bf16[512,2048]{1,0:T(8,128)(2,1)}, u32[]{:S(2)}, u32[]{:S(2)}) %collective-permute-start.58) | collective-permute-done | bytes 2097184 | tf_op jit(solution)/shard_map/ppermute | solution.py:623
  824.0 12.4 collective-permute-done.60
  842.0 9.8 collective-permute-done.61
  858.3 8.5 collective-permute-done.62
  869.0 33.3 %shard_map.290 = (bf16[1024,1536]{1,0:T(8,128)(2,1)}, f32[2,8,1536]{2,1,0:T(8,128)}, f32[2,8,1536]{2,1,0:T(8,128)}, f32[2,8,1536]{2,1,0:T(8,128)}, f32[1024,128]{1,0:T(8,128)}) custom-call(f32[1024,1536]{1,0:T(8,128)} %shard_map.276.pre, f32[1024,1664]{1,0:T(8,128)} %shard_map.272.pre.beta, f32[1,128]{1,0:T(1,128)} %pad_bitcast_fusion.bias, ...), custom_call_target="tpu_custom_call" | custom-call | flops 4026531840 | bytes 20971520 | tf_op jit(solution)/shard_map/pallas_call | solution.py:318
  903.9 9.4 convolution_convert_fusion
  914.9 5.0 convolution_convert_fusion.3
  919.9 4.8 collective-permute-start.82
  929.8 33.6 %shard_map.291 = (bf16[1024,1536]{1,0:T(8,128)(2,1)}, f32[2,8,1536]{2,1,0:T(8,128)}, f32[2,8,1536]{2,1,0:T(8,128)}, f32[2,8,1536]{2,1,0:T(8,128)}, f32[1024,128]{1,0:T(8,128)}) custom-call(f32[1024,1664]{1,0:T(8,128)} %shard_map.272.pre.beta, f32[1024,1664]{1,0:T(8,128)} %shard_map.272.pre.beta, f32[1,128]{1,0:T(1,128)} %pad_bitcast_fusion.bias, ...), custom_call_target="tpu_custom_call" | custom-call | flops 4026531840 | bytes 20971520 | tf_op jit(solution)/shard_map/pallas_call | solution.py:318
  966.5 9.8 collective-permute-done.66
  977.9 5.7 convolution_convert_fusion.2
  988.9 21.5 %shard_map.292 = bf16[1024,2048]{1,0:T(8,128)(2,1)} custom-call(s32[1]{0:T(128)} %bitcast.1.place, bf16[1024,1664]{1,0:T(8,128)(2,1)} %pad_maximum_fusion.3.refs_0_, bf16[1024,1536]{1,0:T(8,128)(2,1)} %bitcast.171, bf16[512,1664]{1,0:T(8,128)(2,1)} %pad_maximum_fusion.7.refs_0_.refs_2_, bf16[512,1664]{1,0:T(8,128)(2,1)} %collective-permute-done.9.refs_1_.refs_3_, ...), custom_call_target="tpu_custom_call" | custom-call | flops 13421772800 | bytes 17301504 | tf_op jit(solution)/shard_map/pallas_call | solution.py:587
  1029.5 6.3 fusion.28
  1035.8 8.3 collective-permute-done.84
  1050.9 12.9 %collective-permute-start.85 = (bf16[128,1536]{0,1:T(8,128)(2,1)}, bf16[128,1536]{0,1:T(8,128)(2,1)}, u32[]{:S(2)}, u32[]{:S(2)}) collective-permute-start(bf16[128,1536]{0,1:T(8,128)(2,1)} %bitcast.212), channel_id=1, source_target_pairs={{0,1},{1,2},{2,3},{3,0},{4,5},{5,6},{6,7},{7,4},{8,9},{9,10},{10,1... | collective-permute-start | bytes 1179656 | tf_op jit(solution)/shard_map/ppermute | solution.py:628
  1064.7 26.6 %collective-permute-start.86 = (bf16[128,1536]{0,1:T(8,128)(2,1)}, bf16[128,1536]{0,1:T(8,128)(2,1)}, u32[]{:S(2)}, u32[]{:S(2)}) collective-permute-start(bf16[128,1536]{0,1:T(8,128)(2,1)} %bitcast.142), channel_id=1, source_target_pairs={{0,2},{1,3},{2,0},{3,1},{4,6},{5,7},{6,4},{7,5},{8,10},{9,11},{10,... | collective-permute-start | bytes 1179656 | tf_op jit(solution)/shard_map/ppermute | solution.py:628
  1094.1 4.8 fusion.9
  1100.2 13.7 %collective-permute-done.86 = bf16[128,1536]{0,1:T(8,128)(2,1)} collective-permute-done((bf16[128,1536]{0,1:T(8,128)(2,1)}, bf16[128,1536]{0,1:T(8,128)(2,1)}, u32[]{:S(2)}, u32[]{:S(2)}) %collective-permute-start.86) | collective-permute-done | bytes 393248 | tf_op jit(solution)/shard_map/ppermute | solution.py:628
  1126.2 4.6 fusion.18
  1131.8 13.4 %collective-permute-done.71 = f32[16640]{0:T(1024)S(1)} collective-permute-done((f32[16640]{0:T(1024)S(1)}, f32[16640]{0:T(1024)S(1)}, u32[]{:S(2)}, u32[]{:S(2)}) %collective-permute-start.71) | collective-permute-done | bytes 66592 | tf_op jit(solution)/shard_map/ppermute | solution.py:623
  1145.2 8.4 collective-permute-start.72
  1157.0 8.9 fusion.5
  1173.8 4.8 all-to-all-start.1
  1200.6 16.9 %collective-permute-done.79 = bf16[128,1664]{0,1:T(8,128)(2,1)} collective-permute-done((bf16[128,1664]{0,1:T(8,128)(2,1)}, bf16[128,1664]{0,1:T(8,128)(2,1)}, u32[]{:S(2)}, u32[]{:S(2)}) %collective-permute-start.79) | collective-permute-done | bytes 426016 | tf_op jit(solution)/shard_map/ppermute | solution.py:628
  (535 shorter events, 340.7 us)
Async XLA Ops:
  11.7 51.4 %collective-permute-start = (bf16[128,1664]{1,0:T(8,128)(2,1)S(1)}, bf16[128,1664]{1,0:T(8,128)(2,1)}, u32[]{:S(2)}, u32[]{:S(2)}) collective-permute-start(bf16[128,1664]{1,0:T(8,128)(2,1)S(1)} %constant_dynamic-update-slice_fusion.12), channel_id=1, source_target_pairs={{0,1},{1,2},{2,3},{3,0},{4,5},{5,6},{6,7},{7,4},{8,9},{9,10},{10,1... | collective-permute-start | bytes 1277960 | tf_op jit(solution)/shard_map/ppermute | solution.py:628
  14.8 48.4 %collective-permute-start.1 = (bf16[128,1664]{1,0:T(8,128)(2,1)S(1)}, bf16[128,1664]{1,0:T(8,128)(2,1)}, u32[]{:S(2)}, u32[]{:S(2)}) collective-permute-start(bf16[128,1664]{1,0:T(8,128)(2,1)S(1)} %constant_dynamic-update-slice_fusion.12), channel_id=1, source_target_pairs={{0,2},{1,3},{2,0},{3,1},{4,6},{5,7},{6,4},{7,5},{8,10},{9,11},{10,... | collective-permute-start | bytes 1277960 | tf_op jit(solution)/shard_map/ppermute | solution.py:628
  17.4 45.8 %collective-permute-start.2 = (bf16[128,1664]{1,0:T(8,128)(2,1)S(1)}, bf16[128,1664]{1,0:T(8,128)(2,1)}, u32[]{:S(2)}, u32[]{:S(2)}) collective-permute-start(bf16[128,1664]{1,0:T(8,128)(2,1)S(1)} %constant_dynamic-update-slice_fusion.12), channel_id=1, source_target_pairs={{0,3},{1,0},{2,1},{3,2},{4,7},{5,4},{6,5},{7,6},{8,11},{9,8},{10,9... | collective-permute-start | bytes 1277960 | tf_op jit(solution)/shard_map/ppermute | solution.py:628
  22.8 28.6 %all-to-all-start = ((bf16[4,2112,128]{2,1,0:T(8,128)(2,1)}), bf16[4,2112,128]{2,1,0:T(8,128)(2,1)S(1)}, u32[]{:S(2)}, u32[]{:S(2)}) async-start(bf16[4,2112,128]{2,1,0:T(8,128)(2,1)} %bitcast.181), calls=%async_computation | async-start | bytes 4325376 | tf_op jit(solution)/shard_map/all_to_all | solution.py:875
  26.5 358.3 %all-gather.5.cloned.1.call-start = ((), (), s32[]{:S(2)}) async-start(), calls=%async_computation.5 | async-start | bytes 7208960 | tf_op jit(solution)/shard_map/all_gather | solution.py:877
  57.8 391.9 %all-gather.3.cloned.1.call-start = ((), (), s32[]{:S(2)}) async-start(), calls=%async_computation.4 | async-start | bytes 3604480 | tf_op jit(solution)/shard_map/all_gather | solution.py:878
  66.3 86.0 %collective-permute-start.9 = (bf16[512,1664]{1,0:T(8,128)(2,1)}, bf16[512,1664]{1,0:T(8,128)(2,1)}, u32[]{:S(2)}, u32[]{:S(2)}) collective-permute-start(bf16[512,1664]{1,0:T(8,128)(2,1)} %pad_maximum_fusion.7.refs_0_.refs_2_), channel_id=1, source_target_pairs={{0,8},{8,0},{16,24},{24,16},{1,9},{9,1},{17,25},{25,17},{2,10},{10... | collective-permute-start | bytes 5111816 | tf_op jit(solution)/shard_map/ppermute | solution.py:623
  67.8 87.9 %collective-permute-start.10 = (bf16[512,1664]{1,0:T(8,128)(2,1)}, bf16[512,1664]{1,0:T(8,128)(2,1)}, u32[]{:S(2)}, u32[]{:S(2)}) collective-permute-start(bf16[512,1664]{1,0:T(8,128)(2,1)} %pad_maximum_fusion.7.refs_0_.refs_2_), channel_id=1, source_target_pairs={{0,16},{8,24},{16,0},{24,8},{1,17},{9,25},{17,1},{25,9},{2,18},{10... | collective-permute-start | bytes 5111816 | tf_op jit(solution)/shard_map/ppermute | solution.py:623
  71.2 48.6 %collective-permute-start.4 = (bf16[128,1536]{1,0:T(8,128)(2,1)S(1)}, bf16[128,1536]{1,0:T(8,128)(2,1)S(1)}, u32[]{:S(2)}, u32[]{:S(2)}) collective-permute-start(bf16[128,1536]{1,0:T(8,128)(2,1)S(1)} %copy-done.55), channel_id=1, source_target_pairs={{0,2},{1,3},{2,0},{3,1},{4,6},{5,7},{6,4},{7,5},{8,10},{9,11},{10,... | collective-permute-start | bytes 1179656 | tf_op jit(solution)/shard_map/ppermute | solution.py:628
  71.4 50.2 %collective-permute-start.5 = (bf16[128,1536]{1,0:T(8,128)(2,1)S(1)}, bf16[128,1536]{1,0:T(8,128)(2,1)S(1)}, u32[]{:S(2)}, u32[]{:S(2)}) collective-permute-start(bf16[128,1536]{1,0:T(8,128)(2,1)S(1)} %copy-done.55), channel_id=1, source_target_pairs={{0,3},{1,0},{2,1},{3,2},{4,7},{5,4},{6,5},{7,6},{8,11},{9,8},{10,9... | collective-permute-start | bytes 1179656 | tf_op jit(solution)/shard_map/ppermute | solution.py:628
  123.1 39.5 %collective-permute-start.6 = (bf16[128,1024]{1,0:T(8,128)(2,1)S(1)}, bf16[128,1024]{1,0:T(8,128)(2,1)S(1)}, u32[]{:S(2)}, u32[]{:S(2)}) collective-permute-start(bf16[128,1024]{1,0:T(8,128)(2,1)S(1)} %bitcast.202), channel_id=1, source_target_pairs={{0,1},{1,2},{2,3},{3,0},{4,5},{5,6},{6,7},{7,4},{8,9},{9,10},{10,1... | collective-permute-start | bytes 786440 | tf_op jit(solution)/shard_map/ppermute | solution.py:628
  149.6 29.3 %collective-permute-start.7 = (bf16[128,1024]{1,0:T(8,128)(2,1)S(1)}, bf16[128,1024]{1,0:T(8,128)(2,1)S(1)}, u32[]{:S(2)}, u32[]{:S(2)}) collective-permute-start(bf16[128,1024]{1,0:T(8,128)(2,1)S(1)} %bitcast.203), channel_id=1, source_target_pairs={{0,2},{1,3},{2,0},{3,1},{4,6},{5,7},{6,4},{7,5},{8,10},{9,11},{10,... | collective-permute-start | bytes 786440 | tf_op jit(solution)/shard_map/ppermute | solution.py:628
  150.5 32.9 %collective-permute-start.8 = (bf16[128,1024]{1,0:T(8,128)(2,1)S(1)}, bf16[128,1024]{1,0:T(8,128)(2,1)S(1)}, u32[]{:S(2)}, u32[]{:S(2)}) collective-permute-start(bf16[128,1024]{1,0:T(8,128)(2,1)S(1)} %bitcast.204), channel_id=1, source_target_pairs={{0,3},{1,0},{2,1},{3,2},{4,7},{5,4},{6,5},{7,6},{8,11},{9,8},{10,9... | collective-permute-start | bytes 786440 | tf_op jit(solution)/shard_map/ppermute | solution.py:628
  154.1 31.9 %collective-permute-start.11 = (bf16[256,1664]{1,0:T(8,128)(2,1)S(1)}, bf16[256,1664]{1,0:T(8,128)(2,1)S(1)}, u32[]{:S(2)}, u32[]{:S(2)}) collective-permute-start(bf16[256,1664]{1,0:T(8,128)(2,1)S(1)} %slice.637), channel_id=1, source_target_pairs={{0,16},{8,24},{16,0},{24,8},{1,17},{9,25},{17,1},{25,9},{2,18},{10... | collective-permute-start | bytes 2555912 | tf_op jit(solution)/shard_map/ppermute | solution.py:623
  156.9 29.1 %collective-permute-start.12 = (bf16[256,1664]{1,0:T(8,128)(2,1)S(1)}, bf16[256,1664]{1,0:T(8,128)(2,1)}, u32[]{:S(2)}, u32[]{:S(2)}) collective-permute-start(bf16[256,1664]{1,0:T(8,128)(2,1)S(1)} %slice.638), channel_id=1, source_target_pairs={{0,8},{8,0},{16,24},{24,16},{1,9},{9,1},{17,25},{25,17},{2,10},{10... | collective-permute-start | bytes 2555912 | tf_op jit(solution)/shard_map/ppermute | solution.py:623
  186.0 81.9 %collective-permute-start.17 = (bf16[512,1536]{1,0:T(8,128)(2,1)}, bf16[512,1536]{1,0:T(8,128)(2,1)}, u32[]{:S(2)}, u32[]{:S(2)}) collective-permute-start(bf16[512,1536]{1,0:T(8,128)(2,1)} %pad_maximum_fusion.8.refs_0_.refs_7_), channel_id=1, source_target_pairs={{0,8},{8,0},{16,24},{24,16},{1,9},{9,1},{17,25},{25,17},{2,10},{10... | collective-permute-start | bytes 4718600 | tf_op jit(solution)/shard_map/ppermute | solution.py:623
  187.6 81.6 %collective-permute-start.18 = (bf16[512,1536]{1,0:T(8,128)(2,1)}, bf16[512,1536]{1,0:T(8,128)(2,1)}, u32[]{:S(2)}, u32[]{:S(2)}) collective-permute-start(bf16[512,1536]{1,0:T(8,128)(2,1)} %pad_maximum_fusion.8.refs_0_.refs_7_), channel_id=1, source_target_pairs={{0,16},{8,24},{16,0},{24,8},{1,17},{9,25},{17,1},{25,9},{2,18},{10... | collective-permute-start | bytes 4718600 | tf_op jit(solution)/shard_map/ppermute | solution.py:623
  194.4 26.5 %collective-permute-start.13 = (f32[2,8,1536]{2,1,0:T(8,128)S(1)}, f32[2,8,1536]{2,1,0:T(8,128)S(1)}, u32[]{:S(2)}, u32[]{:S(2)}) collective-permute-start(f32[2,8,1536]{2,1,0:T(8,128)S(1)} %slice_bitcast_fusion.4), channel_id=1, source_target_pairs={{0,8},{8,16},{16,24},{1,9},{9,17},{17,25},{2,10},{10,18},{18,26},{... | collective-permute-start | bytes 294920 | tf_op jit(solution)/shard_map/ppermute | solution.py:634
  249.0 61.6 %collective-permute-start.21 = (bf16[512,2048]{1,0:T(8,128)(2,1)S(1)}, bf16[512,2048]{1,0:T(8,128)(2,1)}, u32[]{:S(2)}, u32[]{:S(2)}) collective-permute-start(bf16[512,2048]{1,0:T(8,128)(2,1)S(1)} %bitcast.163), channel_id=1, source_target_pairs={{0,8},{8,0},{16,24},{24,16},{1,9},{9,1},{17,25},{25,17},{2,10},{10... | collective-permute-start | bytes 6291464 | tf_op jit(solution)/shard_map/ppermute | solution.py:623
  251.6 61.3 %collective-permute-start.22 = (bf16[512,2048]{1,0:T(8,128)(2,1)S(1)}, bf16[512,2048]{1,0:T(8,128)(2,1)}, u32[]{:S(2)}, u32[]{:S(2)}) collective-permute-start(bf16[512,2048]{1,0:T(8,128)(2,1)S(1)} %bitcast.164), channel_id=1, source_target_pairs={{0,16},{8,24},{16,0},{24,8},{1,17},{9,25},{17,1},{25,9},{2,18},{10... | collective-permute-start | bytes 6291464 | tf_op jit(solution)/shard_map/ppermute | solution.py:623
  255.4 48.0 %collective-permute-start.14 = (bf16[2,4,128,128]{3,2,1,0:T(8,128)(2,1)}, bf16[2,4,128,128]{3,2,1,0:T(8,128)(2,1)}, u32[]{:S(2)}, u32[]{:S(2)}) collective-permute-start(bf16[2,4,128,128]{3,2,1,0:T(8,128)(2,1)} %get-tuple-element.345), channel_id=1, source_target_pairs={{0,8},{8,16},{16,24},{1,9},{9,17},{17,25},{2,10},{10,18},{18,26},{... | collective-permute-start | bytes 786440 | tf_op jit(solution)/shard_map/ppermute | solution.py:634
  267.8 662.0 %reduce-scatter.3.cloned.1.call-start = ((), (), s32[]{:S(2)}) async-start(), calls=%async_computation.6 | async-start | bytes 11141120 | tf_op jit(solution)/shard_map/reduce_scatter | solution.py:994
  270.4 57.2 %collective-permute-start.19 = (bf16[256,1536]{1,0:T(8,128)(2,1)S(1)}, bf16[256,1536]{1,0:T(8,128)(2,1)}, u32[]{:S(2)}, u32[]{:S(2)}) collective-permute-start(bf16[256,1536]{1,0:T(8,128)(2,1)S(1)} %slice.655), channel_id=1, source_target_pairs={{0,16},{8,24},{16,0},{24,8},{1,17},{9,25},{17,1},{25,9},{2,18},{10... | collective-permute-start | bytes 2359304 | tf_op jit(solution)/shard_map/ppermute | solution.py:623
  270.4 58.4 %collective-permute-start.20 = (bf16[256,1536]{1,0:T(8,128)(2,1)S(1)}, bf16[256,1536]{1,0:T(8,128)(2,1)}, u32[]{:S(2)}, u32[]{:S(2)}) collective-permute-start(bf16[256,1536]{1,0:T(8,128)(2,1)S(1)} %slice.656), channel_id=1, source_target_pairs={{0,8},{8,0},{16,24},{24,16},{1,9},{9,1},{17,25},{25,17},{2,10},{10... | collective-permute-start | bytes 2359304 | tf_op jit(solution)/shard_map/ppermute | solution.py:623
  310.6 125.9 %collective-permute-start.29 = (bf16[512,2048]{1,0:T(8,128)(2,1)S(1)}, bf16[512,2048]{1,0:T(8,128)(2,1)}, u32[]{:S(2)}, u32[]{:S(2)}) collective-permute-start(bf16[512,2048]{1,0:T(8,128)(2,1)S(1)} %bitcast.165), channel_id=1, source_target_pairs={{0,4},{4,0},{1,5},{5,1},{2,6},{6,2},{3,7},{7,3},{8,12},{12,8},{9,1... | collective-permute-start | bytes 6291464 | tf_op jit(solution)/shard_map/ppermute | solution.py:623
  312.9 71.8 %collective-permute-start.24 = (bf16[256,2048]{1,0:T(8,128)(2,1)}, bf16[256,2048]{1,0:T(8,128)(2,1)}, u32[]{:S(2)}, u32[]{:S(2)}) collective-permute-start(bf16[256,2048]{1,0:T(8,128)(2,1)} %slice.671), channel_id=1, source_target_pairs={{0,16},{8,24},{16,0},{24,8},{1,17},{9,25},{17,1},{25,9},{2,18},{10... | collective-permute-start | bytes 3145736 | tf_op jit(solution)/shard_map/ppermute | solution.py:623
  322.6 62.2 %collective-permute-start.25 = (bf16[256,2048]{1,0:T(8,128)(2,1)}, bf16[256,2048]{1,0:T(8,128)(2,1)}, u32[]{:S(2)}, u32[]{:S(2)}) collective-permute-start(bf16[256,2048]{1,0:T(8,128)(2,1)} %slice.672), channel_id=1, source_target_pairs={{0,8},{8,0},{16,24},{24,16},{1,9},{9,1},{17,25},{25,17},{2,10},{10... | collective-permute-start | bytes 3145736 | tf_op jit(solution)/shard_map/ppermute | solution.py:623
  327.6 66.4 %collective-permute-start.16 = (bf16[2,4,128,128]{3,2,1,0:T(8,128)(2,1)}, bf16[2,4,128,128]{3,2,1,0:T(8,128)(2,1)S(1)}, u32[]{:S(2)}, u32[]{:S(2)}) collective-permute-start(bf16[2,4,128,128]{3,2,1,0:T(8,128)(2,1)} %fusion.23), channel_id=1, source_target_pairs={{0,8},{8,16},{16,24},{1,9},{9,17},{17,25},{2,10},{10,18},{18,26},{... | collective-permute-start | bytes 786440 | tf_op jit(solution)/shard_map/ppermute | solution.py:634
  353.7 40.9 %collective-permute-start.33 = (bf16[512,1024]{1,0:T(8,128)(2,1)}, bf16[512,1024]{1,0:T(8,128)(2,1)}, u32[]{:S(2)}, u32[]{:S(2)}) collective-permute-start(bf16[512,1024]{1,0:T(8,128)(2,1)} %pad_maximum_fusion.9.refs_1_.refs_0_), channel_id=1, source_target_pairs={{0,8},{8,0},{16,24},{24,16},{1,9},{9,1},{17,25},{25,17},{2,10},{10... | collective-permute-start | bytes 3145736 | tf_op jit(solution)/shard_map/ppermute | solution.py:623
  384.7 74.1 %collective-permute-start.30 = (bf16[512,2048]{1,0:T(8,128)(2,1)}, bf16[512,2048]{1,0:T(8,128)(2,1)}, u32[]{:S(2)}, u32[]{:S(2)}) collective-permute-start(bf16[512,2048]{1,0:T(8,128)(2,1)} %collective-permute-done.21.mine_grads.refs_18_), channel_id=1, source_target_pairs={{0,4},{4,0},{1,5},{5,1},{2,6},{6,2},{3,7},{7,3},{8,12},{12,8},{9,1... | collective-permute-start | bytes 6291464 | tf_op jit(solution)/shard_map/ppermute | solution.py:623
  393.7 65.1 %collective-permute-start.31 = (bf16[512,2048]{1,0:T(8,128)(2,1)}, bf16[512,2048]{1,0:T(8,128)(2,1)}, u32[]{:S(2)}, u32[]{:S(2)}) collective-permute-start(bf16[512,2048]{1,0:T(8,128)(2,1)} %collective-permute-done.22.mine_grads.refs_20_), channel_id=1, source_target_pairs={{0,4},{4,0},{1,5},{5,1},{2,6},{6,2},{3,7},{7,3},{8,12},{12,8},{9,1... | collective-permute-start | bytes 6291464 | tf_op jit(solution)/shard_map/ppermute | solution.py:623
  394.0 64.9 %collective-permute-start.32 = (bf16[512,2048]{1,0:T(8,128)(2,1)}, bf16[512,2048]{1,0:T(8,128)(2,1)}, u32[]{:S(2)}, u32[]{:S(2)}) collective-permute-start(bf16[512,2048]{1,0:T(8,128)(2,1)} %constant_dynamic-update-slice_fusion.49.mine_grads.refs_22_), channel_id=1, source_target_pairs={{0,4},{4,0},{1,5},{5,1},{2,6},{6,2},{3,7},{7,3},{8,12},{12,8},{9,1... | collective-permute-start | bytes 6291464 | tf_op jit(solution)/shard_map/ppermute | solution.py:623
  404.9 28.0 %collective-permute-start.34 = (bf16[512,1024]{1,0:T(8,128)(2,1)}, bf16[512,1024]{1,0:T(8,128)(2,1)S(1)}, u32[]{:S(2)}, u32[]{:S(2)}) collective-permute-start(bf16[512,1024]{1,0:T(8,128)(2,1)} %pad_maximum_fusion.9.refs_1_.refs_0_), channel_id=1, source_target_pairs={{0,16},{8,24},{16,0},{24,8},{1,17},{9,25},{17,1},{25,9},{2,18},{10... | collective-permute-start | bytes 3145736 | tf_op jit(solution)/shard_map/ppermute | solution.py:623
  482.2 25.1 %collective-permute-start.38 = (bf16[512,2048]{1,0:T(8,128)(2,1)S(1)}, bf16[512,2048]{1,0:T(8,128)(2,1)}, u32[]{:S(2)}, u32[]{:S(2)}) collective-permute-start(bf16[512,2048]{1,0:T(8,128)(2,1)S(1)} %get-tuple-element.306.mine.refs_8_), channel_id=1, source_target_pairs={{0,4},{4,0},{1,5},{5,1},{2,6},{6,2},{3,7},{7,3},{8,12},{12,8},{9,1... | collective-permute-start | bytes 6291464 | tf_op jit(solution)/shard_map/ppermute | solution.py:623
  482.4 54.6 %collective-permute-start.40 = (bf16[512,2048]{1,0:T(8,128)(2,1)S(1)}, bf16[512,2048]{1,0:T(8,128)(2,1)}, u32[]{:S(2)}, u32[]{:S(2)}) collective-permute-start(bf16[512,2048]{1,0:T(8,128)(2,1)S(1)} %get-tuple-element.306.mine.refs_8_), channel_id=1, source_target_pairs={{0,8},{8,0},{16,24},{24,16},{1,9},{9,1},{17,25},{25,17},{2,10},{10... | collective-permute-start | bytes 6291464 | tf_op jit(solution)/shard_map/ppermute | solution.py:623
  503.5 49.8 %collective-permute-start.44 = (bf16[512,2048]{1,0:T(8,128)(2,1)S(1)}, bf16[512,2048]{1,0:T(8,128)(2,1)}, u32[]{:S(2)}, u32[]{:S(2)}) collective-permute-start(bf16[512,2048]{1,0:T(8,128)(2,1)S(1)} %get-tuple-element.306.mine.refs_8_), channel_id=1, source_target_pairs={{0,16},{8,24},{16,0},{24,8},{1,17},{9,25},{17,1},{25,9},{2,18},{10... | collective-permute-start | bytes 6291464 | tf_op jit(solution)/shard_map/ppermute | solution.py:623
  553.3 35.4 %collective-permute-start.47 = (bf16[512,2048]{1,0:T(8,128)(2,1)}, bf16[512,2048]{1,0:T(8,128)(2,1)}, u32[]{:S(2)}, u32[]{:S(2)}) collective-permute-start(bf16[512,2048]{1,0:T(8,128)(2,1)} %collective-permute-done.44.mine.refs_12_), channel_id=1, source_target_pairs={{0,4},{4,0},{1,5},{5,1},{2,6},{6,2},{3,7},{7,3},{8,12},{12,8},{9,1... | collective-permute-start | bytes 6291464 | tf_op jit(solution)/shard_map/ppermute | solution.py:623
  556.9 31.8 %collective-permute-start.45 = (bf16[256,2048]{1,0:T(8,128)(2,1)}, bf16[256,2048]{1,0:T(8,128)(2,1)S(1)}, u32[]{:S(2)}, u32[]{:S(2)}) collective-permute-start(bf16[256,2048]{1,0:T(8,128)(2,1)} %slice.676), channel_id=1, source_target_pairs={{0,16},{8,24},{16,0},{24,8},{1,17},{9,25},{17,1},{25,9},{2,18},{10... | collective-permute-start | bytes 3145736 | tf_op jit(solution)/shard_map/ppermute | solution.py:623
  558.7 30.0 %collective-permute-start.46 = (bf16[256,2048]{1,0:T(8,128)(2,1)S(1)}, bf16[256,2048]{1,0:T(8,128)(2,1)S(1)}, u32[]{:S(2)}, u32[]{:S(2)}) collective-permute-start(bf16[256,2048]{1,0:T(8,128)(2,1)S(1)} %slice.677), channel_id=1, source_target_pairs={{0,8},{8,0},{16,24},{24,16},{1,9},{9,1},{17,25},{25,17},{2,10},{10... | collective-permute-start | bytes 3145736 | tf_op jit(solution)/shard_map/ppermute | solution.py:623
  624.9 47.9 %collective-permute-start.49 = (bf16[512,2048]{1,0:T(8,128)(2,1)}, bf16[512,2048]{1,0:T(8,128)(2,1)S(1)}, u32[]{:S(2)}, u32[]{:S(2)}) collective-permute-start(bf16[512,2048]{1,0:T(8,128)(2,1)} %add_convert_fusion.5), channel_id=1, source_target_pairs={{0,16},{8,24},{16,0},{24,8},{1,17},{9,25},{17,1},{25,9},{2,18},{10... | collective-permute-start | bytes 6291464 | tf_op jit(solution)/shard_map/ppermute | solution.py:623
  630.9 48.0 %collective-permute-start.43 = (bf16[512,2048]{1,0:T(8,128)(2,1)}, bf16[512,2048]{1,0:T(8,128)(2,1)}, u32[]{:S(2)}, u32[]{:S(2)}) collective-permute-start(bf16[512,2048]{1,0:T(8,128)(2,1)} %add_convert_fusion.6), channel_id=1, source_target_pairs={{0,8},{8,0},{16,24},{24,16},{1,9},{9,1},{17,25},{25,17},{2,10},{10... | collective-permute-start | bytes 6291464 | tf_op jit(solution)/shard_map/ppermute | solution.py:623
  686.9 49.0 %collective-permute-start.52 = (bf16[512,2048]{1,0:T(8,128)(2,1)}, bf16[512,2048]{1,0:T(8,128)(2,1)}, u32[]{:S(2)}, u32[]{:S(2)}) collective-permute-start(bf16[512,2048]{1,0:T(8,128)(2,1)} %add_convert_fusion.4), channel_id=1, source_target_pairs={{0,24},{8,16},{16,8},{24,0},{1,25},{9,17},{17,9},{25,1},{2,26},{10... | collective-permute-start | bytes 6291464 | tf_op jit(solution)/shard_map/ppermute | solution.py:623
  747.7 430.9 %reduce-scatter.5.cloned.1.call-start = ((), (), s32[]{:S(2)}) async-start(), calls=%async_computation.7 | async-start | bytes 4456448 | tf_op jit(solution)/shard_map/reduce_scatter | solution.py:997
  768.8 48.0 %collective-permute-start.58 = (bf16[512,2048]{1,0:T(8,128)(2,1)}, bf16[512,2048]{1,0:T(8,128)(2,1)}, u32[]{:S(2)}, u32[]{:S(2)}) collective-permute-start(bf16[512,2048]{1,0:T(8,128)(2,1)} %add_convert_fusion.2), channel_id=1, source_target_pairs={{0,16},{8,24},{16,0},{24,8},{1,17},{9,25},{17,1},{25,9},{2,18},{10... | collective-permute-start | bytes 6291464 | tf_op jit(solution)/shard_map/ppermute | solution.py:623
  772.7 47.7 %collective-permute-start.56 = (bf16[512,2048]{1,0:T(8,128)(2,1)}, bf16[512,2048]{1,0:T(8,128)(2,1)}, u32[]{:S(2)}, u32[]{:S(2)}) collective-permute-start(bf16[512,2048]{1,0:T(8,128)(2,1)} %add_convert_fusion.3), channel_id=1, source_target_pairs={{0,8},{8,0},{16,24},{24,16},{1,9},{9,1},{17,25},{25,17},{2,10},{10... | collective-permute-start | bytes 6291464 | tf_op jit(solution)/shard_map/ppermute | solution.py:623
  778.7 75.8 %collective-permute-start.59 = (bf16[512,2048]{1,0:T(8,128)(2,1)}, bf16[512,2048]{1,0:T(8,128)(2,1)}, u32[]{:S(2)}, u32[]{:S(2)}) collective-permute-start(bf16[512,2048]{1,0:T(8,128)(2,1)} %get-tuple-element.172), channel_id=1, source_target_pairs={{0,4},{4,0},{1,5},{5,1},{2,6},{6,2},{3,7},{7,3},{8,12},{12,8},{9,1... | collective-permute-start | bytes 6291464 | tf_op jit(solution)/shard_map/ppermute | solution.py:623
  866.8 48.1 %collective-permute-start.63 = (bf16[512,2048]{1,0:T(8,128)(2,1)}, bf16[512,2048]{1,0:T(8,128)(2,1)}, u32[]{:S(2)}, u32[]{:S(2)}) collective-permute-start(bf16[512,2048]{1,0:T(8,128)(2,1)} %add_convert_fusion.1), channel_id=1, source_target_pairs={{0,24},{8,16},{16,8},{24,0},{1,25},{9,17},{17,9},{25,1},{2,26},{10... | collective-permute-start | bytes 6291464 | tf_op jit(solution)/shard_map/ppermute | solution.py:623
  919.9 93.9 %collective-permute-start.82 = (bf16[512,1536]{1,0:T(8,128)(2,1)}, bf16[512,1536]{1,0:T(8,128)(2,1)}, u32[]{:S(2)}, u32[]{:S(2)}) collective-permute-start(bf16[512,1536]{1,0:T(8,128)(2,1)} %convolution_convert_fusion.3), channel_id=1, source_target_pairs={{0,16},{8,24},{16,0},{24,8},{1,17},{9,25},{17,1},{25,9},{2,18},{10... | collective-permute-start | bytes 4718600 | tf_op jit(solution)/shard_map/ppermute | solution.py:623
  927.8 86.0 %collective-permute-start.81 = (bf16[512,1536]{1,0:T(8,128)(2,1)}, bf16[512,1536]{1,0:T(8,128)(2,1)}, u32[]{:S(2)}, u32[]{:S(2)}) collective-permute-start(bf16[512,1536]{1,0:T(8,128)(2,1)} %convolution_convert_fusion.4), channel_id=1, source_target_pairs={{0,8},{8,0},{16,24},{24,16},{1,9},{9,1},{17,25},{25,17},{2,10},{10... | collective-permute-start | bytes 4718600 | tf_op jit(solution)/shard_map/ppermute | solution.py:623
  1013.8 80.1 %collective-permute-start.67 = (bf16[2,256,2048]{2,1,0:T(8,128)(2,1)}, bf16[2,256,2048]{2,1,0:T(8,128)(2,1)}, u32[]{:S(2)}, u32[]{:S(2)}) collective-permute-start(bf16[2,256,2048]{2,1,0:T(8,128)(2,1)} %constant_dynamic-slice_fusion.11), channel_id=1, source_target_pairs={{0,4},{4,0},{1,5},{5,1},{2,6},{6,2},{3,7},{7,3},{8,12},{12,8},{9,1... | collective-permute-start | bytes 6291464 | tf_op jit(solution)/shard_map/ppermute | solution.py:623
  1017.5 26.6 %collective-permute-start.84 = (bf16[256,1536]{1,0:T(8,128)(2,1)S(1)}, bf16[256,1536]{1,0:T(8,128)(2,1)}, u32[]{:S(2)}, u32[]{:S(2)}) collective-permute-start(bf16[256,1536]{1,0:T(8,128)(2,1)S(1)} %fusion.15), channel_id=1, source_target_pairs={{0,16},{8,24},{16,0},{24,8},{1,17},{9,25},{17,1},{25,9},{2,18},{10... | collective-permute-start | bytes 2359304 | tf_op jit(solution)/shard_map/ppermute | solution.py:623
  1021.3 24.3 %collective-permute-start.83 = (bf16[256,1536]{1,0:T(8,128)(2,1)}, bf16[256,1536]{1,0:T(8,128)(2,1)}, u32[]{:S(2)}, u32[]{:S(2)}) collective-permute-start(bf16[256,1536]{1,0:T(8,128)(2,1)} %fusion.14), channel_id=1, source_target_pairs={{0,8},{8,0},{16,24},{24,16},{1,9},{9,1},{17,25},{25,17},{2,10},{10... | collective-permute-start | bytes 2359304 | tf_op jit(solution)/shard_map/ppermute | solution.py:623
  1027.0 89.1 %collective-permute-start.76 = (bf16[512,1664]{1,0:T(8,128)(2,1)}, bf16[512,1664]{1,0:T(8,128)(2,1)}, u32[]{:S(2)}, u32[]{:S(2)}) collective-permute-start(bf16[512,1664]{1,0:T(8,128)(2,1)} %convolution_convert_fusion.2), channel_id=1, source_target_pairs={{0,8},{8,0},{16,24},{24,16},{1,9},{9,1},{17,25},{25,17},{2,10},{10... | collective-permute-start | bytes 5111816 | tf_op jit(solution)/shard_map/ppermute | solution.py:623
  1027.5 96.1 %collective-permute-start.74 = (bf16[512,1664]{1,0:T(8,128)(2,1)}, bf16[512,1664]{1,0:T(8,128)(2,1)}, u32[]{:S(2)}, u32[]{:S(2)}) collective-permute-start(bf16[512,1664]{1,0:T(8,128)(2,1)} %convolution_convert_fusion.1), channel_id=1, source_target_pairs={{0,16},{8,24},{16,0},{24,8},{1,17},{9,25},{17,1},{25,9},{2,18},{10... | collective-permute-start | bytes 5111816 | tf_op jit(solution)/shard_map/ppermute | solution.py:623
  1050.9 49.4 %collective-permute-start.85 = (bf16[128,1536]{0,1:T(8,128)(2,1)}, bf16[128,1536]{0,1:T(8,128)(2,1)}, u32[]{:S(2)}, u32[]{:S(2)}) collective-permute-start(bf16[128,1536]{0,1:T(8,128)(2,1)} %bitcast.212), channel_id=1, source_target_pairs={{0,1},{1,2},{2,3},{3,0},{4,5},{5,6},{6,7},{7,4},{8,9},{9,10},{10,1... | collective-permute-start | bytes 1179656 | tf_op jit(solution)/shard_map/ppermute | solution.py:628
  1064.7 49.2 %collective-permute-start.86 = (bf16[128,1536]{0,1:T(8,128)(2,1)}, bf16[128,1536]{0,1:T(8,128)(2,1)}, u32[]{:S(2)}, u32[]{:S(2)}) collective-permute-start(bf16[128,1536]{0,1:T(8,128)(2,1)} %bitcast.142), channel_id=1, source_target_pairs={{0,2},{1,3},{2,0},{3,1},{4,6},{5,7},{6,4},{7,5},{8,10},{9,11},{10,... | collective-permute-start | bytes 1179656 | tf_op jit(solution)/shard_map/ppermute | solution.py:628
  1100.2 56.7 %collective-permute-start.54 = (bf16[512,2048]{1,0:T(8,128)(2,1)S(1)}, bf16[512,2048]{1,0:T(8,128)(2,1)}, u32[]{:S(2)}, u32[]{:S(2)}) collective-permute-start(bf16[512,2048]{1,0:T(8,128)(2,1)S(1)} %copy-done.82), channel_id=1, source_target_pairs={{0,4},{4,0},{1,5},{5,1},{2,6},{6,2},{3,7},{7,3},{8,12},{12,8},{9,1... | collective-permute-start | bytes 6291464 | tf_op jit(solution)/shard_map/ppermute | solution.py:623
  1122.2 46.6 %collective-permute-start.77 = (bf16[256,1664]{1,0:T(8,128)(2,1)}, bf16[256,1664]{1,0:T(8,128)(2,1)S(1)}, u32[]{:S(2)}, u32[]{:S(2)}) collective-permute-start(bf16[256,1664]{1,0:T(8,128)(2,1)} %fusion.17), channel_id=1, source_target_pairs={{0,16},{8,24},{16,0},{24,8},{1,17},{9,25},{17,1},{25,9},{2,18},{10... | collective-permute-start | bytes 2555912 | tf_op jit(solution)/shard_map/ppermute | solution.py:623
  1130.8 38.0 %collective-permute-start.75 = (bf16[256,1664]{1,0:T(8,128)(2,1)}, bf16[256,1664]{1,0:T(8,128)(2,1)}, u32[]{:S(2)}, u32[]{:S(2)}) collective-permute-start(bf16[256,1664]{1,0:T(8,128)(2,1)} %fusion.18), channel_id=1, source_target_pairs={{0,8},{8,0},{16,24},{24,16},{1,9},{9,1},{17,25},{25,17},{2,10},{10... | collective-permute-start | bytes 2555912 | tf_op jit(solution)/shard_map/ppermute | solution.py:623
  1165.9 64.0 %collective-permute-start.64 = (bf16[2,256,2048]{2,1,0:T(8,128)(2,1)}, bf16[2,256,2048]{2,1,0:T(8,128)(2,1)}, u32[]{:S(2)}, u32[]{:S(2)}) collective-permute-start(bf16[2,256,2048]{2,1,0:T(8,128)(2,1)} %bitcast.30), channel_id=1, source_target_pairs={{0,4},{4,0},{1,5},{5,1},{2,6},{6,2},{3,7},{7,3},{8,12},{12,8},{9,1... | collective-permute-start | bytes 6291464 | tf_op jit(solution)/shard_map/ppermute | solution.py:623
  1165.9 64.0 %collective-permute-start.68 = (bf16[2,256,2048]{2,1,0:T(8,128)(2,1)}, bf16[2,256,2048]{2,1,0:T(8,128)(2,1)}, u32[]{:S(2)}, u32[]{:S(2)}) collective-permute-start(bf16[2,256,2048]{2,1,0:T(8,128)(2,1)} %bitcast.37), channel_id=1, source_target_pairs={{0,4},{4,0},{1,5},{5,1},{2,6},{6,2},{3,7},{7,3},{8,12},{12,8},{9,1... | collective-permute-start | bytes 6291464 | tf_op jit(solution)/shard_map/ppermute | solution.py:623
  1173.8 49.0 %all-to-all-start.1 = ((bf16[4,2112,128]{2,1,0:T(8,128)(2,1)}), bf16[4,2112,128]{2,1,0:T(8,128)(2,1)}, u32[]{:S(2)}, u32[]{:S(2)}) async-start(bf16[4,2112,128]{2,1,0:T(8,128)(2,1)} %copy.187), calls=%async_computation.3 | async-start | bytes 4325376 | tf_op jit(solution)/shard_map/all_to_all | solution.py:1047
  1188.3 29.3 %collective-permute-start.79 = (bf16[128,1664]{0,1:T(8,128)(2,1)}, bf16[128,1664]{0,1:T(8,128)(2,1)}, u32[]{:S(2)}, u32[]{:S(2)}) collective-permute-start(bf16[128,1664]{0,1:T(8,128)(2,1)} %bitcast.209), channel_id=1, source_target_pairs={{0,2},{1,3},{2,0},{3,1},{4,6},{5,7},{6,4},{7,5},{8,10},{9,11},{10,... | collective-permute-start | bytes 1277960 | tf_op jit(solution)/shard_map/ppermute | solution.py:628
  1193.1 24.4 %collective-permute-start.80 = (bf16[128,1664]{0,1:T(8,128)(2,1)}, bf16[128,1664]{0,1:T(8,128)(2,1)}, u32[]{:S(2)}, u32[]{:S(2)}) collective-permute-start(bf16[128,1664]{0,1:T(8,128)(2,1)} %bitcast.210), channel_id=1, source_target_pairs={{0,3},{1,0},{2,1},{3,2},{4,7},{5,4},{6,5},{7,6},{8,11},{9,8},{10,9... | collective-permute-start | bytes 1277960 | tf_op jit(solution)/shard_map/ppermute | solution.py:628
  (118 other events, 1956.6 us)
Sparse Core Ops, SparseCore 0:
  57.9 159.7 all-gather.4
  268.0 76.2 all-gather.2
  747.8 172.4 reduce-scatter.2
  922.5 111.7 reduce-scatter.4

commit v6 on v5

--- a/solution.py
+++ b/solution.py
@@ -600,18 +600,23 @@
     )(jnp.reshape(place, (1,)).astype(jnp.int32), *factors, *flat)
 
 
-def join_kernel(source, target):
-    target[...] = source[0]
+def join_kernel(squares, source, target):
+    lines, _, columns = source.shape
+    part = columns // squares
+    for i in range(lines):
+        for j in range(squares):
+            at = (j * lines + i) * part
+            target[:, at : at + part] = source[i, :, j * part : (j + 1) * part]
 
 
 def columns_join(parts, squares):
     lines, rows, columns = parts.shape
-    part = columns // squares
+    tile = 176 if rows % 176 == 0 else rows
     return pl.pallas_call(
-        join_kernel,
-        grid=(lines, squares),
-        in_specs=[pl.BlockSpec((1, rows, part), lambda i, j: (i, 0, j))],
-        out_specs=pl.BlockSpec((rows, part), lambda i, j: (0, j * lines + i)),
+        functools.partial(join_kernel, squares),
+        grid=(rows // tile,),
+        in_specs=[pl.BlockSpec((lines, tile, columns), lambda i: (0, i, 0))],
+        out_specs=pl.BlockSpec((tile, lines * columns), lambda i: (i, 0)),
         out_shape=jax.ShapeDtypeStruct((rows, lines * columns), parts.dtype),
         compiler_params=pltpu.CompilerParams(vmem_limit_bytes=VMEM_BYTES),
         cost_estimate=pl.CostEstimate(flops=0, bytes_accessed=4 * parts.size, transcendentals=0),
@@ -700,12 +705,15 @@
     return [lax.dynamic_slice_in_dim(rows, (place ^ bit) * width, width, 1) for bit in range(4)]
 
 
-def line_sum(own):
+def line_sum(own, *late):
     count, place = own.shape[0], lax.axis_index("fsdp")
     total = lax.dynamic_index_in_dim(own, place, 0, keepdims=False)
+    arrived = []
     for distance in range(1, count):
         piece = lax.dynamic_index_in_dim(own, (place + distance) % count, 0, keepdims=False)
-        total = total + wide(shift(low(piece), "fsdp", distance))
+        arrived.append(shift(low(piece), "fsdp", distance))
+    for part in lax.optimization_barrier(tuple(arrived) + late)[: len(arrived)]:
+        total = total + wide(part)
     return total
 
 
@@ -728,20 +736,25 @@
         if earlier:
             first = lax.optimization_barrier(first + earlier)[:2]
         beside, across = (wide(part) for part in first)
-        beside_upper = flip(low(outer_rows(self.side(1, 0), self.grads) + across[: self.half]), "ctx", 1)
-        across_lower = flip(low(outer_rows(self.side(2, 1), self.grads) + beside[: self.half]), "ctx", 2)
-        self.last = (beside_upper, across_lower)
+        upper = low(outer_rows(self.side(1, 0), self.grads) + across[: self.half])
+        lower = low(outer_rows(self.side(2, 1), self.grads) + beside[: self.half])
+        self.last = (flip(upper, "ctx", 1), flip(lower, "ctx", 2))
         self.kept = (beside, across)
-
-    def finish(self, *earlier):
-        beside_upper, across_lower = lax.optimization_barrier(self.last + earlier)[:2]
+        return upper, lower
+
+    def finish(self, last, *ties):
+        beside_upper, across_lower = self.last
+        if not last:
+            beside_upper, across_lower = lax.optimization_barrier(self.last + ties)[:2]
         beside, across = self.kept
         own = outer_rows(self.columns[0], self.grads)
         upper = own[: self.half] + wide(beside_upper) + across[self.half :]
         lower = own[self.half :] + beside[self.half :] + wide(across_lower)
         own = jnp.concatenate([upper, lower], axis=0)
         lines = lax.axis_size("fsdp")
-        return line_sum(own.reshape(lines, own.shape[0] // lines, own.shape[1]))
+        if not last:
+            return wide(lax.psum_scatter(low(own), "fsdp", scatter_dimension=0, tiled=True))
+        return line_sum(own.reshape(lines, own.shape[0] // lines, own.shape[1]), *ties)
 
 
 def butterfly(value, axes):
@@ -822,12 +835,14 @@
     ]
 
 
-def pass_states(own, transfer, forward):
+def pass_states(own, transfer, forward, *beside):
     rule = "shij,shjk->shik" if forward == 1 else "shji,shjk->shik"
     leaving = own
     entered = low(jnp.zeros_like(own))
     for repeat in range(lax.axis_size("ctx") - 1):
         entered = from_behind(low(leaving), "ctx", forward)
+        if repeat == 0 and beside:
+            entered = tie(entered, *beside)
         leaving = own + jnp.einsum(rule, transfer, entered, preferred_element_type=jnp.float32)
     return wide(entered)
 
@@ -874,8 +889,6 @@
     pieces = pieces.reshape(3, 4, units, shard_rows).transpose(1, 0, 2, 3)
     ffn_line = lax.all_to_all(pieces.reshape(4, 3 * units, shard_rows), "ctx", 0, 0)
     ffn_line = ffn_line.transpose(1, 0, 2).reshape(3 * units, 4 * shard_rows)
-    gate_up_parts = lax.all_gather(ffn_line[: 2 * units], "fsdp", axis=0)
-    down_parts = lax.all_gather(ffn_line[2 * units :], "fsdp", axis=0)
     line_count = lax.axis_size("fsdp")
 
     ctx_place = lax.axis_index("ctx")
@@ -892,11 +905,13 @@
     grads_mine = rows_mine(out_grad).reshape(-1, width)
 
     square = Square(tie(lines[0], ffn_line)).forward()
+    gate_up_parts = lax.all_gather(tie(ffn_line[: 2 * units], lines[parts - 1], *square.done()), "fsdp", axis=0)
+    down_parts = lax.all_gather(ffn_line[2 * units :], "fsdp", axis=0)
     mix_full, kept, pre = [], [], []
     for p in range(parts):
         mix_full.append(square.pieces())
         square = Square(tie(lines[p + 1], *square.done()))
-        rows = tie(normed_mix, lines[-1]) if p == 0 else normed_mix
+        rows = normed_mix
         ends = rows.reshape(seq_count, local_len, width)[:, local_len - HALO :].reshape(seq_count * HALO, width)
         ends = gathered_times(ends, ctx_place, mix_full[p])[:, :part_cols]
         halo = from_behind(ends.reshape(seq_count, HALO, part_cols), "ctx", 1)
@@ -913,9 +928,9 @@
                 )
             )
         )
-        square.forward(kept[p][2])
+        square.forward(kept[p][2], lines[-1])
         if p == 0:
-            grad_square = Square(tie(grads_mine, kept[p][2]))
+            grad_square = Square(tie(grads_mine, kept[p][2], square.beside, square.across))
         if p == parts - 1:
             grad_square.forward()
     out_full = square.pieces()
@@ -926,9 +941,10 @@
         first = final[..., :LANES]
         if len(entered) == parts - 1:
             first, gate_up_parts = lax.optimization_barrier((first, gate_up_parts) + grad_square.done())[:2]
+            gate_up_full = columns_join(gate_up_parts, 4)
         entered.append(pass_states(first, transfers[-1], 1))
         if len(entered) == parts:
-            carry, down_parts = lax.optimization_barrier((carry, down_parts))
+            carry = tie(carry, gate_up_full)
         mixed_rows.append(mixer_output(own, carry, entered[-1], gain_head, group))
     mixed_rows = jnp.concatenate(mixed_rows, axis=1)
     grad_rows = [
@@ -937,10 +953,11 @@
     mixed_rows = tie(mixed_rows, *(other for _, other in grad_rows))
 
     branch = gathered_times_transposed([mixed_rows], ctx_place, [out_full]).reshape(seq_count, local_len, width)
+    branch, down_parts = lax.optimization_barrier((branch, down_parts))
     residual = inputs_mine + rows_scatter(branch).reshape(-1, width)
     scale_ffn = rms_scale(residual, EPSILON)
     square = Square(low(residual * scale_ffn * gain_ffn))
-    ffn_full = (columns_join(gate_up_parts, 4), columns_join(down_parts, 4))
+    ffn_full = (gate_up_full, columns_join(down_parts, 4))
 
     ffn_rows = [both_sides(square.own)]
     ffn_out = [ffn_both(ffn_rows[0], grad_rows[0], *ffn_full)]
@@ -989,8 +1006,7 @@
         backs.append(back)
         acrosses.append(across)
         gain_o_part = gain_o_part + jnp.sum(gain_part, axis=(0, 1, 2))
-    acrosses[0] = tie(acrosses[0], *result_near)
-    grad_end = pass_states(jnp.concatenate(acrosses, axis=1), jnp.concatenate(transfers, axis=1), -1)
+    grad_end = pass_states(jnp.concatenate(acrosses, axis=1), jnp.concatenate(transfers, axis=1), -1, *result_near)
     total = lax.psum_scatter(sums, "fsdp", scatter_dimension=0, tiled=True)
 
     out_grad_w = low(outer_rows(grad_branch, mixed_rows))
@@ -1017,15 +1033,16 @@
         grad_mix = put(grad_mix.reshape(seq_count, local_len, -1), tail, 0, local_len - HALO, 0)
         grad_mix = grad_mix.reshape(row_count, -1)
         if scatter is not None:
-            scatter.second(grad_mix)
-            mix_grads[p + 1] = scatter.finish()
+            scatter.second(before)
+            earlier_scatter = scatter
         else:
             grad_mix = tie(grad_mix, result_far)
         if p == 0:
             grad_mix = jnp.concatenate([grad_mix, low(logits)], axis=1)
         grad_mixes[p] = grad_mix
         scatter = Scatter(columns, grad_mix)
-    grad_mixes[0] = tie(grad_mixes[0], *scatter.sent)
+    ready = scatter.second()
+    grad_mixes[0] = tie(grad_mixes[0], *ready)
     mix_back = gathered_times_transposed(grad_mixes, ctx_place, mix_full)
     mix_back = rows_scatter(mix_back.reshape(seq_count, local_len, width)).reshape(-1, width)
     back_mix, unit_mix = norm_backward(mix_back, inputs_mine, rms_scale(inputs_mine, EPSILON), gain_mix)
@@ -1035,9 +1052,12 @@
     conv_cols = jnp.concatenate([jnp.sum(part, axis=0)[:taps] for part in conv_parts], axis=1)
     gains = butterfly(jnp.concatenate([gain_mix_part, gain_ffn_part, gain_o_part]), ("tp",))
     sums = jnp.concatenate([gains, conv_cols.reshape(-1), jnp.sum(logits, axis=0)])
-    scatter.second()
+    for p in range(1, parts):
+        mix_grads[p] = earlier_scatter.finish(False, *ready)
     sums = butterfly(sums, ("ctx", "fsdp"))
-    mix_grads[0] = scatter.finish(sums)
+    mix_grads[0] = scatter.finish(True, sums)
+    query_grad, key_grad, value_grad = by_kind([grad[:, :part_cols] for grad in mix_grads])
+    beta_grad = mix_grads[0][:, part_cols : part_cols + heads_here]
     ends = [width, 2 * width, 2 * width + LANES, sums.shape[0] - LANES]
     gain_mix_grad, gain_ffn_grad, gain_o_grad, conv_grad, bias_grad = jnp.split(sums, ends)
     conv_grad = jnp.stack(by_kind([conv_grad.reshape(taps, -1)]))
@@ -1049,8 +1069,6 @@
     result = result_own + wide(result_near[0]) + wide(result_near[1])
     result = result + wide(result_far)
     block_output = rows_full(low(residual + result).reshape(seq_count, -1, width))
-    query_grad, key_grad, value_grad = by_kind([grad[:, :part_cols] for grad in mix_grads])
-    beta_grad = mix_grads[0][:, part_cols : part_cols + heads_here]
 
     return (
         block_output,

time: 1260 us -> 1200 us (0.952)
  starting transfers between devices: 198 us -> 152 us
    ppermute x60, waiting for transfers between devices: 126 us -> 198 us  [flip(): return lax.ppermute(value, axis, [(i, i ^ bit) for i in devices])]
    ppermute x15 -> x12, waiting for transfers between devices: 104 us -> 52.6 us  [shift(): lax.ppermute(value, axis, [(i, (i + distance) % count) for i in range(cou...]
    ppermute x15 -> x12, starting transfers between devices: 84.5 us -> 47.9 us  [shift(): lax.ppermute(value, axis, [(i, (i + distance) % count) for i in range(cou...]
    all_to_all x1, waiting for transfers between devices: 21.6 us -> 0.01 us  [local(): lax.all_to_all(pieces.reshape(4, 3 * units, shard_rows), 'ctx', 0, 0)]
    unnamed x234 -> x198, local copies, waits for them, and re-layouts: 30.6 us -> 19.8 us
  transfers between devices with their start and end apart: 94 -> 92, of which waited for: 37 -> 35; matrix products, arithmetic and copies ran while one was open for 19% -> 19% of each run, Pallas kernels for 29% -> 31%
where the time goes in v6:
time: 1200 us; the launch traced here: 1190 us
  Pallas kernels  394 us (33%)
  waiting for transfers between devices  353 us (29%)
  starting transfers between devices  152 us (13%)
  other arithmetic  128 us (11%)
  local copies, waits for them, and re-layouts  95.8 us (8%)
  matrix products  54.7 us (5%)
  between operations  15.4 us (1%)
    ppermute x60, waiting for transfers between devices, flip(): return lax.ppermute(value, axis, [(i, i ^ bit) for i in devices])  198 us
    pallas_call x4, Pallas kernels, ffn_both(): pl.pallas_call(ffn_kernel, grid=(count // tile,), in_specs=[wide_rows] *...  118 us
    ppermute x13, waiting for transfers between devices, from_behind(): return lax.ppermute(block, axis, route)  102 us
    pallas_call x2, Pallas kernels, mixer_backward(): pl.pallas_call(functools.partial(backward_kernel, taps, group, first), gr...  66.7 us
    ppermute x60, starting transfers between devices, flip(): return lax.ppermute(value, axis, [(i, i ^ bit) for i in devices])  59.8 us
    pallas_call x2, Pallas kernels, mixer_forward(): pl.pallas_call(functools.partial(forward_kernel, taps, group, first), gri...  55.1 us
    ppermute x12, waiting for transfers between devices, shift(): lax.ppermute(value, axis, [(i, (i + distance) % count) for i in range(cou...  52.6 us
    dot_general x11, matrix products, outer_rows(): lax.dot_general(left, right, (((0,), (0,)), ((), ())), preferred_element_...  48.8 us
  transfers between devices with their start and end apart: 92, of which 35 were waited for; matrix products, arithmetic and copies ran while one was open for 19% of the time, Pallas kernels for 31%

profile of v6, /device:TPU:0, one launch (start us, length us, event | category | flops | bytes accessed | tf_op | source)
XLA Modules:
  0.0 1192.3 jit_solution(16938283120784488132)
XLA Ops:
  18.6 8.9 collective-permute-done
  27.5 17.4 %collective-permute-done.1 = bf16[128,1664]{1,0:T(8,128)(2,1)S(1)} collective-permute-done((bf16[128,1664]{1,0:T(8,128)(2,1)S(1)}, bf16[128,1664]{1,0:T(8,128)(2,1)S(1)}, u32[]{:S(2)}, u32[]{:S(2)}) %collective-permute-start.1) | collective-permute-done | bytes 426016 | tf_op jit(solution)/shard_map/ppermute | solution.py:633
  58.3 9.8 collective-permute-start.11
  70.5 17.5 %collective-permute-done.3.refs_1_.refs_3_ = bf16[512,1664]{1,0:T(8,128)(2,1)} collective-permute-done((bf16[512,1664]{1,0:T(8,128)(2,1)}, bf16[512,1664]{1,0:T(8,128)(2,1)}, u32[]{:S(2)}, u32[]{:S(2)}) %collective-permute-start.3) | collective-permute-done | bytes 1703968 | tf_op jit(solution)/shard_map/ppermute | solution.py:628
  91.6 9.5 collective-permute-done.4.refs_2_.refs_4_
  106.3 6.5 convert_element_type.411
  119.4 10.1 collective-permute-done.5.refs_3_.refs_5_
  129.6 5.4 fusion.1.rows
  142.9 5.3 shard_map.271
  152.8 12.9 %shard_map.272.pre.beta = f32[1024,1664]{1,0:T(8,128)} custom-call(s32[1]{0:T(128)} %bitcast.1.place, bf16[1024,2048]{1,0:T(8,128)(2,1)} %fusion.1.rows, bf16[512,1664]{1,0:T(8,128)(2,1)} %pad_maximum_fusion.6.refs_0_.refs_2_, bf16[512,1664]{1,0:T(8,128)(2,1)} %collective-permute-done.3.refs_1_.refs_3_, ...), custom_call_target="tpu_custom_call" | custom-call | flops 6979321856 | bytes 11010048 | tf_op jit(solution)/shard_map/pallas_call | solution.py:551
  165.7 10.2 collective-permute-done.7.halo
  176.5 27.5 %shard_map.273 = (f32[1024,512]{1,0:T(8,128)}, bf16[1024,512]{1,0:T(8,128)(2,1)}, f32[2,4,128,256]{3,2,1,0:T(8,128)}, bf16[2,4,4,128,128]{4,3,2,1,0:T(8,128)(2,1...) custom-call(f32[1024,1664]{1,0:T(8,128)} %shard_map.272.pre.beta, ...), custom_call_target="tpu_custom_call" | custom-call | flops 4026531840 | bytes 20971520 | tf_op jit(solution)/shard_map/pallas_call | solution.py:160
  208.2 10.2 collective-permute-start.16
  222.2 8.5 collective-permute-done.16
  234.3 15.1 %collective-permute-done.17 = bf16[128,1024]{1,0:T(8,128)(2,1)S(1)} collective-permute-done((bf16[128,1024]{1,0:T(8,128)(2,1)S(1)}, bf16[128,1024]{1,0:T(8,128)(2,1)S(1)}, u32[]{:S(2)}, u32[]{:S(2)}) %collective-permute-start.17) | collective-permute-done | bytes 262176 | tf_op jit(solution)/shard_map/ppermute | solution.py:633
  272.9 10.0 collective-permute-done.9
  297.9 11.5 shard_map.276.pre
  311.1 27.5 %shard_map.277 = (f32[1024,512]{1,0:T(8,128)}, bf16[1024,512]{1,0:T(8,128)(2,1)}, f32[2,4,128,256]{3,2,1,0:T(8,128)}, bf16[2,4,4,128,128]{4,3,2,1,0:T(8,128)(2,1...) custom-call(f32[1024,1536]{1,0:T(8,128)} %shard_map.276.pre, ...), custom_call_target="tpu_custom_call" | custom-call | flops 4026531840 | bytes 20971520 | tf_op jit(solution)/shard_map/pallas_call | solution.py:160
  339.8 8.2 copy.143
  362.0 5.7 collective-permute-done.27
  367.7 5.1 collective-permute-start.34
  373.0 22.5 %collective-permute-done.34.refs_3_.refs_2_ = bf16[512,1024]{1,0:T(8,128)(2,1)S(1)} collective-permute-done((bf16[512,1024]{1,0:T(8,128)(2,1)}, bf16[512,1024]{1,0:T(8,128)(2,1)S(1)}, u32[]{:S(2)}, u32[]{:S(2)}) %collective-permute-start.34) | collective-permute-done | bytes 1048608 | tf_op jit(solution)/shard_map/ppermute | solution.py:628
  401.4 5.6 collective-permute-start.36
  407.8 4.5 shard_map.274
  412.3 8.0 shard_map.278.gate_w.up_w
  422.3 4.5 shard_map.279
  431.2 8.6 shard_map.280
  453.1 4.9 shard_map.281.down_w
  461.5 29.5 %shard_map.282 = (bf16[3,512,704]{2,1,0:T(8,128)(2,1)}, bf16[512,2048]{1,0:T(8,128)(2,1)}, bf16[512,2048]{1,0:T(8,128)(2,1)}, bf16[3,512,704]{2,1,0:T(8,128)(2,1...) custom-call(bf16[512,2048]{1,0:T(8,128)(2,1)} %copy-done.36, ...), custom_call_target="tpu_custom_call" | custom-call | flops 17716740096 | bytes 25427968 | tf_op jit(solution)/shard_map/pallas_call | solution.py:469
  491.0 10.1 collective-permute-done.40.mine.refs_10_
  501.1 6.4 collective-permute-done.44.mine.refs_12_
  513.6 29.5 %shard_map.283 = (bf16[3,512,704]{2,1,0:T(8,128)(2,1)}, bf16[512,2048]{1,0:T(8,128)(2,1)}, bf16[512,2048]{1,0:T(8,128)(2,1)}, bf16[3,512,704]{2,1,0:T(8,128)(2,1...) custom-call(bf16[512,2048]{1,0:T(8,128)(2,1)} %collective-permute-done.40.mine.refs_10_, ...), custom_call_target="tpu_custom_call" | custom-call | flops 17716740096 | bytes 25427968 | tf_op jit(solution)/shard_map/pallas_call | solution.py:469
  543.2 29.7 %shard_map.284 = (bf16[3,512,704]{2,1,0:T(8,128)(2,1)}, bf16[512,2048]{1,0:T(8,128)(2,1)}, bf16[512,2048]{1,0:T(8,128)(2,1)}, bf16[3,512,704]{2,1,0:T(8,128)(2,1...) custom-call(bf16[512,2048]{1,0:T(8,128)(2,1)} %collective-permute-done.44.mine.refs_12_, ...), custom_call_target="tpu_custom_call" | custom-call | flops 17716740096 | bytes 25427968 | tf_op jit(solution)/shard_map/pallas_call | solution.py:469
  586.8 29.5 %shard_map.285 = (bf16[3,512,704]{2,1,0:T(8,128)(2,1)}, bf16[512,2048]{1,0:T(8,128)(2,1)}, bf16[512,2048]{1,0:T(8,128)(2,1)}, bf16[3,512,704]{2,1,0:T(8,128)(2,1...) custom-call(bf16[512,2048]{1,0:T(8,128)(2,1)} %copy-done.42, ...), custom_call_target="tpu_custom_call" | custom-call | flops 17716740096 | bytes 25427968 | tf_op jit(solution)/shard_map/pallas_call | solution.py:469
  616.3 10.9 collective-permute-done.49
  627.3 6.1 collective-permute-done.43
  642.6 47.8 %shard_map.286 = bf16[4,3,704,512]{3,2,1,0:T(8,128)(2,1)} custom-call(bf16[3,512,704]{2,1,0:T(8,128)(2,1)} %get-tuple-element.158.refs_0_, bf16[3,512,704]{2,1,0:T(8,128)(2,1)} %get-tuple-element.159.refs_1_, bf16[3,512,704]{2,1,0:T(8,128)(2,1)} %get-tuple-element.148.refs_2_, bf16[3,512,704]{2,1,0:T(8,128)(2,1)} %get-tuple-element.160.refs_3_, ...), custom_call_target="tpu_custom_call" | custom-call | flops 35433480192 | bytes 67108864 | tf_op jit(solution)/shard_map/pallas_call | solution.py:516
  690.4 11.7 copy.147
  704.2 6.6 collective-permute-done.39
  710.8 6.4 multiply_reduce_fusion.1
  720.0 5.1 add_convert_fusion.2
  736.7 8.9 shard_map.287.grad
  745.6 5.7 shard_map.288
  751.3 5.8 shard_map.289
  760.8 28.8 %collective-permute-done.60 = bf16[2,8,128,128]{3,2,1,0:T(8,128)(2,1)S(1)} collective-permute-done((bf16[2,8,128,128]{3,2,1,0:T(8,128)(2,1)S(1)}, bf16[2,8,128,128]{3,2,1,0:T(8,128)(2,1)S(1)}, u32[]{:S(2)}, u32[]{:S(2)}) %collective-permute-start.60) | collective-permute-done | bytes 524320 | tf_op jit(solution)/shard_map/ppermute | solution.py:639
  792.1 14.0 %collective-permute-done.61 = bf16[2,8,128,128]{3,2,1,0:T(8,128)(2,1)} collective-permute-done((bf16[2,8,128,128]{3,2,1,0:T(8,128)(2,1)}, bf16[2,8,128,128]{3,2,1,0:T(8,128)(2,1)}, u32[]{:S(2)}, u32[]{:S(2)}) %collective-permute-start.61) | collective-permute-done | bytes 524320 | tf_op jit(solution)/shard_map/ppermute | solution.py:639
  812.7 9.1 collective-permute-done.62
  824.1 33.5 %shard_map.290 = (bf16[1024,1536]{1,0:T(8,128)(2,1)}, f32[2,8,1536]{2,1,0:T(8,128)}, f32[2,8,1536]{2,1,0:T(8,128)}, f32[2,8,1536]{2,1,0:T(8,128)}, f32[1024,128]{1,0:T(8,128)}) custom-call(f32[1024,1536]{1,0:T(8,128)} %shard_map.276.pre, f32[1024,1664]{1,0:T(8,128)} %shard_map.272.pre.beta, f32[1,128]{1,0:T(1,128)} %pad_bitcast_fusion.bias, ...), custom_call_target="tpu_custom_call" | custom-call | flops 4026531840 | bytes 20971520 | tf_op jit(solution)/shard_map/pallas_call | solution.py:318
  859.0 9.5 convolution_convert_fusion
  870.5 5.0 convolution_convert_fusion.3
  884.7 33.2 %shard_map.291 = (bf16[1024,1536]{1,0:T(8,128)(2,1)}, f32[2,8,1536]{2,1,0:T(8,128)}, f32[2,8,1536]{2,1,0:T(8,128)}, f32[2,8,1536]{2,1,0:T(8,128)}, f32[1024,128]{1,0:T(8,128)}) custom-call(f32[1024,1664]{1,0:T(8,128)} %shard_map.272.pre.beta, f32[1024,1664]{1,0:T(8,128)} %shard_map.272.pre.beta, f32[1,128]{1,0:T(1,128)} %pad_bitcast_fusion.bias, ...), custom_call_target="tpu_custom_call" | custom-call | flops 4026531840 | bytes 20971520 | tf_op jit(solution)/shard_map/pallas_call | solution.py:318
  920.6 20.4 %collective-permute-done.66 = f32[2,8,1536]{2,1,0:T(8,128)S(1)} collective-permute-done((f32[2,8,1536]{2,1,0:T(8,128)}, f32[2,8,1536]{2,1,0:T(8,128)S(1)}, u32[]{:S(2)}, u32[]{:S(2)}) %collective-permute-start.66) | collective-permute-done | bytes 98336 | tf_op jit(solution)/shard_map/ppermute | solution.py:639
  942.5 5.7 convolution_convert_fusion.1
  953.6 5.9 fusion.28
  962.3 4.9 fusion.15
  976.4 26.1 %collective-permute-done.68 = bf16[512,1664]{1,0:T(8,128)(2,1)} collective-permute-done((bf16[512,1664]{1,0:T(8,128)(2,1)}, bf16[512,1664]{1,0:T(8,128)(2,1)}, u32[]{:S(2)}, u32[]{:S(2)}) %collective-permute-start.68) | collective-permute-done | bytes 1703968 | tf_op jit(solution)/shard_map/ppermute | solution.py:628
  1011.4 21.4 %shard_map.292 = bf16[1024,2048]{1,0:T(8,128)(2,1)} custom-call(s32[1]{0:T(128)} %bitcast.1.place, bf16[1024,1664]{1,0:T(8,128)(2,1)} %pad_maximum_fusion.3.refs_0_, bf16[1024,1536]{1,0:T(8,128)(2,1)} %bitcast.152, bf16[512,1664]{1,0:T(8,128)(2,1)} %pad_maximum_fusion.6.refs_0_.refs_2_, bf16[512,1664]{1,0:T(8,128)(2,1)} %collective-permute-done.3.refs_1_.refs_3_, ...), custom_call_target="tpu_custom_call" | custom-call | flops 13421772800 | bytes 17301504 | tf_op jit(solution)/shard_map/pallas_call | solution.py:587
  1036.3 5.3 fusion.30
  1046.3 16.8 %collective-permute-done.77 = bf16[256,1664]{1,0:T(8,128)(2,1)S(1)} collective-permute-done((bf16[256,1664]{1,0:T(8,128)(2,1)}, bf16[256,1664]{1,0:T(8,128)(2,1)S(1)}, u32[]{:S(2)}, u32[]{:S(2)}) %collective-permute-start.77) | collective-permute-done | bytes 852000 | tf_op jit(solution)/shard_map/ppermute | solution.py:628
  1077.7 5.3 fusion.9
  1087.4 11.6 collective-permute-done.72
  1102.6 16.0 %collective-permute-start.79 = (bf16[128,1664]{1,0:T(8,128)(2,1)}, bf16[128,1664]{1,0:T(8,128)(2,1)S(1)}, u32[]{:S(2)}, u32[]{:S(2)}) collective-permute-start(bf16[128,1664]{1,0:T(8,128)(2,1)} %get-tuple-element.342), channel_id=1, source_target_pairs={{0,2},{1,3},{2,0},{3,1},{4,6},{5,7},{6,4},{7,5},{8,10},{9,11},{10,... | collective-permute-start | bytes 1277960 | tf_op jit(solution)/shard_map/ppermute | solution.py:633
  1120.7 26.0 %collective-permute-done.74 = f32[16640]{0:T(1024)S(1)} collective-permute-done((f32[16640]{0:T(1024)S(1)}, f32[16640]{0:T(1024)S(1)}, u32[]{:S(2)}, u32[]{:S(2)}) %collective-permute-start.74) | collective-permute-done | bytes 66592 | tf_op jit(solution)/shard_map/ppermute | solution.py:628
  1147.3 12.7 %fusion.5 = (bf16[512,2048]{1,0:T(8,128)(2,1)}, bf16[512,2048]{1,0:T(8,128)(2,1)}) fusion(f32[2,256,2048]{2,1,0:T(8,128)} %get-tuple-element.327, f32[512]{0:T(512)S(1)} %bitcast.199, f32[2048]{0:T(1024)S(1)} %copy-done.51, f32[512]{0:T(512)S(1)} %bitcast.198, bf16[2,512,2048]{2,1,0:T(8,128)(2,1)} %param.16, s32[]{:T(128)S(6)} %select_n.387, ...), kind=kLoop, calls=%fused_computation.11 | loop fusion | flops 27262976 | bytes 31481860 | tf_op jit(solution)/shard_map/convert_element_type | solution.py:19
  (491 shorter events, 314.1 us)
Async XLA Ops:
  14.7 30.2 %collective-permute-start.1 = (bf16[128,1664]{1,0:T(8,128)(2,1)S(1)}, bf16[128,1664]{1,0:T(8,128)(2,1)S(1)}, u32[]{:S(2)}, u32[]{:S(2)}) collective-permute-start(bf16[128,1664]{1,0:T(8,128)(2,1)S(1)} %constant_dynamic-update-slice_fusion), channel_id=1, source_target_pairs={{0,2},{1,3},{2,0},{3,1},{4,6},{5,7},{6,4},{7,5},{8,10},{9,11},{10,... | collective-permute-start | bytes 1277960 | tf_op jit(solution)/shard_map/ppermute | solution.py:633
  17.3 27.6 %collective-permute-start.2 = (bf16[128,1664]{1,0:T(8,128)(2,1)S(1)}, bf16[128,1664]{1,0:T(8,128)(2,1)}, u32[]{:S(2)}, u32[]{:S(2)}) collective-permute-start(bf16[128,1664]{1,0:T(8,128)(2,1)S(1)} %constant_dynamic-update-slice_fusion), channel_id=1, source_target_pairs={{0,3},{1,0},{2,1},{3,2},{4,7},{5,4},{6,5},{7,6},{8,11},{9,8},{10,9... | collective-permute-start | bytes 1277960 | tf_op jit(solution)/shard_map/ppermute | solution.py:633
  47.6 40.4 %collective-permute-start.3 = (bf16[512,1664]{1,0:T(8,128)(2,1)}, bf16[512,1664]{1,0:T(8,128)(2,1)}, u32[]{:S(2)}, u32[]{:S(2)}) collective-permute-start(bf16[512,1664]{1,0:T(8,128)(2,1)} %pad_maximum_fusion.6.refs_0_.refs_2_), channel_id=1, source_target_pairs={{0,8},{8,0},{16,24},{24,16},{1,9},{9,1},{17,25},{25,17},{2,10},{10... | collective-permute-start | bytes 5111816 | tf_op jit(solution)/shard_map/ppermute | solution.py:628
  49.1 52.0 %collective-permute-start.4 = (bf16[512,1664]{1,0:T(8,128)(2,1)}, bf16[512,1664]{1,0:T(8,128)(2,1)}, u32[]{:S(2)}, u32[]{:S(2)}) collective-permute-start(bf16[512,1664]{1,0:T(8,128)(2,1)} %pad_maximum_fusion.6.refs_0_.refs_2_), channel_id=1, source_target_pairs={{0,16},{8,24},{16,0},{24,8},{1,17},{9,25},{17,1},{25,9},{2,18},{10... | collective-permute-start | bytes 5111816 | tf_op jit(solution)/shard_map/ppermute | solution.py:628
  54.6 60.9 %all-to-all-start = ((bf16[4,2112,128]{2,1,0:T(8,128)(2,1)}), bf16[4,2112,128]{2,1,0:T(8,128)(2,1)S(1)}, u32[]{:S(2)}, u32[]{:S(2)}) async-start(bf16[4,2112,128]{2,1,0:T(8,128)(2,1)} %bitcast.160), calls=%async_computation | async-start | bytes 4325376 | tf_op jit(solution)/shard_map/all_to_all | solution.py:890
  58.2 281.5 %all-gather.6.cloned.1.call-start = ((), (), s32[]{:S(2)}) async-start(), calls=%async_computation.9 | async-start | bytes 7208960 | tf_op jit(solution)/shard_map/all_gather | solution.py:908
  58.3 54.6 %collective-permute-start.11 = (bf16[128,1536]{1,0:T(8,128)(2,1)S(1)}, bf16[128,1536]{1,0:T(8,128)(2,1)}, u32[]{:S(2)}, u32[]{:S(2)}) collective-permute-start(bf16[128,1536]{1,0:T(8,128)(2,1)S(1)} %get-tuple-element.118), channel_id=1, source_target_pairs={{0,1},{1,2},{2,3},{3,0},{4,5},{5,6},{6,7},{7,4},{8,9},{9,10},{10,1... | collective-permute-start | bytes 1179656 | tf_op jit(solution)/shard_map/ppermute | solution.py:633
  68.0 44.8 %collective-permute-start.12 = (bf16[128,1536]{1,0:T(8,128)(2,1)S(1)}, bf16[128,1536]{1,0:T(8,128)(2,1)}, u32[]{:S(2)}, u32[]{:S(2)}) collective-permute-start(bf16[128,1536]{1,0:T(8,128)(2,1)S(1)} %get-tuple-element.118), channel_id=1, source_target_pairs={{0,2},{1,3},{2,0},{3,1},{4,6},{5,7},{6,4},{7,5},{8,10},{9,11},{10,... | collective-permute-start | bytes 1179656 | tf_op jit(solution)/shard_map/ppermute | solution.py:633
  69.5 43.3 %collective-permute-start.13 = (bf16[128,1536]{1,0:T(8,128)(2,1)S(1)}, bf16[128,1536]{1,0:T(8,128)(2,1)}, u32[]{:S(2)}, u32[]{:S(2)}) collective-permute-start(bf16[128,1536]{1,0:T(8,128)(2,1)S(1)} %get-tuple-element.118), channel_id=1, source_target_pairs={{0,3},{1,0},{2,1},{3,2},{4,7},{5,4},{6,5},{7,6},{8,11},{9,8},{10,9... | collective-permute-start | bytes 1179656 | tf_op jit(solution)/shard_map/ppermute | solution.py:633
  90.1 39.4 %collective-permute-start.5 = (bf16[256,1664]{1,0:T(8,128)(2,1)}, bf16[256,1664]{1,0:T(8,128)(2,1)S(1)}, u32[]{:S(2)}, u32[]{:S(2)}) collective-permute-start(bf16[256,1664]{1,0:T(8,128)(2,1)} %slice.626), channel_id=1, source_target_pairs={{0,16},{8,24},{16,0},{24,8},{1,17},{9,25},{17,1},{25,9},{2,18},{10... | collective-permute-start | bytes 2555912 | tf_op jit(solution)/shard_map/ppermute | solution.py:628
  103.2 26.2 %collective-permute-start.6 = (bf16[256,1664]{1,0:T(8,128)(2,1)}, bf16[256,1664]{1,0:T(8,128)(2,1)}, u32[]{:S(2)}, u32[]{:S(2)}) collective-permute-start(bf16[256,1664]{1,0:T(8,128)(2,1)} %slice.627), channel_id=1, source_target_pairs={{0,8},{8,0},{16,24},{24,16},{1,9},{9,1},{17,25},{25,17},{2,10},{10... | collective-permute-start | bytes 2555912 | tf_op jit(solution)/shard_map/ppermute | solution.py:628
  129.5 310.4 %all-gather.4.cloned.1.call-start = ((), (), s32[]{:S(2)}) async-start(), calls=%async_computation.5 | async-start | bytes 3604480 | tf_op jit(solution)/shard_map/all_gather | solution.py:909
  140.3 63.7 %collective-permute-start.14 = (bf16[512,1536]{1,0:T(8,128)(2,1)}, bf16[512,1536]{1,0:T(8,128)(2,1)}, u32[]{:S(2)}, u32[]{:S(2)}) collective-permute-start(bf16[512,1536]{1,0:T(8,128)(2,1)} %pad_maximum_fusion.7.refs_0_.refs_7_), channel_id=1, source_target_pairs={{0,8},{8,0},{16,24},{24,16},{1,9},{9,1},{17,25},{25,17},{2,10},{10... | collective-permute-start | bytes 4718600 | tf_op jit(solution)/shard_map/ppermute | solution.py:628
  140.9 63.2 %collective-permute-start.15 = (bf16[512,1536]{1,0:T(8,128)(2,1)}, bf16[512,1536]{1,0:T(8,128)(2,1)}, u32[]{:S(2)}, u32[]{:S(2)}) collective-permute-start(bf16[512,1536]{1,0:T(8,128)(2,1)} %pad_maximum_fusion.7.refs_0_.refs_7_), channel_id=1, source_target_pairs={{0,16},{8,24},{16,0},{24,8},{1,17},{9,25},{17,1},{25,9},{2,18},{10... | collective-permute-start | bytes 4718600 | tf_op jit(solution)/shard_map/ppermute | solution.py:628
  149.1 26.8 %collective-permute-start.7 = (f32[2,8,1536]{2,1,0:T(8,128)S(1)}, f32[2,8,1536]{2,1,0:T(8,128)S(1)}, u32[]{:S(2)}, u32[]{:S(2)}) collective-permute-start(f32[2,8,1536]{2,1,0:T(8,128)S(1)} %slice_bitcast_fusion.3), channel_id=1, source_target_pairs={{0,8},{8,16},{16,24},{1,9},{9,17},{17,25},{2,10},{10,18},{18,26},{... | collective-permute-start | bytes 294920 | tf_op jit(solution)/shard_map/ppermute | solution.py:639
  204.1 62.4 %collective-permute-start.21 = (bf16[512,2048]{1,0:T(8,128)(2,1)S(1)}, bf16[512,2048]{1,0:T(8,128)(2,1)}, u32[]{:S(2)}, u32[]{:S(2)}) collective-permute-start(bf16[512,2048]{1,0:T(8,128)(2,1)S(1)} %bitcast.143), channel_id=1, source_target_pairs={{0,8},{8,0},{16,24},{24,16},{1,9},{9,1},{17,25},{25,17},{2,10},{10... | collective-permute-start | bytes 6291464 | tf_op jit(solution)/shard_map/ppermute | solution.py:628
  206.6 63.0 %collective-permute-start.22 = (bf16[512,2048]{1,0:T(8,128)(2,1)S(1)}, bf16[512,2048]{1,0:T(8,128)(2,1)}, u32[]{:S(2)}, u32[]{:S(2)}) collective-permute-start(bf16[512,2048]{1,0:T(8,128)(2,1)S(1)} %bitcast.144), channel_id=1, source_target_pairs={{0,16},{8,24},{16,0},{24,8},{1,17},{9,25},{17,1},{25,9},{2,18},{10... | collective-permute-start | bytes 6291464 | tf_op jit(solution)/shard_map/ppermute | solution.py:628
  218.5 30.9 %collective-permute-start.17 = (bf16[128,1024]{1,0:T(8,128)(2,1)S(1)}, bf16[128,1024]{1,0:T(8,128)(2,1)S(1)}, u32[]{:S(2)}, u32[]{:S(2)}) collective-permute-start(bf16[128,1024]{1,0:T(8,128)(2,1)S(1)} %bitcast.180), channel_id=1, source_target_pairs={{0,2},{1,3},{2,0},{3,1},{4,6},{5,7},{6,4},{7,5},{8,10},{9,11},{10,... | collective-permute-start | bytes 786440 | tf_op jit(solution)/shard_map/ppermute | solution.py:633
  218.5 33.6 %collective-permute-start.18 = (bf16[128,1024]{1,0:T(8,128)(2,1)S(1)}, bf16[128,1024]{1,0:T(8,128)(2,1)S(1)}, u32[]{:S(2)}, u32[]{:S(2)}) collective-permute-start(bf16[128,1024]{1,0:T(8,128)(2,1)S(1)} %bitcast.181), channel_id=1, source_target_pairs={{0,3},{1,0},{2,1},{3,2},{4,7},{5,4},{6,5},{7,6},{8,11},{9,8},{10,9... | collective-permute-start | bytes 786440 | tf_op jit(solution)/shard_map/ppermute | solution.py:633
  230.7 28.3 %collective-permute-start.8 = (bf16[2,4,128,128]{3,2,1,0:T(8,128)(2,1)S(1)}, bf16[2,4,128,128]{3,2,1,0:T(8,128)(2,1)S(1)}, u32[]{:S(2)}, u32[]{:S(2)}) collective-permute-start(bf16[2,4,128,128]{3,2,1,0:T(8,128)(2,1)S(1)} %get-tuple-element.361), channel_id=1, source_target_pairs={{0,8},{8,16},{16,24},{1,9},{9,17},{17,25},{2,10},{10,18},{18,26},{... | collective-permute-start | bytes 786440 | tf_op jit(solution)/shard_map/ppermute | solution.py:639
  257.4 31.9 %collective-permute-start.19 = (bf16[256,1536]{1,0:T(8,128)(2,1)}, bf16[256,1536]{1,0:T(8,128)(2,1)}, u32[]{:S(2)}, u32[]{:S(2)}) collective-permute-start(bf16[256,1536]{1,0:T(8,128)(2,1)} %slice.654), channel_id=1, source_target_pairs={{0,16},{8,24},{16,0},{24,8},{1,17},{9,25},{17,1},{25,9},{2,18},{10... | collective-permute-start | bytes 2359304 | tf_op jit(solution)/shard_map/ppermute | solution.py:628
  257.9 31.4 %collective-permute-start.20 = (bf16[256,1536]{1,0:T(8,128)(2,1)}, bf16[256,1536]{1,0:T(8,128)(2,1)}, u32[]{:S(2)}, u32[]{:S(2)}) collective-permute-start(bf16[256,1536]{1,0:T(8,128)(2,1)} %slice.655), channel_id=1, source_target_pairs={{0,8},{8,0},{16,24},{24,16},{1,9},{9,1},{17,25},{25,17},{2,10},{10... | collective-permute-start | bytes 2359304 | tf_op jit(solution)/shard_map/ppermute | solution.py:628
  259.9 23.0 %collective-permute-start.9 = (bf16[2,4,128,128]{3,2,1,0:T(8,128)(2,1)}, bf16[2,4,128,128]{3,2,1,0:T(8,128)(2,1)}, u32[]{:S(2)}, u32[]{:S(2)}) collective-permute-start(bf16[2,4,128,128]{3,2,1,0:T(8,128)(2,1)} %fusion.24), channel_id=1, source_target_pairs={{0,8},{8,16},{16,24},{1,9},{9,17},{17,25},{2,10},{10,18},{18,26},{... | collective-permute-start | bytes 786440 | tf_op jit(solution)/shard_map/ppermute | solution.py:639
  266.4 618.4 %reduce-scatter.4.cloned.1.call-start = ((), (), s32[]{:S(2)}) async-start(), calls=%async_computation.6 | async-start | bytes 11141120 | tf_op jit(solution)/shard_map/reduce_scatter | solution.py:1010
  268.8 79.2 %collective-permute-start.24 = (bf16[256,2048]{1,0:T(8,128)(2,1)}, bf16[256,2048]{1,0:T(8,128)(2,1)}, u32[]{:S(2)}, u32[]{:S(2)}) collective-permute-start(bf16[256,2048]{1,0:T(8,128)(2,1)} %slice.669), channel_id=1, source_target_pairs={{0,16},{8,24},{16,0},{24,8},{1,17},{9,25},{17,1},{25,9},{2,18},{10... | collective-permute-start | bytes 3145736 | tf_op jit(solution)/shard_map/ppermute | solution.py:628
  271.9 76.1 %collective-permute-start.25 = (bf16[256,2048]{1,0:T(8,128)(2,1)}, bf16[256,2048]{1,0:T(8,128)(2,1)}, u32[]{:S(2)}, u32[]{:S(2)}) collective-permute-start(bf16[256,2048]{1,0:T(8,128)(2,1)} %slice.670), channel_id=1, source_target_pairs={{0,8},{8,0},{16,24},{24,16},{1,9},{9,1},{17,25},{25,17},{2,10},{10... | collective-permute-start | bytes 3145736 | tf_op jit(solution)/shard_map/ppermute | solution.py:628
  284.8 72.2 %collective-permute-start.10 = (bf16[2,4,128,128]{3,2,1,0:T(8,128)(2,1)}, bf16[2,4,128,128]{3,2,1,0:T(8,128)(2,1)S(1)}, u32[]{:S(2)}, u32[]{:S(2)}) collective-permute-start(bf16[2,4,128,128]{3,2,1,0:T(8,128)(2,1)} %fusion.25), channel_id=1, source_target_pairs={{0,8},{8,16},{16,24},{1,9},{9,17},{17,25},{2,10},{10,18},{18,26},{... | collective-permute-start | bytes 786440 | tf_op jit(solution)/shard_map/ppermute | solution.py:639
  289.2 109.9 %collective-permute-start.29 = (bf16[512,2048]{1,0:T(8,128)(2,1)S(1)}, bf16[512,2048]{1,0:T(8,128)(2,1)}, u32[]{:S(2)}, u32[]{:S(2)}) collective-permute-start(bf16[512,2048]{1,0:T(8,128)(2,1)S(1)} %bitcast.145), channel_id=1, source_target_pairs={{0,4},{4,0},{1,5},{5,1},{2,6},{6,2},{3,7},{7,3},{8,12},{12,8},{9,1... | collective-permute-start | bytes 6291464 | tf_op jit(solution)/shard_map/ppermute | solution.py:628
  309.5 48.1 %collective-permute-start.33 = (bf16[512,1024]{1,0:T(8,128)(2,1)}, bf16[512,1024]{1,0:T(8,128)(2,1)}, u32[]{:S(2)}, u32[]{:S(2)}) collective-permute-start(bf16[512,1024]{1,0:T(8,128)(2,1)} %pad_maximum_fusion.9.refs_1_.refs_0_), channel_id=1, source_target_pairs={{0,8},{8,0},{16,24},{24,16},{1,9},{9,1},{17,25},{25,17},{2,10},{10... | collective-permute-start | bytes 3145736 | tf_op jit(solution)/shard_map/ppermute | solution.py:628
  348.0 81.6 %collective-permute-start.30 = (bf16[512,2048]{1,0:T(8,128)(2,1)}, bf16[512,2048]{1,0:T(8,128)(2,1)}, u32[]{:S(2)}, u32[]{:S(2)}) collective-permute-start(bf16[512,2048]{1,0:T(8,128)(2,1)} %collective-permute-done.21.mine_grads.refs_18_), channel_id=1, source_target_pairs={{0,4},{4,0},{1,5},{5,1},{2,6},{6,2},{3,7},{7,3},{8,12},{12,8},{9,1... | collective-permute-start | bytes 6291464 | tf_op jit(solution)/shard_map/ppermute | solution.py:628
  356.8 72.8 %collective-permute-start.31 = (bf16[512,2048]{1,0:T(8,128)(2,1)}, bf16[512,2048]{1,0:T(8,128)(2,1)}, u32[]{:S(2)}, u32[]{:S(2)}) collective-permute-start(bf16[512,2048]{1,0:T(8,128)(2,1)} %collective-permute-done.22.mine_grads.refs_20_), channel_id=1, source_target_pairs={{0,4},{4,0},{1,5},{5,1},{2,6},{6,2},{3,7},{7,3},{8,12},{12,8},{9,1... | collective-permute-start | bytes 6291464 | tf_op jit(solution)/shard_map/ppermute | solution.py:628
  357.0 72.6 %collective-permute-start.32 = (bf16[512,2048]{1,0:T(8,128)(2,1)}, bf16[512,2048]{1,0:T(8,128)(2,1)}, u32[]{:S(2)}, u32[]{:S(2)}) collective-permute-start(bf16[512,2048]{1,0:T(8,128)(2,1)} %constant_dynamic-update-slice_fusion.49.mine_grads.refs_22_), channel_id=1, source_target_pairs={{0,4},{4,0},{1,5},{5,1},{2,6},{6,2},{3,7},{7,3},{8,12},{12,8},{9,1... | collective-permute-start | bytes 6291464 | tf_op jit(solution)/shard_map/ppermute | solution.py:628
  367.7 27.8 %collective-permute-start.34 = (bf16[512,1024]{1,0:T(8,128)(2,1)}, bf16[512,1024]{1,0:T(8,128)(2,1)S(1)}, u32[]{:S(2)}, u32[]{:S(2)}) collective-permute-start(bf16[512,1024]{1,0:T(8,128)(2,1)} %pad_maximum_fusion.9.refs_1_.refs_0_), channel_id=1, source_target_pairs={{0,16},{8,24},{16,0},{24,8},{1,17},{9,25},{17,1},{25,9},{2,18},{10... | collective-permute-start | bytes 3145736 | tf_op jit(solution)/shard_map/ppermute | solution.py:628
  399.1 30.5 %collective-permute-start.35 = (bf16[256,1024]{1,0:T(8,128)(2,1)S(1)}, bf16[256,1024]{1,0:T(8,128)(2,1)S(1)}, u32[]{:S(2)}, u32[]{:S(2)}) collective-permute-start(bf16[256,1024]{1,0:T(8,128)(2,1)S(1)} %slice.672), channel_id=1, source_target_pairs={{0,16},{8,24},{16,0},{24,8},{1,17},{9,25},{17,1},{25,9},{2,18},{10... | collective-permute-start | bytes 1572872 | tf_op jit(solution)/shard_map/ppermute | solution.py:628
  401.4 28.3 %collective-permute-start.36 = (bf16[256,1024]{1,0:T(8,128)(2,1)S(1)}, bf16[256,1024]{1,0:T(8,128)(2,1)S(1)}, u32[]{:S(2)}, u32[]{:S(2)}) collective-permute-start(bf16[256,1024]{1,0:T(8,128)(2,1)S(1)} %slice.673), channel_id=1, source_target_pairs={{0,8},{8,0},{16,24},{24,16},{1,9},{9,1},{17,25},{25,17},{2,10},{10... | collective-permute-start | bytes 1572872 | tf_op jit(solution)/shard_map/ppermute | solution.py:628
  453.1 48.0 %collective-permute-start.40 = (bf16[512,2048]{1,0:T(8,128)(2,1)S(1)}, bf16[512,2048]{1,0:T(8,128)(2,1)}, u32[]{:S(2)}, u32[]{:S(2)}) collective-permute-start(bf16[512,2048]{1,0:T(8,128)(2,1)S(1)} %get-tuple-element.325.mine.refs_8_), channel_id=1, source_target_pairs={{0,8},{8,0},{16,24},{24,16},{1,9},{9,1},{17,25},{25,17},{2,10},{10... | collective-permute-start | bytes 6291464 | tf_op jit(solution)/shard_map/ppermute | solution.py:628
  458.0 49.5 %collective-permute-start.44 = (bf16[512,2048]{1,0:T(8,128)(2,1)S(1)}, bf16[512,2048]{1,0:T(8,128)(2,1)}, u32[]{:S(2)}, u32[]{:S(2)}) collective-permute-start(bf16[512,2048]{1,0:T(8,128)(2,1)S(1)} %get-tuple-element.325.mine.refs_8_), channel_id=1, source_target_pairs={{0,16},{8,24},{16,0},{24,8},{1,17},{9,25},{17,1},{25,9},{2,18},{10... | collective-permute-start | bytes 6291464 | tf_op jit(solution)/shard_map/ppermute | solution.py:628
  507.5 35.7 %collective-permute-start.47 = (bf16[512,2048]{1,0:T(8,128)(2,1)}, bf16[512,2048]{1,0:T(8,128)(2,1)}, u32[]{:S(2)}, u32[]{:S(2)}) collective-permute-start(bf16[512,2048]{1,0:T(8,128)(2,1)} %collective-permute-done.44.mine.refs_12_), channel_id=1, source_target_pairs={{0,4},{4,0},{1,5},{5,1},{2,6},{6,2},{3,7},{7,3},{8,12},{12,8},{9,1... | collective-permute-start | bytes 6291464 | tf_op jit(solution)/shard_map/ppermute | solution.py:628
  511.1 32.0 %collective-permute-start.45 = (bf16[256,2048]{1,0:T(8,128)(2,1)}, bf16[256,2048]{1,0:T(8,128)(2,1)S(1)}, u32[]{:S(2)}, u32[]{:S(2)}) collective-permute-start(bf16[256,2048]{1,0:T(8,128)(2,1)} %slice.675), channel_id=1, source_target_pairs={{0,16},{8,24},{16,0},{24,8},{1,17},{9,25},{17,1},{25,9},{2,18},{10... | collective-permute-start | bytes 3145736 | tf_op jit(solution)/shard_map/ppermute | solution.py:628
  512.9 30.2 %collective-permute-start.46 = (bf16[256,2048]{1,0:T(8,128)(2,1)S(1)}, bf16[256,2048]{1,0:T(8,128)(2,1)S(1)}, u32[]{:S(2)}, u32[]{:S(2)}) collective-permute-start(bf16[256,2048]{1,0:T(8,128)(2,1)S(1)} %slice.676), channel_id=1, source_target_pairs={{0,8},{8,0},{16,24},{24,16},{1,9},{9,1},{17,25},{25,17},{2,10},{10... | collective-permute-start | bytes 3145736 | tf_op jit(solution)/shard_map/ppermute | solution.py:628
  579.4 47.9 %collective-permute-start.49 = (bf16[512,2048]{1,0:T(8,128)(2,1)}, bf16[512,2048]{1,0:T(8,128)(2,1)S(1)}, u32[]{:S(2)}, u32[]{:S(2)}) collective-permute-start(bf16[512,2048]{1,0:T(8,128)(2,1)} %add_convert_fusion.5), channel_id=1, source_target_pairs={{0,16},{8,24},{16,0},{24,8},{1,17},{9,25},{17,1},{25,9},{2,18},{10... | collective-permute-start | bytes 6291464 | tf_op jit(solution)/shard_map/ppermute | solution.py:628
  585.4 48.0 %collective-permute-start.43 = (bf16[512,2048]{1,0:T(8,128)(2,1)}, bf16[512,2048]{1,0:T(8,128)(2,1)}, u32[]{:S(2)}, u32[]{:S(2)}) collective-permute-start(bf16[512,2048]{1,0:T(8,128)(2,1)} %add_convert_fusion.6), channel_id=1, source_target_pairs={{0,8},{8,0},{16,24},{24,16},{1,9},{9,1},{17,25},{25,17},{2,10},{10... | collective-permute-start | bytes 6291464 | tf_op jit(solution)/shard_map/ppermute | solution.py:628
  641.5 48.9 %collective-permute-start.52 = (bf16[512,2048]{1,0:T(8,128)(2,1)}, bf16[512,2048]{1,0:T(8,128)(2,1)}, u32[]{:S(2)}, u32[]{:S(2)}) collective-permute-start(bf16[512,2048]{1,0:T(8,128)(2,1)} %add_convert_fusion.4), channel_id=1, source_target_pairs={{0,24},{8,16},{16,8},{24,0},{1,25},{9,17},{17,9},{25,1},{2,26},{10... | collective-permute-start | bytes 6291464 | tf_op jit(solution)/shard_map/ppermute | solution.py:628
  702.1 385.3 %reduce-scatter.8.cloned.1.call-start = ((), (), s32[]{:S(2)}) async-start(), calls=%async_computation.8 | async-start | bytes 4456448 | tf_op jit(solution)/shard_map/reduce_scatter | solution.py:1013
  725.1 64.5 %collective-permute-start.58 = (bf16[512,2048]{1,0:T(8,128)(2,1)}, bf16[512,2048]{1,0:T(8,128)(2,1)}, u32[]{:S(2)}, u32[]{:S(2)}) collective-permute-start(bf16[512,2048]{1,0:T(8,128)(2,1)} %add_convert_fusion.2), channel_id=1, source_target_pairs={{0,16},{8,24},{16,0},{24,8},{1,17},{9,25},{17,1},{25,9},{2,18},{10... | collective-permute-start | bytes 6291464 | tf_op jit(solution)/shard_map/ppermute | solution.py:628
  730.6 59.0 %collective-permute-start.56 = (bf16[512,2048]{1,0:T(8,128)(2,1)}, bf16[512,2048]{1,0:T(8,128)(2,1)}, u32[]{:S(2)}, u32[]{:S(2)}) collective-permute-start(bf16[512,2048]{1,0:T(8,128)(2,1)} %add_convert_fusion.3), channel_id=1, source_target_pairs={{0,8},{8,0},{16,24},{24,16},{1,9},{9,1},{17,25},{25,17},{2,10},{10... | collective-permute-start | bytes 6291464 | tf_op jit(solution)/shard_map/ppermute | solution.py:628
  736.7 72.2 %collective-permute-start.59 = (bf16[512,2048]{1,0:T(8,128)(2,1)}, bf16[512,2048]{1,0:T(8,128)(2,1)}, u32[]{:S(2)}, u32[]{:S(2)}) collective-permute-start(bf16[512,2048]{1,0:T(8,128)(2,1)} %get-tuple-element.175), channel_id=1, source_target_pairs={{0,4},{4,0},{1,5},{5,1},{2,6},{6,2},{3,7},{7,3},{8,12},{12,8},{9,1... | collective-permute-start | bytes 6291464 | tf_op jit(solution)/shard_map/ppermute | solution.py:628
  758.4 31.2 %collective-permute-start.60 = (bf16[2,8,128,128]{3,2,1,0:T(8,128)(2,1)S(1)}, bf16[2,8,128,128]{3,2,1,0:T(8,128)(2,1)S(1)}, u32[]{:S(2)}, u32[]{:S(2)}) collective-permute-start(bf16[2,8,128,128]{3,2,1,0:T(8,128)(2,1)S(1)} %convert_element_type.367), channel_id=1, source_target_pairs={{8,0},{16,8},{24,16},{9,1},{17,9},{25,17},{10,2},{18,10},{26,18},{... | collective-permute-start | bytes 1572872 | tf_op jit(solution)/shard_map/ppermute | solution.py:639
  821.8 48.7 %collective-permute-start.63 = (bf16[512,2048]{1,0:T(8,128)(2,1)}, bf16[512,2048]{1,0:T(8,128)(2,1)}, u32[]{:S(2)}, u32[]{:S(2)}) collective-permute-start(bf16[512,2048]{1,0:T(8,128)(2,1)} %add_convert_fusion.1), channel_id=1, source_target_pairs={{0,24},{8,16},{16,8},{24,0},{1,25},{9,17},{17,9},{25,1},{2,26},{10... | collective-permute-start | bytes 6291464 | tf_op jit(solution)/shard_map/ppermute | solution.py:628
  868.5 304.3 %reduce-scatter.6.cloned.1.call-start = ((), (), s32[]{:S(2)}) async-start(), calls=%async_computation.7 | async-start | bytes 1966080 | tf_op jit(solution)/shard_map/reduce_scatter | solution.py:756
  875.5 84.0 %collective-permute-start.82 = (bf16[512,1536]{1,0:T(8,128)(2,1)}, bf16[512,1536]{1,0:T(8,128)(2,1)}, u32[]{:S(2)}, u32[]{:S(2)}) collective-permute-start(bf16[512,1536]{1,0:T(8,128)(2,1)} %convolution_convert_fusion.3), channel_id=1, source_target_pairs={{0,16},{8,24},{16,0},{24,8},{1,17},{9,25},{17,1},{25,9},{2,18},{10... | collective-permute-start | bytes 4718600 | tf_op jit(solution)/shard_map/ppermute | solution.py:628
  882.7 76.9 %collective-permute-start.81 = (bf16[512,1536]{1,0:T(8,128)(2,1)}, bf16[512,1536]{1,0:T(8,128)(2,1)}, u32[]{:S(2)}, u32[]{:S(2)}) collective-permute-start(bf16[512,1536]{1,0:T(8,128)(2,1)} %convolution_convert_fusion.4), channel_id=1, source_target_pairs={{0,8},{8,0},{16,24},{24,16},{1,9},{9,1},{17,25},{25,17},{2,10},{10... | collective-permute-start | bytes 4718600 | tf_op jit(solution)/shard_map/ppermute | solution.py:628
  917.9 23.1 %collective-permute-start.66 = (f32[2,8,1536]{2,1,0:T(8,128)}, f32[2,8,1536]{2,1,0:T(8,128)S(1)}, u32[]{:S(2)}, u32[]{:S(2)}) collective-permute-start(f32[2,8,1536]{2,1,0:T(8,128)} %get-tuple-element.196), channel_id=1, source_target_pairs={{8,0},{16,8},{24,16},{9,1},{17,9},{25,17},{10,2},{18,10},{26,18},{... | collective-permute-start | bytes 294920 | tf_op jit(solution)/shard_map/ppermute | solution.py:639
  948.2 54.2 %collective-permute-start.68 = (bf16[512,1664]{1,0:T(8,128)(2,1)}, bf16[512,1664]{1,0:T(8,128)(2,1)}, u32[]{:S(2)}, u32[]{:S(2)}) collective-permute-start(bf16[512,1664]{1,0:T(8,128)(2,1)} %convolution_convert_fusion.1), channel_id=1, source_target_pairs={{0,8},{8,0},{16,24},{24,16},{1,9},{9,1},{17,25},{25,17},{2,10},{10... | collective-permute-start | bytes 5111816 | tf_op jit(solution)/shard_map/ppermute | solution.py:628
  953.4 52.1 %collective-permute-start.67 = (bf16[512,1664]{1,0:T(8,128)(2,1)}, bf16[512,1664]{1,0:T(8,128)(2,1)}, u32[]{:S(2)}, u32[]{:S(2)}) collective-permute-start(bf16[512,1664]{1,0:T(8,128)(2,1)} %convolution_convert_fusion.2), channel_id=1, source_target_pairs={{0,16},{8,24},{16,0},{24,8},{1,17},{9,25},{17,1},{25,9},{2,18},{10... | collective-permute-start | bytes 5111816 | tf_op jit(solution)/shard_map/ppermute | solution.py:628
  953.5 193.8 %collective-permute-start.54 = (bf16[512,2048]{1,0:T(8,128)(2,1)}, bf16[512,2048]{1,0:T(8,128)(2,1)}, u32[]{:S(2)}, u32[]{:S(2)}) collective-permute-start(bf16[512,2048]{1,0:T(8,128)(2,1)} %get-tuple-element.166), channel_id=1, source_target_pairs={{0,4},{4,0},{1,5},{5,1},{2,6},{6,2},{3,7},{7,3},{8,12},{12,8},{9,1... | collective-permute-start | bytes 6291464 | tf_op jit(solution)/shard_map/ppermute | solution.py:628
  967.2 74.7 %collective-permute-start.84 = (bf16[256,1536]{1,0:T(8,128)(2,1)}, bf16[256,1536]{1,0:T(8,128)(2,1)}, u32[]{:S(2)}, u32[]{:S(2)}) collective-permute-start(bf16[256,1536]{1,0:T(8,128)(2,1)} %fusion.15), channel_id=1, source_target_pairs={{0,16},{8,24},{16,0},{24,8},{1,17},{9,25},{17,1},{25,9},{2,18},{10... | collective-permute-start | bytes 2359304 | tf_op jit(solution)/shard_map/ppermute | solution.py:628
  973.0 69.6 %collective-permute-start.83 = (bf16[256,1536]{1,0:T(8,128)(2,1)}, bf16[256,1536]{1,0:T(8,128)(2,1)}, u32[]{:S(2)}, u32[]{:S(2)}) collective-permute-start(bf16[256,1536]{1,0:T(8,128)(2,1)} %fusion.14), channel_id=1, source_target_pairs={{0,8},{8,0},{16,24},{24,16},{1,9},{9,1},{17,25},{25,17},{2,10},{10... | collective-permute-start | bytes 2359304 | tf_op jit(solution)/shard_map/ppermute | solution.py:628
  1036.2 39.6 %collective-permute-start.69 = (bf16[2,256,2048]{2,1,0:T(8,128)(2,1)}, bf16[2,256,2048]{2,1,0:T(8,128)(2,1)}, u32[]{:S(2)}, u32[]{:S(2)}) collective-permute-start(bf16[2,256,2048]{2,1,0:T(8,128)(2,1)} %constant_dynamic-slice_fusion.3), channel_id=1, source_target_pairs={{0,4},{4,0},{1,5},{5,1},{2,6},{6,2},{3,7},{7,3},{8,12},{12,8},{9,1... | collective-permute-start | bytes 6291464 | tf_op jit(solution)/shard_map/ppermute | solution.py:628
  1067.4 97.8 %all-to-all-start.1 = ((bf16[4,2112,128]{2,1,0:T(8,128)(2,1)}), bf16[4,2112,128]{2,1,0:T(8,128)(2,1)}, u32[]{:S(2)}, u32[]{:S(2)}) async-start(bf16[4,2112,128]{2,1,0:T(8,128)(2,1)} %copy.150), calls=%async_computation.4 | async-start | bytes 4325376 | tf_op jit(solution)/shard_map/all_to_all | solution.py:1067
  1102.5 58.2 %collective-permute-start.78 = (bf16[128,1664]{1,0:T(8,128)(2,1)}, bf16[128,1664]{1,0:T(8,128)(2,1)S(1)}, u32[]{:S(2)}, u32[]{:S(2)}) collective-permute-start(bf16[128,1664]{1,0:T(8,128)(2,1)} %get-tuple-element.343), channel_id=1, source_target_pairs={{0,1},{1,2},{2,3},{3,0},{4,5},{5,6},{6,7},{7,4},{8,9},{9,10},{10,1... | collective-permute-start | bytes 1277960 | tf_op jit(solution)/shard_map/ppermute | solution.py:633
  1102.6 58.2 %collective-permute-start.79 = (bf16[128,1664]{1,0:T(8,128)(2,1)}, bf16[128,1664]{1,0:T(8,128)(2,1)S(1)}, u32[]{:S(2)}, u32[]{:S(2)}) collective-permute-start(bf16[128,1664]{1,0:T(8,128)(2,1)} %get-tuple-element.342), channel_id=1, source_target_pairs={{0,2},{1,3},{2,0},{3,1},{4,6},{5,7},{6,4},{7,5},{8,10},{9,11},{10,... | collective-permute-start | bytes 1277960 | tf_op jit(solution)/shard_map/ppermute | solution.py:633
  1118.5 42.2 %collective-permute-start.80 = (bf16[128,1664]{1,0:T(8,128)(2,1)}, bf16[128,1664]{1,0:T(8,128)(2,1)S(1)}, u32[]{:S(2)}, u32[]{:S(2)}) collective-permute-start(bf16[128,1664]{1,0:T(8,128)(2,1)} %get-tuple-element.341), channel_id=1, source_target_pairs={{0,3},{1,0},{2,1},{3,2},{4,7},{5,4},{6,5},{7,6},{8,11},{9,8},{10,9... | collective-permute-start | bytes 1277960 | tf_op jit(solution)/shard_map/ppermute | solution.py:633
  1118.6 28.1 %collective-permute-start.74 = (f32[16640]{0:T(1024)S(1)}, f32[16640]{0:T(1024)S(1)}, u32[]{:S(2)}, u32[]{:S(2)}) collective-permute-start(f32[16640]{0:T(1024)S(1)} %add.320), channel_id=1, source_target_pairs={{0,1},{1,0},{2,3},{3,2},{4,5},{5,4},{6,7},{7,6},{8,9},{9,8},{10,11... | collective-permute-start | bytes 199688 | tf_op jit(solution)/shard_map/ppermute | solution.py:628
  (103 other events, 1147.8 us)
Sparse Core Ops, SparseCore 0:
  129.6 135.5 all-gather.5
  266.8 69.1 all-gather.3
  702.2 164.9 reduce-scatter.3
  869.4 111.7 reduce-scatter.7
  1046.4 48.2 reduce-scatter.5

commit v7 on v6

--- a/solution.py
+++ b/solution.py
@@ -705,16 +705,23 @@
     return [lax.dynamic_slice_in_dim(rows, (place ^ bit) * width, width, 1) for bit in range(4)]
 
 
-def line_sum(own, *late):
-    count, place = own.shape[0], lax.axis_index("fsdp")
-    total = lax.dynamic_index_in_dim(own, place, 0, keepdims=False)
-    arrived = []
-    for distance in range(1, count):
-        piece = lax.dynamic_index_in_dim(own, (place + distance) % count, 0, keepdims=False)
-        arrived.append(shift(low(piece), "fsdp", distance))
-    for part in lax.optimization_barrier(tuple(arrived) + late)[: len(arrived)]:
-        total = total + wide(part)
-    return total
+class Line:
+    def __init__(self, own):
+        count, place = lax.axis_size("fsdp"), lax.axis_index("fsdp")
+        own = own.reshape(count, own.shape[0] // count, own.shape[1])
+
+        def part(distance):
+            return lax.dynamic_index_in_dim(own, (place + distance) % count, 0, keepdims=False)
+
+        self.kept = part(0)
+        self.sent = [low(part(distance)) for distance in range(1, count)]
+        self.arrived = [shift(piece, "fsdp", distance + 1) for distance, piece in enumerate(self.sent)]
+
+    def total(self, *late):
+        total = self.kept
+        for part in lax.optimization_barrier(tuple(self.arrived) + late)[: len(self.arrived)]:
+            total = total + wide(part)
+        return total
 
 
 class Scatter:
@@ -742,19 +749,15 @@
         self.kept = (beside, across)
         return upper, lower
 
-    def finish(self, last, *ties):
+    def own(self, *ties):
         beside_upper, across_lower = self.last
-        if not last:
+        if ties:
             beside_upper, across_lower = lax.optimization_barrier(self.last + ties)[:2]
         beside, across = self.kept
         own = outer_rows(self.columns[0], self.grads)
         upper = own[: self.half] + wide(beside_upper) + across[self.half :]
         lower = own[self.half :] + beside[self.half :] + wide(across_lower)
-        own = jnp.concatenate([upper, lower], axis=0)
-        lines = lax.axis_size("fsdp")
-        if not last:
-            return wide(lax.psum_scatter(low(own), "fsdp", scatter_dimension=0, tiled=True))
-        return line_sum(own.reshape(lines, own.shape[0] // lines, own.shape[1]), *ties)
+        return jnp.concatenate([upper, lower], axis=0)
 
 
 def butterfly(value, axes):
@@ -882,13 +885,13 @@
     shards[0] = jnp.concatenate([shards[0], jnp.pad(low(beta_weight), ((0, 0), (0, spare)))], axis=1)
     shards.append(low(out_weight).T)
     lines = []
-    for shard in shards:
+    for shard in shards[:parts]:
         lines.append(gather_line(tie(shard, lines[-1]) if lines else shard))
     units = units_here // 4
     pieces = jnp.stack([low(gate_weight).T, low(up_weight).T, low(down_weight)])
     pieces = pieces.reshape(3, 4, units, shard_rows).transpose(1, 0, 2, 3)
-    ffn_line = lax.all_to_all(pieces.reshape(4, 3 * units, shard_rows), "ctx", 0, 0)
-    ffn_line = ffn_line.transpose(1, 0, 2).reshape(3 * units, 4 * shard_rows)
+    ffn_swapped = lax.all_to_all(pieces.reshape(4, 3 * units, shard_rows), "ctx", 0, 0)
+    ffn_line = ffn_swapped.transpose(1, 0, 2).reshape(3 * units, 4 * shard_rows)
     line_count = lax.axis_size("fsdp")
 
     ctx_place = lax.axis_index("ctx")
@@ -904,56 +907,52 @@
     inputs_mine = wide(rows_mine(block_input).reshape(-1, width))
     grads_mine = rows_mine(out_grad).reshape(-1, width)
 
-    square = Square(tie(lines[0], ffn_line)).forward()
+    square = Square(tie(lines[0], ffn_swapped)).forward()
     gate_up_parts = lax.all_gather(tie(ffn_line[: 2 * units], lines[parts - 1], *square.done()), "fsdp", axis=0)
     down_parts = lax.all_gather(ffn_line[2 * units :], "fsdp", axis=0)
     mix_full, kept, pre = [], [], []
     for p in range(parts):
         mix_full.append(square.pieces())
         square = Square(tie(lines[p + 1], *square.done()))
-        rows = normed_mix
-        ends = rows.reshape(seq_count, local_len, width)[:, local_len - HALO :].reshape(seq_count * HALO, width)
-        ends = gathered_times(ends, ctx_place, mix_full[p])[:, :part_cols]
-        halo = from_behind(ends.reshape(seq_count, HALO, part_cols), "ctx", 1)
-        pre.append(gathered_times(tie(rows, ends), ctx_place, mix_full[p]))
+        ends = normed_mix.reshape(seq_count, local_len, width)[:, local_len - HALO :].reshape(seq_count * HALO, width)
+        ends = gathered_times(ends, ctx_place, mix_full[p])
+        halo = from_behind(ends[:, :part_cols].reshape(seq_count, HALO, part_cols), "ctx", 1)
+        pre.append(gathered_times(tie(normed_mix, ends), ctx_place, mix_full[p]))
         convs = conv[:, p * part_cols : (p + 1) * part_cols]
-        held = pre[p]
-        if p > 0:
-            held = tie(held, grad_square.beside, grad_square.across)
         kept.append(
             [halo, convs]
             + list(
                 mixer_forward(
-                    held, pre[0], bias, halo, convs, col, row, taps, p * part_heads, part_heads, group
+                    pre[p], pre[0], bias, halo, convs, col, row, taps, p * part_heads, part_heads, group
                 )
             )
         )
-        square.forward(kept[p][2], lines[-1])
+        square.forward(kept[p][2])
         if p == 0:
-            grad_square = Square(tie(grads_mine, kept[p][2], square.beside, square.across))
+            lines.append(gather_line(tie(shards[-1], kept[p][2], square.beside)))
+            grad_square = Square(tie(grads_mine, kept[p][2], *square.done()))
+    out_full = square.pieces()
+
+    gate_up_full = columns_join(gate_up_parts, 4)
+    finals = jnp.concatenate([some[4] for some in kept], axis=1)
+    transfer = low(finals[..., LANES:])
+    first = tie(finals[..., :LANES], gate_up_parts, grad_square.beside, grad_square.across)
+    entering = pass_states(first, transfer, 1)
+    entered = [entering[:, p * part_heads : (p + 1) * part_heads] for p in range(parts)]
+    grad_square.forward(entering)
+    grad_rows = [both_sides(part) for part in (grad_square.own, grad_square.beside, grad_square.across)]
+    mixed_rows = []
+    for p in range(parts):
+        own, carry = kept[p][2:4]
         if p == parts - 1:
-            grad_square.forward()
-    out_full = square.pieces()
-
-    entered, transfers, mixed_rows = [], [], []
-    for _, _, own, carry, final, _, _, _ in kept:
-        transfers.append(low(final[..., LANES:]))
-        first = final[..., :LANES]
-        if len(entered) == parts - 1:
-            first, gate_up_parts = lax.optimization_barrier((first, gate_up_parts) + grad_square.done())[:2]
-            gate_up_full = columns_join(gate_up_parts, 4)
-        entered.append(pass_states(first, transfers[-1], 1))
-        if len(entered) == parts:
-            carry = tie(carry, gate_up_full)
-        mixed_rows.append(mixer_output(own, carry, entered[-1], gain_head, group))
+            own = tie(own, gate_up_full)
+        mixed_rows.append(mixer_output(own, carry, entered[p], gain_head, group))
     mixed_rows = jnp.concatenate(mixed_rows, axis=1)
-    grad_rows = [
-        both_sides(part) for part in (grad_square.own, grad_square.beside, grad_square.across, grad_square.far())
-    ]
     mixed_rows = tie(mixed_rows, *(other for _, other in grad_rows))
+    grad_rows.append(both_sides(grad_square.far()))
 
     branch = gathered_times_transposed([mixed_rows], ctx_place, [out_full]).reshape(seq_count, local_len, width)
-    branch, down_parts = lax.optimization_barrier((branch, down_parts))
+    branch = tie(branch, down_parts)
     residual = inputs_mine + rows_scatter(branch).reshape(-1, width)
     scale_ffn = rms_scale(residual, EPSILON)
     square = Square(low(residual * scale_ffn * gain_ffn))
@@ -1006,7 +1005,7 @@
         backs.append(back)
         acrosses.append(across)
         gain_o_part = gain_o_part + jnp.sum(gain_part, axis=(0, 1, 2))
-    grad_end = pass_states(jnp.concatenate(acrosses, axis=1), jnp.concatenate(transfers, axis=1), -1, *result_near)
+    grad_end = pass_states(jnp.concatenate(acrosses, axis=1), transfer, -1, *result_near)
     total = lax.psum_scatter(sums, "fsdp", scatter_dimension=0, tiled=True)
 
     out_grad_w = low(outer_rows(grad_branch, mixed_rows))
@@ -1043,7 +1042,7 @@
         scatter = Scatter(columns, grad_mix)
     ready = scatter.second()
     grad_mixes[0] = tie(grad_mixes[0], *ready)
-    mix_back = gathered_times_transposed(grad_mixes, ctx_place, mix_full)
+    mix_back = tie(gathered_times_transposed(grad_mixes, ctx_place, mix_full), *scatter.last)
     mix_back = rows_scatter(mix_back.reshape(seq_count, local_len, width)).reshape(-1, width)
     back_mix, unit_mix = norm_backward(mix_back, inputs_mine, rms_scale(inputs_mine, EPSILON), gain_mix)
     input_grad = rows_full(low(grad_residual + back_mix).reshape(seq_count, -1, width))
@@ -1053,9 +1052,11 @@
     gains = butterfly(jnp.concatenate([gain_mix_part, gain_ffn_part, gain_o_part]), ("tp",))
     sums = jnp.concatenate([gains, conv_cols.reshape(-1), jnp.sum(logits, axis=0)])
     for p in range(1, parts):
-        mix_grads[p] = earlier_scatter.finish(False, *ready)
-    sums = butterfly(sums, ("ctx", "fsdp"))
-    mix_grads[0] = scatter.finish(True, sums)
+        own = low(earlier_scatter.own(*ready))
+        mix_grads[p] = wide(lax.psum_scatter(own, "fsdp", scatter_dimension=0, tiled=True))
+    last_line = Line(scatter.own())
+    sums = butterfly(tie(sums, *last_line.sent), ("ctx", "fsdp"))
+    mix_grads[0] = last_line.total(sums)
     query_grad, key_grad, value_grad = by_kind([grad[:, :part_cols] for grad in mix_grads])
     beta_grad = mix_grads[0][:, part_cols : part_cols + heads_here]
     ends = [width, 2 * width, 2 * width + LANES, sums.shape[0] - LANES]

time: 1200 us -> 1150 us (0.958)
  waiting for transfers between devices: 353 us -> 327 us
  starting transfers between devices: 152 us -> 134 us
  matrix products: 54.7 us -> 41.2 us
  local copies, waits for them, and re-layouts: 95.8 us -> 108 us
    ppermute x12, waiting for transfers between devices: 52.6 us -> 27.7 us  [shift(): lax.ppermute(value, axis, [(i, (i + distance) % count) for i in range(cou...]
    ppermute x13 -> x10, starting transfers between devices: 35.7 us -> 21.5 us  [from_behind(): return lax.ppermute(block, axis, route)]
    unnamed x198 -> x221, local copies, waits for them, and re-layouts: 19.8 us -> 33.7 us
    ppermute x13 -> x10, waiting for transfers between devices: 102 us -> 88.3 us  [from_behind(): return lax.ppermute(block, axis, route)]
    ppermute x12, starting transfers between devices: 47.9 us -> 35.4 us  [shift(): lax.ppermute(value, axis, [(i, (i + distance) % count) for i in range(cou...]
  transfers between devices with their start and end apart: 92 -> 89, of which waited for: 35 -> 36; matrix products, arithmetic and copies ran while one was open for 19% -> 19% of each run, Pallas kernels for 31% -> 34%
where the time goes in v7:
time: 1150 us
  Pallas kernels  394 us (34%)
  waiting for transfers between devices  327 us (28%)
  starting transfers between devices  134 us (12%)
  other arithmetic  124 us (11%)
  local copies, waits for them, and re-layouts  108 us (9%)
  matrix products  41.2 us (4%)
  between operations  15.9 us (1%)
    ppermute x60, waiting for transfers between devices, flip(): return lax.ppermute(value, axis, [(i, i ^ bit) for i in devices])  203 us
    pallas_call x4, Pallas kernels, ffn_both(): pl.pallas_call(ffn_kernel, grid=(count // tile,), in_specs=[wide_rows] *...  118 us
    ppermute x10, waiting for transfers between devices, from_behind(): return lax.ppermute(block, axis, route)  88.3 us
    ppermute x60, starting transfers between devices, flip(): return lax.ppermute(value, axis, [(i, i ^ bit) for i in devices])  67.4 us
    pallas_call x2, Pallas kernels, mixer_backward(): pl.pallas_call(functools.partial(backward_kernel, taps, group, first), gr...  66.9 us
    pallas_call x2, Pallas kernels, mixer_forward(): pl.pallas_call(functools.partial(forward_kernel, taps, group, first), gri...  55.1 us
    pallas_call x1, Pallas kernels, ffn_weights(): pl.pallas_call(functools.partial(ffn_weights_kernel, count, lines), grid=...  47.9 us
    convert_element_type x17, other arithmetic, low(): return value.astype(jnp.bfloat16)  46.9 us
  transfers between devices with their start and end apart: 89, of which 36 were waited for; matrix products, arithmetic and copies ran while one was open for 19% of the time, Pallas kernels for 34%

profile of v7, /device:TPU:0, one launch (start us, length us, event | category | flops | bytes accessed | tf_op | source)
XLA Modules:
  0.0 1145.0 jit_solution(2390514492814667578)
XLA Ops:
  12.6 5.3 all-to-all-start
  27.8 9.3 collective-permute-done
  37.1 17.1 %collective-permute-done.1 = bf16[128,1664]{1,0:T(8,128)(2,1)S(1)} collective-permute-done((bf16[128,1664]{1,0:T(8,128)(2,1)}, bf16[128,1664]{1,0:T(8,128)(2,1)S(1)}, u32[]{:S(2)}, u32[]{:S(2)}) %collective-permute-start.1) | collective-permute-done | bytes 426016 | tf_op jit(solution)/shard_map/ppermute | solution.py:633
  60.1 10.6 collective-permute-start.10
  71.3 24.9 %collective-permute-done.3.refs_1_.refs_3_ = bf16[512,1664]{1,0:T(8,128)(2,1)S(1)} collective-permute-done((bf16[512,1664]{1,0:T(8,128)(2,1)}, bf16[512,1664]{1,0:T(8,128)(2,1)S(1)}, u32[]{:S(2)}, u32[]{:S(2)}) %collective-permute-start.3) | collective-permute-done | bytes 1703968 | tf_op jit(solution)/shard_map/ppermute | solution.py:628
  110.2 8.4 collective-permute-done.5.refs_3_.refs_5_
  122.4 6.7 convert_element_type.394
  133.5 5.5 fusion.1.rows
  141.4 4.6 shard_map.271
  149.5 12.8 %shard_map.272.pre.beta = f32[1024,1664]{1,0:T(8,128)} custom-call(s32[1]{0:T(128)} %bitcast.1.place, bf16[1024,2048]{1,0:T(8,128)(2,1)} %fusion.1.rows, bf16[512,1664]{1,0:T(8,128)(2,1)} %pad_maximum_fusion.6.refs_0_.refs_2_, bf16[512,1664]{1,0:T(8,128)(2,1)} %copy-done.24, bf16[512,1664]{1,0:T(8,128)(2,1)} %copy-done.25, bf16[256,1664]{1,0:T(8,128)(2,1)} %copy-done.36, ...), custom_call_target="tpu_custom_call" | custom-call | flops 6979321856 | bytes 11010048 | tf_op jit(solution)/shard_map/pallas_call | solution.py:551
  162.3 11.8 %collective-permute-done.7.halo = f32[2,8,1536]{2,1,0:T(8,128)S(1)} collective-permute-done((f32[2,8,1536]{2,1,0:T(8,128)S(1)}, f32[2,8,1536]{2,1,0:T(8,128)S(1)}, u32[]{:S(2)}, u32[]{:S(2)}) %collective-permute-start.7) | collective-permute-done | bytes 98336 | tf_op jit(solution)/shard_map/ppermute | solution.py:639
  174.8 27.5 %shard_map.273 = (f32[1024,512]{1,0:T(8,128)}, bf16[1024,512]{1,0:T(8,128)(2,1)}, f32[2,4,128,256]{3,2,1,0:T(8,128)}, bf16[2,4,4,128,128]{4,3,2,1,0:T(8,128)(2,1...) custom-call(f32[1024,1664]{1,0:T(8,128)} %shard_map.272.pre.beta, ...), custom_call_target="tpu_custom_call" | custom-call | flops 4026531840 | bytes 20971520 | tf_op jit(solution)/shard_map/pallas_call | solution.py:160
  210.2 12.5 %collective-permute-done.13.refs_3_.refs_10_ = bf16[256,1536]{1,0:T(8,128)(2,1)S(1)} collective-permute-done((bf16[256,1536]{1,0:T(8,128)(2,1)}, bf16[256,1536]{1,0:T(8,128)(2,1)S(1)}, u32[]{:S(2)}, u32[]{:S(2)}) %collective-permute-start.13) | collective-permute-done | bytes 786464 | tf_op jit(solution)/shard_map/ppermute | solution.py:628
  234.2 9.7 collective-permute-start.24
  244.0 4.8 shard_map.274
  250.7 11.5 %shard_map.275.pre = f32[1024,1536]{1,0:T(8,128)} custom-call(s32[1]{0:T(128)} %bitcast.1.place, bf16[1024,2048]{1,0:T(8,128)(2,1)} %fusion.1.rows, bf16[512,1536]{1,0:T(8,128)(2,1)} %pad_maximum_fusion.7.refs_0_.refs_7_, bf16[512,1536]{1,0:T(8,128)(2,1)} %copy-done.26, bf16[512,1536]{1,0:T(8,128)(2,1)} %collective-permute-done.12.refs_2_.refs_9_, ...), custom_call_target="tpu_custom_call" | custom-call | flops 6442450944 | bytes 10485760 | tf_op jit(solution)/shard_map/pallas_call | solution.py:551
  262.2 7.4 collective-permute-done.15.halo
  269.5 5.1 collective-permute-start.26
  274.6 27.5 %shard_map.276 = (f32[1024,512]{1,0:T(8,128)}, bf16[1024,512]{1,0:T(8,128)(2,1)}, f32[2,4,128,256]{3,2,1,0:T(8,128)}, bf16[2,4,4,128,128]{4,3,2,1,0:T(8,128)(2,1...) custom-call(f32[1024,1536]{1,0:T(8,128)} %shard_map.275.pre, ...), custom_call_target="tpu_custom_call" | custom-call | flops 4026531840 | bytes 20971520 | tf_op jit(solution)/shard_map/pallas_call | solution.py:160
  305.8 8.4 copy.142
  320.1 8.1 collective-permute-done.18
  336.5 5.5 collective-permute-done.19
  341.9 7.7 collective-permute-start.28
  350.0 15.8 %collective-permute-done.27.refs_2_.refs_1_ = bf16[512,1024]{1,0:T(8,128)(2,1)S(1)} collective-permute-done((bf16[512,1024]{1,0:T(8,128)(2,1)S(1)}, bf16[512,1024]{1,0:T(8,128)(2,1)S(1)}, u32[]{:S(2)}, u32[]{:S(2)}) %collective-permute-start.27) | collective-permute-done | bytes 1048608 | tf_op jit(solution)/shard_map/ppermute | solution.py:628
  369.0 8.6 collective-permute-start.29
  379.0 8.0 shard_map.278.gate_w.up_w
  388.1 4.5 shard_map.277
  392.6 4.6 shard_map.279
  400.0 8.7 shard_map.280
  422.7 4.5 shard_map.281.down_w
  429.3 29.4 %shard_map.282 = (bf16[3,512,704]{2,1,0:T(8,128)(2,1)}, bf16[512,2048]{1,0:T(8,128)(2,1)}, bf16[512,2048]{1,0:T(8,128)(2,1)}, bf16[3,512,704]{2,1,0:T(8,128)(2,1...) custom-call(bf16[512,2048]{1,0:T(8,128)(2,1)} %copy-done.33, ...), custom_call_target="tpu_custom_call" | custom-call | flops 17716740096 | bytes 25427968 | tf_op jit(solution)/shard_map/pallas_call | solution.py:469
  458.7 11.2 collective-permute-done.34.mine.refs_10_
  469.9 5.3 collective-permute-done.38.mine.refs_12_
  487.6 29.4 %shard_map.283 = (bf16[3,512,704]{2,1,0:T(8,128)(2,1)}, bf16[512,2048]{1,0:T(8,128)(2,1)}, bf16[512,2048]{1,0:T(8,128)(2,1)}, bf16[3,512,704]{2,1,0:T(8,128)(2,1...) custom-call(bf16[512,2048]{1,0:T(8,128)(2,1)} %collective-permute-done.34.mine.refs_10_, ...), custom_call_target="tpu_custom_call" | custom-call | flops 17716740096 | bytes 25427968 | tf_op jit(solution)/shard_map/pallas_call | solution.py:469
  517.0 10.2 collective-permute-done.39
  528.5 29.7 %shard_map.284 = (bf16[3,512,704]{2,1,0:T(8,128)(2,1)}, bf16[512,2048]{1,0:T(8,128)(2,1)}, bf16[512,2048]{1,0:T(8,128)(2,1)}, bf16[3,512,704]{2,1,0:T(8,128)(2,1...) custom-call(bf16[512,2048]{1,0:T(8,128)(2,1)} %collective-permute-done.38.mine.refs_12_, ...), custom_call_target="tpu_custom_call" | custom-call | flops 17716740096 | bytes 25427968 | tf_op jit(solution)/shard_map/pallas_call | solution.py:469
  572.8 29.5 %shard_map.285 = (bf16[3,512,704]{2,1,0:T(8,128)(2,1)}, bf16[512,2048]{1,0:T(8,128)(2,1)}, bf16[512,2048]{1,0:T(8,128)(2,1)}, bf16[3,512,704]{2,1,0:T(8,128)(2,1...) custom-call(bf16[512,2048]{1,0:T(8,128)(2,1)} %copy-done.42, ...), custom_call_target="tpu_custom_call" | custom-call | flops 17716740096 | bytes 25427968 | tf_op jit(solution)/shard_map/pallas_call | solution.py:469
  602.3 10.9 collective-permute-done.43
  613.2 5.7 collective-permute-done.37
  627.6 47.9 %shard_map.286 = bf16[4,3,704,512]{3,2,1,0:T(8,128)(2,1)} custom-call(bf16[3,512,704]{2,1,0:T(8,128)(2,1)} %get-tuple-element.160.refs_0_, bf16[3,512,704]{2,1,0:T(8,128)(2,1)} %get-tuple-element.161.refs_1_, bf16[3,512,704]{2,1,0:T(8,128)(2,1)} %get-tuple-element.148.refs_2_, bf16[3,512,704]{2,1,0:T(8,128)(2,1)} %get-tuple-element.162.refs_3_, ...), custom_call_target="tpu_custom_call" | custom-call | flops 35433480192 | bytes 67108864 | tf_op jit(solution)/shard_map/pallas_call | solution.py:516
  675.8 11.7 %copy.147 = bf16[4,2112,512]{1,2,0:T(8,128)(2,1)} copy(bf16[4,2112,512]{2,1,0:T(8,128)(2,1)} %bitcast.153) | data formatting | bytes 17301504 | tf_op jit(solution)/shard_map/optimization_barrier | solution.py:987
  689.7 6.6 collective-permute-done.33
  696.3 6.5 multiply_reduce_fusion.1
  705.8 4.6 add_convert_fusion.2
  722.1 8.9 shard_map.287.grad
  731.0 5.7 shard_map.288
  736.7 5.8 shard_map.289
  745.2 29.3 %collective-permute-done.57 = bf16[2,8,128,128]{3,2,1,0:T(8,128)(2,1)S(1)} collective-permute-done((bf16[2,8,128,128]{3,2,1,0:T(8,128)(2,1)S(1)}, bf16[2,8,128,128]{3,2,1,0:T(8,128)(2,1)S(1)}, u32[]{:S(2)}, u32[]{:S(2)}) %collective-permute-start.57) | collective-permute-done | bytes 524320 | tf_op jit(solution)/shard_map/ppermute | solution.py:639
  777.0 14.0 %collective-permute-done.58 = bf16[2,8,128,128]{3,2,1,0:T(8,128)(2,1)} collective-permute-done((bf16[2,8,128,128]{3,2,1,0:T(8,128)(2,1)}, bf16[2,8,128,128]{3,2,1,0:T(8,128)(2,1)}, u32[]{:S(2)}, u32[]{:S(2)}) %collective-permute-start.58) | collective-permute-done | bytes 524320 | tf_op jit(solution)/shard_map/ppermute | solution.py:639
  797.9 9.3 collective-permute-done.59
  809.6 33.7 %shard_map.290 = (bf16[1024,1536]{1,0:T(8,128)(2,1)}, f32[2,8,1536]{2,1,0:T(8,128)}, f32[2,8,1536]{2,1,0:T(8,128)}, f32[2,8,1536]{2,1,0:T(8,128)}, f32[1024,128]{1,0:T(8,128)}) custom-call(f32[1024,1536]{1,0:T(8,128)} %shard_map.275.pre, f32[1024,1664]{1,0:T(8,128)} %shard_map.272.pre.beta, f32[1,128]{1,0:T(1,128)} %pad_bitcast_fusion.bias, ...), custom_call_target="tpu_custom_call" | custom-call | flops 4026531840 | bytes 20971520 | tf_op jit(solution)/shard_map/pallas_call | solution.py:318
  844.6 9.4 convolution_convert_fusion
  856.0 5.1 convolution_convert_fusion.3
  872.2 5.8 fusion.26
  878.0 33.2 %shard_map.291 = (bf16[1024,1536]{1,0:T(8,128)(2,1)}, f32[2,8,1536]{2,1,0:T(8,128)}, f32[2,8,1536]{2,1,0:T(8,128)}, f32[2,8,1536]{2,1,0:T(8,128)}, f32[1024,128]{1,0:T(8,128)}) custom-call(f32[1024,1664]{1,0:T(8,128)} %shard_map.272.pre.beta, f32[1024,1664]{1,0:T(8,128)} %shard_map.272.pre.beta, f32[1,128]{1,0:T(1,128)} %pad_bitcast_fusion.bias, ...), custom_call_target="tpu_custom_call" | custom-call | flops 4026531840 | bytes 20971520 | tf_op jit(solution)/shard_map/pallas_call | solution.py:318
  915.6 8.4 collective-permute-done.79
  923.9 11.4 collective-permute-done.78
  960.8 26.4 %collective-permute-done.65 = bf16[512,1664]{1,0:T(8,128)(2,1)S(1)} collective-permute-done((bf16[512,1664]{1,0:T(8,128)(2,1)S(1)}, bf16[512,1664]{1,0:T(8,128)(2,1)S(1)}, u32[]{:S(2)}, u32[]{:S(2)}) %collective-permute-start.65) | collective-permute-done | bytes 1703968 | tf_op jit(solution)/shard_map/ppermute | solution.py:628
  993.1 13.5 %collective-permute-done.81 = bf16[256,1536]{1,0:T(8,128)(2,1)} collective-permute-done((bf16[256,1536]{1,0:T(8,128)(2,1)S(1)}, bf16[256,1536]{1,0:T(8,128)(2,1)}, u32[]{:S(2)}, u32[]{:S(2)}) %collective-permute-start.81) | collective-permute-done | bytes 786464 | tf_op jit(solution)/shard_map/ppermute | solution.py:628
  1006.6 21.4 %shard_map.292 = bf16[1024,2048]{1,0:T(8,128)(2,1)} custom-call(s32[1]{0:T(128)} %bitcast.1.place, bf16[1024,1664]{1,0:T(8,128)(2,1)} %pad_maximum_fusion.3.refs_0_, bf16[1024,1536]{1,0:T(8,128)(2,1)} %bitcast.147, bf16[512,1664]{1,0:T(8,128)(2,1)} %pad_maximum_fusion.6.refs_0_.refs_2_, bf16[512,1664]{1,0:T(8,128)(2,1)} %copy-done.24, ...), custom_call_target="tpu_custom_call" | custom-call | flops 13421772800 | bytes 17301504 | tf_op jit(solution)/shard_map/pallas_call | solution.py:587
  1057.7 5.8 fusion.9
  1063.6 8.0 all-to-all-done.1
  1087.2 10.0 collective-permute-done.73
  1099.7 12.5 %fusion.5 = (bf16[512,2048]{1,0:T(8,128)(2,1)}, bf16[512,2048]{1,0:T(8,128)(2,1)}) fusion(f32[2,256,2048]{2,1,0:T(8,128)} %get-tuple-element.331, f32[512]{0:T(512)S(1)} %bitcast.196, f32[2048]{0:T(1024)S(1)} %copy-done.58, f32[512]{0:T(512)} %bitcast.195, bf16[2,512,2048]{2,1,0:T(8,128)(2,1)} %param.16, s32[]{:T(128)S(6)} %select_n.389, f32[512]{0:T(512)} %copy-done.69, ...), kind=kLoop, calls=%fused_computation.11 | loop fusion | flops 27262976 | bytes 31481860 | tf_op jit(solution)/shard_map/convert_element_type | solution.py:19
  (503 shorter events, 305.5 us)
Async XLA Ops:
  12.6 44.5 %all-to-all-start = ((bf16[4,2112,128]{2,1,0:T(8,128)(2,1)}), bf16[4,2112,128]{2,1,0:T(8,128)(2,1)S(1)}, u32[]{:S(2)}, u32[]{:S(2)}) async-start(bf16[4,2112,128]{2,1,0:T(8,128)(2,1)} %bitcast.156), calls=%async_computation | async-start | bytes 4325376 | tf_op jit(solution)/shard_map/all_to_all | solution.py:893
  17.8 287.9 %all-gather.6.cloned.1.call-start = ((), (), s32[]{:S(2)}) async-start(), calls=%async_computation.9 | async-start | bytes 7208960 | tf_op jit(solution)/shard_map/all_gather | solution.py:911
  23.8 30.4 %collective-permute-start.1 = (bf16[128,1664]{1,0:T(8,128)(2,1)}, bf16[128,1664]{1,0:T(8,128)(2,1)S(1)}, u32[]{:S(2)}, u32[]{:S(2)}) collective-permute-start(bf16[128,1664]{1,0:T(8,128)(2,1)} %constant_dynamic-update-slice_fusion), channel_id=1, source_target_pairs={{0,2},{1,3},{2,0},{3,1},{4,6},{5,7},{6,4},{7,5},{8,10},{9,11},{10,... | collective-permute-start | bytes 1277960 | tf_op jit(solution)/shard_map/ppermute | solution.py:633
  26.4 27.8 %collective-permute-start.2 = (bf16[128,1664]{1,0:T(8,128)(2,1)}, bf16[128,1664]{1,0:T(8,128)(2,1)}, u32[]{:S(2)}, u32[]{:S(2)}) collective-permute-start(bf16[128,1664]{1,0:T(8,128)(2,1)} %constant_dynamic-update-slice_fusion), channel_id=1, source_target_pairs={{0,3},{1,0},{2,1},{3,2},{4,7},{5,4},{6,5},{7,6},{8,11},{9,8},{10,9... | collective-permute-start | bytes 1277960 | tf_op jit(solution)/shard_map/ppermute | solution.py:633
  57.0 39.2 %collective-permute-start.3 = (bf16[512,1664]{1,0:T(8,128)(2,1)}, bf16[512,1664]{1,0:T(8,128)(2,1)S(1)}, u32[]{:S(2)}, u32[]{:S(2)}) collective-permute-start(bf16[512,1664]{1,0:T(8,128)(2,1)} %pad_maximum_fusion.6.refs_0_.refs_2_), channel_id=1, source_target_pairs={{0,8},{8,0},{16,24},{24,16},{1,9},{9,1},{17,25},{25,17},{2,10},{10... | collective-permute-start | bytes 5111816 | tf_op jit(solution)/shard_map/ppermute | solution.py:628
  58.7 41.5 %collective-permute-start.4 = (bf16[512,1664]{1,0:T(8,128)(2,1)}, bf16[512,1664]{1,0:T(8,128)(2,1)S(1)}, u32[]{:S(2)}, u32[]{:S(2)}) collective-permute-start(bf16[512,1664]{1,0:T(8,128)(2,1)} %pad_maximum_fusion.6.refs_0_.refs_2_), channel_id=1, source_target_pairs={{0,16},{8,24},{16,0},{24,8},{1,17},{9,25},{17,1},{25,9},{2,18},{10... | collective-permute-start | bytes 5111816 | tf_op jit(solution)/shard_map/ppermute | solution.py:628
  60.1 43.7 %collective-permute-start.10 = (bf16[128,1536]{1,0:T(8,128)(2,1)S(1)}, bf16[128,1536]{1,0:T(8,128)(2,1)S(1)}, u32[]{:S(2)}, u32[]{:S(2)}) collective-permute-start(bf16[128,1536]{1,0:T(8,128)(2,1)S(1)} %copy-done.52), channel_id=1, source_target_pairs={{0,3},{1,0},{2,1},{3,2},{4,7},{5,4},{6,5},{7,6},{8,11},{9,8},{10,9... | collective-permute-start | bytes 1179656 | tf_op jit(solution)/shard_map/ppermute | solution.py:633
  70.8 33.0 %collective-permute-start.8 = (bf16[128,1536]{1,0:T(8,128)(2,1)S(1)}, bf16[128,1536]{1,0:T(8,128)(2,1)S(1)}, u32[]{:S(2)}, u32[]{:S(2)}) collective-permute-start(bf16[128,1536]{1,0:T(8,128)(2,1)S(1)} %copy-done.52), channel_id=1, source_target_pairs={{0,1},{1,2},{2,3},{3,0},{4,5},{5,6},{6,7},{7,4},{8,9},{9,10},{10,1... | collective-permute-start | bytes 1179656 | tf_op jit(solution)/shard_map/ppermute | solution.py:633
  70.8 34.3 %collective-permute-start.9 = (bf16[128,1536]{1,0:T(8,128)(2,1)S(1)}, bf16[128,1536]{1,0:T(8,128)(2,1)S(1)}, u32[]{:S(2)}, u32[]{:S(2)}) collective-permute-start(bf16[128,1536]{1,0:T(8,128)(2,1)S(1)} %copy-done.52), channel_id=1, source_target_pairs={{0,2},{1,3},{2,0},{3,1},{4,6},{5,7},{6,4},{7,5},{8,10},{9,11},{10,... | collective-permute-start | bytes 1179656 | tf_op jit(solution)/shard_map/ppermute | solution.py:633
  98.5 20.1 %collective-permute-start.5 = (bf16[256,1664]{1,0:T(8,128)(2,1)}, bf16[256,1664]{1,0:T(8,128)(2,1)S(1)}, u32[]{:S(2)}, u32[]{:S(2)}) collective-permute-start(bf16[256,1664]{1,0:T(8,128)(2,1)} %slice.625), channel_id=1, source_target_pairs={{0,16},{8,24},{16,0},{24,8},{1,17},{9,25},{17,1},{25,9},{2,18},{10... | collective-permute-start | bytes 2555912 | tf_op jit(solution)/shard_map/ppermute | solution.py:628
  102.3 19.9 %collective-permute-start.6 = (bf16[256,1664]{1,0:T(8,128)(2,1)}, bf16[256,1664]{1,0:T(8,128)(2,1)}, u32[]{:S(2)}, u32[]{:S(2)}) collective-permute-start(bf16[256,1664]{1,0:T(8,128)(2,1)} %slice.626), channel_id=1, source_target_pairs={{0,8},{8,0},{16,24},{24,16},{1,9},{9,1},{17,25},{25,17},{2,10},{10... | collective-permute-start | bytes 2555912 | tf_op jit(solution)/shard_map/ppermute | solution.py:628
  122.3 286.4 %all-gather.4.cloned.1.call-start = ((), (), s32[]{:S(2)}) async-start(), calls=%async_computation.5 | async-start | bytes 3604480 | tf_op jit(solution)/shard_map/all_gather | solution.py:912
  139.0 63.3 %collective-permute-start.11 = (bf16[512,1536]{1,0:T(8,128)(2,1)S(1)}, bf16[512,1536]{1,0:T(8,128)(2,1)S(1)}, u32[]{:S(2)}, u32[]{:S(2)}) collective-permute-start(bf16[512,1536]{1,0:T(8,128)(2,1)S(1)} %copy-done.21), channel_id=1, source_target_pairs={{0,8},{8,0},{16,24},{24,16},{1,9},{9,1},{17,25},{25,17},{2,10},{10... | collective-permute-start | bytes 4718600 | tf_op jit(solution)/shard_map/ppermute | solution.py:628
  140.4 62.9 %collective-permute-start.12 = (bf16[512,1536]{1,0:T(8,128)(2,1)S(1)}, bf16[512,1536]{1,0:T(8,128)(2,1)}, u32[]{:S(2)}, u32[]{:S(2)}) collective-permute-start(bf16[512,1536]{1,0:T(8,128)(2,1)S(1)} %copy-done.21), channel_id=1, source_target_pairs={{0,16},{8,24},{16,0},{24,8},{1,17},{9,25},{17,1},{25,9},{2,18},{10... | collective-permute-start | bytes 4718600 | tf_op jit(solution)/shard_map/ppermute | solution.py:628
  146.9 27.2 %collective-permute-start.7 = (f32[2,8,1536]{2,1,0:T(8,128)S(1)}, f32[2,8,1536]{2,1,0:T(8,128)S(1)}, u32[]{:S(2)}, u32[]{:S(2)}) collective-permute-start(f32[2,8,1536]{2,1,0:T(8,128)S(1)} %slice_bitcast_fusion), channel_id=1, source_target_pairs={{0,8},{8,16},{16,24},{1,9},{9,17},{17,25},{2,10},{10,18},{18,26},{... | collective-permute-start | bytes 294920 | tf_op jit(solution)/shard_map/ppermute | solution.py:639
  205.4 17.2 %collective-permute-start.13 = (bf16[256,1536]{1,0:T(8,128)(2,1)}, bf16[256,1536]{1,0:T(8,128)(2,1)S(1)}, u32[]{:S(2)}, u32[]{:S(2)}) collective-permute-start(bf16[256,1536]{1,0:T(8,128)(2,1)} %slice.652), channel_id=1, source_target_pairs={{0,16},{8,24},{16,0},{24,8},{1,17},{9,25},{17,1},{25,9},{2,18},{10... | collective-permute-start | bytes 2359304 | tf_op jit(solution)/shard_map/ppermute | solution.py:628
  208.0 17.9 %collective-permute-start.14 = (bf16[256,1536]{1,0:T(8,128)(2,1)}, bf16[256,1536]{1,0:T(8,128)(2,1)}, u32[]{:S(2)}, u32[]{:S(2)}) collective-permute-start(bf16[256,1536]{1,0:T(8,128)(2,1)} %slice.653), channel_id=1, source_target_pairs={{0,8},{8,0},{16,24},{24,16},{1,9},{9,1},{17,25},{25,17},{2,10},{10... | collective-permute-start | bytes 2359304 | tf_op jit(solution)/shard_map/ppermute | solution.py:628
  225.9 88.3 %collective-permute-start.16 = (bf16[512,2048]{1,0:T(8,128)(2,1)S(1)}, bf16[512,2048]{1,0:T(8,128)(2,1)}, u32[]{:S(2)}, u32[]{:S(2)}) collective-permute-start(bf16[512,2048]{1,0:T(8,128)(2,1)S(1)} %bitcast.139), channel_id=1, source_target_pairs={{0,8},{8,0},{16,24},{24,16},{1,9},{9,1},{17,25},{25,17},{2,10},{10... | collective-permute-start | bytes 6291464 | tf_op jit(solution)/shard_map/ppermute | solution.py:628
  226.4 87.8 %collective-permute-start.17 = (bf16[512,2048]{1,0:T(8,128)(2,1)S(1)}, bf16[512,2048]{1,0:T(8,128)(2,1)}, u32[]{:S(2)}, u32[]{:S(2)}) collective-permute-start(bf16[512,2048]{1,0:T(8,128)(2,1)S(1)} %bitcast.140), channel_id=1, source_target_pairs={{0,16},{8,24},{16,0},{24,8},{1,17},{9,25},{17,1},{25,9},{2,18},{10... | collective-permute-start | bytes 6291464 | tf_op jit(solution)/shard_map/ppermute | solution.py:628
  231.9 646.1 %reduce-scatter.4.cloned.1.call-start = ((), (), s32[]{:S(2)}) async-start(), calls=%async_computation.6 | async-start | bytes 11141120 | tf_op jit(solution)/shard_map/reduce_scatter | solution.py:1009
  234.2 84.5 %collective-permute-start.24 = (bf16[128,1024]{1,0:T(8,128)(2,1)S(1)}, bf16[128,1024]{1,0:T(8,128)(2,1)}, u32[]{:S(2)}, u32[]{:S(2)}) collective-permute-start(bf16[128,1024]{1,0:T(8,128)(2,1)S(1)} %bitcast.177), channel_id=1, source_target_pairs={{0,1},{1,2},{2,3},{3,0},{4,5},{5,6},{6,7},{7,4},{8,9},{9,10},{10,1... | collective-permute-start | bytes 786440 | tf_op jit(solution)/shard_map/ppermute | solution.py:633
  244.0 74.8 %collective-permute-start.25 = (bf16[128,1024]{1,0:T(8,128)(2,1)S(1)}, bf16[128,1024]{1,0:T(8,128)(2,1)}, u32[]{:S(2)}, u32[]{:S(2)}) collective-permute-start(bf16[128,1024]{1,0:T(8,128)(2,1)S(1)} %bitcast.178), channel_id=1, source_target_pairs={{0,2},{1,3},{2,0},{3,1},{4,6},{5,7},{6,4},{7,5},{8,10},{9,11},{10,... | collective-permute-start | bytes 786440 | tf_op jit(solution)/shard_map/ppermute | solution.py:633
  248.8 20.8 %collective-permute-start.15 = (f32[2,8,1536]{2,1,0:T(8,128)}, f32[2,8,1536]{2,1,0:T(8,128)S(1)}, u32[]{:S(2)}, u32[]{:S(2)}) collective-permute-start(f32[2,8,1536]{2,1,0:T(8,128)} %bitcast.182), channel_id=1, source_target_pairs={{0,8},{8,16},{16,24},{1,9},{9,17},{17,25},{2,10},{10,18},{18,26},{... | collective-permute-start | bytes 294920 | tf_op jit(solution)/shard_map/ppermute | solution.py:639
  269.5 49.2 %collective-permute-start.26 = (bf16[128,1024]{1,0:T(8,128)(2,1)S(1)}, bf16[128,1024]{1,0:T(8,128)(2,1)}, u32[]{:S(2)}, u32[]{:S(2)}) collective-permute-start(bf16[128,1024]{1,0:T(8,128)(2,1)S(1)} %bitcast.179), channel_id=1, source_target_pairs={{0,3},{1,0},{2,1},{3,2},{4,7},{5,4},{6,5},{7,6},{8,11},{9,8},{10,9... | collective-permute-start | bytes 786440 | tf_op jit(solution)/shard_map/ppermute | solution.py:633
  332.9 67.1 %collective-permute-start.21 = (bf16[512,2048]{1,0:T(8,128)(2,1)S(1)}, bf16[512,2048]{1,0:T(8,128)(2,1)}, u32[]{:S(2)}, u32[]{:S(2)}) collective-permute-start(bf16[512,2048]{1,0:T(8,128)(2,1)S(1)} %bitcast.141), channel_id=1, source_target_pairs={{0,4},{4,0},{1,5},{5,1},{2,6},{6,2},{3,7},{7,3},{8,12},{12,8},{9,1... | collective-permute-start | bytes 6291464 | tf_op jit(solution)/shard_map/ppermute | solution.py:628
  333.0 67.1 %collective-permute-start.22 = (bf16[512,2048]{1,0:T(8,128)(2,1)}, bf16[512,2048]{1,0:T(8,128)(2,1)}, u32[]{:S(2)}, u32[]{:S(2)}) collective-permute-start(bf16[512,2048]{1,0:T(8,128)(2,1)} %collective-permute-done.16.mine_grads.refs_18_), channel_id=1, source_target_pairs={{0,4},{4,0},{1,5},{5,1},{2,6},{6,2},{3,7},{7,3},{8,12},{12,8},{9,1... | collective-permute-start | bytes 6291464 | tf_op jit(solution)/shard_map/ppermute | solution.py:628
  333.5 66.6 %collective-permute-start.23 = (bf16[512,2048]{1,0:T(8,128)(2,1)}, bf16[512,2048]{1,0:T(8,128)(2,1)}, u32[]{:S(2)}, u32[]{:S(2)}) collective-permute-start(bf16[512,2048]{1,0:T(8,128)(2,1)} %collective-permute-done.17.mine_grads.refs_20_), channel_id=1, source_target_pairs={{0,4},{4,0},{1,5},{5,1},{2,6},{6,2},{3,7},{7,3},{8,12},{12,8},{9,1... | collective-permute-start | bytes 6291464 | tf_op jit(solution)/shard_map/ppermute | solution.py:628
  333.5 32.3 %collective-permute-start.27 = (bf16[512,1024]{1,0:T(8,128)(2,1)S(1)}, bf16[512,1024]{1,0:T(8,128)(2,1)S(1)}, u32[]{:S(2)}, u32[]{:S(2)}) collective-permute-start(bf16[512,1024]{1,0:T(8,128)(2,1)S(1)} %pad_maximum_fusion.9.refs_1_.refs_0_), channel_id=1, source_target_pairs={{0,8},{8,0},{16,24},{24,16},{1,9},{9,1},{17,25},{25,17},{2,10},{10... | collective-permute-start | bytes 3145736 | tf_op jit(solution)/shard_map/ppermute | solution.py:628
  341.9 26.2 %collective-permute-start.28 = (bf16[512,1024]{1,0:T(8,128)(2,1)S(1)}, bf16[512,1024]{1,0:T(8,128)(2,1)S(1)}, u32[]{:S(2)}, u32[]{:S(2)}) collective-permute-start(bf16[512,1024]{1,0:T(8,128)(2,1)S(1)} %pad_maximum_fusion.9.refs_1_.refs_0_), channel_id=1, source_target_pairs={{0,16},{8,24},{16,0},{24,8},{1,17},{9,25},{17,1},{25,9},{2,18},{10... | collective-permute-start | bytes 3145736 | tf_op jit(solution)/shard_map/ppermute | solution.py:628
  369.0 31.0 %collective-permute-start.29 = (bf16[256,1024]{1,0:T(8,128)(2,1)}, bf16[256,1024]{1,0:T(8,128)(2,1)}, u32[]{:S(2)}, u32[]{:S(2)}) collective-permute-start(bf16[256,1024]{1,0:T(8,128)(2,1)} %slice.671), channel_id=1, source_target_pairs={{0,16},{8,24},{16,0},{24,8},{1,17},{9,25},{17,1},{25,9},{2,18},{10... | collective-permute-start | bytes 1572872 | tf_op jit(solution)/shard_map/ppermute | solution.py:628
  377.7 22.4 %collective-permute-start.30 = (bf16[256,1024]{1,0:T(8,128)(2,1)}, bf16[256,1024]{1,0:T(8,128)(2,1)}, u32[]{:S(2)}, u32[]{:S(2)}) collective-permute-start(bf16[256,1024]{1,0:T(8,128)(2,1)} %slice.672), channel_id=1, source_target_pairs={{0,8},{8,0},{16,24},{24,16},{1,9},{9,1},{17,25},{25,17},{2,10},{10... | collective-permute-start | bytes 1572872 | tf_op jit(solution)/shard_map/ppermute | solution.py:628
  421.9 48.0 %collective-permute-start.34 = (bf16[512,2048]{1,0:T(8,128)(2,1)S(1)}, bf16[512,2048]{1,0:T(8,128)(2,1)}, u32[]{:S(2)}, u32[]{:S(2)}) collective-permute-start(bf16[512,2048]{1,0:T(8,128)(2,1)S(1)} %get-tuple-element.329.mine.refs_8_), channel_id=1, source_target_pairs={{0,8},{8,0},{16,24},{24,16},{1,9},{9,1},{17,25},{25,17},{2,10},{10... | collective-permute-start | bytes 6291464 | tf_op jit(solution)/shard_map/ppermute | solution.py:628
  427.1 48.1 %collective-permute-start.38 = (bf16[512,2048]{1,0:T(8,128)(2,1)S(1)}, bf16[512,2048]{1,0:T(8,128)(2,1)}, u32[]{:S(2)}, u32[]{:S(2)}) collective-permute-start(bf16[512,2048]{1,0:T(8,128)(2,1)S(1)} %get-tuple-element.329.mine.refs_8_), channel_id=1, source_target_pairs={{0,16},{8,24},{16,0},{24,8},{1,17},{9,25},{17,1},{25,9},{2,18},{10... | collective-permute-start | bytes 6291464 | tf_op jit(solution)/shard_map/ppermute | solution.py:628
  475.2 53.3 %collective-permute-start.41 = (bf16[512,2048]{1,0:T(8,128)(2,1)}, bf16[512,2048]{1,0:T(8,128)(2,1)}, u32[]{:S(2)}, u32[]{:S(2)}) collective-permute-start(bf16[512,2048]{1,0:T(8,128)(2,1)} %collective-permute-done.38.mine.refs_12_), channel_id=1, source_target_pairs={{0,4},{4,0},{1,5},{5,1},{2,6},{6,2},{3,7},{7,3},{8,12},{12,8},{9,1... | collective-permute-start | bytes 6291464 | tf_op jit(solution)/shard_map/ppermute | solution.py:628
  478.9 80.0 %collective-permute-start.45 = (bf16[256,2048]{1,0:T(8,128)(2,1)}, bf16[256,2048]{1,0:T(8,128)(2,1)}, u32[]{:S(2)}, u32[]{:S(2)}) collective-permute-start(bf16[256,2048]{1,0:T(8,128)(2,1)} %slice.676), channel_id=1, source_target_pairs={{0,16},{8,24},{16,0},{24,8},{1,17},{9,25},{17,1},{25,9},{2,18},{10... | collective-permute-start | bytes 3145736 | tf_op jit(solution)/shard_map/ppermute | solution.py:628
  480.7 79.5 %collective-permute-start.46 = (bf16[256,2048]{1,0:T(8,128)(2,1)S(1)}, bf16[256,2048]{1,0:T(8,128)(2,1)S(1)}, u32[]{:S(2)}, u32[]{:S(2)}) collective-permute-start(bf16[256,2048]{1,0:T(8,128)(2,1)S(1)} %slice.677), channel_id=1, source_target_pairs={{0,8},{8,0},{16,24},{24,16},{1,9},{9,1},{17,25},{25,17},{2,10},{10... | collective-permute-start | bytes 3145736 | tf_op jit(solution)/shard_map/ppermute | solution.py:628
  485.9 41.3 %collective-permute-start.39 = (bf16[256,2048]{1,0:T(8,128)(2,1)}, bf16[256,2048]{1,0:T(8,128)(2,1)S(1)}, u32[]{:S(2)}, u32[]{:S(2)}) collective-permute-start(bf16[256,2048]{1,0:T(8,128)(2,1)} %slice.674), channel_id=1, source_target_pairs={{0,16},{8,24},{16,0},{24,8},{1,17},{9,25},{17,1},{25,9},{2,18},{10... | collective-permute-start | bytes 3145736 | tf_op jit(solution)/shard_map/ppermute | solution.py:628
  486.5 42.1 %collective-permute-start.40 = (bf16[256,2048]{1,0:T(8,128)(2,1)}, bf16[256,2048]{1,0:T(8,128)(2,1)}, u32[]{:S(2)}, u32[]{:S(2)}) collective-permute-start(bf16[256,2048]{1,0:T(8,128)(2,1)} %slice.675), channel_id=1, source_target_pairs={{0,8},{8,0},{16,24},{24,16},{1,9},{9,1},{17,25},{25,17},{2,10},{10... | collective-permute-start | bytes 3145736 | tf_op jit(solution)/shard_map/ppermute | solution.py:628
  565.2 48.0 %collective-permute-start.43 = (bf16[512,2048]{1,0:T(8,128)(2,1)}, bf16[512,2048]{1,0:T(8,128)(2,1)S(1)}, u32[]{:S(2)}, u32[]{:S(2)}) collective-permute-start(bf16[512,2048]{1,0:T(8,128)(2,1)} %add_convert_fusion.5), channel_id=1, source_target_pairs={{0,16},{8,24},{16,0},{24,8},{1,17},{9,25},{17,1},{25,9},{2,18},{10... | collective-permute-start | bytes 6291464 | tf_op jit(solution)/shard_map/ppermute | solution.py:628
  570.9 48.0 %collective-permute-start.37 = (bf16[512,2048]{1,0:T(8,128)(2,1)}, bf16[512,2048]{1,0:T(8,128)(2,1)}, u32[]{:S(2)}, u32[]{:S(2)}) collective-permute-start(bf16[512,2048]{1,0:T(8,128)(2,1)} %add_convert_fusion.6), channel_id=1, source_target_pairs={{0,8},{8,0},{16,24},{24,16},{1,9},{9,1},{17,25},{25,17},{2,10},{10... | collective-permute-start | bytes 6291464 | tf_op jit(solution)/shard_map/ppermute | solution.py:628
  627.0 48.9 %collective-permute-start.49 = (bf16[512,2048]{1,0:T(8,128)(2,1)}, bf16[512,2048]{1,0:T(8,128)(2,1)}, u32[]{:S(2)}, u32[]{:S(2)}) collective-permute-start(bf16[512,2048]{1,0:T(8,128)(2,1)} %add_convert_fusion.4), channel_id=1, source_target_pairs={{0,24},{8,16},{16,8},{24,0},{1,25},{9,17},{17,9},{25,1},{2,26},{10... | collective-permute-start | bytes 6291464 | tf_op jit(solution)/shard_map/ppermute | solution.py:628
  687.6 357.4 %reduce-scatter.8.cloned.1.call-start = ((), (), s32[]{:S(2)}) async-start(), calls=%async_computation.8 | async-start | bytes 4456448 | tf_op jit(solution)/shard_map/reduce_scatter | solution.py:1012
  689.7 22.2 %collective-permute-start.52 = (bf16[512,2048]{1,0:T(8,128)(2,1)}, bf16[512,2048]{1,0:T(8,128)(2,1)}, u32[]{:S(2)}, u32[]{:S(2)}) collective-permute-start(bf16[512,2048]{1,0:T(8,128)(2,1)} %get-tuple-element.171), channel_id=1, source_target_pairs={{0,4},{4,0},{1,5},{5,1},{2,6},{6,2},{3,7},{7,3},{8,12},{12,8},{9,1... | collective-permute-start | bytes 6291464 | tf_op jit(solution)/shard_map/ppermute | solution.py:628
  710.4 64.1 %collective-permute-start.55 = (bf16[512,2048]{1,0:T(8,128)(2,1)}, bf16[512,2048]{1,0:T(8,128)(2,1)}, u32[]{:S(2)}, u32[]{:S(2)}) collective-permute-start(bf16[512,2048]{1,0:T(8,128)(2,1)} %add_convert_fusion.2), channel_id=1, source_target_pairs={{0,16},{8,24},{16,0},{24,8},{1,17},{9,25},{17,1},{25,9},{2,18},{10... | collective-permute-start | bytes 6291464 | tf_op jit(solution)/shard_map/ppermute | solution.py:628
  715.5 59.0 %collective-permute-start.53 = (bf16[512,2048]{1,0:T(8,128)(2,1)}, bf16[512,2048]{1,0:T(8,128)(2,1)}, u32[]{:S(2)}, u32[]{:S(2)}) collective-permute-start(bf16[512,2048]{1,0:T(8,128)(2,1)} %add_convert_fusion.3), channel_id=1, source_target_pairs={{0,8},{8,0},{16,24},{24,16},{1,9},{9,1},{17,25},{25,17},{2,10},{10... | collective-permute-start | bytes 6291464 | tf_op jit(solution)/shard_map/ppermute | solution.py:628
  722.1 71.9 %collective-permute-start.56 = (bf16[512,2048]{1,0:T(8,128)(2,1)}, bf16[512,2048]{1,0:T(8,128)(2,1)}, u32[]{:S(2)}, u32[]{:S(2)}) collective-permute-start(bf16[512,2048]{1,0:T(8,128)(2,1)} %get-tuple-element.177), channel_id=1, source_target_pairs={{0,4},{4,0},{1,5},{5,1},{2,6},{6,2},{3,7},{7,3},{8,12},{12,8},{9,1... | collective-permute-start | bytes 6291464 | tf_op jit(solution)/shard_map/ppermute | solution.py:628
  743.9 30.6 %collective-permute-start.57 = (bf16[2,8,128,128]{3,2,1,0:T(8,128)(2,1)S(1)}, bf16[2,8,128,128]{3,2,1,0:T(8,128)(2,1)S(1)}, u32[]{:S(2)}, u32[]{:S(2)}) collective-permute-start(bf16[2,8,128,128]{3,2,1,0:T(8,128)(2,1)S(1)} %convert_element_type.350), channel_id=1, source_target_pairs={{8,0},{16,8},{24,16},{9,1},{17,9},{25,17},{10,2},{18,10},{26,18},{... | collective-permute-start | bytes 1572872 | tf_op jit(solution)/shard_map/ppermute | solution.py:639
  807.2 48.8 %collective-permute-start.60 = (bf16[512,2048]{1,0:T(8,128)(2,1)}, bf16[512,2048]{1,0:T(8,128)(2,1)}, u32[]{:S(2)}, u32[]{:S(2)}) collective-permute-start(bf16[512,2048]{1,0:T(8,128)(2,1)} %add_convert_fusion.1), channel_id=1, source_target_pairs={{0,24},{8,16},{16,8},{24,0},{1,25},{9,17},{17,9},{25,1},{2,26},{10... | collective-permute-start | bytes 6291464 | tf_op jit(solution)/shard_map/ppermute | solution.py:628
  854.1 258.2 %reduce-scatter.6.cloned.1.call-start = ((), (), s32[]{:S(2)}) async-start(), calls=%async_computation.7 | async-start | bytes 1966080 | tf_op jit(solution)/shard_map/reduce_scatter | solution.py:1056
  861.1 62.8 %collective-permute-start.79 = (bf16[512,1536]{1,0:T(8,128)(2,1)}, bf16[512,1536]{1,0:T(8,128)(2,1)}, u32[]{:S(2)}, u32[]{:S(2)}) collective-permute-start(bf16[512,1536]{1,0:T(8,128)(2,1)} %convolution_convert_fusion.3), channel_id=1, source_target_pairs={{0,16},{8,24},{16,0},{24,8},{1,17},{9,25},{17,1},{25,9},{2,18},{10... | collective-permute-start | bytes 4718600 | tf_op jit(solution)/shard_map/ppermute | solution.py:628
  868.4 67.0 %collective-permute-start.78 = (bf16[512,1536]{1,0:T(8,128)(2,1)}, bf16[512,1536]{1,0:T(8,128)(2,1)}, u32[]{:S(2)}, u32[]{:S(2)}) collective-permute-start(bf16[512,1536]{1,0:T(8,128)(2,1)} %convolution_convert_fusion.4), channel_id=1, source_target_pairs={{0,8},{8,0},{16,24},{24,16},{1,9},{9,1},{17,25},{25,17},{2,10},{10... | collective-permute-start | bytes 4718600 | tf_op jit(solution)/shard_map/ppermute | solution.py:628
  871.5 228.1 %collective-permute-start.51 = (bf16[512,2048]{1,0:T(8,128)(2,1)}, bf16[512,2048]{1,0:T(8,128)(2,1)}, u32[]{:S(2)}, u32[]{:S(2)}) collective-permute-start(bf16[512,2048]{1,0:T(8,128)(2,1)} %get-tuple-element.168), channel_id=1, source_target_pairs={{0,4},{4,0},{1,5},{5,1},{2,6},{6,2},{3,7},{7,3},{8,12},{12,8},{9,1... | collective-permute-start | bytes 6291464 | tf_op jit(solution)/shard_map/ppermute | solution.py:628
  911.2 27.9 %collective-permute-start.63 = (f32[2,8,1536]{2,1,0:T(8,128)}, f32[2,8,1536]{2,1,0:T(8,128)S(1)}, u32[]{:S(2)}, u32[]{:S(2)}) collective-permute-start(f32[2,8,1536]{2,1,0:T(8,128)} %get-tuple-element.198), channel_id=1, source_target_pairs={{8,0},{16,8},{24,16},{9,1},{17,9},{25,17},{10,2},{18,10},{26,18},{... | collective-permute-start | bytes 294920 | tf_op jit(solution)/shard_map/ppermute | solution.py:639
  941.3 45.8 %collective-permute-start.65 = (bf16[512,1664]{1,0:T(8,128)(2,1)S(1)}, bf16[512,1664]{1,0:T(8,128)(2,1)S(1)}, u32[]{:S(2)}, u32[]{:S(2)}) collective-permute-start(bf16[512,1664]{1,0:T(8,128)(2,1)S(1)} %convolution_convert_fusion.1), channel_id=1, source_target_pairs={{0,8},{8,0},{16,24},{24,16},{1,9},{9,1},{17,25},{25,17},{2,10},{10... | collective-permute-start | bytes 5111816 | tf_op jit(solution)/shard_map/ppermute | solution.py:628
  947.0 43.1 %collective-permute-start.64 = (bf16[512,1664]{1,0:T(8,128)(2,1)S(1)}, bf16[512,1664]{1,0:T(8,128)(2,1)S(1)}, u32[]{:S(2)}, u32[]{:S(2)}) collective-permute-start(bf16[512,1664]{1,0:T(8,128)(2,1)S(1)} %convolution_convert_fusion.2), channel_id=1, source_target_pairs={{0,16},{8,24},{16,0},{24,8},{1,17},{9,25},{17,1},{25,9},{2,18},{10... | collective-permute-start | bytes 5111816 | tf_op jit(solution)/shard_map/ppermute | solution.py:628
  948.2 58.5 %collective-permute-start.81 = (bf16[256,1536]{1,0:T(8,128)(2,1)S(1)}, bf16[256,1536]{1,0:T(8,128)(2,1)}, u32[]{:S(2)}, u32[]{:S(2)}) collective-permute-start(bf16[256,1536]{1,0:T(8,128)(2,1)S(1)} %fusion.15), channel_id=1, source_target_pairs={{0,16},{8,24},{16,0},{24,8},{1,17},{9,25},{17,1},{25,9},{2,18},{10... | collective-permute-start | bytes 2359304 | tf_op jit(solution)/shard_map/ppermute | solution.py:628
  954.7 51.9 %collective-permute-start.80 = (bf16[256,1536]{1,0:T(8,128)(2,1)S(1)}, bf16[256,1536]{1,0:T(8,128)(2,1)}, u32[]{:S(2)}, u32[]{:S(2)}) collective-permute-start(bf16[256,1536]{1,0:T(8,128)(2,1)S(1)} %fusion.14), channel_id=1, source_target_pairs={{0,8},{8,0},{16,24},{24,16},{1,9},{9,1},{17,25},{25,17},{2,10},{10... | collective-permute-start | bytes 2359304 | tf_op jit(solution)/shard_map/ppermute | solution.py:628
  989.5 38.6 %collective-permute-start.67 = (bf16[256,1664]{1,0:T(8,128)(2,1)}, bf16[256,1664]{1,0:T(8,128)(2,1)S(1)}, u32[]{:S(2)}, u32[]{:S(2)}) collective-permute-start(bf16[256,1664]{1,0:T(8,128)(2,1)} %fusion.17), channel_id=1, source_target_pairs={{0,16},{8,24},{16,0},{24,8},{1,17},{9,25},{17,1},{25,9},{2,18},{10... | collective-permute-start | bytes 2555912 | tf_op jit(solution)/shard_map/ppermute | solution.py:628
  992.4 35.7 %collective-permute-start.66 = (bf16[256,1664]{1,0:T(8,128)(2,1)}, bf16[256,1664]{1,0:T(8,128)(2,1)}, u32[]{:S(2)}, u32[]{:S(2)}) collective-permute-start(bf16[256,1664]{1,0:T(8,128)(2,1)} %fusion.18), channel_id=1, source_target_pairs={{0,8},{8,0},{16,24},{24,16},{1,9},{9,1},{17,25},{25,17},{2,10},{10... | collective-permute-start | bytes 2555912 | tf_op jit(solution)/shard_map/ppermute | solution.py:628
  1031.4 26.2 %collective-permute-start.68 = (bf16[2,256,2048]{2,1,0:T(8,128)(2,1)}, bf16[2,256,2048]{2,1,0:T(8,128)(2,1)}, u32[]{:S(2)}, u32[]{:S(2)}) collective-permute-start(bf16[2,256,2048]{2,1,0:T(8,128)(2,1)} %constant_dynamic-slice_fusion.3), channel_id=1, source_target_pairs={{0,4},{4,0},{1,5},{5,1},{2,6},{6,2},{3,7},{7,3},{8,12},{12,8},{9,1... | collective-permute-start | bytes 6291464 | tf_op jit(solution)/shard_map/ppermute | solution.py:628
  1040.5 31.0 %all-to-all-start.1 = ((bf16[4,2112,128]{2,1,0:T(8,128)(2,1)}), bf16[4,2112,128]{2,1,0:T(8,128)(2,1)}, u32[]{:S(2)}, u32[]{:S(2)}) async-start(bf16[4,2112,128]{2,1,0:T(8,128)(2,1)} %copy.150), calls=%async_computation.4 | async-start | bytes 4325376 | tf_op jit(solution)/shard_map/all_to_all | solution.py:1068
  1053.9 60.9 %collective-permute-start.75 = (bf16[128,1664]{1,0:T(8,128)(2,1)}, bf16[128,1664]{1,0:T(8,128)(2,1)}, u32[]{:S(2)}, u32[]{:S(2)}) collective-permute-start(bf16[128,1664]{1,0:T(8,128)(2,1)} %get-tuple-element.347), channel_id=1, source_target_pairs={{0,1},{1,2},{2,3},{3,0},{4,5},{5,6},{6,7},{7,4},{8,9},{9,10},{10,1... | collective-permute-start | bytes 1277960 | tf_op jit(solution)/shard_map/ppermute | solution.py:633
  1053.9 61.0 %collective-permute-start.76 = (bf16[128,1664]{1,0:T(8,128)(2,1)}, bf16[128,1664]{1,0:T(8,128)(2,1)}, u32[]{:S(2)}, u32[]{:S(2)}) collective-permute-start(bf16[128,1664]{1,0:T(8,128)(2,1)} %get-tuple-element.346), channel_id=1, source_target_pairs={{0,2},{1,3},{2,0},{3,1},{4,6},{5,7},{6,4},{7,5},{8,10},{9,11},{10,... | collective-permute-start | bytes 1277960 | tf_op jit(solution)/shard_map/ppermute | solution.py:633
  1054.3 60.5 %collective-permute-start.77 = (bf16[128,1664]{1,0:T(8,128)(2,1)}, bf16[128,1664]{1,0:T(8,128)(2,1)}, u32[]{:S(2)}, u32[]{:S(2)}) collective-permute-start(bf16[128,1664]{1,0:T(8,128)(2,1)} %get-tuple-element.345), channel_id=1, source_target_pairs={{0,3},{1,0},{2,1},{3,2},{4,7},{5,4},{6,5},{7,6},{8,11},{9,8},{10,9... | collective-permute-start | bytes 1277960 | tf_op jit(solution)/shard_map/ppermute | solution.py:633
  (110 other events, 1482.6 us)
Sparse Core Ops, SparseCore 0:
  122.4 114.8 all-gather.5
  238.8 69.4 all-gather.3
  687.7 154.9 reduce-scatter.3
  854.2 102.1 reduce-scatter.7
  1036.5 48.9 reduce-scatter.5

commit v8 on v7

--- a/solution.py
+++ b/solution.py
@@ -907,16 +907,18 @@
     inputs_mine = wide(rows_mine(block_input).reshape(-1, width))
     grads_mine = rows_mine(out_grad).reshape(-1, width)
 
-    square = Square(tie(lines[0], ffn_swapped)).forward()
+    square = Square(tie(lines[0], ffn_swapped)).forward(normed_mix)
     gate_up_parts = lax.all_gather(tie(ffn_line[: 2 * units], lines[parts - 1], *square.done()), "fsdp", axis=0)
     down_parts = lax.all_gather(ffn_line[2 * units :], "fsdp", axis=0)
     mix_full, kept, pre = [], [], []
     for p in range(parts):
         mix_full.append(square.pieces())
-        square = Square(tie(lines[p + 1], *square.done()))
+        arrived = square.done()
         ends = normed_mix.reshape(seq_count, local_len, width)[:, local_len - HALO :].reshape(seq_count * HALO, width)
         ends = gathered_times(ends, ctx_place, mix_full[p])
-        halo = from_behind(ends[:, :part_cols].reshape(seq_count, HALO, part_cols), "ctx", 1)
+        ends = low(ends)
+        square = Square(tie(lines[p + 1], ends, *arrived))
+        halo = wide(from_behind(ends[:, :part_cols].reshape(seq_count, HALO, part_cols), "ctx", 1))
         pre.append(gathered_times(tie(normed_mix, ends), ctx_place, mix_full[p]))
         convs = conv[:, p * part_cols : (p + 1) * part_cols]
         kept.append(
@@ -936,7 +938,7 @@
     gate_up_full = columns_join(gate_up_parts, 4)
     finals = jnp.concatenate([some[4] for some in kept], axis=1)
     transfer = low(finals[..., LANES:])
-    first = tie(finals[..., :LANES], gate_up_parts, grad_square.beside, grad_square.across)
+    first = tie(finals[..., :LANES], gate_up_full, grad_square.beside, grad_square.across)
     entering = pass_states(first, transfer, 1)
     entered = [entering[:, p * part_heads : (p + 1) * part_heads] for p in range(parts)]
     grad_square.forward(entering)
@@ -944,8 +946,6 @@
     mixed_rows = []
     for p in range(parts):
         own, carry = kept[p][2:4]
-        if p == parts - 1:
-            own = tie(own, gate_up_full)
         mixed_rows.append(mixer_output(own, carry, entered[p], gain_head, group))
     mixed_rows = jnp.concatenate(mixed_rows, axis=1)
     mixed_rows = tie(mixed_rows, *(other for _, other in grad_rows))
@@ -974,7 +974,9 @@
     mine, other = (side[1] for side in ffn_out[3])
     far_sums = low(core_sum(mine, tie(other, *near_sums)))
     acts = [side[0] for outs in ffn_out for side in outs]
-    acts[0] = tie(acts[0], far_sums)
+    own_sums = core_sum(*(side[1] for side in ffn_out[0]))
+    result_low = [low(core_sum(*(side[2] for side in ffn_out[bit]))) for bit in (1, 2)]
+    acts[0] = tie(acts[0], far_sums, own_sums, *result_low)
     far_sums = flip(far_sums, "ctx", 3)
     sums = ffn_weights(
         acts,
@@ -985,12 +987,8 @@
     ).reshape(line_count, 3 * units, 4 * shard_rows)
 
     far_sums, sums = lax.optimization_barrier((far_sums, sums))
-    result_near = []
-    for bit in (1, 2):
-        mine, other = (side[2] for side in ffn_out[bit])
-        result_near.append(flip(low(core_sum(mine, tie(other, far_sums))), "ctx", bit))
-    grad_normed = core_sum(*(side[1] for side in ffn_out[0]))
-    grad_normed = grad_normed + wide(near_sums[0]) + wide(near_sums[1]) + wide(far_sums)
+    result_near = [flip(tie(part, far_sums), "ctx", bit) for part, bit in zip(result_low, (1, 2))]
+    grad_normed = own_sums + wide(near_sums[0]) + wide(near_sums[1]) + wide(far_sums)
     back_ffn, unit_ffn = norm_backward(grad_normed, residual, scale_ffn, gain_ffn)
     grad_residual = wide(grads_mine) + back_ffn
     gain_ffn_part = jnp.sum(grad_normed * unit_ffn, axis=0)
@@ -1009,6 +1007,7 @@
     total = lax.psum_scatter(sums, "fsdp", scatter_dimension=0, tiled=True)
 
     out_grad_w = low(outer_rows(grad_branch, mixed_rows))
+    out_part = out_grad_w
     out_grad_w = lax.psum_scatter(out_grad_w, ("ctx", "fsdp"), scatter_dimension=0, tiled=True)
 
     mine, other = (side[2] for side in ffn_out[0])
@@ -1022,12 +1021,14 @@
     for p in reversed(range(parts)):
         halo, convs, own, carry, final, inverses, updates, states = kept[p]
         heads = slice(p * part_heads, (p + 1) * part_heads)
-        back = backs[p] if scatter is None else tie(backs[p], total, *scatter.sent)
+        back = tie(backs[p], out_part) if scatter is None else tie(backs[p], total, *scatter.sent)
         grad_mix, tail, before, conv_parts[p], logit = mixer_backward(
             pre[p], pre[0], bias, halo, convs, col, row, back, inverses, updates, states,
             entered[p], grad_end[:, heads], taps, p * part_heads, part_heads, group,
         )
         logits = logits + logit
+        if scatter is None:
+            result_far = tie(result_far, before)
         tail = low(tail + from_behind(before, "ctx", -1))
         grad_mix = put(grad_mix.reshape(seq_count, local_len, -1), tail, 0, local_len - HALO, 0)
         grad_mix = grad_mix.reshape(row_count, -1)
@@ -1040,7 +1041,10 @@
             grad_mix = jnp.concatenate([grad_mix, low(logits)], axis=1)
         grad_mixes[p] = grad_mix
         scatter = Scatter(columns, grad_mix)
-    ready = scatter.second()
+    result = result_own + wide(result_near[0]) + wide(result_near[1])
+    result = result + wide(result_far)
+    block_output = rows_full(low(residual + result).reshape(seq_count, -1, width))
+    ready = scatter.second(block_output)
     grad_mixes[0] = tie(grad_mixes[0], *ready)
     mix_back = tie(gathered_times_transposed(grad_mixes, ctx_place, mix_full), *scatter.last)
     mix_back = rows_scatter(mix_back.reshape(seq_count, local_len, width)).reshape(-1, width)
@@ -1067,9 +1071,6 @@
     pieces = tie(total, *scatter.last).reshape(3 * units, 4, shard_rows).transpose(1, 0, 2)
     arrived = lax.all_to_all(pieces, "ctx", 0, 0).reshape(4, 3, units, shard_rows)
     gate_grad, up_grad, down_grad = (wide(arrived[:, i].reshape(units_here, shard_rows)) for i in range(3))
-    result = result_own + wide(result_near[0]) + wide(result_near[1])
-    result = result + wide(result_far)
-    block_output = rows_full(low(residual + result).reshape(seq_count, -1, width))
 
     return (
         block_output,

time: 1150 us -> 1150 us (level)
  waiting for transfers between devices: 327 us -> 312 us
  other arithmetic: 124 us -> 136 us
    ppermute x60, waiting for transfers between devices: 203 us -> 173 us  [flip(): return lax.ppermute(value, axis, [(i, i ^ bit) for i in devices])]
    unnamed x221 -> x211, local copies, waits for them, and re-layouts: 33.7 us -> 31.2 us
    convert_element_type x17 -> x19, other arithmetic: 46.9 us -> 46.6 us  [low(): return value.astype(jnp.bfloat16)]
  transfers between devices with their start and end apart: 89 -> 89, of which waited for: 36 -> 41; matrix products, arithmetic and copies ran while one was open for 19% -> 21% of each run, Pallas kernels for 34% -> 35%
where the time goes in v8:
time: 1150 us; the launch traced here: 1140 us
  Pallas kernels  393 us (34%)
  waiting for transfers between devices  312 us (27%)
  other arithmetic  136 us (12%)
  starting transfers between devices  134 us (12%)
  local copies, waits for them, and re-layouts  103 us (9%)
  matrix products  44.9 us (4%)
  between operations  15.6 us (1%)
    ppermute x60, waiting for transfers between devices, flip(): return lax.ppermute(value, axis, [(i, i ^ bit) for i in devices])  173 us
    pallas_call x4, Pallas kernels, ffn_both(): pl.pallas_call(ffn_kernel, grid=(count // tile,), in_specs=[wide_rows] *...  118 us
    ppermute x10, waiting for transfers between devices, from_behind(): return lax.ppermute(block, axis, route)  99.5 us
    pallas_call x2, Pallas kernels, mixer_backward(): pl.pallas_call(functools.partial(backward_kernel, taps, group, first), gr...  66.4 us
    ppermute x60, starting transfers between devices, flip(): return lax.ppermute(value, axis, [(i, i ^ bit) for i in devices])  64.9 us
    pallas_call x2, Pallas kernels, mixer_forward(): pl.pallas_call(functools.partial(forward_kernel, taps, group, first), gri...  55 us
    pallas_call x1, Pallas kernels, ffn_weights(): pl.pallas_call(functools.partial(ffn_weights_kernel, count, lines), grid=...  48.2 us
    convert_element_type x19, other arithmetic, low(): return value.astype(jnp.bfloat16)  46.6 us
  transfers between devices with their start and end apart: 89, of which 41 were waited for; matrix products, arithmetic and copies ran while one was open for 21% of the time, Pallas kernels for 35%

profile of v8, /device:TPU:0, one launch (start us, length us, event | category | flops | bytes accessed | tf_op | source)
XLA Modules:
  0.0 1139.5 jit_solution(14683276081866226549)
XLA Ops:
  12.6 5.3 all-to-all-start
  27.8 9.3 collective-permute-done
  37.1 17.1 %collective-permute-done.1 = bf16[128,1664]{1,0:T(8,128)(2,1)S(1)} collective-permute-done((bf16[128,1664]{1,0:T(8,128)(2,1)}, bf16[128,1664]{1,0:T(8,128)(2,1)S(1)}, u32[]{:S(2)}, u32[]{:S(2)}) %collective-permute-start.1) | collective-permute-done | bytes 426016 | tf_op jit(solution)/shard_map/ppermute | solution.py:633
  63.1 10.7 collective-permute-start.10
  77.5 18.7 %collective-permute-done.3.refs_1_.refs_3_ = bf16[512,1664]{1,0:T(8,128)(2,1)S(1)} collective-permute-done((bf16[512,1664]{1,0:T(8,128)(2,1)}, bf16[512,1664]{1,0:T(8,128)(2,1)S(1)}, u32[]{:S(2)}, u32[]{:S(2)}) %collective-permute-start.3) | collective-permute-done | bytes 1703968 | tf_op jit(solution)/shard_map/ppermute | solution.py:628
  101.4 6.6 collective-permute-done.9
  113.2 5.2 collective-permute-done.5.refs_3_.refs_5_
  120.0 6.5 convert_element_type.410
  130.0 4.8 shard_map.271
  140.8 12.8 %shard_map.272.pre.beta = f32[1024,1664]{1,0:T(8,128)} custom-call(s32[1]{0:T(128)} %bitcast.1.place, bf16[1024,2048]{1,0:T(8,128)(2,1)} %fusion.1.rows, bf16[512,1664]{1,0:T(8,128)(2,1)} %pad_maximum_fusion.6.refs_0_.refs_2_, bf16[512,1664]{1,0:T(8,128)(2,1)} %copy-done.25, bf16[512,1664]{1,0:T(8,128)(2,1)} %copy-done.26, bf16[256,1664]{1,0:T(8,128)(2,1)} %copy-done.39, ...), custom_call_target="tpu_custom_call" | custom-call | flops 6979321856 | bytes 11010048 | tf_op jit(solution)/shard_map/pallas_call | solution.py:551
  153.6 16.3 %collective-permute-done.7 = bf16[2,8,1536]{2,1,0:T(8,128)(2,1)S(1)} collective-permute-done((bf16[2,8,1536]{2,1,0:T(8,128)(2,1)S(1)}, bf16[2,8,1536]{2,1,0:T(8,128)(2,1)S(1)}, u32[]{:S(2)}, u32[]{:S(2)}) %collective-permute-start.7) | collective-permute-done | bytes 49184 | tf_op jit(solution)/shard_map/ppermute | solution.py:639
  170.6 27.5 %shard_map.273 = (f32[1024,512]{1,0:T(8,128)}, bf16[1024,512]{1,0:T(8,128)(2,1)}, f32[2,4,128,256]{3,2,1,0:T(8,128)}, bf16[2,4,4,128,128]{4,3,2,1,0:T(8,128)(2,1...) custom-call(f32[1024,1664]{1,0:T(8,128)} %shard_map.272.pre.beta, ...), custom_call_target="tpu_custom_call" | custom-call | flops 4026531840 | bytes 20971520 | tf_op jit(solution)/shard_map/pallas_call | solution.py:160
  206.1 12.1 %collective-permute-done.13.refs_3_.refs_10_ = bf16[256,1536]{1,0:T(8,128)(2,1)S(1)} collective-permute-done((bf16[256,1536]{1,0:T(8,128)(2,1)}, bf16[256,1536]{1,0:T(8,128)(2,1)S(1)}, u32[]{:S(2)}, u32[]{:S(2)}) %collective-permute-start.13) | collective-permute-done | bytes 786464 | tf_op jit(solution)/shard_map/ppermute | solution.py:628
  230.0 9.8 collective-permute-start.24
  247.3 11.5 %shard_map.275.pre = f32[1024,1536]{1,0:T(8,128)} custom-call(s32[1]{0:T(128)} %bitcast.1.place, bf16[1024,2048]{1,0:T(8,128)(2,1)} %fusion.1.rows, bf16[512,1536]{1,0:T(8,128)(2,1)} %pad_maximum_fusion.7.refs_0_.refs_7_, bf16[512,1536]{1,0:T(8,128)(2,1)} %copy-done.27, bf16[512,1536]{1,0:T(8,128)(2,1)} %collective-permute-done.12.refs_2_.refs_9_, ...), custom_call_target="tpu_custom_call" | custom-call | flops 6442450944 | bytes 10485760 | tf_op jit(solution)/shard_map/pallas_call | solution.py:551
  258.8 5.8 collective-permute-done.15
  264.5 5.2 collective-permute-start.26
  270.4 27.5 %shard_map.276 = (f32[1024,512]{1,0:T(8,128)}, bf16[1024,512]{1,0:T(8,128)(2,1)}, f32[2,4,128,256]{3,2,1,0:T(8,128)}, bf16[2,4,4,128,128]{4,3,2,1,0:T(8,128)(2,1...) custom-call(f32[1024,1536]{1,0:T(8,128)} %shard_map.275.pre, ...), custom_call_target="tpu_custom_call" | custom-call | flops 4026531840 | bytes 20971520 | tf_op jit(solution)/shard_map/pallas_call | solution.py:160
  301.5 8.4 copy.142
  309.9 7.9 shard_map.277.gate_w.up_w
  323.9 7.7 collective-permute-done.18
  340.0 5.3 collective-permute-done.19
  345.4 7.9 collective-permute-start.28
  353.6 15.8 %collective-permute-done.27.refs_2_.refs_1_ = bf16[512,1024]{1,0:T(8,128)(2,1)S(1)} collective-permute-done((bf16[512,1024]{1,0:T(8,128)(2,1)S(1)}, bf16[512,1024]{1,0:T(8,128)(2,1)S(1)}, u32[]{:S(2)}, u32[]{:S(2)}) %collective-permute-start.27) | collective-permute-done | bytes 1048608 | tf_op jit(solution)/shard_map/ppermute | solution.py:628
  372.6 8.6 collective-permute-start.29
  395.6 8.7 shard_map.280
  424.6 29.6 %shard_map.282 = (bf16[3,512,704]{2,1,0:T(8,128)(2,1)}, bf16[512,2048]{1,0:T(8,128)(2,1)}, bf16[512,2048]{1,0:T(8,128)(2,1)}, bf16[3,512,704]{2,1,0:T(8,128)(2,1...) custom-call(bf16[512,2048]{1,0:T(8,128)(2,1)} %copy-done.36, ...), custom_call_target="tpu_custom_call" | custom-call | flops 17716740096 | bytes 25427968 | tf_op jit(solution)/shard_map/pallas_call | solution.py:469
  454.2 11.2 collective-permute-done.34.mine.refs_10_
  465.4 5.2 collective-permute-done.38.mine.refs_12_
  483.1 29.5 %shard_map.283 = (bf16[3,512,704]{2,1,0:T(8,128)(2,1)}, bf16[512,2048]{1,0:T(8,128)(2,1)}, bf16[512,2048]{1,0:T(8,128)(2,1)}, bf16[3,512,704]{2,1,0:T(8,128)(2,1...) custom-call(bf16[512,2048]{1,0:T(8,128)(2,1)} %collective-permute-done.34.mine.refs_10_, ...), custom_call_target="tpu_custom_call" | custom-call | flops 17716740096 | bytes 25427968 | tf_op jit(solution)/shard_map/pallas_call | solution.py:469
  512.5 10.1 collective-permute-done.39
  524.0 29.7 %shard_map.284 = (bf16[3,512,704]{2,1,0:T(8,128)(2,1)}, bf16[512,2048]{1,0:T(8,128)(2,1)}, bf16[512,2048]{1,0:T(8,128)(2,1)}, bf16[3,512,704]{2,1,0:T(8,128)(2,1...) custom-call(bf16[512,2048]{1,0:T(8,128)(2,1)} %collective-permute-done.38.mine.refs_12_, ...), custom_call_target="tpu_custom_call" | custom-call | flops 17716740096 | bytes 25427968 | tf_op jit(solution)/shard_map/pallas_call | solution.py:469
  568.7 29.6 %shard_map.285 = (bf16[3,512,704]{2,1,0:T(8,128)(2,1)}, bf16[512,2048]{1,0:T(8,128)(2,1)}, bf16[512,2048]{1,0:T(8,128)(2,1)}, bf16[3,512,704]{2,1,0:T(8,128)(2,1...) custom-call(bf16[512,2048]{1,0:T(8,128)(2,1)} %copy-done.45, ...), custom_call_target="tpu_custom_call" | custom-call | flops 17716740096 | bytes 25427968 | tf_op jit(solution)/shard_map/pallas_call | solution.py:469
  598.3 10.2 collective-permute-done.43
  608.6 5.7 collective-permute-done.37
  614.2 4.6 add_convert_fusion.2
  624.2 48.2 %shard_map.286 = bf16[4,3,704,512]{3,2,1,0:T(8,128)(2,1)} custom-call(bf16[3,512,704]{2,1,0:T(8,128)(2,1)} %get-tuple-element.170.refs_0_, bf16[3,512,704]{2,1,0:T(8,128)(2,1)} %get-tuple-element.171.refs_1_, bf16[3,512,704]{2,1,0:T(8,128)(2,1)} %get-tuple-element.154.refs_2_, bf16[3,512,704]{2,1,0:T(8,128)(2,1)} %get-tuple-element.172.refs_3_, ...), custom_call_target="tpu_custom_call" | custom-call | flops 35433480192 | bytes 67108864 | tf_op jit(solution)/shard_map/pallas_call | solution.py:516
  672.6 11.6 %copy.148 = bf16[4,2112,512]{1,2,0:T(8,128)(2,1)} copy(bf16[4,2112,512]{2,1,0:T(8,128)(2,1)} %bitcast.154) | data formatting | bytes 17301504 | tf_op jit(solution)/shard_map/optimization_barrier | solution.py:989
  690.0 7.0 multiply_reduce_fusion.1
  709.6 8.9 shard_map.287.grad
  718.5 5.7 shard_map.289
  724.2 5.8 shard_map.288
  732.8 15.3 %collective-permute-done.55 = bf16[512,2048]{1,0:T(8,128)(2,1)} collective-permute-done((bf16[512,2048]{1,0:T(8,128)(2,1)}, bf16[512,2048]{1,0:T(8,128)(2,1)}, u32[]{:S(2)}, u32[]{:S(2)}) %collective-permute-start.55) | collective-permute-done | bytes 2097184 | tf_op jit(solution)/shard_map/ppermute | solution.py:628
  750.1 10.2 collective-permute-done.57
  762.0 13.7 %collective-permute-done.58 = bf16[2,8,128,128]{3,2,1,0:T(8,128)(2,1)S(1)} collective-permute-done((bf16[2,8,128,128]{3,2,1,0:T(8,128)(2,1)S(1)}, bf16[2,8,128,128]{3,2,1,0:T(8,128)(2,1)S(1)}, u32[]{:S(2)}, u32[]{:S(2)}) %collective-permute-start.58) | collective-permute-done | bytes 524320 | tf_op jit(solution)/shard_map/ppermute | solution.py:639
  781.2 9.2 collective-permute-done.59
  790.5 9.4 convolution_convert_fusion
  800.9 33.3 %shard_map.290 = (bf16[1024,1536]{1,0:T(8,128)(2,1)}, f32[2,8,1536]{2,1,0:T(8,128)}, f32[2,8,1536]{2,1,0:T(8,128)}, f32[2,8,1536]{2,1,0:T(8,128)}, f32[1024,128]{1,0:T(8,128)}) custom-call(f32[1024,1536]{1,0:T(8,128)} %shard_map.275.pre, f32[1024,1664]{1,0:T(8,128)} %shard_map.272.pre.beta, f32[1,128]{1,0:T(1,128)} %pad_bitcast_fusion.bias, ...), custom_call_target="tpu_custom_call" | custom-call | flops 4026531840 | bytes 20971520 | tf_op jit(solution)/shard_map/pallas_call | solution.py:318
  837.0 9.5 add_convert_fusion
  857.5 5.3 convolution_convert_fusion.3
  868.4 4.7 fusion.26
  873.1 4.6 broadcast_select_fusion.3
  877.7 33.2 %shard_map.291 = (bf16[1024,1536]{1,0:T(8,128)(2,1)}, f32[2,8,1536]{2,1,0:T(8,128)}, f32[2,8,1536]{2,1,0:T(8,128)}, f32[2,8,1536]{2,1,0:T(8,128)}, f32[1024,128]{1,0:T(8,128)}) custom-call(f32[1024,1664]{1,0:T(8,128)} %shard_map.272.pre.beta, f32[1024,1664]{1,0:T(8,128)} %shard_map.272.pre.beta, f32[1,128]{1,0:T(1,128)} %pad_bitcast_fusion.bias, ...), custom_call_target="tpu_custom_call" | custom-call | flops 4026531840 | bytes 20971520 | tf_op jit(solution)/shard_map/pallas_call | solution.py:318
  914.1 26.7 %collective-permute-done.63 = f32[2,8,1536]{2,1,0:T(8,128)S(1)} collective-permute-done((f32[2,8,1536]{2,1,0:T(8,128)}, f32[2,8,1536]{2,1,0:T(8,128)S(1)}, u32[]{:S(2)}, u32[]{:S(2)}) %collective-permute-start.63) | collective-permute-done | bytes 98336 | tf_op jit(solution)/shard_map/ppermute | solution.py:639
  942.3 5.7 convolution_convert_fusion.1
  976.6 11.9 %collective-permute-done.65 = bf16[512,1664]{1,0:T(8,128)(2,1)} collective-permute-done((bf16[512,1664]{1,0:T(8,128)(2,1)}, bf16[512,1664]{1,0:T(8,128)(2,1)}, u32[]{:S(2)}, u32[]{:S(2)}) %collective-permute-start.65) | collective-permute-done | bytes 1703968 | tf_op jit(solution)/shard_map/ppermute | solution.py:628
  988.5 5.2 collective-permute-done.64
  1005.4 5.2 collective-permute-done.80
  1010.6 21.4 %shard_map.292 = bf16[1024,2048]{1,0:T(8,128)(2,1)} custom-call(s32[1]{0:T(128)} %bitcast.1.place, bf16[1024,1664]{1,0:T(8,128)(2,1)} %pad_maximum_fusion.3.refs_0_, bf16[1024,1536]{1,0:T(8,128)(2,1)} %bitcast.148, bf16[512,1664]{1,0:T(8,128)(2,1)} %pad_maximum_fusion.6.refs_0_.refs_2_, bf16[512,1664]{1,0:T(8,128)(2,1)} %copy-done.25, ...), custom_call_target="tpu_custom_call" | custom-call | flops 13421772800 | bytes 17301504 | tf_op jit(solution)/shard_map/pallas_call | solution.py:587
  1057.7 5.0 collective-permute-start.76
  1062.8 5.8 fusion.9
  1068.6 6.8 all-to-all-done.1
  1091.1 13.8 %collective-permute-done.73 = f32[16640]{0:T(1024)S(1)} collective-permute-done((f32[16640]{0:T(1024)S(1)}, f32[16640]{0:T(1024)S(1)}, u32[]{:S(2)}, u32[]{:S(2)}) %collective-permute-start.73) | collective-permute-done | bytes 66592 | tf_op jit(solution)/shard_map/ppermute | solution.py:628
  1107.4 7.6 fusion.5
  (499 shorter events, 324.7 us)
Async XLA Ops:
  12.6 44.4 %all-to-all-start = ((bf16[4,2112,128]{2,1,0:T(8,128)(2,1)}), bf16[4,2112,128]{2,1,0:T(8,128)(2,1)S(1)}, u32[]{:S(2)}, u32[]{:S(2)}) async-start(bf16[4,2112,128]{2,1,0:T(8,128)(2,1)} %bitcast.157), calls=%async_computation | async-start | bytes 4325376 | tf_op jit(solution)/shard_map/all_to_all | solution.py:893
  17.8 283.6 %all-gather.6.cloned.1.call-start = ((), (), s32[]{:S(2)}) async-start(), calls=%async_computation.9 | async-start | bytes 7208960 | tf_op jit(solution)/shard_map/all_gather | solution.py:911
  23.8 30.4 %collective-permute-start.1 = (bf16[128,1664]{1,0:T(8,128)(2,1)}, bf16[128,1664]{1,0:T(8,128)(2,1)S(1)}, u32[]{:S(2)}, u32[]{:S(2)}) collective-permute-start(bf16[128,1664]{1,0:T(8,128)(2,1)} %constant_dynamic-update-slice_fusion), channel_id=1, source_target_pairs={{0,2},{1,3},{2,0},{3,1},{4,6},{5,7},{6,4},{7,5},{8,10},{9,11},{10,... | collective-permute-start | bytes 1277960 | tf_op jit(solution)/shard_map/ppermute | solution.py:633
  26.4 27.8 %collective-permute-start.2 = (bf16[128,1664]{1,0:T(8,128)(2,1)}, bf16[128,1664]{1,0:T(8,128)(2,1)S(1)}, u32[]{:S(2)}, u32[]{:S(2)}) collective-permute-start(bf16[128,1664]{1,0:T(8,128)(2,1)} %constant_dynamic-update-slice_fusion), channel_id=1, source_target_pairs={{0,3},{1,0},{2,1},{3,2},{4,7},{5,4},{6,5},{7,6},{8,11},{9,8},{10,9... | collective-permute-start | bytes 1277960 | tf_op jit(solution)/shard_map/ppermute | solution.py:633
  56.9 39.2 %collective-permute-start.3 = (bf16[512,1664]{1,0:T(8,128)(2,1)}, bf16[512,1664]{1,0:T(8,128)(2,1)S(1)}, u32[]{:S(2)}, u32[]{:S(2)}) collective-permute-start(bf16[512,1664]{1,0:T(8,128)(2,1)} %pad_maximum_fusion.6.refs_0_.refs_2_), channel_id=1, source_target_pairs={{0,8},{8,0},{16,24},{24,16},{1,9},{9,1},{17,25},{25,17},{2,10},{10... | collective-permute-start | bytes 5111816 | tf_op jit(solution)/shard_map/ppermute | solution.py:628
  58.6 39.0 %collective-permute-start.4 = (bf16[512,1664]{1,0:T(8,128)(2,1)}, bf16[512,1664]{1,0:T(8,128)(2,1)S(1)}, u32[]{:S(2)}, u32[]{:S(2)}) collective-permute-start(bf16[512,1664]{1,0:T(8,128)(2,1)} %pad_maximum_fusion.6.refs_0_.refs_2_), channel_id=1, source_target_pairs={{0,16},{8,24},{16,0},{24,8},{1,17},{9,25},{17,1},{25,9},{2,18},{10... | collective-permute-start | bytes 5111816 | tf_op jit(solution)/shard_map/ppermute | solution.py:628
  63.1 38.3 %collective-permute-start.10 = (bf16[128,1536]{1,0:T(8,128)(2,1)S(1)}, bf16[128,1536]{1,0:T(8,128)(2,1)S(1)}, u32[]{:S(2)}, u32[]{:S(2)}) collective-permute-start(bf16[128,1536]{1,0:T(8,128)(2,1)S(1)} %copy-done.49), channel_id=1, source_target_pairs={{0,3},{1,0},{2,1},{3,2},{4,7},{5,4},{6,5},{7,6},{8,11},{9,8},{10,9... | collective-permute-start | bytes 1179656 | tf_op jit(solution)/shard_map/ppermute | solution.py:633
  73.8 27.6 %collective-permute-start.8 = (bf16[128,1536]{1,0:T(8,128)(2,1)S(1)}, bf16[128,1536]{1,0:T(8,128)(2,1)S(1)}, u32[]{:S(2)}, u32[]{:S(2)}) collective-permute-start(bf16[128,1536]{1,0:T(8,128)(2,1)S(1)} %copy-done.49), channel_id=1, source_target_pairs={{0,1},{1,2},{2,3},{3,0},{4,5},{5,6},{6,7},{7,4},{8,9},{9,10},{10,1... | collective-permute-start | bytes 1179656 | tf_op jit(solution)/shard_map/ppermute | solution.py:633
  73.8 34.2 %collective-permute-start.9 = (bf16[128,1536]{1,0:T(8,128)(2,1)S(1)}, bf16[128,1536]{1,0:T(8,128)(2,1)S(1)}, u32[]{:S(2)}, u32[]{:S(2)}) collective-permute-start(bf16[128,1536]{1,0:T(8,128)(2,1)S(1)} %copy-done.49), channel_id=1, source_target_pairs={{0,2},{1,3},{2,0},{3,1},{4,6},{5,7},{6,4},{7,5},{8,10},{9,11},{10,... | collective-permute-start | bytes 1179656 | tf_op jit(solution)/shard_map/ppermute | solution.py:633
  98.6 19.8 %collective-permute-start.5 = (bf16[256,1664]{1,0:T(8,128)(2,1)}, bf16[256,1664]{1,0:T(8,128)(2,1)S(1)}, u32[]{:S(2)}, u32[]{:S(2)}) collective-permute-start(bf16[256,1664]{1,0:T(8,128)(2,1)} %slice.625), channel_id=1, source_target_pairs={{0,16},{8,24},{16,0},{24,8},{1,17},{9,25},{17,1},{25,9},{2,18},{10... | collective-permute-start | bytes 2555912 | tf_op jit(solution)/shard_map/ppermute | solution.py:628
  100.0 19.8 %collective-permute-start.6 = (bf16[256,1664]{1,0:T(8,128)(2,1)}, bf16[256,1664]{1,0:T(8,128)(2,1)}, u32[]{:S(2)}, u32[]{:S(2)}) collective-permute-start(bf16[256,1664]{1,0:T(8,128)(2,1)} %slice.626), channel_id=1, source_target_pairs={{0,8},{8,0},{16,24},{24,16},{1,9},{9,1},{17,25},{25,17},{2,10},{10... | collective-permute-start | bytes 2555912 | tf_op jit(solution)/shard_map/ppermute | solution.py:628
  119.9 284.3 %all-gather.4.cloned.1.call-start = ((), (), s32[]{:S(2)}) async-start(), calls=%async_computation.5 | async-start | bytes 3604480 | tf_op jit(solution)/shard_map/all_gather | solution.py:912
  135.8 62.3 %collective-permute-start.11 = (bf16[512,1536]{1,0:T(8,128)(2,1)S(1)}, bf16[512,1536]{1,0:T(8,128)(2,1)S(1)}, u32[]{:S(2)}, u32[]{:S(2)}) collective-permute-start(bf16[512,1536]{1,0:T(8,128)(2,1)S(1)} %copy-done.22), channel_id=1, source_target_pairs={{0,8},{8,0},{16,24},{24,16},{1,9},{9,1},{17,25},{25,17},{2,10},{10... | collective-permute-start | bytes 4718600 | tf_op jit(solution)/shard_map/ppermute | solution.py:628
  137.2 61.8 %collective-permute-start.12 = (bf16[512,1536]{1,0:T(8,128)(2,1)S(1)}, bf16[512,1536]{1,0:T(8,128)(2,1)}, u32[]{:S(2)}, u32[]{:S(2)}) collective-permute-start(bf16[512,1536]{1,0:T(8,128)(2,1)S(1)} %copy-done.22), channel_id=1, source_target_pairs={{0,16},{8,24},{16,0},{24,8},{1,17},{9,25},{17,1},{25,9},{2,18},{10... | collective-permute-start | bytes 4718600 | tf_op jit(solution)/shard_map/ppermute | solution.py:628
  138.3 31.7 %collective-permute-start.7 = (bf16[2,8,1536]{2,1,0:T(8,128)(2,1)S(1)}, bf16[2,8,1536]{2,1,0:T(8,128)(2,1)S(1)}, u32[]{:S(2)}, u32[]{:S(2)}) collective-permute-start(bf16[2,8,1536]{2,1,0:T(8,128)(2,1)S(1)} %slice_bitcast_fusion), channel_id=1, source_target_pairs={{0,8},{8,16},{16,24},{1,9},{9,17},{17,25},{2,10},{10,18},{18,26},{... | collective-permute-start | bytes 147464 | tf_op jit(solution)/shard_map/ppermute | solution.py:639
  203.6 17.7 %collective-permute-start.14 = (bf16[256,1536]{1,0:T(8,128)(2,1)}, bf16[256,1536]{1,0:T(8,128)(2,1)}, u32[]{:S(2)}, u32[]{:S(2)}) collective-permute-start(bf16[256,1536]{1,0:T(8,128)(2,1)} %slice.653), channel_id=1, source_target_pairs={{0,8},{8,0},{16,24},{24,16},{1,9},{9,1},{17,25},{25,17},{2,10},{10... | collective-permute-start | bytes 2359304 | tf_op jit(solution)/shard_map/ppermute | solution.py:628
  221.3 96.5 %collective-permute-start.16 = (bf16[512,2048]{1,0:T(8,128)(2,1)S(1)}, bf16[512,2048]{1,0:T(8,128)(2,1)}, u32[]{:S(2)}, u32[]{:S(2)}) collective-permute-start(bf16[512,2048]{1,0:T(8,128)(2,1)S(1)} %bitcast.140), channel_id=1, source_target_pairs={{0,8},{8,0},{16,24},{24,16},{1,9},{9,1},{17,25},{25,17},{2,10},{10... | collective-permute-start | bytes 6291464 | tf_op jit(solution)/shard_map/ppermute | solution.py:628
  222.3 95.6 %collective-permute-start.17 = (bf16[512,2048]{1,0:T(8,128)(2,1)S(1)}, bf16[512,2048]{1,0:T(8,128)(2,1)}, u32[]{:S(2)}, u32[]{:S(2)}) collective-permute-start(bf16[512,2048]{1,0:T(8,128)(2,1)S(1)} %bitcast.141), channel_id=1, source_target_pairs={{0,16},{8,24},{16,0},{24,8},{1,17},{9,25},{17,1},{25,9},{2,18},{10... | collective-permute-start | bytes 6291464 | tf_op jit(solution)/shard_map/ppermute | solution.py:628
  227.6 650.1 %reduce-scatter.4.cloned.1.call-start = ((), (), s32[]{:S(2)}) async-start(), calls=%async_computation.6 | async-start | bytes 11141120 | tf_op jit(solution)/shard_map/reduce_scatter | solution.py:1007
  230.0 92.6 %collective-permute-start.24 = (bf16[128,1024]{1,0:T(8,128)(2,1)S(1)}, bf16[128,1024]{1,0:T(8,128)(2,1)}, u32[]{:S(2)}, u32[]{:S(2)}) collective-permute-start(bf16[128,1024]{1,0:T(8,128)(2,1)S(1)} %bitcast.176), channel_id=1, source_target_pairs={{0,1},{1,2},{2,3},{3,0},{4,5},{5,6},{6,7},{7,4},{8,9},{9,10},{10,1... | collective-permute-start | bytes 786440 | tf_op jit(solution)/shard_map/ppermute | solution.py:633
  239.8 82.8 %collective-permute-start.25 = (bf16[128,1024]{1,0:T(8,128)(2,1)S(1)}, bf16[128,1024]{1,0:T(8,128)(2,1)}, u32[]{:S(2)}, u32[]{:S(2)}) collective-permute-start(bf16[128,1024]{1,0:T(8,128)(2,1)S(1)} %bitcast.177), channel_id=1, source_target_pairs={{0,2},{1,3},{2,0},{3,1},{4,6},{5,7},{6,4},{7,5},{8,10},{9,11},{10,... | collective-permute-start | bytes 786440 | tf_op jit(solution)/shard_map/ppermute | solution.py:633
  245.2 19.3 %collective-permute-start.15 = (bf16[2,8,1536]{2,1,0:T(8,128)(2,1)S(1)}, bf16[2,8,1536]{2,1,0:T(8,128)(2,1)S(1)}, u32[]{:S(2)}, u32[]{:S(2)}) collective-permute-start(bf16[2,8,1536]{2,1,0:T(8,128)(2,1)S(1)} %convert_bitcast_fusion.4), channel_id=1, source_target_pairs={{0,8},{8,16},{16,24},{1,9},{9,17},{17,25},{2,10},{10,18},{18,26},{... | collective-permute-start | bytes 147464 | tf_op jit(solution)/shard_map/ppermute | solution.py:639
  264.5 58.0 %collective-permute-start.26 = (bf16[128,1024]{1,0:T(8,128)(2,1)S(1)}, bf16[128,1024]{1,0:T(8,128)(2,1)}, u32[]{:S(2)}, u32[]{:S(2)}) collective-permute-start(bf16[128,1024]{1,0:T(8,128)(2,1)S(1)} %bitcast.178), channel_id=1, source_target_pairs={{0,3},{1,0},{2,1},{3,2},{4,7},{5,4},{6,5},{7,6},{8,11},{9,8},{10,9... | collective-permute-start | bytes 786440 | tf_op jit(solution)/shard_map/ppermute | solution.py:633
  336.4 59.2 %collective-permute-start.21 = (bf16[512,2048]{1,0:T(8,128)(2,1)S(1)}, bf16[512,2048]{1,0:T(8,128)(2,1)}, u32[]{:S(2)}, u32[]{:S(2)}) collective-permute-start(bf16[512,2048]{1,0:T(8,128)(2,1)S(1)} %bitcast.142), channel_id=1, source_target_pairs={{0,4},{4,0},{1,5},{5,1},{2,6},{6,2},{3,7},{7,3},{8,12},{12,8},{9,1... | collective-permute-start | bytes 6291464 | tf_op jit(solution)/shard_map/ppermute | solution.py:628
  336.5 59.1 %collective-permute-start.22 = (bf16[512,2048]{1,0:T(8,128)(2,1)}, bf16[512,2048]{1,0:T(8,128)(2,1)}, u32[]{:S(2)}, u32[]{:S(2)}) collective-permute-start(bf16[512,2048]{1,0:T(8,128)(2,1)} %collective-permute-done.16.mine_grads.refs_18_), channel_id=1, source_target_pairs={{0,4},{4,0},{1,5},{5,1},{2,6},{6,2},{3,7},{7,3},{8,12},{12,8},{9,1... | collective-permute-start | bytes 6291464 | tf_op jit(solution)/shard_map/ppermute | solution.py:628
  336.9 58.6 %collective-permute-start.23 = (bf16[512,2048]{1,0:T(8,128)(2,1)}, bf16[512,2048]{1,0:T(8,128)(2,1)}, u32[]{:S(2)}, u32[]{:S(2)}) collective-permute-start(bf16[512,2048]{1,0:T(8,128)(2,1)} %collective-permute-done.17.mine_grads.refs_20_), channel_id=1, source_target_pairs={{0,4},{4,0},{1,5},{5,1},{2,6},{6,2},{3,7},{7,3},{8,12},{12,8},{9,1... | collective-permute-start | bytes 6291464 | tf_op jit(solution)/shard_map/ppermute | solution.py:628
  337.0 32.4 %collective-permute-start.27 = (bf16[512,1024]{1,0:T(8,128)(2,1)S(1)}, bf16[512,1024]{1,0:T(8,128)(2,1)S(1)}, u32[]{:S(2)}, u32[]{:S(2)}) collective-permute-start(bf16[512,1024]{1,0:T(8,128)(2,1)S(1)} %pad_maximum_fusion.9.refs_1_.refs_0_), channel_id=1, source_target_pairs={{0,8},{8,0},{16,24},{24,16},{1,9},{9,1},{17,25},{25,17},{2,10},{10... | collective-permute-start | bytes 3145736 | tf_op jit(solution)/shard_map/ppermute | solution.py:628
  345.4 26.4 %collective-permute-start.28 = (bf16[512,1024]{1,0:T(8,128)(2,1)S(1)}, bf16[512,1024]{1,0:T(8,128)(2,1)S(1)}, u32[]{:S(2)}, u32[]{:S(2)}) collective-permute-start(bf16[512,1024]{1,0:T(8,128)(2,1)S(1)} %pad_maximum_fusion.9.refs_1_.refs_0_), channel_id=1, source_target_pairs={{0,16},{8,24},{16,0},{24,8},{1,17},{9,25},{17,1},{25,9},{2,18},{10... | collective-permute-start | bytes 3145736 | tf_op jit(solution)/shard_map/ppermute | solution.py:628
  372.6 22.9 %collective-permute-start.29 = (bf16[256,1024]{1,0:T(8,128)(2,1)}, bf16[256,1024]{1,0:T(8,128)(2,1)}, u32[]{:S(2)}, u32[]{:S(2)}) collective-permute-start(bf16[256,1024]{1,0:T(8,128)(2,1)} %slice.671), channel_id=1, source_target_pairs={{0,16},{8,24},{16,0},{24,8},{1,17},{9,25},{17,1},{25,9},{2,18},{10... | collective-permute-start | bytes 1572872 | tf_op jit(solution)/shard_map/ppermute | solution.py:628
  417.4 48.0 %collective-permute-start.34 = (bf16[512,2048]{1,0:T(8,128)(2,1)S(1)}, bf16[512,2048]{1,0:T(8,128)(2,1)}, u32[]{:S(2)}, u32[]{:S(2)}) collective-permute-start(bf16[512,2048]{1,0:T(8,128)(2,1)S(1)} %get-tuple-element.339.mine.refs_8_), channel_id=1, source_target_pairs={{0,8},{8,0},{16,24},{24,16},{1,9},{9,1},{17,25},{25,17},{2,10},{10... | collective-permute-start | bytes 6291464 | tf_op jit(solution)/shard_map/ppermute | solution.py:628
  422.5 48.1 %collective-permute-start.38 = (bf16[512,2048]{1,0:T(8,128)(2,1)S(1)}, bf16[512,2048]{1,0:T(8,128)(2,1)}, u32[]{:S(2)}, u32[]{:S(2)}) collective-permute-start(bf16[512,2048]{1,0:T(8,128)(2,1)S(1)} %get-tuple-element.339.mine.refs_8_), channel_id=1, source_target_pairs={{0,16},{8,24},{16,0},{24,8},{1,17},{9,25},{17,1},{25,9},{2,18},{10... | collective-permute-start | bytes 6291464 | tf_op jit(solution)/shard_map/ppermute | solution.py:628
  470.6 53.4 %collective-permute-start.41 = (bf16[512,2048]{1,0:T(8,128)(2,1)}, bf16[512,2048]{1,0:T(8,128)(2,1)}, u32[]{:S(2)}, u32[]{:S(2)}) collective-permute-start(bf16[512,2048]{1,0:T(8,128)(2,1)} %collective-permute-done.38.mine.refs_12_), channel_id=1, source_target_pairs={{0,4},{4,0},{1,5},{5,1},{2,6},{6,2},{3,7},{7,3},{8,12},{12,8},{9,1... | collective-permute-start | bytes 6291464 | tf_op jit(solution)/shard_map/ppermute | solution.py:628
  474.3 79.9 %collective-permute-start.45 = (bf16[256,2048]{1,0:T(8,128)(2,1)}, bf16[256,2048]{1,0:T(8,128)(2,1)}, u32[]{:S(2)}, u32[]{:S(2)}) collective-permute-start(bf16[256,2048]{1,0:T(8,128)(2,1)} %slice.676), channel_id=1, source_target_pairs={{0,16},{8,24},{16,0},{24,8},{1,17},{9,25},{17,1},{25,9},{2,18},{10... | collective-permute-start | bytes 3145736 | tf_op jit(solution)/shard_map/ppermute | solution.py:628
  476.1 79.4 %collective-permute-start.46 = (bf16[256,2048]{1,0:T(8,128)(2,1)S(1)}, bf16[256,2048]{1,0:T(8,128)(2,1)S(1)}, u32[]{:S(2)}, u32[]{:S(2)}) collective-permute-start(bf16[256,2048]{1,0:T(8,128)(2,1)S(1)} %slice.677), channel_id=1, source_target_pairs={{0,8},{8,0},{16,24},{24,16},{1,9},{9,1},{17,25},{25,17},{2,10},{10... | collective-permute-start | bytes 3145736 | tf_op jit(solution)/shard_map/ppermute | solution.py:628
  481.4 41.3 %collective-permute-start.39 = (bf16[256,2048]{1,0:T(8,128)(2,1)}, bf16[256,2048]{1,0:T(8,128)(2,1)S(1)}, u32[]{:S(2)}, u32[]{:S(2)}) collective-permute-start(bf16[256,2048]{1,0:T(8,128)(2,1)} %slice.674), channel_id=1, source_target_pairs={{0,16},{8,24},{16,0},{24,8},{1,17},{9,25},{17,1},{25,9},{2,18},{10... | collective-permute-start | bytes 3145736 | tf_op jit(solution)/shard_map/ppermute | solution.py:628
  482.0 42.1 %collective-permute-start.40 = (bf16[256,2048]{1,0:T(8,128)(2,1)}, bf16[256,2048]{1,0:T(8,128)(2,1)}, u32[]{:S(2)}, u32[]{:S(2)}) collective-permute-start(bf16[256,2048]{1,0:T(8,128)(2,1)} %slice.675), channel_id=1, source_target_pairs={{0,8},{8,0},{16,24},{24,16},{1,9},{9,1},{17,25},{25,17},{2,10},{10... | collective-permute-start | bytes 3145736 | tf_op jit(solution)/shard_map/ppermute | solution.py:628
  560.5 48.0 %collective-permute-start.43 = (bf16[512,2048]{1,0:T(8,128)(2,1)}, bf16[512,2048]{1,0:T(8,128)(2,1)S(1)}, u32[]{:S(2)}, u32[]{:S(2)}) collective-permute-start(bf16[512,2048]{1,0:T(8,128)(2,1)} %add_convert_fusion.5), channel_id=1, source_target_pairs={{0,16},{8,24},{16,0},{24,8},{1,17},{9,25},{17,1},{25,9},{2,18},{10... | collective-permute-start | bytes 6291464 | tf_op jit(solution)/shard_map/ppermute | solution.py:628
  566.2 48.0 %collective-permute-start.37 = (bf16[512,2048]{1,0:T(8,128)(2,1)}, bf16[512,2048]{1,0:T(8,128)(2,1)}, u32[]{:S(2)}, u32[]{:S(2)}) collective-permute-start(bf16[512,2048]{1,0:T(8,128)(2,1)} %add_convert_fusion.6), channel_id=1, source_target_pairs={{0,8},{8,0},{16,24},{24,16},{1,9},{9,1},{17,25},{25,17},{2,10},{10... | collective-permute-start | bytes 6291464 | tf_op jit(solution)/shard_map/ppermute | solution.py:628
  566.9 47.3 %collective-permute-start.51 = (bf16[512,2048]{1,0:T(8,128)(2,1)}, bf16[512,2048]{1,0:T(8,128)(2,1)}, u32[]{:S(2)}, u32[]{:S(2)}) collective-permute-start(bf16[512,2048]{1,0:T(8,128)(2,1)} %get-tuple-element.169), channel_id=1, source_target_pairs={{0,4},{4,0},{1,5},{5,1},{2,6},{6,2},{3,7},{7,3},{8,12},{12,8},{9,1... | collective-permute-start | bytes 6291464 | tf_op jit(solution)/shard_map/ppermute | solution.py:628
  568.2 50.6 %collective-permute-start.50 = (bf16[512,2048]{1,0:T(8,128)(2,1)}, bf16[512,2048]{1,0:T(8,128)(2,1)}, u32[]{:S(2)}, u32[]{:S(2)}) collective-permute-start(bf16[512,2048]{1,0:T(8,128)(2,1)} %get-tuple-element.167), channel_id=1, source_target_pairs={{0,4},{4,0},{1,5},{5,1},{2,6},{6,2},{3,7},{7,3},{8,12},{12,8},{9,1... | collective-permute-start | bytes 6291464 | tf_op jit(solution)/shard_map/ppermute | solution.py:628
  623.5 49.1 %collective-permute-start.49 = (bf16[512,2048]{1,0:T(8,128)(2,1)S(1)}, bf16[512,2048]{1,0:T(8,128)(2,1)}, u32[]{:S(2)}, u32[]{:S(2)}) collective-permute-start(bf16[512,2048]{1,0:T(8,128)(2,1)S(1)} %add_convert_fusion.4), channel_id=1, source_target_pairs={{0,24},{8,16},{16,8},{24,0},{1,25},{9,17},{17,9},{25,1},{2,26},{10... | collective-permute-start | bytes 6291464 | tf_op jit(solution)/shard_map/ppermute | solution.py:628
  684.2 364.6 %reduce-scatter.8.cloned.1.call-start = ((), (), s32[]{:S(2)}) async-start(), calls=%async_computation.8 | async-start | bytes 4456448 | tf_op jit(solution)/shard_map/reduce_scatter | solution.py:1011
  700.0 48.2 %collective-permute-start.55 = (bf16[512,2048]{1,0:T(8,128)(2,1)}, bf16[512,2048]{1,0:T(8,128)(2,1)}, u32[]{:S(2)}, u32[]{:S(2)}) collective-permute-start(bf16[512,2048]{1,0:T(8,128)(2,1)} %add_convert_fusion.2), channel_id=1, source_target_pairs={{0,16},{8,24},{16,0},{24,8},{1,17},{9,25},{17,1},{25,9},{2,18},{10... | collective-permute-start | bytes 6291464 | tf_op jit(solution)/shard_map/ppermute | solution.py:628
  701.3 48.8 %collective-permute-start.54 = (bf16[512,2048]{1,0:T(8,128)(2,1)}, bf16[512,2048]{1,0:T(8,128)(2,1)}, u32[]{:S(2)}, u32[]{:S(2)}) collective-permute-start(bf16[512,2048]{1,0:T(8,128)(2,1)} %add_convert_fusion.3), channel_id=1, source_target_pairs={{0,8},{8,0},{16,24},{24,16},{1,9},{9,1},{17,25},{25,17},{2,10},{10... | collective-permute-start | bytes 6291464 | tf_op jit(solution)/shard_map/ppermute | solution.py:628
  709.4 68.1 %collective-permute-start.56 = (bf16[512,2048]{1,0:T(8,128)(2,1)}, bf16[512,2048]{1,0:T(8,128)(2,1)}, u32[]{:S(2)}, u32[]{:S(2)}) collective-permute-start(bf16[512,2048]{1,0:T(8,128)(2,1)} %get-tuple-element.183), channel_id=1, source_target_pairs={{0,4},{4,0},{1,5},{5,1},{2,6},{6,2},{3,7},{7,3},{8,12},{12,8},{9,1... | collective-permute-start | bytes 6291464 | tf_op jit(solution)/shard_map/ppermute | solution.py:628
  731.4 28.9 %collective-permute-start.57 = (bf16[2,8,128,128]{3,2,1,0:T(8,128)(2,1)S(1)}, bf16[2,8,128,128]{3,2,1,0:T(8,128)(2,1)S(1)}, u32[]{:S(2)}, u32[]{:S(2)}) collective-permute-start(bf16[2,8,128,128]{3,2,1,0:T(8,128)(2,1)S(1)} %convert_element_type.366), channel_id=1, source_target_pairs={{8,0},{16,8},{24,16},{9,1},{17,9},{25,17},{10,2},{18,10},{26,18},{... | collective-permute-start | bytes 1572872 | tf_op jit(solution)/shard_map/ppermute | solution.py:639
  790.4 46.6 %collective-permute-start.60 = (bf16[512,2048]{1,0:T(8,128)(2,1)}, bf16[512,2048]{1,0:T(8,128)(2,1)}, u32[]{:S(2)}, u32[]{:S(2)}) collective-permute-start(bf16[512,2048]{1,0:T(8,128)(2,1)} %add_convert_fusion.1), channel_id=1, source_target_pairs={{0,24},{8,16},{16,8},{24,0},{1,25},{9,17},{17,9},{25,1},{2,26},{10... | collective-permute-start | bytes 6291464 | tf_op jit(solution)/shard_map/ppermute | solution.py:628
  790.5 46.6 %collective-permute-start.53 = (bf16[512,2048]{1,0:T(8,128)(2,1)}, bf16[512,2048]{1,0:T(8,128)(2,1)}, u32[]{:S(2)}, u32[]{:S(2)}) collective-permute-start(bf16[512,2048]{1,0:T(8,128)(2,1)} %get-tuple-element.178), channel_id=1, source_target_pairs={{0,4},{4,0},{1,5},{5,1},{2,6},{6,2},{3,7},{7,3},{8,12},{12,8},{9,1... | collective-permute-start | bytes 6291464 | tf_op jit(solution)/shard_map/ppermute | solution.py:628
  846.5 26.6 %collective-permute-start.61 = (bf16[2,256,2048]{2,1,0:T(8,128)(2,1)}, bf16[2,256,2048]{2,1,0:T(8,128)(2,1)}, u32[]{:S(2)}, u32[]{:S(2)}) collective-permute-start(bf16[2,256,2048]{2,1,0:T(8,128)(2,1)} %bitcast.29), channel_id=1, source_target_pairs={{0,4},{4,0},{1,5},{5,1},{2,6},{6,2},{3,7},{7,3},{8,12},{12,8},{9,1... | collective-permute-start | bytes 6291464 | tf_op jit(solution)/shard_map/ppermute | solution.py:628
  850.4 264.6 %reduce-scatter.6.cloned.1.call-start = ((), (), s32[]{:S(2)}) async-start(), calls=%async_computation.7 | async-start | bytes 1966080 | tf_op jit(solution)/shard_map/reduce_scatter | solution.py:1060
  862.8 94.4 %collective-permute-start.79 = (bf16[512,1536]{1,0:T(8,128)(2,1)}, bf16[512,1536]{1,0:T(8,128)(2,1)}, u32[]{:S(2)}, u32[]{:S(2)}) collective-permute-start(bf16[512,1536]{1,0:T(8,128)(2,1)} %convolution_convert_fusion.3), channel_id=1, source_target_pairs={{0,16},{8,24},{16,0},{24,8},{1,17},{9,25},{17,1},{25,9},{2,18},{10... | collective-permute-start | bytes 4718600 | tf_op jit(solution)/shard_map/ppermute | solution.py:628
  866.5 90.7 %collective-permute-start.78 = (bf16[512,1536]{1,0:T(8,128)(2,1)}, bf16[512,1536]{1,0:T(8,128)(2,1)}, u32[]{:S(2)}, u32[]{:S(2)}) collective-permute-start(bf16[512,1536]{1,0:T(8,128)(2,1)} %convolution_convert_fusion.4), channel_id=1, source_target_pairs={{0,8},{8,0},{16,24},{24,16},{1,9},{9,1},{17,25},{25,17},{2,10},{10... | collective-permute-start | bytes 4718600 | tf_op jit(solution)/shard_map/ppermute | solution.py:628
  910.9 29.9 %collective-permute-start.63 = (f32[2,8,1536]{2,1,0:T(8,128)}, f32[2,8,1536]{2,1,0:T(8,128)S(1)}, u32[]{:S(2)}, u32[]{:S(2)}) collective-permute-start(f32[2,8,1536]{2,1,0:T(8,128)} %get-tuple-element.206), channel_id=1, source_target_pairs={{8,0},{16,8},{24,16},{9,1},{17,9},{25,17},{10,2},{18,10},{26,18},{... | collective-permute-start | bytes 294920 | tf_op jit(solution)/shard_map/ppermute | solution.py:639
  948.1 40.5 %collective-permute-start.65 = (bf16[512,1664]{1,0:T(8,128)(2,1)}, bf16[512,1664]{1,0:T(8,128)(2,1)}, u32[]{:S(2)}, u32[]{:S(2)}) collective-permute-start(bf16[512,1664]{1,0:T(8,128)(2,1)} %convolution_convert_fusion.1), channel_id=1, source_target_pairs={{0,16},{8,24},{16,0},{24,8},{1,17},{9,25},{17,1},{25,9},{2,18},{10... | collective-permute-start | bytes 5111816 | tf_op jit(solution)/shard_map/ppermute | solution.py:628
  953.3 40.5 %collective-permute-start.64 = (bf16[512,1664]{1,0:T(8,128)(2,1)}, bf16[512,1664]{1,0:T(8,128)(2,1)}, u32[]{:S(2)}, u32[]{:S(2)}) collective-permute-start(bf16[512,1664]{1,0:T(8,128)(2,1)} %convolution_convert_fusion.2), channel_id=1, source_target_pairs={{0,8},{8,0},{16,24},{24,16},{1,9},{9,1},{17,25},{25,17},{2,10},{10... | collective-permute-start | bytes 5111816 | tf_op jit(solution)/shard_map/ppermute | solution.py:628
  963.7 41.7 %collective-permute-start.81 = (bf16[256,1536]{1,0:T(8,128)(2,1)S(1)}, bf16[256,1536]{1,0:T(8,128)(2,1)}, u32[]{:S(2)}, u32[]{:S(2)}) collective-permute-start(bf16[256,1536]{1,0:T(8,128)(2,1)S(1)} %fusion.20), channel_id=1, source_target_pairs={{0,16},{8,24},{16,0},{24,8},{1,17},{9,25},{17,1},{25,9},{2,18},{10... | collective-permute-start | bytes 2359304 | tf_op jit(solution)/shard_map/ppermute | solution.py:628
  969.3 41.3 %collective-permute-start.80 = (bf16[256,1536]{1,0:T(8,128)(2,1)S(1)}, bf16[256,1536]{1,0:T(8,128)(2,1)}, u32[]{:S(2)}, u32[]{:S(2)}) collective-permute-start(bf16[256,1536]{1,0:T(8,128)(2,1)S(1)} %fusion.21), channel_id=1, source_target_pairs={{0,8},{8,0},{16,24},{24,16},{1,9},{9,1},{17,25},{25,17},{2,10},{10... | collective-permute-start | bytes 2359304 | tf_op jit(solution)/shard_map/ppermute | solution.py:628
  997.5 34.4 %collective-permute-start.67 = (bf16[256,1664]{1,0:T(8,128)(2,1)}, bf16[256,1664]{1,0:T(8,128)(2,1)S(1)}, u32[]{:S(2)}, u32[]{:S(2)}) collective-permute-start(bf16[256,1664]{1,0:T(8,128)(2,1)} %fusion.15), channel_id=1, source_target_pairs={{0,16},{8,24},{16,0},{24,8},{1,17},{9,25},{17,1},{25,9},{2,18},{10... | collective-permute-start | bytes 2555912 | tf_op jit(solution)/shard_map/ppermute | solution.py:628
  1002.5 29.5 %collective-permute-start.66 = (bf16[256,1664]{1,0:T(8,128)(2,1)}, bf16[256,1664]{1,0:T(8,128)(2,1)}, u32[]{:S(2)}, u32[]{:S(2)}) collective-permute-start(bf16[256,1664]{1,0:T(8,128)(2,1)} %fusion.16), channel_id=1, source_target_pairs={{0,8},{8,0},{16,24},{24,16},{1,9},{9,1},{17,25},{25,17},{2,10},{10... | collective-permute-start | bytes 2555912 | tf_op jit(solution)/shard_map/ppermute | solution.py:628
  1035.3 27.4 %collective-permute-start.68 = (bf16[2,256,2048]{2,1,0:T(8,128)(2,1)}, bf16[2,256,2048]{2,1,0:T(8,128)(2,1)}, u32[]{:S(2)}, u32[]{:S(2)}) collective-permute-start(bf16[2,256,2048]{2,1,0:T(8,128)(2,1)} %constant_dynamic-slice_fusion.3), channel_id=1, source_target_pairs={{0,4},{4,0},{1,5},{5,1},{2,6},{6,2},{3,7},{7,3},{8,12},{12,8},{9,1... | collective-permute-start | bytes 6291464 | tf_op jit(solution)/shard_map/ppermute | solution.py:628
  1044.4 31.0 %all-to-all-start.1 = ((bf16[4,2112,128]{2,1,0:T(8,128)(2,1)}), bf16[4,2112,128]{2,1,0:T(8,128)(2,1)}, u32[]{:S(2)}, u32[]{:S(2)}) async-start(bf16[4,2112,128]{2,1,0:T(8,128)(2,1)} %copy.150), calls=%async_computation.4 | async-start | bytes 4325376 | tf_op jit(solution)/shard_map/all_to_all | solution.py:1072
  1057.7 58.8 %collective-permute-start.75 = (bf16[128,1664]{1,0:T(8,128)(2,1)}, bf16[128,1664]{1,0:T(8,128)(2,1)}, u32[]{:S(2)}, u32[]{:S(2)}) collective-permute-start(bf16[128,1664]{1,0:T(8,128)(2,1)} %get-tuple-element.355), channel_id=1, source_target_pairs={{0,1},{1,2},{2,3},{3,0},{4,5},{5,6},{6,7},{7,4},{8,9},{9,10},{10,1... | collective-permute-start | bytes 1277960 | tf_op jit(solution)/shard_map/ppermute | solution.py:633
  1057.7 58.8 %collective-permute-start.76 = (bf16[128,1664]{1,0:T(8,128)(2,1)}, bf16[128,1664]{1,0:T(8,128)(2,1)}, u32[]{:S(2)}, u32[]{:S(2)}) collective-permute-start(bf16[128,1664]{1,0:T(8,128)(2,1)} %get-tuple-element.354), channel_id=1, source_target_pairs={{0,2},{1,3},{2,0},{3,1},{4,6},{5,7},{6,4},{7,5},{8,10},{9,11},{10,... | collective-permute-start | bytes 1277960 | tf_op jit(solution)/shard_map/ppermute | solution.py:633
  1062.7 53.8 %collective-permute-start.77 = (bf16[128,1664]{1,0:T(8,128)(2,1)}, bf16[128,1664]{1,0:T(8,128)(2,1)}, u32[]{:S(2)}, u32[]{:S(2)}) collective-permute-start(bf16[128,1664]{1,0:T(8,128)(2,1)} %get-tuple-element.353), channel_id=1, source_target_pairs={{0,3},{1,0},{2,1},{3,2},{4,7},{5,4},{6,5},{7,6},{8,11},{9,8},{10,9... | collective-permute-start | bytes 1277960 | tf_op jit(solution)/shard_map/ppermute | solution.py:633
  (105 other events, 1303.3 us)
Sparse Core Ops, SparseCore 0:
  120.0 115.3 all-gather.5
  237.0 67.1 all-gather.3
  684.3 155.0 reduce-scatter.3
  850.5 100.7 reduce-scatter.7
  1040.3 54.5 reduce-scatter.5

commit v9 on v8

--- a/solution.py
+++ b/solution.py
@@ -904,12 +904,12 @@
     tokens = block_input.reshape(row_count, width)
     inputs = wide(tokens)
     normed_mix = low(inputs * rms_scale(inputs, EPSILON) * gain_mix)
-    inputs_mine = wide(rows_mine(block_input).reshape(-1, width))
     grads_mine = rows_mine(out_grad).reshape(-1, width)
 
     square = Square(tie(lines[0], ffn_swapped)).forward(normed_mix)
-    gate_up_parts = lax.all_gather(tie(ffn_line[: 2 * units], lines[parts - 1], *square.done()), "fsdp", axis=0)
-    down_parts = lax.all_gather(ffn_line[2 * units :], "fsdp", axis=0)
+    gate_up_parts = tie(ffn_line[None, : 2 * units], lines[parts - 1], *square.done())
+    gate_up_parts = lax.all_gather(gate_up_parts, "fsdp", axis=0, tiled=True)
+    down_parts = lax.all_gather(ffn_line[None, 2 * units :], "fsdp", axis=0, tiled=True)
     mix_full, kept, pre = [], [], []
     for p in range(parts):
         mix_full.append(square.pieces())
@@ -917,9 +917,10 @@
         ends = normed_mix.reshape(seq_count, local_len, width)[:, local_len - HALO :].reshape(seq_count * HALO, width)
         ends = gathered_times(ends, ctx_place, mix_full[p])
         ends = low(ends)
-        square = Square(tie(lines[p + 1], ends, *arrived))
-        halo = wide(from_behind(ends[:, :part_cols].reshape(seq_count, HALO, part_cols), "ctx", 1))
+        halo = from_behind(ends[:, :part_cols].reshape(seq_count, HALO, part_cols), "ctx", 1)
         pre.append(gathered_times(tie(normed_mix, ends), ctx_place, mix_full[p]))
+        square = Square(tie(lines[p + 1], halo, pre[p], *arrived))
+        halo = wide(halo)
         convs = conv[:, p * part_cols : (p + 1) * part_cols]
         kept.append(
             [halo, convs]
@@ -935,6 +936,7 @@
             grad_square = Square(tie(grads_mine, kept[p][2], *square.done()))
     out_full = square.pieces()
 
+    inputs_mine = wide(rows_mine(tie(block_input, kept[0][2])).reshape(-1, width))
     gate_up_full = columns_join(gate_up_parts, 4)
     finals = jnp.concatenate([some[4] for some in kept], axis=1)
     transfer = low(finals[..., LANES:])
@@ -984,7 +986,7 @@
         [side for sides in grad_rows for side in sides],
         line_count,
         4,
-    ).reshape(line_count, 3 * units, 4 * shard_rows)
+    )
 
     far_sums, sums = lax.optimization_barrier((far_sums, sums))
     result_near = [flip(tie(part, far_sums), "ctx", bit) for part, bit in zip(result_low, (1, 2))]
@@ -1027,8 +1029,6 @@
             entered[p], grad_end[:, heads], taps, p * part_heads, part_heads, group,
         )
         logits = logits + logit
-        if scatter is None:
-            result_far = tie(result_far, before)
         tail = low(tail + from_behind(before, "ctx", -1))
         grad_mix = put(grad_mix.reshape(seq_count, local_len, -1), tail, 0, local_len - HALO, 0)
         grad_mix = grad_mix.reshape(row_count, -1)
@@ -1041,6 +1041,8 @@
             grad_mix = jnp.concatenate([grad_mix, low(logits)], axis=1)
         grad_mixes[p] = grad_mix
         scatter = Scatter(columns, grad_mix)
+        if p > 0:
+            result_far = tie(result_far, *scatter.sent)
     result = result_own + wide(result_near[0]) + wide(result_near[1])
     result = result + wide(result_far)
     block_output = rows_full(low(residual + result).reshape(seq_count, -1, width))
@@ -1059,7 +1061,7 @@
         own = low(earlier_scatter.own(*ready))
         mix_grads[p] = wide(lax.psum_scatter(own, "fsdp", scatter_dimension=0, tiled=True))
     last_line = Line(scatter.own())
-    sums = butterfly(tie(sums, *last_line.sent), ("ctx", "fsdp"))
+    sums = butterfly(tie(sums, input_grad, *last_line.sent), ("ctx", "fsdp"))
     mix_grads[0] = last_line.total(sums)
     query_grad, key_grad, value_grad = by_kind([grad[:, :part_cols] for grad in mix_grads])
     beta_grad = mix_grads[0][:, part_cols : part_cols + heads_here]

time: 1150 us -> 1130 us (0.983)
  other arithmetic: 136 us -> 124 us
  waiting for transfers between devices: 312 us -> 324 us
    ppermute x60, waiting for transfers between devices: 173 us -> 199 us  [flip(): return lax.ppermute(value, axis, [(i, i ^ bit) for i in devices])]
    ppermute x60, starting transfers between devices: 64.9 us -> 53.4 us  [flip(): return lax.ppermute(value, axis, [(i, i ^ bit) for i in devices])]
    unnamed x211 -> x214, local copies, waits for them, and re-layouts: 31.2 us -> 34.4 us
  transfers between devices with their start and end apart: 89 -> 89, of which waited for: 41 -> 40; matrix products, arithmetic and copies ran while one was open for 21% -> 20% of each run, Pallas kernels for 35% -> 35%
where the time goes in v9:
time: 1130 us; the launch traced here: 1120 us
  Pallas kernels  394 us (35%)
  waiting for transfers between devices  324 us (29%)
  other arithmetic  124 us (11%)
  starting transfers between devices  124 us (11%)
  local copies, waits for them, and re-layouts  91.7 us (8%)
  matrix products  50.2 us (4%)
  between operations  15.5 us (1%)
    ppermute x60, waiting for transfers between devices, flip(): return lax.ppermute(value, axis, [(i, i ^ bit) for i in devices])  199 us
    pallas_call x4, Pallas kernels, ffn_both(): pl.pallas_call(ffn_kernel, grid=(count // tile,), in_specs=[wide_rows] *...  119 us
    ppermute x10, waiting for transfers between devices, from_behind(): return lax.ppermute(block, axis, route)  91.5 us
    pallas_call x2, Pallas kernels, mixer_backward(): pl.pallas_call(functools.partial(backward_kernel, taps, group, first), gr...  66.7 us
    pallas_call x2, Pallas kernels, mixer_forward(): pl.pallas_call(functools.partial(forward_kernel, taps, group, first), gri...  55.2 us
    ppermute x60, starting transfers between devices, flip(): return lax.ppermute(value, axis, [(i, i ^ bit) for i in devices])  53.4 us
    pallas_call x1, Pallas kernels, ffn_weights(): pl.pallas_call(functools.partial(ffn_weights_kernel, count, lines), grid=...  48 us
    dot_general x11, matrix products, outer_rows(): lax.dot_general(left, right, (((0,), (0,)), ((), ())), preferred_element_...  46.7 us
  transfers between devices with their start and end apart: 89, of which 40 were waited for; matrix products, arithmetic and copies ran while one was open for 20% of the time, Pallas kernels for 35%

profile of v9, /device:TPU:0, one launch (start us, length us, event | category | flops | bytes accessed | tf_op | source)
XLA Modules:
  0.0 1124.0 jit_solution(10582630885805018626)
XLA Ops:
  12.6 5.3 all-to-all-start
  27.8 9.3 collective-permute-done
  37.1 17.1 %collective-permute-done.1 = bf16[128,1664]{1,0:T(8,128)(2,1)S(1)} collective-permute-done((bf16[128,1664]{1,0:T(8,128)(2,1)}, bf16[128,1664]{1,0:T(8,128)(2,1)S(1)}, u32[]{:S(2)}, u32[]{:S(2)}) %collective-permute-start.1) | collective-permute-done | bytes 426016 | tf_op jit(solution)/shard_map/ppermute | solution.py:633
  63.1 10.7 collective-permute-start.10
  77.4 18.7 %collective-permute-done.3.refs_1_.refs_3_ = bf16[512,1664]{1,0:T(8,128)(2,1)S(1)} collective-permute-done((bf16[512,1664]{1,0:T(8,128)(2,1)}, bf16[512,1664]{1,0:T(8,128)(2,1)S(1)}, u32[]{:S(2)}, u32[]{:S(2)}) %collective-permute-start.3) | collective-permute-done | bytes 1703968 | tf_op jit(solution)/shard_map/ppermute | solution.py:628
  101.3 6.6 collective-permute-done.9
  112.4 5.9 collective-permute-done.5.refs_3_.refs_5_
  121.4 6.6 convert_element_type.409
  131.4 4.7 shard_map.271
  140.7 12.8 %shard_map.272.pre.beta = f32[1024,1664]{1,0:T(8,128)} custom-call(s32[1]{0:T(128)} %bitcast.place, bf16[1024,2048]{1,0:T(8,128)(2,1)} %fusion.1.rows, bf16[512,1664]{1,0:T(8,128)(2,1)} %pad_maximum_fusion.6.refs_0_.refs_2_, bf16[512,1664]{1,0:T(8,128)(2,1)} %copy-done.26, bf16[512,1664]{1,0:T(8,128)(2,1)} %copy-done.27, bf16[256,1664]{1,0:T(8,128)(2,1)} %copy-done.46, ...), custom_call_target="tpu_custom_call" | custom-call | flops 6979321856 | bytes 11010048 | tf_op jit(solution)/shard_map/pallas_call | solution.py:551
  155.4 27.5 %shard_map.273 = (f32[1024,512]{1,0:T(8,128)}, bf16[1024,512]{1,0:T(8,128)(2,1)}, f32[2,4,128,256]{3,2,1,0:T(8,128)}, bf16[2,4,4,128,128]{4,3,2,1,0:T(8,128)(2,1...) custom-call(f32[1024,1664]{1,0:T(8,128)} %shard_map.272.pre.beta, ...), custom_call_target="tpu_custom_call" | custom-call | flops 4026531840 | bytes 20971520 | tf_op jit(solution)/shard_map/pallas_call | solution.py:160
  182.9 4.8 collective-permute-done.11.refs_1_.refs_8_
  194.3 13.6 %collective-permute-done.13.refs_3_.refs_10_ = bf16[256,1536]{1,0:T(8,128)(2,1)S(1)} collective-permute-done((bf16[256,1536]{1,0:T(8,128)(2,1)}, bf16[256,1536]{1,0:T(8,128)(2,1)S(1)}, u32[]{:S(2)}, u32[]{:S(2)}) %collective-permute-start.13) | collective-permute-done | bytes 786464 | tf_op jit(solution)/shard_map/ppermute | solution.py:628
  218.1 10.1 collective-permute-start.24
  228.2 4.4 shard_map.274
  236.6 11.5 %shard_map.275.pre = f32[1024,1536]{1,0:T(8,128)} custom-call(s32[1]{0:T(128)} %bitcast.place, bf16[1024,2048]{1,0:T(8,128)(2,1)} %fusion.1.rows, bf16[512,1536]{1,0:T(8,128)(2,1)} %pad_maximum_fusion.7.refs_0_.refs_7_, bf16[512,1536]{1,0:T(8,128)(2,1)} %copy-done.28, bf16[512,1536]{1,0:T(8,128)(2,1)} %collective-permute-done.12.refs_2_.refs_9_, ...), custom_call_target="tpu_custom_call" | custom-call | flops 6442450944 | bytes 10485760 | tf_op jit(solution)/shard_map/pallas_call | solution.py:551
  252.4 4.9 collective-permute-start.26
  257.9 27.7 %shard_map.276 = (f32[1024,512]{1,0:T(8,128)}, bf16[1024,512]{1,0:T(8,128)(2,1)}, f32[2,4,128,256]{3,2,1,0:T(8,128)}, bf16[2,4,4,128,128]{4,3,2,1,0:T(8,128)(2,1...) custom-call(f32[1024,1536]{1,0:T(8,128)} %shard_map.275.pre, ...), custom_call_target="tpu_custom_call" | custom-call | flops 4026531840 | bytes 20971520 | tf_op jit(solution)/shard_map/pallas_call | solution.py:160
  289.3 8.1 shard_map.277.gate_w.up_w
  297.5 4.5 collective-permute-start.18
  303.3 8.0 collective-permute-done.18
  311.6 4.4 collective-permute-start.19
  318.8 7.2 collective-permute-done.19
  326.0 6.0 collective-permute-start.28
  332.3 15.4 %collective-permute-done.27.refs_2_.refs_1_ = bf16[512,1024]{1,0:T(8,128)(2,1)S(1)} collective-permute-done((bf16[512,1024]{1,0:T(8,128)(2,1)S(1)}, bf16[512,1024]{1,0:T(8,128)(2,1)S(1)}, u32[]{:S(2)}, u32[]{:S(2)}) %collective-permute-start.27) | collective-permute-done | bytes 1048608 | tf_op jit(solution)/shard_map/ppermute | solution.py:628
  353.9 5.0 collective-permute-done.20
  362.5 4.5 shard_map.278
  367.0 4.6 shard_map.279
  374.4 8.7 shard_map.280
  396.2 4.9 shard_map.281.down_w
  403.7 29.7 %shard_map.282 = (bf16[3,512,704]{2,1,0:T(8,128)(2,1)}, bf16[512,2048]{1,0:T(8,128)(2,1)}, bf16[512,2048]{1,0:T(8,128)(2,1)}, bf16[3,512,704]{2,1,0:T(8,128)(2,1...) custom-call(bf16[512,2048]{1,0:T(8,128)(2,1)} %copy-done.41, ...), custom_call_target="tpu_custom_call" | custom-call | flops 17716740096 | bytes 25427968 | tf_op jit(solution)/shard_map/pallas_call | solution.py:469
  433.4 10.9 collective-permute-done.34.mine.refs_10_
  444.2 5.4 collective-permute-done.38.mine.refs_12_
  462.0 29.6 %shard_map.283 = (bf16[3,512,704]{2,1,0:T(8,128)(2,1)}, bf16[512,2048]{1,0:T(8,128)(2,1)}, bf16[512,2048]{1,0:T(8,128)(2,1)}, bf16[3,512,704]{2,1,0:T(8,128)(2,1...) custom-call(bf16[512,2048]{1,0:T(8,128)(2,1)} %collective-permute-done.34.mine.refs_10_, ...), custom_call_target="tpu_custom_call" | custom-call | flops 17716740096 | bytes 25427968 | tf_op jit(solution)/shard_map/pallas_call | solution.py:469
  491.6 10.0 collective-permute-done.39
  503.0 29.5 %shard_map.284 = (bf16[3,512,704]{2,1,0:T(8,128)(2,1)}, bf16[512,2048]{1,0:T(8,128)(2,1)}, bf16[512,2048]{1,0:T(8,128)(2,1)}, bf16[3,512,704]{2,1,0:T(8,128)(2,1...) custom-call(bf16[512,2048]{1,0:T(8,128)(2,1)} %collective-permute-done.38.mine.refs_12_, ...), custom_call_target="tpu_custom_call" | custom-call | flops 17716740096 | bytes 25427968 | tf_op jit(solution)/shard_map/pallas_call | solution.py:469
  548.2 29.7 %shard_map.285 = (bf16[3,512,704]{2,1,0:T(8,128)(2,1)}, bf16[512,2048]{1,0:T(8,128)(2,1)}, bf16[512,2048]{1,0:T(8,128)(2,1)}, bf16[3,512,704]{2,1,0:T(8,128)(2,1...) custom-call(bf16[512,2048]{1,0:T(8,128)(2,1)} %copy-done.52, ...), custom_call_target="tpu_custom_call" | custom-call | flops 17716740096 | bytes 25427968 | tf_op jit(solution)/shard_map/pallas_call | solution.py:469
  577.9 9.4 collective-permute-done.43
  587.3 5.7 collective-permute-done.37
  593.0 4.6 add_convert_fusion.2
  604.7 48.0 %shard_map.286 = bf16[4,3,704,512]{3,2,1,0:T(8,128)(2,1)} custom-call(bf16[3,512,704]{2,1,0:T(8,128)(2,1)} %get-tuple-element.172.refs_0_, bf16[3,512,704]{2,1,0:T(8,128)(2,1)} %get-tuple-element.173.refs_1_, bf16[3,512,704]{2,1,0:T(8,128)(2,1)} %get-tuple-element.156.refs_2_, bf16[3,512,704]{2,1,0:T(8,128)(2,1)} %get-tuple-element.174.refs_3_, ...), custom_call_target="tpu_custom_call" | custom-call | flops 35433480192 | bytes 67108864 | tf_op jit(solution)/shard_map/pallas_call | solution.py:516
  658.5 7.0 multiply_reduce_fusion.1
  678.2 9.0 shard_map.287.grad
  687.1 5.7 shard_map.289
  692.9 5.8 shard_map.288
  701.4 15.3 %collective-permute-done.55 = bf16[512,2048]{1,0:T(8,128)(2,1)} collective-permute-done((bf16[512,2048]{1,0:T(8,128)(2,1)}, bf16[512,2048]{1,0:T(8,128)(2,1)}, u32[]{:S(2)}, u32[]{:S(2)}) %collective-permute-start.55) | collective-permute-done | bytes 2097184 | tf_op jit(solution)/shard_map/ppermute | solution.py:628
  719.0 10.2 collective-permute-done.57
  731.7 14.0 %collective-permute-done.58 = bf16[2,8,128,128]{3,2,1,0:T(8,128)(2,1)} collective-permute-done((bf16[2,8,128,128]{3,2,1,0:T(8,128)(2,1)}, bf16[2,8,128,128]{3,2,1,0:T(8,128)(2,1)}, u32[]{:S(2)}, u32[]{:S(2)}) %collective-permute-start.58) | collective-permute-done | bytes 524320 | tf_op jit(solution)/shard_map/ppermute | solution.py:639
  752.8 8.8 collective-permute-done.59
  761.6 6.3 convolution_convert_fusion
  769.0 33.1 %shard_map.290 = (bf16[1024,1536]{1,0:T(8,128)(2,1)}, f32[2,8,1536]{2,1,0:T(8,128)}, f32[2,8,1536]{2,1,0:T(8,128)}, f32[2,8,1536]{2,1,0:T(8,128)}, f32[1024,128]{1,0:T(8,128)}) custom-call(f32[1024,1536]{1,0:T(8,128)} %shard_map.275.pre, f32[1024,1664]{1,0:T(8,128)} %shard_map.272.pre.beta, f32[1,128]{1,0:T(1,128)} %pad_bitcast_fusion.bias, ...), custom_call_target="tpu_custom_call" | custom-call | flops 4026531840 | bytes 20971520 | tf_op jit(solution)/shard_map/pallas_call | solution.py:318
  811.0 5.4 convolution_convert_fusion.3
  822.7 7.4 add_convert_fusion
  830.1 33.6 %shard_map.291 = (bf16[1024,1536]{1,0:T(8,128)(2,1)}, f32[2,8,1536]{2,1,0:T(8,128)}, f32[2,8,1536]{2,1,0:T(8,128)}, f32[2,8,1536]{2,1,0:T(8,128)}, f32[1024,128]{1,0:T(8,128)}) custom-call(f32[1024,1664]{1,0:T(8,128)} %shard_map.272.pre.beta, f32[1024,1664]{1,0:T(8,128)} %shard_map.272.pre.beta, f32[1,128]{1,0:T(1,128)} %pad_bitcast_fusion.bias, ...), custom_call_target="tpu_custom_call" | custom-call | flops 4026531840 | bytes 20971520 | tf_op jit(solution)/shard_map/pallas_call | solution.py:318
  866.4 30.1 %collective-permute-done.63 = f32[2,8,1536]{2,1,0:T(8,128)S(1)} collective-permute-done((f32[2,8,1536]{2,1,0:T(8,128)}, f32[2,8,1536]{2,1,0:T(8,128)S(1)}, u32[]{:S(2)}, u32[]{:S(2)}) %collective-permute-start.63) | collective-permute-done | bytes 98336 | tf_op jit(solution)/shard_map/ppermute | solution.py:639
  898.0 5.7 convolution_convert_fusion.1
  919.4 25.8 %collective-permute-done.65 = bf16[512,1664]{1,0:T(8,128)(2,1)} collective-permute-done((bf16[512,1664]{1,0:T(8,128)(2,1)}, bf16[512,1664]{1,0:T(8,128)(2,1)}, u32[]{:S(2)}, u32[]{:S(2)}) %collective-permute-start.65) | collective-permute-done | bytes 1703968 | tf_op jit(solution)/shard_map/ppermute | solution.py:628
  959.0 21.4 %shard_map.292 = bf16[1024,2048]{1,0:T(8,128)(2,1)} custom-call(s32[1]{0:T(128)} %bitcast.place, bf16[1024,1664]{1,0:T(8,128)(2,1)} %pad_maximum_fusion.3.refs_0_, bf16[1024,1536]{1,0:T(8,128)(2,1)} %bitcast.146, bf16[512,1664]{1,0:T(8,128)(2,1)} %pad_maximum_fusion.6.refs_0_.refs_2_, bf16[512,1664]{1,0:T(8,128)(2,1)} %copy-done.26, ...), custom_call_target="tpu_custom_call" | custom-call | flops 13421772800 | bytes 17301504 | tf_op jit(solution)/shard_map/pallas_call | solution.py:587
  997.0 6.2 fusion.28
  1003.2 5.3 collective-permute-done.81
  1018.9 4.5 fusion.5
  1030.3 4.7 all-to-all-start.1
  1054.0 9.1 collective-permute-done.71
  1070.3 17.3 %collective-permute-done.73 = f32[16640]{0:T(1024)S(1)} collective-permute-done((f32[16640]{0:T(1024)S(1)}, f32[16640]{0:T(1024)S(1)}, u32[]{:S(2)}, u32[]{:S(2)}) %collective-permute-start.73) | collective-permute-done | bytes 66592 | tf_op jit(solution)/shard_map/ppermute | solution.py:628
  (503 shorter events, 321.0 us)
Async XLA Ops:
  12.6 44.3 %all-to-all-start = ((bf16[4,2112,128]{2,1,0:T(8,128)(2,1)}), bf16[4,2112,128]{2,1,0:T(8,128)(2,1)S(1)}, u32[]{:S(2)}, u32[]{:S(2)}) async-start(bf16[4,2112,128]{2,1,0:T(8,128)(2,1)} %bitcast.155), calls=%async_computation | async-start | bytes 4325376 | tf_op jit(solution)/shard_map/all_to_all | solution.py:893
  17.8 271.4 %all-gather.3.cloned.1.call-start = ((), (), s32[]{:S(2)}) async-start(), calls=%async_computation.5 | async-start | bytes 7208960 | tf_op jit(solution)/shard_map/all_gather | solution.py:911
  23.8 30.4 %collective-permute-start.1 = (bf16[128,1664]{1,0:T(8,128)(2,1)}, bf16[128,1664]{1,0:T(8,128)(2,1)S(1)}, u32[]{:S(2)}, u32[]{:S(2)}) collective-permute-start(bf16[128,1664]{1,0:T(8,128)(2,1)} %constant_dynamic-update-slice_fusion), channel_id=1, source_target_pairs={{0,2},{1,3},{2,0},{3,1},{4,6},{5,7},{6,4},{7,5},{8,10},{9,11},{10,... | collective-permute-start | bytes 1277960 | tf_op jit(solution)/shard_map/ppermute | solution.py:633
  26.4 27.8 %collective-permute-start.2 = (bf16[128,1664]{1,0:T(8,128)(2,1)}, bf16[128,1664]{1,0:T(8,128)(2,1)S(1)}, u32[]{:S(2)}, u32[]{:S(2)}) collective-permute-start(bf16[128,1664]{1,0:T(8,128)(2,1)} %constant_dynamic-update-slice_fusion), channel_id=1, source_target_pairs={{0,3},{1,0},{2,1},{3,2},{4,7},{5,4},{6,5},{7,6},{8,11},{9,8},{10,9... | collective-permute-start | bytes 1277960 | tf_op jit(solution)/shard_map/ppermute | solution.py:633
  56.8 39.2 %collective-permute-start.3 = (bf16[512,1664]{1,0:T(8,128)(2,1)}, bf16[512,1664]{1,0:T(8,128)(2,1)S(1)}, u32[]{:S(2)}, u32[]{:S(2)}) collective-permute-start(bf16[512,1664]{1,0:T(8,128)(2,1)} %pad_maximum_fusion.6.refs_0_.refs_2_), channel_id=1, source_target_pairs={{0,8},{8,0},{16,24},{24,16},{1,9},{9,1},{17,25},{25,17},{2,10},{10... | collective-permute-start | bytes 5111816 | tf_op jit(solution)/shard_map/ppermute | solution.py:628
  58.5 39.0 %collective-permute-start.4 = (bf16[512,1664]{1,0:T(8,128)(2,1)}, bf16[512,1664]{1,0:T(8,128)(2,1)S(1)}, u32[]{:S(2)}, u32[]{:S(2)}) collective-permute-start(bf16[512,1664]{1,0:T(8,128)(2,1)} %pad_maximum_fusion.6.refs_0_.refs_2_), channel_id=1, source_target_pairs={{0,16},{8,24},{16,0},{24,8},{1,17},{9,25},{17,1},{25,9},{2,18},{10... | collective-permute-start | bytes 5111816 | tf_op jit(solution)/shard_map/ppermute | solution.py:628
  63.1 38.2 %collective-permute-start.10 = (bf16[128,1536]{1,0:T(8,128)(2,1)S(1)}, bf16[128,1536]{1,0:T(8,128)(2,1)S(1)}, u32[]{:S(2)}, u32[]{:S(2)}) collective-permute-start(bf16[128,1536]{1,0:T(8,128)(2,1)S(1)} %copy-done.56), channel_id=1, source_target_pairs={{0,3},{1,0},{2,1},{3,2},{4,7},{5,4},{6,5},{7,6},{8,11},{9,8},{10,9... | collective-permute-start | bytes 1179656 | tf_op jit(solution)/shard_map/ppermute | solution.py:633
  73.7 27.5 %collective-permute-start.8 = (bf16[128,1536]{1,0:T(8,128)(2,1)S(1)}, bf16[128,1536]{1,0:T(8,128)(2,1)S(1)}, u32[]{:S(2)}, u32[]{:S(2)}) collective-permute-start(bf16[128,1536]{1,0:T(8,128)(2,1)S(1)} %copy-done.56), channel_id=1, source_target_pairs={{0,1},{1,2},{2,3},{3,0},{4,5},{5,6},{6,7},{7,4},{8,9},{9,10},{10,1... | collective-permute-start | bytes 1179656 | tf_op jit(solution)/shard_map/ppermute | solution.py:633
  73.7 34.2 %collective-permute-start.9 = (bf16[128,1536]{1,0:T(8,128)(2,1)S(1)}, bf16[128,1536]{1,0:T(8,128)(2,1)S(1)}, u32[]{:S(2)}, u32[]{:S(2)}) collective-permute-start(bf16[128,1536]{1,0:T(8,128)(2,1)S(1)} %copy-done.56), channel_id=1, source_target_pairs={{0,2},{1,3},{2,0},{3,1},{4,6},{5,7},{6,4},{7,5},{8,10},{9,11},{10,... | collective-permute-start | bytes 1179656 | tf_op jit(solution)/shard_map/ppermute | solution.py:633
  98.5 19.8 %collective-permute-start.5 = (bf16[256,1664]{1,0:T(8,128)(2,1)}, bf16[256,1664]{1,0:T(8,128)(2,1)S(1)}, u32[]{:S(2)}, u32[]{:S(2)}) collective-permute-start(bf16[256,1664]{1,0:T(8,128)(2,1)} %slice.622), channel_id=1, source_target_pairs={{0,16},{8,24},{16,0},{24,8},{1,17},{9,25},{17,1},{25,9},{2,18},{10... | collective-permute-start | bytes 2555912 | tf_op jit(solution)/shard_map/ppermute | solution.py:628
  100.0 19.8 %collective-permute-start.6 = (bf16[256,1664]{1,0:T(8,128)(2,1)}, bf16[256,1664]{1,0:T(8,128)(2,1)}, u32[]{:S(2)}, u32[]{:S(2)}) collective-permute-start(bf16[256,1664]{1,0:T(8,128)(2,1)} %slice.623), channel_id=1, source_target_pairs={{0,8},{8,0},{16,24},{24,16},{1,9},{9,1},{17,25},{25,17},{2,10},{10... | collective-permute-start | bytes 2555912 | tf_op jit(solution)/shard_map/ppermute | solution.py:628
  121.3 261.8 %all-gather.5.cloned.1.call-start = ((), (), s32[]{:S(2)}) async-start(), calls=%async_computation.6 | async-start | bytes 3604480 | tf_op jit(solution)/shard_map/all_gather | solution.py:912
  153.5 34.2 %collective-permute-start.11 = (bf16[512,1536]{1,0:T(8,128)(2,1)S(1)}, bf16[512,1536]{1,0:T(8,128)(2,1)S(1)}, u32[]{:S(2)}, u32[]{:S(2)}) collective-permute-start(bf16[512,1536]{1,0:T(8,128)(2,1)S(1)} %copy-done.22), channel_id=1, source_target_pairs={{0,8},{8,0},{16,24},{24,16},{1,9},{9,1},{17,25},{25,17},{2,10},{10... | collective-permute-start | bytes 4718600 | tf_op jit(solution)/shard_map/ppermute | solution.py:628
  154.0 34.8 %collective-permute-start.12 = (bf16[512,1536]{1,0:T(8,128)(2,1)S(1)}, bf16[512,1536]{1,0:T(8,128)(2,1)}, u32[]{:S(2)}, u32[]{:S(2)}) collective-permute-start(bf16[512,1536]{1,0:T(8,128)(2,1)S(1)} %copy-done.22), channel_id=1, source_target_pairs={{0,16},{8,24},{16,0},{24,8},{1,17},{9,25},{17,1},{25,9},{2,18},{10... | collective-permute-start | bytes 4718600 | tf_op jit(solution)/shard_map/ppermute | solution.py:628
  209.6 87.8 %collective-permute-start.16 = (bf16[512,2048]{1,0:T(8,128)(2,1)S(1)}, bf16[512,2048]{1,0:T(8,128)(2,1)}, u32[]{:S(2)}, u32[]{:S(2)}) collective-permute-start(bf16[512,2048]{1,0:T(8,128)(2,1)S(1)} %bitcast.139), channel_id=1, source_target_pairs={{0,8},{8,0},{16,24},{24,16},{1,9},{9,1},{17,25},{25,17},{2,10},{10... | collective-permute-start | bytes 6291464 | tf_op jit(solution)/shard_map/ppermute | solution.py:628
  210.4 87.0 %collective-permute-start.17 = (bf16[512,2048]{1,0:T(8,128)(2,1)S(1)}, bf16[512,2048]{1,0:T(8,128)(2,1)}, u32[]{:S(2)}, u32[]{:S(2)}) collective-permute-start(bf16[512,2048]{1,0:T(8,128)(2,1)S(1)} %bitcast.140), channel_id=1, source_target_pairs={{0,16},{8,24},{16,0},{24,8},{1,17},{9,25},{17,1},{25,9},{2,18},{10... | collective-permute-start | bytes 6291464 | tf_op jit(solution)/shard_map/ppermute | solution.py:628
  215.8 614.3 %reduce-scatter.4.cloned.1.call-start = ((), (), s32[]{:S(2)}) async-start(), calls=%async_computation.7 | async-start | bytes 10813440 | tf_op jit(solution)/shard_map/reduce_scatter | solution.py:1009
  218.1 83.8 %collective-permute-start.24 = (bf16[128,1024]{1,0:T(8,128)(2,1)S(1)}, bf16[128,1024]{1,0:T(8,128)(2,1)}, u32[]{:S(2)}, u32[]{:S(2)}) collective-permute-start(bf16[128,1024]{1,0:T(8,128)(2,1)S(1)} %bitcast.173), channel_id=1, source_target_pairs={{0,1},{1,2},{2,3},{3,0},{4,5},{5,6},{6,7},{7,4},{8,9},{9,10},{10,1... | collective-permute-start | bytes 786440 | tf_op jit(solution)/shard_map/ppermute | solution.py:633
  228.2 73.7 %collective-permute-start.25 = (bf16[128,1024]{1,0:T(8,128)(2,1)S(1)}, bf16[128,1024]{1,0:T(8,128)(2,1)}, u32[]{:S(2)}, u32[]{:S(2)}) collective-permute-start(bf16[128,1024]{1,0:T(8,128)(2,1)S(1)} %bitcast.174), channel_id=1, source_target_pairs={{0,2},{1,3},{2,0},{3,1},{4,6},{5,7},{6,4},{7,5},{8,10},{9,11},{10,... | collective-permute-start | bytes 786440 | tf_op jit(solution)/shard_map/ppermute | solution.py:633
  233.5 18.9 %collective-permute-start.15 = (bf16[2,8,1536]{2,1,0:T(8,128)(2,1)S(1)}, bf16[2,8,1536]{2,1,0:T(8,128)(2,1)S(1)}, u32[]{:S(2)}, u32[]{:S(2)}) collective-permute-start(bf16[2,8,1536]{2,1,0:T(8,128)(2,1)S(1)} %convert_bitcast_fusion.4), channel_id=1, source_target_pairs={{0,8},{8,16},{16,24},{1,9},{9,17},{17,25},{2,10},{10,18},{18,26},{... | collective-permute-start | bytes 147464 | tf_op jit(solution)/shard_map/ppermute | solution.py:639
  252.4 49.6 %collective-permute-start.26 = (bf16[128,1024]{1,0:T(8,128)(2,1)S(1)}, bf16[128,1024]{1,0:T(8,128)(2,1)}, u32[]{:S(2)}, u32[]{:S(2)}) collective-permute-start(bf16[128,1024]{1,0:T(8,128)(2,1)S(1)} %bitcast.175), channel_id=1, source_target_pairs={{0,3},{1,0},{2,1},{3,2},{4,7},{5,4},{6,5},{7,6},{8,11},{9,8},{10,9... | collective-permute-start | bytes 786440 | tf_op jit(solution)/shard_map/ppermute | solution.py:633
  316.0 58.3 %collective-permute-start.21 = (bf16[512,2048]{1,0:T(8,128)(2,1)S(1)}, bf16[512,2048]{1,0:T(8,128)(2,1)}, u32[]{:S(2)}, u32[]{:S(2)}) collective-permute-start(bf16[512,2048]{1,0:T(8,128)(2,1)S(1)} %bitcast.141), channel_id=1, source_target_pairs={{0,4},{4,0},{1,5},{5,1},{2,6},{6,2},{3,7},{7,3},{8,12},{12,8},{9,1... | collective-permute-start | bytes 6291464 | tf_op jit(solution)/shard_map/ppermute | solution.py:628
  316.1 58.3 %collective-permute-start.22 = (bf16[512,2048]{1,0:T(8,128)(2,1)}, bf16[512,2048]{1,0:T(8,128)(2,1)}, u32[]{:S(2)}, u32[]{:S(2)}) collective-permute-start(bf16[512,2048]{1,0:T(8,128)(2,1)} %collective-permute-done.16.mine_grads.refs_18_), channel_id=1, source_target_pairs={{0,4},{4,0},{1,5},{5,1},{2,6},{6,2},{3,7},{7,3},{8,12},{12,8},{9,1... | collective-permute-start | bytes 6291464 | tf_op jit(solution)/shard_map/ppermute | solution.py:628
  316.6 57.8 %collective-permute-start.23 = (bf16[512,2048]{1,0:T(8,128)(2,1)}, bf16[512,2048]{1,0:T(8,128)(2,1)}, u32[]{:S(2)}, u32[]{:S(2)}) collective-permute-start(bf16[512,2048]{1,0:T(8,128)(2,1)} %collective-permute-done.17.mine_grads.refs_20_), channel_id=1, source_target_pairs={{0,4},{4,0},{1,5},{5,1},{2,6},{6,2},{3,7},{7,3},{8,12},{12,8},{9,1... | collective-permute-start | bytes 6291464 | tf_op jit(solution)/shard_map/ppermute | solution.py:628
  316.7 31.0 %collective-permute-start.27 = (bf16[512,1024]{1,0:T(8,128)(2,1)S(1)}, bf16[512,1024]{1,0:T(8,128)(2,1)S(1)}, u32[]{:S(2)}, u32[]{:S(2)}) collective-permute-start(bf16[512,1024]{1,0:T(8,128)(2,1)S(1)} %pad_maximum_fusion.9.refs_1_.refs_0_), channel_id=1, source_target_pairs={{0,8},{8,0},{16,24},{24,16},{1,9},{9,1},{17,25},{25,17},{2,10},{10... | collective-permute-start | bytes 3145736 | tf_op jit(solution)/shard_map/ppermute | solution.py:628
  326.0 24.4 %collective-permute-start.28 = (bf16[512,1024]{1,0:T(8,128)(2,1)S(1)}, bf16[512,1024]{1,0:T(8,128)(2,1)S(1)}, u32[]{:S(2)}, u32[]{:S(2)}) collective-permute-start(bf16[512,1024]{1,0:T(8,128)(2,1)S(1)} %pad_maximum_fusion.9.refs_1_.refs_0_), channel_id=1, source_target_pairs={{0,16},{8,24},{16,0},{24,8},{1,17},{9,25},{17,1},{25,9},{2,18},{10... | collective-permute-start | bytes 3145736 | tf_op jit(solution)/shard_map/ppermute | solution.py:628
  351.3 23.1 %collective-permute-start.29 = (bf16[256,1024]{1,0:T(8,128)(2,1)}, bf16[256,1024]{1,0:T(8,128)(2,1)}, u32[]{:S(2)}, u32[]{:S(2)}) collective-permute-start(bf16[256,1024]{1,0:T(8,128)(2,1)} %slice.668), channel_id=1, source_target_pairs={{0,16},{8,24},{16,0},{24,8},{1,17},{9,25},{17,1},{25,9},{2,18},{10... | collective-permute-start | bytes 1572872 | tf_op jit(solution)/shard_map/ppermute | solution.py:628
  396.2 48.0 %collective-permute-start.34 = (bf16[512,2048]{1,0:T(8,128)(2,1)S(1)}, bf16[512,2048]{1,0:T(8,128)(2,1)}, u32[]{:S(2)}, u32[]{:S(2)}) collective-permute-start(bf16[512,2048]{1,0:T(8,128)(2,1)S(1)} %get-tuple-element.326.mine.refs_8_), channel_id=1, source_target_pairs={{0,8},{8,0},{16,24},{24,16},{1,9},{9,1},{17,25},{25,17},{2,10},{10... | collective-permute-start | bytes 6291464 | tf_op jit(solution)/shard_map/ppermute | solution.py:628
  401.1 48.5 %collective-permute-start.38 = (bf16[512,2048]{1,0:T(8,128)(2,1)S(1)}, bf16[512,2048]{1,0:T(8,128)(2,1)}, u32[]{:S(2)}, u32[]{:S(2)}) collective-permute-start(bf16[512,2048]{1,0:T(8,128)(2,1)S(1)} %get-tuple-element.326.mine.refs_8_), channel_id=1, source_target_pairs={{0,16},{8,24},{16,0},{24,8},{1,17},{9,25},{17,1},{25,9},{2,18},{10... | collective-permute-start | bytes 6291464 | tf_op jit(solution)/shard_map/ppermute | solution.py:628
  449.6 53.3 %collective-permute-start.41 = (bf16[512,2048]{1,0:T(8,128)(2,1)}, bf16[512,2048]{1,0:T(8,128)(2,1)}, u32[]{:S(2)}, u32[]{:S(2)}) collective-permute-start(bf16[512,2048]{1,0:T(8,128)(2,1)} %collective-permute-done.38.mine.refs_12_), channel_id=1, source_target_pairs={{0,4},{4,0},{1,5},{5,1},{2,6},{6,2},{3,7},{7,3},{8,12},{12,8},{9,1... | collective-permute-start | bytes 6291464 | tf_op jit(solution)/shard_map/ppermute | solution.py:628
  453.3 79.7 %collective-permute-start.45 = (bf16[256,2048]{1,0:T(8,128)(2,1)}, bf16[256,2048]{1,0:T(8,128)(2,1)}, u32[]{:S(2)}, u32[]{:S(2)}) collective-permute-start(bf16[256,2048]{1,0:T(8,128)(2,1)} %slice.673), channel_id=1, source_target_pairs={{0,16},{8,24},{16,0},{24,8},{1,17},{9,25},{17,1},{25,9},{2,18},{10... | collective-permute-start | bytes 3145736 | tf_op jit(solution)/shard_map/ppermute | solution.py:628
  455.1 79.2 %collective-permute-start.46 = (bf16[256,2048]{1,0:T(8,128)(2,1)S(1)}, bf16[256,2048]{1,0:T(8,128)(2,1)S(1)}, u32[]{:S(2)}, u32[]{:S(2)}) collective-permute-start(bf16[256,2048]{1,0:T(8,128)(2,1)S(1)} %slice.674), channel_id=1, source_target_pairs={{0,8},{8,0},{16,24},{24,16},{1,9},{9,1},{17,25},{25,17},{2,10},{10... | collective-permute-start | bytes 3145736 | tf_op jit(solution)/shard_map/ppermute | solution.py:628
  461.1 40.5 %collective-permute-start.39 = (bf16[256,2048]{1,0:T(8,128)(2,1)}, bf16[256,2048]{1,0:T(8,128)(2,1)S(1)}, u32[]{:S(2)}, u32[]{:S(2)}) collective-permute-start(bf16[256,2048]{1,0:T(8,128)(2,1)} %slice.671), channel_id=1, source_target_pairs={{0,16},{8,24},{16,0},{24,8},{1,17},{9,25},{17,1},{25,9},{2,18},{10... | collective-permute-start | bytes 3145736 | tf_op jit(solution)/shard_map/ppermute | solution.py:628
  461.4 41.6 %collective-permute-start.40 = (bf16[256,2048]{1,0:T(8,128)(2,1)}, bf16[256,2048]{1,0:T(8,128)(2,1)}, u32[]{:S(2)}, u32[]{:S(2)}) collective-permute-start(bf16[256,2048]{1,0:T(8,128)(2,1)} %slice.672), channel_id=1, source_target_pairs={{0,8},{8,0},{16,24},{24,16},{1,9},{9,1},{17,25},{25,17},{2,10},{10... | collective-permute-start | bytes 3145736 | tf_op jit(solution)/shard_map/ppermute | solution.py:628
  539.3 48.0 %collective-permute-start.43 = (bf16[512,2048]{1,0:T(8,128)(2,1)}, bf16[512,2048]{1,0:T(8,128)(2,1)S(1)}, u32[]{:S(2)}, u32[]{:S(2)}) collective-permute-start(bf16[512,2048]{1,0:T(8,128)(2,1)} %add_convert_fusion.5), channel_id=1, source_target_pairs={{0,16},{8,24},{16,0},{24,8},{1,17},{9,25},{17,1},{25,9},{2,18},{10... | collective-permute-start | bytes 6291464 | tf_op jit(solution)/shard_map/ppermute | solution.py:628
  545.0 48.0 %collective-permute-start.37 = (bf16[512,2048]{1,0:T(8,128)(2,1)}, bf16[512,2048]{1,0:T(8,128)(2,1)}, u32[]{:S(2)}, u32[]{:S(2)}) collective-permute-start(bf16[512,2048]{1,0:T(8,128)(2,1)} %add_convert_fusion.6), channel_id=1, source_target_pairs={{0,8},{8,0},{16,24},{24,16},{1,9},{9,1},{17,25},{25,17},{2,10},{10... | collective-permute-start | bytes 6291464 | tf_op jit(solution)/shard_map/ppermute | solution.py:628
  546.4 46.6 %collective-permute-start.51 = (bf16[512,2048]{1,0:T(8,128)(2,1)}, bf16[512,2048]{1,0:T(8,128)(2,1)}, u32[]{:S(2)}, u32[]{:S(2)}) collective-permute-start(bf16[512,2048]{1,0:T(8,128)(2,1)} %get-tuple-element.171), channel_id=1, source_target_pairs={{0,4},{4,0},{1,5},{5,1},{2,6},{6,2},{3,7},{7,3},{8,12},{12,8},{9,1... | collective-permute-start | bytes 6291464 | tf_op jit(solution)/shard_map/ppermute | solution.py:628
  547.7 49.9 %collective-permute-start.50 = (bf16[512,2048]{1,0:T(8,128)(2,1)}, bf16[512,2048]{1,0:T(8,128)(2,1)}, u32[]{:S(2)}, u32[]{:S(2)}) collective-permute-start(bf16[512,2048]{1,0:T(8,128)(2,1)} %get-tuple-element.169), channel_id=1, source_target_pairs={{0,4},{4,0},{1,5},{5,1},{2,6},{6,2},{3,7},{7,3},{8,12},{12,8},{9,1... | collective-permute-start | bytes 6291464 | tf_op jit(solution)/shard_map/ppermute | solution.py:628
  603.6 49.2 %collective-permute-start.49 = (bf16[512,2048]{1,0:T(8,128)(2,1)}, bf16[512,2048]{1,0:T(8,128)(2,1)S(1)}, u32[]{:S(2)}, u32[]{:S(2)}) collective-permute-start(bf16[512,2048]{1,0:T(8,128)(2,1)} %add_convert_fusion.4), channel_id=1, source_target_pairs={{0,24},{8,16},{16,8},{24,0},{1,25},{9,17},{17,9},{25,1},{2,26},{10... | collective-permute-start | bytes 6291464 | tf_op jit(solution)/shard_map/ppermute | solution.py:628
  654.1 386.2 %reduce-scatter.8.cloned.1.call-start = ((), (), s32[]{:S(2)}) async-start(), calls=%async_computation.9 | async-start | bytes 4456448 | tf_op jit(solution)/shard_map/reduce_scatter | solution.py:1013
  668.6 48.1 %collective-permute-start.55 = (bf16[512,2048]{1,0:T(8,128)(2,1)}, bf16[512,2048]{1,0:T(8,128)(2,1)}, u32[]{:S(2)}, u32[]{:S(2)}) collective-permute-start(bf16[512,2048]{1,0:T(8,128)(2,1)} %add_convert_fusion.2), channel_id=1, source_target_pairs={{0,16},{8,24},{16,0},{24,8},{1,17},{9,25},{17,1},{25,9},{2,18},{10... | collective-permute-start | bytes 6291464 | tf_op jit(solution)/shard_map/ppermute | solution.py:628
  670.2 48.8 %collective-permute-start.54 = (bf16[512,2048]{1,0:T(8,128)(2,1)}, bf16[512,2048]{1,0:T(8,128)(2,1)}, u32[]{:S(2)}, u32[]{:S(2)}) collective-permute-start(bf16[512,2048]{1,0:T(8,128)(2,1)} %add_convert_fusion.3), channel_id=1, source_target_pairs={{0,8},{8,0},{16,24},{24,16},{1,9},{9,1},{17,25},{25,17},{2,10},{10... | collective-permute-start | bytes 6291464 | tf_op jit(solution)/shard_map/ppermute | solution.py:628
  677.9 71.0 %collective-permute-start.56 = (bf16[512,2048]{1,0:T(8,128)(2,1)}, bf16[512,2048]{1,0:T(8,128)(2,1)}, u32[]{:S(2)}, u32[]{:S(2)}) collective-permute-start(bf16[512,2048]{1,0:T(8,128)(2,1)} %get-tuple-element.185), channel_id=1, source_target_pairs={{0,4},{4,0},{1,5},{5,1},{2,6},{6,2},{3,7},{7,3},{8,12},{12,8},{9,1... | collective-permute-start | bytes 6291464 | tf_op jit(solution)/shard_map/ppermute | solution.py:628
  700.1 29.1 %collective-permute-start.57 = (bf16[2,8,128,128]{3,2,1,0:T(8,128)(2,1)S(1)}, bf16[2,8,128,128]{3,2,1,0:T(8,128)(2,1)S(1)}, u32[]{:S(2)}, u32[]{:S(2)}) collective-permute-start(bf16[2,8,128,128]{3,2,1,0:T(8,128)(2,1)S(1)} %convert_element_type.366), channel_id=1, source_target_pairs={{8,0},{16,8},{24,16},{9,1},{17,9},{25,17},{10,2},{18,10},{26,18},{... | collective-permute-start | bytes 1572872 | tf_op jit(solution)/shard_map/ppermute | solution.py:639
  761.6 49.4 %collective-permute-start.60 = (bf16[512,2048]{1,0:T(8,128)(2,1)}, bf16[512,2048]{1,0:T(8,128)(2,1)}, u32[]{:S(2)}, u32[]{:S(2)}) collective-permute-start(bf16[512,2048]{1,0:T(8,128)(2,1)} %add_convert_fusion.1), channel_id=1, source_target_pairs={{0,24},{8,16},{16,8},{24,0},{1,25},{9,17},{17,9},{25,1},{2,26},{10... | collective-permute-start | bytes 6291464 | tf_op jit(solution)/shard_map/ppermute | solution.py:628
  767.9 54.8 %collective-permute-start.53 = (bf16[512,2048]{1,0:T(8,128)(2,1)}, bf16[512,2048]{1,0:T(8,128)(2,1)}, u32[]{:S(2)}, u32[]{:S(2)}) collective-permute-start(bf16[512,2048]{1,0:T(8,128)(2,1)} %get-tuple-element.180), channel_id=1, source_target_pairs={{0,4},{4,0},{1,5},{5,1},{2,6},{6,2},{3,7},{7,3},{8,12},{12,8},{9,1... | collective-permute-start | bytes 6291464 | tf_op jit(solution)/shard_map/ppermute | solution.py:628
  806.2 290.9 %reduce-scatter.6.cloned.1.call-start = ((), (), s32[]{:S(2)}) async-start(), calls=%async_computation.8 | async-start | bytes 1966080 | tf_op jit(solution)/shard_map/reduce_scatter | solution.py:1062
  816.3 97.5 %collective-permute-start.79 = (bf16[512,1536]{1,0:T(8,128)(2,1)}, bf16[512,1536]{1,0:T(8,128)(2,1)}, u32[]{:S(2)}, u32[]{:S(2)}) collective-permute-start(bf16[512,1536]{1,0:T(8,128)(2,1)} %convolution_convert_fusion.3), channel_id=1, source_target_pairs={{0,16},{8,24},{16,0},{24,8},{1,17},{9,25},{17,1},{25,9},{2,18},{10... | collective-permute-start | bytes 4718600 | tf_op jit(solution)/shard_map/ppermute | solution.py:628
  822.6 91.3 %collective-permute-start.78 = (bf16[512,1536]{1,0:T(8,128)(2,1)}, bf16[512,1536]{1,0:T(8,128)(2,1)}, u32[]{:S(2)}, u32[]{:S(2)}) collective-permute-start(bf16[512,1536]{1,0:T(8,128)(2,1)} %convolution_convert_fusion.4), channel_id=1, source_target_pairs={{0,8},{8,0},{16,24},{24,16},{1,9},{9,1},{17,25},{25,17},{2,10},{10... | collective-permute-start | bytes 4718600 | tf_op jit(solution)/shard_map/ppermute | solution.py:628
  830.1 78.6 %collective-permute-start.62 = (bf16[2,256,2048]{2,1,0:T(8,128)(2,1)}, bf16[2,256,2048]{2,1,0:T(8,128)(2,1)}, u32[]{:S(2)}, u32[]{:S(2)}) collective-permute-start(bf16[2,256,2048]{2,1,0:T(8,128)(2,1)} %bitcast.29), channel_id=1, source_target_pairs={{0,4},{4,0},{1,5},{5,1},{2,6},{6,2},{3,7},{7,3},{8,12},{12,8},{9,1... | collective-permute-start | bytes 6291464 | tf_op jit(solution)/shard_map/ppermute | solution.py:628
  863.7 32.8 %collective-permute-start.63 = (f32[2,8,1536]{2,1,0:T(8,128)}, f32[2,8,1536]{2,1,0:T(8,128)S(1)}, u32[]{:S(2)}, u32[]{:S(2)}) collective-permute-start(f32[2,8,1536]{2,1,0:T(8,128)} %get-tuple-element.208), channel_id=1, source_target_pairs={{8,0},{16,8},{24,16},{9,1},{17,9},{25,17},{10,2},{18,10},{26,18},{... | collective-permute-start | bytes 294920 | tf_op jit(solution)/shard_map/ppermute | solution.py:639
  907.2 38.0 %collective-permute-start.65 = (bf16[512,1664]{1,0:T(8,128)(2,1)}, bf16[512,1664]{1,0:T(8,128)(2,1)}, u32[]{:S(2)}, u32[]{:S(2)}) collective-permute-start(bf16[512,1664]{1,0:T(8,128)(2,1)} %convolution_convert_fusion.1), channel_id=1, source_target_pairs={{0,16},{8,24},{16,0},{24,8},{1,17},{9,25},{17,1},{25,9},{2,18},{10... | collective-permute-start | bytes 5111816 | tf_op jit(solution)/shard_map/ppermute | solution.py:628
  907.7 38.2 %collective-permute-start.64 = (bf16[512,1664]{1,0:T(8,128)(2,1)}, bf16[512,1664]{1,0:T(8,128)(2,1)}, u32[]{:S(2)}, u32[]{:S(2)}) collective-permute-start(bf16[512,1664]{1,0:T(8,128)(2,1)} %convolution_convert_fusion.2), channel_id=1, source_target_pairs={{0,8},{8,0},{16,24},{24,16},{1,9},{9,1},{17,25},{25,17},{2,10},{10... | collective-permute-start | bytes 5111816 | tf_op jit(solution)/shard_map/ppermute | solution.py:628
  951.1 29.3 %collective-permute-start.67 = (bf16[256,1664]{1,0:T(8,128)(2,1)}, bf16[256,1664]{1,0:T(8,128)(2,1)S(1)}, u32[]{:S(2)}, u32[]{:S(2)}) collective-permute-start(bf16[256,1664]{1,0:T(8,128)(2,1)} %fusion.17), channel_id=1, source_target_pairs={{0,16},{8,24},{16,0},{24,8},{1,17},{9,25},{17,1},{25,9},{2,18},{10... | collective-permute-start | bytes 2555912 | tf_op jit(solution)/shard_map/ppermute | solution.py:628
  957.4 23.0 %collective-permute-start.66 = (bf16[256,1664]{1,0:T(8,128)(2,1)}, bf16[256,1664]{1,0:T(8,128)(2,1)}, u32[]{:S(2)}, u32[]{:S(2)}) collective-permute-start(bf16[256,1664]{1,0:T(8,128)(2,1)} %fusion.18), channel_id=1, source_target_pairs={{0,8},{8,0},{16,24},{24,16},{1,9},{9,1},{17,25},{25,17},{2,10},{10... | collective-permute-start | bytes 2555912 | tf_op jit(solution)/shard_map/ppermute | solution.py:628
  983.9 30.8 %collective-permute-start.68 = (bf16[2,256,2048]{2,1,0:T(8,128)(2,1)}, bf16[2,256,2048]{2,1,0:T(8,128)(2,1)}, u32[]{:S(2)}, u32[]{:S(2)}) collective-permute-start(bf16[2,256,2048]{2,1,0:T(8,128)(2,1)} %constant_dynamic-slice_fusion.3), channel_id=1, source_target_pairs={{0,4},{4,0},{1,5},{5,1},{2,6},{6,2},{3,7},{7,3},{8,12},{12,8},{9,1... | collective-permute-start | bytes 6291464 | tf_op jit(solution)/shard_map/ppermute | solution.py:628
  988.2 20.3 %collective-permute-start.81 = (bf16[256,1536]{1,0:T(8,128)(2,1)}, bf16[256,1536]{1,0:T(8,128)(2,1)}, u32[]{:S(2)}, u32[]{:S(2)}) collective-permute-start(bf16[256,1536]{1,0:T(8,128)(2,1)} %fusion.15), channel_id=1, source_target_pairs={{0,16},{8,24},{16,0},{24,8},{1,17},{9,25},{17,1},{25,9},{2,18},{10... | collective-permute-start | bytes 2359304 | tf_op jit(solution)/shard_map/ppermute | solution.py:628
  992.5 20.2 %collective-permute-start.80 = (bf16[256,1536]{1,0:T(8,128)(2,1)}, bf16[256,1536]{1,0:T(8,128)(2,1)S(1)}, u32[]{:S(2)}, u32[]{:S(2)}) collective-permute-start(bf16[256,1536]{1,0:T(8,128)(2,1)} %fusion.14), channel_id=1, source_target_pairs={{0,8},{8,0},{16,24},{24,16},{1,9},{9,1},{17,25},{25,17},{2,10},{10... | collective-permute-start | bytes 2359304 | tf_op jit(solution)/shard_map/ppermute | solution.py:628
  1023.4 20.9 %collective-permute-start.69 = (bf16[2,256,2048]{2,1,0:T(8,128)(2,1)}, bf16[2,256,2048]{2,1,0:T(8,128)(2,1)}, u32[]{:S(2)}, u32[]{:S(2)}) collective-permute-start(bf16[2,256,2048]{2,1,0:T(8,128)(2,1)} %bitcast.34), channel_id=1, source_target_pairs={{0,4},{4,0},{1,5},{5,1},{2,6},{6,2},{3,7},{7,3},{8,12},{12,8},{9,1... | collective-permute-start | bytes 6291464 | tf_op jit(solution)/shard_map/ppermute | solution.py:628
  1030.3 35.2 %all-to-all-start.1 = ((bf16[4,2112,128]{2,1,0:T(8,128)(2,1)}), bf16[4,2112,128]{2,1,0:T(8,128)(2,1)}, u32[]{:S(2)}, u32[]{:S(2)}) async-start(bf16[4,2112,128]{2,1,0:T(8,128)(2,1)} %bitcast.138), calls=%async_computation.4 | async-start | bytes 4325376 | tf_op jit(solution)/shard_map/all_to_all | solution.py:1074
  1040.3 58.8 %collective-permute-start.75 = (bf16[128,1664]{1,0:T(8,128)(2,1)}, bf16[128,1664]{1,0:T(8,128)(2,1)}, u32[]{:S(2)}, u32[]{:S(2)}) collective-permute-start(bf16[128,1664]{1,0:T(8,128)(2,1)} %get-tuple-element.342), channel_id=1, source_target_pairs={{0,1},{1,2},{2,3},{3,0},{4,5},{5,6},{6,7},{7,4},{8,9},{9,10},{10,1... | collective-permute-start | bytes 1277960 | tf_op jit(solution)/shard_map/ppermute | solution.py:633
  1040.3 58.9 %collective-permute-start.76 = (bf16[128,1664]{1,0:T(8,128)(2,1)}, bf16[128,1664]{1,0:T(8,128)(2,1)}, u32[]{:S(2)}, u32[]{:S(2)}) collective-permute-start(bf16[128,1664]{1,0:T(8,128)(2,1)} %get-tuple-element.341), channel_id=1, source_target_pairs={{0,2},{1,3},{2,0},{3,1},{4,6},{5,7},{6,4},{7,5},{8,10},{9,11},{10,... | collective-permute-start | bytes 1277960 | tf_op jit(solution)/shard_map/ppermute | solution.py:633
  1044.3 54.9 %collective-permute-start.77 = (bf16[128,1664]{1,0:T(8,128)(2,1)}, bf16[128,1664]{1,0:T(8,128)(2,1)}, u32[]{:S(2)}, u32[]{:S(2)}) collective-permute-start(bf16[128,1664]{1,0:T(8,128)(2,1)} %get-tuple-element.340), channel_id=1, source_target_pairs={{0,3},{1,0},{2,1},{3,2},{4,7},{5,4},{6,5},{7,6},{8,11},{9,8},{10,9... | collective-permute-start | bytes 1277960 | tf_op jit(solution)/shard_map/ppermute | solution.py:633
  1068.3 19.2 %collective-permute-start.73 = (f32[16640]{0:T(1024)S(1)}, f32[16640]{0:T(1024)S(1)}, u32[]{:S(2)}, u32[]{:S(2)}) collective-permute-start(f32[16640]{0:T(1024)S(1)} %add.327), channel_id=1, source_target_pairs={{0,1},{1,0},{2,3},{3,2},{4,5},{5,4},{6,7},{7,6},{8,9},{9,8},{10,11... | collective-permute-start | bytes 199688 | tf_op jit(solution)/shard_map/ppermute | solution.py:628
  (107 other events, 1097.3 us)
Sparse Core Ops, SparseCore 0:
  121.4 129.8 all-gather.2
  252.9 60.0 all-gather.4
  653.0 151.1 reduce-scatter.3
  806.3 102.4 reduce-scatter.7
  1024.8 53.6 reduce-scatter.5

commit v10 on v9

--- a/solution.py
+++ b/solution.py
@@ -728,6 +728,7 @@
     def __init__(self, columns, grads):
         self.columns, self.grads = columns, grads
         self.half = columns[0].shape[1] // 2
+        self.mine = outer_rows(columns[0], grads)
         beside, across = (
             jnp.concatenate([self.side(3, 1), self.side(1, 1)], axis=1),
             jnp.concatenate([self.side(3, 0), self.side(2, 0)], axis=1),
@@ -754,7 +755,7 @@
         if ties:
             beside_upper, across_lower = lax.optimization_barrier(self.last + ties)[:2]
         beside, across = self.kept
-        own = outer_rows(self.columns[0], self.grads)
+        own = self.mine
         upper = own[: self.half] + wide(beside_upper) + across[self.half :]
         lower = own[self.half :] + beside[self.half :] + wide(across_lower)
         return jnp.concatenate([upper, lower], axis=0)
@@ -844,7 +845,7 @@
     entered = low(jnp.zeros_like(own))
     for repeat in range(lax.axis_size("ctx") - 1):
         entered = from_behind(low(leaving), "ctx", forward)
-        if repeat == 0 and beside:
+        if repeat == 1 and beside:
             entered = tie(entered, *beside)
         leaving = own + jnp.einsum(rule, transfer, entered, preferred_element_type=jnp.float32)
     return wide(entered)
@@ -919,6 +920,8 @@
         ends = low(ends)
         halo = from_behind(ends[:, :part_cols].reshape(seq_count, HALO, part_cols), "ctx", 1)
         pre.append(gathered_times(tie(normed_mix, ends), ctx_place, mix_full[p]))
+        if p == parts - 1:
+            lines.append(gather_line(tie(shards[-1], pre[p])))
         square = Square(tie(lines[p + 1], halo, pre[p], *arrived))
         halo = wide(halo)
         convs = conv[:, p * part_cols : (p + 1) * part_cols]
@@ -932,11 +935,10 @@
         )
         square.forward(kept[p][2])
         if p == 0:
-            lines.append(gather_line(tie(shards[-1], kept[p][2], square.beside)))
             grad_square = Square(tie(grads_mine, kept[p][2], *square.done()))
     out_full = square.pieces()
 
-    inputs_mine = wide(rows_mine(tie(block_input, kept[0][2])).reshape(-1, width))
+    inputs_mine = wide(tie(rows_mine(block_input).reshape(-1, width), kept[0][2]))
     gate_up_full = columns_join(gate_up_parts, 4)
     finals = jnp.concatenate([some[4] for some in kept], axis=1)
     transfer = low(finals[..., LANES:])
@@ -977,7 +979,10 @@
     far_sums = low(core_sum(mine, tie(other, *near_sums)))
     acts = [side[0] for outs in ffn_out for side in outs]
     own_sums = core_sum(*(side[1] for side in ffn_out[0]))
-    result_low = [low(core_sum(*(side[2] for side in ffn_out[bit]))) for bit in (1, 2)]
+    result_low = []
+    for bit in (1, 2):
+        mine, other = (side[2] for side in ffn_out[bit])
+        result_low.append(low(core_sum(tie(mine, far_sums), other)))
     acts[0] = tie(acts[0], far_sums, own_sums, *result_low)
     far_sums = flip(far_sums, "ctx", 3)
     sums = ffn_weights(
@@ -1033,7 +1038,7 @@
         grad_mix = put(grad_mix.reshape(seq_count, local_len, -1), tail, 0, local_len - HALO, 0)
         grad_mix = grad_mix.reshape(row_count, -1)
         if scatter is not None:
-            scatter.second(before)
+            earlier_ready = scatter.second(before)
             earlier_scatter = scatter
         else:
             grad_mix = tie(grad_mix, result_far)
@@ -1046,7 +1051,10 @@
     result = result_own + wide(result_near[0]) + wide(result_near[1])
     result = result + wide(result_far)
     block_output = rows_full(low(residual + result).reshape(seq_count, -1, width))
-    ready = scatter.second(block_output)
+    ready = (block_output, scatter.mine)
+    if parts > 1:
+        ready = ready + tuple(earlier_ready) + (earlier_scatter.mine,)
+    ready = scatter.second(*ready)
     grad_mixes[0] = tie(grad_mixes[0], *ready)
     mix_back = tie(gathered_times_transposed(grad_mixes, ctx_place, mix_full), *scatter.last)
     mix_back = rows_scatter(mix_back.reshape(seq_count, local_len, width)).reshape(-1, width)
@@ -1057,10 +1065,10 @@
     conv_cols = jnp.concatenate([jnp.sum(part, axis=0)[:taps] for part in conv_parts], axis=1)
     gains = butterfly(jnp.concatenate([gain_mix_part, gain_ffn_part, gain_o_part]), ("tp",))
     sums = jnp.concatenate([gains, conv_cols.reshape(-1), jnp.sum(logits, axis=0)])
+    last_line = Line(scatter.own())
     for p in range(1, parts):
-        own = low(earlier_scatter.own(*ready))
+        own = low(earlier_scatter.own(*last_line.sent))
         mix_grads[p] = wide(lax.psum_scatter(own, "fsdp", scatter_dimension=0, tiled=True))
-    last_line = Line(scatter.own())
     sums = butterfly(tie(sums, input_grad, *last_line.sent), ("ctx", "fsdp"))
     mix_grads[0] = last_line.total(sums)
     query_grad, key_grad, value_grad = by_kind([grad[:, :part_cols] for grad in mix_grads])

time: 1130 us -> 1120 us (level)
    ppermute x60, waiting for transfers between devices: 199 us -> 187 us  [flip(): return lax.ppermute(value, axis, [(i, i ^ bit) for i in devices])]
    unnamed x214 -> x222, local copies, waits for them, and re-layouts: 34.4 us -> 40.2 us
  transfers between devices with their start and end apart: 89 -> 89, of which waited for: 40 -> 38; matrix products, arithmetic and copies ran while one was open for 20% -> 19% of each run, Pallas kernels for 35% -> 36%
where the time goes in v10:
time: 1120 us; the launch traced here: 1110 us
  Pallas kernels  393 us (35%)
  waiting for transfers between devices  316 us (28%)
  starting transfers between devices  128 us (11%)
  other arithmetic  117 us (10%)
  local copies, waits for them, and re-layouts  98.1 us (9%)
  matrix products  39.9 us (4%)
  between operations  15.6 us (1%)
    ppermute x60, waiting for transfers between devices, flip(): return lax.ppermute(value, axis, [(i, i ^ bit) for i in devices])  187 us
    pallas_call x4, Pallas kernels, ffn_both(): pl.pallas_call(ffn_kernel, grid=(count // tile,), in_specs=[wide_rows] *...  118 us
    ppermute x10, waiting for transfers between devices, from_behind(): return lax.ppermute(block, axis, route)  91.7 us
    pallas_call x2, Pallas kernels, mixer_backward(): pl.pallas_call(functools.partial(backward_kernel, taps, group, first), gr...  66.4 us
    pallas_call x2, Pallas kernels, mixer_forward(): pl.pallas_call(functools.partial(forward_kernel, taps, group, first), gri...  55 us
    ppermute x60, starting transfers between devices, flip(): return lax.ppermute(value, axis, [(i, i ^ bit) for i in devices])  55 us
    pallas_call x1, Pallas kernels, ffn_weights(): pl.pallas_call(functools.partial(ffn_weights_kernel, count, lines), grid=...  48 us
    pallas_call x5, Pallas kernels, gathered_times(): pl.pallas_call(gathered_kernel, grid_spec=pltpu.PrefetchScalarGridSpec(nu...  42.3 us
  transfers between devices with their start and end apart: 89, of which 38 were waited for; matrix products, arithmetic and copies ran while one was open for 19% of the time, Pallas kernels for 36%

profile of v10, /device:TPU:0, one launch (start us, length us, event | category | flops | bytes accessed | tf_op | source)
XLA Modules:
  0.0 1107.2 jit_solution(5479684767425826888)
XLA Ops:
  12.6 5.3 all-to-all-start
  27.8 9.3 collective-permute-done
  37.1 17.1 %collective-permute-done.1 = bf16[128,1664]{1,0:T(8,128)(2,1)S(1)} collective-permute-done((bf16[128,1664]{1,0:T(8,128)(2,1)}, bf16[128,1664]{1,0:T(8,128)(2,1)S(1)}, u32[]{:S(2)}, u32[]{:S(2)}) %collective-permute-start.1) | collective-permute-done | bytes 426016 | tf_op jit(solution)/shard_map/ppermute | solution.py:633
  63.1 10.7 collective-permute-start.10
  77.5 18.7 %collective-permute-done.3.refs_1_.refs_3_ = bf16[512,1664]{1,0:T(8,128)(2,1)S(1)} collective-permute-done((bf16[512,1664]{1,0:T(8,128)(2,1)}, bf16[512,1664]{1,0:T(8,128)(2,1)S(1)}, u32[]{:S(2)}, u32[]{:S(2)}) %collective-permute-start.3) | collective-permute-done | bytes 1703968 | tf_op jit(solution)/shard_map/ppermute | solution.py:628
  101.3 6.6 collective-permute-done.9
  112.5 5.9 collective-permute-done.5.refs_3_.refs_5_
  121.4 6.6 convert_element_type.398
  131.5 4.7 shard_map.271
  140.8 12.8 %shard_map.272.pre.beta = f32[1024,1664]{1,0:T(8,128)} custom-call(s32[1]{0:T(128)} %bitcast.1.place, bf16[1024,2048]{1,0:T(8,128)(2,1)} %fusion.1.rows, bf16[512,1664]{1,0:T(8,128)(2,1)} %pad_maximum_fusion.6.refs_0_.refs_2_, bf16[512,1664]{1,0:T(8,128)(2,1)} %copy-done.32, bf16[512,1664]{1,0:T(8,128)(2,1)} %copy-done.33, bf16[256,1664]{1,0:T(8,128)(2,1)} %copy-done.49, ...), custom_call_target="tpu_custom_call" | custom-call | flops 6979321856 | bytes 11010048 | tf_op jit(solution)/shard_map/pallas_call | solution.py:551
  155.6 27.5 %shard_map.273 = (f32[1024,512]{1,0:T(8,128)}, bf16[1024,512]{1,0:T(8,128)(2,1)}, f32[2,4,128,256]{3,2,1,0:T(8,128)}, bf16[2,4,4,128,128]{4,3,2,1,0:T(8,128)(2,1...) custom-call(f32[1024,1664]{1,0:T(8,128)} %shard_map.272.pre.beta, ...), custom_call_target="tpu_custom_call" | custom-call | flops 4026531840 | bytes 20971520 | tf_op jit(solution)/shard_map/pallas_call | solution.py:160
  183.1 4.8 collective-permute-done.11.refs_1_.refs_8_
  194.3 13.6 %collective-permute-done.13.refs_3_.refs_10_ = bf16[256,1536]{1,0:T(8,128)(2,1)S(1)} collective-permute-done((bf16[256,1536]{1,0:T(8,128)(2,1)}, bf16[256,1536]{1,0:T(8,128)(2,1)S(1)}, u32[]{:S(2)}, u32[]{:S(2)}) %collective-permute-start.13) | collective-permute-done | bytes 786464 | tf_op jit(solution)/shard_map/ppermute | solution.py:628
  218.2 4.4 shard_map.274
  226.5 11.5 %shard_map.275.pre = f32[1024,1536]{1,0:T(8,128)} custom-call(s32[1]{0:T(128)} %bitcast.1.place, bf16[1024,2048]{1,0:T(8,128)(2,1)} %fusion.1.rows, bf16[512,1536]{1,0:T(8,128)(2,1)} %pad_maximum_fusion.7.refs_0_.refs_7_, bf16[512,1536]{1,0:T(8,128)(2,1)} %copy-done.34, bf16[512,1536]{1,0:T(8,128)(2,1)} %collective-permute-done.12.refs_2_.refs_9_, ...), custom_call_target="tpu_custom_call" | custom-call | flops 6442450944 | bytes 10485760 | tf_op jit(solution)/shard_map/pallas_call | solution.py:551
  238.0 10.2 collective-permute-start.24
  252.4 5.2 collective-permute-start.26
  258.3 27.5 %shard_map.276 = (f32[1024,512]{1,0:T(8,128)}, bf16[1024,512]{1,0:T(8,128)(2,1)}, f32[2,4,128,256]{3,2,1,0:T(8,128)}, bf16[2,4,4,128,128]{4,3,2,1,0:T(8,128)(2,1...) custom-call(f32[1024,1536]{1,0:T(8,128)} %shard_map.275.pre, ...), custom_call_target="tpu_custom_call" | custom-call | flops 4026531840 | bytes 20971520 | tf_op jit(solution)/shard_map/pallas_call | solution.py:160
  289.5 8.1 shard_map.277.gate_w.up_w
  297.7 4.6 collective-permute-start.18
  303.7 6.1 collective-permute-done.18
  310.1 4.4 collective-permute-start.19
  317.7 6.7 collective-permute-done.19
  324.4 6.8 collective-permute-start.28
  331.5 15.2 %collective-permute-done.27.refs_2_.refs_1_ = bf16[512,1024]{1,0:T(8,128)(2,1)S(1)} collective-permute-done((bf16[512,1024]{1,0:T(8,128)(2,1)S(1)}, bf16[512,1024]{1,0:T(8,128)(2,1)S(1)}, u32[]{:S(2)}, u32[]{:S(2)}) %collective-permute-start.27) | collective-permute-done | bytes 1048608 | tf_op jit(solution)/shard_map/ppermute | solution.py:628
  348.9 6.3 collective-permute-done.28.refs_3_.refs_2_
  361.0 4.5 shard_map.278
  365.5 4.6 shard_map.279
  373.0 8.7 shard_map.280
  393.4 4.4 shard_map.281.down_w
  402.0 29.5 %shard_map.282 = (bf16[3,512,704]{2,1,0:T(8,128)(2,1)}, bf16[512,2048]{1,0:T(8,128)(2,1)}, bf16[512,2048]{1,0:T(8,128)(2,1)}, bf16[3,512,704]{2,1,0:T(8,128)(2,1...) custom-call(bf16[512,2048]{1,0:T(8,128)(2,1)} %copy-done.39, ...), custom_call_target="tpu_custom_call" | custom-call | flops 17716740096 | bytes 25427968 | tf_op jit(solution)/shard_map/pallas_call | solution.py:469
  431.5 8.7 collective-permute-done.34.mine.refs_10_
  440.3 7.8 collective-permute-done.38.mine.refs_12_
  460.5 29.5 %shard_map.283 = (bf16[3,512,704]{2,1,0:T(8,128)(2,1)}, bf16[512,2048]{1,0:T(8,128)(2,1)}, bf16[512,2048]{1,0:T(8,128)(2,1)}, bf16[3,512,704]{2,1,0:T(8,128)(2,1...) custom-call(bf16[512,2048]{1,0:T(8,128)(2,1)} %collective-permute-done.34.mine.refs_10_, ...), custom_call_target="tpu_custom_call" | custom-call | flops 17716740096 | bytes 25427968 | tf_op jit(solution)/shard_map/pallas_call | solution.py:469
  490.0 10.1 collective-permute-done.39
  501.4 29.7 %shard_map.284 = (bf16[3,512,704]{2,1,0:T(8,128)(2,1)}, bf16[512,2048]{1,0:T(8,128)(2,1)}, bf16[512,2048]{1,0:T(8,128)(2,1)}, bf16[3,512,704]{2,1,0:T(8,128)(2,1...) custom-call(bf16[512,2048]{1,0:T(8,128)(2,1)} %collective-permute-done.38.mine.refs_12_, ...), custom_call_target="tpu_custom_call" | custom-call | flops 17716740096 | bytes 25427968 | tf_op jit(solution)/shard_map/pallas_call | solution.py:469
  546.3 29.5 %shard_map.285 = (bf16[3,512,704]{2,1,0:T(8,128)(2,1)}, bf16[512,2048]{1,0:T(8,128)(2,1)}, bf16[512,2048]{1,0:T(8,128)(2,1)}, bf16[3,512,704]{2,1,0:T(8,128)(2,1...) custom-call(bf16[512,2048]{1,0:T(8,128)(2,1)} %copy-done.55, ...), custom_call_target="tpu_custom_call" | custom-call | flops 17716740096 | bytes 25427968 | tf_op jit(solution)/shard_map/pallas_call | solution.py:469
  575.8 10.2 collective-permute-done.43
  586.0 5.6 collective-permute-done.37
  605.3 48.0 %shard_map.286 = bf16[4,3,704,512]{3,2,1,0:T(8,128)(2,1)} custom-call(bf16[3,512,704]{2,1,0:T(8,128)(2,1)} %get-tuple-element.176.refs_0_, bf16[3,512,704]{2,1,0:T(8,128)(2,1)} %get-tuple-element.177.refs_1_, bf16[3,512,704]{2,1,0:T(8,128)(2,1)} %get-tuple-element.158.refs_2_, bf16[3,512,704]{2,1,0:T(8,128)(2,1)} %get-tuple-element.178.refs_3_, ...), custom_call_target="tpu_custom_call" | custom-call | flops 35433480192 | bytes 67108864 | tf_op jit(solution)/shard_map/pallas_call | solution.py:516
  659.1 7.0 multiply_reduce_fusion.1
  678.7 9.0 shard_map.287.grad
  687.6 5.7 shard_map.289
  693.4 5.8 shard_map.288
  701.9 27.9 %collective-permute-done.57 = bf16[2,8,128,128]{3,2,1,0:T(8,128)(2,1)S(1)} collective-permute-done((bf16[2,8,128,128]{3,2,1,0:T(8,128)(2,1)S(1)}, bf16[2,8,128,128]{3,2,1,0:T(8,128)(2,1)S(1)}, u32[]{:S(2)}, u32[]{:S(2)}) %collective-permute-start.57) | collective-permute-done | bytes 524320 | tf_op jit(solution)/shard_map/ppermute | solution.py:639
  732.3 14.0 %collective-permute-done.58 = bf16[2,8,128,128]{3,2,1,0:T(8,128)(2,1)} collective-permute-done((bf16[2,8,128,128]{3,2,1,0:T(8,128)(2,1)}, bf16[2,8,128,128]{3,2,1,0:T(8,128)(2,1)}, u32[]{:S(2)}, u32[]{:S(2)}) %collective-permute-start.58) | collective-permute-done | bytes 524320 | tf_op jit(solution)/shard_map/ppermute | solution.py:639
  753.7 8.5 collective-permute-done.59
  762.2 6.3 convolution_convert_fusion
  769.5 33.1 %shard_map.290 = (bf16[1024,1536]{1,0:T(8,128)(2,1)}, f32[2,8,1536]{2,1,0:T(8,128)}, f32[2,8,1536]{2,1,0:T(8,128)}, f32[2,8,1536]{2,1,0:T(8,128)}, f32[1024,128]{1,0:T(8,128)}) custom-call(f32[1024,1536]{1,0:T(8,128)} %shard_map.275.pre, f32[1024,1664]{1,0:T(8,128)} %shard_map.272.pre.beta, f32[1,128]{1,0:T(1,128)} %pad_bitcast_fusion.bias, ...), custom_call_target="tpu_custom_call" | custom-call | flops 4026531840 | bytes 20971520 | tf_op jit(solution)/shard_map/pallas_call | solution.py:318
  806.1 4.4 collective-permute-done.61
  816.6 7.4 add_convert_fusion
  827.3 5.7 fusion.24
  833.0 4.6 broadcast_select_fusion.3
  837.6 33.3 %shard_map.291 = (bf16[1024,1536]{1,0:T(8,128)(2,1)}, f32[2,8,1536]{2,1,0:T(8,128)}, f32[2,8,1536]{2,1,0:T(8,128)}, f32[2,8,1536]{2,1,0:T(8,128)}, f32[1024,128]{1,0:T(8,128)}) custom-call(f32[1024,1664]{1,0:T(8,128)} %shard_map.272.pre.beta, f32[1024,1664]{1,0:T(8,128)} %shard_map.272.pre.beta, f32[1,128]{1,0:T(1,128)} %pad_bitcast_fusion.bias, ...), custom_call_target="tpu_custom_call" | custom-call | flops 4026531840 | bytes 20971520 | tf_op jit(solution)/shard_map/pallas_call | solution.py:318
  873.7 19.8 %collective-permute-done.63 = f32[2,8,1536]{2,1,0:T(8,128)S(1)} collective-permute-done((f32[2,8,1536]{2,1,0:T(8,128)}, f32[2,8,1536]{2,1,0:T(8,128)S(1)}, u32[]{:S(2)}, u32[]{:S(2)}) %collective-permute-start.63) | collective-permute-done | bytes 98336 | tf_op jit(solution)/shard_map/ppermute | solution.py:639
  895.0 4.5 convolution_convert_fusion.1
  921.4 27.6 %collective-permute-done.65 = bf16[512,1664]{1,0:T(8,128)(2,1)S(1)} collective-permute-done((bf16[512,1664]{1,0:T(8,128)(2,1)S(1)}, bf16[512,1664]{1,0:T(8,128)(2,1)S(1)}, u32[]{:S(2)}, u32[]{:S(2)}) %collective-permute-start.65) | collective-permute-done | bytes 1703968 | tf_op jit(solution)/shard_map/ppermute | solution.py:628
  956.5 21.6 %shard_map.292 = bf16[1024,2048]{1,0:T(8,128)(2,1)} custom-call(s32[1]{0:T(128)} %bitcast.1.place, bf16[1024,1664]{1,0:T(8,128)(2,1)} %pad_maximum_fusion.3.refs_0_, bf16[1024,1536]{1,0:T(8,128)(2,1)} %bitcast.132, bf16[512,1664]{1,0:T(8,128)(2,1)} %pad_maximum_fusion.6.refs_0_.refs_2_, bf16[512,1664]{1,0:T(8,128)(2,1)} %copy-done.32, ...), custom_call_target="tpu_custom_call" | custom-call | flops 13421772800 | bytes 17301504 | tf_op jit(solution)/shard_map/pallas_call | solution.py:587
  983.5 4.8 reshape.209
  991.5 4.5 all-to-all-start.1
  1005.3 4.3 fusion.9
  1010.9 5.7 collective-permute-start.78
  1039.8 23.2 %collective-permute-done.75 = f32[16640]{0:T(1024)S(1)} collective-permute-done((f32[16640]{0:T(1024)S(1)}, f32[16640]{0:T(1024)S(1)}, u32[]{:S(2)}, u32[]{:S(2)}) %collective-permute-start.75) | collective-permute-done | bytes 66592 | tf_op jit(solution)/shard_map/ppermute | solution.py:628
  1075.5 6.9 collective-permute-done.76
  (512 shorter events, 304.7 us)
Async XLA Ops:
  12.6 44.3 %all-to-all-start = ((bf16[4,2112,128]{2,1,0:T(8,128)(2,1)}), bf16[4,2112,128]{2,1,0:T(8,128)(2,1)S(1)}, u32[]{:S(2)}, u32[]{:S(2)}) async-start(bf16[4,2112,128]{2,1,0:T(8,128)(2,1)} %bitcast.139), calls=%async_computation | async-start | bytes 4325376 | tf_op jit(solution)/shard_map/all_to_all | solution.py:894
  17.8 271.6 %all-gather.3.cloned.1.call-start = ((), (), s32[]{:S(2)}) async-start(), calls=%async_computation.5 | async-start | bytes 7208960 | tf_op jit(solution)/shard_map/all_gather | solution.py:912
  23.8 30.4 %collective-permute-start.1 = (bf16[128,1664]{1,0:T(8,128)(2,1)}, bf16[128,1664]{1,0:T(8,128)(2,1)S(1)}, u32[]{:S(2)}, u32[]{:S(2)}) collective-permute-start(bf16[128,1664]{1,0:T(8,128)(2,1)} %constant_dynamic-update-slice_fusion), channel_id=1, source_target_pairs={{0,2},{1,3},{2,0},{3,1},{4,6},{5,7},{6,4},{7,5},{8,10},{9,11},{10,... | collective-permute-start | bytes 1277960 | tf_op jit(solution)/shard_map/ppermute | solution.py:633
  26.4 27.8 %collective-permute-start.2 = (bf16[128,1664]{1,0:T(8,128)(2,1)}, bf16[128,1664]{1,0:T(8,128)(2,1)S(1)}, u32[]{:S(2)}, u32[]{:S(2)}) collective-permute-start(bf16[128,1664]{1,0:T(8,128)(2,1)} %constant_dynamic-update-slice_fusion), channel_id=1, source_target_pairs={{0,3},{1,0},{2,1},{3,2},{4,7},{5,4},{6,5},{7,6},{8,11},{9,8},{10,9... | collective-permute-start | bytes 1277960 | tf_op jit(solution)/shard_map/ppermute | solution.py:633
  56.9 39.2 %collective-permute-start.3 = (bf16[512,1664]{1,0:T(8,128)(2,1)}, bf16[512,1664]{1,0:T(8,128)(2,1)S(1)}, u32[]{:S(2)}, u32[]{:S(2)}) collective-permute-start(bf16[512,1664]{1,0:T(8,128)(2,1)} %pad_maximum_fusion.6.refs_0_.refs_2_), channel_id=1, source_target_pairs={{0,8},{8,0},{16,24},{24,16},{1,9},{9,1},{17,25},{25,17},{2,10},{10... | collective-permute-start | bytes 5111816 | tf_op jit(solution)/shard_map/ppermute | solution.py:628
  58.5 39.0 %collective-permute-start.4 = (bf16[512,1664]{1,0:T(8,128)(2,1)}, bf16[512,1664]{1,0:T(8,128)(2,1)S(1)}, u32[]{:S(2)}, u32[]{:S(2)}) collective-permute-start(bf16[512,1664]{1,0:T(8,128)(2,1)} %pad_maximum_fusion.6.refs_0_.refs_2_), channel_id=1, source_target_pairs={{0,16},{8,24},{16,0},{24,8},{1,17},{9,25},{17,1},{25,9},{2,18},{10... | collective-permute-start | bytes 5111816 | tf_op jit(solution)/shard_map/ppermute | solution.py:628
  63.1 38.2 %collective-permute-start.10 = (bf16[128,1536]{1,0:T(8,128)(2,1)S(1)}, bf16[128,1536]{1,0:T(8,128)(2,1)S(1)}, u32[]{:S(2)}, u32[]{:S(2)}) collective-permute-start(bf16[128,1536]{1,0:T(8,128)(2,1)S(1)} %copy-done.61), channel_id=1, source_target_pairs={{0,3},{1,0},{2,1},{3,2},{4,7},{5,4},{6,5},{7,6},{8,11},{9,8},{10,9... | collective-permute-start | bytes 1179656 | tf_op jit(solution)/shard_map/ppermute | solution.py:633
  73.8 27.5 %collective-permute-start.8 = (bf16[128,1536]{1,0:T(8,128)(2,1)S(1)}, bf16[128,1536]{1,0:T(8,128)(2,1)S(1)}, u32[]{:S(2)}, u32[]{:S(2)}) collective-permute-start(bf16[128,1536]{1,0:T(8,128)(2,1)S(1)} %copy-done.61), channel_id=1, source_target_pairs={{0,1},{1,2},{2,3},{3,0},{4,5},{5,6},{6,7},{7,4},{8,9},{9,10},{10,1... | collective-permute-start | bytes 1179656 | tf_op jit(solution)/shard_map/ppermute | solution.py:633
  73.8 34.2 %collective-permute-start.9 = (bf16[128,1536]{1,0:T(8,128)(2,1)S(1)}, bf16[128,1536]{1,0:T(8,128)(2,1)S(1)}, u32[]{:S(2)}, u32[]{:S(2)}) collective-permute-start(bf16[128,1536]{1,0:T(8,128)(2,1)S(1)} %copy-done.61), channel_id=1, source_target_pairs={{0,2},{1,3},{2,0},{3,1},{4,6},{5,7},{6,4},{7,5},{8,10},{9,11},{10,... | collective-permute-start | bytes 1179656 | tf_op jit(solution)/shard_map/ppermute | solution.py:633
  98.5 19.8 %collective-permute-start.5 = (bf16[256,1664]{1,0:T(8,128)(2,1)}, bf16[256,1664]{1,0:T(8,128)(2,1)S(1)}, u32[]{:S(2)}, u32[]{:S(2)}) collective-permute-start(bf16[256,1664]{1,0:T(8,128)(2,1)} %slice.622), channel_id=1, source_target_pairs={{0,16},{8,24},{16,0},{24,8},{1,17},{9,25},{17,1},{25,9},{2,18},{10... | collective-permute-start | bytes 2555912 | tf_op jit(solution)/shard_map/ppermute | solution.py:628
  100.0 19.8 %collective-permute-start.6 = (bf16[256,1664]{1,0:T(8,128)(2,1)}, bf16[256,1664]{1,0:T(8,128)(2,1)}, u32[]{:S(2)}, u32[]{:S(2)}) collective-permute-start(bf16[256,1664]{1,0:T(8,128)(2,1)} %slice.623), channel_id=1, source_target_pairs={{0,8},{8,0},{16,24},{24,16},{1,9},{9,1},{17,25},{25,17},{2,10},{10... | collective-permute-start | bytes 2555912 | tf_op jit(solution)/shard_map/ppermute | solution.py:628
  121.4 260.3 %all-gather.5.cloned.1.call-start = ((), (), s32[]{:S(2)}) async-start(), calls=%async_computation.6 | async-start | bytes 3604480 | tf_op jit(solution)/shard_map/all_gather | solution.py:913
  153.7 34.2 %collective-permute-start.11 = (bf16[512,1536]{1,0:T(8,128)(2,1)S(1)}, bf16[512,1536]{1,0:T(8,128)(2,1)S(1)}, u32[]{:S(2)}, u32[]{:S(2)}) collective-permute-start(bf16[512,1536]{1,0:T(8,128)(2,1)S(1)} %copy-done.27), channel_id=1, source_target_pairs={{0,8},{8,0},{16,24},{24,16},{1,9},{9,1},{17,25},{25,17},{2,10},{10... | collective-permute-start | bytes 4718600 | tf_op jit(solution)/shard_map/ppermute | solution.py:628
  154.1 34.8 %collective-permute-start.12 = (bf16[512,1536]{1,0:T(8,128)(2,1)S(1)}, bf16[512,1536]{1,0:T(8,128)(2,1)}, u32[]{:S(2)}, u32[]{:S(2)}) collective-permute-start(bf16[512,1536]{1,0:T(8,128)(2,1)S(1)} %copy-done.27), channel_id=1, source_target_pairs={{0,16},{8,24},{16,0},{24,8},{1,17},{9,25},{17,1},{25,9},{2,18},{10... | collective-permute-start | bytes 4718600 | tf_op jit(solution)/shard_map/ppermute | solution.py:628
  191.0 16.9 %collective-permute-start.13 = (bf16[256,1536]{1,0:T(8,128)(2,1)}, bf16[256,1536]{1,0:T(8,128)(2,1)S(1)}, u32[]{:S(2)}, u32[]{:S(2)}) collective-permute-start(bf16[256,1536]{1,0:T(8,128)(2,1)} %slice.649), channel_id=1, source_target_pairs={{0,16},{8,24},{16,0},{24,8},{1,17},{9,25},{17,1},{25,9},{2,18},{10... | collective-permute-start | bytes 2359304 | tf_op jit(solution)/shard_map/ppermute | solution.py:628
  191.7 17.9 %collective-permute-start.14 = (bf16[256,1536]{1,0:T(8,128)(2,1)}, bf16[256,1536]{1,0:T(8,128)(2,1)}, u32[]{:S(2)}, u32[]{:S(2)}) collective-permute-start(bf16[256,1536]{1,0:T(8,128)(2,1)} %slice.650), channel_id=1, source_target_pairs={{0,8},{8,0},{16,24},{24,16},{1,9},{9,1},{17,25},{25,17},{2,10},{10... | collective-permute-start | bytes 2359304 | tf_op jit(solution)/shard_map/ppermute | solution.py:628
  209.6 87.9 %collective-permute-start.16 = (bf16[512,2048]{1,0:T(8,128)(2,1)S(1)}, bf16[512,2048]{1,0:T(8,128)(2,1)}, u32[]{:S(2)}, u32[]{:S(2)}) collective-permute-start(bf16[512,2048]{1,0:T(8,128)(2,1)S(1)} %bitcast.123), channel_id=1, source_target_pairs={{0,8},{8,0},{16,24},{24,16},{1,9},{9,1},{17,25},{25,17},{2,10},{10... | collective-permute-start | bytes 6291464 | tf_op jit(solution)/shard_map/ppermute | solution.py:628
  210.4 87.2 %collective-permute-start.17 = (bf16[512,2048]{1,0:T(8,128)(2,1)S(1)}, bf16[512,2048]{1,0:T(8,128)(2,1)}, u32[]{:S(2)}, u32[]{:S(2)}) collective-permute-start(bf16[512,2048]{1,0:T(8,128)(2,1)S(1)} %bitcast.124), channel_id=1, source_target_pairs={{0,16},{8,24},{16,0},{24,8},{1,17},{9,25},{17,1},{25,9},{2,18},{10... | collective-permute-start | bytes 6291464 | tf_op jit(solution)/shard_map/ppermute | solution.py:628
  215.8 621.8 %reduce-scatter.4.cloned.1.call-start = ((), (), s32[]{:S(2)}) async-start(), calls=%async_computation.7 | async-start | bytes 10813440 | tf_op jit(solution)/shard_map/reduce_scatter | solution.py:1014
  223.4 29.0 %collective-permute-start.15 = (bf16[2,8,1536]{2,1,0:T(8,128)(2,1)S(1)}, bf16[2,8,1536]{2,1,0:T(8,128)(2,1)S(1)}, u32[]{:S(2)}, u32[]{:S(2)}) collective-permute-start(bf16[2,8,1536]{2,1,0:T(8,128)(2,1)S(1)} %convert_bitcast_fusion.4), channel_id=1, source_target_pairs={{0,8},{8,16},{16,24},{1,9},{9,17},{17,25},{2,10},{10,18},{18,26},{... | collective-permute-start | bytes 147464 | tf_op jit(solution)/shard_map/ppermute | solution.py:639
  238.0 64.4 %collective-permute-start.24 = (bf16[128,1024]{1,0:T(8,128)(2,1)S(1)}, bf16[128,1024]{1,0:T(8,128)(2,1)}, u32[]{:S(2)}, u32[]{:S(2)}) collective-permute-start(bf16[128,1024]{1,0:T(8,128)(2,1)S(1)} %bitcast.158), channel_id=1, source_target_pairs={{0,1},{1,2},{2,3},{3,0},{4,5},{5,6},{6,7},{7,4},{8,9},{9,10},{10,1... | collective-permute-start | bytes 786440 | tf_op jit(solution)/shard_map/ppermute | solution.py:633
  248.2 54.2 %collective-permute-start.25 = (bf16[128,1024]{1,0:T(8,128)(2,1)S(1)}, bf16[128,1024]{1,0:T(8,128)(2,1)}, u32[]{:S(2)}, u32[]{:S(2)}) collective-permute-start(bf16[128,1024]{1,0:T(8,128)(2,1)S(1)} %bitcast.159), channel_id=1, source_target_pairs={{0,2},{1,3},{2,0},{3,1},{4,6},{5,7},{6,4},{7,5},{8,10},{9,11},{10,... | collective-permute-start | bytes 786440 | tf_op jit(solution)/shard_map/ppermute | solution.py:633
  252.4 50.0 %collective-permute-start.26 = (bf16[128,1024]{1,0:T(8,128)(2,1)S(1)}, bf16[128,1024]{1,0:T(8,128)(2,1)}, u32[]{:S(2)}, u32[]{:S(2)}) collective-permute-start(bf16[128,1024]{1,0:T(8,128)(2,1)S(1)} %bitcast.160), channel_id=1, source_target_pairs={{0,3},{1,0},{2,1},{3,2},{4,7},{5,4},{6,5},{7,6},{8,11},{9,8},{10,9... | collective-permute-start | bytes 786440 | tf_op jit(solution)/shard_map/ppermute | solution.py:633
  302.3 70.6 %collective-permute-start.21 = (bf16[512,2048]{1,0:T(8,128)(2,1)S(1)}, bf16[512,2048]{1,0:T(8,128)(2,1)}, u32[]{:S(2)}, u32[]{:S(2)}) collective-permute-start(bf16[512,2048]{1,0:T(8,128)(2,1)S(1)} %bitcast.125), channel_id=1, source_target_pairs={{0,4},{4,0},{1,5},{5,1},{2,6},{6,2},{3,7},{7,3},{8,12},{12,8},{9,1... | collective-permute-start | bytes 6291464 | tf_op jit(solution)/shard_map/ppermute | solution.py:628
  314.6 58.4 %collective-permute-start.22 = (bf16[512,2048]{1,0:T(8,128)(2,1)}, bf16[512,2048]{1,0:T(8,128)(2,1)}, u32[]{:S(2)}, u32[]{:S(2)}) collective-permute-start(bf16[512,2048]{1,0:T(8,128)(2,1)} %collective-permute-done.16.mine_grads.refs_18_), channel_id=1, source_target_pairs={{0,4},{4,0},{1,5},{5,1},{2,6},{6,2},{3,7},{7,3},{8,12},{12,8},{9,1... | collective-permute-start | bytes 6291464 | tf_op jit(solution)/shard_map/ppermute | solution.py:628
  314.7 58.3 %collective-permute-start.23 = (bf16[512,2048]{1,0:T(8,128)(2,1)}, bf16[512,2048]{1,0:T(8,128)(2,1)}, u32[]{:S(2)}, u32[]{:S(2)}) collective-permute-start(bf16[512,2048]{1,0:T(8,128)(2,1)} %collective-permute-done.17.mine_grads.refs_20_), channel_id=1, source_target_pairs={{0,4},{4,0},{1,5},{5,1},{2,6},{6,2},{3,7},{7,3},{8,12},{12,8},{9,1... | collective-permute-start | bytes 6291464 | tf_op jit(solution)/shard_map/ppermute | solution.py:628
  315.2 31.5 %collective-permute-start.27 = (bf16[512,1024]{1,0:T(8,128)(2,1)S(1)}, bf16[512,1024]{1,0:T(8,128)(2,1)S(1)}, u32[]{:S(2)}, u32[]{:S(2)}) collective-permute-start(bf16[512,1024]{1,0:T(8,128)(2,1)S(1)} %pad_maximum_fusion.9.refs_1_.refs_0_), channel_id=1, source_target_pairs={{0,8},{8,0},{16,24},{24,16},{1,9},{9,1},{17,25},{25,17},{2,10},{10... | collective-permute-start | bytes 3145736 | tf_op jit(solution)/shard_map/ppermute | solution.py:628
  324.4 30.8 %collective-permute-start.28 = (bf16[512,1024]{1,0:T(8,128)(2,1)S(1)}, bf16[512,1024]{1,0:T(8,128)(2,1)S(1)}, u32[]{:S(2)}, u32[]{:S(2)}) collective-permute-start(bf16[512,1024]{1,0:T(8,128)(2,1)S(1)} %pad_maximum_fusion.9.refs_1_.refs_0_), channel_id=1, source_target_pairs={{0,16},{8,24},{16,0},{24,8},{1,17},{9,25},{17,1},{25,9},{2,18},{10... | collective-permute-start | bytes 3145736 | tf_op jit(solution)/shard_map/ppermute | solution.py:628
  356.1 16.9 %collective-permute-start.29 = (bf16[256,1024]{1,0:T(8,128)(2,1)}, bf16[256,1024]{1,0:T(8,128)(2,1)}, u32[]{:S(2)}, u32[]{:S(2)}) collective-permute-start(bf16[256,1024]{1,0:T(8,128)(2,1)} %slice.668), channel_id=1, source_target_pairs={{0,16},{8,24},{16,0},{24,8},{1,17},{9,25},{17,1},{25,9},{2,18},{10... | collective-permute-start | bytes 1572872 | tf_op jit(solution)/shard_map/ppermute | solution.py:628
  392.2 48.0 %collective-permute-start.34 = (bf16[512,2048]{1,0:T(8,128)(2,1)S(1)}, bf16[512,2048]{1,0:T(8,128)(2,1)}, u32[]{:S(2)}, u32[]{:S(2)}) collective-permute-start(bf16[512,2048]{1,0:T(8,128)(2,1)S(1)} %multiply_convert_fusion.mine.refs_8_), channel_id=1, source_target_pairs={{0,8},{8,0},{16,24},{24,16},{1,9},{9,1},{17,25},{25,17},{2,10},{10... | collective-permute-start | bytes 6291464 | tf_op jit(solution)/shard_map/ppermute | solution.py:628
  397.8 50.2 %collective-permute-start.38 = (bf16[512,2048]{1,0:T(8,128)(2,1)S(1)}, bf16[512,2048]{1,0:T(8,128)(2,1)}, u32[]{:S(2)}, u32[]{:S(2)}) collective-permute-start(bf16[512,2048]{1,0:T(8,128)(2,1)S(1)} %multiply_convert_fusion.mine.refs_8_), channel_id=1, source_target_pairs={{0,16},{8,24},{16,0},{24,8},{1,17},{9,25},{17,1},{25,9},{2,18},{10... | collective-permute-start | bytes 6291464 | tf_op jit(solution)/shard_map/ppermute | solution.py:628
  440.2 19.6 %collective-permute-start.35 = (bf16[512,2048]{1,0:T(8,128)(2,1)}, bf16[512,2048]{1,0:T(8,128)(2,1)}, u32[]{:S(2)}, u32[]{:S(2)}) collective-permute-start(bf16[512,2048]{1,0:T(8,128)(2,1)} %collective-permute-done.34.mine.refs_10_), channel_id=1, source_target_pairs={{0,4},{4,0},{1,5},{5,1},{2,6},{6,2},{3,7},{7,3},{8,12},{12,8},{9,1... | collective-permute-start | bytes 6291464 | tf_op jit(solution)/shard_map/ppermute | solution.py:628
  448.1 53.3 %collective-permute-start.41 = (bf16[512,2048]{1,0:T(8,128)(2,1)}, bf16[512,2048]{1,0:T(8,128)(2,1)}, u32[]{:S(2)}, u32[]{:S(2)}) collective-permute-start(bf16[512,2048]{1,0:T(8,128)(2,1)} %collective-permute-done.38.mine.refs_12_), channel_id=1, source_target_pairs={{0,4},{4,0},{1,5},{5,1},{2,6},{6,2},{3,7},{7,3},{8,12},{12,8},{9,1... | collective-permute-start | bytes 6291464 | tf_op jit(solution)/shard_map/ppermute | solution.py:628
  451.7 79.9 %collective-permute-start.45 = (bf16[256,2048]{1,0:T(8,128)(2,1)}, bf16[256,2048]{1,0:T(8,128)(2,1)}, u32[]{:S(2)}, u32[]{:S(2)}) collective-permute-start(bf16[256,2048]{1,0:T(8,128)(2,1)} %slice.673), channel_id=1, source_target_pairs={{0,16},{8,24},{16,0},{24,8},{1,17},{9,25},{17,1},{25,9},{2,18},{10... | collective-permute-start | bytes 3145736 | tf_op jit(solution)/shard_map/ppermute | solution.py:628
  453.5 79.4 %collective-permute-start.46 = (bf16[256,2048]{1,0:T(8,128)(2,1)S(1)}, bf16[256,2048]{1,0:T(8,128)(2,1)S(1)}, u32[]{:S(2)}, u32[]{:S(2)}) collective-permute-start(bf16[256,2048]{1,0:T(8,128)(2,1)S(1)} %slice.674), channel_id=1, source_target_pairs={{0,8},{8,0},{16,24},{24,16},{1,9},{9,1},{17,25},{25,17},{2,10},{10... | collective-permute-start | bytes 3145736 | tf_op jit(solution)/shard_map/ppermute | solution.py:628
  459.5 40.5 %collective-permute-start.39 = (bf16[256,2048]{1,0:T(8,128)(2,1)}, bf16[256,2048]{1,0:T(8,128)(2,1)S(1)}, u32[]{:S(2)}, u32[]{:S(2)}) collective-permute-start(bf16[256,2048]{1,0:T(8,128)(2,1)} %slice.671), channel_id=1, source_target_pairs={{0,16},{8,24},{16,0},{24,8},{1,17},{9,25},{17,1},{25,9},{2,18},{10... | collective-permute-start | bytes 3145736 | tf_op jit(solution)/shard_map/ppermute | solution.py:628
  459.8 41.6 %collective-permute-start.40 = (bf16[256,2048]{1,0:T(8,128)(2,1)}, bf16[256,2048]{1,0:T(8,128)(2,1)}, u32[]{:S(2)}, u32[]{:S(2)}) collective-permute-start(bf16[256,2048]{1,0:T(8,128)(2,1)} %slice.672), channel_id=1, source_target_pairs={{0,8},{8,0},{16,24},{24,16},{1,9},{9,1},{17,25},{25,17},{2,10},{10... | collective-permute-start | bytes 3145736 | tf_op jit(solution)/shard_map/ppermute | solution.py:628
  537.9 48.0 %collective-permute-start.43 = (bf16[512,2048]{1,0:T(8,128)(2,1)}, bf16[512,2048]{1,0:T(8,128)(2,1)S(1)}, u32[]{:S(2)}, u32[]{:S(2)}) collective-permute-start(bf16[512,2048]{1,0:T(8,128)(2,1)} %add_convert_fusion.5), channel_id=1, source_target_pairs={{0,16},{8,24},{16,0},{24,8},{1,17},{9,25},{17,1},{25,9},{2,18},{10... | collective-permute-start | bytes 6291464 | tf_op jit(solution)/shard_map/ppermute | solution.py:628
  543.6 48.0 %collective-permute-start.37 = (bf16[512,2048]{1,0:T(8,128)(2,1)}, bf16[512,2048]{1,0:T(8,128)(2,1)}, u32[]{:S(2)}, u32[]{:S(2)}) collective-permute-start(bf16[512,2048]{1,0:T(8,128)(2,1)} %add_convert_fusion.6), channel_id=1, source_target_pairs={{0,8},{8,0},{16,24},{24,16},{1,9},{9,1},{17,25},{25,17},{2,10},{10... | collective-permute-start | bytes 6291464 | tf_op jit(solution)/shard_map/ppermute | solution.py:628
  599.8 53.5 %collective-permute-start.49 = (bf16[512,2048]{1,0:T(8,128)(2,1)}, bf16[512,2048]{1,0:T(8,128)(2,1)}, u32[]{:S(2)}, u32[]{:S(2)}) collective-permute-start(bf16[512,2048]{1,0:T(8,128)(2,1)} %add_convert_fusion.4), channel_id=1, source_target_pairs={{0,24},{8,16},{16,8},{24,0},{1,25},{9,17},{17,9},{25,1},{2,26},{10... | collective-permute-start | bytes 6291464 | tf_op jit(solution)/shard_map/ppermute | solution.py:628
  653.4 367.1 %reduce-scatter.8.cloned.1.call-start = ((), (), s32[]{:S(2)}) async-start(), calls=%async_computation.9 | async-start | bytes 4456448 | tf_op jit(solution)/shard_map/reduce_scatter | solution.py:1018
  669.1 63.2 %collective-permute-start.55 = (bf16[512,2048]{1,0:T(8,128)(2,1)}, bf16[512,2048]{1,0:T(8,128)(2,1)}, u32[]{:S(2)}, u32[]{:S(2)}) collective-permute-start(bf16[512,2048]{1,0:T(8,128)(2,1)} %add_convert_fusion.2), channel_id=1, source_target_pairs={{0,16},{8,24},{16,0},{24,8},{1,17},{9,25},{17,1},{25,9},{2,18},{10... | collective-permute-start | bytes 6291464 | tf_op jit(solution)/shard_map/ppermute | solution.py:628
  670.7 61.5 %collective-permute-start.54 = (bf16[512,2048]{1,0:T(8,128)(2,1)}, bf16[512,2048]{1,0:T(8,128)(2,1)}, u32[]{:S(2)}, u32[]{:S(2)}) collective-permute-start(bf16[512,2048]{1,0:T(8,128)(2,1)} %add_convert_fusion.3), channel_id=1, source_target_pairs={{0,8},{8,0},{16,24},{24,16},{1,9},{9,1},{17,25},{25,17},{2,10},{10... | collective-permute-start | bytes 6291464 | tf_op jit(solution)/shard_map/ppermute | solution.py:628
  678.5 71.2 %collective-permute-start.56 = (bf16[512,2048]{1,0:T(8,128)(2,1)}, bf16[512,2048]{1,0:T(8,128)(2,1)}, u32[]{:S(2)}, u32[]{:S(2)}) collective-permute-start(bf16[512,2048]{1,0:T(8,128)(2,1)} %get-tuple-element.189), channel_id=1, source_target_pairs={{0,4},{4,0},{1,5},{5,1},{2,6},{6,2},{3,7},{7,3},{8,12},{12,8},{9,1... | collective-permute-start | bytes 6291464 | tf_op jit(solution)/shard_map/ppermute | solution.py:628
  700.6 29.2 %collective-permute-start.57 = (bf16[2,8,128,128]{3,2,1,0:T(8,128)(2,1)S(1)}, bf16[2,8,128,128]{3,2,1,0:T(8,128)(2,1)S(1)}, u32[]{:S(2)}, u32[]{:S(2)}) collective-permute-start(bf16[2,8,128,128]{3,2,1,0:T(8,128)(2,1)S(1)} %convert_element_type.355), channel_id=1, source_target_pairs={{8,0},{16,8},{24,16},{9,1},{17,9},{25,17},{10,2},{18,10},{26,18},{... | collective-permute-start | bytes 1572872 | tf_op jit(solution)/shard_map/ppermute | solution.py:639
  762.2 48.4 %collective-permute-start.60 = (bf16[512,2048]{1,0:T(8,128)(2,1)}, bf16[512,2048]{1,0:T(8,128)(2,1)}, u32[]{:S(2)}, u32[]{:S(2)}) collective-permute-start(bf16[512,2048]{1,0:T(8,128)(2,1)} %add_convert_fusion.1), channel_id=1, source_target_pairs={{0,24},{8,16},{16,8},{24,0},{1,25},{9,17},{17,9},{25,1},{2,26},{10... | collective-permute-start | bytes 6291464 | tf_op jit(solution)/shard_map/ppermute | solution.py:628
  768.5 48.1 %collective-permute-start.53 = (bf16[512,2048]{1,0:T(8,128)(2,1)}, bf16[512,2048]{1,0:T(8,128)(2,1)}, u32[]{:S(2)}, u32[]{:S(2)}) collective-permute-start(bf16[512,2048]{1,0:T(8,128)(2,1)} %get-tuple-element.184), channel_id=1, source_target_pairs={{0,4},{4,0},{1,5},{5,1},{2,6},{6,2},{3,7},{7,3},{8,12},{12,8},{9,1... | collective-permute-start | bytes 6291464 | tf_op jit(solution)/shard_map/ppermute | solution.py:628
  824.0 81.0 %collective-permute-start.67 = (bf16[512,1536]{1,0:T(8,128)(2,1)}, bf16[512,1536]{1,0:T(8,128)(2,1)}, u32[]{:S(2)}, u32[]{:S(2)}) collective-permute-start(bf16[512,1536]{1,0:T(8,128)(2,1)} %convolution_convert_fusion.3), channel_id=1, source_target_pairs={{0,16},{8,24},{16,0},{24,8},{1,17},{9,25},{17,1},{25,9},{2,18},{10... | collective-permute-start | bytes 4718600 | tf_op jit(solution)/shard_map/ppermute | solution.py:628
  827.3 77.8 %collective-permute-start.66 = (bf16[512,1536]{1,0:T(8,128)(2,1)}, bf16[512,1536]{1,0:T(8,128)(2,1)}, u32[]{:S(2)}, u32[]{:S(2)}) collective-permute-start(bf16[512,1536]{1,0:T(8,128)(2,1)} %convolution_convert_fusion.4), channel_id=1, source_target_pairs={{0,8},{8,0},{16,24},{24,16},{1,9},{9,1},{17,25},{25,17},{2,10},{10... | collective-permute-start | bytes 4718600 | tf_op jit(solution)/shard_map/ppermute | solution.py:628
  871.0 22.5 %collective-permute-start.63 = (f32[2,8,1536]{2,1,0:T(8,128)}, f32[2,8,1536]{2,1,0:T(8,128)S(1)}, u32[]{:S(2)}, u32[]{:S(2)}) collective-permute-start(f32[2,8,1536]{2,1,0:T(8,128)} %get-tuple-element.212), channel_id=1, source_target_pairs={{8,0},{16,8},{24,16},{9,1},{17,9},{25,17},{10,2},{18,10},{26,18},{... | collective-permute-start | bytes 294920 | tf_op jit(solution)/shard_map/ppermute | solution.py:639
  899.5 49.5 %collective-permute-start.65 = (bf16[512,1664]{1,0:T(8,128)(2,1)S(1)}, bf16[512,1664]{1,0:T(8,128)(2,1)S(1)}, u32[]{:S(2)}, u32[]{:S(2)}) collective-permute-start(bf16[512,1664]{1,0:T(8,128)(2,1)S(1)} %convolution_convert_fusion.1), channel_id=1, source_target_pairs={{0,16},{8,24},{16,0},{24,8},{1,17},{9,25},{17,1},{25,9},{2,18},{10... | collective-permute-start | bytes 5111816 | tf_op jit(solution)/shard_map/ppermute | solution.py:628
  901.7 47.9 %collective-permute-start.64 = (bf16[512,1664]{1,0:T(8,128)(2,1)S(1)}, bf16[512,1664]{1,0:T(8,128)(2,1)S(1)}, u32[]{:S(2)}, u32[]{:S(2)}) collective-permute-start(bf16[512,1664]{1,0:T(8,128)(2,1)S(1)} %convolution_convert_fusion.2), channel_id=1, source_target_pairs={{0,8},{8,0},{16,24},{24,16},{1,9},{9,1},{17,25},{25,17},{2,10},{10... | collective-permute-start | bytes 5111816 | tf_op jit(solution)/shard_map/ppermute | solution.py:628
  951.9 26.2 %collective-permute-start.69 = (bf16[256,1664]{1,0:T(8,128)(2,1)}, bf16[256,1664]{1,0:T(8,128)(2,1)S(1)}, u32[]{:S(2)}, u32[]{:S(2)}) collective-permute-start(bf16[256,1664]{1,0:T(8,128)(2,1)} %fusion.15), channel_id=1, source_target_pairs={{0,16},{8,24},{16,0},{24,8},{1,17},{9,25},{17,1},{25,9},{2,18},{10... | collective-permute-start | bytes 2555912 | tf_op jit(solution)/shard_map/ppermute | solution.py:628
  955.9 22.2 %collective-permute-start.68 = (bf16[256,1664]{1,0:T(8,128)(2,1)}, bf16[256,1664]{1,0:T(8,128)(2,1)}, u32[]{:S(2)}, u32[]{:S(2)}) collective-permute-start(bf16[256,1664]{1,0:T(8,128)(2,1)} %fusion.16), channel_id=1, source_target_pairs={{0,8},{8,0},{16,24},{24,16},{1,9},{9,1},{17,25},{25,17},{2,10},{10... | collective-permute-start | bytes 2555912 | tf_op jit(solution)/shard_map/ppermute | solution.py:628
  981.4 18.5 %collective-permute-start.70 = (bf16[2,256,2048]{2,1,0:T(8,128)(2,1)}, bf16[2,256,2048]{2,1,0:T(8,128)(2,1)}, u32[]{:S(2)}, u32[]{:S(2)}) collective-permute-start(bf16[2,256,2048]{2,1,0:T(8,128)(2,1)} %constant_dynamic-slice_fusion.3), channel_id=1, source_target_pairs={{0,4},{4,0},{1,5},{5,1},{2,6},{6,2},{3,7},{7,3},{8,12},{12,8},{9,1... | collective-permute-start | bytes 6291464 | tf_op jit(solution)/shard_map/ppermute | solution.py:628
  981.5 35.1 %collective-permute-start.81 = (bf16[256,1536]{1,0:T(8,128)(2,1)}, bf16[256,1536]{1,0:T(8,128)(2,1)}, u32[]{:S(2)}, u32[]{:S(2)}) collective-permute-start(bf16[256,1536]{1,0:T(8,128)(2,1)} %fusion.13), channel_id=1, source_target_pairs={{0,16},{8,24},{16,0},{24,8},{1,17},{9,25},{17,1},{25,9},{2,18},{10... | collective-permute-start | bytes 2359304 | tf_op jit(solution)/shard_map/ppermute | solution.py:628
  981.9 34.8 %collective-permute-start.80 = (bf16[256,1536]{1,0:T(8,128)(2,1)}, bf16[256,1536]{1,0:T(8,128)(2,1)}, u32[]{:S(2)}, u32[]{:S(2)}) collective-permute-start(bf16[256,1536]{1,0:T(8,128)(2,1)} %fusion.12), channel_id=1, source_target_pairs={{0,8},{8,0},{16,24},{24,16},{1,9},{9,1},{17,25},{25,17},{2,10},{10... | collective-permute-start | bytes 2359304 | tf_op jit(solution)/shard_map/ppermute | solution.py:628
  991.5 41.8 %all-to-all-start.1 = ((bf16[4,2112,128]{2,1,0:T(8,128)(2,1)}), bf16[4,2112,128]{2,1,0:T(8,128)(2,1)}, u32[]{:S(2)}, u32[]{:S(2)}) async-start(bf16[4,2112,128]{2,1,0:T(8,128)(2,1)} %bitcast.140), calls=%async_computation.4 | async-start | bytes 4325376 | tf_op jit(solution)/shard_map/all_to_all | solution.py:1082
  996.0 77.6 %reduce-scatter.6.cloned.1.call-start = ((), (), s32[]{:S(2)}) async-start(), calls=%async_computation.8 | async-start | bytes 1966080 | tf_op jit(solution)/shard_map/reduce_scatter | solution.py:1071
  1010.9 71.5 %collective-permute-start.77 = (bf16[128,1664]{1,0:T(8,128)(2,1)}, bf16[128,1664]{1,0:T(8,128)(2,1)}, u32[]{:S(2)}, u32[]{:S(2)}) collective-permute-start(bf16[128,1664]{1,0:T(8,128)(2,1)} %get-tuple-element.342), channel_id=1, source_target_pairs={{0,1},{1,2},{2,3},{3,0},{4,5},{5,6},{6,7},{7,4},{8,9},{9,10},{10,1... | collective-permute-start | bytes 1277960 | tf_op jit(solution)/shard_map/ppermute | solution.py:633
  1010.9 71.5 %collective-permute-start.78 = (bf16[128,1664]{1,0:T(8,128)(2,1)}, bf16[128,1664]{1,0:T(8,128)(2,1)}, u32[]{:S(2)}, u32[]{:S(2)}) collective-permute-start(bf16[128,1664]{1,0:T(8,128)(2,1)} %get-tuple-element.341), channel_id=1, source_target_pairs={{0,2},{1,3},{2,0},{3,1},{4,6},{5,7},{6,4},{7,5},{8,10},{9,11},{10,... | collective-permute-start | bytes 1277960 | tf_op jit(solution)/shard_map/ppermute | solution.py:633
  1016.6 65.9 %collective-permute-start.79 = (bf16[128,1664]{1,0:T(8,128)(2,1)}, bf16[128,1664]{1,0:T(8,128)(2,1)}, u32[]{:S(2)}, u32[]{:S(2)}) collective-permute-start(bf16[128,1664]{1,0:T(8,128)(2,1)} %get-tuple-element.340), channel_id=1, source_target_pairs={{0,3},{1,0},{2,1},{3,2},{4,7},{5,4},{6,5},{7,6},{8,11},{9,8},{10,9... | collective-permute-start | bytes 1277960 | tf_op jit(solution)/shard_map/ppermute | solution.py:633
  1035.9 27.1 %collective-permute-start.75 = (f32[16640]{0:T(1024)S(1)}, f32[16640]{0:T(1024)S(1)}, u32[]{:S(2)}, u32[]{:S(2)}) collective-permute-start(f32[16640]{0:T(1024)S(1)} %add.322), channel_id=1, source_target_pairs={{0,1},{1,0},{2,3},{3,2},{4,5},{5,4},{6,7},{7,6},{8,9},{9,8},{10,11... | collective-permute-start | bytes 199688 | tf_op jit(solution)/shard_map/ppermute | solution.py:628
  1063.0 19.4 %collective-permute-start.76 = (f32[16640]{0:T(1024)S(1)}, f32[16640]{0:T(1024)S(1)}, u32[]{:S(2)}, u32[]{:S(2)}) collective-permute-start(f32[16640]{0:T(1024)S(1)} %add.323), channel_id=1, source_target_pairs={{0,2},{1,3},{2,0},{3,1},{4,6},{5,7},{6,4},{7,5},{8,10},{9,11},{10,... | collective-permute-start | bytes 199688 | tf_op jit(solution)/shard_map/ppermute | solution.py:628
  (111 other events, 1012.9 us)
Sparse Core Ops, SparseCore 0:
  121.5 113.1 all-gather.2
  236.3 74.8 all-gather.4
  653.5 151.3 reduce-scatter.3
  824.1 100.6 reduce-scatter.7
  1020.7 52.8 reduce-scatter.5

commit v11 on v10

--- a/solution.py
+++ b/solution.py
@@ -1064,7 +1064,8 @@
 
     conv_cols = jnp.concatenate([jnp.sum(part, axis=0)[:taps] for part in conv_parts], axis=1)
     gains = butterfly(jnp.concatenate([gain_mix_part, gain_ffn_part, gain_o_part]), ("tp",))
-    sums = jnp.concatenate([gains, conv_cols.reshape(-1), jnp.sum(logits, axis=0)])
+    conv_kinds = jnp.stack(by_kind([conv_cols]))
+    sums = jnp.concatenate([gains, conv_kinds.reshape(-1), jnp.sum(logits, axis=0)])
     last_line = Line(scatter.own())
     for p in range(1, parts):
         own = low(earlier_scatter.own(*last_line.sent))
@@ -1075,7 +1076,7 @@
     beta_grad = mix_grads[0][:, part_cols : part_cols + heads_here]
     ends = [width, 2 * width, 2 * width + LANES, sums.shape[0] - LANES]
     gain_mix_grad, gain_ffn_grad, gain_o_grad, conv_grad, bias_grad = jnp.split(sums, ends)
-    conv_grad = jnp.stack(by_kind([conv_grad.reshape(taps, -1)]))
+    conv_grad = conv_grad.reshape(conv_kinds.shape)
     bias_grad = bias_grad[:heads_here]
     out_grad_w = wide(tie(out_grad_w, *scatter.last)).T
     pieces = tie(total, *scatter.last).reshape(3 * units, 4, shard_rows).transpose(1, 0, 2)

time: 1120 us -> 1120 us (level)
    ppermute x10, waiting for transfers between devices: 91.7 us -> 71.9 us  [from_behind(): return lax.ppermute(block, axis, route)]
    ppermute x60, waiting for transfers between devices: 187 us -> 206 us  [flip(): return lax.ppermute(value, axis, [(i, i ^ bit) for i in devices])]
    unnamed x222 -> x224, local copies, waits for them, and re-layouts: 40.2 us -> 35.7 us
  transfers between devices with their start and end apart: 89 -> 89, of which waited for: 38 -> 38; matrix products, arithmetic and copies ran while one was open for 19% -> 20% of each run, Pallas kernels for 36% -> 35%
where the time goes in v11:
time: 1120 us; the launch traced here: 1110 us
  Pallas kernels  394 us (35%)
  waiting for transfers between devices  314 us (28%)
  starting transfers between devices  129 us (12%)
  other arithmetic  115 us (10%)
  local copies, waits for them, and re-layouts  93.4 us (8%)
  matrix products  47.4 us (4%)
  between operations  15.6 us (1%)
    ppermute x60, waiting for transfers between devices, flip(): return lax.ppermute(value, axis, [(i, i ^ bit) for i in devices])  206 us
    pallas_call x4, Pallas kernels, ffn_both(): pl.pallas_call(ffn_kernel, grid=(count // tile,), in_specs=[wide_rows] *...  118 us
    ppermute x10, waiting for transfers between devices, from_behind(): return lax.ppermute(block, axis, route)  71.9 us
    pallas_call x2, Pallas kernels, mixer_backward(): pl.pallas_call(functools.partial(backward_kernel, taps, group, first), gr...  66.4 us
    ppermute x60, starting transfers between devices, flip(): return lax.ppermute(value, axis, [(i, i ^ bit) for i in devices])  55.8 us
    pallas_call x2, Pallas kernels, mixer_forward(): pl.pallas_call(functools.partial(forward_kernel, taps, group, first), gri...  55 us
    pallas_call x1, Pallas kernels, ffn_weights(): pl.pallas_call(functools.partial(ffn_weights_kernel, count, lines), grid=...  48 us
    dot_general x11, matrix products, outer_rows(): lax.dot_general(left, right, (((0,), (0,)), ((), ())), preferred_element_...  43.9 us
  transfers between devices with their start and end apart: 89, of which 38 were waited for; matrix products, arithmetic and copies ran while one was open for 20% of the time, Pallas kernels for 35%

profile of v11, /device:TPU:0, one launch (start us, length us, event | category | flops | bytes accessed | tf_op | source)
XLA Modules:
  0.0 1108.8 jit_solution(6276533601797984621)
XLA Ops:
  12.6 5.3 all-to-all-start
  27.8 9.3 collective-permute-done
  37.1 17.1 %collective-permute-done.1 = bf16[128,1664]{1,0:T(8,128)(2,1)S(1)} collective-permute-done((bf16[128,1664]{1,0:T(8,128)(2,1)}, bf16[128,1664]{1,0:T(8,128)(2,1)S(1)}, u32[]{:S(2)}, u32[]{:S(2)}) %collective-permute-start.1) | collective-permute-done | bytes 426016 | tf_op jit(solution)/shard_map/ppermute | solution.py:633
  63.1 10.7 collective-permute-start.10
  77.5 18.7 %collective-permute-done.3.refs_1_.refs_3_ = bf16[512,1664]{1,0:T(8,128)(2,1)S(1)} collective-permute-done((bf16[512,1664]{1,0:T(8,128)(2,1)}, bf16[512,1664]{1,0:T(8,128)(2,1)S(1)}, u32[]{:S(2)}, u32[]{:S(2)}) %collective-permute-start.3) | collective-permute-done | bytes 1703968 | tf_op jit(solution)/shard_map/ppermute | solution.py:628
  101.3 6.6 collective-permute-done.9
  112.5 5.9 collective-permute-done.5.refs_3_.refs_5_
  121.4 6.6 convert_element_type.398
  131.5 4.7 shard_map.271
  140.8 12.8 %shard_map.272.pre.beta = f32[1024,1664]{1,0:T(8,128)} custom-call(s32[1]{0:T(128)} %bitcast.1.place, bf16[1024,2048]{1,0:T(8,128)(2,1)} %fusion.1.rows, bf16[512,1664]{1,0:T(8,128)(2,1)} %pad_maximum_fusion.6.refs_0_.refs_2_, bf16[512,1664]{1,0:T(8,128)(2,1)} %copy-done.29, bf16[512,1664]{1,0:T(8,128)(2,1)} %copy-done.30, bf16[256,1664]{1,0:T(8,128)(2,1)} %copy-done.48, ...), custom_call_target="tpu_custom_call" | custom-call | flops 6979321856 | bytes 11010048 | tf_op jit(solution)/shard_map/pallas_call | solution.py:551
  155.6 27.5 %shard_map.273 = (f32[1024,512]{1,0:T(8,128)}, bf16[1024,512]{1,0:T(8,128)(2,1)}, f32[2,4,128,256]{3,2,1,0:T(8,128)}, bf16[2,4,4,128,128]{4,3,2,1,0:T(8,128)(2,1...) custom-call(f32[1024,1664]{1,0:T(8,128)} %shard_map.272.pre.beta, ...), custom_call_target="tpu_custom_call" | custom-call | flops 4026531840 | bytes 20971520 | tf_op jit(solution)/shard_map/pallas_call | solution.py:160
  183.1 4.8 collective-permute-done.11.refs_1_.refs_8_
  194.3 13.6 %collective-permute-done.13.refs_3_.refs_10_ = bf16[256,1536]{1,0:T(8,128)(2,1)S(1)} collective-permute-done((bf16[256,1536]{1,0:T(8,128)(2,1)}, bf16[256,1536]{1,0:T(8,128)(2,1)S(1)}, u32[]{:S(2)}, u32[]{:S(2)}) %collective-permute-start.13) | collective-permute-done | bytes 786464 | tf_op jit(solution)/shard_map/ppermute | solution.py:628
  218.2 4.4 shard_map.274
  226.5 11.5 %shard_map.275.pre = f32[1024,1536]{1,0:T(8,128)} custom-call(s32[1]{0:T(128)} %bitcast.1.place, bf16[1024,2048]{1,0:T(8,128)(2,1)} %fusion.1.rows, bf16[512,1536]{1,0:T(8,128)(2,1)} %pad_maximum_fusion.7.refs_0_.refs_7_, bf16[512,1536]{1,0:T(8,128)(2,1)} %copy-done.31, bf16[512,1536]{1,0:T(8,128)(2,1)} %collective-permute-done.12.refs_2_.refs_9_, ...), custom_call_target="tpu_custom_call" | custom-call | flops 6442450944 | bytes 10485760 | tf_op jit(solution)/shard_map/pallas_call | solution.py:551
  238.0 10.2 collective-permute-start.24
  252.5 5.2 collective-permute-start.26
  258.3 27.5 %shard_map.276 = (f32[1024,512]{1,0:T(8,128)}, bf16[1024,512]{1,0:T(8,128)(2,1)}, f32[2,4,128,256]{3,2,1,0:T(8,128)}, bf16[2,4,4,128,128]{4,3,2,1,0:T(8,128)(2,1...) custom-call(f32[1024,1536]{1,0:T(8,128)} %shard_map.275.pre, ...), custom_call_target="tpu_custom_call" | custom-call | flops 4026531840 | bytes 20971520 | tf_op jit(solution)/shard_map/pallas_call | solution.py:160
  289.5 8.1 shard_map.277.gate_w.up_w
  297.7 4.6 collective-permute-start.18
  303.7 6.1 collective-permute-done.18
  310.1 4.4 collective-permute-start.19
  317.7 6.7 collective-permute-done.19
  324.4 6.8 collective-permute-start.28
  331.5 15.2 %collective-permute-done.27.refs_2_.refs_1_ = bf16[512,1024]{1,0:T(8,128)(2,1)S(1)} collective-permute-done((bf16[512,1024]{1,0:T(8,128)(2,1)S(1)}, bf16[512,1024]{1,0:T(8,128)(2,1)S(1)}, u32[]{:S(2)}, u32[]{:S(2)}) %collective-permute-start.27) | collective-permute-done | bytes 1048608 | tf_op jit(solution)/shard_map/ppermute | solution.py:628
  349.0 6.3 collective-permute-done.28.refs_3_.refs_2_
  361.1 4.5 shard_map.278
  365.6 4.6 shard_map.279
  373.0 8.7 shard_map.280
  393.5 4.4 shard_map.281.down_w
  402.1 29.5 %shard_map.282 = (bf16[3,512,704]{2,1,0:T(8,128)(2,1)}, bf16[512,2048]{1,0:T(8,128)(2,1)}, bf16[512,2048]{1,0:T(8,128)(2,1)}, bf16[3,512,704]{2,1,0:T(8,128)(2,1...) custom-call(bf16[512,2048]{1,0:T(8,128)(2,1)} %copy-done.38, ...), custom_call_target="tpu_custom_call" | custom-call | flops 17716740096 | bytes 25427968 | tf_op jit(solution)/shard_map/pallas_call | solution.py:469
  431.6 8.7 collective-permute-done.34.mine.refs_10_
  440.3 7.8 collective-permute-done.38.mine.refs_12_
  460.5 29.6 %shard_map.283 = (bf16[3,512,704]{2,1,0:T(8,128)(2,1)}, bf16[512,2048]{1,0:T(8,128)(2,1)}, bf16[512,2048]{1,0:T(8,128)(2,1)}, bf16[3,512,704]{2,1,0:T(8,128)(2,1...) custom-call(bf16[512,2048]{1,0:T(8,128)(2,1)} %collective-permute-done.34.mine.refs_10_, ...), custom_call_target="tpu_custom_call" | custom-call | flops 17716740096 | bytes 25427968 | tf_op jit(solution)/shard_map/pallas_call | solution.py:469
  490.1 10.0 collective-permute-done.39
  501.5 29.7 %shard_map.284 = (bf16[3,512,704]{2,1,0:T(8,128)(2,1)}, bf16[512,2048]{1,0:T(8,128)(2,1)}, bf16[512,2048]{1,0:T(8,128)(2,1)}, bf16[3,512,704]{2,1,0:T(8,128)(2,1...) custom-call(bf16[512,2048]{1,0:T(8,128)(2,1)} %collective-permute-done.38.mine.refs_12_, ...), custom_call_target="tpu_custom_call" | custom-call | flops 17716740096 | bytes 25427968 | tf_op jit(solution)/shard_map/pallas_call | solution.py:469
  546.4 29.5 %shard_map.285 = (bf16[3,512,704]{2,1,0:T(8,128)(2,1)}, bf16[512,2048]{1,0:T(8,128)(2,1)}, bf16[512,2048]{1,0:T(8,128)(2,1)}, bf16[3,512,704]{2,1,0:T(8,128)(2,1...) custom-call(bf16[512,2048]{1,0:T(8,128)(2,1)} %copy-done.54, ...), custom_call_target="tpu_custom_call" | custom-call | flops 17716740096 | bytes 25427968 | tf_op jit(solution)/shard_map/pallas_call | solution.py:469
  575.9 10.1 collective-permute-done.43
  586.0 5.7 collective-permute-done.37
  605.4 48.0 %shard_map.286 = bf16[4,3,704,512]{3,2,1,0:T(8,128)(2,1)} custom-call(bf16[3,512,704]{2,1,0:T(8,128)(2,1)} %get-tuple-element.176.refs_0_, bf16[3,512,704]{2,1,0:T(8,128)(2,1)} %get-tuple-element.177.refs_1_, bf16[3,512,704]{2,1,0:T(8,128)(2,1)} %get-tuple-element.158.refs_2_, bf16[3,512,704]{2,1,0:T(8,128)(2,1)} %get-tuple-element.178.refs_3_, ...), custom_call_target="tpu_custom_call" | custom-call | flops 35433480192 | bytes 67108864 | tf_op jit(solution)/shard_map/pallas_call | solution.py:516
  659.2 7.0 multiply_reduce_fusion.1
  678.8 9.0 shard_map.287.grad
  687.7 5.7 shard_map.289
  693.5 5.8 shard_map.288
  701.9 27.9 %collective-permute-done.57 = bf16[2,8,128,128]{3,2,1,0:T(8,128)(2,1)S(1)} collective-permute-done((bf16[2,8,128,128]{3,2,1,0:T(8,128)(2,1)S(1)}, bf16[2,8,128,128]{3,2,1,0:T(8,128)(2,1)S(1)}, u32[]{:S(2)}, u32[]{:S(2)}) %collective-permute-start.57) | collective-permute-done | bytes 524320 | tf_op jit(solution)/shard_map/ppermute | solution.py:639
  732.4 14.0 %collective-permute-done.58 = bf16[2,8,128,128]{3,2,1,0:T(8,128)(2,1)} collective-permute-done((bf16[2,8,128,128]{3,2,1,0:T(8,128)(2,1)}, bf16[2,8,128,128]{3,2,1,0:T(8,128)(2,1)}, u32[]{:S(2)}, u32[]{:S(2)}) %collective-permute-start.58) | collective-permute-done | bytes 524320 | tf_op jit(solution)/shard_map/ppermute | solution.py:639
  753.8 8.5 collective-permute-done.59
  762.3 6.3 convolution_convert_fusion
  769.6 33.1 %shard_map.290 = (bf16[1024,1536]{1,0:T(8,128)(2,1)}, f32[2,8,1536]{2,1,0:T(8,128)}, f32[2,8,1536]{2,1,0:T(8,128)}, f32[2,8,1536]{2,1,0:T(8,128)}, f32[1024,128]{1,0:T(8,128)}) custom-call(f32[1024,1536]{1,0:T(8,128)} %shard_map.275.pre, f32[1024,1664]{1,0:T(8,128)} %shard_map.272.pre.beta, f32[1,128]{1,0:T(1,128)} %pad_bitcast_fusion.bias, ...), custom_call_target="tpu_custom_call" | custom-call | flops 4026531840 | bytes 20971520 | tf_op jit(solution)/shard_map/pallas_call | solution.py:318
  806.3 4.4 collective-permute-done.61
  816.7 7.4 add_convert_fusion
  828.3 5.7 fusion.24
  839.2 33.3 %shard_map.291 = (bf16[1024,1536]{1,0:T(8,128)(2,1)}, f32[2,8,1536]{2,1,0:T(8,128)}, f32[2,8,1536]{2,1,0:T(8,128)}, f32[2,8,1536]{2,1,0:T(8,128)}, f32[1024,128]{1,0:T(8,128)}) custom-call(f32[1024,1664]{1,0:T(8,128)} %shard_map.272.pre.beta, f32[1024,1664]{1,0:T(8,128)} %shard_map.272.pre.beta, f32[1,128]{1,0:T(1,128)} %pad_bitcast_fusion.bias, ...), custom_call_target="tpu_custom_call" | custom-call | flops 4026531840 | bytes 20971520 | tf_op jit(solution)/shard_map/pallas_call | solution.py:318
  875.3 10.8 collective-permute-done.67
  886.1 5.5 collective-permute-done.66
  914.0 6.3 fusion.26
  922.2 30.6 %collective-permute-done.65 = bf16[512,1664]{1,0:T(8,128)(2,1)} collective-permute-done((bf16[512,1664]{1,0:T(8,128)(2,1)}, bf16[512,1664]{1,0:T(8,128)(2,1)}, u32[]{:S(2)}, u32[]{:S(2)}) %collective-permute-start.65) | collective-permute-done | bytes 1703968 | tf_op jit(solution)/shard_map/ppermute | solution.py:628
  964.7 21.6 %shard_map.292 = bf16[1024,2048]{1,0:T(8,128)(2,1)} custom-call(s32[1]{0:T(128)} %bitcast.1.place, bf16[1024,1664]{1,0:T(8,128)(2,1)} %pad_maximum_fusion.3.refs_0_, bf16[1024,1536]{1,0:T(8,128)(2,1)} %bitcast.132, bf16[512,1664]{1,0:T(8,128)(2,1)} %pad_maximum_fusion.6.refs_0_.refs_2_, bf16[512,1664]{1,0:T(8,128)(2,1)} %copy-done.29, ...), custom_call_target="tpu_custom_call" | custom-call | flops 13421772800 | bytes 17301504 | tf_op jit(solution)/shard_map/pallas_call | solution.py:587
  989.6 4.8 reshape.209
  997.7 4.5 all-to-all-start.1
  1011.4 4.3 fusion.9
  1017.6 6.1 collective-permute-start.78
  1046.7 23.3 %collective-permute-done.75 = f32[16640]{0:T(1024)S(1)} collective-permute-done((f32[16640]{0:T(1024)S(1)}, f32[16640]{0:T(1024)S(1)}, u32[]{:S(2)}, u32[]{:S(2)}) %collective-permute-start.75) | collective-permute-done | bytes 66592 | tf_op jit(solution)/shard_map/ppermute | solution.py:628
  1082.2 6.8 collective-permute-done.76
  (511 shorter events, 309.1 us)
Async XLA Ops:
  12.6 44.3 %all-to-all-start = ((bf16[4,2112,128]{2,1,0:T(8,128)(2,1)}), bf16[4,2112,128]{2,1,0:T(8,128)(2,1)S(1)}, u32[]{:S(2)}, u32[]{:S(2)}) async-start(bf16[4,2112,128]{2,1,0:T(8,128)(2,1)} %bitcast.139), calls=%async_computation | async-start | bytes 4325376 | tf_op jit(solution)/shard_map/all_to_all | solution.py:894
  17.8 271.7 %all-gather.3.cloned.1.call-start = ((), (), s32[]{:S(2)}) async-start(), calls=%async_computation.5 | async-start | bytes 7208960 | tf_op jit(solution)/shard_map/all_gather | solution.py:912
  23.8 30.4 %collective-permute-start.1 = (bf16[128,1664]{1,0:T(8,128)(2,1)}, bf16[128,1664]{1,0:T(8,128)(2,1)S(1)}, u32[]{:S(2)}, u32[]{:S(2)}) collective-permute-start(bf16[128,1664]{1,0:T(8,128)(2,1)} %constant_dynamic-update-slice_fusion), channel_id=1, source_target_pairs={{0,2},{1,3},{2,0},{3,1},{4,6},{5,7},{6,4},{7,5},{8,10},{9,11},{10,... | collective-permute-start | bytes 1277960 | tf_op jit(solution)/shard_map/ppermute | solution.py:633
  26.4 27.8 %collective-permute-start.2 = (bf16[128,1664]{1,0:T(8,128)(2,1)}, bf16[128,1664]{1,0:T(8,128)(2,1)S(1)}, u32[]{:S(2)}, u32[]{:S(2)}) collective-permute-start(bf16[128,1664]{1,0:T(8,128)(2,1)} %constant_dynamic-update-slice_fusion), channel_id=1, source_target_pairs={{0,3},{1,0},{2,1},{3,2},{4,7},{5,4},{6,5},{7,6},{8,11},{9,8},{10,9... | collective-permute-start | bytes 1277960 | tf_op jit(solution)/shard_map/ppermute | solution.py:633
  56.9 39.2 %collective-permute-start.3 = (bf16[512,1664]{1,0:T(8,128)(2,1)}, bf16[512,1664]{1,0:T(8,128)(2,1)S(1)}, u32[]{:S(2)}, u32[]{:S(2)}) collective-permute-start(bf16[512,1664]{1,0:T(8,128)(2,1)} %pad_maximum_fusion.6.refs_0_.refs_2_), channel_id=1, source_target_pairs={{0,8},{8,0},{16,24},{24,16},{1,9},{9,1},{17,25},{25,17},{2,10},{10... | collective-permute-start | bytes 5111816 | tf_op jit(solution)/shard_map/ppermute | solution.py:628
  58.5 39.0 %collective-permute-start.4 = (bf16[512,1664]{1,0:T(8,128)(2,1)}, bf16[512,1664]{1,0:T(8,128)(2,1)S(1)}, u32[]{:S(2)}, u32[]{:S(2)}) collective-permute-start(bf16[512,1664]{1,0:T(8,128)(2,1)} %pad_maximum_fusion.6.refs_0_.refs_2_), channel_id=1, source_target_pairs={{0,16},{8,24},{16,0},{24,8},{1,17},{9,25},{17,1},{25,9},{2,18},{10... | collective-permute-start | bytes 5111816 | tf_op jit(solution)/shard_map/ppermute | solution.py:628
  63.1 38.2 %collective-permute-start.10 = (bf16[128,1536]{1,0:T(8,128)(2,1)S(1)}, bf16[128,1536]{1,0:T(8,128)(2,1)S(1)}, u32[]{:S(2)}, u32[]{:S(2)}) collective-permute-start(bf16[128,1536]{1,0:T(8,128)(2,1)S(1)} %copy-done.62), channel_id=1, source_target_pairs={{0,3},{1,0},{2,1},{3,2},{4,7},{5,4},{6,5},{7,6},{8,11},{9,8},{10,9... | collective-permute-start | bytes 1179656 | tf_op jit(solution)/shard_map/ppermute | solution.py:633
  73.8 27.6 %collective-permute-start.8 = (bf16[128,1536]{1,0:T(8,128)(2,1)S(1)}, bf16[128,1536]{1,0:T(8,128)(2,1)S(1)}, u32[]{:S(2)}, u32[]{:S(2)}) collective-permute-start(bf16[128,1536]{1,0:T(8,128)(2,1)S(1)} %copy-done.62), channel_id=1, source_target_pairs={{0,1},{1,2},{2,3},{3,0},{4,5},{5,6},{6,7},{7,4},{8,9},{9,10},{10,1... | collective-permute-start | bytes 1179656 | tf_op jit(solution)/shard_map/ppermute | solution.py:633
  73.8 34.2 %collective-permute-start.9 = (bf16[128,1536]{1,0:T(8,128)(2,1)S(1)}, bf16[128,1536]{1,0:T(8,128)(2,1)S(1)}, u32[]{:S(2)}, u32[]{:S(2)}) collective-permute-start(bf16[128,1536]{1,0:T(8,128)(2,1)S(1)} %copy-done.62), channel_id=1, source_target_pairs={{0,2},{1,3},{2,0},{3,1},{4,6},{5,7},{6,4},{7,5},{8,10},{9,11},{10,... | collective-permute-start | bytes 1179656 | tf_op jit(solution)/shard_map/ppermute | solution.py:633
  98.5 19.8 %collective-permute-start.5 = (bf16[256,1664]{1,0:T(8,128)(2,1)}, bf16[256,1664]{1,0:T(8,128)(2,1)S(1)}, u32[]{:S(2)}, u32[]{:S(2)}) collective-permute-start(bf16[256,1664]{1,0:T(8,128)(2,1)} %slice.640), channel_id=1, source_target_pairs={{0,16},{8,24},{16,0},{24,8},{1,17},{9,25},{17,1},{25,9},{2,18},{10... | collective-permute-start | bytes 2555912 | tf_op jit(solution)/shard_map/ppermute | solution.py:628
  100.0 19.8 %collective-permute-start.6 = (bf16[256,1664]{1,0:T(8,128)(2,1)}, bf16[256,1664]{1,0:T(8,128)(2,1)}, u32[]{:S(2)}, u32[]{:S(2)}) collective-permute-start(bf16[256,1664]{1,0:T(8,128)(2,1)} %slice.641), channel_id=1, source_target_pairs={{0,8},{8,0},{16,24},{24,16},{1,9},{9,1},{17,25},{25,17},{2,10},{10... | collective-permute-start | bytes 2555912 | tf_op jit(solution)/shard_map/ppermute | solution.py:628
  121.4 260.4 %all-gather.5.cloned.1.call-start = ((), (), s32[]{:S(2)}) async-start(), calls=%async_computation.6 | async-start | bytes 3604480 | tf_op jit(solution)/shard_map/all_gather | solution.py:913
  137.1 16.6 %collective-permute-start.7 = (bf16[2,8,1536]{2,1,0:T(8,128)(2,1)S(1)}, bf16[2,8,1536]{2,1,0:T(8,128)(2,1)S(1)}, u32[]{:S(2)}, u32[]{:S(2)}) collective-permute-start(bf16[2,8,1536]{2,1,0:T(8,128)(2,1)S(1)} %slice_bitcast_fusion), channel_id=1, source_target_pairs={{0,8},{8,16},{16,24},{1,9},{9,17},{17,25},{2,10},{10,18},{18,26},{... | collective-permute-start | bytes 147464 | tf_op jit(solution)/shard_map/ppermute | solution.py:639
  153.7 34.2 %collective-permute-start.11 = (bf16[512,1536]{1,0:T(8,128)(2,1)S(1)}, bf16[512,1536]{1,0:T(8,128)(2,1)S(1)}, u32[]{:S(2)}, u32[]{:S(2)}) collective-permute-start(bf16[512,1536]{1,0:T(8,128)(2,1)S(1)} %copy-done.24), channel_id=1, source_target_pairs={{0,8},{8,0},{16,24},{24,16},{1,9},{9,1},{17,25},{25,17},{2,10},{10... | collective-permute-start | bytes 4718600 | tf_op jit(solution)/shard_map/ppermute | solution.py:628
  154.1 34.8 %collective-permute-start.12 = (bf16[512,1536]{1,0:T(8,128)(2,1)S(1)}, bf16[512,1536]{1,0:T(8,128)(2,1)}, u32[]{:S(2)}, u32[]{:S(2)}) collective-permute-start(bf16[512,1536]{1,0:T(8,128)(2,1)S(1)} %copy-done.24), channel_id=1, source_target_pairs={{0,16},{8,24},{16,0},{24,8},{1,17},{9,25},{17,1},{25,9},{2,18},{10... | collective-permute-start | bytes 4718600 | tf_op jit(solution)/shard_map/ppermute | solution.py:628
  191.0 16.9 %collective-permute-start.13 = (bf16[256,1536]{1,0:T(8,128)(2,1)}, bf16[256,1536]{1,0:T(8,128)(2,1)S(1)}, u32[]{:S(2)}, u32[]{:S(2)}) collective-permute-start(bf16[256,1536]{1,0:T(8,128)(2,1)} %slice.667), channel_id=1, source_target_pairs={{0,16},{8,24},{16,0},{24,8},{1,17},{9,25},{17,1},{25,9},{2,18},{10... | collective-permute-start | bytes 2359304 | tf_op jit(solution)/shard_map/ppermute | solution.py:628
  191.8 17.9 %collective-permute-start.14 = (bf16[256,1536]{1,0:T(8,128)(2,1)}, bf16[256,1536]{1,0:T(8,128)(2,1)}, u32[]{:S(2)}, u32[]{:S(2)}) collective-permute-start(bf16[256,1536]{1,0:T(8,128)(2,1)} %slice.668), channel_id=1, source_target_pairs={{0,8},{8,0},{16,24},{24,16},{1,9},{9,1},{17,25},{25,17},{2,10},{10... | collective-permute-start | bytes 2359304 | tf_op jit(solution)/shard_map/ppermute | solution.py:628
  209.7 88.0 %collective-permute-start.16 = (bf16[512,2048]{1,0:T(8,128)(2,1)S(1)}, bf16[512,2048]{1,0:T(8,128)(2,1)}, u32[]{:S(2)}, u32[]{:S(2)}) collective-permute-start(bf16[512,2048]{1,0:T(8,128)(2,1)S(1)} %bitcast.123), channel_id=1, source_target_pairs={{0,8},{8,0},{16,24},{24,16},{1,9},{9,1},{17,25},{25,17},{2,10},{10... | collective-permute-start | bytes 6291464 | tf_op jit(solution)/shard_map/ppermute | solution.py:628
  210.3 87.3 %collective-permute-start.17 = (bf16[512,2048]{1,0:T(8,128)(2,1)S(1)}, bf16[512,2048]{1,0:T(8,128)(2,1)}, u32[]{:S(2)}, u32[]{:S(2)}) collective-permute-start(bf16[512,2048]{1,0:T(8,128)(2,1)S(1)} %bitcast.124), channel_id=1, source_target_pairs={{0,16},{8,24},{16,0},{24,8},{1,17},{9,25},{17,1},{25,9},{2,18},{10... | collective-permute-start | bytes 6291464 | tf_op jit(solution)/shard_map/ppermute | solution.py:628
  215.9 623.4 %reduce-scatter.4.cloned.1.call-start = ((), (), s32[]{:S(2)}) async-start(), calls=%async_computation.7 | async-start | bytes 10813440 | tf_op jit(solution)/shard_map/reduce_scatter | solution.py:1014
  223.4 29.0 %collective-permute-start.15 = (bf16[2,8,1536]{2,1,0:T(8,128)(2,1)S(1)}, bf16[2,8,1536]{2,1,0:T(8,128)(2,1)S(1)}, u32[]{:S(2)}, u32[]{:S(2)}) collective-permute-start(bf16[2,8,1536]{2,1,0:T(8,128)(2,1)S(1)} %convert_bitcast_fusion.4), channel_id=1, source_target_pairs={{0,8},{8,16},{16,24},{1,9},{9,17},{17,25},{2,10},{10,18},{18,26},{... | collective-permute-start | bytes 147464 | tf_op jit(solution)/shard_map/ppermute | solution.py:639
  238.0 64.4 %collective-permute-start.24 = (bf16[128,1024]{1,0:T(8,128)(2,1)S(1)}, bf16[128,1024]{1,0:T(8,128)(2,1)}, u32[]{:S(2)}, u32[]{:S(2)}) collective-permute-start(bf16[128,1024]{1,0:T(8,128)(2,1)S(1)} %bitcast.158), channel_id=1, source_target_pairs={{0,1},{1,2},{2,3},{3,0},{4,5},{5,6},{6,7},{7,4},{8,9},{9,10},{10,1... | collective-permute-start | bytes 786440 | tf_op jit(solution)/shard_map/ppermute | solution.py:633
  248.2 54.2 %collective-permute-start.25 = (bf16[128,1024]{1,0:T(8,128)(2,1)S(1)}, bf16[128,1024]{1,0:T(8,128)(2,1)}, u32[]{:S(2)}, u32[]{:S(2)}) collective-permute-start(bf16[128,1024]{1,0:T(8,128)(2,1)S(1)} %bitcast.159), channel_id=1, source_target_pairs={{0,2},{1,3},{2,0},{3,1},{4,6},{5,7},{6,4},{7,5},{8,10},{9,11},{10,... | collective-permute-start | bytes 786440 | tf_op jit(solution)/shard_map/ppermute | solution.py:633
  252.5 50.0 %collective-permute-start.26 = (bf16[128,1024]{1,0:T(8,128)(2,1)S(1)}, bf16[128,1024]{1,0:T(8,128)(2,1)}, u32[]{:S(2)}, u32[]{:S(2)}) collective-permute-start(bf16[128,1024]{1,0:T(8,128)(2,1)S(1)} %bitcast.160), channel_id=1, source_target_pairs={{0,3},{1,0},{2,1},{3,2},{4,7},{5,4},{6,5},{7,6},{8,11},{9,8},{10,9... | collective-permute-start | bytes 786440 | tf_op jit(solution)/shard_map/ppermute | solution.py:633
  302.4 70.7 %collective-permute-start.21 = (bf16[512,2048]{1,0:T(8,128)(2,1)S(1)}, bf16[512,2048]{1,0:T(8,128)(2,1)}, u32[]{:S(2)}, u32[]{:S(2)}) collective-permute-start(bf16[512,2048]{1,0:T(8,128)(2,1)S(1)} %bitcast.125), channel_id=1, source_target_pairs={{0,4},{4,0},{1,5},{5,1},{2,6},{6,2},{3,7},{7,3},{8,12},{12,8},{9,1... | collective-permute-start | bytes 6291464 | tf_op jit(solution)/shard_map/ppermute | solution.py:628
  314.6 58.4 %collective-permute-start.22 = (bf16[512,2048]{1,0:T(8,128)(2,1)}, bf16[512,2048]{1,0:T(8,128)(2,1)}, u32[]{:S(2)}, u32[]{:S(2)}) collective-permute-start(bf16[512,2048]{1,0:T(8,128)(2,1)} %collective-permute-done.16.mine_grads.refs_18_), channel_id=1, source_target_pairs={{0,4},{4,0},{1,5},{5,1},{2,6},{6,2},{3,7},{7,3},{8,12},{12,8},{9,1... | collective-permute-start | bytes 6291464 | tf_op jit(solution)/shard_map/ppermute | solution.py:628
  314.7 58.3 %collective-permute-start.23 = (bf16[512,2048]{1,0:T(8,128)(2,1)}, bf16[512,2048]{1,0:T(8,128)(2,1)}, u32[]{:S(2)}, u32[]{:S(2)}) collective-permute-start(bf16[512,2048]{1,0:T(8,128)(2,1)} %collective-permute-done.17.mine_grads.refs_20_), channel_id=1, source_target_pairs={{0,4},{4,0},{1,5},{5,1},{2,6},{6,2},{3,7},{7,3},{8,12},{12,8},{9,1... | collective-permute-start | bytes 6291464 | tf_op jit(solution)/shard_map/ppermute | solution.py:628
  315.2 31.5 %collective-permute-start.27 = (bf16[512,1024]{1,0:T(8,128)(2,1)S(1)}, bf16[512,1024]{1,0:T(8,128)(2,1)S(1)}, u32[]{:S(2)}, u32[]{:S(2)}) collective-permute-start(bf16[512,1024]{1,0:T(8,128)(2,1)S(1)} %pad_maximum_fusion.9.refs_1_.refs_0_), channel_id=1, source_target_pairs={{0,8},{8,0},{16,24},{24,16},{1,9},{9,1},{17,25},{25,17},{2,10},{10... | collective-permute-start | bytes 3145736 | tf_op jit(solution)/shard_map/ppermute | solution.py:628
  324.4 30.8 %collective-permute-start.28 = (bf16[512,1024]{1,0:T(8,128)(2,1)S(1)}, bf16[512,1024]{1,0:T(8,128)(2,1)S(1)}, u32[]{:S(2)}, u32[]{:S(2)}) collective-permute-start(bf16[512,1024]{1,0:T(8,128)(2,1)S(1)} %pad_maximum_fusion.9.refs_1_.refs_0_), channel_id=1, source_target_pairs={{0,16},{8,24},{16,0},{24,8},{1,17},{9,25},{17,1},{25,9},{2,18},{10... | collective-permute-start | bytes 3145736 | tf_op jit(solution)/shard_map/ppermute | solution.py:628
  356.1 16.9 %collective-permute-start.29 = (bf16[256,1024]{1,0:T(8,128)(2,1)}, bf16[256,1024]{1,0:T(8,128)(2,1)}, u32[]{:S(2)}, u32[]{:S(2)}) collective-permute-start(bf16[256,1024]{1,0:T(8,128)(2,1)} %slice.686), channel_id=1, source_target_pairs={{0,16},{8,24},{16,0},{24,8},{1,17},{9,25},{17,1},{25,9},{2,18},{10... | collective-permute-start | bytes 1572872 | tf_op jit(solution)/shard_map/ppermute | solution.py:628
  392.3 48.0 %collective-permute-start.34 = (bf16[512,2048]{1,0:T(8,128)(2,1)S(1)}, bf16[512,2048]{1,0:T(8,128)(2,1)}, u32[]{:S(2)}, u32[]{:S(2)}) collective-permute-start(bf16[512,2048]{1,0:T(8,128)(2,1)S(1)} %multiply_convert_fusion.mine.refs_8_), channel_id=1, source_target_pairs={{0,8},{8,0},{16,24},{24,16},{1,9},{9,1},{17,25},{25,17},{2,10},{10... | collective-permute-start | bytes 6291464 | tf_op jit(solution)/shard_map/ppermute | solution.py:628
  397.9 50.2 %collective-permute-start.38 = (bf16[512,2048]{1,0:T(8,128)(2,1)S(1)}, bf16[512,2048]{1,0:T(8,128)(2,1)}, u32[]{:S(2)}, u32[]{:S(2)}) collective-permute-start(bf16[512,2048]{1,0:T(8,128)(2,1)S(1)} %multiply_convert_fusion.mine.refs_8_), channel_id=1, source_target_pairs={{0,16},{8,24},{16,0},{24,8},{1,17},{9,25},{17,1},{25,9},{2,18},{10... | collective-permute-start | bytes 6291464 | tf_op jit(solution)/shard_map/ppermute | solution.py:628
  440.3 19.6 %collective-permute-start.35 = (bf16[512,2048]{1,0:T(8,128)(2,1)}, bf16[512,2048]{1,0:T(8,128)(2,1)}, u32[]{:S(2)}, u32[]{:S(2)}) collective-permute-start(bf16[512,2048]{1,0:T(8,128)(2,1)} %collective-permute-done.34.mine.refs_10_), channel_id=1, source_target_pairs={{0,4},{4,0},{1,5},{5,1},{2,6},{6,2},{3,7},{7,3},{8,12},{12,8},{9,1... | collective-permute-start | bytes 6291464 | tf_op jit(solution)/shard_map/ppermute | solution.py:628
  448.1 53.3 %collective-permute-start.41 = (bf16[512,2048]{1,0:T(8,128)(2,1)}, bf16[512,2048]{1,0:T(8,128)(2,1)}, u32[]{:S(2)}, u32[]{:S(2)}) collective-permute-start(bf16[512,2048]{1,0:T(8,128)(2,1)} %collective-permute-done.38.mine.refs_12_), channel_id=1, source_target_pairs={{0,4},{4,0},{1,5},{5,1},{2,6},{6,2},{3,7},{7,3},{8,12},{12,8},{9,1... | collective-permute-start | bytes 6291464 | tf_op jit(solution)/shard_map/ppermute | solution.py:628
  451.8 79.9 %collective-permute-start.45 = (bf16[256,2048]{1,0:T(8,128)(2,1)}, bf16[256,2048]{1,0:T(8,128)(2,1)}, u32[]{:S(2)}, u32[]{:S(2)}) collective-permute-start(bf16[256,2048]{1,0:T(8,128)(2,1)} %slice.691), channel_id=1, source_target_pairs={{0,16},{8,24},{16,0},{24,8},{1,17},{9,25},{17,1},{25,9},{2,18},{10... | collective-permute-start | bytes 3145736 | tf_op jit(solution)/shard_map/ppermute | solution.py:628
  453.6 79.4 %collective-permute-start.46 = (bf16[256,2048]{1,0:T(8,128)(2,1)S(1)}, bf16[256,2048]{1,0:T(8,128)(2,1)S(1)}, u32[]{:S(2)}, u32[]{:S(2)}) collective-permute-start(bf16[256,2048]{1,0:T(8,128)(2,1)S(1)} %slice.692), channel_id=1, source_target_pairs={{0,8},{8,0},{16,24},{24,16},{1,9},{9,1},{17,25},{25,17},{2,10},{10... | collective-permute-start | bytes 3145736 | tf_op jit(solution)/shard_map/ppermute | solution.py:628
  459.6 40.5 %collective-permute-start.39 = (bf16[256,2048]{1,0:T(8,128)(2,1)}, bf16[256,2048]{1,0:T(8,128)(2,1)S(1)}, u32[]{:S(2)}, u32[]{:S(2)}) collective-permute-start(bf16[256,2048]{1,0:T(8,128)(2,1)} %slice.689), channel_id=1, source_target_pairs={{0,16},{8,24},{16,0},{24,8},{1,17},{9,25},{17,1},{25,9},{2,18},{10... | collective-permute-start | bytes 3145736 | tf_op jit(solution)/shard_map/ppermute | solution.py:628
  459.9 41.6 %collective-permute-start.40 = (bf16[256,2048]{1,0:T(8,128)(2,1)}, bf16[256,2048]{1,0:T(8,128)(2,1)}, u32[]{:S(2)}, u32[]{:S(2)}) collective-permute-start(bf16[256,2048]{1,0:T(8,128)(2,1)} %slice.690), channel_id=1, source_target_pairs={{0,8},{8,0},{16,24},{24,16},{1,9},{9,1},{17,25},{25,17},{2,10},{10... | collective-permute-start | bytes 3145736 | tf_op jit(solution)/shard_map/ppermute | solution.py:628
  538.0 48.0 %collective-permute-start.43 = (bf16[512,2048]{1,0:T(8,128)(2,1)}, bf16[512,2048]{1,0:T(8,128)(2,1)S(1)}, u32[]{:S(2)}, u32[]{:S(2)}) collective-permute-start(bf16[512,2048]{1,0:T(8,128)(2,1)} %add_convert_fusion.5), channel_id=1, source_target_pairs={{0,16},{8,24},{16,0},{24,8},{1,17},{9,25},{17,1},{25,9},{2,18},{10... | collective-permute-start | bytes 6291464 | tf_op jit(solution)/shard_map/ppermute | solution.py:628
  543.7 48.0 %collective-permute-start.37 = (bf16[512,2048]{1,0:T(8,128)(2,1)}, bf16[512,2048]{1,0:T(8,128)(2,1)}, u32[]{:S(2)}, u32[]{:S(2)}) collective-permute-start(bf16[512,2048]{1,0:T(8,128)(2,1)} %add_convert_fusion.6), channel_id=1, source_target_pairs={{0,8},{8,0},{16,24},{24,16},{1,9},{9,1},{17,25},{25,17},{2,10},{10... | collective-permute-start | bytes 6291464 | tf_op jit(solution)/shard_map/ppermute | solution.py:628
  599.9 53.5 %collective-permute-start.49 = (bf16[512,2048]{1,0:T(8,128)(2,1)}, bf16[512,2048]{1,0:T(8,128)(2,1)}, u32[]{:S(2)}, u32[]{:S(2)}) collective-permute-start(bf16[512,2048]{1,0:T(8,128)(2,1)} %add_convert_fusion.4), channel_id=1, source_target_pairs={{0,24},{8,16},{16,8},{24,0},{1,25},{9,17},{17,9},{25,1},{2,26},{10... | collective-permute-start | bytes 6291464 | tf_op jit(solution)/shard_map/ppermute | solution.py:628
  653.5 374.2 %reduce-scatter.8.cloned.1.call-start = ((), (), s32[]{:S(2)}) async-start(), calls=%async_computation.9 | async-start | bytes 4456448 | tf_op jit(solution)/shard_map/reduce_scatter | solution.py:1018
  669.2 63.2 %collective-permute-start.55 = (bf16[512,2048]{1,0:T(8,128)(2,1)}, bf16[512,2048]{1,0:T(8,128)(2,1)}, u32[]{:S(2)}, u32[]{:S(2)}) collective-permute-start(bf16[512,2048]{1,0:T(8,128)(2,1)} %add_convert_fusion.2), channel_id=1, source_target_pairs={{0,16},{8,24},{16,0},{24,8},{1,17},{9,25},{17,1},{25,9},{2,18},{10... | collective-permute-start | bytes 6291464 | tf_op jit(solution)/shard_map/ppermute | solution.py:628
  670.8 61.5 %collective-permute-start.54 = (bf16[512,2048]{1,0:T(8,128)(2,1)}, bf16[512,2048]{1,0:T(8,128)(2,1)}, u32[]{:S(2)}, u32[]{:S(2)}) collective-permute-start(bf16[512,2048]{1,0:T(8,128)(2,1)} %add_convert_fusion.3), channel_id=1, source_target_pairs={{0,8},{8,0},{16,24},{24,16},{1,9},{9,1},{17,25},{25,17},{2,10},{10... | collective-permute-start | bytes 6291464 | tf_op jit(solution)/shard_map/ppermute | solution.py:628
  678.6 71.2 %collective-permute-start.56 = (bf16[512,2048]{1,0:T(8,128)(2,1)}, bf16[512,2048]{1,0:T(8,128)(2,1)}, u32[]{:S(2)}, u32[]{:S(2)}) collective-permute-start(bf16[512,2048]{1,0:T(8,128)(2,1)} %get-tuple-element.189), channel_id=1, source_target_pairs={{0,4},{4,0},{1,5},{5,1},{2,6},{6,2},{3,7},{7,3},{8,12},{12,8},{9,1... | collective-permute-start | bytes 6291464 | tf_op jit(solution)/shard_map/ppermute | solution.py:628
  700.6 29.2 %collective-permute-start.57 = (bf16[2,8,128,128]{3,2,1,0:T(8,128)(2,1)S(1)}, bf16[2,8,128,128]{3,2,1,0:T(8,128)(2,1)S(1)}, u32[]{:S(2)}, u32[]{:S(2)}) collective-permute-start(bf16[2,8,128,128]{3,2,1,0:T(8,128)(2,1)S(1)} %convert_element_type.355), channel_id=1, source_target_pairs={{8,0},{16,8},{24,16},{9,1},{17,9},{25,17},{10,2},{18,10},{26,18},{... | collective-permute-start | bytes 1572872 | tf_op jit(solution)/shard_map/ppermute | solution.py:639
  762.2 48.4 %collective-permute-start.60 = (bf16[512,2048]{1,0:T(8,128)(2,1)}, bf16[512,2048]{1,0:T(8,128)(2,1)}, u32[]{:S(2)}, u32[]{:S(2)}) collective-permute-start(bf16[512,2048]{1,0:T(8,128)(2,1)} %add_convert_fusion.1), channel_id=1, source_target_pairs={{0,24},{8,16},{16,8},{24,0},{1,25},{9,17},{17,9},{25,1},{2,26},{10... | collective-permute-start | bytes 6291464 | tf_op jit(solution)/shard_map/ppermute | solution.py:628
  768.5 48.1 %collective-permute-start.53 = (bf16[512,2048]{1,0:T(8,128)(2,1)}, bf16[512,2048]{1,0:T(8,128)(2,1)}, u32[]{:S(2)}, u32[]{:S(2)}) collective-permute-start(bf16[512,2048]{1,0:T(8,128)(2,1)} %get-tuple-element.184), channel_id=1, source_target_pairs={{0,4},{4,0},{1,5},{5,1},{2,6},{6,2},{3,7},{7,3},{8,12},{12,8},{9,1... | collective-permute-start | bytes 6291464 | tf_op jit(solution)/shard_map/ppermute | solution.py:628
  825.0 61.1 %collective-permute-start.67 = (bf16[512,1536]{1,0:T(8,128)(2,1)}, bf16[512,1536]{1,0:T(8,128)(2,1)}, u32[]{:S(2)}, u32[]{:S(2)}) collective-permute-start(bf16[512,1536]{1,0:T(8,128)(2,1)} %convolution_convert_fusion.3), channel_id=1, source_target_pairs={{0,16},{8,24},{16,0},{24,8},{1,17},{9,25},{17,1},{25,9},{2,18},{10... | collective-permute-start | bytes 4718600 | tf_op jit(solution)/shard_map/ppermute | solution.py:628
  828.3 63.3 %collective-permute-start.66 = (bf16[512,1536]{1,0:T(8,128)(2,1)}, bf16[512,1536]{1,0:T(8,128)(2,1)}, u32[]{:S(2)}, u32[]{:S(2)}) collective-permute-start(bf16[512,1536]{1,0:T(8,128)(2,1)} %convolution_convert_fusion.4), channel_id=1, source_target_pairs={{0,8},{8,0},{16,24},{24,16},{1,9},{9,1},{17,25},{25,17},{2,10},{10... | collective-permute-start | bytes 4718600 | tf_op jit(solution)/shard_map/ppermute | solution.py:628
  872.6 23.9 %collective-permute-start.63 = (f32[2,8,1536]{2,1,0:T(8,128)}, f32[2,8,1536]{2,1,0:T(8,128)S(1)}, u32[]{:S(2)}, u32[]{:S(2)}) collective-permute-start(f32[2,8,1536]{2,1,0:T(8,128)} %get-tuple-element.212), channel_id=1, source_target_pairs={{8,0},{16,8},{24,16},{9,1},{17,9},{25,17},{10,2},{18,10},{26,18},{... | collective-permute-start | bytes 294920 | tf_op jit(solution)/shard_map/ppermute | solution.py:639
  904.0 48.7 %collective-permute-start.65 = (bf16[512,1664]{1,0:T(8,128)(2,1)}, bf16[512,1664]{1,0:T(8,128)(2,1)}, u32[]{:S(2)}, u32[]{:S(2)}) collective-permute-start(bf16[512,1664]{1,0:T(8,128)(2,1)} %convolution_convert_fusion.1), channel_id=1, source_target_pairs={{0,16},{8,24},{16,0},{24,8},{1,17},{9,25},{17,1},{25,9},{2,18},{10... | collective-permute-start | bytes 5111816 | tf_op jit(solution)/shard_map/ppermute | solution.py:628
  904.0 48.7 %collective-permute-start.64 = (bf16[512,1664]{1,0:T(8,128)(2,1)}, bf16[512,1664]{1,0:T(8,128)(2,1)}, u32[]{:S(2)}, u32[]{:S(2)}) collective-permute-start(bf16[512,1664]{1,0:T(8,128)(2,1)} %convolution_convert_fusion.2), channel_id=1, source_target_pairs={{0,8},{8,0},{16,24},{24,16},{1,9},{9,1},{17,25},{25,17},{2,10},{10... | collective-permute-start | bytes 5111816 | tf_op jit(solution)/shard_map/ppermute | solution.py:628
  908.7 115.0 %collective-permute-start.81 = (bf16[256,1536]{1,0:T(8,128)(2,1)}, bf16[256,1536]{1,0:T(8,128)(2,1)}, u32[]{:S(2)}, u32[]{:S(2)}) collective-permute-start(bf16[256,1536]{1,0:T(8,128)(2,1)} %fusion.13), channel_id=1, source_target_pairs={{0,16},{8,24},{16,0},{24,8},{1,17},{9,25},{17,1},{25,9},{2,18},{10... | collective-permute-start | bytes 2359304 | tf_op jit(solution)/shard_map/ppermute | solution.py:628
  911.9 112.0 %collective-permute-start.80 = (bf16[256,1536]{1,0:T(8,128)(2,1)}, bf16[256,1536]{1,0:T(8,128)(2,1)}, u32[]{:S(2)}, u32[]{:S(2)}) collective-permute-start(bf16[256,1536]{1,0:T(8,128)(2,1)} %fusion.12), channel_id=1, source_target_pairs={{0,8},{8,0},{16,24},{24,16},{1,9},{9,1},{17,25},{25,17},{2,10},{10... | collective-permute-start | bytes 2359304 | tf_op jit(solution)/shard_map/ppermute | solution.py:628
  958.0 28.3 %collective-permute-start.69 = (bf16[256,1664]{1,0:T(8,128)(2,1)}, bf16[256,1664]{1,0:T(8,128)(2,1)S(1)}, u32[]{:S(2)}, u32[]{:S(2)}) collective-permute-start(bf16[256,1664]{1,0:T(8,128)(2,1)} %fusion.15), channel_id=1, source_target_pairs={{0,16},{8,24},{16,0},{24,8},{1,17},{9,25},{17,1},{25,9},{2,18},{10... | collective-permute-start | bytes 2555912 | tf_op jit(solution)/shard_map/ppermute | solution.py:628
  964.5 21.8 %collective-permute-start.68 = (bf16[256,1664]{1,0:T(8,128)(2,1)}, bf16[256,1664]{1,0:T(8,128)(2,1)}, u32[]{:S(2)}, u32[]{:S(2)}) collective-permute-start(bf16[256,1664]{1,0:T(8,128)(2,1)} %fusion.16), channel_id=1, source_target_pairs={{0,8},{8,0},{16,24},{24,16},{1,9},{9,1},{17,25},{25,17},{2,10},{10... | collective-permute-start | bytes 2555912 | tf_op jit(solution)/shard_map/ppermute | solution.py:628
  997.7 42.5 %all-to-all-start.1 = ((bf16[4,2112,128]{2,1,0:T(8,128)(2,1)}), bf16[4,2112,128]{2,1,0:T(8,128)(2,1)}, u32[]{:S(2)}, u32[]{:S(2)}) async-start(bf16[4,2112,128]{2,1,0:T(8,128)(2,1)} %bitcast.140), calls=%async_computation.4 | async-start | bytes 4325376 | tf_op jit(solution)/shard_map/all_to_all | solution.py:1083
  1002.1 78.1 %reduce-scatter.6.cloned.1.call-start = ((), (), s32[]{:S(2)}) async-start(), calls=%async_computation.8 | async-start | bytes 1966080 | tf_op jit(solution)/shard_map/reduce_scatter | solution.py:1072
  1017.6 71.5 %collective-permute-start.77 = (bf16[128,1664]{1,0:T(8,128)(2,1)}, bf16[128,1664]{1,0:T(8,128)(2,1)}, u32[]{:S(2)}, u32[]{:S(2)}) collective-permute-start(bf16[128,1664]{1,0:T(8,128)(2,1)} %get-tuple-element.342), channel_id=1, source_target_pairs={{0,1},{1,2},{2,3},{3,0},{4,5},{5,6},{6,7},{7,4},{8,9},{9,10},{10,1... | collective-permute-start | bytes 1277960 | tf_op jit(solution)/shard_map/ppermute | solution.py:633
  1017.6 71.5 %collective-permute-start.78 = (bf16[128,1664]{1,0:T(8,128)(2,1)}, bf16[128,1664]{1,0:T(8,128)(2,1)}, u32[]{:S(2)}, u32[]{:S(2)}) collective-permute-start(bf16[128,1664]{1,0:T(8,128)(2,1)} %get-tuple-element.341), channel_id=1, source_target_pairs={{0,2},{1,3},{2,0},{3,1},{4,6},{5,7},{6,4},{7,5},{8,10},{9,11},{10,... | collective-permute-start | bytes 1277960 | tf_op jit(solution)/shard_map/ppermute | solution.py:633
  1023.7 65.4 %collective-permute-start.79 = (bf16[128,1664]{1,0:T(8,128)(2,1)}, bf16[128,1664]{1,0:T(8,128)(2,1)}, u32[]{:S(2)}, u32[]{:S(2)}) collective-permute-start(bf16[128,1664]{1,0:T(8,128)(2,1)} %get-tuple-element.340), channel_id=1, source_target_pairs={{0,3},{1,0},{2,1},{3,2},{4,7},{5,4},{6,5},{7,6},{8,11},{9,8},{10,9... | collective-permute-start | bytes 1277960 | tf_op jit(solution)/shard_map/ppermute | solution.py:633
  1042.8 27.2 %collective-permute-start.75 = (f32[16640]{0:T(1024)S(1)}, f32[16640]{0:T(1024)S(1)}, u32[]{:S(2)}, u32[]{:S(2)}) collective-permute-start(f32[16640]{0:T(1024)S(1)} %add.322), channel_id=1, source_target_pairs={{0,1},{1,0},{2,3},{3,2},{4,5},{5,4},{6,7},{7,6},{8,9},{9,8},{10,11... | collective-permute-start | bytes 199688 | tf_op jit(solution)/shard_map/ppermute | solution.py:628
  1070.0 19.0 %collective-permute-start.76 = (f32[16640]{0:T(1024)S(1)}, f32[16640]{0:T(1024)S(1)}, u32[]{:S(2)}, u32[]{:S(2)}) collective-permute-start(f32[16640]{0:T(1024)S(1)} %add.323), channel_id=1, source_target_pairs={{0,2},{1,3},{2,0},{3,1},{4,6},{5,7},{6,4},{7,5},{8,10},{9,11},{10,... | collective-permute-start | bytes 199688 | tf_op jit(solution)/shard_map/ppermute | solution.py:628
  (112 other events, 1039.5 us)
Sparse Core Ops, SparseCore 0:
  121.5 113.1 all-gather.2
  236.3 74.8 all-gather.4
  653.6 151.4 reduce-scatter.3
  824.4 100.6 reduce-scatter.7
  1027.8 52.4 reduce-scatter.5

commit v12 on v11

--- a/solution.py
+++ b/solution.py
@@ -1069,9 +1069,18 @@
     last_line = Line(scatter.own())
     for p in range(1, parts):
         own = low(earlier_scatter.own(*last_line.sent))
-        mix_grads[p] = wide(lax.psum_scatter(own, "fsdp", scatter_dimension=0, tiled=True))
-    sums = butterfly(tie(sums, input_grad, *last_line.sent), ("ctx", "fsdp"))
+        mix_grads[p] = lax.psum_scatter(own, "fsdp", scatter_dimension=0, tiled=True)
+    sums = butterfly(tie(sums, input_grad, *last_line.sent), ("ctx",))
     mix_grads[0] = last_line.total(sums)
+    count = lax.axis_size("fsdp")
+    bit = 1
+    while bit < count // 2:
+        sums = sums + flip(sums, "fsdp", bit)
+        bit *= 2
+    for p in range(1, parts):
+        mix_grads[p] = wide(tie(mix_grads[p], sums))
+    if count > 1:
+        sums = sums + flip(sums, "fsdp", bit)
     query_grad, key_grad, value_grad = by_kind([grad[:, :part_cols] for grad in mix_grads])
     beta_grad = mix_grads[0][:, part_cols : part_cols + heads_here]
     ends = [width, 2 * width, 2 * width + LANES, sums.shape[0] - LANES]

time: 1120 us -> 1120 us (level)
  starting transfers between devices: 129 us -> 148 us
    ppermute x60, starting transfers between devices: 55.8 us -> 74.8 us  [flip(): return lax.ppermute(value, axis, [(i, i ^ bit) for i in devices])]
    ppermute x12, waiting for transfers between devices: 33.1 us -> 52 us  [shift(): lax.ppermute(value, axis, [(i, (i + distance) % count) for i in range(cou...]
    ppermute x60, waiting for transfers between devices: 206 us -> 193 us  [flip(): return lax.ppermute(value, axis, [(i, i ^ bit) for i in devices])]
    unnamed x224 -> x210, local copies, waits for them, and re-layouts: 35.7 us -> 26.2 us
  transfers between devices with their start and end apart: 89 -> 89, of which waited for: 38 -> 37; matrix products, arithmetic and copies ran while one was open for 20% -> 19% of each run, Pallas kernels for 35% -> 35%
where the time goes in v12:
time: 1120 us; the launch traced here: 1110 us
  Pallas kernels  394 us (35%)
  waiting for transfers between devices  317 us (28%)
  starting transfers between devices  148 us (13%)
  other arithmetic  111 us (10%)
  local copies, waits for them, and re-layouts  83 us (7%)
  matrix products  42.6 us (4%)
  between operations  15.6 us (1%)
    ppermute x60, waiting for transfers between devices, flip(): return lax.ppermute(value, axis, [(i, i ^ bit) for i in devices])  193 us
    pallas_call x4, Pallas kernels, ffn_both(): pl.pallas_call(ffn_kernel, grid=(count // tile,), in_specs=[wide_rows] *...  118 us
    ppermute x60, starting transfers between devices, flip(): return lax.ppermute(value, axis, [(i, i ^ bit) for i in devices])  74.8 us
    ppermute x10, waiting for transfers between devices, from_behind(): return lax.ppermute(block, axis, route)  72 us
    pallas_call x2, Pallas kernels, mixer_backward(): pl.pallas_call(functools.partial(backward_kernel, taps, group, first), gr...  66.4 us
    pallas_call x2, Pallas kernels, mixer_forward(): pl.pallas_call(functools.partial(forward_kernel, taps, group, first), gri...  55.1 us
    ppermute x12, waiting for transfers between devices, shift(): lax.ppermute(value, axis, [(i, (i + distance) % count) for i in range(cou...  52 us
    pallas_call x1, Pallas kernels, ffn_weights(): pl.pallas_call(functools.partial(ffn_weights_kernel, count, lines), grid=...  48.1 us
  transfers between devices with their start and end apart: 89, of which 37 were waited for; matrix products, arithmetic and copies ran while one was open for 19% of the time, Pallas kernels for 35%

profile of v12, /device:TPU:0, one launch (start us, length us, event | category | flops | bytes accessed | tf_op | source)
XLA Modules:
  0.0 1109.6 jit_solution(4347494941081212526)
XLA Ops:
  12.6 5.3 all-to-all-start
  27.8 9.3 collective-permute-done
  37.1 17.1 %collective-permute-done.1 = bf16[128,1664]{1,0:T(8,128)(2,1)S(1)} collective-permute-done((bf16[128,1664]{1,0:T(8,128)(2,1)}, bf16[128,1664]{1,0:T(8,128)(2,1)S(1)}, u32[]{:S(2)}, u32[]{:S(2)}) %collective-permute-start.1) | collective-permute-done | bytes 426016 | tf_op jit(solution)/shard_map/ppermute | solution.py:633
  63.1 10.7 collective-permute-start.10
  77.4 18.7 %collective-permute-done.3.refs_1_.refs_3_ = bf16[512,1664]{1,0:T(8,128)(2,1)S(1)} collective-permute-done((bf16[512,1664]{1,0:T(8,128)(2,1)}, bf16[512,1664]{1,0:T(8,128)(2,1)S(1)}, u32[]{:S(2)}, u32[]{:S(2)}) %collective-permute-start.3) | collective-permute-done | bytes 1703968 | tf_op jit(solution)/shard_map/ppermute | solution.py:628
  101.3 6.6 collective-permute-done.9
  112.4 5.9 collective-permute-done.5.refs_3_.refs_5_
  121.4 6.6 convert_element_type.398
  131.5 4.7 shard_map.271
  140.8 12.8 %shard_map.272.pre.beta = f32[1024,1664]{1,0:T(8,128)} custom-call(s32[1]{0:T(128)} %bitcast.1.place, bf16[1024,2048]{1,0:T(8,128)(2,1)} %fusion.1.rows, bf16[512,1664]{1,0:T(8,128)(2,1)} %pad_maximum_fusion.6.refs_0_.refs_2_, bf16[512,1664]{1,0:T(8,128)(2,1)} %copy-done.29, bf16[512,1664]{1,0:T(8,128)(2,1)} %copy-done.30, bf16[256,1664]{1,0:T(8,128)(2,1)} %copy-done.44, ...), custom_call_target="tpu_custom_call" | custom-call | flops 6979321856 | bytes 11010048 | tf_op jit(solution)/shard_map/pallas_call | solution.py:551
  155.6 27.5 %shard_map.273 = (f32[1024,512]{1,0:T(8,128)}, bf16[1024,512]{1,0:T(8,128)(2,1)}, f32[2,4,128,256]{3,2,1,0:T(8,128)}, bf16[2,4,4,128,128]{4,3,2,1,0:T(8,128)(2,1...) custom-call(f32[1024,1664]{1,0:T(8,128)} %shard_map.272.pre.beta, ...), custom_call_target="tpu_custom_call" | custom-call | flops 4026531840 | bytes 20971520 | tf_op jit(solution)/shard_map/pallas_call | solution.py:160
  183.1 4.8 collective-permute-done.11.refs_1_.refs_8_
  194.3 13.6 %collective-permute-done.13.refs_3_.refs_10_ = bf16[256,1536]{1,0:T(8,128)(2,1)S(1)} collective-permute-done((bf16[256,1536]{1,0:T(8,128)(2,1)}, bf16[256,1536]{1,0:T(8,128)(2,1)S(1)}, u32[]{:S(2)}, u32[]{:S(2)}) %collective-permute-start.13) | collective-permute-done | bytes 786464 | tf_op jit(solution)/shard_map/ppermute | solution.py:628
  218.2 4.4 shard_map.274
  226.5 11.5 %shard_map.275.pre = f32[1024,1536]{1,0:T(8,128)} custom-call(s32[1]{0:T(128)} %bitcast.1.place, bf16[1024,2048]{1,0:T(8,128)(2,1)} %fusion.1.rows, bf16[512,1536]{1,0:T(8,128)(2,1)} %pad_maximum_fusion.7.refs_0_.refs_7_, bf16[512,1536]{1,0:T(8,128)(2,1)} %copy-done.31, bf16[512,1536]{1,0:T(8,128)(2,1)} %collective-permute-done.12.refs_2_.refs_9_, ...), custom_call_target="tpu_custom_call" | custom-call | flops 6442450944 | bytes 10485760 | tf_op jit(solution)/shard_map/pallas_call | solution.py:551
  238.0 10.2 collective-permute-start.24
  248.2 4.3 collective-permute-done.15
  252.4 5.3 collective-permute-start.26
  258.4 27.5 %shard_map.276 = (f32[1024,512]{1,0:T(8,128)}, bf16[1024,512]{1,0:T(8,128)(2,1)}, f32[2,4,128,256]{3,2,1,0:T(8,128)}, bf16[2,4,4,128,128]{4,3,2,1,0:T(8,128)(2,1...) custom-call(f32[1024,1536]{1,0:T(8,128)} %shard_map.275.pre, ...), custom_call_target="tpu_custom_call" | custom-call | flops 4026531840 | bytes 20971520 | tf_op jit(solution)/shard_map/pallas_call | solution.py:160
  289.5 8.1 shard_map.277.gate_w.up_w
  297.8 4.6 collective-permute-start.18
  303.7 6.1 collective-permute-done.18
  310.2 4.4 collective-permute-start.19
  317.7 6.7 collective-permute-done.19
  324.5 6.7 collective-permute-start.28
  331.5 15.2 %collective-permute-done.27.refs_2_.refs_1_ = bf16[512,1024]{1,0:T(8,128)(2,1)S(1)} collective-permute-done((bf16[512,1024]{1,0:T(8,128)(2,1)S(1)}, bf16[512,1024]{1,0:T(8,128)(2,1)S(1)}, u32[]{:S(2)}, u32[]{:S(2)}) %collective-permute-start.27) | collective-permute-done | bytes 1048608 | tf_op jit(solution)/shard_map/ppermute | solution.py:628
  349.0 6.3 collective-permute-done.28.refs_3_.refs_2_
  361.1 4.5 shard_map.278
  365.6 4.6 shard_map.279
  373.0 8.7 shard_map.280
  393.5 4.4 shard_map.281.down_w
  402.1 29.4 %shard_map.282 = (bf16[3,512,704]{2,1,0:T(8,128)(2,1)}, bf16[512,2048]{1,0:T(8,128)(2,1)}, bf16[512,2048]{1,0:T(8,128)(2,1)}, bf16[3,512,704]{2,1,0:T(8,128)(2,1...) custom-call(bf16[512,2048]{1,0:T(8,128)(2,1)} %copy-done.34, ...), custom_call_target="tpu_custom_call" | custom-call | flops 17716740096 | bytes 25427968 | tf_op jit(solution)/shard_map/pallas_call | solution.py:469
  431.5 8.8 collective-permute-done.34.mine.refs_10_
  440.3 7.8 collective-permute-done.38.mine.refs_12_
  460.5 29.6 %shard_map.283 = (bf16[3,512,704]{2,1,0:T(8,128)(2,1)}, bf16[512,2048]{1,0:T(8,128)(2,1)}, bf16[512,2048]{1,0:T(8,128)(2,1)}, bf16[3,512,704]{2,1,0:T(8,128)(2,1...) custom-call(bf16[512,2048]{1,0:T(8,128)(2,1)} %collective-permute-done.34.mine.refs_10_, ...), custom_call_target="tpu_custom_call" | custom-call | flops 17716740096 | bytes 25427968 | tf_op jit(solution)/shard_map/pallas_call | solution.py:469
  490.1 10.0 collective-permute-done.39
  501.5 29.7 %shard_map.284 = (bf16[3,512,704]{2,1,0:T(8,128)(2,1)}, bf16[512,2048]{1,0:T(8,128)(2,1)}, bf16[512,2048]{1,0:T(8,128)(2,1)}, bf16[3,512,704]{2,1,0:T(8,128)(2,1...) custom-call(bf16[512,2048]{1,0:T(8,128)(2,1)} %collective-permute-done.38.mine.refs_12_, ...), custom_call_target="tpu_custom_call" | custom-call | flops 17716740096 | bytes 25427968 | tf_op jit(solution)/shard_map/pallas_call | solution.py:469
  546.3 29.5 %shard_map.285 = (bf16[3,512,704]{2,1,0:T(8,128)(2,1)}, bf16[512,2048]{1,0:T(8,128)(2,1)}, bf16[512,2048]{1,0:T(8,128)(2,1)}, bf16[3,512,704]{2,1,0:T(8,128)(2,1...) custom-call(bf16[512,2048]{1,0:T(8,128)(2,1)} %copy-done.51, ...), custom_call_target="tpu_custom_call" | custom-call | flops 17716740096 | bytes 25427968 | tf_op jit(solution)/shard_map/pallas_call | solution.py:469
  575.9 10.1 collective-permute-done.43
  586.0 5.7 collective-permute-done.37
  605.3 48.1 %shard_map.286 = bf16[4,3,704,512]{3,2,1,0:T(8,128)(2,1)} custom-call(bf16[3,512,704]{2,1,0:T(8,128)(2,1)} %get-tuple-element.177.refs_0_, bf16[3,512,704]{2,1,0:T(8,128)(2,1)} %get-tuple-element.178.refs_1_, bf16[3,512,704]{2,1,0:T(8,128)(2,1)} %get-tuple-element.159.refs_2_, bf16[3,512,704]{2,1,0:T(8,128)(2,1)} %get-tuple-element.179.refs_3_, ...), custom_call_target="tpu_custom_call" | custom-call | flops 35433480192 | bytes 67108864 | tf_op jit(solution)/shard_map/pallas_call | solution.py:516
  659.2 7.0 multiply_reduce_fusion.1
  678.8 9.0 shard_map.287.grad
  687.7 5.7 shard_map.289
  693.5 5.8 shard_map.288
  701.9 27.9 %collective-permute-done.57 = bf16[2,8,128,128]{3,2,1,0:T(8,128)(2,1)S(1)} collective-permute-done((bf16[2,8,128,128]{3,2,1,0:T(8,128)(2,1)S(1)}, bf16[2,8,128,128]{3,2,1,0:T(8,128)(2,1)S(1)}, u32[]{:S(2)}, u32[]{:S(2)}) %collective-permute-start.57) | collective-permute-done | bytes 524320 | tf_op jit(solution)/shard_map/ppermute | solution.py:639
  732.4 14.0 %collective-permute-done.58 = bf16[2,8,128,128]{3,2,1,0:T(8,128)(2,1)} collective-permute-done((bf16[2,8,128,128]{3,2,1,0:T(8,128)(2,1)}, bf16[2,8,128,128]{3,2,1,0:T(8,128)(2,1)}, u32[]{:S(2)}, u32[]{:S(2)}) %collective-permute-start.58) | collective-permute-done | bytes 524320 | tf_op jit(solution)/shard_map/ppermute | solution.py:639
  753.8 8.5 collective-permute-done.59
  762.3 6.3 convolution_convert_fusion
  769.6 33.1 %shard_map.290 = (bf16[1024,1536]{1,0:T(8,128)(2,1)}, f32[2,8,1536]{2,1,0:T(8,128)}, f32[2,8,1536]{2,1,0:T(8,128)}, f32[2,8,1536]{2,1,0:T(8,128)}, f32[1024,128]{1,0:T(8,128)}) custom-call(f32[1024,1536]{1,0:T(8,128)} %shard_map.275.pre, f32[1024,1664]{1,0:T(8,128)} %shard_map.272.pre.beta, f32[1,128]{1,0:T(1,128)} %pad_bitcast_fusion.bias, ...), custom_call_target="tpu_custom_call" | custom-call | flops 4026531840 | bytes 20971520 | tf_op jit(solution)/shard_map/pallas_call | solution.py:318
  806.2 4.4 collective-permute-done.61
  816.7 7.4 add_convert_fusion
  828.3 5.7 fusion.24
  839.2 33.3 %shard_map.291 = (bf16[1024,1536]{1,0:T(8,128)(2,1)}, f32[2,8,1536]{2,1,0:T(8,128)}, f32[2,8,1536]{2,1,0:T(8,128)}, f32[2,8,1536]{2,1,0:T(8,128)}, f32[1024,128]{1,0:T(8,128)}) custom-call(f32[1024,1664]{1,0:T(8,128)} %shard_map.272.pre.beta, f32[1024,1664]{1,0:T(8,128)} %shard_map.272.pre.beta, f32[1,128]{1,0:T(1,128)} %pad_bitcast_fusion.bias, ...), custom_call_target="tpu_custom_call" | custom-call | flops 4026531840 | bytes 20971520 | tf_op jit(solution)/shard_map/pallas_call | solution.py:318
  874.1 12.0 %collective-permute-done.67 = bf16[512,1536]{1,0:T(8,128)(2,1)} collective-permute-done((bf16[512,1536]{1,0:T(8,128)(2,1)}, bf16[512,1536]{1,0:T(8,128)(2,1)}, u32[]{:S(2)}, u32[]{:S(2)}) %collective-permute-start.67) | collective-permute-done | bytes 1572896 | tf_op jit(solution)/shard_map/ppermute | solution.py:628
  886.1 5.5 collective-permute-done.66
  907.6 4.5 convolution_convert_fusion.1
  922.6 42.0 %collective-permute-done.65 = bf16[512,1664]{1,0:T(8,128)(2,1)S(1)} collective-permute-done((bf16[512,1664]{1,0:T(8,128)(2,1)S(1)}, bf16[512,1664]{1,0:T(8,128)(2,1)S(1)}, u32[]{:S(2)}, u32[]{:S(2)}) %collective-permute-start.65) | collective-permute-done | bytes 1703968 | tf_op jit(solution)/shard_map/ppermute | solution.py:628
  972.5 21.6 %shard_map.292 = bf16[1024,2048]{1,0:T(8,128)(2,1)} custom-call(s32[1]{0:T(128)} %bitcast.1.place, bf16[1024,1664]{1,0:T(8,128)(2,1)} %pad_maximum_fusion.3.refs_0_, bf16[1024,1536]{1,0:T(8,128)(2,1)} %bitcast.132, bf16[512,1664]{1,0:T(8,128)(2,1)} %pad_maximum_fusion.6.refs_0_.refs_2_, bf16[512,1664]{1,0:T(8,128)(2,1)} %copy-done.29, ...), custom_call_target="tpu_custom_call" | custom-call | flops 13421772800 | bytes 17301504 | tf_op jit(solution)/shard_map/pallas_call | solution.py:587
  997.4 4.8 reshape.209
  1005.5 4.4 all-to-all-start.1
  1028.1 5.6 collective-permute-start.78
  1058.3 19.0 %collective-permute-done.78 = bf16[128,1664]{1,0:T(8,128)(2,1)} collective-permute-done((bf16[128,1664]{1,0:T(8,128)(2,1)}, bf16[128,1664]{1,0:T(8,128)(2,1)}, u32[]{:S(2)}, u32[]{:S(2)}) %collective-permute-start.78) | collective-permute-done | bytes 426016 | tf_op jit(solution)/shard_map/ppermute | solution.py:633
  1079.7 18.5 %collective-permute-start.76 = (f32[16640]{0:T(1024)S(1)}, f32[16640]{0:T(1024)S(1)}, u32[]{:S(2)}, u32[]{:S(2)}) collective-permute-start(f32[16640]{0:T(1024)S(1)} %add.323), channel_id=1, source_target_pairs={{0,2},{1,3},{2,0},{3,1},{4,6},{5,7},{6,4},{7,5},{8,10},{9,11},{10,... | collective-permute-start | bytes 199688 | tf_op jit(solution)/shard_map/ppermute | solution.py:628
  (497 shorter events, 292.2 us)
Async XLA Ops:
  12.6 44.3 %all-to-all-start = ((bf16[4,2112,128]{2,1,0:T(8,128)(2,1)}), bf16[4,2112,128]{2,1,0:T(8,128)(2,1)S(1)}, u32[]{:S(2)}, u32[]{:S(2)}) async-start(bf16[4,2112,128]{2,1,0:T(8,128)(2,1)} %bitcast.139), calls=%async_computation | async-start | bytes 4325376 | tf_op jit(solution)/shard_map/all_to_all | solution.py:894
  17.8 271.7 %all-gather.3.cloned.1.call-start = ((), (), s32[]{:S(2)}) async-start(), calls=%async_computation.5 | async-start | bytes 7208960 | tf_op jit(solution)/shard_map/all_gather | solution.py:912
  23.8 30.4 %collective-permute-start.1 = (bf16[128,1664]{1,0:T(8,128)(2,1)}, bf16[128,1664]{1,0:T(8,128)(2,1)S(1)}, u32[]{:S(2)}, u32[]{:S(2)}) collective-permute-start(bf16[128,1664]{1,0:T(8,128)(2,1)} %constant_dynamic-update-slice_fusion), channel_id=1, source_target_pairs={{0,2},{1,3},{2,0},{3,1},{4,6},{5,7},{6,4},{7,5},{8,10},{9,11},{10,... | collective-permute-start | bytes 1277960 | tf_op jit(solution)/shard_map/ppermute | solution.py:633
  26.4 27.8 %collective-permute-start.2 = (bf16[128,1664]{1,0:T(8,128)(2,1)}, bf16[128,1664]{1,0:T(8,128)(2,1)S(1)}, u32[]{:S(2)}, u32[]{:S(2)}) collective-permute-start(bf16[128,1664]{1,0:T(8,128)(2,1)} %constant_dynamic-update-slice_fusion), channel_id=1, source_target_pairs={{0,3},{1,0},{2,1},{3,2},{4,7},{5,4},{6,5},{7,6},{8,11},{9,8},{10,9... | collective-permute-start | bytes 1277960 | tf_op jit(solution)/shard_map/ppermute | solution.py:633
  56.9 39.2 %collective-permute-start.3 = (bf16[512,1664]{1,0:T(8,128)(2,1)}, bf16[512,1664]{1,0:T(8,128)(2,1)S(1)}, u32[]{:S(2)}, u32[]{:S(2)}) collective-permute-start(bf16[512,1664]{1,0:T(8,128)(2,1)} %pad_maximum_fusion.6.refs_0_.refs_2_), channel_id=1, source_target_pairs={{0,8},{8,0},{16,24},{24,16},{1,9},{9,1},{17,25},{25,17},{2,10},{10... | collective-permute-start | bytes 5111816 | tf_op jit(solution)/shard_map/ppermute | solution.py:628
  58.5 39.0 %collective-permute-start.4 = (bf16[512,1664]{1,0:T(8,128)(2,1)}, bf16[512,1664]{1,0:T(8,128)(2,1)S(1)}, u32[]{:S(2)}, u32[]{:S(2)}) collective-permute-start(bf16[512,1664]{1,0:T(8,128)(2,1)} %pad_maximum_fusion.6.refs_0_.refs_2_), channel_id=1, source_target_pairs={{0,16},{8,24},{16,0},{24,8},{1,17},{9,25},{17,1},{25,9},{2,18},{10... | collective-permute-start | bytes 5111816 | tf_op jit(solution)/shard_map/ppermute | solution.py:628
  63.1 38.2 %collective-permute-start.10 = (bf16[128,1536]{1,0:T(8,128)(2,1)S(1)}, bf16[128,1536]{1,0:T(8,128)(2,1)S(1)}, u32[]{:S(2)}, u32[]{:S(2)}) collective-permute-start(bf16[128,1536]{1,0:T(8,128)(2,1)S(1)} %copy-done.57), channel_id=1, source_target_pairs={{0,3},{1,0},{2,1},{3,2},{4,7},{5,4},{6,5},{7,6},{8,11},{9,8},{10,9... | collective-permute-start | bytes 1179656 | tf_op jit(solution)/shard_map/ppermute | solution.py:633
  73.8 27.6 %collective-permute-start.8 = (bf16[128,1536]{1,0:T(8,128)(2,1)S(1)}, bf16[128,1536]{1,0:T(8,128)(2,1)S(1)}, u32[]{:S(2)}, u32[]{:S(2)}) collective-permute-start(bf16[128,1536]{1,0:T(8,128)(2,1)S(1)} %copy-done.57), channel_id=1, source_target_pairs={{0,1},{1,2},{2,3},{3,0},{4,5},{5,6},{6,7},{7,4},{8,9},{9,10},{10,1... | collective-permute-start | bytes 1179656 | tf_op jit(solution)/shard_map/ppermute | solution.py:633
  73.8 34.2 %collective-permute-start.9 = (bf16[128,1536]{1,0:T(8,128)(2,1)S(1)}, bf16[128,1536]{1,0:T(8,128)(2,1)S(1)}, u32[]{:S(2)}, u32[]{:S(2)}) collective-permute-start(bf16[128,1536]{1,0:T(8,128)(2,1)S(1)} %copy-done.57), channel_id=1, source_target_pairs={{0,2},{1,3},{2,0},{3,1},{4,6},{5,7},{6,4},{7,5},{8,10},{9,11},{10,... | collective-permute-start | bytes 1179656 | tf_op jit(solution)/shard_map/ppermute | solution.py:633
  98.5 19.8 %collective-permute-start.5 = (bf16[256,1664]{1,0:T(8,128)(2,1)}, bf16[256,1664]{1,0:T(8,128)(2,1)S(1)}, u32[]{:S(2)}, u32[]{:S(2)}) collective-permute-start(bf16[256,1664]{1,0:T(8,128)(2,1)} %slice.640), channel_id=1, source_target_pairs={{0,16},{8,24},{16,0},{24,8},{1,17},{9,25},{17,1},{25,9},{2,18},{10... | collective-permute-start | bytes 2555912 | tf_op jit(solution)/shard_map/ppermute | solution.py:628
  100.0 19.8 %collective-permute-start.6 = (bf16[256,1664]{1,0:T(8,128)(2,1)}, bf16[256,1664]{1,0:T(8,128)(2,1)}, u32[]{:S(2)}, u32[]{:S(2)}) collective-permute-start(bf16[256,1664]{1,0:T(8,128)(2,1)} %slice.641), channel_id=1, source_target_pairs={{0,8},{8,0},{16,24},{24,16},{1,9},{9,1},{17,25},{25,17},{2,10},{10... | collective-permute-start | bytes 2555912 | tf_op jit(solution)/shard_map/ppermute | solution.py:628
  121.4 260.3 %all-gather.5.cloned.1.call-start = ((), (), s32[]{:S(2)}) async-start(), calls=%async_computation.6 | async-start | bytes 3604480 | tf_op jit(solution)/shard_map/all_gather | solution.py:913
  153.7 34.2 %collective-permute-start.11 = (bf16[512,1536]{1,0:T(8,128)(2,1)S(1)}, bf16[512,1536]{1,0:T(8,128)(2,1)S(1)}, u32[]{:S(2)}, u32[]{:S(2)}) collective-permute-start(bf16[512,1536]{1,0:T(8,128)(2,1)S(1)} %copy-done.24), channel_id=1, source_target_pairs={{0,8},{8,0},{16,24},{24,16},{1,9},{9,1},{17,25},{25,17},{2,10},{10... | collective-permute-start | bytes 4718600 | tf_op jit(solution)/shard_map/ppermute | solution.py:628
  154.1 34.8 %collective-permute-start.12 = (bf16[512,1536]{1,0:T(8,128)(2,1)S(1)}, bf16[512,1536]{1,0:T(8,128)(2,1)}, u32[]{:S(2)}, u32[]{:S(2)}) collective-permute-start(bf16[512,1536]{1,0:T(8,128)(2,1)S(1)} %copy-done.24), channel_id=1, source_target_pairs={{0,16},{8,24},{16,0},{24,8},{1,17},{9,25},{17,1},{25,9},{2,18},{10... | collective-permute-start | bytes 4718600 | tf_op jit(solution)/shard_map/ppermute | solution.py:628
  191.0 16.9 %collective-permute-start.13 = (bf16[256,1536]{1,0:T(8,128)(2,1)}, bf16[256,1536]{1,0:T(8,128)(2,1)S(1)}, u32[]{:S(2)}, u32[]{:S(2)}) collective-permute-start(bf16[256,1536]{1,0:T(8,128)(2,1)} %slice.667), channel_id=1, source_target_pairs={{0,16},{8,24},{16,0},{24,8},{1,17},{9,25},{17,1},{25,9},{2,18},{10... | collective-permute-start | bytes 2359304 | tf_op jit(solution)/shard_map/ppermute | solution.py:628
  191.8 17.9 %collective-permute-start.14 = (bf16[256,1536]{1,0:T(8,128)(2,1)}, bf16[256,1536]{1,0:T(8,128)(2,1)}, u32[]{:S(2)}, u32[]{:S(2)}) collective-permute-start(bf16[256,1536]{1,0:T(8,128)(2,1)} %slice.668), channel_id=1, source_target_pairs={{0,8},{8,0},{16,24},{24,16},{1,9},{9,1},{17,25},{25,17},{2,10},{10... | collective-permute-start | bytes 2359304 | tf_op jit(solution)/shard_map/ppermute | solution.py:628
  209.7 88.0 %collective-permute-start.16 = (bf16[512,2048]{1,0:T(8,128)(2,1)S(1)}, bf16[512,2048]{1,0:T(8,128)(2,1)}, u32[]{:S(2)}, u32[]{:S(2)}) collective-permute-start(bf16[512,2048]{1,0:T(8,128)(2,1)S(1)} %bitcast.123), channel_id=1, source_target_pairs={{0,8},{8,0},{16,24},{24,16},{1,9},{9,1},{17,25},{25,17},{2,10},{10... | collective-permute-start | bytes 6291464 | tf_op jit(solution)/shard_map/ppermute | solution.py:628
  210.3 87.3 %collective-permute-start.17 = (bf16[512,2048]{1,0:T(8,128)(2,1)S(1)}, bf16[512,2048]{1,0:T(8,128)(2,1)}, u32[]{:S(2)}, u32[]{:S(2)}) collective-permute-start(bf16[512,2048]{1,0:T(8,128)(2,1)S(1)} %bitcast.124), channel_id=1, source_target_pairs={{0,16},{8,24},{16,0},{24,8},{1,17},{9,25},{17,1},{25,9},{2,18},{10... | collective-permute-start | bytes 6291464 | tf_op jit(solution)/shard_map/ppermute | solution.py:628
  215.9 623.4 %reduce-scatter.4.cloned.1.call-start = ((), (), s32[]{:S(2)}) async-start(), calls=%async_computation.7 | async-start | bytes 10813440 | tf_op jit(solution)/shard_map/reduce_scatter | solution.py:1014
  223.5 29.0 %collective-permute-start.15 = (bf16[2,8,1536]{2,1,0:T(8,128)(2,1)S(1)}, bf16[2,8,1536]{2,1,0:T(8,128)(2,1)S(1)}, u32[]{:S(2)}, u32[]{:S(2)}) collective-permute-start(bf16[2,8,1536]{2,1,0:T(8,128)(2,1)S(1)} %convert_bitcast_fusion.4), channel_id=1, source_target_pairs={{0,8},{8,16},{16,24},{1,9},{9,17},{17,25},{2,10},{10,18},{18,26},{... | collective-permute-start | bytes 147464 | tf_op jit(solution)/shard_map/ppermute | solution.py:639
  238.0 64.5 %collective-permute-start.24 = (bf16[128,1024]{1,0:T(8,128)(2,1)S(1)}, bf16[128,1024]{1,0:T(8,128)(2,1)}, u32[]{:S(2)}, u32[]{:S(2)}) collective-permute-start(bf16[128,1024]{1,0:T(8,128)(2,1)S(1)} %bitcast.158), channel_id=1, source_target_pairs={{0,1},{1,2},{2,3},{3,0},{4,5},{5,6},{6,7},{7,4},{8,9},{9,10},{10,1... | collective-permute-start | bytes 786440 | tf_op jit(solution)/shard_map/ppermute | solution.py:633
  248.2 54.3 %collective-permute-start.25 = (bf16[128,1024]{1,0:T(8,128)(2,1)S(1)}, bf16[128,1024]{1,0:T(8,128)(2,1)}, u32[]{:S(2)}, u32[]{:S(2)}) collective-permute-start(bf16[128,1024]{1,0:T(8,128)(2,1)S(1)} %bitcast.159), channel_id=1, source_target_pairs={{0,2},{1,3},{2,0},{3,1},{4,6},{5,7},{6,4},{7,5},{8,10},{9,11},{10,... | collective-permute-start | bytes 786440 | tf_op jit(solution)/shard_map/ppermute | solution.py:633
  252.4 50.0 %collective-permute-start.26 = (bf16[128,1024]{1,0:T(8,128)(2,1)S(1)}, bf16[128,1024]{1,0:T(8,128)(2,1)}, u32[]{:S(2)}, u32[]{:S(2)}) collective-permute-start(bf16[128,1024]{1,0:T(8,128)(2,1)S(1)} %bitcast.160), channel_id=1, source_target_pairs={{0,3},{1,0},{2,1},{3,2},{4,7},{5,4},{6,5},{7,6},{8,11},{9,8},{10,9... | collective-permute-start | bytes 786440 | tf_op jit(solution)/shard_map/ppermute | solution.py:633
  302.4 70.6 %collective-permute-start.21 = (bf16[512,2048]{1,0:T(8,128)(2,1)S(1)}, bf16[512,2048]{1,0:T(8,128)(2,1)}, u32[]{:S(2)}, u32[]{:S(2)}) collective-permute-start(bf16[512,2048]{1,0:T(8,128)(2,1)S(1)} %bitcast.125), channel_id=1, source_target_pairs={{0,4},{4,0},{1,5},{5,1},{2,6},{6,2},{3,7},{7,3},{8,12},{12,8},{9,1... | collective-permute-start | bytes 6291464 | tf_op jit(solution)/shard_map/ppermute | solution.py:628
  314.7 58.3 %collective-permute-start.22 = (bf16[512,2048]{1,0:T(8,128)(2,1)}, bf16[512,2048]{1,0:T(8,128)(2,1)}, u32[]{:S(2)}, u32[]{:S(2)}) collective-permute-start(bf16[512,2048]{1,0:T(8,128)(2,1)} %collective-permute-done.16.mine_grads.refs_18_), channel_id=1, source_target_pairs={{0,4},{4,0},{1,5},{5,1},{2,6},{6,2},{3,7},{7,3},{8,12},{12,8},{9,1... | collective-permute-start | bytes 6291464 | tf_op jit(solution)/shard_map/ppermute | solution.py:628
  314.8 58.2 %collective-permute-start.23 = (bf16[512,2048]{1,0:T(8,128)(2,1)}, bf16[512,2048]{1,0:T(8,128)(2,1)}, u32[]{:S(2)}, u32[]{:S(2)}) collective-permute-start(bf16[512,2048]{1,0:T(8,128)(2,1)} %collective-permute-done.17.mine_grads.refs_20_), channel_id=1, source_target_pairs={{0,4},{4,0},{1,5},{5,1},{2,6},{6,2},{3,7},{7,3},{8,12},{12,8},{9,1... | collective-permute-start | bytes 6291464 | tf_op jit(solution)/shard_map/ppermute | solution.py:628
  315.3 31.4 %collective-permute-start.27 = (bf16[512,1024]{1,0:T(8,128)(2,1)S(1)}, bf16[512,1024]{1,0:T(8,128)(2,1)S(1)}, u32[]{:S(2)}, u32[]{:S(2)}) collective-permute-start(bf16[512,1024]{1,0:T(8,128)(2,1)S(1)} %pad_maximum_fusion.9.refs_1_.refs_0_), channel_id=1, source_target_pairs={{0,8},{8,0},{16,24},{24,16},{1,9},{9,1},{17,25},{25,17},{2,10},{10... | collective-permute-start | bytes 3145736 | tf_op jit(solution)/shard_map/ppermute | solution.py:628
  324.5 30.8 %collective-permute-start.28 = (bf16[512,1024]{1,0:T(8,128)(2,1)S(1)}, bf16[512,1024]{1,0:T(8,128)(2,1)S(1)}, u32[]{:S(2)}, u32[]{:S(2)}) collective-permute-start(bf16[512,1024]{1,0:T(8,128)(2,1)S(1)} %pad_maximum_fusion.9.refs_1_.refs_0_), channel_id=1, source_target_pairs={{0,16},{8,24},{16,0},{24,8},{1,17},{9,25},{17,1},{25,9},{2,18},{10... | collective-permute-start | bytes 3145736 | tf_op jit(solution)/shard_map/ppermute | solution.py:628
  356.2 16.8 %collective-permute-start.29 = (bf16[256,1024]{1,0:T(8,128)(2,1)}, bf16[256,1024]{1,0:T(8,128)(2,1)}, u32[]{:S(2)}, u32[]{:S(2)}) collective-permute-start(bf16[256,1024]{1,0:T(8,128)(2,1)} %slice.686), channel_id=1, source_target_pairs={{0,16},{8,24},{16,0},{24,8},{1,17},{9,25},{17,1},{25,9},{2,18},{10... | collective-permute-start | bytes 1572872 | tf_op jit(solution)/shard_map/ppermute | solution.py:628
  392.3 48.0 %collective-permute-start.34 = (bf16[512,2048]{1,0:T(8,128)(2,1)S(1)}, bf16[512,2048]{1,0:T(8,128)(2,1)}, u32[]{:S(2)}, u32[]{:S(2)}) collective-permute-start(bf16[512,2048]{1,0:T(8,128)(2,1)S(1)} %multiply_convert_fusion.mine.refs_8_), channel_id=1, source_target_pairs={{0,8},{8,0},{16,24},{24,16},{1,9},{9,1},{17,25},{25,17},{2,10},{10... | collective-permute-start | bytes 6291464 | tf_op jit(solution)/shard_map/ppermute | solution.py:628
  397.9 50.2 %collective-permute-start.38 = (bf16[512,2048]{1,0:T(8,128)(2,1)S(1)}, bf16[512,2048]{1,0:T(8,128)(2,1)}, u32[]{:S(2)}, u32[]{:S(2)}) collective-permute-start(bf16[512,2048]{1,0:T(8,128)(2,1)S(1)} %multiply_convert_fusion.mine.refs_8_), channel_id=1, source_target_pairs={{0,16},{8,24},{16,0},{24,8},{1,17},{9,25},{17,1},{25,9},{2,18},{10... | collective-permute-start | bytes 6291464 | tf_op jit(solution)/shard_map/ppermute | solution.py:628
  440.3 19.6 %collective-permute-start.35 = (bf16[512,2048]{1,0:T(8,128)(2,1)}, bf16[512,2048]{1,0:T(8,128)(2,1)}, u32[]{:S(2)}, u32[]{:S(2)}) collective-permute-start(bf16[512,2048]{1,0:T(8,128)(2,1)} %collective-permute-done.34.mine.refs_10_), channel_id=1, source_target_pairs={{0,4},{4,0},{1,5},{5,1},{2,6},{6,2},{3,7},{7,3},{8,12},{12,8},{9,1... | collective-permute-start | bytes 6291464 | tf_op jit(solution)/shard_map/ppermute | solution.py:628
  448.1 53.4 %collective-permute-start.41 = (bf16[512,2048]{1,0:T(8,128)(2,1)}, bf16[512,2048]{1,0:T(8,128)(2,1)}, u32[]{:S(2)}, u32[]{:S(2)}) collective-permute-start(bf16[512,2048]{1,0:T(8,128)(2,1)} %collective-permute-done.38.mine.refs_12_), channel_id=1, source_target_pairs={{0,4},{4,0},{1,5},{5,1},{2,6},{6,2},{3,7},{7,3},{8,12},{12,8},{9,1... | collective-permute-start | bytes 6291464 | tf_op jit(solution)/shard_map/ppermute | solution.py:628
  451.8 79.9 %collective-permute-start.45 = (bf16[256,2048]{1,0:T(8,128)(2,1)}, bf16[256,2048]{1,0:T(8,128)(2,1)}, u32[]{:S(2)}, u32[]{:S(2)}) collective-permute-start(bf16[256,2048]{1,0:T(8,128)(2,1)} %slice.691), channel_id=1, source_target_pairs={{0,16},{8,24},{16,0},{24,8},{1,17},{9,25},{17,1},{25,9},{2,18},{10... | collective-permute-start | bytes 3145736 | tf_op jit(solution)/shard_map/ppermute | solution.py:628
  453.6 79.4 %collective-permute-start.46 = (bf16[256,2048]{1,0:T(8,128)(2,1)S(1)}, bf16[256,2048]{1,0:T(8,128)(2,1)S(1)}, u32[]{:S(2)}, u32[]{:S(2)}) collective-permute-start(bf16[256,2048]{1,0:T(8,128)(2,1)S(1)} %slice.692), channel_id=1, source_target_pairs={{0,8},{8,0},{16,24},{24,16},{1,9},{9,1},{17,25},{25,17},{2,10},{10... | collective-permute-start | bytes 3145736 | tf_op jit(solution)/shard_map/ppermute | solution.py:628
  459.6 40.5 %collective-permute-start.39 = (bf16[256,2048]{1,0:T(8,128)(2,1)}, bf16[256,2048]{1,0:T(8,128)(2,1)S(1)}, u32[]{:S(2)}, u32[]{:S(2)}) collective-permute-start(bf16[256,2048]{1,0:T(8,128)(2,1)} %slice.689), channel_id=1, source_target_pairs={{0,16},{8,24},{16,0},{24,8},{1,17},{9,25},{17,1},{25,9},{2,18},{10... | collective-permute-start | bytes 3145736 | tf_op jit(solution)/shard_map/ppermute | solution.py:628
  459.9 41.6 %collective-permute-start.40 = (bf16[256,2048]{1,0:T(8,128)(2,1)}, bf16[256,2048]{1,0:T(8,128)(2,1)}, u32[]{:S(2)}, u32[]{:S(2)}) collective-permute-start(bf16[256,2048]{1,0:T(8,128)(2,1)} %slice.690), channel_id=1, source_target_pairs={{0,8},{8,0},{16,24},{24,16},{1,9},{9,1},{17,25},{25,17},{2,10},{10... | collective-permute-start | bytes 3145736 | tf_op jit(solution)/shard_map/ppermute | solution.py:628
  538.0 48.0 %collective-permute-start.43 = (bf16[512,2048]{1,0:T(8,128)(2,1)}, bf16[512,2048]{1,0:T(8,128)(2,1)S(1)}, u32[]{:S(2)}, u32[]{:S(2)}) collective-permute-start(bf16[512,2048]{1,0:T(8,128)(2,1)} %add_convert_fusion.5), channel_id=1, source_target_pairs={{0,16},{8,24},{16,0},{24,8},{1,17},{9,25},{17,1},{25,9},{2,18},{10... | collective-permute-start | bytes 6291464 | tf_op jit(solution)/shard_map/ppermute | solution.py:628
  543.7 48.0 %collective-permute-start.37 = (bf16[512,2048]{1,0:T(8,128)(2,1)}, bf16[512,2048]{1,0:T(8,128)(2,1)}, u32[]{:S(2)}, u32[]{:S(2)}) collective-permute-start(bf16[512,2048]{1,0:T(8,128)(2,1)} %add_convert_fusion.6), channel_id=1, source_target_pairs={{0,8},{8,0},{16,24},{24,16},{1,9},{9,1},{17,25},{25,17},{2,10},{10... | collective-permute-start | bytes 6291464 | tf_op jit(solution)/shard_map/ppermute | solution.py:628
  599.9 53.6 %collective-permute-start.49 = (bf16[512,2048]{1,0:T(8,128)(2,1)}, bf16[512,2048]{1,0:T(8,128)(2,1)}, u32[]{:S(2)}, u32[]{:S(2)}) collective-permute-start(bf16[512,2048]{1,0:T(8,128)(2,1)} %add_convert_fusion.4), channel_id=1, source_target_pairs={{0,24},{8,16},{16,8},{24,0},{1,25},{9,17},{17,9},{25,1},{2,26},{10... | collective-permute-start | bytes 6291464 | tf_op jit(solution)/shard_map/ppermute | solution.py:628
  653.5 356.5 %reduce-scatter.8.cloned.1.call-start = ((), (), s32[]{:S(2)}) async-start(), calls=%async_computation.9 | async-start | bytes 4456448 | tf_op jit(solution)/shard_map/reduce_scatter | solution.py:1018
  669.2 63.2 %collective-permute-start.55 = (bf16[512,2048]{1,0:T(8,128)(2,1)}, bf16[512,2048]{1,0:T(8,128)(2,1)}, u32[]{:S(2)}, u32[]{:S(2)}) collective-permute-start(bf16[512,2048]{1,0:T(8,128)(2,1)} %add_convert_fusion.2), channel_id=1, source_target_pairs={{0,16},{8,24},{16,0},{24,8},{1,17},{9,25},{17,1},{25,9},{2,18},{10... | collective-permute-start | bytes 6291464 | tf_op jit(solution)/shard_map/ppermute | solution.py:628
  670.8 61.5 %collective-permute-start.54 = (bf16[512,2048]{1,0:T(8,128)(2,1)}, bf16[512,2048]{1,0:T(8,128)(2,1)}, u32[]{:S(2)}, u32[]{:S(2)}) collective-permute-start(bf16[512,2048]{1,0:T(8,128)(2,1)} %add_convert_fusion.3), channel_id=1, source_target_pairs={{0,8},{8,0},{16,24},{24,16},{1,9},{9,1},{17,25},{25,17},{2,10},{10... | collective-permute-start | bytes 6291464 | tf_op jit(solution)/shard_map/ppermute | solution.py:628
  678.6 71.2 %collective-permute-start.56 = (bf16[512,2048]{1,0:T(8,128)(2,1)}, bf16[512,2048]{1,0:T(8,128)(2,1)}, u32[]{:S(2)}, u32[]{:S(2)}) collective-permute-start(bf16[512,2048]{1,0:T(8,128)(2,1)} %get-tuple-element.190), channel_id=1, source_target_pairs={{0,4},{4,0},{1,5},{5,1},{2,6},{6,2},{3,7},{7,3},{8,12},{12,8},{9,1... | collective-permute-start | bytes 6291464 | tf_op jit(solution)/shard_map/ppermute | solution.py:628
  700.6 29.2 %collective-permute-start.57 = (bf16[2,8,128,128]{3,2,1,0:T(8,128)(2,1)S(1)}, bf16[2,8,128,128]{3,2,1,0:T(8,128)(2,1)S(1)}, u32[]{:S(2)}, u32[]{:S(2)}) collective-permute-start(bf16[2,8,128,128]{3,2,1,0:T(8,128)(2,1)S(1)} %convert_element_type.355), channel_id=1, source_target_pairs={{8,0},{16,8},{24,16},{9,1},{17,9},{25,17},{10,2},{18,10},{26,18},{... | collective-permute-start | bytes 1572872 | tf_op jit(solution)/shard_map/ppermute | solution.py:639
  762.2 48.4 %collective-permute-start.60 = (bf16[512,2048]{1,0:T(8,128)(2,1)}, bf16[512,2048]{1,0:T(8,128)(2,1)}, u32[]{:S(2)}, u32[]{:S(2)}) collective-permute-start(bf16[512,2048]{1,0:T(8,128)(2,1)} %add_convert_fusion.1), channel_id=1, source_target_pairs={{0,24},{8,16},{16,8},{24,0},{1,25},{9,17},{17,9},{25,1},{2,26},{10... | collective-permute-start | bytes 6291464 | tf_op jit(solution)/shard_map/ppermute | solution.py:628
  768.5 48.1 %collective-permute-start.53 = (bf16[512,2048]{1,0:T(8,128)(2,1)}, bf16[512,2048]{1,0:T(8,128)(2,1)}, u32[]{:S(2)}, u32[]{:S(2)}) collective-permute-start(bf16[512,2048]{1,0:T(8,128)(2,1)} %get-tuple-element.185), channel_id=1, source_target_pairs={{0,4},{4,0},{1,5},{5,1},{2,6},{6,2},{3,7},{7,3},{8,12},{12,8},{9,1... | collective-permute-start | bytes 6291464 | tf_op jit(solution)/shard_map/ppermute | solution.py:628
  825.0 61.1 %collective-permute-start.67 = (bf16[512,1536]{1,0:T(8,128)(2,1)}, bf16[512,1536]{1,0:T(8,128)(2,1)}, u32[]{:S(2)}, u32[]{:S(2)}) collective-permute-start(bf16[512,1536]{1,0:T(8,128)(2,1)} %convolution_convert_fusion.3), channel_id=1, source_target_pairs={{0,16},{8,24},{16,0},{24,8},{1,17},{9,25},{17,1},{25,9},{2,18},{10... | collective-permute-start | bytes 4718600 | tf_op jit(solution)/shard_map/ppermute | solution.py:628
  828.3 63.3 %collective-permute-start.66 = (bf16[512,1536]{1,0:T(8,128)(2,1)}, bf16[512,1536]{1,0:T(8,128)(2,1)}, u32[]{:S(2)}, u32[]{:S(2)}) collective-permute-start(bf16[512,1536]{1,0:T(8,128)(2,1)} %convolution_convert_fusion.4), channel_id=1, source_target_pairs={{0,8},{8,0},{16,24},{24,16},{1,9},{9,1},{17,25},{25,17},{2,10},{10... | collective-permute-start | bytes 4718600 | tf_op jit(solution)/shard_map/ppermute | solution.py:628
  872.6 33.5 %collective-permute-start.63 = (f32[2,8,1536]{2,1,0:T(8,128)}, f32[2,8,1536]{2,1,0:T(8,128)}, u32[]{:S(2)}, u32[]{:S(2)}) collective-permute-start(f32[2,8,1536]{2,1,0:T(8,128)} %get-tuple-element.213), channel_id=1, source_target_pairs={{8,0},{16,8},{24,16},{9,1},{17,9},{25,17},{10,2},{18,10},{26,18},{... | collective-permute-start | bytes 294920 | tf_op jit(solution)/shard_map/ppermute | solution.py:639
  900.3 133.5 %collective-permute-start.81 = (bf16[256,1536]{1,0:T(8,128)(2,1)}, bf16[256,1536]{1,0:T(8,128)(2,1)}, u32[]{:S(2)}, u32[]{:S(2)}) collective-permute-start(bf16[256,1536]{1,0:T(8,128)(2,1)} %fusion.13), channel_id=1, source_target_pairs={{0,16},{8,24},{16,0},{24,8},{1,17},{9,25},{17,1},{25,9},{2,18},{10... | collective-permute-start | bytes 2359304 | tf_op jit(solution)/shard_map/ppermute | solution.py:628
  903.3 130.7 %collective-permute-start.80 = (bf16[256,1536]{1,0:T(8,128)(2,1)}, bf16[256,1536]{1,0:T(8,128)(2,1)}, u32[]{:S(2)}, u32[]{:S(2)}) collective-permute-start(bf16[256,1536]{1,0:T(8,128)(2,1)} %fusion.12), channel_id=1, source_target_pairs={{0,8},{8,0},{16,24},{24,16},{1,9},{9,1},{17,25},{25,17},{2,10},{10... | collective-permute-start | bytes 2359304 | tf_op jit(solution)/shard_map/ppermute | solution.py:628
  912.1 52.5 %collective-permute-start.65 = (bf16[512,1664]{1,0:T(8,128)(2,1)S(1)}, bf16[512,1664]{1,0:T(8,128)(2,1)S(1)}, u32[]{:S(2)}, u32[]{:S(2)}) collective-permute-start(bf16[512,1664]{1,0:T(8,128)(2,1)S(1)} %convolution_convert_fusion.1), channel_id=1, source_target_pairs={{0,16},{8,24},{16,0},{24,8},{1,17},{9,25},{17,1},{25,9},{2,18},{10... | collective-permute-start | bytes 5111816 | tf_op jit(solution)/shard_map/ppermute | solution.py:628
  914.6 51.1 %collective-permute-start.64 = (bf16[512,1664]{1,0:T(8,128)(2,1)S(1)}, bf16[512,1664]{1,0:T(8,128)(2,1)S(1)}, u32[]{:S(2)}, u32[]{:S(2)}) collective-permute-start(bf16[512,1664]{1,0:T(8,128)(2,1)S(1)} %convolution_convert_fusion.2), channel_id=1, source_target_pairs={{0,8},{8,0},{16,24},{24,16},{1,9},{9,1},{17,25},{25,17},{2,10},{10... | collective-permute-start | bytes 5111816 | tf_op jit(solution)/shard_map/ppermute | solution.py:628
  968.1 26.1 %collective-permute-start.69 = (bf16[256,1664]{1,0:T(8,128)(2,1)}, bf16[256,1664]{1,0:T(8,128)(2,1)S(1)}, u32[]{:S(2)}, u32[]{:S(2)}) collective-permute-start(bf16[256,1664]{1,0:T(8,128)(2,1)} %fusion.15), channel_id=1, source_target_pairs={{0,16},{8,24},{16,0},{24,8},{1,17},{9,25},{17,1},{25,9},{2,18},{10... | collective-permute-start | bytes 2555912 | tf_op jit(solution)/shard_map/ppermute | solution.py:628
  972.0 22.2 %collective-permute-start.68 = (bf16[256,1664]{1,0:T(8,128)(2,1)}, bf16[256,1664]{1,0:T(8,128)(2,1)}, u32[]{:S(2)}, u32[]{:S(2)}) collective-permute-start(bf16[256,1664]{1,0:T(8,128)(2,1)} %fusion.16), channel_id=1, source_target_pairs={{0,8},{8,0},{16,24},{24,16},{1,9},{9,1},{17,25},{25,17},{2,10},{10... | collective-permute-start | bytes 2555912 | tf_op jit(solution)/shard_map/ppermute | solution.py:628
  997.3 17.7 %collective-permute-start.70 = (bf16[2,256,2048]{2,1,0:T(8,128)(2,1)}, bf16[2,256,2048]{2,1,0:T(8,128)(2,1)}, u32[]{:S(2)}, u32[]{:S(2)}) collective-permute-start(bf16[2,256,2048]{2,1,0:T(8,128)(2,1)} %constant_dynamic-slice_fusion.3), channel_id=1, source_target_pairs={{0,4},{4,0},{1,5},{5,1},{2,6},{6,2},{3,7},{7,3},{8,12},{12,8},{9,1... | collective-permute-start | bytes 6291464 | tf_op jit(solution)/shard_map/ppermute | solution.py:628
  1005.5 34.0 %all-to-all-start.1 = ((bf16[4,2112,128]{2,1,0:T(8,128)(2,1)}), bf16[4,2112,128]{2,1,0:T(8,128)(2,1)}, u32[]{:S(2)}, u32[]{:S(2)}) async-start(bf16[4,2112,128]{2,1,0:T(8,128)(2,1)} %bitcast.140), calls=%async_computation.4 | async-start | bytes 4325376 | tf_op jit(solution)/shard_map/all_to_all | solution.py:1092
  1009.9 88.3 %reduce-scatter.6.cloned.1.call-start = ((), (), s32[]{:S(2)}) async-start(), calls=%async_computation.8 | async-start | bytes 1966080 | tf_op jit(solution)/shard_map/reduce_scatter | solution.py:1072
  1028.1 30.2 %collective-permute-start.77 = (bf16[128,1664]{1,0:T(8,128)(2,1)}, bf16[128,1664]{1,0:T(8,128)(2,1)S(1)}, u32[]{:S(2)}, u32[]{:S(2)}) collective-permute-start(bf16[128,1664]{1,0:T(8,128)(2,1)} %get-tuple-element.344), channel_id=1, source_target_pairs={{0,1},{1,2},{2,3},{3,0},{4,5},{5,6},{6,7},{7,4},{8,9},{9,10},{10,1... | collective-permute-start | bytes 1277960 | tf_op jit(solution)/shard_map/ppermute | solution.py:633
  1028.1 49.1 %collective-permute-start.78 = (bf16[128,1664]{1,0:T(8,128)(2,1)}, bf16[128,1664]{1,0:T(8,128)(2,1)}, u32[]{:S(2)}, u32[]{:S(2)}) collective-permute-start(bf16[128,1664]{1,0:T(8,128)(2,1)} %get-tuple-element.343), channel_id=1, source_target_pairs={{0,2},{1,3},{2,0},{3,1},{4,6},{5,7},{6,4},{7,5},{8,10},{9,11},{10,... | collective-permute-start | bytes 1277960 | tf_op jit(solution)/shard_map/ppermute | solution.py:633
  1033.8 43.5 %collective-permute-start.79 = (bf16[128,1664]{1,0:T(8,128)(2,1)}, bf16[128,1664]{1,0:T(8,128)(2,1)}, u32[]{:S(2)}, u32[]{:S(2)}) collective-permute-start(bf16[128,1664]{1,0:T(8,128)(2,1)} %get-tuple-element.342), channel_id=1, source_target_pairs={{0,3},{1,0},{2,1},{3,2},{4,7},{5,4},{6,5},{7,6},{8,11},{9,8},{10,9... | collective-permute-start | bytes 1277960 | tf_op jit(solution)/shard_map/ppermute | solution.py:633
  1056.3 23.4 %collective-permute-start.75 = (f32[16640]{0:T(1024)S(1)}, f32[16640]{0:T(1024)S(1)}, u32[]{:S(2)}, u32[]{:S(2)}) collective-permute-start(f32[16640]{0:T(1024)S(1)} %add.322), channel_id=1, source_target_pairs={{0,1},{1,0},{2,3},{3,2},{4,5},{5,4},{6,7},{7,6},{8,9},{9,8},{10,11... | collective-permute-start | bytes 199688 | tf_op jit(solution)/shard_map/ppermute | solution.py:628
  1079.7 20.9 %collective-permute-start.76 = (f32[16640]{0:T(1024)S(1)}, f32[16640]{0:T(1024)S(1)}, u32[]{:S(2)}, u32[]{:S(2)}) collective-permute-start(f32[16640]{0:T(1024)S(1)} %add.323), channel_id=1, source_target_pairs={{0,2},{1,3},{2,0},{3,1},{4,6},{5,7},{6,4},{7,5},{8,10},{9,11},{10,... | collective-permute-start | bytes 199688 | tf_op jit(solution)/shard_map/ppermute | solution.py:628
  (105 other events, 967.3 us)
Sparse Core Ops, SparseCore 0:
  121.5 113.1 all-gather.2
  236.3 74.9 all-gather.4
  653.6 151.4 reduce-scatter.3
  824.4 100.6 reduce-scatter.7
  1039.5 49.9 reduce-scatter.5

commit v13 on v12

--- a/solution.py
+++ b/solution.py
@@ -1064,8 +1064,7 @@
 
     conv_cols = jnp.concatenate([jnp.sum(part, axis=0)[:taps] for part in conv_parts], axis=1)
     gains = butterfly(jnp.concatenate([gain_mix_part, gain_ffn_part, gain_o_part]), ("tp",))
-    conv_kinds = jnp.stack(by_kind([conv_cols]))
-    sums = jnp.concatenate([gains, conv_kinds.reshape(-1), jnp.sum(logits, axis=0)])
+    sums = jnp.concatenate([gains, conv_cols.reshape(-1), jnp.sum(logits, axis=0)])
     last_line = Line(scatter.own())
     for p in range(1, parts):
         own = low(earlier_scatter.own(*last_line.sent))
@@ -1085,7 +1084,7 @@
     beta_grad = mix_grads[0][:, part_cols : part_cols + heads_here]
     ends = [width, 2 * width, 2 * width + LANES, sums.shape[0] - LANES]
     gain_mix_grad, gain_ffn_grad, gain_o_grad, conv_grad, bias_grad = jnp.split(sums, ends)
-    conv_grad = conv_grad.reshape(conv_kinds.shape)
+    conv_grad = jnp.stack(by_kind([conv_grad.reshape(taps, -1)]))
     bias_grad = bias_grad[:heads_here]
     out_grad_w = wide(tie(out_grad_w, *scatter.last)).T
     pieces = tie(total, *scatter.last).reshape(3 * units, 4, shard_rows).transpose(1, 0, 2)

time: 1120 us -> 1110 us (level)
  waiting for transfers between devices: 317 us -> 304 us
    ppermute x60, waiting for transfers between devices: 193 us -> 160 us  [flip(): return lax.ppermute(value, axis, [(i, i ^ bit) for i in devices])]
    ppermute x10, waiting for transfers between devices: 72 us -> 91.6 us  [from_behind(): return lax.ppermute(block, axis, route)]
    unnamed x210 -> x216, local copies, waits for them, and re-layouts: 26.2 us -> 31.5 us
  transfers between devices with their start and end apart: 89 -> 89, of which waited for: 37 -> 37; matrix products, arithmetic and copies ran while one was open for 19% -> 19% of each run, Pallas kernels for 35% -> 36%
where the time goes in v13:
time: 1110 us; the launch traced here: 1100 us
  Pallas kernels  393 us (35%)
  waiting for transfers between devices  304 us (27%)
  starting transfers between devices  147 us (13%)
  other arithmetic  114 us (10%)
  local copies, waits for them, and re-layouts  88.5 us (8%)
  matrix products  39.9 us (4%)
  between operations  15.6 us (1%)
    ppermute x60, waiting for transfers between devices, flip(): return lax.ppermute(value, axis, [(i, i ^ bit) for i in devices])  160 us
    pallas_call x4, Pallas kernels, ffn_both(): pl.pallas_call(ffn_kernel, grid=(count // tile,), in_specs=[wide_rows] *...  118 us
    ppermute x10, waiting for transfers between devices, from_behind(): return lax.ppermute(block, axis, route)  91.6 us
    ppermute x60, starting transfers between devices, flip(): return lax.ppermute(value, axis, [(i, i ^ bit) for i in devices])  74.1 us
    pallas_call x2, Pallas kernels, mixer_backward(): pl.pallas_call(functools.partial(backward_kernel, taps, group, first), gr...  66.4 us
    pallas_call x2, Pallas kernels, mixer_forward(): pl.pallas_call(functools.partial(forward_kernel, taps, group, first), gri...  55 us
    ppermute x12, waiting for transfers between devices, shift(): lax.ppermute(value, axis, [(i, (i + distance) % count) for i in range(cou...  52.1 us
    pallas_call x1, Pallas kernels, ffn_weights(): pl.pallas_call(functools.partial(ffn_weights_kernel, count, lines), grid=...  48.1 us
  transfers between devices with their start and end apart: 89, of which 37 were waited for; matrix products, arithmetic and copies ran while one was open for 19% of the time, Pallas kernels for 36%

profile of v13, /device:TPU:0, one launch (start us, length us, event | category | flops | bytes accessed | tf_op | source)
XLA Modules:
  0.0 1101.4 jit_solution(17612036907856453401)
XLA Ops:
  12.6 5.3 all-to-all-start
  27.8 9.3 collective-permute-done
  37.1 17.1 %collective-permute-done.1 = bf16[128,1664]{1,0:T(8,128)(2,1)S(1)} collective-permute-done((bf16[128,1664]{1,0:T(8,128)(2,1)}, bf16[128,1664]{1,0:T(8,128)(2,1)S(1)}, u32[]{:S(2)}, u32[]{:S(2)}) %collective-permute-start.1) | collective-permute-done | bytes 426016 | tf_op jit(solution)/shard_map/ppermute | solution.py:633
  63.1 10.7 collective-permute-start.10
  77.4 18.7 %collective-permute-done.3.refs_1_.refs_3_ = bf16[512,1664]{1,0:T(8,128)(2,1)S(1)} collective-permute-done((bf16[512,1664]{1,0:T(8,128)(2,1)}, bf16[512,1664]{1,0:T(8,128)(2,1)S(1)}, u32[]{:S(2)}, u32[]{:S(2)}) %collective-permute-start.3) | collective-permute-done | bytes 1703968 | tf_op jit(solution)/shard_map/ppermute | solution.py:628
  101.3 6.6 collective-permute-done.9
  112.4 5.9 collective-permute-done.5.refs_3_.refs_5_
  121.4 6.6 convert_element_type.398
  131.4 4.7 shard_map.271
  140.8 12.8 %shard_map.272.pre.beta = f32[1024,1664]{1,0:T(8,128)} custom-call(s32[1]{0:T(128)} %bitcast.1.place, bf16[1024,2048]{1,0:T(8,128)(2,1)} %fusion.1.rows, bf16[512,1664]{1,0:T(8,128)(2,1)} %pad_maximum_fusion.6.refs_0_.refs_2_, bf16[512,1664]{1,0:T(8,128)(2,1)} %copy-done.31, bf16[512,1664]{1,0:T(8,128)(2,1)} %copy-done.32, bf16[256,1664]{1,0:T(8,128)(2,1)} %copy-done.46, ...), custom_call_target="tpu_custom_call" | custom-call | flops 6979321856 | bytes 11010048 | tf_op jit(solution)/shard_map/pallas_call | solution.py:551
  155.6 27.5 %shard_map.273 = (f32[1024,512]{1,0:T(8,128)}, bf16[1024,512]{1,0:T(8,128)(2,1)}, f32[2,4,128,256]{3,2,1,0:T(8,128)}, bf16[2,4,4,128,128]{4,3,2,1,0:T(8,128)(2,1...) custom-call(f32[1024,1664]{1,0:T(8,128)} %shard_map.272.pre.beta, ...), custom_call_target="tpu_custom_call" | custom-call | flops 4026531840 | bytes 20971520 | tf_op jit(solution)/shard_map/pallas_call | solution.py:160
  183.1 4.8 collective-permute-done.11.refs_1_.refs_8_
  194.3 13.6 %collective-permute-done.13.refs_3_.refs_10_ = bf16[256,1536]{1,0:T(8,128)(2,1)S(1)} collective-permute-done((bf16[256,1536]{1,0:T(8,128)(2,1)}, bf16[256,1536]{1,0:T(8,128)(2,1)S(1)}, u32[]{:S(2)}, u32[]{:S(2)}) %collective-permute-start.13) | collective-permute-done | bytes 786464 | tf_op jit(solution)/shard_map/ppermute | solution.py:628
  218.1 4.4 shard_map.274
  226.5 11.5 %shard_map.275.pre = f32[1024,1536]{1,0:T(8,128)} custom-call(s32[1]{0:T(128)} %bitcast.1.place, bf16[1024,2048]{1,0:T(8,128)(2,1)} %fusion.1.rows, bf16[512,1536]{1,0:T(8,128)(2,1)} %pad_maximum_fusion.7.refs_0_.refs_7_, bf16[512,1536]{1,0:T(8,128)(2,1)} %copy-done.33, bf16[512,1536]{1,0:T(8,128)(2,1)} %collective-permute-done.12.refs_2_.refs_9_, ...), custom_call_target="tpu_custom_call" | custom-call | flops 6442450944 | bytes 10485760 | tf_op jit(solution)/shard_map/pallas_call | solution.py:551
  238.0 10.2 collective-permute-start.24
  252.4 5.3 collective-permute-start.26
  258.3 27.5 %shard_map.276 = (f32[1024,512]{1,0:T(8,128)}, bf16[1024,512]{1,0:T(8,128)(2,1)}, f32[2,4,128,256]{3,2,1,0:T(8,128)}, bf16[2,4,4,128,128]{4,3,2,1,0:T(8,128)(2,1...) custom-call(f32[1024,1536]{1,0:T(8,128)} %shard_map.275.pre, ...), custom_call_target="tpu_custom_call" | custom-call | flops 4026531840 | bytes 20971520 | tf_op jit(solution)/shard_map/pallas_call | solution.py:160
  289.5 8.1 shard_map.277.gate_w.up_w
  297.7 4.6 collective-permute-start.18
  303.6 6.1 collective-permute-done.18
  310.1 4.4 collective-permute-start.19
  317.7 6.7 collective-permute-done.19
  324.3 6.8 collective-permute-start.28
  331.4 15.2 %collective-permute-done.27.refs_2_.refs_1_ = bf16[512,1024]{1,0:T(8,128)(2,1)S(1)} collective-permute-done((bf16[512,1024]{1,0:T(8,128)(2,1)S(1)}, bf16[512,1024]{1,0:T(8,128)(2,1)S(1)}, u32[]{:S(2)}, u32[]{:S(2)}) %collective-permute-start.27) | collective-permute-done | bytes 1048608 | tf_op jit(solution)/shard_map/ppermute | solution.py:628
  348.9 6.3 collective-permute-done.28.refs_3_.refs_2_
  361.0 4.5 shard_map.278
  365.5 4.6 shard_map.279
  373.0 8.7 shard_map.280
  393.4 4.4 shard_map.281.down_w
  402.0 29.5 %shard_map.282 = (bf16[3,512,704]{2,1,0:T(8,128)(2,1)}, bf16[512,2048]{1,0:T(8,128)(2,1)}, bf16[512,2048]{1,0:T(8,128)(2,1)}, bf16[3,512,704]{2,1,0:T(8,128)(2,1...) custom-call(bf16[512,2048]{1,0:T(8,128)(2,1)} %copy-done.36, ...), custom_call_target="tpu_custom_call" | custom-call | flops 17716740096 | bytes 25427968 | tf_op jit(solution)/shard_map/pallas_call | solution.py:469
  431.5 8.7 collective-permute-done.34.mine.refs_10_
  440.2 7.8 collective-permute-done.38.mine.refs_12_
  460.4 29.5 %shard_map.283 = (bf16[3,512,704]{2,1,0:T(8,128)(2,1)}, bf16[512,2048]{1,0:T(8,128)(2,1)}, bf16[512,2048]{1,0:T(8,128)(2,1)}, bf16[3,512,704]{2,1,0:T(8,128)(2,1...) custom-call(bf16[512,2048]{1,0:T(8,128)(2,1)} %collective-permute-done.34.mine.refs_10_, ...), custom_call_target="tpu_custom_call" | custom-call | flops 17716740096 | bytes 25427968 | tf_op jit(solution)/shard_map/pallas_call | solution.py:469
  490.0 10.1 collective-permute-done.39
  501.4 29.7 %shard_map.284 = (bf16[3,512,704]{2,1,0:T(8,128)(2,1)}, bf16[512,2048]{1,0:T(8,128)(2,1)}, bf16[512,2048]{1,0:T(8,128)(2,1)}, bf16[3,512,704]{2,1,0:T(8,128)(2,1...) custom-call(bf16[512,2048]{1,0:T(8,128)(2,1)} %collective-permute-done.38.mine.refs_12_, ...), custom_call_target="tpu_custom_call" | custom-call | flops 17716740096 | bytes 25427968 | tf_op jit(solution)/shard_map/pallas_call | solution.py:469
  546.3 29.5 %shard_map.285 = (bf16[3,512,704]{2,1,0:T(8,128)(2,1)}, bf16[512,2048]{1,0:T(8,128)(2,1)}, bf16[512,2048]{1,0:T(8,128)(2,1)}, bf16[3,512,704]{2,1,0:T(8,128)(2,1...) custom-call(bf16[512,2048]{1,0:T(8,128)(2,1)} %copy-done.52, ...), custom_call_target="tpu_custom_call" | custom-call | flops 17716740096 | bytes 25427968 | tf_op jit(solution)/shard_map/pallas_call | solution.py:469
  575.8 10.2 collective-permute-done.43
  586.0 5.6 collective-permute-done.37
  605.2 48.1 %shard_map.286 = bf16[4,3,704,512]{3,2,1,0:T(8,128)(2,1)} custom-call(bf16[3,512,704]{2,1,0:T(8,128)(2,1)} %get-tuple-element.177.refs_0_, bf16[3,512,704]{2,1,0:T(8,128)(2,1)} %get-tuple-element.178.refs_1_, bf16[3,512,704]{2,1,0:T(8,128)(2,1)} %get-tuple-element.159.refs_2_, bf16[3,512,704]{2,1,0:T(8,128)(2,1)} %get-tuple-element.179.refs_3_, ...), custom_call_target="tpu_custom_call" | custom-call | flops 35433480192 | bytes 67108864 | tf_op jit(solution)/shard_map/pallas_call | solution.py:516
  659.1 7.0 multiply_reduce_fusion.1
  678.7 9.0 shard_map.287.grad
  687.6 5.7 shard_map.289
  693.4 5.8 shard_map.288
  701.8 27.9 %collective-permute-done.57 = bf16[2,8,128,128]{3,2,1,0:T(8,128)(2,1)S(1)} collective-permute-done((bf16[2,8,128,128]{3,2,1,0:T(8,128)(2,1)S(1)}, bf16[2,8,128,128]{3,2,1,0:T(8,128)(2,1)S(1)}, u32[]{:S(2)}, u32[]{:S(2)}) %collective-permute-start.57) | collective-permute-done | bytes 524320 | tf_op jit(solution)/shard_map/ppermute | solution.py:639
  732.3 14.0 %collective-permute-done.58 = bf16[2,8,128,128]{3,2,1,0:T(8,128)(2,1)} collective-permute-done((bf16[2,8,128,128]{3,2,1,0:T(8,128)(2,1)}, bf16[2,8,128,128]{3,2,1,0:T(8,128)(2,1)}, u32[]{:S(2)}, u32[]{:S(2)}) %collective-permute-start.58) | collective-permute-done | bytes 524320 | tf_op jit(solution)/shard_map/ppermute | solution.py:639
  753.7 8.5 collective-permute-done.59
  762.2 6.3 convolution_convert_fusion
  769.5 33.1 %shard_map.290 = (bf16[1024,1536]{1,0:T(8,128)(2,1)}, f32[2,8,1536]{2,1,0:T(8,128)}, f32[2,8,1536]{2,1,0:T(8,128)}, f32[2,8,1536]{2,1,0:T(8,128)}, f32[1024,128]{1,0:T(8,128)}) custom-call(f32[1024,1536]{1,0:T(8,128)} %shard_map.275.pre, f32[1024,1664]{1,0:T(8,128)} %shard_map.272.pre.beta, f32[1,128]{1,0:T(1,128)} %pad_bitcast_fusion.bias, ...), custom_call_target="tpu_custom_call" | custom-call | flops 4026531840 | bytes 20971520 | tf_op jit(solution)/shard_map/pallas_call | solution.py:318
  806.1 4.4 collective-permute-done.61
  816.6 7.4 add_convert_fusion
  827.3 5.7 fusion.24
  833.0 4.6 broadcast_select_fusion.3
  837.6 33.3 %shard_map.291 = (bf16[1024,1536]{1,0:T(8,128)(2,1)}, f32[2,8,1536]{2,1,0:T(8,128)}, f32[2,8,1536]{2,1,0:T(8,128)}, f32[2,8,1536]{2,1,0:T(8,128)}, f32[1024,128]{1,0:T(8,128)}) custom-call(f32[1024,1664]{1,0:T(8,128)} %shard_map.272.pre.beta, f32[1024,1664]{1,0:T(8,128)} %shard_map.272.pre.beta, f32[1,128]{1,0:T(1,128)} %pad_bitcast_fusion.bias, ...), custom_call_target="tpu_custom_call" | custom-call | flops 4026531840 | bytes 20971520 | tf_op jit(solution)/shard_map/pallas_call | solution.py:318
  873.7 19.7 %collective-permute-done.63 = f32[2,8,1536]{2,1,0:T(8,128)S(1)} collective-permute-done((f32[2,8,1536]{2,1,0:T(8,128)}, f32[2,8,1536]{2,1,0:T(8,128)S(1)}, u32[]{:S(2)}, u32[]{:S(2)}) %collective-permute-start.63) | collective-permute-done | bytes 98336 | tf_op jit(solution)/shard_map/ppermute | solution.py:639
  895.0 4.5 convolution_convert_fusion.1
  921.3 27.7 %collective-permute-done.65 = bf16[512,1664]{1,0:T(8,128)(2,1)S(1)} collective-permute-done((bf16[512,1664]{1,0:T(8,128)(2,1)S(1)}, bf16[512,1664]{1,0:T(8,128)(2,1)S(1)}, u32[]{:S(2)}, u32[]{:S(2)}) %collective-permute-start.65) | collective-permute-done | bytes 1703968 | tf_op jit(solution)/shard_map/ppermute | solution.py:628
  956.5 21.6 %shard_map.292 = bf16[1024,2048]{1,0:T(8,128)(2,1)} custom-call(s32[1]{0:T(128)} %bitcast.1.place, bf16[1024,1664]{1,0:T(8,128)(2,1)} %pad_maximum_fusion.3.refs_0_, bf16[1024,1536]{1,0:T(8,128)(2,1)} %bitcast.132, bf16[512,1664]{1,0:T(8,128)(2,1)} %pad_maximum_fusion.6.refs_0_.refs_2_, bf16[512,1664]{1,0:T(8,128)(2,1)} %copy-done.31, ...), custom_call_target="tpu_custom_call" | custom-call | flops 13421772800 | bytes 17301504 | tf_op jit(solution)/shard_map/pallas_call | solution.py:587
  983.5 4.8 reshape.209
  991.5 4.4 all-to-all-start.1
  1008.4 4.3 fusion.9
  1013.7 5.6 collective-permute-start.78
  1044.2 18.9 %collective-permute-done.78 = bf16[128,1664]{1,0:T(8,128)(2,1)} collective-permute-done((bf16[128,1664]{1,0:T(8,128)(2,1)}, bf16[128,1664]{1,0:T(8,128)(2,1)}, u32[]{:S(2)}, u32[]{:S(2)}) %collective-permute-start.78) | collective-permute-done | bytes 426016 | tf_op jit(solution)/shard_map/ppermute | solution.py:633
  1065.5 18.8 %collective-permute-start.76 = (f32[16640]{0:T(1024)S(1)}, f32[16640]{0:T(1024)S(1)}, u32[]{:S(2)}, u32[]{:S(2)}) collective-permute-start(f32[16640]{0:T(1024)S(1)} %add.323), channel_id=1, source_target_pairs={{0,2},{1,3},{2,0},{3,1},{4,6},{5,7},{6,4},{7,5},{8,10},{9,11},{10,... | collective-permute-start | bytes 199688 | tf_op jit(solution)/shard_map/ppermute | solution.py:628
  (506 shorter events, 291.3 us)
Async XLA Ops:
  12.6 44.3 %all-to-all-start = ((bf16[4,2112,128]{2,1,0:T(8,128)(2,1)}), bf16[4,2112,128]{2,1,0:T(8,128)(2,1)S(1)}, u32[]{:S(2)}, u32[]{:S(2)}) async-start(bf16[4,2112,128]{2,1,0:T(8,128)(2,1)} %bitcast.139), calls=%async_computation | async-start | bytes 4325376 | tf_op jit(solution)/shard_map/all_to_all | solution.py:894
  17.8 271.6 %all-gather.3.cloned.1.call-start = ((), (), s32[]{:S(2)}) async-start(), calls=%async_computation.5 | async-start | bytes 7208960 | tf_op jit(solution)/shard_map/all_gather | solution.py:912
  23.8 30.4 %collective-permute-start.1 = (bf16[128,1664]{1,0:T(8,128)(2,1)}, bf16[128,1664]{1,0:T(8,128)(2,1)S(1)}, u32[]{:S(2)}, u32[]{:S(2)}) collective-permute-start(bf16[128,1664]{1,0:T(8,128)(2,1)} %constant_dynamic-update-slice_fusion), channel_id=1, source_target_pairs={{0,2},{1,3},{2,0},{3,1},{4,6},{5,7},{6,4},{7,5},{8,10},{9,11},{10,... | collective-permute-start | bytes 1277960 | tf_op jit(solution)/shard_map/ppermute | solution.py:633
  26.4 27.8 %collective-permute-start.2 = (bf16[128,1664]{1,0:T(8,128)(2,1)}, bf16[128,1664]{1,0:T(8,128)(2,1)S(1)}, u32[]{:S(2)}, u32[]{:S(2)}) collective-permute-start(bf16[128,1664]{1,0:T(8,128)(2,1)} %constant_dynamic-update-slice_fusion), channel_id=1, source_target_pairs={{0,3},{1,0},{2,1},{3,2},{4,7},{5,4},{6,5},{7,6},{8,11},{9,8},{10,9... | collective-permute-start | bytes 1277960 | tf_op jit(solution)/shard_map/ppermute | solution.py:633
  56.9 39.2 %collective-permute-start.3 = (bf16[512,1664]{1,0:T(8,128)(2,1)}, bf16[512,1664]{1,0:T(8,128)(2,1)S(1)}, u32[]{:S(2)}, u32[]{:S(2)}) collective-permute-start(bf16[512,1664]{1,0:T(8,128)(2,1)} %pad_maximum_fusion.6.refs_0_.refs_2_), channel_id=1, source_target_pairs={{0,8},{8,0},{16,24},{24,16},{1,9},{9,1},{17,25},{25,17},{2,10},{10... | collective-permute-start | bytes 5111816 | tf_op jit(solution)/shard_map/ppermute | solution.py:628
  58.5 39.0 %collective-permute-start.4 = (bf16[512,1664]{1,0:T(8,128)(2,1)}, bf16[512,1664]{1,0:T(8,128)(2,1)S(1)}, u32[]{:S(2)}, u32[]{:S(2)}) collective-permute-start(bf16[512,1664]{1,0:T(8,128)(2,1)} %pad_maximum_fusion.6.refs_0_.refs_2_), channel_id=1, source_target_pairs={{0,16},{8,24},{16,0},{24,8},{1,17},{9,25},{17,1},{25,9},{2,18},{10... | collective-permute-start | bytes 5111816 | tf_op jit(solution)/shard_map/ppermute | solution.py:628
  63.1 38.2 %collective-permute-start.10 = (bf16[128,1536]{1,0:T(8,128)(2,1)S(1)}, bf16[128,1536]{1,0:T(8,128)(2,1)S(1)}, u32[]{:S(2)}, u32[]{:S(2)}) collective-permute-start(bf16[128,1536]{1,0:T(8,128)(2,1)S(1)} %copy-done.58), channel_id=1, source_target_pairs={{0,3},{1,0},{2,1},{3,2},{4,7},{5,4},{6,5},{7,6},{8,11},{9,8},{10,9... | collective-permute-start | bytes 1179656 | tf_op jit(solution)/shard_map/ppermute | solution.py:633
  73.8 27.5 %collective-permute-start.8 = (bf16[128,1536]{1,0:T(8,128)(2,1)S(1)}, bf16[128,1536]{1,0:T(8,128)(2,1)S(1)}, u32[]{:S(2)}, u32[]{:S(2)}) collective-permute-start(bf16[128,1536]{1,0:T(8,128)(2,1)S(1)} %copy-done.58), channel_id=1, source_target_pairs={{0,1},{1,2},{2,3},{3,0},{4,5},{5,6},{6,7},{7,4},{8,9},{9,10},{10,1... | collective-permute-start | bytes 1179656 | tf_op jit(solution)/shard_map/ppermute | solution.py:633
  73.8 34.2 %collective-permute-start.9 = (bf16[128,1536]{1,0:T(8,128)(2,1)S(1)}, bf16[128,1536]{1,0:T(8,128)(2,1)S(1)}, u32[]{:S(2)}, u32[]{:S(2)}) collective-permute-start(bf16[128,1536]{1,0:T(8,128)(2,1)S(1)} %copy-done.58), channel_id=1, source_target_pairs={{0,2},{1,3},{2,0},{3,1},{4,6},{5,7},{6,4},{7,5},{8,10},{9,11},{10,... | collective-permute-start | bytes 1179656 | tf_op jit(solution)/shard_map/ppermute | solution.py:633
  98.5 19.8 %collective-permute-start.5 = (bf16[256,1664]{1,0:T(8,128)(2,1)}, bf16[256,1664]{1,0:T(8,128)(2,1)S(1)}, u32[]{:S(2)}, u32[]{:S(2)}) collective-permute-start(bf16[256,1664]{1,0:T(8,128)(2,1)} %slice.622), channel_id=1, source_target_pairs={{0,16},{8,24},{16,0},{24,8},{1,17},{9,25},{17,1},{25,9},{2,18},{10... | collective-permute-start | bytes 2555912 | tf_op jit(solution)/shard_map/ppermute | solution.py:628
  100.0 19.8 %collective-permute-start.6 = (bf16[256,1664]{1,0:T(8,128)(2,1)}, bf16[256,1664]{1,0:T(8,128)(2,1)}, u32[]{:S(2)}, u32[]{:S(2)}) collective-permute-start(bf16[256,1664]{1,0:T(8,128)(2,1)} %slice.623), channel_id=1, source_target_pairs={{0,8},{8,0},{16,24},{24,16},{1,9},{9,1},{17,25},{25,17},{2,10},{10... | collective-permute-start | bytes 2555912 | tf_op jit(solution)/shard_map/ppermute | solution.py:628
  121.3 260.3 %all-gather.5.cloned.1.call-start = ((), (), s32[]{:S(2)}) async-start(), calls=%async_computation.6 | async-start | bytes 3604480 | tf_op jit(solution)/shard_map/all_gather | solution.py:913
  153.6 34.2 %collective-permute-start.11 = (bf16[512,1536]{1,0:T(8,128)(2,1)S(1)}, bf16[512,1536]{1,0:T(8,128)(2,1)S(1)}, u32[]{:S(2)}, u32[]{:S(2)}) collective-permute-start(bf16[512,1536]{1,0:T(8,128)(2,1)S(1)} %copy-done.26), channel_id=1, source_target_pairs={{0,8},{8,0},{16,24},{24,16},{1,9},{9,1},{17,25},{25,17},{2,10},{10... | collective-permute-start | bytes 4718600 | tf_op jit(solution)/shard_map/ppermute | solution.py:628
  154.1 34.8 %collective-permute-start.12 = (bf16[512,1536]{1,0:T(8,128)(2,1)S(1)}, bf16[512,1536]{1,0:T(8,128)(2,1)}, u32[]{:S(2)}, u32[]{:S(2)}) collective-permute-start(bf16[512,1536]{1,0:T(8,128)(2,1)S(1)} %copy-done.26), channel_id=1, source_target_pairs={{0,16},{8,24},{16,0},{24,8},{1,17},{9,25},{17,1},{25,9},{2,18},{10... | collective-permute-start | bytes 4718600 | tf_op jit(solution)/shard_map/ppermute | solution.py:628
  190.9 16.9 %collective-permute-start.13 = (bf16[256,1536]{1,0:T(8,128)(2,1)}, bf16[256,1536]{1,0:T(8,128)(2,1)S(1)}, u32[]{:S(2)}, u32[]{:S(2)}) collective-permute-start(bf16[256,1536]{1,0:T(8,128)(2,1)} %slice.649), channel_id=1, source_target_pairs={{0,16},{8,24},{16,0},{24,8},{1,17},{9,25},{17,1},{25,9},{2,18},{10... | collective-permute-start | bytes 2359304 | tf_op jit(solution)/shard_map/ppermute | solution.py:628
  191.7 17.9 %collective-permute-start.14 = (bf16[256,1536]{1,0:T(8,128)(2,1)}, bf16[256,1536]{1,0:T(8,128)(2,1)}, u32[]{:S(2)}, u32[]{:S(2)}) collective-permute-start(bf16[256,1536]{1,0:T(8,128)(2,1)} %slice.650), channel_id=1, source_target_pairs={{0,8},{8,0},{16,24},{24,16},{1,9},{9,1},{17,25},{25,17},{2,10},{10... | collective-permute-start | bytes 2359304 | tf_op jit(solution)/shard_map/ppermute | solution.py:628
  209.6 88.0 %collective-permute-start.16 = (bf16[512,2048]{1,0:T(8,128)(2,1)S(1)}, bf16[512,2048]{1,0:T(8,128)(2,1)}, u32[]{:S(2)}, u32[]{:S(2)}) collective-permute-start(bf16[512,2048]{1,0:T(8,128)(2,1)S(1)} %bitcast.123), channel_id=1, source_target_pairs={{0,8},{8,0},{16,24},{24,16},{1,9},{9,1},{17,25},{25,17},{2,10},{10... | collective-permute-start | bytes 6291464 | tf_op jit(solution)/shard_map/ppermute | solution.py:628
  210.4 87.2 %collective-permute-start.17 = (bf16[512,2048]{1,0:T(8,128)(2,1)S(1)}, bf16[512,2048]{1,0:T(8,128)(2,1)}, u32[]{:S(2)}, u32[]{:S(2)}) collective-permute-start(bf16[512,2048]{1,0:T(8,128)(2,1)S(1)} %bitcast.124), channel_id=1, source_target_pairs={{0,16},{8,24},{16,0},{24,8},{1,17},{9,25},{17,1},{25,9},{2,18},{10... | collective-permute-start | bytes 6291464 | tf_op jit(solution)/shard_map/ppermute | solution.py:628
  215.8 621.8 %reduce-scatter.4.cloned.1.call-start = ((), (), s32[]{:S(2)}) async-start(), calls=%async_computation.7 | async-start | bytes 10813440 | tf_op jit(solution)/shard_map/reduce_scatter | solution.py:1014
  223.4 29.0 %collective-permute-start.15 = (bf16[2,8,1536]{2,1,0:T(8,128)(2,1)S(1)}, bf16[2,8,1536]{2,1,0:T(8,128)(2,1)S(1)}, u32[]{:S(2)}, u32[]{:S(2)}) collective-permute-start(bf16[2,8,1536]{2,1,0:T(8,128)(2,1)S(1)} %convert_bitcast_fusion.4), channel_id=1, source_target_pairs={{0,8},{8,16},{16,24},{1,9},{9,17},{17,25},{2,10},{10,18},{18,26},{... | collective-permute-start | bytes 147464 | tf_op jit(solution)/shard_map/ppermute | solution.py:639
  238.0 64.4 %collective-permute-start.24 = (bf16[128,1024]{1,0:T(8,128)(2,1)S(1)}, bf16[128,1024]{1,0:T(8,128)(2,1)}, u32[]{:S(2)}, u32[]{:S(2)}) collective-permute-start(bf16[128,1024]{1,0:T(8,128)(2,1)S(1)} %bitcast.158), channel_id=1, source_target_pairs={{0,1},{1,2},{2,3},{3,0},{4,5},{5,6},{6,7},{7,4},{8,9},{9,10},{10,1... | collective-permute-start | bytes 786440 | tf_op jit(solution)/shard_map/ppermute | solution.py:633
  248.1 54.3 %collective-permute-start.25 = (bf16[128,1024]{1,0:T(8,128)(2,1)S(1)}, bf16[128,1024]{1,0:T(8,128)(2,1)}, u32[]{:S(2)}, u32[]{:S(2)}) collective-permute-start(bf16[128,1024]{1,0:T(8,128)(2,1)S(1)} %bitcast.159), channel_id=1, source_target_pairs={{0,2},{1,3},{2,0},{3,1},{4,6},{5,7},{6,4},{7,5},{8,10},{9,11},{10,... | collective-permute-start | bytes 786440 | tf_op jit(solution)/shard_map/ppermute | solution.py:633
  252.4 50.0 %collective-permute-start.26 = (bf16[128,1024]{1,0:T(8,128)(2,1)S(1)}, bf16[128,1024]{1,0:T(8,128)(2,1)}, u32[]{:S(2)}, u32[]{:S(2)}) collective-permute-start(bf16[128,1024]{1,0:T(8,128)(2,1)S(1)} %bitcast.160), channel_id=1, source_target_pairs={{0,3},{1,0},{2,1},{3,2},{4,7},{5,4},{6,5},{7,6},{8,11},{9,8},{10,9... | collective-permute-start | bytes 786440 | tf_op jit(solution)/shard_map/ppermute | solution.py:633
  302.3 70.6 %collective-permute-start.21 = (bf16[512,2048]{1,0:T(8,128)(2,1)S(1)}, bf16[512,2048]{1,0:T(8,128)(2,1)}, u32[]{:S(2)}, u32[]{:S(2)}) collective-permute-start(bf16[512,2048]{1,0:T(8,128)(2,1)S(1)} %bitcast.125), channel_id=1, source_target_pairs={{0,4},{4,0},{1,5},{5,1},{2,6},{6,2},{3,7},{7,3},{8,12},{12,8},{9,1... | collective-permute-start | bytes 6291464 | tf_op jit(solution)/shard_map/ppermute | solution.py:628
  314.6 58.4 %collective-permute-start.22 = (bf16[512,2048]{1,0:T(8,128)(2,1)}, bf16[512,2048]{1,0:T(8,128)(2,1)}, u32[]{:S(2)}, u32[]{:S(2)}) collective-permute-start(bf16[512,2048]{1,0:T(8,128)(2,1)} %collective-permute-done.16.mine_grads.refs_18_), channel_id=1, source_target_pairs={{0,4},{4,0},{1,5},{5,1},{2,6},{6,2},{3,7},{7,3},{8,12},{12,8},{9,1... | collective-permute-start | bytes 6291464 | tf_op jit(solution)/shard_map/ppermute | solution.py:628
  314.7 58.3 %collective-permute-start.23 = (bf16[512,2048]{1,0:T(8,128)(2,1)}, bf16[512,2048]{1,0:T(8,128)(2,1)}, u32[]{:S(2)}, u32[]{:S(2)}) collective-permute-start(bf16[512,2048]{1,0:T(8,128)(2,1)} %collective-permute-done.17.mine_grads.refs_20_), channel_id=1, source_target_pairs={{0,4},{4,0},{1,5},{5,1},{2,6},{6,2},{3,7},{7,3},{8,12},{12,8},{9,1... | collective-permute-start | bytes 6291464 | tf_op jit(solution)/shard_map/ppermute | solution.py:628
  315.2 31.5 %collective-permute-start.27 = (bf16[512,1024]{1,0:T(8,128)(2,1)S(1)}, bf16[512,1024]{1,0:T(8,128)(2,1)S(1)}, u32[]{:S(2)}, u32[]{:S(2)}) collective-permute-start(bf16[512,1024]{1,0:T(8,128)(2,1)S(1)} %pad_maximum_fusion.9.refs_1_.refs_0_), channel_id=1, source_target_pairs={{0,8},{8,0},{16,24},{24,16},{1,9},{9,1},{17,25},{25,17},{2,10},{10... | collective-permute-start | bytes 3145736 | tf_op jit(solution)/shard_map/ppermute | solution.py:628
  324.3 30.9 %collective-permute-start.28 = (bf16[512,1024]{1,0:T(8,128)(2,1)S(1)}, bf16[512,1024]{1,0:T(8,128)(2,1)S(1)}, u32[]{:S(2)}, u32[]{:S(2)}) collective-permute-start(bf16[512,1024]{1,0:T(8,128)(2,1)S(1)} %pad_maximum_fusion.9.refs_1_.refs_0_), channel_id=1, source_target_pairs={{0,16},{8,24},{16,0},{24,8},{1,17},{9,25},{17,1},{25,9},{2,18},{10... | collective-permute-start | bytes 3145736 | tf_op jit(solution)/shard_map/ppermute | solution.py:628
  356.1 16.9 %collective-permute-start.29 = (bf16[256,1024]{1,0:T(8,128)(2,1)}, bf16[256,1024]{1,0:T(8,128)(2,1)}, u32[]{:S(2)}, u32[]{:S(2)}) collective-permute-start(bf16[256,1024]{1,0:T(8,128)(2,1)} %slice.668), channel_id=1, source_target_pairs={{0,16},{8,24},{16,0},{24,8},{1,17},{9,25},{17,1},{25,9},{2,18},{10... | collective-permute-start | bytes 1572872 | tf_op jit(solution)/shard_map/ppermute | solution.py:628
  392.2 48.0 %collective-permute-start.34 = (bf16[512,2048]{1,0:T(8,128)(2,1)S(1)}, bf16[512,2048]{1,0:T(8,128)(2,1)}, u32[]{:S(2)}, u32[]{:S(2)}) collective-permute-start(bf16[512,2048]{1,0:T(8,128)(2,1)S(1)} %multiply_convert_fusion.mine.refs_8_), channel_id=1, source_target_pairs={{0,8},{8,0},{16,24},{24,16},{1,9},{9,1},{17,25},{25,17},{2,10},{10... | collective-permute-start | bytes 6291464 | tf_op jit(solution)/shard_map/ppermute | solution.py:628
  397.8 50.2 %collective-permute-start.38 = (bf16[512,2048]{1,0:T(8,128)(2,1)S(1)}, bf16[512,2048]{1,0:T(8,128)(2,1)}, u32[]{:S(2)}, u32[]{:S(2)}) collective-permute-start(bf16[512,2048]{1,0:T(8,128)(2,1)S(1)} %multiply_convert_fusion.mine.refs_8_), channel_id=1, source_target_pairs={{0,16},{8,24},{16,0},{24,8},{1,17},{9,25},{17,1},{25,9},{2,18},{10... | collective-permute-start | bytes 6291464 | tf_op jit(solution)/shard_map/ppermute | solution.py:628
  440.2 19.6 %collective-permute-start.35 = (bf16[512,2048]{1,0:T(8,128)(2,1)}, bf16[512,2048]{1,0:T(8,128)(2,1)}, u32[]{:S(2)}, u32[]{:S(2)}) collective-permute-start(bf16[512,2048]{1,0:T(8,128)(2,1)} %collective-permute-done.34.mine.refs_10_), channel_id=1, source_target_pairs={{0,4},{4,0},{1,5},{5,1},{2,6},{6,2},{3,7},{7,3},{8,12},{12,8},{9,1... | collective-permute-start | bytes 6291464 | tf_op jit(solution)/shard_map/ppermute | solution.py:628
  448.0 53.3 %collective-permute-start.41 = (bf16[512,2048]{1,0:T(8,128)(2,1)}, bf16[512,2048]{1,0:T(8,128)(2,1)}, u32[]{:S(2)}, u32[]{:S(2)}) collective-permute-start(bf16[512,2048]{1,0:T(8,128)(2,1)} %collective-permute-done.38.mine.refs_12_), channel_id=1, source_target_pairs={{0,4},{4,0},{1,5},{5,1},{2,6},{6,2},{3,7},{7,3},{8,12},{12,8},{9,1... | collective-permute-start | bytes 6291464 | tf_op jit(solution)/shard_map/ppermute | solution.py:628
  451.7 79.9 %collective-permute-start.45 = (bf16[256,2048]{1,0:T(8,128)(2,1)}, bf16[256,2048]{1,0:T(8,128)(2,1)}, u32[]{:S(2)}, u32[]{:S(2)}) collective-permute-start(bf16[256,2048]{1,0:T(8,128)(2,1)} %slice.673), channel_id=1, source_target_pairs={{0,16},{8,24},{16,0},{24,8},{1,17},{9,25},{17,1},{25,9},{2,18},{10... | collective-permute-start | bytes 3145736 | tf_op jit(solution)/shard_map/ppermute | solution.py:628
  453.5 79.4 %collective-permute-start.46 = (bf16[256,2048]{1,0:T(8,128)(2,1)S(1)}, bf16[256,2048]{1,0:T(8,128)(2,1)S(1)}, u32[]{:S(2)}, u32[]{:S(2)}) collective-permute-start(bf16[256,2048]{1,0:T(8,128)(2,1)S(1)} %slice.674), channel_id=1, source_target_pairs={{0,8},{8,0},{16,24},{24,16},{1,9},{9,1},{17,25},{25,17},{2,10},{10... | collective-permute-start | bytes 3145736 | tf_op jit(solution)/shard_map/ppermute | solution.py:628
  459.5 40.5 %collective-permute-start.39 = (bf16[256,2048]{1,0:T(8,128)(2,1)}, bf16[256,2048]{1,0:T(8,128)(2,1)S(1)}, u32[]{:S(2)}, u32[]{:S(2)}) collective-permute-start(bf16[256,2048]{1,0:T(8,128)(2,1)} %slice.671), channel_id=1, source_target_pairs={{0,16},{8,24},{16,0},{24,8},{1,17},{9,25},{17,1},{25,9},{2,18},{10... | collective-permute-start | bytes 3145736 | tf_op jit(solution)/shard_map/ppermute | solution.py:628
  459.8 41.6 %collective-permute-start.40 = (bf16[256,2048]{1,0:T(8,128)(2,1)}, bf16[256,2048]{1,0:T(8,128)(2,1)}, u32[]{:S(2)}, u32[]{:S(2)}) collective-permute-start(bf16[256,2048]{1,0:T(8,128)(2,1)} %slice.672), channel_id=1, source_target_pairs={{0,8},{8,0},{16,24},{24,16},{1,9},{9,1},{17,25},{25,17},{2,10},{10... | collective-permute-start | bytes 3145736 | tf_op jit(solution)/shard_map/ppermute | solution.py:628
  537.9 48.0 %collective-permute-start.43 = (bf16[512,2048]{1,0:T(8,128)(2,1)}, bf16[512,2048]{1,0:T(8,128)(2,1)S(1)}, u32[]{:S(2)}, u32[]{:S(2)}) collective-permute-start(bf16[512,2048]{1,0:T(8,128)(2,1)} %add_convert_fusion.5), channel_id=1, source_target_pairs={{0,16},{8,24},{16,0},{24,8},{1,17},{9,25},{17,1},{25,9},{2,18},{10... | collective-permute-start | bytes 6291464 | tf_op jit(solution)/shard_map/ppermute | solution.py:628
  543.6 48.0 %collective-permute-start.37 = (bf16[512,2048]{1,0:T(8,128)(2,1)}, bf16[512,2048]{1,0:T(8,128)(2,1)}, u32[]{:S(2)}, u32[]{:S(2)}) collective-permute-start(bf16[512,2048]{1,0:T(8,128)(2,1)} %add_convert_fusion.6), channel_id=1, source_target_pairs={{0,8},{8,0},{16,24},{24,16},{1,9},{9,1},{17,25},{25,17},{2,10},{10... | collective-permute-start | bytes 6291464 | tf_op jit(solution)/shard_map/ppermute | solution.py:628
  599.8 53.5 %collective-permute-start.49 = (bf16[512,2048]{1,0:T(8,128)(2,1)}, bf16[512,2048]{1,0:T(8,128)(2,1)}, u32[]{:S(2)}, u32[]{:S(2)}) collective-permute-start(bf16[512,2048]{1,0:T(8,128)(2,1)} %add_convert_fusion.4), channel_id=1, source_target_pairs={{0,24},{8,16},{16,8},{24,0},{1,25},{9,17},{17,9},{25,1},{2,26},{10... | collective-permute-start | bytes 6291464 | tf_op jit(solution)/shard_map/ppermute | solution.py:628
  653.4 342.7 %reduce-scatter.8.cloned.1.call-start = ((), (), s32[]{:S(2)}) async-start(), calls=%async_computation.9 | async-start | bytes 4456448 | tf_op jit(solution)/shard_map/reduce_scatter | solution.py:1018
  669.1 63.2 %collective-permute-start.55 = (bf16[512,2048]{1,0:T(8,128)(2,1)}, bf16[512,2048]{1,0:T(8,128)(2,1)}, u32[]{:S(2)}, u32[]{:S(2)}) collective-permute-start(bf16[512,2048]{1,0:T(8,128)(2,1)} %add_convert_fusion.2), channel_id=1, source_target_pairs={{0,16},{8,24},{16,0},{24,8},{1,17},{9,25},{17,1},{25,9},{2,18},{10... | collective-permute-start | bytes 6291464 | tf_op jit(solution)/shard_map/ppermute | solution.py:628
  670.7 61.5 %collective-permute-start.54 = (bf16[512,2048]{1,0:T(8,128)(2,1)}, bf16[512,2048]{1,0:T(8,128)(2,1)}, u32[]{:S(2)}, u32[]{:S(2)}) collective-permute-start(bf16[512,2048]{1,0:T(8,128)(2,1)} %add_convert_fusion.3), channel_id=1, source_target_pairs={{0,8},{8,0},{16,24},{24,16},{1,9},{9,1},{17,25},{25,17},{2,10},{10... | collective-permute-start | bytes 6291464 | tf_op jit(solution)/shard_map/ppermute | solution.py:628
  678.5 71.2 %collective-permute-start.56 = (bf16[512,2048]{1,0:T(8,128)(2,1)}, bf16[512,2048]{1,0:T(8,128)(2,1)}, u32[]{:S(2)}, u32[]{:S(2)}) collective-permute-start(bf16[512,2048]{1,0:T(8,128)(2,1)} %get-tuple-element.190), channel_id=1, source_target_pairs={{0,4},{4,0},{1,5},{5,1},{2,6},{6,2},{3,7},{7,3},{8,12},{12,8},{9,1... | collective-permute-start | bytes 6291464 | tf_op jit(solution)/shard_map/ppermute | solution.py:628
  700.5 29.2 %collective-permute-start.57 = (bf16[2,8,128,128]{3,2,1,0:T(8,128)(2,1)S(1)}, bf16[2,8,128,128]{3,2,1,0:T(8,128)(2,1)S(1)}, u32[]{:S(2)}, u32[]{:S(2)}) collective-permute-start(bf16[2,8,128,128]{3,2,1,0:T(8,128)(2,1)S(1)} %convert_element_type.355), channel_id=1, source_target_pairs={{8,0},{16,8},{24,16},{9,1},{17,9},{25,17},{10,2},{18,10},{26,18},{... | collective-permute-start | bytes 1572872 | tf_op jit(solution)/shard_map/ppermute | solution.py:639
  762.1 48.4 %collective-permute-start.60 = (bf16[512,2048]{1,0:T(8,128)(2,1)}, bf16[512,2048]{1,0:T(8,128)(2,1)}, u32[]{:S(2)}, u32[]{:S(2)}) collective-permute-start(bf16[512,2048]{1,0:T(8,128)(2,1)} %add_convert_fusion.1), channel_id=1, source_target_pairs={{0,24},{8,16},{16,8},{24,0},{1,25},{9,17},{17,9},{25,1},{2,26},{10... | collective-permute-start | bytes 6291464 | tf_op jit(solution)/shard_map/ppermute | solution.py:628
  768.4 48.1 %collective-permute-start.53 = (bf16[512,2048]{1,0:T(8,128)(2,1)}, bf16[512,2048]{1,0:T(8,128)(2,1)}, u32[]{:S(2)}, u32[]{:S(2)}) collective-permute-start(bf16[512,2048]{1,0:T(8,128)(2,1)} %get-tuple-element.185), channel_id=1, source_target_pairs={{0,4},{4,0},{1,5},{5,1},{2,6},{6,2},{3,7},{7,3},{8,12},{12,8},{9,1... | collective-permute-start | bytes 6291464 | tf_op jit(solution)/shard_map/ppermute | solution.py:628
  824.0 81.0 %collective-permute-start.67 = (bf16[512,1536]{1,0:T(8,128)(2,1)}, bf16[512,1536]{1,0:T(8,128)(2,1)}, u32[]{:S(2)}, u32[]{:S(2)}) collective-permute-start(bf16[512,1536]{1,0:T(8,128)(2,1)} %convolution_convert_fusion.3), channel_id=1, source_target_pairs={{0,16},{8,24},{16,0},{24,8},{1,17},{9,25},{17,1},{25,9},{2,18},{10... | collective-permute-start | bytes 4718600 | tf_op jit(solution)/shard_map/ppermute | solution.py:628
  827.3 77.8 %collective-permute-start.66 = (bf16[512,1536]{1,0:T(8,128)(2,1)}, bf16[512,1536]{1,0:T(8,128)(2,1)}, u32[]{:S(2)}, u32[]{:S(2)}) collective-permute-start(bf16[512,1536]{1,0:T(8,128)(2,1)} %convolution_convert_fusion.4), channel_id=1, source_target_pairs={{0,8},{8,0},{16,24},{24,16},{1,9},{9,1},{17,25},{25,17},{2,10},{10... | collective-permute-start | bytes 4718600 | tf_op jit(solution)/shard_map/ppermute | solution.py:628
  871.0 22.5 %collective-permute-start.63 = (f32[2,8,1536]{2,1,0:T(8,128)}, f32[2,8,1536]{2,1,0:T(8,128)S(1)}, u32[]{:S(2)}, u32[]{:S(2)}) collective-permute-start(f32[2,8,1536]{2,1,0:T(8,128)} %get-tuple-element.213), channel_id=1, source_target_pairs={{8,0},{16,8},{24,16},{9,1},{17,9},{25,17},{10,2},{18,10},{26,18},{... | collective-permute-start | bytes 294920 | tf_op jit(solution)/shard_map/ppermute | solution.py:639
  899.5 49.5 %collective-permute-start.65 = (bf16[512,1664]{1,0:T(8,128)(2,1)S(1)}, bf16[512,1664]{1,0:T(8,128)(2,1)S(1)}, u32[]{:S(2)}, u32[]{:S(2)}) collective-permute-start(bf16[512,1664]{1,0:T(8,128)(2,1)S(1)} %convolution_convert_fusion.1), channel_id=1, source_target_pairs={{0,16},{8,24},{16,0},{24,8},{1,17},{9,25},{17,1},{25,9},{2,18},{10... | collective-permute-start | bytes 5111816 | tf_op jit(solution)/shard_map/ppermute | solution.py:628
  901.7 47.9 %collective-permute-start.64 = (bf16[512,1664]{1,0:T(8,128)(2,1)S(1)}, bf16[512,1664]{1,0:T(8,128)(2,1)S(1)}, u32[]{:S(2)}, u32[]{:S(2)}) collective-permute-start(bf16[512,1664]{1,0:T(8,128)(2,1)S(1)} %convolution_convert_fusion.2), channel_id=1, source_target_pairs={{0,8},{8,0},{16,24},{24,16},{1,9},{9,1},{17,25},{25,17},{2,10},{10... | collective-permute-start | bytes 5111816 | tf_op jit(solution)/shard_map/ppermute | solution.py:628
  951.9 26.2 %collective-permute-start.69 = (bf16[256,1664]{1,0:T(8,128)(2,1)}, bf16[256,1664]{1,0:T(8,128)(2,1)S(1)}, u32[]{:S(2)}, u32[]{:S(2)}) collective-permute-start(bf16[256,1664]{1,0:T(8,128)(2,1)} %fusion.15), channel_id=1, source_target_pairs={{0,16},{8,24},{16,0},{24,8},{1,17},{9,25},{17,1},{25,9},{2,18},{10... | collective-permute-start | bytes 2555912 | tf_op jit(solution)/shard_map/ppermute | solution.py:628
  955.9 22.3 %collective-permute-start.68 = (bf16[256,1664]{1,0:T(8,128)(2,1)}, bf16[256,1664]{1,0:T(8,128)(2,1)}, u32[]{:S(2)}, u32[]{:S(2)}) collective-permute-start(bf16[256,1664]{1,0:T(8,128)(2,1)} %fusion.16), channel_id=1, source_target_pairs={{0,8},{8,0},{16,24},{24,16},{1,9},{9,1},{17,25},{25,17},{2,10},{10... | collective-permute-start | bytes 2555912 | tf_op jit(solution)/shard_map/ppermute | solution.py:628
  981.4 19.7 %collective-permute-start.70 = (bf16[2,256,2048]{2,1,0:T(8,128)(2,1)}, bf16[2,256,2048]{2,1,0:T(8,128)(2,1)}, u32[]{:S(2)}, u32[]{:S(2)}) collective-permute-start(bf16[2,256,2048]{2,1,0:T(8,128)(2,1)} %constant_dynamic-slice_fusion.3), channel_id=1, source_target_pairs={{0,4},{4,0},{1,5},{5,1},{2,6},{6,2},{3,7},{7,3},{8,12},{12,8},{9,1... | collective-permute-start | bytes 6291464 | tf_op jit(solution)/shard_map/ppermute | solution.py:628
  981.5 37.8 %collective-permute-start.81 = (bf16[256,1536]{1,0:T(8,128)(2,1)}, bf16[256,1536]{1,0:T(8,128)(2,1)}, u32[]{:S(2)}, u32[]{:S(2)}) collective-permute-start(bf16[256,1536]{1,0:T(8,128)(2,1)} %fusion.13), channel_id=1, source_target_pairs={{0,16},{8,24},{16,0},{24,8},{1,17},{9,25},{17,1},{25,9},{2,18},{10... | collective-permute-start | bytes 2359304 | tf_op jit(solution)/shard_map/ppermute | solution.py:628
  982.0 37.6 %collective-permute-start.80 = (bf16[256,1536]{1,0:T(8,128)(2,1)}, bf16[256,1536]{1,0:T(8,128)(2,1)}, u32[]{:S(2)}, u32[]{:S(2)}) collective-permute-start(bf16[256,1536]{1,0:T(8,128)(2,1)} %fusion.12), channel_id=1, source_target_pairs={{0,8},{8,0},{16,24},{24,16},{1,9},{9,1},{17,25},{25,17},{2,10},{10... | collective-permute-start | bytes 2359304 | tf_op jit(solution)/shard_map/ppermute | solution.py:628
  991.5 33.6 %all-to-all-start.1 = ((bf16[4,2112,128]{2,1,0:T(8,128)(2,1)}), bf16[4,2112,128]{2,1,0:T(8,128)(2,1)}, u32[]{:S(2)}, u32[]{:S(2)}) async-start(bf16[4,2112,128]{2,1,0:T(8,128)(2,1)} %bitcast.140), calls=%async_computation.4 | async-start | bytes 4325376 | tf_op jit(solution)/shard_map/all_to_all | solution.py:1091
  996.0 88.3 %reduce-scatter.6.cloned.1.call-start = ((), (), s32[]{:S(2)}) async-start(), calls=%async_computation.8 | async-start | bytes 1966080 | tf_op jit(solution)/shard_map/reduce_scatter | solution.py:1071
  1013.7 30.5 %collective-permute-start.77 = (bf16[128,1664]{1,0:T(8,128)(2,1)}, bf16[128,1664]{1,0:T(8,128)(2,1)S(1)}, u32[]{:S(2)}, u32[]{:S(2)}) collective-permute-start(bf16[128,1664]{1,0:T(8,128)(2,1)} %get-tuple-element.344), channel_id=1, source_target_pairs={{0,1},{1,2},{2,3},{3,0},{4,5},{5,6},{6,7},{7,4},{8,9},{9,10},{10,1... | collective-permute-start | bytes 1277960 | tf_op jit(solution)/shard_map/ppermute | solution.py:633
  1013.7 49.4 %collective-permute-start.78 = (bf16[128,1664]{1,0:T(8,128)(2,1)}, bf16[128,1664]{1,0:T(8,128)(2,1)}, u32[]{:S(2)}, u32[]{:S(2)}) collective-permute-start(bf16[128,1664]{1,0:T(8,128)(2,1)} %get-tuple-element.343), channel_id=1, source_target_pairs={{0,2},{1,3},{2,0},{3,1},{4,6},{5,7},{6,4},{7,5},{8,10},{9,11},{10,... | collective-permute-start | bytes 1277960 | tf_op jit(solution)/shard_map/ppermute | solution.py:633
  1019.4 43.8 %collective-permute-start.79 = (bf16[128,1664]{1,0:T(8,128)(2,1)}, bf16[128,1664]{1,0:T(8,128)(2,1)}, u32[]{:S(2)}, u32[]{:S(2)}) collective-permute-start(bf16[128,1664]{1,0:T(8,128)(2,1)} %get-tuple-element.342), channel_id=1, source_target_pairs={{0,3},{1,0},{2,1},{3,2},{4,7},{5,4},{6,5},{7,6},{8,11},{9,8},{10,9... | collective-permute-start | bytes 1277960 | tf_op jit(solution)/shard_map/ppermute | solution.py:633
  1042.1 23.4 %collective-permute-start.75 = (f32[16640]{0:T(1024)S(1)}, f32[16640]{0:T(1024)S(1)}, u32[]{:S(2)}, u32[]{:S(2)}) collective-permute-start(f32[16640]{0:T(1024)S(1)} %add.322), channel_id=1, source_target_pairs={{0,1},{1,0},{2,3},{3,2},{4,5},{5,4},{6,7},{7,6},{8,9},{9,8},{10,11... | collective-permute-start | bytes 199688 | tf_op jit(solution)/shard_map/ppermute | solution.py:628
  1065.5 21.2 %collective-permute-start.76 = (f32[16640]{0:T(1024)S(1)}, f32[16640]{0:T(1024)S(1)}, u32[]{:S(2)}, u32[]{:S(2)}) collective-permute-start(f32[16640]{0:T(1024)S(1)} %add.323), channel_id=1, source_target_pairs={{0,2},{1,3},{2,0},{3,1},{4,6},{5,7},{6,4},{7,5},{8,10},{9,11},{10,... | collective-permute-start | bytes 199688 | tf_op jit(solution)/shard_map/ppermute | solution.py:628
  (108 other events, 1021.4 us)
Sparse Core Ops, SparseCore 0:
  121.5 113.1 all-gather.2
  236.2 74.9 all-gather.4
  653.5 151.4 reduce-scatter.3
  824.1 100.6 reduce-scatter.7
  1025.1 50.4 reduce-scatter.5
